TPU v7x, 32 devices: a whole 2x2x4 slice. The times are simulated.
32 devices in a mesh: dom: 8 (over y, x, core), rot: 4 (over z).
Axes of the slice: x: 2, y: 2, z: 4, core: 2. Of those that a mesh axis runs over, the one named last changes fastest.
Arguments:
- raw_images: bfloat16 [12288, 4096], P('dom'), may hold values from -200 to 200, as said below
- defocus_bin: int32 [12288], P('dom'), may hold values from 0 to 63
- dest_row: int32 [12288], P('dom'), may hold values from -1 to 6143, as said below
- ctf_table: float32 [64, 2048], replicated, may hold values from -1 to 1
- inv_noise: float32 [2048], replicated, may hold values from 0.4 to 4
- panels: bfloat16 [5760, 4096], P('rot', 'dom'), may hold values from -0.1796875 to 0.1796875
Outputs:
- class_sums: float32 [4096, 5760], P('dom', 'rot')
- bin_weights: float32 [64, 5760], P(None, 'rot')
- log_evidence: float32 [6144], P('dom')
Inputs may be any that keep to these rules, and one draw needn't show every extreme that they name: `dest_row`: each row 0 to 6143 of the balanced layout is named by exactly one slot and -1 marks an empty slot. The slots of one device name at most 192 rows of any one block of 768 rows, and some device names exactly 192 rows of every block. `raw_images`: rows of empty slots are not read.
All inputs are finite; a program needn't handle non-finite values.
Results may differ from a plain program's by a relative error of at most 0.0095.
Values may be sent and summed in bfloat16 or wider, within the bound.
No kernel may reach another device: no remote copies, remote signals or barrier semaphores. Data moves between devices by JAX's collectives and lax.ppermute only.
A program may use at most 192 MiB of HBM per device.

v0:
```python
import jax
import jax.numpy as jnp
from jax import lax
from jax.sharding import PartitionSpec as P


def energy_block(gain_block, panel_piece):
    widened = panel_piece.astype(jnp.float32)
    return lax.dot_general(
        gain_block, widened * widened, (((1,), (1,)), ((), ())), precision=lax.Precision.HIGHEST
    )


def on_device(raw_images, defocus_bin, dest_row, ctf_table, inv_noise, panels):
    dom_count = lax.axis_size("dom")
    bin_count = ctf_table.shape[0]
    columns = raw_images.shape[1]
    hold_rows = raw_images.shape[0]
    shard_rows = hold_rows // 2
    capacity = 2 * shard_rows // dom_count
    is_live = dest_row >= 0
    target = jnp.where(is_live, dest_row // shard_rows, dom_count)
    local_row = dest_row % shard_rows
    marks = (target[:, None] == jnp.arange(dom_count, dtype=jnp.int32)[None, :]).astype(jnp.int32)
    slot_rank = jnp.sum((jnp.cumsum(marks, axis=0) - marks) * marks, axis=1)
    row_code = jnp.where(is_live, local_row * bin_count + defocus_bin, -1)
    padded_images = jnp.concatenate([raw_images, jnp.zeros((1, columns), raw_images.dtype)], axis=0)
    padded_code = jnp.concatenate([row_code, jnp.full((1,), -1, jnp.int32)], axis=0)
    position = jnp.where(is_live, target * capacity + slot_rank, dom_count * capacity)
    slot_count = dom_count * capacity
    source = (
        jnp.full((slot_count,), hold_rows, jnp.int32)
        .at[position]
        .set(jnp.arange(hold_rows, dtype=jnp.int32), mode="drop")
    )
    send_images = padded_images[source].reshape(dom_count, capacity, columns)
    send_code = padded_code[source].reshape(dom_count, capacity)
    recv_images, recv_code = (
        lax.all_to_all(send_images, "dom", split_axis=0, concat_axis=0, tiled=True),
        lax.all_to_all(send_code, "dom", split_axis=0, concat_axis=0, tiled=True),
    )
    flat_images = recv_images.reshape(-1, columns)
    flat_code = recv_code.reshape(-1)
    arrived = flat_code >= 0
    row_of = jnp.where(arrived, flat_code // bin_count, shard_rows)
    row_order = (
        jnp.zeros((shard_rows,), jnp.int32)
        .at[row_of]
        .set(jnp.arange(flat_code.shape[0], dtype=jnp.int32), mode="drop")
    )
    images = flat_images[row_order]
    bin_ids = flat_code[row_order] % bin_count
    bin_table = (bin_ids[:, None] == jnp.arange(bin_count, dtype=jnp.int32)[None, :]).astype(
        jnp.float32
    )
    ctf_rows = jnp.dot(bin_table, ctf_table, precision=lax.Precision.HIGHEST)
    factor = ctf_rows * inv_noise[None, :]
    weighted = (images.astype(jnp.float32) * jnp.concatenate([factor, factor], axis=1)).astype(
        jnp.bfloat16
    )
    gain_half = ctf_table * ctf_table * inv_noise[None, :]
    gain_full = jnp.concatenate([gain_half, gain_half], axis=1)
    panel_piece = lax.all_gather(panels, "dom", axis=1, tiled=True)
    col_block = weighted
    cross_term = lax.dot_general(
        col_block, panel_piece, (((1,), (1,)), ((), ())), preferred_element_type=jnp.float32
    )
    energy = energy_block(gain_full, panel_piece)
    scores = cross_term - 0.5 * jnp.dot(bin_table, energy, precision=lax.Precision.HIGHEST)
    local_peak = jnp.max(scores, axis=1)
    row_peak = lax.pmax(local_peak, "rot")
    shifted = jnp.exp(scores - row_peak[:, None])
    row_total = lax.psum(jnp.sum(shifted, axis=1), "rot")
    posterior = (shifted / row_total[:, None]).astype(jnp.bfloat16)
    log_evidence = row_peak + jnp.log(row_total)
    col_block = weighted
    class_sums = lax.psum_scatter(
        lax.dot_general(
            col_block, posterior, (((0,), (0,)), ((), ())), preferred_element_type=jnp.float32
        ).astype(jnp.bfloat16),
        "dom",
        scatter_dimension=0,
        tiled=True,
    ).astype(jnp.float32)
    local_mass = lax.dot_general(
        bin_table.astype(jnp.bfloat16),
        posterior,
        (((0,), (0,)), ((), ())),
        preferred_element_type=jnp.float32,
    )
    bin_weights = lax.psum(local_mass.astype(jnp.bfloat16), "dom").astype(jnp.float32)
    return (class_sums, bin_weights, log_evidence)


def solution(mesh):
    return jax.shard_map(
        on_device,
        mesh=mesh,
        in_specs=(P("dom", None), P("dom"), P("dom"), P(), P(), P("rot", "dom")),
        out_specs=(P("dom", "rot"), P(None, "rot"), P("dom")),
        check_vma=False,
    )
```

profile of v0, /device:TPU:0, one launch (start us, length us, event | category | flops | bytes accessed | tf_op | source)
XLA Modules:
  0.0 464.2 jit_solution(919226110993476938)
XLA Ops:
  7.2 0.0 all-gather.2.cloned.1.call-start
  7.2 0.7 all-gather.2.cloned.1.call-update
  7.9 0.7 fusion.18
  8.6 2.3 reduce-window.6
  10.9 0.3 slice_reduce_fusion
  11.2 0.2 reduce-window.9
  11.4 0.1 add_bitcast_fusion
  11.5 0.7 compare_select_fusion.3
  12.3 6.2 %scatter_custom_fusion = s32[1536]{0:T(1024)S(1)} fusion(s32[1536]{0:T(1024)S(1)} %get-tuple-element.3, s32[1536]{0:T(1024)S(1)} %iota.18, s32[]{:T(128)} %constant.58.clone.1), kind=kCustom, calls=%fused_computation.65 | custom fusion | bytes 6148 | tf_op jit(solution)/shard_map/scatter | solution.py:34
  18.5 8.4 %gather_fusion.1 = s32[1536]{0:T(1024)S(1)} fusion(s32[1537]{0:T(1024)S(1)} %pad_add_fusion, s32[2048]{0:T(1024)S(1)} %pad_clamp_fusion), kind=kCustom, calls=%fused_computation.1 | custom fusion | bytes 18432 | tf_op jit(solution)/shard_map/gather | solution.py:37
  26.9 0.7 all_to_all.10
  27.6 5.2 %all-to-all-start.1 = ((s32[8,1,192]{2,1,0:T(1,128)}), s32[8,1,192]{2,1,0:T(1,128)S(1)}, u32[]{:S(2)}, u32[]{:S(2)}) async-start(s32[8,1,192]{2,1,0:T(1,128)} %all_to_all.10), calls=%async_computation.1 | async-start | bytes 16384 | tf_op jit(solution)/shard_map/all_to_all | solution.py:40
  32.7 10.8 %concatenate.12 = bf16[1537,4096]{1,0:T(8,128)(2,1)} pad(bf16[1536,4096]{1,0:T(8,128)(2,1)} %param.6, bf16[]{:T(256)} %constant.57.clone.1), padding=0_1x0_0 | pad | bytes 25174018 | tf_op jit(solution)/shard_map/concatenate | solution.py:27
  43.5 29.7 %gather_fusion = bf16[1536,4096]{1,0:T(8,128)(2,1)} fusion(bf16[1537,4096]{1,0:T(8,128)(2,1)} %concatenate.12, s32[2048]{0:T(1024)S(1)} %pad_clamp_fusion), kind=kCustom, calls=%fused_computation | custom fusion | bytes 25171968 | tf_op jit(solution)/shard_map/gather | solution.py:36
  73.2 0.0 all-to-all-done.1
  73.2 0.0 copy-start.1
  73.2 0.0 copy-start.2
  73.2 5.5 %all-to-all-start = ((bf16[8,192,4096]{2,1,0:T(8,128)(2,1)}), bf16[8,192,4096]{2,1,0:T(8,128)(2,1)}, u32[]{:S(2)}, u32[]{:S(2)}) async-start(bf16[8,192,4096]{2,1,0:T(8,128)(2,1)} %bitcast.28), calls=%async_computation | async-start | bytes 25165824 | tf_op jit(solution)/shard_map/all_to_all | solution.py:39
  78.7 0.0 all-reduce.3.cloned.1.call-start
  78.8 0.0 copy-done.1
  78.8 0.0 copy-done.2
  78.8 0.8 multiply_multiply_fusion
  79.7 0.1 reshape.149
  79.8 0.1 reshape.150
  79.8 0.1 fusion.23
  79.9 6.7 %scatter_custom_fusion.1 = s32[768]{0:T(1024)S(1)} fusion(s32[1536]{0:T(1024)S(1)} %fusion.23, s32[1536]{0:T(1024)S(1)} %iota.19, s32[]{:T(128)} %constant.59.clone.1), kind=kCustom, calls=%fused_computation.67 | custom fusion | bytes 3076 | tf_op jit(solution)/shard_map/scatter | solution.py:49
  86.6 4.5 gather_fusion.3
  91.1 4.6 convolution_multiply_fusion
  95.7 122.1 %all-to-all-done = bf16[8,192,4096]{2,1,0:T(8,128)(2,1)} async-done(((bf16[8,192,4096]{2,1,0:T(8,128)(2,1)}), bf16[8,192,4096]{2,1,0:T(8,128)(2,1)}, u32[]{:S(2)}, u32[]{:S(2)}) %all-to-all-start) | async-done | bytes 12582944 | tf_op jit(solution)/shard_map/all_to_all | solution.py:39
  217.7 18.2 %gather_fusion.2 = bf16[768,4096]{1,0:T(8,128)(2,1)} fusion(bf16[1536,4096]{1,0:T(8,128)(2,1)} %bitcast.3, s32[1024]{0:T(1024)S(1)} %pad_clamp_fusion.1), kind=kCustom, calls=%fused_computation.2 | custom fusion | bytes 12585984 | tf_op jit(solution)/shard_map/gather | solution.py:51
  235.9 0.0 all-gather.2.cloned.1.call-done
  235.9 0.0 copy-start
  235.9 25.1 %fusion = f32[64,1440]{1,0:T(8,128)S(1)} fusion(bf16[1440,4096]{1,0:T(8,128)(2,1)} %all-gather.2.cloned.1.call-done, f32[64,2048]{1,0:T(8,128)} %multiply_multiply_fusion), kind=kOutput, calls=%fused_computation.6 | convolution fusion | flops 4541906944 | bytes 12689408 | tf_op jit(solution)/shard_map/dot_general | solution.py:9
  261.0 0.0 copy-done
  261.1 16.0 %fusion.12 = f32[768,1440]{0,1:T(8,128)} fusion(bf16[1440,4096]{1,0:T(8,128)(2,1)} %all-gather.2.cloned.1.call-done, f32[768,2048]{1,0:T(8,128)S(1)} %copy-done, bf16[768,4096]{1,0:T(8,128)(2,1)} %gather_fusion.2), kind=kOutput, calls=%fused_computation.27 | convolution fusion | flops 9072279552 | bytes 28803072 | tf_op jit(solution)/shard_map/dot_general | solution.py:65
  277.1 6.6 %fusion.33 = (f32[768]{0:T(1024)S(1)}, f32[768,1440]{0,1:T(8,128)}) fusion(f32[768,1440]{0,1:T(8,128)} %fusion.12, f32[64,1440]{1,0:T(8,128)S(1)} %fusion, s32[768]{0:T(1024)S(1)} %add_select_fusion.2), kind=kOutput, calls=%fused_computation.73 | convolution fusion | flops 852712704 | bytes 9222144 | tf_op jit(solution)/shard_map/dot_general | solution.py:69
  283.7 12.0 %pmax.7 = f32[768]{0:T(1024)S(1)} all-reduce(f32[768]{0:T(1024)S(1)} %get-tuple-element.7), channel_id=1, replica_groups=mesh['dom'=8,'rot'=4] {'rot'}, use_global_device_ids=true, to_apply=%region_6.7 | all-reduce | flops 768 | bytes 6144 | tf_op jit(solution)/shard_map/pmax | solution.py:71
  295.6 2.9 fusion.4
  298.5 8.4 %psum.14 = f32[768]{0:T(1024)S(1)} all-reduce(f32[768]{0:T(1024)S(1)} %fusion.4), channel_id=1, replica_groups=mesh['dom'=8,'rot'=4] {'rot'}, use_global_device_ids=true, to_apply=%region_8.9 | all-reduce | flops 768 | bytes 6144 | tf_op jit(solution)/shard_map/psum | solution.py:73
  306.9 3.0 divide_convert_fusion
  309.9 1.6 convolution_convert_fusion.1
  311.4 0.0 all-reduce.3.cloned.1.call-update
  311.5 0.0 reduce-scatter.2.cloned.1.call-start
  311.5 19.2 %convolution_convert_fusion = bf16[4096,1440]{0,1:T(8,128)(2,1)} fusion(bf16[768,1440]{0,1:T(8,128)(2,1)S(1)} %divide_convert_fusion, f32[768,2048]{1,0:T(8,128)} %convolution_multiply_fusion, bf16[768,4096]{1,0:T(8,128)(2,1)} %gather_fusion.2), kind=kOutput, calls=%fused_computation.9 | convolution fusion | flops 9078177792 | bytes 26591232 | tf_op jit(solution)/shard_map/dot_general | solution.py:78
  330.7 0.0 reduce-scatter.2.cloned.1.call-update
  330.7 0.6 log_add_fusion
  331.3 31.6 %all-reduce.3.cloned.1.call-done = bf16[64,1440]{1,0:T(8,128)(2,1)} async-done(((bf16[64,1440]{1,0:T(8,128)(2,1)}), bf16[64,1440]{1,0:T(8,128)(2,1)}) %all-reduce.3.cloned.1.call-update) | async-done | bytes 184336 | tf_op jit(solution)/shard_map/psum | solution.py:91
  362.9 1.7 convert_element_type.48
  364.6 89.4 %reduce-scatter.2.cloned.1.call-done = bf16[512,1440]{0,1:T(8,128)(2,1)} async-done(((bf16[4096,1440]{0,1:T(8,128)(2,1)}), bf16[512,1440]{0,1:T(8,128)(2,1)}) %reduce-scatter.2.cloned.1.call-update) | async-done | bytes 1474576 | tf_op jit(solution)/shard_map/reduce_scatter | solution.py:77
  454.0 3.4 convert_element_type.44
  (11 shorter events, 0.1 us)
Async XLA Ops:
  7.2 228.8 %all-gather.2.cloned.1.call-start = ((), (), s32[]{:S(2)}) async-start(), calls=%async_computation.3 | async-start | bytes 13271040 | tf_op jit(solution)/shard_map/all_gather | solution.py:63
  27.6 45.7 %all-to-all-start.1 = ((s32[8,1,192]{2,1,0:T(1,128)}), s32[8,1,192]{2,1,0:T(1,128)S(1)}, u32[]{:S(2)}, u32[]{:S(2)}) async-start(s32[8,1,192]{2,1,0:T(1,128)} %all_to_all.10), calls=%async_computation.1 | async-start | bytes 16384 | tf_op jit(solution)/shard_map/all_to_all | solution.py:40
  73.2 5.6 %copy-start.1 = (f32[64,2048]{1,0:T(8,128)S(1)}, f32[64,2048]{1,0:T(8,128)}, u32[]{:S(2)}) copy-start(f32[64,2048]{1,0:T(8,128)} %param.9) | copy-start | bytes 1572868
  73.2 5.6 %copy-start.2 = (f32[2048]{0:T(1024)S(1)}, f32[2048]{0:T(1024)}, u32[]{:S(2)}) copy-start(f32[2048]{0:T(1024)} %param.10) | copy-start | bytes 24580
  73.2 144.5 %all-to-all-start = ((bf16[8,192,4096]{2,1,0:T(8,128)(2,1)}), bf16[8,192,4096]{2,1,0:T(8,128)(2,1)}, u32[]{:S(2)}, u32[]{:S(2)}) async-start(bf16[8,192,4096]{2,1,0:T(8,128)(2,1)} %bitcast.28), calls=%async_computation | async-start | bytes 25165824 | tf_op jit(solution)/shard_map/all_to_all | solution.py:39
  78.7 284.2 %all-reduce.3.cloned.1.call-start = ((), (), s32[]{:S(2)}) async-start(), calls=%async_computation.5 | async-start | bytes 393216 | tf_op jit(solution)/shard_map/psum | solution.py:91
  235.9 25.1 %copy-start = (f32[768,2048]{1,0:T(8,128)S(1)}, f32[768,2048]{1,0:T(8,128)}, u32[]{:S(2)}) copy-start(f32[768,2048]{1,0:T(8,128)} %convolution_multiply_fusion) | copy-start | bytes 18874372
  311.5 142.6 %reduce-scatter.2.cloned.1.call-start = ((), (), s32[]{:S(2)}) async-start(), calls=%async_computation.4 | async-start | bytes 13271040 | tf_op jit(solution)/shard_map/reduce_scatter | solution.py:77
Sparse Core Ops, SparseCore 0:
  9.9 75.4 all-gather.1
  311.6 51.2 all-reduce.2
  366.4 87.5 reduce-scatter.1
where the time goes:
time: 472 us; the launch traced here: 464 us
  waiting for transfers between devices  244 us (52%)
  local copies, waits for them, and re-layouts  85.6 us (18%)
  matrix products  73 us (15%)
  blocking collectives  20.3 us (4%)
  other arithmetic  16.5 us (3%)
  between operations  14.2 us (3%)
  starting transfers between devices  10.8 us (2%)
    all_to_all x1, waiting for transfers between devices, on_device(): lax.all_to_all(send_images, 'dom', split_axis=0, concat_axis=0, tiled=True)  122 us
    reduce_scatter x1, waiting for transfers between devices, on_device(): lax.psum_scatter(lax.dot_general(col_block, posterior, (((0,), (0,)), (()...  89.4 us
    psum x1, waiting for transfers between devices, on_device(): lax.psum(local_mass.astype(jnp.bfloat16), 'dom').astype(jnp.float32)  31.6 us
    gather x1, local copies, waits for them, and re-layouts, on_device(): send_images = padded_images[source].reshape(dom_count, capacity, columns)  29.7 us
    dot_general x1, matrix products, energy_block(): lax.dot_general(gain_block, widened * widened, (((1,), (1,)), ((), ())),...  25.1 us
    dot_general x1, matrix products, on_device(): lax.dot_general(col_block, posterior, (((0,), (0,)), ((), ())), preferred...  19.2 us
    gather x1, local copies, waits for them, and re-layouts, on_device(): images = flat_images[row_order]  18.2 us
    dot_general x1, matrix products, on_device(): lax.dot_general(col_block, panel_piece, (((1,), (1,)), ((), ())), preferr...  16 us
  transfers between devices with their start and end apart: 5, of which 3 were waited for; matrix products, arithmetic and copies ran while one was open for 25% of the time, Pallas kernels for 0%

commit v1 on v0

--- a/solution.py
+++ b/solution.py
@@ -1,7 +1,530 @@
+import functools
+
 import jax
 import jax.numpy as jnp
 from jax import lax
+from jax.experimental import pallas as pl
+from jax.experimental.pallas import tpu as pltpu
 from jax.sharding import PartitionSpec as P
+
+NN = (((1,), (0,)), ((), ()))
+NT = (((1,), (1,)), ((), ()))
+F32, BF16, I32 = jnp.float32, jnp.bfloat16, jnp.int32
+VMEM_BYTES = 50 * 1024 * 1024
+
+
+def mm(a, b, dims):
+    return lax.dot_general(a, b, dims, preferred_element_type=F32)
+
+
+def split3(x):
+    hi = x.astype(BF16)
+    rest = x - hi.astype(F32)
+    mid = rest.astype(BF16)
+    low = (rest - mid.astype(F32)).astype(BF16)
+    return hi, mid, low
+
+
+def call(body, grid, in_specs, out_specs, out_shape, scratch=(), alias=None, flops=0, moved=0):
+    return pl.pallas_call(
+        body,
+        grid_spec=pltpu.PrefetchScalarGridSpec(
+            num_scalar_prefetch=1,
+            grid=grid,
+            in_specs=in_specs,
+            out_specs=out_specs,
+            scratch_shapes=list(scratch),
+        ),
+        out_shape=out_shape,
+        input_output_aliases=alias or {},
+        compiler_params=pltpu.CompilerParams(vmem_limit_bytes=VMEM_BYTES),
+        cost_estimate=pl.CostEstimate(flops=flops, bytes_accessed=moved, transcendentals=0),
+    )
+
+
+def sds(shape, dtype):
+    return jax.ShapeDtypeStruct(shape, dtype)
+
+
+def one_hot_rows(out_ref, wanted):
+    rows, width = out_ref.shape
+    step = 256 if rows % 256 == 0 else rows
+    for start in range(0, rows, step):
+        index = lax.broadcasted_iota(I32, (step, width), 0) + start
+        out_ref[start : start + step, :] = jnp.where(index == wanted, 1.0, 0.0).astype(BF16)
+
+
+def pack_body(dom, shard_rows, cap, meta, dest_ref, bin_ref, raw_ref, out_ref, code_ref, pick_ref):
+    @pl.when(pl.program_id(0) == 0)
+    def _():
+        dest = dest_ref[...]
+        hold = dest.shape[1]
+        low = lax.broadcasted_iota(I32, (dom, hold), 0) * shard_rows
+        inside = jnp.logical_and(dest >= low, dest < low + shard_rows)
+        marks = jnp.where(inside, 1.0, 0.0)
+        base = jnp.sum(jnp.where(inside, low, 0), axis=0, keepdims=True)
+        local = dest - base
+        lanes = 128
+        before = (
+            lax.broadcasted_iota(I32, (lanes, lanes), 0)
+            < lax.broadcasted_iota(I32, (lanes, lanes), 1)
+        )
+        upper = jnp.where(before, 1.0, 0.0).astype(BF16)
+        carry = jnp.zeros((dom, 1), F32)
+        first_slot = lax.broadcasted_iota(I32, (dom, lanes), 0).astype(F32) * cap
+        places = []
+        for start in range(0, hold, lanes):
+            part = marks[:, start : start + lanes]
+            rank = mm(part.astype(BF16), upper, NN) + carry
+            places.append(
+                jnp.sum(jnp.where(part > 0, rank + first_slot + 1.0, 0.0), axis=0, keepdims=True)
+            )
+            carry = carry + jnp.sum(part, axis=1, keepdims=True)
+        place = jnp.concatenate(places, axis=1).astype(I32) - 1
+        one_hot_rows(pick_ref, place)
+        which = lax.broadcasted_iota(I32, (8, hold), 0)
+        digits = jnp.where(
+            which == 0,
+            local >> 4,
+            jnp.where(which == 1, local & 15, jnp.where(which == 2, bin_ref[...], 1)),
+        )
+        digits = jnp.where(dest >= 0, digits, 0).astype(F32).astype(BF16)
+        got = mm(digits, pick_ref[...], NT)
+        code = got[0:1] * 1024.0 + got[1:2] * 64.0 + got[2:3] + got[3:4] - 1.0
+        code_ref[...] = code.astype(I32)
+
+    out_ref[...] = mm(pick_ref[...], raw_ref[...], NN).astype(BF16)
+
+
+def pack(meta, raw_images, dest, bins, dom, width, block):
+    hold, _ = raw_images.shape
+    shard_rows = hold // 2
+    cap = hold // dom
+    slots = dom * cap
+    steps = width // block
+    body = functools.partial(pack_body, dom, shard_rows, cap)
+    return call(
+        body,
+        (steps,),
+        [
+            pl.BlockSpec((1, hold), lambda j, m: (0, 0)),
+            pl.BlockSpec((1, hold), lambda j, m: (0, 0)),
+            pl.BlockSpec((hold, block), lambda j, m: (0, m[1] * steps + j)),
+        ],
+        [
+            pl.BlockSpec((slots, block), lambda j, m: (0, j)),
+            pl.BlockSpec((1, slots), lambda j, m: (0, 0)),
+        ],
+        [sds((slots, width), BF16), sds((1, slots), I32)],
+        scratch=[pltpu.VMEM((slots, hold), BF16)],
+        flops=2 * slots * hold * width,
+        moved=4 * hold * width,
+    )(meta, dest, bins, raw_images)
+
+
+def unpack_body(bins, meta, code_ref, recv_ref, ctf_ref, inv_ref, out_ref, hot_ref, pick, wide):
+    shard_rows = out_ref.shape[0]
+
+    @pl.when(pl.program_id(0) == 0)
+    def _():
+        code = code_ref[...]
+        one_hot_rows(pick, code >> 6)
+        slot_bin = (code & 63).astype(F32).astype(BF16)
+        slot_bins = jnp.broadcast_to(slot_bin, (8, slot_bin.shape[1]))
+        down = mm(pick[...], slot_bins, NT)[:, 0:1].astype(I32)
+        across = mm(slot_bins, pick[...], NT)[0:1].astype(I32)
+        lane = lax.broadcasted_iota(I32, (shard_rows, 3 * bins), 1)
+        wide[...] = jnp.where((lane & 63) == down, 1.0, 0.0).astype(BF16)
+        row = lax.broadcasted_iota(I32, (3 * bins, shard_rows), 0)
+        hot_ref[...] = jnp.where((row & 63) == across, 1.0, 0.0).astype(BF16)
+
+    image = mm(pick[...], recv_ref[...], NN)
+    table = jnp.concatenate(split3(ctf_ref[...] * inv_ref[...]), axis=0)
+    factor = mm(wide[...], table, NN)
+    out_ref[...] = (image * factor).astype(BF16)
+
+
+def unpack(meta, code, recv, ctf, inv, block):
+    slots, width = recv.shape
+    shard_rows = slots // 2
+    bins, pix = ctf.shape
+    steps = width // block
+    wrap = pix // block
+    return call(
+        functools.partial(unpack_body, bins),
+        (steps,),
+        [
+            pl.BlockSpec((1, slots), lambda j, m: (0, 0)),
+            pl.BlockSpec((slots, block), lambda j, m: (0, j)),
+            pl.BlockSpec((bins, block), lambda j, m: (0, lax.rem(m[1] * steps + j, wrap))),
+            pl.BlockSpec((1, block), lambda j, m: (0, lax.rem(m[1] * steps + j, wrap))),
+        ],
+        [
+            pl.BlockSpec((shard_rows, block), lambda j, m: (0, j)),
+            pl.BlockSpec((3 * bins, shard_rows), lambda j, m: (0, 0)),
+        ],
+        [sds((shard_rows, width), BF16), sds((3 * bins, shard_rows), BF16)],
+        scratch=[
+            pltpu.VMEM((shard_rows, slots), BF16),
+            pltpu.VMEM((shard_rows, 3 * bins), BF16),
+        ],
+        flops=2 * slots * shard_rows * width,
+        moved=2 * (slots + shard_rows) * width,
+    )(meta, code, recv, ctf, inv)
+
+
+def energy_body(bins, count, meta, *refs):
+    pieces, (ctf_ref, inv_ref, panel_ref, extra_ref, total) = refs[:count], refs[count:]
+    step = pl.program_id(0)
+
+    @pl.when(step == 0)
+    def _():
+        total[...] = jnp.zeros_like(total)
+
+    gain = ctf_ref[...] * ctf_ref[...] * inv_ref[...]
+    gain3 = jnp.concatenate(split3(gain), axis=0)
+    for index, piece in enumerate(pieces):
+
+        @pl.when(step == index)
+        def _():
+            panel = piece[...]
+            panel_ref[...] = panel
+            wide = panel.astype(F32)
+            square = wide * wide
+            high = square.astype(BF16)
+            low = (square - high.astype(F32)).astype(BF16)
+            total[...] += mm(high, gain3, NT) + mm(low, gain3, NT)
+
+    @pl.when(step == count - 1)
+    def _():
+        whole = total[:, :bins] + total[:, bins : 2 * bins] + total[:, 2 * bins :]
+        extra_ref[...] = jnp.concatenate(split3(-0.5 * whole), axis=1)
+
+
+def energy(meta, pieces, ctf, inv):
+    count = len(pieces)
+    rows, width = pieces[0].shape
+    bins, pix = ctf.shape
+    wrap = pix // width
+    return call(
+        functools.partial(energy_body, bins, count),
+        (count,),
+        [pl.BlockSpec((rows, width), lambda j, m: (0, 0))] * count
+        + [
+            pl.BlockSpec((bins, width), lambda j, m: (0, lax.rem(m[0] ^ j, wrap))),
+            pl.BlockSpec((1, width), lambda j, m: (0, lax.rem(m[0] ^ j, wrap))),
+        ],
+        [
+            pl.BlockSpec((rows, width), lambda j, m: (0, m[0] ^ j)),
+            pl.BlockSpec((rows, 3 * bins), lambda j, m: (0, 0)),
+        ],
+        [sds((rows, count * width), BF16), sds((rows, 3 * bins), BF16)],
+        scratch=[pltpu.VMEM((rows, 3 * bins), F32)],
+        flops=2 * 4 * rows * bins * count * width * 3,
+        moved=4 * rows * count * width,
+    )(meta, *pieces, ctf, inv)
+
+
+def score_body(first, last, meta, own_ref, sib_ref, panel_ref, *refs):
+    if first:
+        acc_out, full_ref = refs
+    elif last:
+        acc_ref, _, hot_own, hot_sib, extra_ref, shifted_ref, stat_ref, full_ref = refs
+    else:
+        acc_ref, _, acc_out, full_ref = refs
+    half = pl.num_programs(0) // 2
+
+    def tile(source, hot):
+        block = source[...]
+        full_ref[...] = block
+        total = mm(panel_ref[...], block, NT)
+        if not first:
+            total = acc_ref[...] + total
+        if not last:
+            acc_out[...] = total
+            return
+        total = total + mm(extra_ref[...], hot[...], NN)
+        peak = jnp.max(total, axis=0, keepdims=True)
+        shifted = jnp.exp(total - peak)
+        shifted_ref[...] = shifted
+        mass = jnp.sum(shifted, axis=0, keepdims=True)
+        which = lax.broadcasted_iota(I32, stat_ref.shape, 0)
+        stat_ref[...] = jnp.where(which == 0, peak, mass)
+
+    @pl.when(pl.program_id(0) < half)
+    def _():
+        tile(own_ref, hot_own if last else None)
+
+    @pl.when(pl.program_id(0) >= half)
+    def _():
+        tile(sib_ref, hot_sib if last else None)
+
+
+def score(meta, turn, turns, own, sib, panels, acc, full, hots=None, extra=None):
+    rows, width = own.shape
+    tile = 256
+    half = rows // tile
+    count = panels.shape[0]
+    first, last = turn == 0, turn == turns - 1
+
+    def share(m):
+        return lax.rem(m[1] + turns - turn, turns)
+
+    front = pl.BlockSpec((tile, width), lambda j, m: (jnp.minimum(j, half - 1), 0))
+    back = pl.BlockSpec((tile, width), lambda j, m: (jnp.maximum(j - half, 0), 0))
+    acc_spec = pl.BlockSpec((count, tile), lambda j, m: (0, j))
+    full_spec = pl.BlockSpec((tile, width), lambda j, m: (j, share(m)))
+    in_specs = [front, back, pl.BlockSpec((count, width), lambda j, m: (0, share(m)))]
+    operands = [meta, own, sib, panels]
+    alias = {}
+    if not first:
+        in_specs += [acc_spec, pl.BlockSpec(memory_space=pl.ANY)]
+        operands += [acc, full]
+        alias = {4: 0, 5: 2 if last else 1}
+    out_specs = [acc_spec, full_spec]
+    full_shape = sds((2 * rows, width * turns), BF16)
+    out_shape = [sds((count, 2 * rows), F32), full_shape]
+    if last:
+        depth = extra.shape[1]
+        in_specs += [
+            pl.BlockSpec((depth, tile), lambda j, m: (0, jnp.minimum(j, half - 1))),
+            pl.BlockSpec((depth, tile), lambda j, m: (0, jnp.maximum(j - half, 0))),
+            pl.BlockSpec((count, depth), lambda j, m: (0, 0)),
+        ]
+        operands += [*hots, extra]
+        out_specs = [acc_spec, pl.BlockSpec((8, tile), lambda j, m: (0, j)), full_spec]
+        out_shape = [out_shape[0], sds((8, 2 * rows), F32), full_shape]
+    return call(
+        functools.partial(score_body, first, last),
+        (2 * half,),
+        in_specs,
+        out_specs,
+        out_shape,
+        alias=alias,
+        flops=2 * count * 2 * rows * width,
+        moved=8 * count * 2 * rows + 8 * rows * width,
+    )(*operands)
+
+
+def merge_body(meta, mine_ref, other_ref, out_ref):
+    rows = mine_ref.shape[1] // 2
+    other = other_ref[...]
+    other = jnp.concatenate([other[:, rows:], other[:, :rows]], axis=1)
+    mine = mine_ref[...]
+    peak = jnp.maximum(mine[0:1], other[0:1])
+    mass = mine[1:2] * jnp.exp(mine[0:1] - peak) + other[1:2] * jnp.exp(other[0:1] - peak)
+    which = lax.broadcasted_iota(I32, out_ref.shape, 0)
+    out_ref[...] = jnp.where(which == 0, peak, mass)
+
+
+def merge(meta, mine, other):
+    spec = pl.BlockSpec(mine.shape, lambda j, m: (0, 0))
+    return call(merge_body, (1,), [spec, spec], spec, sds(mine.shape, F32))(meta, mine, other)
+
+
+def class_body(kind, meta, *refs):
+    if kind == "first":
+        shifted_ref, stat_ref, a_ref, b_ref, c_ref, d_ref, full_ref = refs[:7]
+        out_ref, post_ref, log_ref = refs[7:]
+
+        @pl.when(pl.program_id(0) == 0)
+        def _():
+            stats = [r[...] for r in (a_ref, b_ref, c_ref, d_ref)]
+            peaks = [s[0:1] for s in stats]
+            peak = jnp.maximum(
+                jnp.maximum(peaks[0], peaks[1]), jnp.maximum(peaks[2], peaks[3])
+            )
+            parts = [s[1:2] * jnp.exp(p - peak) for s, p in zip(stats, peaks)]
+            mass = (parts[0] + parts[1]) + (parts[2] + parts[3])
+            factor = jnp.exp(stat_ref[0:1] - peak) / mass
+            post_ref[...] = (shifted_ref[...] * factor).astype(BF16)
+            log_ref[...] = (peak + jnp.log(mass))[:, : log_ref.shape[1]]
+
+    elif kind == "mass":
+        post_ref, hot_own, hot_sib, full_ref, out_ref, mass_ref = refs
+        bins, columns = mass_ref.shape
+        rows = hot_own.shape[1]
+
+        @pl.when(pl.program_id(0) == 0)
+        def _():
+            mass_ref[...] = mm(hot_own[:bins, :], post_ref[:, :rows], NT) + mm(
+                hot_sib[:bins, :], post_ref[:, rows:], NT
+            )
+
+    else:
+        post_ref, full_ref, out_ref = refs
+    out_ref[...] = mm(post_ref[...], full_ref[...], NN).astype(out_ref.dtype)
+
+
+def class_sums_part(meta, kind, offset, steps, full, post=None, shifted=None, stats=None, hots=None, bins=0):
+    rows, columns = full.shape
+    width = columns // 8
+    count = (shifted if post is None else post).shape[0]
+    whole = lambda shape: pl.BlockSpec(shape, lambda j, m: (0, 0))
+    full_spec = pl.BlockSpec((rows, width), lambda j, m: (0, m[offset + j]))
+    out_spec = pl.BlockSpec((count, width), lambda j, m: (0, j))
+    dtype = F32 if kind == "rest" else BF16
+    out_shape = sds((count, steps * width), dtype)
+    if kind == "first":
+        operands = [shifted, *stats, full]
+        in_specs = [whole(shifted.shape)] + [whole(stats[0].shape)] * 5 + [full_spec]
+        out_specs = [out_spec, whole((count, rows)), whole((1, rows // 2))]
+        out_shape = [out_shape, sds((count, rows), BF16), sds((1, rows // 2), F32)]
+    elif kind == "mass":
+        operands = [post, *hots, full]
+        in_specs = [whole(post.shape), whole(hots[0].shape), whole(hots[1].shape), full_spec]
+        out_specs = [out_spec, whole((bins, count))]
+        out_shape = [out_shape, sds((bins, count), F32)]
+    else:
+        operands = [post, full]
+        in_specs = [whole(post.shape), full_spec]
+        out_specs = out_spec
+    return call(
+        functools.partial(class_body, kind),
+        (steps,),
+        in_specs,
+        out_specs,
+        out_shape,
+        flops=2 * count * rows * width * steps,
+        moved=2 * rows * width * steps + 4 * count * (rows + width * steps),
+    )(meta, *operands)
+
+
+def forward_body(meta, y_ref, x_ref, down_ref, left_ref, a_ref, b_ref):
+    vertical = (y_ref[...] + down_ref[...].astype(F32)).astype(BF16)
+    side = (x_ref[...] + left_ref[...].astype(F32)).astype(BF16)
+    even = meta[0] % 2 == 0
+    a_ref[...] = jnp.where(even, vertical, side)
+    b_ref[...] = jnp.where(even, side, vertical)
+
+
+def forward(meta, rest, got_x, got_y):
+    count, columns = rest.shape
+    width = columns // 4
+    tile = count // 5
+    at = lambda k: pl.BlockSpec((tile, width), lambda j, m: (j, k))
+    shape = sds((count, width), BF16)
+    return call(
+        forward_body, (5,), [at(2), at(3), at(1), at(1)], [at(0), at(0)], [shape, shape]
+    )(meta, rest, rest, got_x, got_y)
+
+
+def settle_body(meta, first_ref, second_ref, down_ref, left_ref, keep_ref, give_ref):
+    first = first_ref[...] + down_ref[...].astype(F32)
+    second = second_ref[...] + left_ref[...].astype(F32)
+    even = meta[0] % 2 == 0
+    keep_ref[...] = jnp.where(even, first, second)
+    give_ref[...] = jnp.where(even, second, first).astype(BF16)
+
+
+def settle(meta, rest, got_x, got_y):
+    count, columns = rest.shape
+    width = columns // 4
+    tile = count // 5
+    at = lambda k: pl.BlockSpec((tile, width), lambda j, m: (j, k))
+    return call(
+        settle_body,
+        (5,),
+        [at(0), at(1), at(0), at(0)],
+        [at(0), at(0)],
+        [sds((count, width), F32), sds((count, width), BF16)],
+    )(meta, rest, rest, got_x, got_y)
+
+
+def finish_body(meta, keep_ref, a_ref, give_ref, b_ref, out_ref, tall):
+    count = keep_ref.shape[0]
+    core = meta[0] % 2
+    mine = pl.multiple_of(core * count, 8)
+    other = pl.multiple_of((1 - core) * count, 8)
+    tall[pl.ds(mine, count), :] = keep_ref[...] + a_ref[...].astype(F32)
+    tall[pl.ds(other, count), :] = give_ref[...].astype(F32) + b_ref[...].astype(F32)
+    out_ref[...] = tall[...].T[:, : 2 * count]
+
+
+def finish(meta, keep, got_a, got_self, got_b):
+    count, width = keep.shape
+    lanes = 128
+    tall = -(-2 * count // lanes) * lanes
+    spec = pl.BlockSpec((count, lanes), lambda j, m: (0, j))
+    return call(
+        finish_body,
+        (width // lanes,),
+        [spec] * 4,
+        pl.BlockSpec((lanes, 2 * count), lambda j, m: (j, 0)),
+        sds((width, 2 * count), F32),
+        scratch=[pltpu.VMEM((tall, lanes), F32)],
+    )(meta, keep, got_a, got_self, got_b)
+
+
+def two_by_two(raw_images, defocus_bin, dest_row, ctf_table, inv_noise, panels):
+    dom, turns = lax.axis_size("dom"), lax.axis_size("rot")
+    device, plane = lax.axis_index("dom"), lax.axis_index("rot")
+    bins = ctf_table.shape[0]
+    hold, columns = raw_images.shape
+    cap = hold // dom
+    chip, core = device // 2, device % 2
+    order = [(1, 0), (3, 0), (2, 1), (3, 1), (0, 0), (0, 1), (2, 0), (1, 1)]
+    meta = jnp.stack(
+        [device, plane] + [((chip ^ apart) * 2 + half) for apart, half in order]
+    ).astype(I32)
+    inv = inv_noise[None, :]
+
+    def across(value, apart):
+        return lax.ppermute(value, "dom", [(i, i ^ apart) for i in range(dom)])
+
+    width = columns // turns
+    packed, code = pack(meta, raw_images, dest_row[None, :], defocus_bin[None, :], dom, width, 256)
+    got_code = lax.all_to_all(code.reshape(dom, cap), "dom", 0, 0, tiled=True)
+    recv = lax.all_to_all(packed, "dom", 0, 0, tiled=True)
+
+    count = panels.shape[0] // 2
+    pieces = [None] * 8
+    pieces[0] = lax.dynamic_slice_in_dim(panels, core * count, count, 0)
+    pieces[1] = across(lax.dynamic_slice_in_dim(panels, (1 - core) * count, count, 0), 1)
+    pieces[2], pieces[4] = across(pieces[0], 2), across(pieces[0], 4)
+    pieces[3], pieces[5] = across(pieces[1], 2), across(pieces[1], 4)
+    pieces[6], pieces[7] = across(pieces[2], 4), across(pieces[5], 2)
+    panel_full, extra = energy(meta, pieces, ctf_table, inv)
+
+    share, hot = unpack(meta, got_code.reshape(1, hold), recv, ctf_table, inv, 256)
+    hots = (hot, across(hot, 1))
+    acc = full = None
+    for turn in range(turns):
+        other = across(share, 1)
+        if turn == turns - 1:
+            shifted, stat, full = score(
+                meta, turn, turns, share, other, panel_full, acc, full, hots, extra
+            )
+        else:
+            acc, full = score(meta, turn, turns, share, other, panel_full, acc, full)
+            share = lax.ppermute(share, "rot", [(i, (i + 1) % turns) for i in range(turns)])
+
+    pair = merge(meta, stat, across(stat, 1))
+    others = [
+        lax.ppermute(pair, "rot", [(i, i ^ apart) for i in range(turns)]) for apart in (1, 2, 3)
+    ]
+    to_x, post, log_evidence = class_sums_part(
+        meta, "first", 2, 2, full, shifted=shifted, stats=[stat, pair, *others]
+    )
+    got_x = across(to_x, 2)
+    to_y, mass = class_sums_part(meta, "mass", 4, 2, full, post=post, hots=hots, bins=bins)
+    got_y = across(to_y, 4)
+    rest = class_sums_part(meta, "rest", 6, 4, full, post=post)
+    mass = mass + across(mass, 2)
+    mass = mass + across(mass, 4)
+    mass_other = across(mass, 1)
+    bin_weights = jnp.where(
+        core == 0,
+        jnp.concatenate([mass, mass_other], axis=1),
+        jnp.concatenate([mass_other, mass], axis=1),
+    )
+    message_a, message_b = forward(meta, rest, got_x, got_y)
+    got_a = lax.ppermute(message_a, "dom", [(i, i ^ (4 if i % 2 == 0 else 2)) for i in range(dom)])
+    got_b = lax.ppermute(message_b, "dom", [(i, i ^ (3 if i % 2 == 0 else 5)) for i in range(dom)])
+    keep, give = settle(meta, rest, got_x, got_y)
+    got_self = across(give, 1)
+    class_sums = finish(meta, keep, got_a, got_self, got_b)
+    return class_sums, bin_weights, log_evidence.reshape(-1)
 
 
 def energy_block(gain_block, panel_piece):
@@ -93,8 +616,9 @@
 
 
 def solution(mesh):
+    small = mesh.shape["dom"] == 8 and mesh.shape["rot"] == 4
     return jax.shard_map(
-        on_device,
+        two_by_two if small else on_device,
         mesh=mesh,
         in_specs=(P("dom", None), P("dom"), P("dom"), P(), P(), P("rot", "dom")),
         out_specs=(P("dom", "rot"), P(None, "rot"), P("dom")),

time: 472 us -> 350 us (0.74); the launches traced: 464 us -> 349 us
  Pallas kernels: 0 us -> 102 us
  local copies, waits for them, and re-layouts: 85.6 us -> 9.28 us
  matrix products: 73 us -> 0 us
  waiting for transfers between devices: 244 us -> 187 us
  starting transfers between devices: 10.8 us -> 37.5 us
  other arithmetic: 16.5 us -> 1.63 us
  between operations: 14.2 us -> 0.81 us
  blocking collectives: 20.3 us -> 9.66 us
    ppermute x0 -> x27, waiting for transfers between devices: none -> 150 us  [the longest x19 81.3 us: across(): return lax.ppermute(value, 'dom', [(i, i ^ apart) for i in range(dom)])]
    pallas_call x0 -> x14, Pallas kernels: none -> 102 us  [the longest x4 37.2 us: score(): call(functools.partial(score_body, first, last), (2 * half,), in_specs, o...]
    reduce_scatter x1 -> x0, waiting for transfers between devices: 89.4 us -> none  [on_device(): lax.psum_scatter(lax.dot_general(col_block, posterior, (((0,), (0,)), (()...]
    all_to_all x2 -> x1, waiting for transfers between devices: 122 us -> 37.8 us  [two_by_two(): recv = lax.all_to_all(packed, 'dom', 0, 0, tiled=True)]
    dot_general x6 -> x0, matrix products: 73 us -> none  [the longest x1 25.1 us: energy_block(): lax.dot_general(gain_block, widened * widened, (((1,), (1,)), ((), ())),...]
    gather x4 -> x0, local copies, waits for them, and re-layouts: 60.8 us -> none  [the longest x1 29.7 us: on_device(): send_images = padded_images[source].reshape(dom_count, capacity, columns)]
    ppermute x0 -> x27, starting transfers between devices: none -> 32.9 us  [the longest x19 24.5 us: across(): return lax.ppermute(value, 'dom', [(i, i ^ apart) for i in range(dom)])]
    psum x1 -> x0, waiting for transfers between devices: 31.6 us -> none  [on_device(): lax.psum(local_mass.astype(jnp.bfloat16), 'dom').astype(jnp.float32)]
  transfers between devices with their start and end apart: 5 -> 28, of which waited for: 3 -> 14; matrix products, arithmetic and copies ran while one was open for 25% -> 1% of each run, Pallas kernels for 0% -> 16%
where the time goes in v1:
time: 350 us; the launch traced here: 349 us
  waiting for transfers between devices  187 us (53%)
  Pallas kernels  102 us (29%)
  starting transfers between devices  37.5 us (11%)
  blocking collectives  9.66 us (3%)
  local copies, waits for them, and re-layouts  9.28 us (3%)
    ppermute x19, waiting for transfers between devices, across(): return lax.ppermute(value, 'dom', [(i, i ^ apart) for i in range(dom)])  81.3 us
    ppermute x3, waiting for transfers between devices, two_by_two(): lax.ppermute(share, 'rot', [(i, (i + 1) % turns) for i in range(turns)])  62.6 us
    all_to_all x1, waiting for transfers between devices, two_by_two(): recv = lax.all_to_all(packed, 'dom', 0, 0, tiled=True)  37.8 us
    pallas_call x4, Pallas kernels, score(): call(functools.partial(score_body, first, last), (2 * half,), in_specs, o...  37.2 us
    ppermute x19, starting transfers between devices, across(): return lax.ppermute(value, 'dom', [(i, i ^ apart) for i in range(dom)])  24.5 us
    pallas_call x3, Pallas kernels, class_sums_part(): call(functools.partial(class_body, kind), (steps,), in_specs, out_specs,...  22 us
    pallas_call x1, Pallas kernels, pack(): call(body, (steps,), [pl.BlockSpec((1, hold), lambda j, m: (0, 0)), pl.Bl...  10 us
    pallas_call x1, Pallas kernels, energy(): call(functools.partial(energy_body, bins, count), (count,), [pl.BlockSpec...  9.88 us
  transfers between devices with their start and end apart: 28, of which 14 were waited for; matrix products, arithmetic and copies ran while one was open for 1% of the time, Pallas kernels for 16%

profile of v1, /device:TPU:0, one launch (start us, length us, event | category | flops | bytes accessed | tf_op | source)
XLA Modules:
  0.0 348.5 jit_solution(13470045841679553303)
XLA Ops:
  0.7 0.7 broadcast_in_dim.10.bin_ref
  1.4 0.7 broadcast_in_dim.9.dest_ref
  2.1 0.1 stack.43.meta
  2.1 10.0 %shard_map.85 = (bf16[1536,1024]{1,0:T(8,128)(2,1)}, s32[1,1536]{1,0:T(1,128)S(1)}) custom-call(s32[10]{0:T(128)S(1)} %stack.43.meta, s32[1,1536]{1,0:T(1,128)S(1)} %broadcast_in_dim.9.dest_ref, s32[1,1536]{1,0:T(1,128)S(1)} %broadcast_in_dim.10.bin_ref, bf16[1536,4096]{1,0:T(8,128)(2,1)} %raw_ref.1), custom_call_target="tpu_custom_call" | custom-call | flops 4831838208 | bytes 6291456 | tf_op jit(solution)/shard_map/pallas_call | solution.py:106
  12.2 0.1 all_to_all.18
  12.3 9.7 %all_to_all.21 = s32[8,1,192]{2,1,0:T(1,128)S(1)} all-to-all(s32[8,1,192]{2,1,0:T(1,128)S(1)} %all_to_all.18), channel_id=1, replica_groups=mesh['dom'=8,'rot'=4] {'dom'}, dimensions={0} | all-to-all | bytes 12288 | tf_op jit(solution)/shard_map/all_to_all | solution.py:477
  21.9 4.6 %all-to-all-start.1 = ((bf16[8,192,1024]{2,1,0:T(8,128)(2,1)}), bf16[8,192,1024]{2,1,0:T(8,128)(2,1)}, u32[]{:S(2)}, u32[]{:S(2)}) async-start(bf16[8,192,1024]{2,1,0:T(8,128)(2,1)} %bitcast.10), calls=%async_computation.1 | async-start | bytes 6291456 | tf_op jit(solution)/shard_map/all_to_all | solution.py:478
  26.5 0.1 reshape.19.code_ref
  26.6 37.8 %all-to-all-done.1 = bf16[8,192,1024]{2,1,0:T(8,128)(2,1)} async-done(((bf16[8,192,1024]{2,1,0:T(8,128)(2,1)}), bf16[8,192,1024]{2,1,0:T(8,128)(2,1)}, u32[]{:S(2)}, u32[]{:S(2)}) %all-to-all-start.1) | async-done | bytes 3145760 | tf_op jit(solution)/shard_map/all_to_all | solution.py:478
  64.4 7.3 %shard_map.86 = (bf16[768,1024]{1,0:T(8,128)(2,1)S(1)}, bf16[192,768]{1,0:T(8,128)(2,1)S(1)}) custom-call(s32[10]{0:T(128)S(1)} %stack.43.meta, s32[1,1536]{1,0:T(1,128)S(1)} %reshape.19.code_ref, bf16[1536,1024]{1,0:T(8,128)(2,1)} %bitcast.11.recv_ref, f32[64,2048]{1,0:T(8,128)S(1)} %copy-done.4, f32[1,2048]{1,0:T(1,128)S(1)} %bitcast.13), custom_call_target="tpu_custom_call" | custom-call | flops 2415919104 | bytes 4718592 | tf_op jit(solution)/shard_map/pallas_call | solution.py:153
  71.7 1.6 collective-permute-start
  73.3 33.4 %collective-permute-done.own_ref = bf16[768,1024]{1,0:T(8,128)(2,1)S(1)} collective-permute-done((bf16[768,1024]{1,0:T(8,128)(2,1)S(1)}, bf16[768,1024]{1,0:T(8,128)(2,1)S(1)}, u32[]{:S(2)}, u32[]{:S(2)}) %collective-permute-start) | collective-permute-done | bytes 1572896 | tf_op jit(solution)/shard_map/ppermute | solution.py:500
  106.8 0.5 collective-permute-start.1
  107.3 1.6 constant_dynamic-slice_fusion
  108.8 0.1 collective-permute-start.4
  108.9 3.3 collective-permute-start.5
  112.2 29.1 %collective-permute-done.1.own_ref = bf16[768,1024]{1,0:T(8,128)(2,1)S(1)} collective-permute-done((bf16[768,1024]{1,0:T(8,128)(2,1)S(1)}, bf16[768,1024]{1,0:T(8,128)(2,1)S(1)}, u32[]{:S(2)}, u32[]{:S(2)}) %collective-permute-start.1) | collective-permute-done | bytes 1572896 | tf_op jit(solution)/shard_map/ppermute | solution.py:500
  141.3 0.2 collective-permute-start.2
  141.5 1.7 collective-permute-start.7
  143.2 0.3 collective-permute-start.8
  143.6 6.3 %collective-permute-start.6 = (bf16[720,512]{1,0:T(8,128)(2,1)S(1)}, bf16[720,512]{1,0:T(8,128)(2,1)S(1)}, u32[]{:S(2)}, u32[]{:S(2)}) collective-permute-start(bf16[720,512]{1,0:T(8,128)(2,1)S(1)} %collective-permute-done.4.refs_1_), channel_id=1, source_target_pairs={{0,8},{4,12},{8,0},{12,4},{16,24},{20,28},{24,16},{28,20},{1,9},{5... | collective-permute-start | bytes 2211848 | tf_op jit(solution)/shard_map/ppermute | solution.py:473
  149.9 0.1 collective-permute-start.9
  150.0 11.0 %collective-permute-done.7.refs_4_ = bf16[720,512]{1,0:T(8,128)(2,1)S(1)} collective-permute-done((bf16[720,512]{1,0:T(8,128)(2,1)S(1)}, bf16[720,512]{1,0:T(8,128)(2,1)S(1)}, u32[]{:S(2)}, u32[]{:S(2)}) %collective-permute-start.7) | collective-permute-done | bytes 737312 | tf_op jit(solution)/shard_map/ppermute | solution.py:473
  161.0 0.9 copy-done.8
  161.8 14.9 %collective-permute-done.8.refs_5_ = bf16[720,512]{1,0:T(8,128)(2,1)S(1)} collective-permute-done((bf16[720,512]{1,0:T(8,128)(2,1)S(1)}, bf16[720,512]{1,0:T(8,128)(2,1)S(1)}, u32[]{:S(2)}, u32[]{:S(2)}) %collective-permute-start.8) | collective-permute-done | bytes 737312 | tf_op jit(solution)/shard_map/ppermute | solution.py:473
  176.8 6.4 %collective-permute-start.10 = (bf16[720,512]{1,0:T(8,128)(2,1)S(1)}, bf16[720,512]{1,0:T(8,128)(2,1)}, u32[]{:S(2)}, u32[]{:S(2)}) collective-permute-start(bf16[720,512]{1,0:T(8,128)(2,1)S(1)} %collective-permute-done.8.refs_5_), channel_id=1, source_target_pairs={{0,8},{4,12},{8,0},{12,4},{16,24},{20,28},{24,16},{28,20},{1,9},{5... | collective-permute-start | bytes 2211848 | tf_op jit(solution)/shard_map/ppermute | solution.py:473
  183.2 4.3 %collective-permute-done.9.refs_6_ = bf16[720,512]{1,0:T(8,128)(2,1)S(1)} collective-permute-done((bf16[720,512]{1,0:T(8,128)(2,1)S(1)}, bf16[720,512]{1,0:T(8,128)(2,1)S(1)}, u32[]{:S(2)}, u32[]{:S(2)}) %collective-permute-start.9) | collective-permute-done | bytes 737312 | tf_op jit(solution)/shard_map/ppermute | solution.py:473
  187.5 0.5 collective-permute-start.3
  188.0 0.4 copy-done.10
  188.3 12.0 %collective-permute-done.10.refs_7_ = bf16[720,512]{1,0:T(8,128)(2,1)} collective-permute-done((bf16[720,512]{1,0:T(8,128)(2,1)S(1)}, bf16[720,512]{1,0:T(8,128)(2,1)}, u32[]{:S(2)}, u32[]{:S(2)}) %collective-permute-start.10) | collective-permute-done | bytes 737312 | tf_op jit(solution)/shard_map/ppermute | solution.py:473
  200.4 9.9 %shard_map.87 = (bf16[720,4096]{1,0:T(8,128)(2,1)}, bf16[720,192]{1,0:T(8,128)(2,1)S(1)}) custom-call(s32[10]{0:T(128)S(1)} %stack.43.meta, bf16[720,512]{1,0:T(8,128)(2,1)S(1)} %get-tuple-element.58.refs_0_, bf16[720,512]{1,0:T(8,128)(2,1)S(1)} %collective-permute-done.4.refs_1_, bf16[720,512]{1,0:T(8,128)(2,1)S(1)} %collective-permute-done.5.refs_2_, ...), custom_call_target="tpu_custom_call" | custom-call | flops 4529848320 | bytes 11796480 | tf_op jit(solution)/shard_map/pallas_call | solution.py:209
  210.3 7.9 %shard_map.88 = (f32[720,1536]{1,0:T(8,128)}, bf16[1536,4096]{1,0:T(8,128)(2,1)}) custom-call(s32[10]{0:T(128)S(1)} %stack.43.meta, bf16[768,1024]{1,0:T(8,128)(2,1)S(1)} %copy-done.3, bf16[768,1024]{1,0:T(8,128)(2,1)S(1)} %collective-permute-done.13.sib_ref, bf16[720,4096]{1,0:T(8,128)(2,1)} %get-tuple-element.30.panel_ref), custom_call_target="tpu_custom_call" | custom-call | flops 2264924160 | bytes 15138816 | tf_op jit(solution)/shard_map/pallas_call | solution.py:297
  218.2 9.1 %shard_map.89 = (f32[720,1536]{1,0:T(8,128)}, bf16[1536,4096]{1,0:T(8,128)(2,1)}) custom-call(s32[10]{0:T(128)S(1)} %stack.43.meta, bf16[768,1024]{1,0:T(8,128)(2,1)S(1)} %collective-permute-done.own_ref, bf16[768,1024]{1,0:T(8,128)(2,1)S(1)} %collective-permute-done.12.sib_ref, ...), custom_call_target="tpu_custom_call", output_to_operand_aliasing={{0}: (4, {}), {1}: (5, {})} | custom-call | flops 2264924160 | bytes 15138816 | tf_op jit(solution)/shard_map/pallas_call | solution.py:297
  227.3 9.7 %shard_map.90 = (f32[720,1536]{1,0:T(8,128)}, bf16[1536,4096]{1,0:T(8,128)(2,1)}) custom-call(s32[10]{0:T(128)S(1)} %stack.43.meta, bf16[768,1024]{1,0:T(8,128)(2,1)S(1)} %collective-permute-done.1.own_ref, bf16[768,1024]{1,0:T(8,128)(2,1)} %collective-permute-done.11.sib_ref, ...), custom_call_target="tpu_custom_call", output_to_operand_aliasing={{0}: (4, {}), {1}: (5, {})} | custom-call | flops 2264924160 | bytes 15138816 | tf_op jit(solution)/shard_map/pallas_call | solution.py:297
  237.0 10.5 %shard_map.91 = (f32[720,1536]{1,0:T(8,128)}, f32[8,1536]{1,0:T(8,128)S(1)}, bf16[1536,4096]{1,0:T(8,128)(2,1)}) custom-call(s32[10]{0:T(128)S(1)} %stack.43.meta, bf16[768,1024]{1,0:T(8,128)(2,1)S(1)} %collective-permute-done.2.own_ref, bf16[768,1024]{1,0:T(8,128)(2,1)} %collective-permute-done.3.sib_ref, ...), custom_call_target="tpu_custom_call", output_to_operand_aliasing={{0}: (4, {}), {2}: (5, {})} | custom-call | flops 2264924160 | bytes 15138816 | tf_op jit(solution)/shard_map/pallas_call | solution.py:297
  247.5 0.5 collective-permute-start.15
  248.0 0.9 collective-permute-done.15.other_ref
  248.9 0.6 shard_map.92.refs_2_
  249.5 0.1 collective-permute-start.16
  249.6 4.3 %collective-permute-start.17 = (f32[8,1536]{1,0:T(8,128)S(1)}, f32[8,1536]{1,0:T(8,128)S(1)}, u32[]{:S(2)}, u32[]{:S(2)}) collective-permute-start(f32[8,1536]{1,0:T(8,128)S(1)} %shard_map.92.refs_2_), channel_id=1, source_target_pairs={{0,2},{1,3},{2,0},{3,1},{4,6},{5,7},{6,4},{7,5},{8,10},{9,11},{10,... | collective-permute-start | bytes 147464 | tf_op jit(solution)/shard_map/ppermute | solution.py:504
  253.8 0.1 collective-permute-start.18
  253.9 3.1 collective-permute-done.17.refs_4_
  257.0 2.7 collective-permute-done.18.refs_5_
  259.7 6.4 %shard_map.93 = (bf16[720,1024]{1,0:T(8,128)(2,1)S(1)}, bf16[720,1536]{1,0:T(8,128)(2,1)S(1)}, f32[1,768]{1,0:T(1,128)S(1)}) custom-call(s32[10]{0:T(128)S(1)} %stack.43.meta, f32[720,1536]{1,0:T(8,128)} %get-tuple-element.39.refs_0_, f32[8,1536]{1,0:T(8,128)S(1)} %get-tuple-element.40.mine_ref.refs_1_, f32[8,1536]{1,0:T(8,128)S(1)} %shard_map.92.refs_2_, ...), custom_call_target="tpu_custom_call" | custom-call | flops 2264924160 | bytes 10518528 | tf_op jit(solution)/shard_map/pallas_call | solution.py:382
  266.1 1.3 copy-done
  267.4 6.5 %shard_map.95 = (bf16[720,1024]{1,0:T(8,128)(2,1)S(1)}, f32[64,720]{1,0:T(8,128)S(1)}) custom-call(s32[10]{0:T(128)S(1)} %stack.43.meta, bf16[720,1536]{1,0:T(8,128)(2,1)} %copy-done, bf16[192,768]{1,0:T(8,128)(2,1)S(1)} %get-tuple-element.37.refs_2_.refs_1_, bf16[192,768]{1,0:T(8,128)(2,1)S(1)} %collective-permute-done.14.refs_3_.refs_2_, ...), custom_call_target="tpu_custom_call" | custom-call | flops 2264924160 | bytes 10518528 | tf_op jit(solution)/shard_map/pallas_call | solution.py:382
  273.9 0.1 collective-permute-start.20
  274.0 1.8 collective-permute-start.19
  275.8 0.3 collective-permute-start.24
  276.1 9.2 %shard_map.94.first_ref.second_ref.y_ref.x_ref = f32[720,2048]{1,0:T(8,128)} custom-call(s32[10]{0:T(128)S(1)} %stack.43.meta, bf16[720,1536]{1,0:T(8,128)(2,1)S(1)} %copy-done.1, bf16[1536,4096]{1,0:T(8,128)(2,1)} %get-tuple-element.41.refs_6_.refs_1_.refs_3_), custom_call_target="tpu_custom_call" | custom-call | flops 4529848320 | bytes 16613376 | tf_op jit(solution)/shard_map/pallas_call | solution.py:382
  285.3 21.6 %collective-permute-done.20.left_ref = bf16[720,1024]{1,0:T(8,128)(2,1)S(1)} collective-permute-done((bf16[720,1024]{1,0:T(8,128)(2,1)S(1)}, bf16[720,1024]{1,0:T(8,128)(2,1)S(1)}, u32[]{:S(2)}, u32[]{:S(2)}) %collective-permute-start.20) | collective-permute-done | bytes 1474592 | tf_op jit(solution)/shard_map/ppermute | solution.py:473
  306.8 2.2 collective-permute-done.19.down_ref
  309.0 5.2 %shard_map.97 = (bf16[720,512]{1,0:T(8,128)(2,1)}, bf16[720,512]{1,0:T(8,128)(2,1)}) custom-call(s32[10]{0:T(128)S(1)} %stack.43.meta, f32[720,2048]{1,0:T(8,128)} %shard_map.94.first_ref.second_ref.y_ref.x_ref, f32[720,2048]{1,0:T(8,128)} %shard_map.94.first_ref.second_ref.y_ref.x_ref, bf16[720,1024]{1,0:T(8,128)(2,1)S(1)} %collective-permute-done.19.down_ref, ...), custom_call_target="tpu_custom_call" | custom-call | tf_op jit(solution)/shard_map/pallas_call | solution.py:407
  314.2 1.7 collective-permute-start.21
  315.9 5.0 %shard_map.96 = (f32[720,512]{1,0:T(8,128)S(1)}, bf16[720,512]{1,0:T(8,128)(2,1)}) custom-call(s32[10]{0:T(128)S(1)} %stack.43.meta, f32[720,2048]{1,0:T(8,128)} %shard_map.94.first_ref.second_ref.y_ref.x_ref, f32[720,2048]{1,0:T(8,128)} %shard_map.94.first_ref.second_ref.y_ref.x_ref, bf16[720,1024]{1,0:T(8,128)(2,1)S(1)} %collective-permute-done.19.down_ref, ...), custom_call_target="tpu_custom_call" | custom-call | tf_op jit(solution)/shard_map/pallas_call | solution.py:425
  320.8 0.5 collective-permute-start.22
  321.3 1.7 collective-permute-start.25
  323.1 13.9 %collective-permute-done.25 = f32[64,720]{1,0:T(8,128)S(1)} collective-permute-done((f32[64,720]{1,0:T(8,128)S(1)}, f32[64,720]{1,0:T(8,128)S(1)}, u32[]{:S(2)}, u32[]{:S(2)}) %collective-permute-start.25) | collective-permute-done | bytes 184352 | tf_op jit(solution)/shard_map/ppermute | solution.py:473
  337.0 0.9 collective-permute-start.26
  337.9 0.6 reduce.2
  338.5 0.5 collective-permute-done.26
  339.0 0.9 maximum_select_fusion
  339.9 5.2 %shard_map.98 = f32[512,1440]{1,0:T(8,128)} custom-call(s32[10]{0:T(128)S(1)} %stack.43.meta, f32[720,512]{1,0:T(8,128)S(1)} %get-tuple-element.45.keep_ref, bf16[720,512]{1,0:T(8,128)(2,1)S(1)} %collective-permute-done.21.a_ref, bf16[720,512]{1,0:T(8,128)(2,1)} %collective-permute-done.22.give_ref, bf16[720,512]{1,0:T(8,128)(2,1)S(1)} %collective-permute-done.23.b_ref), custom_call_target="tpu_custom_call" | custom-call | tf_op jit(solution)/shard_map/pallas_call | solution.py:449
  345.1 3.4 copy.17
  (42 shorter events, 0.2 us)
Async XLA Ops:
  21.9 42.5 %copy-start.4 = (f32[64,2048]{1,0:T(8,128)S(1)}, f32[64,2048]{1,0:T(8,128)}, u32[]{:S(2)}) copy-start(f32[64,2048]{1,0:T(8,128)} %refs_8_.1) | copy-start | bytes 1572868
  21.9 42.5 %copy-start.6 = (f32[2048]{0:T(1024)S(1)}, f32[2048]{0:T(1024)}, u32[]{:S(2)}) copy-start(f32[2048]{0:T(1024)} %param.10) | copy-start | bytes 24580
  21.9 42.5 %all-to-all-start.1 = ((bf16[8,192,1024]{2,1,0:T(8,128)(2,1)}), bf16[8,192,1024]{2,1,0:T(8,128)(2,1)}, u32[]{:S(2)}, u32[]{:S(2)}) async-start(bf16[8,192,1024]{2,1,0:T(8,128)(2,1)} %bitcast.10), calls=%async_computation.1 | async-start | bytes 6291456 | tf_op jit(solution)/shard_map/all_to_all | solution.py:478
  71.7 35.1 %copy-start.2 = (bf16[768,1024]{1,0:T(8,128)(2,1)}, bf16[768,1024]{1,0:T(8,128)(2,1)S(1)}, u32[]{:S(2)}) copy-start(bf16[768,1024]{1,0:T(8,128)(2,1)S(1)} %get-tuple-element.29.own_ref) | copy-start | bytes 4718596
  71.7 35.1 %collective-permute-start = (bf16[768,1024]{1,0:T(8,128)(2,1)S(1)}, bf16[768,1024]{1,0:T(8,128)(2,1)S(1)}, u32[]{:S(2)}, u32[]{:S(2)}) collective-permute-start(bf16[768,1024]{1,0:T(8,128)(2,1)S(1)} %get-tuple-element.29.own_ref), channel_id=1, source_target_pairs={{0,1},{1,2},{2,3},{3,0},{4,5},{5,6},{6,7},{7,4},{8,9},{9,10},{10,1... | collective-permute-start | bytes 4718600 | tf_op jit(solution)/shard_map/ppermute | solution.py:500
  106.8 34.6 %collective-permute-start.1 = (bf16[768,1024]{1,0:T(8,128)(2,1)S(1)}, bf16[768,1024]{1,0:T(8,128)(2,1)S(1)}, u32[]{:S(2)}, u32[]{:S(2)}) collective-permute-start(bf16[768,1024]{1,0:T(8,128)(2,1)S(1)} %collective-permute-done.own_ref), channel_id=1, source_target_pairs={{0,1},{1,2},{2,3},{3,0},{4,5},{5,6},{6,7},{7,4},{8,9},{9,10},{10,1... | collective-permute-start | bytes 4718600 | tf_op jit(solution)/shard_map/ppermute | solution.py:500
  107.3 53.7 %copy-start.3 = (bf16[768,1024]{1,0:T(8,128)(2,1)S(1)}, bf16[768,1024]{1,0:T(8,128)(2,1)}, u32[]{:S(2)}) copy-start(bf16[768,1024]{1,0:T(8,128)(2,1)} %copy-done.2) | copy-start | bytes 4718596
  107.3 93.1 %copy-start.5 = (f32[64,2048]{1,0:T(8,128)S(1)}, f32[64,2048]{1,0:T(8,128)}, u32[]{:S(2)}) copy-start(f32[64,2048]{1,0:T(8,128)} %refs_8_.1) | copy-start | bytes 1572868
  108.8 34.4 %collective-permute-start.4 = (bf16[720,512]{1,0:T(8,128)(2,1)S(1)}, bf16[720,512]{1,0:T(8,128)(2,1)S(1)}, u32[]{:S(2)}, u32[]{:S(2)}) collective-permute-start(bf16[720,512]{1,0:T(8,128)(2,1)S(1)} %get-tuple-element.57), channel_id=1, source_target_pairs={{0,4},{4,0},{8,12},{12,8},{16,20},{20,16},{24,28},{28,24},{1,5},{5... | collective-permute-start | bytes 2211848 | tf_op jit(solution)/shard_map/ppermute | solution.py:473
  108.9 41.0 %collective-permute-start.5 = (bf16[720,512]{1,0:T(8,128)(2,1)S(1)}, bf16[720,512]{1,0:T(8,128)(2,1)S(1)}, u32[]{:S(2)}, u32[]{:S(2)}) collective-permute-start(bf16[720,512]{1,0:T(8,128)(2,1)S(1)} %get-tuple-element.58.refs_0_), channel_id=1, source_target_pairs={{0,8},{4,12},{8,0},{12,4},{16,24},{20,28},{24,16},{28,20},{1,9},{5... | collective-permute-start | bytes 2211848 | tf_op jit(solution)/shard_map/ppermute | solution.py:473
  141.3 46.1 %collective-permute-start.2 = (bf16[768,1024]{1,0:T(8,128)(2,1)S(1)}, bf16[768,1024]{1,0:T(8,128)(2,1)S(1)}, u32[]{:S(2)}, u32[]{:S(2)}) collective-permute-start(bf16[768,1024]{1,0:T(8,128)(2,1)S(1)} %collective-permute-done.1.own_ref), channel_id=1, source_target_pairs={{0,1},{1,2},{2,3},{3,0},{4,5},{5,6},{6,7},{7,4},{8,9},{9,10},{10,1... | collective-permute-start | bytes 4718600 | tf_op jit(solution)/shard_map/ppermute | solution.py:500
  141.5 19.4 %collective-permute-start.7 = (bf16[720,512]{1,0:T(8,128)(2,1)S(1)}, bf16[720,512]{1,0:T(8,128)(2,1)S(1)}, u32[]{:S(2)}, u32[]{:S(2)}) collective-permute-start(bf16[720,512]{1,0:T(8,128)(2,1)S(1)} %get-tuple-element.58.refs_0_), channel_id=1, source_target_pairs={{0,16},{4,20},{8,24},{12,28},{16,0},{20,4},{24,8},{28,12},{1,17},{... | collective-permute-start | bytes 2211848 | tf_op jit(solution)/shard_map/ppermute | solution.py:473
  143.2 33.5 %collective-permute-start.8 = (bf16[720,512]{1,0:T(8,128)(2,1)S(1)}, bf16[720,512]{1,0:T(8,128)(2,1)S(1)}, u32[]{:S(2)}, u32[]{:S(2)}) collective-permute-start(bf16[720,512]{1,0:T(8,128)(2,1)S(1)} %collective-permute-done.4.refs_1_), channel_id=1, source_target_pairs={{0,16},{4,20},{8,24},{12,28},{16,0},{20,4},{24,8},{28,12},{1,17},{... | collective-permute-start | bytes 2211848 | tf_op jit(solution)/shard_map/ppermute | solution.py:473
  143.6 33.2 %collective-permute-start.6 = (bf16[720,512]{1,0:T(8,128)(2,1)S(1)}, bf16[720,512]{1,0:T(8,128)(2,1)S(1)}, u32[]{:S(2)}, u32[]{:S(2)}) collective-permute-start(bf16[720,512]{1,0:T(8,128)(2,1)S(1)} %collective-permute-done.4.refs_1_), channel_id=1, source_target_pairs={{0,8},{4,12},{8,0},{12,4},{16,24},{20,28},{24,16},{28,20},{1,9},{5... | collective-permute-start | bytes 2211848 | tf_op jit(solution)/shard_map/ppermute | solution.py:473
  149.9 37.6 %collective-permute-start.9 = (bf16[720,512]{1,0:T(8,128)(2,1)S(1)}, bf16[720,512]{1,0:T(8,128)(2,1)S(1)}, u32[]{:S(2)}, u32[]{:S(2)}) collective-permute-start(bf16[720,512]{1,0:T(8,128)(2,1)S(1)} %collective-permute-done.5.refs_2_), channel_id=1, source_target_pairs={{0,16},{4,20},{8,24},{12,28},{16,0},{20,4},{24,8},{28,12},{1,17},{... | collective-permute-start | bytes 2211848 | tf_op jit(solution)/shard_map/ppermute | solution.py:473
  161.0 0.9 copy-start.8
  161.0 49.3 %collective-permute-start.13 = (bf16[768,1024]{1,0:T(8,128)(2,1)S(1)}, bf16[768,1024]{1,0:T(8,128)(2,1)S(1)}, u32[]{:S(2)}, u32[]{:S(2)}) collective-permute-start(bf16[768,1024]{1,0:T(8,128)(2,1)S(1)} %copy-done.3), channel_id=1, source_target_pairs={{0,4},{4,0},{8,12},{12,8},{16,20},{20,16},{24,28},{28,24},{1,5},{5... | collective-permute-start | bytes 4718600 | tf_op jit(solution)/shard_map/ppermute | solution.py:473
  176.8 11.2 %copy-start.9 = (bf16[720,512]{1,0:T(8,128)(2,1)}, bf16[720,512]{1,0:T(8,128)(2,1)S(1)}, u32[]{:S(2)}) copy-start(bf16[720,512]{1,0:T(8,128)(2,1)S(1)} %collective-permute-done.8.refs_5_) | copy-start | bytes 2211844
  176.8 41.4 %collective-permute-start.12 = (bf16[768,1024]{1,0:T(8,128)(2,1)S(1)}, bf16[768,1024]{1,0:T(8,128)(2,1)S(1)}, u32[]{:S(2)}, u32[]{:S(2)}) collective-permute-start(bf16[768,1024]{1,0:T(8,128)(2,1)S(1)} %collective-permute-done.own_ref), channel_id=1, source_target_pairs={{0,4},{4,0},{8,12},{12,8},{16,20},{20,16},{24,28},{28,24},{1,5},{5... | collective-permute-start | bytes 4718600 | tf_op jit(solution)/shard_map/ppermute | solution.py:473
  176.8 23.6 %collective-permute-start.10 = (bf16[720,512]{1,0:T(8,128)(2,1)S(1)}, bf16[720,512]{1,0:T(8,128)(2,1)}, u32[]{:S(2)}, u32[]{:S(2)}) collective-permute-start(bf16[720,512]{1,0:T(8,128)(2,1)S(1)} %collective-permute-done.8.refs_5_), channel_id=1, source_target_pairs={{0,8},{4,12},{8,0},{12,4},{16,24},{20,28},{24,16},{28,20},{1,9},{5... | collective-permute-start | bytes 2211848 | tf_op jit(solution)/shard_map/ppermute | solution.py:473
  187.5 0.9 copy-start.10
  187.5 39.8 %collective-permute-start.11 = (bf16[768,1024]{1,0:T(8,128)(2,1)S(1)}, bf16[768,1024]{1,0:T(8,128)(2,1)}, u32[]{:S(2)}, u32[]{:S(2)}) collective-permute-start(bf16[768,1024]{1,0:T(8,128)(2,1)S(1)} %collective-permute-done.1.own_ref), channel_id=1, source_target_pairs={{0,4},{4,0},{8,12},{12,8},{16,20},{20,16},{24,28},{28,24},{1,5},{5... | collective-permute-start | bytes 4718600 | tf_op jit(solution)/shard_map/ppermute | solution.py:473
  187.5 49.6 %collective-permute-start.3 = (bf16[768,1024]{1,0:T(8,128)(2,1)S(1)}, bf16[768,1024]{1,0:T(8,128)(2,1)}, u32[]{:S(2)}, u32[]{:S(2)}) collective-permute-start(bf16[768,1024]{1,0:T(8,128)(2,1)S(1)} %collective-permute-done.2.own_ref), channel_id=1, source_target_pairs={{0,4},{4,0},{8,12},{12,8},{16,20},{20,16},{24,28},{28,24},{1,5},{5... | collective-permute-start | bytes 4718600 | tf_op jit(solution)/shard_map/ppermute | solution.py:473
  210.2 26.8 %collective-permute-start.14 = (bf16[192,768]{1,0:T(8,128)(2,1)S(1)}, bf16[192,768]{1,0:T(8,128)(2,1)S(1)}, u32[]{:S(2)}, u32[]{:S(2)}) collective-permute-start(bf16[192,768]{1,0:T(8,128)(2,1)S(1)} %get-tuple-element.37.refs_2_.refs_1_), channel_id=1, source_target_pairs={{0,4},{4,0},{8,12},{12,8},{16,20},{20,16},{24,28},{28,24},{1,5},{5... | collective-permute-start | bytes 884744 | tf_op jit(solution)/shard_map/ppermute | solution.py:473
  247.5 1.4 collective-permute-start.15
  249.5 4.5 %collective-permute-start.16 = (f32[8,1536]{1,0:T(8,128)S(1)}, f32[8,1536]{1,0:T(8,128)S(1)}, u32[]{:S(2)}, u32[]{:S(2)}) collective-permute-start(f32[8,1536]{1,0:T(8,128)S(1)} %shard_map.92.refs_2_), channel_id=1, source_target_pairs={{0,1},{1,0},{2,3},{3,2},{4,5},{5,4},{6,7},{7,6},{8,9},{9,8},{10,11... | collective-permute-start | bytes 147464 | tf_op jit(solution)/shard_map/ppermute | solution.py:504
  249.6 7.5 %collective-permute-start.17 = (f32[8,1536]{1,0:T(8,128)S(1)}, f32[8,1536]{1,0:T(8,128)S(1)}, u32[]{:S(2)}, u32[]{:S(2)}) collective-permute-start(f32[8,1536]{1,0:T(8,128)S(1)} %shard_map.92.refs_2_), channel_id=1, source_target_pairs={{0,2},{1,3},{2,0},{3,1},{4,6},{5,7},{6,4},{7,5},{8,10},{9,11},{10,... | collective-permute-start | bytes 147464 | tf_op jit(solution)/shard_map/ppermute | solution.py:504
  253.8 5.9 %collective-permute-start.18 = (f32[8,1536]{1,0:T(8,128)S(1)}, f32[8,1536]{1,0:T(8,128)S(1)}, u32[]{:S(2)}, u32[]{:S(2)}) collective-permute-start(f32[8,1536]{1,0:T(8,128)S(1)} %shard_map.92.refs_2_), channel_id=1, source_target_pairs={{0,3},{1,2},{2,1},{3,0},{4,7},{5,6},{6,5},{7,4},{8,11},{9,10},{10,... | collective-permute-start | bytes 147464 | tf_op jit(solution)/shard_map/ppermute | solution.py:504
  266.1 1.4 copy-start
  267.4 8.7 %copy-start.1 = (bf16[720,1536]{1,0:T(8,128)(2,1)S(1)}, bf16[720,1536]{1,0:T(8,128)(2,1)}, u32[]{:S(2)}) copy-start(bf16[720,1536]{1,0:T(8,128)(2,1)} %copy-done) | copy-start | bytes 6635524
  273.9 32.9 %collective-permute-start.20 = (bf16[720,1024]{1,0:T(8,128)(2,1)S(1)}, bf16[720,1024]{1,0:T(8,128)(2,1)S(1)}, u32[]{:S(2)}, u32[]{:S(2)}) collective-permute-start(bf16[720,1024]{1,0:T(8,128)(2,1)S(1)} %get-tuple-element.44), channel_id=1, source_target_pairs={{0,16},{4,20},{8,24},{12,28},{16,0},{20,4},{24,8},{28,12},{1,17},{... | collective-permute-start | bytes 4423688 | tf_op jit(solution)/shard_map/ppermute | solution.py:473
  274.0 35.0 %collective-permute-start.19 = (bf16[720,1024]{1,0:T(8,128)(2,1)S(1)}, bf16[720,1024]{1,0:T(8,128)(2,1)S(1)}, u32[]{:S(2)}, u32[]{:S(2)}) collective-permute-start(bf16[720,1024]{1,0:T(8,128)(2,1)S(1)} %get-tuple-element.43), channel_id=1, source_target_pairs={{0,8},{4,12},{8,0},{12,4},{16,24},{20,28},{24,16},{28,20},{1,9},{5... | collective-permute-start | bytes 4423688 | tf_op jit(solution)/shard_map/ppermute | solution.py:473
  275.8 45.5 %collective-permute-start.24 = (f32[64,720]{1,0:T(8,128)S(1)}, f32[64,720]{1,0:T(8,128)S(1)}, u32[]{:S(2)}, u32[]{:S(2)}) collective-permute-start(f32[64,720]{1,0:T(8,128)S(1)} %get-tuple-element.49), channel_id=1, source_target_pairs={{0,8},{4,12},{8,0},{12,4},{16,24},{20,28},{24,16},{28,20},{1,9},{5... | collective-permute-start | bytes 552968 | tf_op jit(solution)/shard_map/ppermute | solution.py:473
  306.8 2.2 copy-start.7
  314.2 25.7 %collective-permute-start.21 = (bf16[720,512]{1,0:T(8,128)(2,1)}, bf16[720,512]{1,0:T(8,128)(2,1)S(1)}, u32[]{:S(2)}, u32[]{:S(2)}) collective-permute-start(bf16[720,512]{1,0:T(8,128)(2,1)} %get-tuple-element.46), channel_id=1, source_target_pairs={{0,16},{4,12},{8,24},{12,4},{16,0},{20,28},{24,8},{28,20},{1,17},{... | collective-permute-start | bytes 2211848 | tf_op jit(solution)/shard_map/ppermute | solution.py:522
  315.9 24.1 %collective-permute-start.23 = (bf16[720,512]{1,0:T(8,128)(2,1)}, bf16[720,512]{1,0:T(8,128)(2,1)S(1)}, u32[]{:S(2)}, u32[]{:S(2)}) collective-permute-start(bf16[720,512]{1,0:T(8,128)(2,1)} %get-tuple-element.48), channel_id=1, source_target_pairs={{0,12},{4,16},{8,4},{12,24},{16,28},{20,0},{24,20},{28,8},{1,13},{... | collective-permute-start | bytes 2211848 | tf_op jit(solution)/shard_map/ppermute | solution.py:523
  320.8 19.1 %collective-permute-start.22 = (bf16[720,512]{1,0:T(8,128)(2,1)}, bf16[720,512]{1,0:T(8,128)(2,1)}, u32[]{:S(2)}, u32[]{:S(2)}) collective-permute-start(bf16[720,512]{1,0:T(8,128)(2,1)} %get-tuple-element.47), channel_id=1, source_target_pairs={{0,4},{4,0},{8,12},{12,8},{16,20},{20,16},{24,28},{28,24},{1,5},{5... | collective-permute-start | bytes 2211848 | tf_op jit(solution)/shard_map/ppermute | solution.py:473
  321.3 15.6 %collective-permute-start.25 = (f32[64,720]{1,0:T(8,128)S(1)}, f32[64,720]{1,0:T(8,128)S(1)}, u32[]{:S(2)}, u32[]{:S(2)}) collective-permute-start(f32[64,720]{1,0:T(8,128)S(1)} %add.36), channel_id=1, source_target_pairs={{0,16},{4,20},{8,24},{12,28},{16,0},{20,4},{24,8},{28,12},{1,17},{... | collective-permute-start | bytes 552968 | tf_op jit(solution)/shard_map/ppermute | solution.py:473
  337.0 2.0 collective-permute-start.26

commit v2 on v1

v2 whole, which is shorter than its diff:
```python
import functools

import jax
import jax.numpy as jnp
from jax import lax
from jax.experimental import pallas as pl
from jax.experimental.pallas import tpu as pltpu
from jax.sharding import PartitionSpec as P

NN = (((1,), (0,)), ((), ()))
NT = (((1,), (1,)), ((), ()))
F32, BF16, I32 = jnp.float32, jnp.bfloat16, jnp.int32
CODE = 128
VMEM_BYTES = 50 * 1024 * 1024


def mm(a, b, dims):
    return lax.dot_general(a, b, dims, preferred_element_type=F32)


def split3(x):
    hi = x.astype(BF16)
    rest = x - hi.astype(F32)
    mid = rest.astype(BF16)
    low = (rest - mid.astype(F32)).astype(BF16)
    return hi, mid, low


def call(body, grid, in_specs, out_specs, out_shape, scratch=(), alias=None, flops=0, moved=0):
    return pl.pallas_call(
        body,
        grid_spec=pltpu.PrefetchScalarGridSpec(
            num_scalar_prefetch=1,
            grid=grid,
            in_specs=in_specs,
            out_specs=out_specs,
            scratch_shapes=list(scratch),
        ),
        out_shape=out_shape,
        input_output_aliases=alias or {},
        compiler_params=pltpu.CompilerParams(vmem_limit_bytes=VMEM_BYTES),
        cost_estimate=pl.CostEstimate(flops=flops, bytes_accessed=moved, transcendentals=0),
    )


def sds(shape, dtype):
    return jax.ShapeDtypeStruct(shape, dtype)


def one_hot_rows(out_ref, wanted):
    rows, width = out_ref.shape
    step = 256 if rows % 256 == 0 else rows
    for start in range(0, rows, step):
        index = lax.broadcasted_iota(I32, (step, width), 0) + start
        out_ref[start : start + step, :] = jnp.where(index == wanted, 1.0, 0.0).astype(BF16)


def places_of(dest, shard_rows, cap, dom):
    hold = dest.shape[1]
    low = lax.broadcasted_iota(I32, (dom, hold), 0) * shard_rows
    inside = jnp.logical_and(dest >= low, dest < low + shard_rows)
    marks = jnp.where(inside, 1.0, 0.0)
    local = dest - jnp.sum(jnp.where(inside, low, 0), axis=0, keepdims=True)
    lanes = 128
    before = lax.broadcasted_iota(I32, (lanes, lanes), 0) < lax.broadcasted_iota(
        I32, (lanes, lanes), 1
    )
    upper = jnp.where(before, 1.0, 0.0).astype(BF16)
    carry = lax.broadcasted_iota(I32, (dom, 1), 0).astype(F32) * cap + 1.0
    found = []
    for start in range(0, hold, lanes):
        part = marks[:, start : start + lanes]
        rank = mm(part.astype(BF16), upper, NN) + carry
        found.append(jnp.sum(jnp.where(part > 0, rank, 0.0), axis=0, keepdims=True))
        carry = carry + jnp.sum(part, axis=1, keepdims=True)
    return jnp.concatenate(found, axis=1).astype(I32) - 1, local


def pack_first_body(dom, shard_rows, cap, meta, dest_ref, bin_ref, raw_ref, out_ref, place_ref, pick):
    dest = dest_ref[...]
    place, local = places_of(dest, shard_rows, cap, dom)
    place_ref[...] = place
    one_hot_rows(pick, place)
    which = lax.broadcasted_iota(I32, (CODE, dest.shape[1]), 0)
    digits = jnp.where(
        which == 0,
        local >> 4,
        jnp.where(which == 1, local & 15, jnp.where(which == 2, bin_ref[...], jnp.where(which == 3, 1, 0))),
    )
    digits = jnp.where(dest >= 0, digits, 0).astype(F32).astype(BF16)
    out_ref[:, :CODE] = mm(pick[...], digits, NT).astype(BF16)
    out_ref[:, CODE:] = mm(pick[...], raw_ref[...], NN).astype(BF16)


def pack_next_body(meta, place_ref, raw_ref, out_ref, pick):
    one_hot_rows(pick, place_ref[...])
    out_ref[...] = mm(pick[...], raw_ref[...], NN).astype(BF16)


def pack_first(meta, raw_images, dest, bins, dom, width, at):
    hold, _ = raw_images.shape
    cap = hold // dom
    slots = dom * cap
    row = pl.BlockSpec((1, hold), lambda j, m: (0, 0))
    return call(
        functools.partial(pack_first_body, dom, hold // 2, cap),
        (1,),
        [row, row, pl.BlockSpec((hold, width), lambda j, m: (0, at(m)))],
        [pl.BlockSpec((slots, CODE + width), lambda j, m: (0, 0)), row],
        [sds((slots, CODE + width), BF16), sds((1, hold), I32)],
        scratch=[pltpu.VMEM((slots, hold), BF16)],
        flops=2 * slots * hold * width,
        moved=4 * hold * width,
    )(meta, dest, bins, raw_images)


def pack_next(meta, raw_images, place, dom, width, at):
    hold, _ = raw_images.shape
    slots = dom * (hold // dom)
    return call(
        pack_next_body,
        (1,),
        [
            pl.BlockSpec((1, hold), lambda j, m: (0, 0)),
            pl.BlockSpec((hold, width), lambda j, m: (0, at(m))),
        ],
        pl.BlockSpec((slots, width), lambda j, m: (0, 0)),
        sds((slots, width), BF16),
        scratch=[pltpu.VMEM((slots, hold), BF16)],
        flops=2 * slots * hold * width,
        moved=4 * hold * width,
    )(meta, place, raw_images)


def weigh(pick, wide, recv, ctf_ref, inv_ref, out_ref):
    table = jnp.concatenate(split3(ctf_ref[...] * inv_ref[...]), axis=0)
    factor = mm(wide, table, NN)
    out_ref[...] = (mm(pick, recv, NN) * factor).astype(BF16)


def unpack_first_body(bins, meta, recv_ref, ctf_ref, inv_ref, out_ref, hot_ref, pick, wide):
    shard_rows = out_ref.shape[0]
    chosen = jnp.where(
        lax.broadcasted_iota(I32, (8, CODE), 0) == lax.broadcasted_iota(I32, (8, CODE), 1), 1.0, 0.0
    ).astype(BF16)
    got = mm(chosen, recv_ref[:, :CODE], NT)
    row = got[0:1] * 16.0 + got[1:2] + got[3:4] * 1024.0 - 1024.0
    one_hot_rows(pick, row.astype(I32))
    slot_bins = jnp.broadcast_to(got[2:3].astype(BF16), (8, got.shape[1]))
    down = mm(pick[...], slot_bins, NT)[:, 0:1].astype(I32)
    across = mm(slot_bins, pick[...], NT)[0:1].astype(I32)
    lane = lax.broadcasted_iota(I32, (shard_rows, 3 * bins), 1)
    wide[...] = jnp.where((lane & (bins - 1)) == down, 1.0, 0.0).astype(BF16)
    deep = lax.broadcasted_iota(I32, (3 * bins, shard_rows), 0)
    hot_ref[...] = jnp.where((deep & (bins - 1)) == across, 1.0, 0.0).astype(BF16)
    weigh(pick[...], wide[...], recv_ref[:, CODE:], ctf_ref, inv_ref, out_ref)


def unpack_next_body(meta, pick_ref, wide_ref, recv_ref, ctf_ref, inv_ref, out_ref):
    weigh(pick_ref[...], wide_ref[...], recv_ref[...], ctf_ref, inv_ref, out_ref)


def unpack_first(meta, recv, ctf, inv, at):
    slots, columns = recv.shape
    width = columns - CODE
    rows = slots // 2
    bins, pix = ctf.shape
    wrap = pix // width
    whole = lambda shape: pl.BlockSpec(shape, lambda j, m: (0, 0))
    shapes = [(rows, width), (3 * bins, rows), (rows, slots), (rows, 3 * bins)]
    return call(
        functools.partial(unpack_first_body, bins),
        (1,),
        [
            whole(recv.shape),
            pl.BlockSpec((bins, width), lambda j, m: (0, lax.rem(at(m), wrap))),
            pl.BlockSpec((1, width), lambda j, m: (0, lax.rem(at(m), wrap))),
        ],
        [whole(s) for s in shapes],
        [sds(s, BF16) for s in shapes],
        flops=2 * slots * rows * width,
        moved=2 * slots * columns,
    )(meta, recv, ctf, inv)


def unpack_next(meta, pick, wide, recv, ctf, inv, at):
    slots, width = recv.shape
    rows = slots // 2
    bins, pix = ctf.shape
    wrap = pix // width
    whole = lambda shape: pl.BlockSpec(shape, lambda j, m: (0, 0))
    return call(
        unpack_next_body,
        (1,),
        [
            whole(pick.shape),
            whole(wide.shape),
            whole(recv.shape),
            pl.BlockSpec((bins, width), lambda j, m: (0, lax.rem(at(m), wrap))),
            pl.BlockSpec((1, width), lambda j, m: (0, lax.rem(at(m), wrap))),
        ],
        whole((rows, width)),
        sds((rows, width), BF16),
        flops=2 * slots * rows * width,
        moved=2 * slots * width,
    )(meta, pick, wide, recv, ctf, inv)


def energy_body(bins, count, meta, *refs):
    pieces, (ctf_ref, inv_ref, panel_ref, extra_ref, total) = refs[:count], refs[count:]
    step = pl.program_id(0)

    @pl.when(step == 0)
    def _():
        total[...] = jnp.zeros_like(total)

    gain = ctf_ref[...] * ctf_ref[...] * inv_ref[...]
    gain3 = jnp.concatenate(split3(gain), axis=0)
    for index, piece in enumerate(pieces):

        @pl.when(step == index)
        def _():
            panel = piece[...]
            panel_ref[...] = panel
            wide = panel.astype(F32)
            square = wide * wide
            high = square.astype(BF16)
            low = (square - high.astype(F32)).astype(BF16)
            total[...] += mm(high, gain3, NT) + mm(low, gain3, NT)

    @pl.when(step == count - 1)
    def _():
        whole = total[:, :bins] + total[:, bins : 2 * bins] + total[:, 2 * bins :]
        extra_ref[...] = jnp.concatenate(split3(-0.5 * whole), axis=1)


def energy(meta, pieces, ctf, inv):
    count = len(pieces)
    rows, width = pieces[0].shape
    bins, pix = ctf.shape
    wrap = pix // width
    return call(
        functools.partial(energy_body, bins, count),
        (count,),
        [pl.BlockSpec((rows, width), lambda j, m: (0, 0))] * count
        + [
            pl.BlockSpec((bins, width), lambda j, m: (0, lax.rem(m[0] ^ j, wrap))),
            pl.BlockSpec((1, width), lambda j, m: (0, lax.rem(m[0] ^ j, wrap))),
        ],
        [
            pl.BlockSpec((rows, width), lambda j, m: (0, m[0] ^ j)),
            pl.BlockSpec((rows, 3 * bins), lambda j, m: (0, 0)),
        ],
        [sds((rows, count * width), BF16), sds((rows, 3 * bins), BF16)],
        scratch=[pltpu.VMEM((rows, 3 * bins), F32)],
        flops=2 * 4 * rows * bins * count * width * 3,
        moved=4 * rows * count * width,
    )(meta, *pieces, ctf, inv)


def score_body(first, last, meta, *refs):
    own, sib, panel_ref, refs = refs[:2], refs[2:4], refs[4], refs[5:]
    if first:
        acc_out, full_ref = refs
    elif last:
        acc_ref, _, hot_own, hot_sib, extra_ref, shifted_ref, stat_ref, full_ref = refs
    else:
        acc_ref, _, acc_out, full_ref = refs
    half = pl.num_programs(0) // 2

    def tile(sources, hot):
        block = jnp.concatenate([source[...] for source in sources], axis=1)
        full_ref[...] = block
        total = mm(panel_ref[...], block, NT)
        if not first:
            total = acc_ref[...] + total
        if not last:
            acc_out[...] = total
            return
        total = total + mm(extra_ref[...], hot[...], NN)
        peak = jnp.max(total, axis=0, keepdims=True)
        shifted = jnp.exp(total - peak)
        shifted_ref[...] = shifted
        mass = jnp.sum(shifted, axis=0, keepdims=True)
        which = lax.broadcasted_iota(I32, stat_ref.shape, 0)
        stat_ref[...] = jnp.where(which == 0, peak, mass)

    @pl.when(pl.program_id(0) < half)
    def _():
        tile(own, hot_own if last else None)

    @pl.when(pl.program_id(0) >= half)
    def _():
        tile(sib, hot_sib if last else None)


def score(meta, turn, turns, own, sib, panels, acc, full, hots=None, extra=None):
    rows, part = own[0].shape
    width = len(own) * part
    tile = 256
    half = rows // tile
    count = panels.shape[0]
    first, last = turn == 0, turn == turns - 1

    def share(m):
        return lax.rem(m[1] + turns - turn, turns)

    front = pl.BlockSpec((tile, part), lambda j, m: (jnp.minimum(j, half - 1), 0))
    back = pl.BlockSpec((tile, part), lambda j, m: (jnp.maximum(j - half, 0), 0))
    acc_spec = pl.BlockSpec((count, tile), lambda j, m: (0, j))
    full_spec = pl.BlockSpec((tile, width), lambda j, m: (j, share(m)))
    in_specs = [front, front, back, back]
    in_specs += [pl.BlockSpec((count, width), lambda j, m: (0, share(m)))]
    operands = [meta, *own, *sib, panels]
    alias = {}
    if not first:
        in_specs += [acc_spec, pl.BlockSpec(memory_space=pl.ANY)]
        operands += [acc, full]
        alias = {6: 0, 7: 2 if last else 1}
    out_specs = [acc_spec, full_spec]
    full_shape = sds((2 * rows, width * turns), BF16)
    out_shape = [sds((count, 2 * rows), F32), full_shape]
    if last:
        depth = extra.shape[1]
        in_specs += [
            pl.BlockSpec((depth, tile), lambda j, m: (0, jnp.minimum(j, half - 1))),
            pl.BlockSpec((depth, tile), lambda j, m: (0, jnp.maximum(j - half, 0))),
            pl.BlockSpec((count, depth), lambda j, m: (0, 0)),
        ]
        operands += [*hots, extra]
        out_specs = [acc_spec, pl.BlockSpec((8, tile), lambda j, m: (0, j)), full_spec]
        out_shape = [out_shape[0], sds((8, 2 * rows), F32), full_shape]
    return call(
        functools.partial(score_body, first, last),
        (2 * half,),
        in_specs,
        out_specs,
        out_shape,
        alias=alias,
        flops=2 * count * 2 * rows * width,
        moved=8 * count * 2 * rows + 8 * rows * width,
    )(*operands)


def merge_body(meta, mine_ref, other_ref, out_ref):
    rows = mine_ref.shape[1] // 2
    other = other_ref[...]
    other = jnp.concatenate([other[:, rows:], other[:, :rows]], axis=1)
    mine = mine_ref[...]
    peak = jnp.maximum(mine[0:1], other[0:1])
    mass = mine[1:2] * jnp.exp(mine[0:1] - peak) + other[1:2] * jnp.exp(other[0:1] - peak)
    which = lax.broadcasted_iota(I32, out_ref.shape, 0)
    out_ref[...] = jnp.where(which == 0, peak, mass)


def merge(meta, mine, other):
    spec = pl.BlockSpec(mine.shape, lambda j, m: (0, 0))
    return call(merge_body, (1,), [spec, spec], spec, sds(mine.shape, F32))(meta, mine, other)


def class_body(kind, steps, meta, *refs):
    if kind == "first":
        (shifted_ref, stat_ref), four, full_ref = refs[:2], refs[2:6], refs[6]
        outs, (post_ref, log_ref) = refs[7 : 7 + steps], refs[7 + steps :]

        @pl.when(pl.program_id(0) == 0)
        def _():
            stats = [ref[...] for ref in four]
            peaks = [s[0:1] for s in stats]
            peak = jnp.maximum(jnp.maximum(peaks[0], peaks[1]), jnp.maximum(peaks[2], peaks[3]))
            parts = [s[1:2] * jnp.exp(p - peak) for s, p in zip(stats, peaks)]
            mass = (parts[0] + parts[1]) + (parts[2] + parts[3])
            factor = jnp.exp(stat_ref[0:1] - peak) / mass
            post_ref[...] = (shifted_ref[...] * factor).astype(BF16)
            log_ref[...] = (peak + jnp.log(mass))[:, : log_ref.shape[1]]

    elif kind == "mass":
        post_ref, hot_own, hot_sib, full_ref = refs[:4]
        outs, mass_ref = refs[4 : 4 + steps], refs[4 + steps]
        bins, _ = mass_ref.shape
        rows = hot_own.shape[1]

        @pl.when(pl.program_id(0) == 0)
        def _():
            mass_ref[...] = mm(hot_own[:bins, :], post_ref[:, :rows], NT) + mm(
                hot_sib[:bins, :], post_ref[:, rows:], NT
            )

    else:
        (post_ref, full_ref), outs = refs[:2], refs[2:]
    for step, out_ref in enumerate(outs):

        @pl.when(pl.program_id(0) == step)
        def _():
            out_ref[...] = mm(post_ref[...], full_ref[...], NN).astype(out_ref.dtype)


def class_part(meta, kind, offset, steps, full, post=None, shifted=None, stats=None, hots=None, bins=0):
    rows, columns = full.shape
    width = columns // 8
    count = (shifted if post is None else post).shape[0]
    whole = lambda shape: pl.BlockSpec(shape, lambda j, m: (0, 0))
    full_spec = pl.BlockSpec((rows, width), lambda j, m: (0, m[offset + j]))
    out_specs = [whole((count, width))] * steps
    out_shape = [sds((count, width), F32 if kind == "rest" else BF16)] * steps
    if kind == "first":
        operands = [shifted, *stats, full]
        in_specs = [whole(shifted.shape)] + [whole(stats[0].shape)] * 5 + [full_spec]
        out_specs += [whole((count, rows)), whole((1, rows // 2))]
        out_shape += [sds((count, rows), BF16), sds((1, rows // 2), F32)]
    elif kind == "mass":
        operands = [post, *hots, full]
        in_specs = [whole(post.shape), whole(hots[0].shape), whole(hots[1].shape), full_spec]
        out_specs += [whole((bins, count))]
        out_shape += [sds((bins, count), F32)]
    else:
        operands = [post, full]
        in_specs = [whole(post.shape), full_spec]
    return call(
        functools.partial(class_body, kind, steps),
        (steps,),
        in_specs,
        out_specs,
        out_shape,
        flops=2 * count * rows * width * steps,
        moved=2 * rows * width * steps + 4 * count * (rows + width * steps),
    )(meta, *operands)


def forward_body(meta, a_sum, b_sum, down_ref, left_ref, a_ref, b_ref):
    even = meta[0] % 2 == 0
    down, left = down_ref[...].astype(F32), left_ref[...].astype(F32)
    a_ref[...] = (a_sum[...] + jnp.where(even, down, left)).astype(BF16)
    b_ref[...] = (b_sum[...] + jnp.where(even, left, down)).astype(BF16)


def forward(meta, a_sum, b_sum, got_x, got_y):
    shape = a_sum.shape
    spec = pl.BlockSpec((shape[0] // 5, shape[1]), lambda j, m: (j, 0))
    return call(forward_body, (5,), [spec] * 4, [spec] * 2, [sds(shape, BF16)] * 2)(
        meta, a_sum, b_sum, got_x, got_y
    )


def finish_body(meta, keep_ref, a_ref, c_ref, other_ref, b_ref, d_ref, out_ref):
    half = pl.num_programs(0) // 2
    wide = lambda ref: ref[...].astype(F32)

    @pl.when(pl.program_id(0) < half)
    def _():
        out_ref[...] = keep_ref[...] + wide(c_ref) + wide(a_ref)

    @pl.when(pl.program_id(0) >= half)
    def _():
        out_ref[...] = wide(other_ref) + wide(d_ref) + wide(b_ref)


def finish(meta, keep, got_a, got_c, got_self, got_b, got_d):
    count, width = keep.shape
    half = 5
    tile = count // half
    front = pl.BlockSpec((tile, width), lambda j, m: (jnp.minimum(j, half - 1), 0))
    back = pl.BlockSpec((tile, width), lambda j, m: (jnp.maximum(j - half, 0), 0))

    def place(j, m):
        core = lax.rem(m[0], 2)
        return jnp.where(j < half, core * half + j, (1 - core) * half + j - half), 0

    return call(
        finish_body,
        (2 * half,),
        [front] * 3 + [back] * 3,
        pl.BlockSpec((tile, width), place),
        sds((2 * count, width), F32),
    )(meta, keep, got_a, got_c, got_self, got_b, got_d)


def two_by_two(raw_images, defocus_bin, dest_row, ctf_table, inv_noise, panels):
    dom, turns = lax.axis_size("dom"), lax.axis_size("rot")
    device, plane = lax.axis_index("dom"), lax.axis_index("rot")
    bins = ctf_table.shape[0]
    columns = raw_images.shape[1]
    chip, core = device // 2, device % 2

    def block(apart, half):
        return (chip ^ apart) * 2 + half

    x_first, y_second = block(1, 0), block(2, 1)
    x_second, y_first = block(1, 1), block(2, 0)
    even = core == 0
    order = [
        device,
        plane,
        block(3, 0),
        block(3, 1),
        jnp.where(even, x_first, y_second),
        jnp.where(even, y_second, x_first),
        block(0, 1 - core),
        jnp.where(even, y_first, x_second),
        jnp.where(even, x_second, y_first),
        block(0, core),
    ]
    meta = jnp.stack(order).astype(I32)
    inv = inv_noise[None, :]

    def across(value, apart):
        return lax.ppermute(value, "dom", [(i, i ^ apart) for i in range(dom)])

    def by_core(value, when_even, when_odd):
        pairs = [(i, i ^ (when_odd if i % 2 else when_even)) for i in range(dom)]
        return lax.ppermute(value, "dom", pairs)

    def onward(value):
        return lax.ppermute(value, "rot", [(i, (i + 1) % turns) for i in range(turns)])

    width = columns // turns // 2
    dest, bin_row = dest_row[None, :], defocus_bin[None, :]
    send_a, place = pack_first(meta, raw_images, dest, bin_row, dom, width, lambda m: 2 * m[1])
    recv_a = lax.all_to_all(send_a, "dom", 0, 0, tiled=True)
    send_b = pack_next(meta, raw_images, place, dom, width, lambda m: 2 * m[1] + 1)
    recv_b = lax.all_to_all(send_b, "dom", 0, 0, tiled=True)

    count = panels.shape[0] // 2
    pieces = [None] * 8
    pieces[0] = lax.dynamic_slice_in_dim(panels, core * count, count, 0)
    pieces[1] = across(lax.dynamic_slice_in_dim(panels, (1 - core) * count, count, 0), 1)
    pieces[2], pieces[4] = across(pieces[0], 2), across(pieces[0], 4)
    pieces[3], pieces[5] = across(pieces[1], 2), across(pieces[1], 4)

    share_a, hot, pick, wide = unpack_first(meta, recv_a, ctf_table, inv, lambda m: 2 * m[1])
    share_b = unpack_next(meta, pick, wide, recv_b, ctf_table, inv, lambda m: 2 * m[1] + 1)
    hots = (hot, across(hot, 1))
    a1, b1 = onward(share_a), onward(share_b)
    a1, *pieces[2:6] = lax.optimization_barrier((a1, *pieces[2:6]))
    pieces[6], pieces[7] = across(pieces[2], 4), across(pieces[5], 2)
    a2, b2 = onward(a1), onward(b1)
    a2, *pieces[6:8] = lax.optimization_barrier((a2, *pieces[6:8]))
    panel_full, extra = energy(meta, pieces, ctf_table, inv)
    a3, b3 = onward(a2), onward(b2)

    own = [(share_a, share_b), (a1, b1), (a2, b2), (a3, b3)]
    acc = full = None
    for turn in range(turns - 1):
        sib = [across(value, 1) for value in own[turn]]
        acc, full = score(meta, turn, turns, own[turn], sib, panel_full, acc, full)
    sib = [across(value, 1) for value in own[-1]]
    shifted, stat, full = score(
        meta, turns - 1, turns, own[-1], sib, panel_full, acc, full, hots, extra
    )

    pair = merge(meta, stat, across(stat, 1))
    others = [
        lax.ppermute(pair, "rot", [(i, i ^ apart) for i in range(turns)]) for apart in (1, 2, 3)
    ]
    to_x, to_y, post, log_evidence = class_part(
        meta, "first", 2, 2, full, shifted=shifted, stats=[stat, pair, *others]
    )
    got_x, got_y = across(to_x, 2), across(to_y, 4)
    send_c, send_d, give, mass = class_part(
        meta, "mass", 4, 3, full, post=post, hots=hots, bins=bins
    )
    a_sum, b_sum, keep = class_part(meta, "rest", 7, 3, full, post=post)
    got_x, got_y, send_c, send_d = lax.optimization_barrier((got_x, got_y, send_c, send_d))
    got_c, got_d = by_core(send_c, 2, 4), by_core(send_d, 5, 3)
    message_a, message_b = forward(meta, a_sum, b_sum, got_x, got_y)
    got_a, got_b = by_core(message_a, 4, 2), by_core(message_b, 3, 5)
    got_self = across(give, 1)
    mass = mass + across(mass, 2)
    mass = mass + across(mass, 4)
    mass_other = across(mass, 1)
    bin_weights = jnp.where(
        even,
        jnp.concatenate([mass, mass_other], axis=1),
        jnp.concatenate([mass_other, mass], axis=1),
    )
    class_sums = finish(meta, keep, got_a, got_c, got_self, got_b, got_d).T
    return class_sums, bin_weights, log_evidence.reshape(-1)


def energy_block(gain_block, panel_piece):
    widened = panel_piece.astype(jnp.float32)
    return lax.dot_general(
        gain_block, widened * widened, (((1,), (1,)), ((), ())), precision=lax.Precision.HIGHEST
    )


def on_device(raw_images, defocus_bin, dest_row, ctf_table, inv_noise, panels):
    dom_count = lax.axis_size("dom")
    bin_count = ctf_table.shape[0]
    columns = raw_images.shape[1]
    hold_rows = raw_images.shape[0]
    shard_rows = hold_rows // 2
    capacity = 2 * shard_rows // dom_count
    is_live = dest_row >= 0
    target = jnp.where(is_live, dest_row // shard_rows, dom_count)
    local_row = dest_row % shard_rows
    marks = (target[:, None] == jnp.arange(dom_count, dtype=jnp.int32)[None, :]).astype(jnp.int32)
    slot_rank = jnp.sum((jnp.cumsum(marks, axis=0) - marks) * marks, axis=1)
    row_code = jnp.where(is_live, local_row * bin_count + defocus_bin, -1)
    padded_images = jnp.concatenate([raw_images, jnp.zeros((1, columns), raw_images.dtype)], axis=0)
    padded_code = jnp.concatenate([row_code, jnp.full((1,), -1, jnp.int32)], axis=0)
    position = jnp.where(is_live, target * capacity + slot_rank, dom_count * capacity)
    slot_count = dom_count * capacity
    source = (
        jnp.full((slot_count,), hold_rows, jnp.int32)
        .at[position]
        .set(jnp.arange(hold_rows, dtype=jnp.int32), mode="drop")
    )
    send_images = padded_images[source].reshape(dom_count, capacity, columns)
    send_code = padded_code[source].reshape(dom_count, capacity)
    recv_images, recv_code = (
        lax.all_to_all(send_images, "dom", split_axis=0, concat_axis=0, tiled=True),
        lax.all_to_all(send_code, "dom", split_axis=0, concat_axis=0, tiled=True),
    )
    flat_images = recv_images.reshape(-1, columns)
    flat_code = recv_code.reshape(-1)
    arrived = flat_code >= 0
    row_of = jnp.where(arrived, flat_code // bin_count, shard_rows)
    row_order = (
        jnp.zeros((shard_rows,), jnp.int32)
        .at[row_of]
        .set(jnp.arange(flat_code.shape[0], dtype=jnp.int32), mode="drop")
    )
    images = flat_images[row_order]
    bin_ids = flat_code[row_order] % bin_count
    bin_table = (bin_ids[:, None] == jnp.arange(bin_count, dtype=jnp.int32)[None, :]).astype(
        jnp.float32
    )
    ctf_rows = jnp.dot(bin_table, ctf_table, precision=lax.Precision.HIGHEST)
    factor = ctf_rows * inv_noise[None, :]
    weighted = (images.astype(jnp.float32) * jnp.concatenate([factor, factor], axis=1)).astype(
        jnp.bfloat16
    )
    gain_half = ctf_table * ctf_table * inv_noise[None, :]
    gain_full = jnp.concatenate([gain_half, gain_half], axis=1)
    panel_piece = lax.all_gather(panels, "dom", axis=1, tiled=True)
    col_block = weighted
    cross_term = lax.dot_general(
        col_block, panel_piece, (((1,), (1,)), ((), ())), preferred_element_type=jnp.float32
    )
    energy = energy_block(gain_full, panel_piece)
    scores = cross_term - 0.5 * jnp.dot(bin_table, energy, precision=lax.Precision.HIGHEST)
    local_peak = jnp.max(scores, axis=1)
    row_peak = lax.pmax(local_peak, "rot")
    shifted = jnp.exp(scores - row_peak[:, None])
    row_total = lax.psum(jnp.sum(shifted, axis=1), "rot")
    posterior = (shifted / row_total[:, None]).astype(jnp.bfloat16)
    log_evidence = row_peak + jnp.log(row_total)
    col_block = weighted
    class_sums = lax.psum_scatter(
        lax.dot_general(
            col_block, posterior, (((0,), (0,)), ((), ())), preferred_element_type=jnp.float32
        ).astype(jnp.bfloat16),
        "dom",
        scatter_dimension=0,
        tiled=True,
    ).astype(jnp.float32)
    local_mass = lax.dot_general(
        bin_table.astype(jnp.bfloat16),
        posterior,
        (((0,), (0,)), ((), ())),
        preferred_element_type=jnp.float32,
    )
    bin_weights = lax.psum(local_mass.astype(jnp.bfloat16), "dom").astype(jnp.float32)
    return (class_sums, bin_weights, log_evidence)


def solution(mesh):
    small = mesh.shape["dom"] == 8 and mesh.shape["rot"] == 4
    return jax.shard_map(
        two_by_two if small else on_device,
        mesh=mesh,
        in_specs=(P("dom", None), P("dom"), P("dom"), P(), P(), P("rot", "dom")),
        out_specs=(P("dom", "rot"), P(None, "rot"), P("dom")),
        check_vma=False,
    )
```

time: 350 us -> 332 us (0.949)
  waiting for transfers between devices: 187 us -> 161 us
  blocking collectives: 9.66 us -> 0 us
  starting transfers between devices: 37.5 us -> 46 us
  local copies, waits for them, and re-layouts: 9.28 us -> 17.6 us
    ppermute x19 -> x23, waiting for transfers between devices: 81.3 us -> 59.2 us  [across(): return lax.ppermute(value, 'dom', [(i, i ^ apart) for i in range(dom)])]
    all_to_all x1 -> x2, waiting for transfers between devices: 37.8 us -> 27.9 us  [the longest x1 19.5 us: two_by_two(): recv_a = lax.all_to_all(send_a, 'dom', 0, 0, tiled=True)]
    all_to_all x1 -> x0, blocking collectives: 9.66 us -> none  [two_by_two(): got_code = lax.all_to_all(code.reshape(dom, cap), 'dom', 0, 0, tiled=True)]
    ppermute x5 -> x10, starting transfers between devices: 3.98 us -> 13.2 us  [the longest x6 9.57 us: onward(): lax.ppermute(value, 'rot', [(i, (i + 1) % turns) for i in range(turns)])]
    ppermute x5 -> x10, waiting for transfers between devices: 62.6 us -> 70.2 us  [the longest x6 40.4 us: onward(): lax.ppermute(value, 'rot', [(i, (i + 1) % turns) for i in range(turns)])]
    unnamed x23 -> x38, local copies, waits for them, and re-layouts: 6.05 us -> 13.5 us
    ppermute x19 -> x23, starting transfers between devices: 24.5 us -> 19.5 us  [across(): return lax.ppermute(value, 'dom', [(i, i ^ apart) for i in range(dom)])]
    all_to_all x1 -> x2, starting transfers between devices: 4.57 us -> 8.88 us  [the longest x1 5.17 us: two_by_two(): recv_a = lax.all_to_all(send_a, 'dom', 0, 0, tiled=True)]
  transfers between devices with their start and end apart: 28 -> 38, of which waited for: 14 -> 20; matrix products, arithmetic and copies ran while one was open for 1% -> 1% of each run, Pallas kernels for 16% -> 22%
where the time goes in v2:
time: 332 us; the launch traced here: 330 us
  waiting for transfers between devices  161 us (48%)
  Pallas kernels  103 us (31%)
  starting transfers between devices  46 us (14%)
  local copies, waits for them, and re-layouts  17.6 us (5%)
    ppermute x23, waiting for transfers between devices, across(): return lax.ppermute(value, 'dom', [(i, i ^ apart) for i in range(dom)])  59.2 us
    ppermute x6, waiting for transfers between devices, onward(): lax.ppermute(value, 'rot', [(i, (i + 1) % turns) for i in range(turns)])  40.4 us
    pallas_call x4, Pallas kernels, score(): call(functools.partial(score_body, first, last), (2 * half,), in_specs, o...  36.4 us
    ppermute x4, waiting for transfers between devices, by_core(): return lax.ppermute(value, 'dom', pairs)  29.8 us
    pallas_call x3, Pallas kernels, class_part(): call(functools.partial(class_body, kind, steps), (steps,), in_specs, out_...  22.8 us
    ppermute x23, starting transfers between devices, across(): return lax.ppermute(value, 'dom', [(i, i ^ apart) for i in range(dom)])  19.5 us
    all_to_all x1, waiting for transfers between devices, two_by_two(): recv_a = lax.all_to_all(send_a, 'dom', 0, 0, tiled=True)  19.5 us
    unnamed x38, local copies, waits for them, and re-layouts  13.5 us
  transfers between devices with their start and end apart: 38, of which 20 were waited for; matrix products, arithmetic and copies ran while one was open for 1% of the time, Pallas kernels for 22%

profile of v2, /device:TPU:0, one launch (start us, length us, event | category | flops | bytes accessed | tf_op | source)
XLA Modules:
  0.0 330.3 jit_solution(17100670329756291573)
XLA Ops:
  2.2 6.0 %shard_map.85 = (bf16[1536,640]{1,0:T(8,128)(2,1)S(1)}, s32[1,1536]{1,0:T(1,128)S(1)}) custom-call(s32[10]{0:T(128)S(1)} %stack.43.meta, s32[1,1536]{1,0:T(1,128)S(1)} %broadcast_in_dim.9.dest_ref, s32[1,1536]{1,0:T(1,128)S(1)} %broadcast_in_dim.10.bin_ref, bf16[1536,4096]{1,0:T(8,128)(2,1)} %raw_ref.3), custom_call_target="tpu_custom_call" | custom-call | flops 2415919104 | bytes 3145728 | tf_op jit(solution)/shard_map/pallas_call | solution.py:105
  8.1 1.3 copy-done.1
  9.4 5.2 %all-to-all-start = ((bf16[8,192,640]{2,1,0:T(8,128)(2,1)}), bf16[8,192,640]{2,1,0:T(8,128)(2,1)S(1)}, u32[]{:S(2)}, u32[]{:S(2)}) async-start(bf16[8,192,640]{2,1,0:T(8,128)(2,1)} %bitcast.18), calls=%async_computation | async-start | bytes 3932160 | tf_op jit(solution)/shard_map/all_to_all | solution.py:519
  14.6 5.7 %shard_map.87 = bf16[1536,512]{1,0:T(8,128)(2,1)} custom-call(s32[10]{0:T(128)S(1)} %stack.43.meta, s32[1,1536]{1,0:T(1,128)S(1)} %get-tuple-element.53.place_ref, bf16[1536,4096]{1,0:T(8,128)(2,1)} %raw_ref.3), custom_call_target="tpu_custom_call" | custom-call | flops 2415919104 | bytes 3145728 | tf_op jit(solution)/shard_map/pallas_call | solution.py:120
  20.3 19.5 %all-to-all-done = bf16[8,192,640]{2,1,0:T(8,128)(2,1)S(1)} async-done(((bf16[8,192,640]{2,1,0:T(8,128)(2,1)}), bf16[8,192,640]{2,1,0:T(8,128)(2,1)S(1)}, u32[]{:S(2)}, u32[]{:S(2)}) %all-to-all-start) | async-done | bytes 1966112 | tf_op jit(solution)/shard_map/all_to_all | solution.py:519
  39.8 3.7 %all-to-all-start.1 = ((bf16[8,192,512]{2,1,0:T(8,128)(2,1)}), bf16[8,192,512]{2,1,0:T(8,128)(2,1)S(1)}, u32[]{:S(2)}, u32[]{:S(2)}) async-start(bf16[8,192,512]{2,1,0:T(8,128)(2,1)} %bitcast.13), calls=%async_computation.1 | async-start | bytes 3145728 | tf_op jit(solution)/shard_map/all_to_all | solution.py:521
  43.6 2.7 constant_dynamic-slice_fusion
  46.6 1.7 collective-permute-start.1
  48.3 5.2 %shard_map.86 = (bf16[768,512]{1,0:T(8,128)(2,1)}, bf16[192,768]{1,0:T(8,128)(2,1)S(1)}, bf16[768,1536]{1,0:T(8,128)(2,1)}, bf16[768,192]{1,0:T(8,128)(2,1)S(1)}) custom-call(s32[10]{0:T(128)S(1)} %stack.43.meta, bf16[1536,640]{1,0:T(8,128)(2,1)S(1)} %bitcast.17, f32[64,2048]{1,0:T(8,128)S(1)} %copy-done.8, f32[1,2048]{1,0:T(1,128)S(1)} %bitcast.19), custom_call_target="tpu_custom_call" | custom-call | flops 1207959552 | bytes 1966080 | tf_op jit(solution)/shard_map/pallas_call | solution.py:171
  53.5 0.7 copy-done.4
  54.2 0.7 copy-done.11
  55.0 1.6 collective-permute-start
  56.5 8.4 %all-to-all-done.1 = bf16[8,192,512]{2,1,0:T(8,128)(2,1)S(1)} async-done(((bf16[8,192,512]{2,1,0:T(8,128)(2,1)}), bf16[8,192,512]{2,1,0:T(8,128)(2,1)S(1)}, u32[]{:S(2)}, u32[]{:S(2)}) %all-to-all-start.1) | async-done | bytes 1572896 | tf_op jit(solution)/shard_map/all_to_all | solution.py:521
  65.0 1.0 copy-done.9
  66.0 1.0 copy-done.12
  67.0 3.8 %shard_map.88.refs_1_ = bf16[768,512]{1,0:T(8,128)(2,1)S(1)} custom-call(s32[10]{0:T(128)S(1)} %stack.43.meta, bf16[768,1536]{1,0:T(8,128)(2,1)} %get-tuple-element.51.pick_ref, bf16[768,192]{1,0:T(8,128)(2,1)S(1)} %copy-done.12, bf16[1536,512]{1,0:T(8,128)(2,1)S(1)} %bitcast.16, f32[64,2048]{1,0:T(8,128)S(1)} %copy-done.9, f32[1,2048]{1,0:T(1,128)S(1)} %bitcast.20), custom_call_target="tpu_custom_call" | custom-call | flops 1207959552 | bytes 1572864 | tf_op jit(solution)/shard_map/pallas_call | solution.py:192
  70.8 1.6 collective-permute-start.10
  73.6 6.4 %collective-permute-done.1.refs_2_ = bf16[720,512]{1,0:T(8,128)(2,1)} collective-permute-done((bf16[720,512]{1,0:T(8,128)(2,1)}, bf16[720,512]{1,0:T(8,128)(2,1)}, u32[]{:S(2)}, u32[]{:S(2)}) %collective-permute-start.1) | collective-permute-done | bytes 737312 | tf_op jit(solution)/shard_map/ppermute | solution.py:507
  79.9 1.5 collective-permute-start.5
  81.4 10.6 %collective-permute-done.4.refs_4_ = bf16[720,512]{1,0:T(8,128)(2,1)S(1)} collective-permute-done((bf16[720,512]{1,0:T(8,128)(2,1)}, bf16[720,512]{1,0:T(8,128)(2,1)S(1)}, u32[]{:S(2)}, u32[]{:S(2)}) %collective-permute-start.4) | collective-permute-done | bytes 737312 | tf_op jit(solution)/shard_map/ppermute | solution.py:507
  92.1 3.1 collective-permute-done.3.refs_3_
  95.2 0.9 copy-done.14
  96.0 7.0 %collective-permute-done.5.refs_5_ = bf16[720,512]{1,0:T(8,128)(2,1)S(1)} collective-permute-done((bf16[720,512]{1,0:T(8,128)(2,1)}, bf16[720,512]{1,0:T(8,128)(2,1)S(1)}, u32[]{:S(2)}, u32[]{:S(2)}) %collective-permute-start.5) | collective-permute-done | bytes 737312 | tf_op jit(solution)/shard_map/ppermute | solution.py:507
  103.1 1.6 collective-permute-start.6
  104.7 1.6 collective-permute-start.11
  106.3 1.4 collective-permute-start.7
  107.7 2.5 collective-permute-start.8
  110.3 10.0 %collective-permute-done.7.refs_6_ = bf16[720,512]{1,0:T(8,128)(2,1)S(1)} collective-permute-done((bf16[720,512]{1,0:T(8,128)(2,1)}, bf16[720,512]{1,0:T(8,128)(2,1)S(1)}, u32[]{:S(2)}, u32[]{:S(2)}) %collective-permute-start.7) | collective-permute-done | bytes 737312 | tf_op jit(solution)/shard_map/ppermute | solution.py:507
  120.2 5.0 %collective-permute-done.8.refs_7_ = bf16[720,512]{1,0:T(8,128)(2,1)} collective-permute-done((bf16[720,512]{1,0:T(8,128)(2,1)S(1)}, bf16[720,512]{1,0:T(8,128)(2,1)}, u32[]{:S(2)}, u32[]{:S(2)}) %collective-permute-start.8) | collective-permute-done | bytes 737312 | tf_op jit(solution)/shard_map/ppermute | solution.py:507
  125.4 12.3 %collective-permute-done.11.refs_1_ = bf16[768,512]{1,0:T(8,128)(2,1)S(1)} collective-permute-done((bf16[768,512]{1,0:T(8,128)(2,1)S(1)}, bf16[768,512]{1,0:T(8,128)(2,1)S(1)}, u32[]{:S(2)}, u32[]{:S(2)}) %collective-permute-start.11) | collective-permute-done | bytes 786464 | tf_op jit(solution)/shard_map/ppermute | solution.py:514
  137.7 1.1 collective-permute-start.12
  138.7 2.1 collective-permute-start.9
  140.8 0.9 copy-done.6
  142.2 17.7 %collective-permute-done.12.refs_1_ = bf16[768,512]{1,0:T(8,128)(2,1)S(1)} collective-permute-done((bf16[768,512]{1,0:T(8,128)(2,1)S(1)}, bf16[768,512]{1,0:T(8,128)(2,1)S(1)}, u32[]{:S(2)}, u32[]{:S(2)}) %collective-permute-start.12) | collective-permute-done | bytes 786464 | tf_op jit(solution)/shard_map/ppermute | solution.py:514
  159.9 10.3 %collective-permute-done.9.refs_0_ = bf16[768,512]{1,0:T(8,128)(2,1)S(1)} collective-permute-done((bf16[768,512]{1,0:T(8,128)(2,1)S(1)}, bf16[768,512]{1,0:T(8,128)(2,1)S(1)}, u32[]{:S(2)}, u32[]{:S(2)}) %collective-permute-start.9) | collective-permute-done | bytes 786464 | tf_op jit(solution)/shard_map/ppermute | solution.py:514
  170.2 1.0 copy-done.10
  171.3 1.1 copy-done.15
  172.4 10.3 %shard_map.89 = (bf16[720,4096]{1,0:T(8,128)(2,1)}, bf16[720,192]{1,0:T(8,128)(2,1)S(1)}) custom-call(s32[10]{0:T(128)S(1)} %stack.43.meta, bf16[720,512]{1,0:T(8,128)(2,1)} %get-tuple-element.88.refs_0_, bf16[720,512]{1,0:T(8,128)(2,1)} %collective-permute-done.2.refs_1_, bf16[720,512]{1,0:T(8,128)(2,1)} %collective-permute-done.1.refs_2_, ...), custom_call_target="tpu_custom_call" | custom-call | flops 4529848320 | bytes 11796480 | tf_op jit(solution)/shard_map/pallas_call | solution.py:242
  182.7 1.1 copy-done.7
  183.8 8.0 %shard_map.90 = (f32[720,1536]{1,0:T(8,128)}, bf16[1536,4096]{1,0:T(8,128)(2,1)}) custom-call(s32[10]{0:T(128)S(1)} %stack.43.meta, bf16[768,512]{1,0:T(8,128)(2,1)} %get-tuple-element.46.refs_0_, bf16[768,512]{1,0:T(8,128)(2,1)S(1)} %shard_map.88.refs_1_, bf16[768,512]{1,0:T(8,128)(2,1)S(1)} %copy-done.7, ...), custom_call_target="tpu_custom_call" | custom-call | flops 2264924160 | bytes 15138816 | tf_op jit(solution)/shard_map/pallas_call | solution.py:333
  192.3 9.1 %shard_map.91 = (f32[720,1536]{1,0:T(8,128)}, bf16[1536,4096]{1,0:T(8,128)(2,1)}) custom-call(s32[10]{0:T(128)S(1)} %stack.43.meta, bf16[768,512]{1,0:T(8,128)(2,1)S(1)} %collective-permute-done.refs_0_, bf16[768,512]{1,0:T(8,128)(2,1)S(1)} %collective-permute-done.10.refs_1_, ...), custom_call_target="tpu_custom_call", output_to_operand_aliasing={{0}: (6, {}), {1}: (7, {})} | custom-call | flops 2264924160 | bytes 15138816 | tf_op jit(solution)/shard_map/pallas_call | solution.py:333
  201.4 9.0 %shard_map.92 = (f32[720,1536]{1,0:T(8,128)}, bf16[1536,4096]{1,0:T(8,128)(2,1)}) custom-call(s32[10]{0:T(128)S(1)} %stack.43.meta, bf16[768,512]{1,0:T(8,128)(2,1)S(1)} %collective-permute-done.6.refs_0_, bf16[768,512]{1,0:T(8,128)(2,1)S(1)} %collective-permute-done.11.refs_1_, ...), custom_call_target="tpu_custom_call", output_to_operand_aliasing={{0}: (6, {}), {1}: (7, {})} | custom-call | flops 2264924160 | bytes 15138816 | tf_op jit(solution)/shard_map/pallas_call | solution.py:333
  210.5 10.3 %shard_map.93 = (f32[720,1536]{1,0:T(8,128)}, f32[8,1536]{1,0:T(8,128)S(1)}, bf16[1536,4096]{1,0:T(8,128)(2,1)}) custom-call(s32[10]{0:T(128)S(1)} %stack.43.meta, bf16[768,512]{1,0:T(8,128)(2,1)S(1)} %collective-permute-done.9.refs_0_, bf16[768,512]{1,0:T(8,128)(2,1)S(1)} %collective-permute-done.12.refs_1_, ...), custom_call_target="tpu_custom_call", output_to_operand_aliasing={{0}: (6, {}), {2}: (7, {})} | custom-call | flops 2264924160 | bytes 15138816 | tf_op jit(solution)/shard_map/pallas_call | solution.py:333
  220.8 1.2 collective-permute-done.22.other_ref
  222.7 1.9 collective-permute-start.24
  224.6 2.5 collective-permute-start.25
  227.4 2.4 collective-permute-done.24.refs_4_
  229.8 0.8 collective-permute-done.25.refs_5_
  230.5 6.0 %shard_map.95 = (bf16[720,512]{1,0:T(8,128)(2,1)S(1)}, bf16[720,512]{1,0:T(8,128)(2,1)S(1)}, bf16[720,1536]{1,0:T(8,128)(2,1)S(1)}, f32[1,768]{1,0:T(1,128)S(1)}) custom-call(s32[10]{0:T(128)S(1)} %stack.43.meta, f32[720,1536]{1,0:T(8,128)} %get-tuple-element.67.refs_0_, f32[8,1536]{1,0:T(8,128)S(1)} %get-tuple-element.68.mine_ref.refs_1_, ...), custom_call_target="tpu_custom_call" | custom-call | flops 2264924160 | bytes 10518528 | tf_op jit(solution)/shard_map/pallas_call | solution.py:419
  236.6 1.3 copy-done
  237.9 9.5 %collective-permute-start.26 = (bf16[720,512]{1,0:T(8,128)(2,1)S(1)}, bf16[720,512]{1,0:T(8,128)(2,1)S(1)}, u32[]{:S(2)}, u32[]{:S(2)}) collective-permute-start(bf16[720,512]{1,0:T(8,128)(2,1)S(1)} %get-tuple-element.74), channel_id=1, source_target_pairs={{0,8},{4,12},{8,0},{12,4},{16,24},{20,28},{24,16},{28,20},{1,9},{5... | collective-permute-start | bytes 2211848 | tf_op jit(solution)/shard_map/ppermute | solution.py:507
  247.4 8.9 %shard_map.97 = (bf16[720,512]{1,0:T(8,128)(2,1)}, bf16[720,512]{1,0:T(8,128)(2,1)}, bf16[720,512]{1,0:T(8,128)(2,1)}, f32[64,720]{1,0:T(8,128)S(1)}) custom-call(s32[10]{0:T(128)S(1)} %stack.43.meta, bf16[720,1536]{1,0:T(8,128)(2,1)} %copy-done, bf16[192,768]{1,0:T(8,128)(2,1)S(1)} %copy-done.5, ...), custom_call_target="tpu_custom_call" | custom-call | flops 3397386240 | bytes 13565952 | tf_op jit(solution)/shard_map/pallas_call | solution.py:419
  256.4 10.3 %collective-permute-done.33 = f32[64,720]{1,0:T(8,128)S(1)} collective-permute-done((f32[64,720]{1,0:T(8,128)S(1)}, f32[64,720]{1,0:T(8,128)S(1)}, u32[]{:S(2)}, u32[]{:S(2)}) %collective-permute-start.33) | collective-permute-done | bytes 184352 | tf_op jit(solution)/shard_map/ppermute | solution.py:507
  266.9 5.6 %collective-permute-done.34 = f32[64,720]{1,0:T(8,128)S(1)} collective-permute-done((f32[64,720]{1,0:T(8,128)S(1)}, f32[64,720]{1,0:T(8,128)S(1)}, u32[]{:S(2)}, u32[]{:S(2)}) %collective-permute-start.34) | collective-permute-done | bytes 184352 | tf_op jit(solution)/shard_map/ppermute | solution.py:507
  272.6 7.8 %shard_map.96 = (f32[720,512]{1,0:T(8,128)S(1)}, f32[720,512]{1,0:T(8,128)S(1)}, f32[720,512]{1,0:T(8,128)}) custom-call(s32[10]{0:T(128)S(1)} %stack.43.meta, bf16[720,1536]{1,0:T(8,128)(2,1)} %copy-done, bf16[1536,4096]{1,0:T(8,128)(2,1)} %get-tuple-element.69.refs_6_.refs_1_.refs_3_), custom_call_target="tpu_custom_call" | custom-call | flops 3397386240 | bytes 13565952 | tf_op jit(solution)/shard_map/pallas_call | solution.py:419
  280.4 1.1 copy-done.2
  281.5 1.1 copy-done.3
  282.7 5.0 %shard_map.98 = (bf16[720,512]{1,0:T(8,128)(2,1)}, bf16[720,512]{1,0:T(8,128)(2,1)}) custom-call(s32[10]{0:T(128)S(1)} %stack.43.meta, f32[720,512]{1,0:T(8,128)} %copy-done.2, f32[720,512]{1,0:T(8,128)} %copy-done.3, bf16[720,512]{1,0:T(8,128)(2,1)S(1)} %collective-permute-done.26.down_ref, bf16[720,512]{1,0:T(8,128)(2,1)S(1)} %collective-permute-done.27.left_ref), custom_call_target="tpu_custom_call" | custom-call | tf_op jit(solution)/shard_map/pallas_call | solution.py:440
  287.7 1.9 collective-permute-start.31
  289.6 1.7 collective-permute-start.29
  291.9 0.9 maximum_select_fusion
  292.8 14.4 %collective-permute-done.28.a_ref = bf16[720,512]{1,0:T(8,128)(2,1)S(1)} collective-permute-done((bf16[720,512]{1,0:T(8,128)(2,1)}, bf16[720,512]{1,0:T(8,128)(2,1)S(1)}, u32[]{:S(2)}, u32[]{:S(2)}) %collective-permute-start.28) | collective-permute-done | bytes 737312 | tf_op jit(solution)/shard_map/ppermute | solution.py:511
  307.2 15.4 %collective-permute-done.29.c_ref = bf16[720,512]{1,0:T(8,128)(2,1)S(1)} collective-permute-done((bf16[720,512]{1,0:T(8,128)(2,1)}, bf16[720,512]{1,0:T(8,128)(2,1)S(1)}, u32[]{:S(2)}, u32[]{:S(2)}) %collective-permute-start.29) | collective-permute-done | bytes 737312 | tf_op jit(solution)/shard_map/ppermute | solution.py:511
  322.6 7.7 %shard_map.99 = f32[1440,512]{1,0:T(8,128)} custom-call(s32[10]{0:T(128)S(1)} %stack.43.meta, f32[720,512]{1,0:T(8,128)} %get-tuple-element.71.keep_ref, bf16[720,512]{1,0:T(8,128)(2,1)S(1)} %collective-permute-done.28.a_ref, bf16[720,512]{1,0:T(8,128)(2,1)S(1)} %collective-permute-done.29.c_ref, bf16[720,512]{1,0:T(8,128)(2,1)S(1)} %collective-permute-done.30.other_ref, ...), custom_call_target="tpu_custom_call" | custom-call | tf_op jit(solution)/shard_map/pallas_call | solution.py:469
  (73 shorter events, 6.2 us)
Async XLA Ops:
  8.1 1.3 copy-start.1
  9.4 30.4 %all-to-all-start = ((bf16[8,192,640]{2,1,0:T(8,128)(2,1)}), bf16[8,192,640]{2,1,0:T(8,128)(2,1)S(1)}, u32[]{:S(2)}, u32[]{:S(2)}) async-start(bf16[8,192,640]{2,1,0:T(8,128)(2,1)} %bitcast.18), calls=%async_computation | async-start | bytes 3932160 | tf_op jit(solution)/shard_map/all_to_all | solution.py:519
  39.8 8.5 %copy-start.13 = (f32[2048]{0:T(1024)S(1)}, f32[2048]{0:T(1024)}, u32[]{:S(2)}) copy-start(f32[2048]{0:T(1024)} %param.10) | copy-start | bytes 24580
  39.8 25.1 %all-to-all-start.1 = ((bf16[8,192,512]{2,1,0:T(8,128)(2,1)}), bf16[8,192,512]{2,1,0:T(8,128)(2,1)S(1)}, u32[]{:S(2)}, u32[]{:S(2)}) async-start(bf16[8,192,512]{2,1,0:T(8,128)(2,1)} %bitcast.13), calls=%async_computation.1 | async-start | bytes 3145728 | tf_op jit(solution)/shard_map/all_to_all | solution.py:521
  43.5 4.7 %copy-start.8 = (f32[64,2048]{1,0:T(8,128)S(1)}, f32[64,2048]{1,0:T(8,128)}, u32[]{:S(2)}) copy-start(f32[64,2048]{1,0:T(8,128)} %refs_8_.1) | copy-start | bytes 1572868
  46.2 26.7 %collective-permute-start.2 = (bf16[720,512]{1,0:T(8,128)(2,1)}, bf16[720,512]{1,0:T(8,128)(2,1)}, u32[]{:S(2)}, u32[]{:S(2)}) collective-permute-start(bf16[720,512]{1,0:T(8,128)(2,1)} %get-tuple-element.87), channel_id=1, source_target_pairs={{0,4},{4,0},{8,12},{12,8},{16,20},{20,16},{24,28},{28,24},{1,5},{5... | collective-permute-start | bytes 2211848 | tf_op jit(solution)/shard_map/ppermute | solution.py:507
  46.6 33.3 %collective-permute-start.1 = (bf16[720,512]{1,0:T(8,128)(2,1)}, bf16[720,512]{1,0:T(8,128)(2,1)}, u32[]{:S(2)}, u32[]{:S(2)}) collective-permute-start(bf16[720,512]{1,0:T(8,128)(2,1)} %get-tuple-element.88.refs_0_), channel_id=1, source_target_pairs={{0,8},{4,12},{8,0},{12,4},{16,24},{20,28},{24,16},{28,20},{1,9},{5... | collective-permute-start | bytes 2211848 | tf_op jit(solution)/shard_map/ppermute | solution.py:507
  53.5 0.7 copy-start.4
  54.2 0.7 copy-start.11
  55.0 48.1 %collective-permute-start = (bf16[768,512]{1,0:T(8,128)(2,1)}, bf16[768,512]{1,0:T(8,128)(2,1)S(1)}, u32[]{:S(2)}, u32[]{:S(2)}) collective-permute-start(bf16[768,512]{1,0:T(8,128)(2,1)} %get-tuple-element.46.refs_0_), channel_id=1, source_target_pairs={{0,1},{1,2},{2,3},{3,0},{4,5},{5,6},{6,7},{7,4},{8,9},{9,10},{10,1... | collective-permute-start | bytes 2359304 | tf_op jit(solution)/shard_map/ppermute | solution.py:514
  65.0 1.0 copy-start.9
  66.0 1.0 copy-start.12
  70.8 33.9 %collective-permute-start.10 = (bf16[768,512]{1,0:T(8,128)(2,1)S(1)}, bf16[768,512]{1,0:T(8,128)(2,1)S(1)}, u32[]{:S(2)}, u32[]{:S(2)}) collective-permute-start(bf16[768,512]{1,0:T(8,128)(2,1)S(1)} %shard_map.88.refs_1_), channel_id=1, source_target_pairs={{0,1},{1,2},{2,3},{3,0},{4,5},{5,6},{6,7},{7,4},{8,9},{9,10},{10,1... | collective-permute-start | bytes 2359304 | tf_op jit(solution)/shard_map/ppermute | solution.py:514
  72.4 19.6 %collective-permute-start.4 = (bf16[720,512]{1,0:T(8,128)(2,1)}, bf16[720,512]{1,0:T(8,128)(2,1)S(1)}, u32[]{:S(2)}, u32[]{:S(2)}) collective-permute-start(bf16[720,512]{1,0:T(8,128)(2,1)} %get-tuple-element.88.refs_0_), channel_id=1, source_target_pairs={{0,16},{4,20},{8,24},{12,28},{16,0},{20,4},{24,8},{28,12},{1,17},{... | collective-permute-start | bytes 2211848 | tf_op jit(solution)/shard_map/ppermute | solution.py:507
  73.0 22.2 %collective-permute-start.3 = (bf16[720,512]{1,0:T(8,128)(2,1)}, bf16[720,512]{1,0:T(8,128)(2,1)S(1)}, u32[]{:S(2)}, u32[]{:S(2)}) collective-permute-start(bf16[720,512]{1,0:T(8,128)(2,1)} %collective-permute-done.2.refs_1_), channel_id=1, source_target_pairs={{0,8},{4,12},{8,0},{12,4},{16,24},{20,28},{24,16},{28,20},{1,9},{5... | collective-permute-start | bytes 2211848 | tf_op jit(solution)/shard_map/ppermute | solution.py:507
  79.9 23.1 %collective-permute-start.5 = (bf16[720,512]{1,0:T(8,128)(2,1)}, bf16[720,512]{1,0:T(8,128)(2,1)S(1)}, u32[]{:S(2)}, u32[]{:S(2)}) collective-permute-start(bf16[720,512]{1,0:T(8,128)(2,1)} %collective-permute-done.2.refs_1_), channel_id=1, source_target_pairs={{0,16},{4,20},{8,24},{12,28},{16,0},{20,4},{24,8},{28,12},{1,17},{... | collective-permute-start | bytes 2211848 | tf_op jit(solution)/shard_map/ppermute | solution.py:507
  92.1 11.0 %copy-start.16 = (bf16[720,512]{1,0:T(8,128)(2,1)}, bf16[720,512]{1,0:T(8,128)(2,1)S(1)}, u32[]{:S(2)}) copy-start(bf16[720,512]{1,0:T(8,128)(2,1)S(1)} %collective-permute-done.4.refs_4_) | copy-start | bytes 2211844
  95.2 0.9 copy-start.14
  103.0 22.3 %copy-start.17 = (bf16[720,512]{1,0:T(8,128)(2,1)}, bf16[720,512]{1,0:T(8,128)(2,1)S(1)}, u32[]{:S(2)}) copy-start(bf16[720,512]{1,0:T(8,128)(2,1)S(1)} %collective-permute-done.5.refs_5_) | copy-start | bytes 2211844
  103.1 22.3 %collective-permute-start.6 = (bf16[768,512]{1,0:T(8,128)(2,1)S(1)}, bf16[768,512]{1,0:T(8,128)(2,1)S(1)}, u32[]{:S(2)}, u32[]{:S(2)}) collective-permute-start(bf16[768,512]{1,0:T(8,128)(2,1)S(1)} %collective-permute-done.refs_0_), channel_id=1, source_target_pairs={{0,1},{1,2},{2,3},{3,0},{4,5},{5,6},{6,7},{7,4},{8,9},{9,10},{10,1... | collective-permute-start | bytes 2359304 | tf_op jit(solution)/shard_map/ppermute | solution.py:514
  104.7 33.0 %collective-permute-start.11 = (bf16[768,512]{1,0:T(8,128)(2,1)S(1)}, bf16[768,512]{1,0:T(8,128)(2,1)S(1)}, u32[]{:S(2)}, u32[]{:S(2)}) collective-permute-start(bf16[768,512]{1,0:T(8,128)(2,1)S(1)} %collective-permute-done.10.refs_1_), channel_id=1, source_target_pairs={{0,1},{1,2},{2,3},{3,0},{4,5},{5,6},{6,7},{7,4},{8,9},{9,10},{10,1... | collective-permute-start | bytes 2359304 | tf_op jit(solution)/shard_map/ppermute | solution.py:514
  106.3 13.9 %collective-permute-start.7 = (bf16[720,512]{1,0:T(8,128)(2,1)}, bf16[720,512]{1,0:T(8,128)(2,1)S(1)}, u32[]{:S(2)}, u32[]{:S(2)}) collective-permute-start(bf16[720,512]{1,0:T(8,128)(2,1)} %collective-permute-done.1.refs_2_), channel_id=1, source_target_pairs={{0,16},{4,20},{8,24},{12,28},{16,0},{20,4},{24,8},{28,12},{1,17},{... | collective-permute-start | bytes 2211848 | tf_op jit(solution)/shard_map/ppermute | solution.py:507
  107.7 17.5 %collective-permute-start.8 = (bf16[720,512]{1,0:T(8,128)(2,1)S(1)}, bf16[720,512]{1,0:T(8,128)(2,1)}, u32[]{:S(2)}, u32[]{:S(2)}) collective-permute-start(bf16[720,512]{1,0:T(8,128)(2,1)S(1)} %collective-permute-done.5.refs_5_), channel_id=1, source_target_pairs={{0,8},{4,12},{8,0},{12,4},{16,24},{20,28},{24,16},{28,20},{1,9},{5... | collective-permute-start | bytes 2211848 | tf_op jit(solution)/shard_map/ppermute | solution.py:507
  110.3 30.6 %collective-permute-start.20 = (bf16[768,512]{1,0:T(8,128)(2,1)S(1)}, bf16[768,512]{1,0:T(8,128)(2,1)S(1)}, u32[]{:S(2)}, u32[]{:S(2)}) collective-permute-start(bf16[768,512]{1,0:T(8,128)(2,1)S(1)} %shard_map.88.refs_1_), channel_id=1, source_target_pairs={{0,4},{4,0},{8,12},{12,8},{16,20},{20,16},{24,28},{28,24},{1,5},{5... | collective-permute-start | bytes 2359304 | tf_op jit(solution)/shard_map/ppermute | solution.py:507
  120.2 5.2 %copy-start.18 = (bf16[720,512]{1,0:T(8,128)(2,1)}, bf16[720,512]{1,0:T(8,128)(2,1)S(1)}, u32[]{:S(2)}) copy-start(bf16[720,512]{1,0:T(8,128)(2,1)S(1)} %collective-permute-done.7.refs_6_) | copy-start | bytes 2211844
  120.2 20.6 %collective-permute-start.19 = (bf16[768,512]{1,0:T(8,128)(2,1)}, bf16[768,512]{1,0:T(8,128)(2,1)S(1)}, u32[]{:S(2)}, u32[]{:S(2)}) collective-permute-start(bf16[768,512]{1,0:T(8,128)(2,1)} %get-tuple-element.46.refs_0_), channel_id=1, source_target_pairs={{0,4},{4,0},{8,12},{12,8},{16,20},{20,16},{24,28},{28,24},{1,5},{5... | collective-permute-start | bytes 2359304 | tf_op jit(solution)/shard_map/ppermute | solution.py:507
  125.2 17.0 %collective-permute-start.18 = (bf16[768,512]{1,0:T(8,128)(2,1)S(1)}, bf16[768,512]{1,0:T(8,128)(2,1)S(1)}, u32[]{:S(2)}, u32[]{:S(2)}) collective-permute-start(bf16[768,512]{1,0:T(8,128)(2,1)S(1)} %collective-permute-done.10.refs_1_), channel_id=1, source_target_pairs={{0,4},{4,0},{8,12},{12,8},{16,20},{20,16},{24,28},{28,24},{1,5},{5... | collective-permute-start | bytes 2359304 | tf_op jit(solution)/shard_map/ppermute | solution.py:507
  137.7 22.3 %collective-permute-start.12 = (bf16[768,512]{1,0:T(8,128)(2,1)S(1)}, bf16[768,512]{1,0:T(8,128)(2,1)S(1)}, u32[]{:S(2)}, u32[]{:S(2)}) collective-permute-start(bf16[768,512]{1,0:T(8,128)(2,1)S(1)} %collective-permute-done.11.refs_1_), channel_id=1, source_target_pairs={{0,1},{1,2},{2,3},{3,0},{4,5},{5,6},{6,7},{7,4},{8,9},{9,10},{10,1... | collective-permute-start | bytes 2359304 | tf_op jit(solution)/shard_map/ppermute | solution.py:514
  138.7 31.5 %collective-permute-start.9 = (bf16[768,512]{1,0:T(8,128)(2,1)S(1)}, bf16[768,512]{1,0:T(8,128)(2,1)S(1)}, u32[]{:S(2)}, u32[]{:S(2)}) collective-permute-start(bf16[768,512]{1,0:T(8,128)(2,1)S(1)} %collective-permute-done.6.refs_0_), channel_id=1, source_target_pairs={{0,1},{1,2},{2,3},{3,0},{4,5},{5,6},{6,7},{7,4},{8,9},{9,10},{10,1... | collective-permute-start | bytes 2359304 | tf_op jit(solution)/shard_map/ppermute | solution.py:514
  140.8 51.0 %collective-permute-start.17 = (bf16[768,512]{1,0:T(8,128)(2,1)S(1)}, bf16[768,512]{1,0:T(8,128)(2,1)S(1)}, u32[]{:S(2)}, u32[]{:S(2)}) collective-permute-start(bf16[768,512]{1,0:T(8,128)(2,1)S(1)} %collective-permute-done.refs_0_), channel_id=1, source_target_pairs={{0,4},{4,0},{8,12},{12,8},{16,20},{20,16},{24,28},{28,24},{1,5},{5... | collective-permute-start | bytes 2359304 | tf_op jit(solution)/shard_map/ppermute | solution.py:507
  140.8 0.9 copy-start.6
  141.7 59.7 %collective-permute-start.15 = (bf16[768,512]{1,0:T(8,128)(2,1)S(1)}, bf16[768,512]{1,0:T(8,128)(2,1)S(1)}, u32[]{:S(2)}, u32[]{:S(2)}) collective-permute-start(bf16[768,512]{1,0:T(8,128)(2,1)S(1)} %collective-permute-done.6.refs_0_), channel_id=1, source_target_pairs={{0,4},{4,0},{8,12},{12,8},{16,20},{20,16},{24,28},{28,24},{1,5},{5... | collective-permute-start | bytes 2359304 | tf_op jit(solution)/shard_map/ppermute | solution.py:507
  142.2 59.2 %collective-permute-start.16 = (bf16[768,512]{1,0:T(8,128)(2,1)S(1)}, bf16[768,512]{1,0:T(8,128)(2,1)S(1)}, u32[]{:S(2)}, u32[]{:S(2)}) collective-permute-start(bf16[768,512]{1,0:T(8,128)(2,1)S(1)} %collective-permute-done.11.refs_1_), channel_id=1, source_target_pairs={{0,4},{4,0},{8,12},{12,8},{16,20},{20,16},{24,28},{28,24},{1,5},{5... | collective-permute-start | bytes 2359304 | tf_op jit(solution)/shard_map/ppermute | solution.py:507
  159.9 50.5 %collective-permute-start.14 = (bf16[768,512]{1,0:T(8,128)(2,1)S(1)}, bf16[768,512]{1,0:T(8,128)(2,1)}, u32[]{:S(2)}, u32[]{:S(2)}) collective-permute-start(bf16[768,512]{1,0:T(8,128)(2,1)S(1)} %collective-permute-done.12.refs_1_), channel_id=1, source_target_pairs={{0,4},{4,0},{8,12},{12,8},{16,20},{20,16},{24,28},{28,24},{1,5},{5... | collective-permute-start | bytes 2359304 | tf_op jit(solution)/shard_map/ppermute | solution.py:507
  170.2 40.3 %collective-permute-start.13 = (bf16[768,512]{1,0:T(8,128)(2,1)S(1)}, bf16[768,512]{1,0:T(8,128)(2,1)S(1)}, u32[]{:S(2)}, u32[]{:S(2)}) collective-permute-start(bf16[768,512]{1,0:T(8,128)(2,1)S(1)} %collective-permute-done.9.refs_0_), channel_id=1, source_target_pairs={{0,4},{4,0},{8,12},{12,8},{16,20},{20,16},{24,28},{28,24},{1,5},{5... | collective-permute-start | bytes 2359304 | tf_op jit(solution)/shard_map/ppermute | solution.py:507
  170.2 1.0 copy-start.10
  171.3 1.1 copy-start.15
  182.7 1.1 copy-start.7
  183.8 8.0 %copy-start.5 = (bf16[192,768]{1,0:T(8,128)(2,1)S(1)}, bf16[192,768]{1,0:T(8,128)(2,1)}, u32[]{:S(2)}) copy-start(bf16[192,768]{1,0:T(8,128)(2,1)} %copy-done.4) | copy-start | bytes 884740
  191.8 18.7 %collective-permute-start.21 = (bf16[192,768]{1,0:T(8,128)(2,1)S(1)}, bf16[192,768]{1,0:T(8,128)(2,1)S(1)}, u32[]{:S(2)}, u32[]{:S(2)}) collective-permute-start(bf16[192,768]{1,0:T(8,128)(2,1)S(1)} %copy-done.5), channel_id=1, source_target_pairs={{0,4},{4,0},{8,12},{12,8},{16,20},{20,16},{24,28},{28,24},{1,5},{5... | collective-permute-start | bytes 884744 | tf_op jit(solution)/shard_map/ppermute | solution.py:507
  220.8 1.2 collective-permute-start.22
  222.6 4.8 %collective-permute-start.23 = (f32[8,1536]{1,0:T(8,128)S(1)}, f32[8,1536]{1,0:T(8,128)S(1)}, u32[]{:S(2)}, u32[]{:S(2)}) collective-permute-start(f32[8,1536]{1,0:T(8,128)S(1)} %shard_map.94.refs_2_), channel_id=1, source_target_pairs={{0,1},{1,0},{2,3},{3,2},{4,5},{5,4},{6,7},{7,6},{8,9},{9,8},{10,11... | collective-permute-start | bytes 147464 | tf_op jit(solution)/shard_map/ppermute | solution.py:553
  222.7 7.1 %collective-permute-start.24 = (f32[8,1536]{1,0:T(8,128)S(1)}, f32[8,1536]{1,0:T(8,128)S(1)}, u32[]{:S(2)}, u32[]{:S(2)}) collective-permute-start(f32[8,1536]{1,0:T(8,128)S(1)} %shard_map.94.refs_2_), channel_id=1, source_target_pairs={{0,2},{1,3},{2,0},{3,1},{4,6},{5,7},{6,4},{7,5},{8,10},{9,11},{10,... | collective-permute-start | bytes 147464 | tf_op jit(solution)/shard_map/ppermute | solution.py:553
  224.6 5.9 %collective-permute-start.25 = (f32[8,1536]{1,0:T(8,128)S(1)}, f32[8,1536]{1,0:T(8,128)S(1)}, u32[]{:S(2)}, u32[]{:S(2)}) collective-permute-start(f32[8,1536]{1,0:T(8,128)S(1)} %shard_map.94.refs_2_), channel_id=1, source_target_pairs={{0,3},{1,2},{2,1},{3,0},{4,7},{5,6},{6,5},{7,4},{8,11},{9,10},{10,... | collective-permute-start | bytes 147464 | tf_op jit(solution)/shard_map/ppermute | solution.py:553
  236.6 1.4 copy-start
  237.9 44.7 %collective-permute-start.26 = (bf16[720,512]{1,0:T(8,128)(2,1)S(1)}, bf16[720,512]{1,0:T(8,128)(2,1)S(1)}, u32[]{:S(2)}, u32[]{:S(2)}) collective-permute-start(bf16[720,512]{1,0:T(8,128)(2,1)S(1)} %get-tuple-element.74), channel_id=1, source_target_pairs={{0,8},{4,12},{8,0},{12,4},{16,24},{20,28},{24,16},{28,20},{1,9},{5... | collective-permute-start | bytes 2211848 | tf_op jit(solution)/shard_map/ppermute | solution.py:507
  247.4 35.2 %collective-permute-start.27 = (bf16[720,512]{1,0:T(8,128)(2,1)S(1)}, bf16[720,512]{1,0:T(8,128)(2,1)S(1)}, u32[]{:S(2)}, u32[]{:S(2)}) collective-permute-start(bf16[720,512]{1,0:T(8,128)(2,1)S(1)} %get-tuple-element.75), channel_id=1, source_target_pairs={{0,16},{4,20},{8,24},{12,28},{16,0},{20,4},{24,8},{28,12},{1,17},{... | collective-permute-start | bytes 2211848 | tf_op jit(solution)/shard_map/ppermute | solution.py:507
  256.4 10.3 %collective-permute-start.33 = (f32[64,720]{1,0:T(8,128)S(1)}, f32[64,720]{1,0:T(8,128)S(1)}, u32[]{:S(2)}, u32[]{:S(2)}) collective-permute-start(f32[64,720]{1,0:T(8,128)S(1)} %get-tuple-element.85), channel_id=1, source_target_pairs={{0,8},{4,12},{8,0},{12,4},{16,24},{20,28},{24,16},{28,20},{1,9},{5... | collective-permute-start | bytes 552968 | tf_op jit(solution)/shard_map/ppermute | solution.py:507
  266.7 5.7 %collective-permute-start.34 = (f32[64,720]{1,0:T(8,128)S(1)}, f32[64,720]{1,0:T(8,128)S(1)}, u32[]{:S(2)}, u32[]{:S(2)}) collective-permute-start(f32[64,720]{1,0:T(8,128)S(1)} %add.40), channel_id=1, source_target_pairs={{0,16},{4,20},{8,24},{12,28},{16,0},{20,4},{24,8},{28,12},{1,17},{... | collective-permute-start | bytes 552968 | tf_op jit(solution)/shard_map/ppermute | solution.py:507
  266.8 26.0 %collective-permute-start.30 = (bf16[720,512]{1,0:T(8,128)(2,1)}, bf16[720,512]{1,0:T(8,128)(2,1)S(1)}, u32[]{:S(2)}, u32[]{:S(2)}) collective-permute-start(bf16[720,512]{1,0:T(8,128)(2,1)} %get-tuple-element.82), channel_id=1, source_target_pairs={{0,4},{4,0},{8,12},{12,8},{16,20},{20,16},{24,28},{28,24},{1,5},{5... | collective-permute-start | bytes 2211848 | tf_op jit(solution)/shard_map/ppermute | solution.py:507
  272.5 18.8 %collective-permute-start.35 = (f32[64,720]{1,0:T(8,128)S(1)}, f32[64,720]{1,0:T(8,128)S(1)}, u32[]{:S(2)}, u32[]{:S(2)}) collective-permute-start(f32[64,720]{1,0:T(8,128)S(1)} %add.41), channel_id=1, source_target_pairs={{0,4},{4,0},{8,12},{12,8},{16,20},{20,16},{24,28},{28,24},{1,5},{5... | collective-permute-start | bytes 552968 | tf_op jit(solution)/shard_map/ppermute | solution.py:507
  280.4 1.1 copy-start.2
  281.5 1.2 copy-start.3
  287.7 19.5 %collective-permute-start.28 = (bf16[720,512]{1,0:T(8,128)(2,1)}, bf16[720,512]{1,0:T(8,128)(2,1)S(1)}, u32[]{:S(2)}, u32[]{:S(2)}) collective-permute-start(bf16[720,512]{1,0:T(8,128)(2,1)} %get-tuple-element.80), channel_id=1, source_target_pairs={{0,16},{4,12},{8,24},{12,4},{16,0},{20,28},{24,8},{28,20},{1,17},{... | collective-permute-start | bytes 2211848 | tf_op jit(solution)/shard_map/ppermute | solution.py:511
  287.7 19.5 %collective-permute-start.31 = (bf16[720,512]{1,0:T(8,128)(2,1)}, bf16[720,512]{1,0:T(8,128)(2,1)S(1)}, u32[]{:S(2)}, u32[]{:S(2)}) collective-permute-start(bf16[720,512]{1,0:T(8,128)(2,1)} %get-tuple-element.83), channel_id=1, source_target_pairs={{0,12},{4,16},{8,4},{12,24},{16,28},{20,0},{24,20},{28,8},{1,13},{... | collective-permute-start | bytes 2211848 | tf_op jit(solution)/shard_map/ppermute | solution.py:511
  289.6 33.0 %collective-permute-start.29 = (bf16[720,512]{1,0:T(8,128)(2,1)}, bf16[720,512]{1,0:T(8,128)(2,1)S(1)}, u32[]{:S(2)}, u32[]{:S(2)}) collective-permute-start(bf16[720,512]{1,0:T(8,128)(2,1)} %get-tuple-element.81), channel_id=1, source_target_pairs={{0,8},{4,20},{8,0},{12,28},{16,24},{20,4},{24,16},{28,12},{1,9},{5... | collective-permute-start | bytes 2211848 | tf_op jit(solution)/shard_map/ppermute | solution.py:511
  291.3 31.3 %collective-permute-start.32 = (bf16[720,512]{1,0:T(8,128)(2,1)}, bf16[720,512]{1,0:T(8,128)(2,1)}, u32[]{:S(2)}, u32[]{:S(2)}) collective-permute-start(bf16[720,512]{1,0:T(8,128)(2,1)} %get-tuple-element.84), channel_id=1, source_target_pairs={{0,20},{4,8},{8,28},{12,0},{16,4},{20,24},{24,12},{28,16},{1,21},{... | collective-permute-start | bytes 2211848 | tf_op jit(solution)/shard_map/ppermute | solution.py:511

commit v3 on v2

--- a/solution.py
+++ b/solution.py
@@ -11,7 +11,7 @@
 NT = (((1,), (1,)), ((), ()))
 F32, BF16, I32 = jnp.float32, jnp.bfloat16, jnp.int32
 CODE = 128
-VMEM_BYTES = 50 * 1024 * 1024
+MIB = 1024 * 1024
 
 
 def mm(a, b, dims):
@@ -26,7 +26,7 @@
     return hi, mid, low
 
 
-def call(body, grid, in_specs, out_specs, out_shape, scratch=(), alias=None, flops=0, moved=0):
+def call(body, grid, in_specs, out_specs, out_shape, scratch=(), alias=None, flops=0, moved=0, room=24):
     return pl.pallas_call(
         body,
         grid_spec=pltpu.PrefetchScalarGridSpec(
@@ -38,7 +38,7 @@
         ),
         out_shape=out_shape,
         input_output_aliases=alias or {},
-        compiler_params=pltpu.CompilerParams(vmem_limit_bytes=VMEM_BYTES),
+        compiler_params=pltpu.CompilerParams(vmem_limit_bytes=room * MIB),
         cost_estimate=pl.CostEstimate(flops=flops, bytes_accessed=moved, transcendentals=0),
     )
 
@@ -55,7 +55,7 @@
         out_ref[start : start + step, :] = jnp.where(index == wanted, 1.0, 0.0).astype(BF16)
 
 
-def places_of(dest, shard_rows, cap, dom):
+def places_of(dest, shard_rows, cap, dom, device):
     hold = dest.shape[1]
     low = lax.broadcasted_iota(I32, (dom, hold), 0) * shard_rows
     inside = jnp.logical_and(dest >= low, dest < low + shard_rows)
@@ -66,7 +66,8 @@
         I32, (lanes, lanes), 1
     )
     upper = jnp.where(before, 1.0, 0.0).astype(BF16)
-    carry = lax.broadcasted_iota(I32, (dom, 1), 0).astype(F32) * cap + 1.0
+    apart = lax.broadcasted_iota(I32, (dom, 1), 0) ^ device
+    carry = apart.astype(F32) * cap + 1.0
     found = []
     for start in range(0, hold, lanes):
         part = marks[:, start : start + lanes]
@@ -76,9 +77,10 @@
     return jnp.concatenate(found, axis=1).astype(I32) - 1, local
 
 
-def pack_first_body(dom, shard_rows, cap, meta, dest_ref, bin_ref, raw_ref, out_ref, place_ref, pick):
+def pack_first_body(dom, shard_rows, cap, meta, dest_ref, bin_ref, raw_ref, *refs):
+    outs, (place_ref, pick) = refs[:dom], refs[dom:]
     dest = dest_ref[...]
-    place, local = places_of(dest, shard_rows, cap, dom)
+    place, local = places_of(dest, shard_rows, cap, dom, meta[0])
     place_ref[...] = place
     one_hot_rows(pick, place)
     which = lax.broadcasted_iota(I32, (CODE, dest.shape[1]), 0)
@@ -88,13 +90,19 @@
         jnp.where(which == 1, local & 15, jnp.where(which == 2, bin_ref[...], jnp.where(which == 3, 1, 0))),
     )
     digits = jnp.where(dest >= 0, digits, 0).astype(F32).astype(BF16)
-    out_ref[:, :CODE] = mm(pick[...], digits, NT).astype(BF16)
-    out_ref[:, CODE:] = mm(pick[...], raw_ref[...], NN).astype(BF16)
-
-
-def pack_next_body(meta, place_ref, raw_ref, out_ref, pick):
+    codes = mm(pick[...], digits, NT).astype(BF16)
+    packed = mm(pick[...], raw_ref[...], NN).astype(BF16)
+    for index, out_ref in enumerate(outs):
+        out_ref[:, :CODE] = codes[index * cap : (index + 1) * cap]
+        out_ref[:, CODE:] = packed[index * cap : (index + 1) * cap]
+
+
+def pack_next_body(cap, meta, place_ref, raw_ref, *refs):
+    outs, pick = refs[:-1], refs[-1]
     one_hot_rows(pick, place_ref[...])
-    out_ref[...] = mm(pick[...], raw_ref[...], NN).astype(BF16)
+    packed = mm(pick[...], raw_ref[...], NN).astype(BF16)
+    for index, out_ref in enumerate(outs):
+        out_ref[...] = packed[index * cap : (index + 1) * cap]
 
 
 def pack_first(meta, raw_images, dest, bins, dom, width, at):
@@ -106,8 +114,8 @@
         functools.partial(pack_first_body, dom, hold // 2, cap),
         (1,),
         [row, row, pl.BlockSpec((hold, width), lambda j, m: (0, at(m)))],
-        [pl.BlockSpec((slots, CODE + width), lambda j, m: (0, 0)), row],
-        [sds((slots, CODE + width), BF16), sds((1, hold), I32)],
+        [pl.BlockSpec((cap, CODE + width), lambda j, m: (0, 0))] * dom + [row],
+        [sds((cap, CODE + width), BF16)] * dom + [sds((1, hold), I32)],
         scratch=[pltpu.VMEM((slots, hold), BF16)],
         flops=2 * slots * hold * width,
         moved=4 * hold * width,
@@ -116,16 +124,17 @@
 
 def pack_next(meta, raw_images, place, dom, width, at):
     hold, _ = raw_images.shape
-    slots = dom * (hold // dom)
+    cap = hold // dom
+    slots = dom * cap
     return call(
-        pack_next_body,
+        functools.partial(pack_next_body, cap),
         (1,),
         [
             pl.BlockSpec((1, hold), lambda j, m: (0, 0)),
             pl.BlockSpec((hold, width), lambda j, m: (0, at(m))),
         ],
-        pl.BlockSpec((slots, width), lambda j, m: (0, 0)),
-        sds((slots, width), BF16),
+        [pl.BlockSpec((cap, width), lambda j, m: (0, 0))] * dom,
+        [sds((cap, width), BF16)] * dom,
         scratch=[pltpu.VMEM((slots, hold), BF16)],
         flops=2 * slots * hold * width,
         moved=4 * hold * width,
@@ -138,7 +147,16 @@
     out_ref[...] = (mm(pick, recv, NN) * factor).astype(BF16)
 
 
-def unpack_first_body(bins, meta, recv_ref, ctf_ref, inv_ref, out_ref, hot_ref, pick, wide):
+def gather(pieces, whole):
+    rows = pieces[0].shape[0]
+    for index, piece in enumerate(pieces):
+        whole[index * rows : (index + 1) * rows, :] = piece[...]
+
+
+def unpack_first_body(dom, bins, meta, *refs):
+    recv_ref = refs[-1]
+    gather(refs[:dom], recv_ref)
+    ctf_ref, inv_ref, out_ref, hot_ref, pick, wide = refs[dom:-1]
     shard_rows = out_ref.shape[0]
     chosen = jnp.where(
         lax.broadcasted_iota(I32, (8, CODE), 0) == lax.broadcasted_iota(I32, (8, CODE), 1), 1.0, 0.0
@@ -156,12 +174,17 @@
     weigh(pick[...], wide[...], recv_ref[:, CODE:], ctf_ref, inv_ref, out_ref)
 
 
-def unpack_next_body(meta, pick_ref, wide_ref, recv_ref, ctf_ref, inv_ref, out_ref):
+def unpack_next_body(dom, meta, *refs):
+    recv_ref = refs[-1]
+    gather(refs[:dom], recv_ref)
+    pick_ref, wide_ref, ctf_ref, inv_ref, out_ref = refs[dom:-1]
     weigh(pick_ref[...], wide_ref[...], recv_ref[...], ctf_ref, inv_ref, out_ref)
 
 
 def unpack_first(meta, recv, ctf, inv, at):
-    slots, columns = recv.shape
+    cap, columns = recv[0].shape
+    dom = len(recv)
+    slots = dom * cap
     width = columns - CODE
     rows = slots // 2
     bins, pix = ctf.shape
@@ -169,41 +192,45 @@
     whole = lambda shape: pl.BlockSpec(shape, lambda j, m: (0, 0))
     shapes = [(rows, width), (3 * bins, rows), (rows, slots), (rows, 3 * bins)]
     return call(
-        functools.partial(unpack_first_body, bins),
+        functools.partial(unpack_first_body, dom, bins),
         (1,),
-        [
-            whole(recv.shape),
+        [whole(recv[0].shape)] * dom
+        + [
             pl.BlockSpec((bins, width), lambda j, m: (0, lax.rem(at(m), wrap))),
             pl.BlockSpec((1, width), lambda j, m: (0, lax.rem(at(m), wrap))),
         ],
         [whole(s) for s in shapes],
         [sds(s, BF16) for s in shapes],
+        scratch=[pltpu.VMEM((slots, columns), BF16)],
         flops=2 * slots * rows * width,
         moved=2 * slots * columns,
-    )(meta, recv, ctf, inv)
+    )(meta, *recv, ctf, inv)
 
 
 def unpack_next(meta, pick, wide, recv, ctf, inv, at):
-    slots, width = recv.shape
+    cap, width = recv[0].shape
+    dom = len(recv)
+    slots = dom * cap
     rows = slots // 2
     bins, pix = ctf.shape
     wrap = pix // width
     whole = lambda shape: pl.BlockSpec(shape, lambda j, m: (0, 0))
     return call(
-        unpack_next_body,
+        functools.partial(unpack_next_body, dom),
         (1,),
-        [
+        [whole(recv[0].shape)] * dom
+        + [
             whole(pick.shape),
             whole(wide.shape),
-            whole(recv.shape),
             pl.BlockSpec((bins, width), lambda j, m: (0, lax.rem(at(m), wrap))),
             pl.BlockSpec((1, width), lambda j, m: (0, lax.rem(at(m), wrap))),
         ],
         whole((rows, width)),
         sds((rows, width), BF16),
+        scratch=[pltpu.VMEM((slots, width), BF16)],
         flops=2 * slots * rows * width,
         moved=2 * slots * width,
-    )(meta, pick, wide, recv, ctf, inv)
+    )(meta, *recv, pick, wide, ctf, inv)
 
 
 def energy_body(bins, count, meta, *refs):
@@ -515,15 +542,22 @@
 
     width = columns // turns // 2
     dest, bin_row = dest_row[None, :], defocus_bin[None, :]
-    send_a, place = pack_first(meta, raw_images, dest, bin_row, dom, width, lambda m: 2 * m[1])
-    recv_a = lax.all_to_all(send_a, "dom", 0, 0, tiled=True)
+    def exchange(blocks):
+        got = [blocks[0]] + [None] * (dom - 1)
+        for apart in (6, 7, 2, 4, 3, 5, 1):
+            got[apart] = across(blocks[apart], apart)
+        return got
+
+    *send_a, place = pack_first(meta, raw_images, dest, bin_row, dom, width, lambda m: 2 * m[1])
+    recv_a = exchange(send_a)
     send_b = pack_next(meta, raw_images, place, dom, width, lambda m: 2 * m[1] + 1)
-    recv_b = lax.all_to_all(send_b, "dom", 0, 0, tiled=True)
+    recv_b = exchange(send_b)
 
     count = panels.shape[0] // 2
     pieces = [None] * 8
     pieces[0] = lax.dynamic_slice_in_dim(panels, core * count, count, 0)
     pieces[1] = across(lax.dynamic_slice_in_dim(panels, (1 - core) * count, count, 0), 1)
+    recv_a[1], *pieces[:2] = lax.optimization_barrier((recv_a[1], *pieces[:2]))
     pieces[2], pieces[4] = across(pieces[0], 2), across(pieces[0], 4)
     pieces[3], pieces[5] = across(pieces[1], 2), across(pieces[1], 4)
 
@@ -531,11 +565,11 @@
     share_b = unpack_next(meta, pick, wide, recv_b, ctf_table, inv, lambda m: 2 * m[1] + 1)
     hots = (hot, across(hot, 1))
     a1, b1 = onward(share_a), onward(share_b)
-    a1, *pieces[2:6] = lax.optimization_barrier((a1, *pieces[2:6]))
+    b1, *pieces[2:6] = lax.optimization_barrier((b1, *pieces[2:6]))
     pieces[6], pieces[7] = across(pieces[2], 4), across(pieces[5], 2)
     a2, b2 = onward(a1), onward(b1)
-    a2, *pieces[6:8] = lax.optimization_barrier((a2, *pieces[6:8]))
     panel_full, extra = energy(meta, pieces, ctf_table, inv)
+    b2, panel_full, extra = lax.optimization_barrier((b2, panel_full, extra))
     a3, b3 = onward(a2), onward(b2)
 
     own = [(share_a, share_b), (a1, b1), (a2, b2), (a3, b3)]
@@ -543,6 +577,8 @@
     for turn in range(turns - 1):
         sib = [across(value, 1) for value in own[turn]]
         acc, full = score(meta, turn, turns, own[turn], sib, panel_full, acc, full)
+    a3, b3, acc, full = lax.optimization_barrier((a3, b3, acc, full))
+    own[-1] = (a3, b3)
     sib = [across(value, 1) for value in own[-1]]
     shifted, stat, full = score(
         meta, turns - 1, turns, own[-1], sib, panel_full, acc, full, hots, extra
@@ -560,7 +596,9 @@
         meta, "mass", 4, 3, full, post=post, hots=hots, bins=bins
     )
     a_sum, b_sum, keep = class_part(meta, "rest", 7, 3, full, post=post)
-    got_x, got_y, send_c, send_d = lax.optimization_barrier((got_x, got_y, send_c, send_d))
+    got_x, got_y, send_c, send_d, a_sum, b_sum, keep = lax.optimization_barrier(
+        (got_x, got_y, send_c, send_d, a_sum, b_sum, keep)
+    )
     got_c, got_d = by_core(send_c, 2, 4), by_core(send_d, 5, 3)
     message_a, message_b = forward(meta, a_sum, b_sum, got_x, got_y)
     got_a, got_b = by_core(message_a, 4, 2), by_core(message_b, 3, 5)

time: 332 us -> 294 us (0.89)
  Pallas kernels: 103 us -> 69.7 us
  local copies, waits for them, and re-layouts: 17.6 us -> 8.41 us
  waiting for transfers between devices: 161 us -> 167 us
    ppermute x23 -> x37, waiting for transfers between devices: 59.2 us -> 98.1 us  [across(): return lax.ppermute(value, 'dom', [(i, i ^ apart) for i in range(dom)])]
    all_to_all x2 -> x0, waiting for transfers between devices: 27.9 us -> none  [the longest x1 19.5 us: two_by_two(): recv_a = lax.all_to_all(send_a, 'dom', 0, 0, tiled=True)]
    pallas_call x4, Pallas kernels: 36.4 us -> 22.6 us  [score(): call(functools.partial(score_body, first, last), (2 * half,), in_specs, o...]
    ppermute x23 -> x37, starting transfers between devices: 19.5 us -> 30.6 us  [across(): return lax.ppermute(value, 'dom', [(i, i ^ apart) for i in range(dom)])]
    all_to_all x2 -> x0, starting transfers between devices: 8.88 us -> none  [the longest x1 5.17 us: two_by_two(): recv_a = lax.all_to_all(send_a, 'dom', 0, 0, tiled=True)]
    unnamed x38 -> x12, local copies, waits for them, and re-layouts: 13.5 us -> 4.62 us
    pallas_call x3, Pallas kernels: 22.8 us -> 15.3 us  [class_part(): call(functools.partial(class_body, kind, steps), (steps,), in_specs, out_...]
    pallas_call x3, Pallas kernels: 14.7 us -> 9.17 us  [the longest x1 3.87 us: unpack_first(): call(functools.partial(unpack_first_body, dom, bins), (1,), [whole(recv[0...]
  transfers between devices with their start and end apart: 38 -> 50, of which waited for: 20 -> 22; matrix products, arithmetic and copies ran while one was open for 1% -> 1% of each run, Pallas kernels for 22% -> 17%
where the time goes in v3:
time: 294 us; the launch traced here: 293 us
  waiting for transfers between devices  167 us (57%)
  Pallas kernels  69.7 us (24%)
  starting transfers between devices  46.4 us (16%)
  local copies, waits for them, and re-layouts  8.41 us (3%)
    ppermute x37, waiting for transfers between devices, across(): return lax.ppermute(value, 'dom', [(i, i ^ apart) for i in range(dom)])  98.1 us
    ppermute x6, waiting for transfers between devices, onward(): lax.ppermute(value, 'rot', [(i, (i + 1) % turns) for i in range(turns)])  35.4 us
    ppermute x37, starting transfers between devices, across(): return lax.ppermute(value, 'dom', [(i, i ^ apart) for i in range(dom)])  30.6 us
    ppermute x4, waiting for transfers between devices, by_core(): return lax.ppermute(value, 'dom', pairs)  30 us
    pallas_call x4, Pallas kernels, score(): call(functools.partial(score_body, first, last), (2 * half,), in_specs, o...  22.6 us
    pallas_call x3, Pallas kernels, class_part(): call(functools.partial(class_body, kind, steps), (steps,), in_specs, out_...  15.3 us
    ppermute x6, starting transfers between devices, onward(): lax.ppermute(value, 'rot', [(i, (i + 1) % turns) for i in range(turns)])  7.83 us
    pallas_call x1, Pallas kernels, finish(): call(finish_body, (2 * half,), [front] * 3 + [back] * 3, pl.BlockSpec((ti...  7.72 us
  transfers between devices with their start and end apart: 50, of which 22 were waited for; matrix products, arithmetic and copies ran while one was open for 1% of the time, Pallas kernels for 17%

profile of v3, /device:TPU:0, one launch (start us, length us, event | category | flops | bytes accessed | tf_op | source)
XLA Modules:
  0.0 293.5 jit_solution(16553740791539708901)
XLA Ops:
  0.7 2.3 constant_dynamic-slice_fusion
  3.4 0.7 broadcast_in_dim.10.bin_ref
  4.9 4.6 %copy-done = bf16[1536,4096]{1,0:T(8,128)(2,1)S(1)} copy-done((bf16[1536,4096]{1,0:T(8,128)(2,1)S(1)}, bf16[1536,4096]{1,0:T(8,128)(2,1)}, u32[]{:S(2)}) %copy-start) | copy-done | bytes 12582936
  9.5 4.5 %shard_map.85 = (bf16[192,640]{1,0:T(8,128)(2,1)S(1)}, bf16[192,640]{1,0:T(8,128)(2,1)S(1)}, bf16[192,640]{1,0:T(8,128)(2,1)S(1)}, bf16[192,640]{1,0:T(8,128)(2,...) custom-call(s32[10]{0:T(128)S(1)} %stack.43.meta, ...), custom_call_target="tpu_custom_call" | custom-call | flops 2415919104 | bytes 3145728 | tf_op jit(solution)/shard_map/pallas_call | solution.py:113
  14.1 3.2 %shard_map.87 = (bf16[192,512]{1,0:T(8,128)(2,1)S(1)}, bf16[192,512]{1,0:T(8,128)(2,1)S(1)}, bf16[192,512]{1,0:T(8,128)(2,1)S(1)}, bf16[192,512]{1,0:T(8,128)(2,...) custom-call(s32[10]{0:T(128)S(1)} %stack.43.meta, ...), custom_call_target="tpu_custom_call" | custom-call | flops 2415919104 | bytes 3145728 | tf_op jit(solution)/shard_map/pallas_call | solution.py:129
  17.4 2.9 %collective-permute-start.12 = (bf16[192,512]{1,0:T(8,128)(2,1)S(1)}, bf16[192,512]{1,0:T(8,128)(2,1)S(1)}, u32[]{:S(2)}, u32[]{:S(2)}) collective-permute-start(bf16[192,512]{1,0:T(8,128)(2,1)S(1)} %get-tuple-element.83), channel_id=1, source_target_pairs={{0,8},{4,12},{8,0},{12,4},{16,24},{20,28},{24,16},{28,20},{1,9},{5... | collective-permute-start | bytes 589832 | tf_op jit(solution)/shard_map/ppermute | solution.py:534
  20.5 1.7 collective-permute-start.13
  22.2 3.8 %collective-permute-done.12.refs_2_ = bf16[192,512]{1,0:T(8,128)(2,1)S(1)} collective-permute-done((bf16[192,512]{1,0:T(8,128)(2,1)S(1)}, bf16[192,512]{1,0:T(8,128)(2,1)S(1)}, u32[]{:S(2)}, u32[]{:S(2)}) %collective-permute-start.12) | collective-permute-done | bytes 196640 | tf_op jit(solution)/shard_map/ppermute | solution.py:534
  26.0 9.0 %collective-permute-done.13.refs_3_ = bf16[192,512]{1,0:T(8,128)(2,1)S(1)} collective-permute-done((bf16[192,512]{1,0:T(8,128)(2,1)S(1)}, bf16[192,512]{1,0:T(8,128)(2,1)S(1)}, u32[]{:S(2)}, u32[]{:S(2)}) %collective-permute-start.13) | collective-permute-done | bytes 196640 | tf_op jit(solution)/shard_map/ppermute | solution.py:534
  35.1 1.5 collective-permute-start.4
  36.6 0.7 collective-permute-start.5
  37.3 2.6 collective-permute-start.6
  40.0 3.0 %collective-permute-start.7 = (bf16[192,640]{1,0:T(8,128)(2,1)S(1)}, bf16[192,640]{1,0:T(8,128)(2,1)S(1)}, u32[]{:S(2)}, u32[]{:S(2)}) collective-permute-start(bf16[192,640]{1,0:T(8,128)(2,1)S(1)} %get-tuple-element.78), channel_id=1, source_target_pairs={{0,28},{4,24},{8,20},{12,16},{16,12},{20,8},{24,4},{28,0},{1,29},{... | collective-permute-start | bytes 737288 | tf_op jit(solution)/shard_map/ppermute | solution.py:534
  43.0 11.4 %collective-permute-done.4.refs_4_ = bf16[192,640]{1,0:T(8,128)(2,1)S(1)} collective-permute-done((bf16[192,640]{1,0:T(8,128)(2,1)S(1)}, bf16[192,640]{1,0:T(8,128)(2,1)S(1)}, u32[]{:S(2)}, u32[]{:S(2)}) %collective-permute-start.4) | collective-permute-done | bytes 245792 | tf_op jit(solution)/shard_map/ppermute | solution.py:534
  54.4 1.4 collective-permute-start.14
  55.8 3.7 %collective-permute-done.5.refs_5_ = bf16[192,640]{1,0:T(8,128)(2,1)S(1)} collective-permute-done((bf16[192,640]{1,0:T(8,128)(2,1)S(1)}, bf16[192,640]{1,0:T(8,128)(2,1)S(1)}, u32[]{:S(2)}, u32[]{:S(2)}) %collective-permute-start.5) | collective-permute-done | bytes 245792 | tf_op jit(solution)/shard_map/ppermute | solution.py:534
  59.5 1.3 collective-permute-start.15
  60.8 1.5 collective-permute-start.16
  62.3 1.4 collective-permute-start.17
  63.7 1.5 collective-permute-start.19
  65.2 3.9 %shard_map.86 = (bf16[768,512]{1,0:T(8,128)(2,1)S(1)}, bf16[192,768]{1,0:T(8,128)(2,1)S(1)}, bf16[768,1536]{1,0:T(8,128)(2,1)S(1)}, bf16[768,192]{1,0:T(8,128)(2,1)S(1)}) custom-call(s32[10]{0:T(128)S(1)} %stack.43.meta, bf16[192,640]{1,0:T(8,128)(2,1)S(1)} %get-tuple-element.70.refs_0_, bf16[192,640]{1,0:T(8,128)(2,1)S(1)} %collective-permute-done.refs_1_, ...), custom_call_target="tpu_custom_call" | custom-call | flops 1207959552 | bytes 1966080 | tf_op jit(solution)/shard_map/pallas_call | solution.py:194
  69.1 7.3 %collective-permute-done.15.refs_5_ = bf16[192,512]{1,0:T(8,128)(2,1)S(1)} collective-permute-done((bf16[192,512]{1,0:T(8,128)(2,1)S(1)}, bf16[192,512]{1,0:T(8,128)(2,1)S(1)}, u32[]{:S(2)}, u32[]{:S(2)}) %collective-permute-start.15) | collective-permute-done | bytes 196640 | tf_op jit(solution)/shard_map/ppermute | solution.py:534
  76.4 2.1 shard_map.88.refs_1_
  78.5 1.8 collective-permute-start.18
  80.3 0.7 collective-permute-start.20
  81.0 1.5 collective-permute-start.21
  83.1 5.5 %collective-permute-done.19.refs_2_ = bf16[720,512]{1,0:T(8,128)(2,1)S(1)} collective-permute-done((bf16[720,512]{1,0:T(8,128)(2,1)S(1)}, bf16[720,512]{1,0:T(8,128)(2,1)S(1)}, u32[]{:S(2)}, u32[]{:S(2)}) %collective-permute-start.19) | collective-permute-done | bytes 737312 | tf_op jit(solution)/shard_map/ppermute | solution.py:534
  88.6 1.6 collective-permute-start.8
  90.1 13.8 %collective-permute-done.20.refs_3_ = bf16[720,512]{1,0:T(8,128)(2,1)S(1)} collective-permute-done((bf16[720,512]{1,0:T(8,128)(2,1)S(1)}, bf16[720,512]{1,0:T(8,128)(2,1)S(1)}, u32[]{:S(2)}, u32[]{:S(2)}) %collective-permute-start.20) | collective-permute-done | bytes 737312 | tf_op jit(solution)/shard_map/ppermute | solution.py:534
  103.9 10.7 %collective-permute-done.22.refs_5_ = bf16[720,512]{1,0:T(8,128)(2,1)S(1)} collective-permute-done((bf16[720,512]{1,0:T(8,128)(2,1)S(1)}, bf16[720,512]{1,0:T(8,128)(2,1)S(1)}, u32[]{:S(2)}, u32[]{:S(2)}) %collective-permute-start.22) | collective-permute-done | bytes 737312 | tf_op jit(solution)/shard_map/ppermute | solution.py:534
  114.6 1.1 collective-permute-start.24
  115.7 1.7 collective-permute-start.25
  117.5 1.6 collective-permute-start.23
  119.1 1.6 collective-permute-start.9
  120.6 10.8 %collective-permute-done.24.refs_6_ = bf16[720,512]{1,0:T(8,128)(2,1)S(1)} collective-permute-done((bf16[720,512]{1,0:T(8,128)(2,1)S(1)}, bf16[720,512]{1,0:T(8,128)(2,1)S(1)}, u32[]{:S(2)}, u32[]{:S(2)}) %collective-permute-start.24) | collective-permute-done | bytes 737312 | tf_op jit(solution)/shard_map/ppermute | solution.py:534
  131.4 0.9 collective-permute-done.25.refs_7_
  132.3 7.4 %collective-permute-done.23.refs_1_ = bf16[768,512]{1,0:T(8,128)(2,1)S(1)} collective-permute-done((bf16[768,512]{1,0:T(8,128)(2,1)S(1)}, bf16[768,512]{1,0:T(8,128)(2,1)S(1)}, u32[]{:S(2)}, u32[]{:S(2)}) %collective-permute-start.23) | collective-permute-done | bytes 786464 | tf_op jit(solution)/shard_map/ppermute | solution.py:541
  139.8 6.8 %shard_map.89 = (bf16[720,4096]{1,0:T(8,128)(2,1)S(1)}, bf16[720,192]{1,0:T(8,128)(2,1)S(1)}) custom-call(s32[10]{0:T(128)S(1)} %stack.43.meta, bf16[720,512]{1,0:T(8,128)(2,1)S(1)} %get-tuple-element.91.refs_0_, bf16[720,512]{1,0:T(8,128)(2,1)S(1)} %collective-permute-done.1.refs_1_, bf16[720,512]{1,0:T(8,128)(2,1)S(1)} %collective-permute-done.19.refs_2_, ...), custom_call_target="tpu_custom_call" | custom-call | flops 4529848320 | bytes 11796480 | tf_op jit(solution)/shard_map/pallas_call | solution.py:269
  147.2 6.3 %collective-permute-done.9.refs_0_ = bf16[768,512]{1,0:T(8,128)(2,1)S(1)} collective-permute-done((bf16[768,512]{1,0:T(8,128)(2,1)S(1)}, bf16[768,512]{1,0:T(8,128)(2,1)S(1)}, u32[]{:S(2)}, u32[]{:S(2)}) %collective-permute-start.9) | collective-permute-done | bytes 786464 | tf_op jit(solution)/shard_map/ppermute | solution.py:541
  153.5 1.3 collective-permute-start.10
  154.9 4.9 %shard_map.90 = (f32[720,1536]{1,0:T(8,128)S(1)}, bf16[1536,4096]{1,0:T(8,128)(2,1)S(1)}) custom-call(s32[10]{0:T(128)S(1)} %stack.43.meta, bf16[768,512]{1,0:T(8,128)(2,1)S(1)} %get-tuple-element.79.refs_0_, bf16[768,512]{1,0:T(8,128)(2,1)S(1)} %shard_map.88.refs_1_, bf16[768,512]{1,0:T(8,128)(2,1)S(1)} %collective-permute-done.31.refs_2_, ...), custom_call_target="tpu_custom_call" | custom-call | flops 2264924160 | bytes 15138816 | tf_op jit(solution)/shard_map/pallas_call | solution.py:360
  159.8 5.3 %shard_map.91 = (f32[720,1536]{1,0:T(8,128)S(1)}, bf16[1536,4096]{1,0:T(8,128)(2,1)S(1)}) custom-call(s32[10]{0:T(128)S(1)} %stack.43.meta, bf16[768,512]{1,0:T(8,128)(2,1)S(1)} %collective-permute-done.8.refs_0_, bf16[768,512]{1,0:T(8,128)(2,1)S(1)} %collective-permute-done.18.refs_1_, ...), custom_call_target="tpu_custom_call", output_to_operand_aliasing={{0}: (6, {}), {1}: (7, {})} | custom-call | flops 2264924160 | bytes 15138816 | tf_op jit(solution)/shard_map/pallas_call | solution.py:360
  165.1 5.3 %shard_map.92 = (f32[720,1536]{1,0:T(8,128)S(1)}, bf16[1536,4096]{1,0:T(8,128)(2,1)S(1)}) custom-call(s32[10]{0:T(128)S(1)} %stack.43.meta, bf16[768,512]{1,0:T(8,128)(2,1)S(1)} %collective-permute-done.9.refs_0_, bf16[768,512]{1,0:T(8,128)(2,1)S(1)} %collective-permute-done.23.refs_1_, ...), custom_call_target="tpu_custom_call", output_to_operand_aliasing={{0}: (6, {}), {1}: (7, {})} | custom-call | flops 2264924160 | bytes 15138816 | tf_op jit(solution)/shard_map/pallas_call | solution.py:360
  170.4 5.2 %collective-permute-done.26.refs_1_ = bf16[768,512]{1,0:T(8,128)(2,1)S(1)} collective-permute-done((bf16[768,512]{1,0:T(8,128)(2,1)S(1)}, bf16[768,512]{1,0:T(8,128)(2,1)S(1)}, u32[]{:S(2)}, u32[]{:S(2)}) %collective-permute-start.26) | collective-permute-done | bytes 786464 | tf_op jit(solution)/shard_map/ppermute | solution.py:541
  175.7 16.5 %collective-permute-done.10.refs_0_ = bf16[768,512]{1,0:T(8,128)(2,1)S(1)} collective-permute-done((bf16[768,512]{1,0:T(8,128)(2,1)S(1)}, bf16[768,512]{1,0:T(8,128)(2,1)S(1)}, u32[]{:S(2)}, u32[]{:S(2)}) %collective-permute-start.10) | collective-permute-done | bytes 786464 | tf_op jit(solution)/shard_map/ppermute | solution.py:541
  192.6 3.3 %collective-permute-done.35.refs_8_.refs_2_ = bf16[192,768]{1,0:T(8,128)(2,1)S(1)} collective-permute-done((bf16[192,768]{1,0:T(8,128)(2,1)S(1)}, bf16[192,768]{1,0:T(8,128)(2,1)S(1)}, u32[]{:S(2)}, u32[]{:S(2)}) %collective-permute-start.35) | collective-permute-done | bytes 294944 | tf_op jit(solution)/shard_map/ppermute | solution.py:534
  196.0 7.1 %shard_map.93 = (f32[720,1536]{1,0:T(8,128)S(1)}, f32[8,1536]{1,0:T(8,128)S(1)}, bf16[1536,4096]{1,0:T(8,128)(2,1)S(1)}) custom-call(s32[10]{0:T(128)S(1)} %stack.43.meta, bf16[768,512]{1,0:T(8,128)(2,1)S(1)} %collective-permute-done.10.refs_0_, bf16[768,512]{1,0:T(8,128)(2,1)S(1)} %collective-permute-done.26.refs_1_, ...), custom_call_target="tpu_custom_call", output_to_operand_aliasing={{0}: (6, {}), {2}: (7, {})} | custom-call | flops 2264924160 | bytes 15138816 | tf_op jit(solution)/shard_map/pallas_call | solution.py:360
  203.3 1.1 collective-permute-done.36.other_ref
  205.1 4.3 %collective-permute-start.39 = (f32[8,1536]{1,0:T(8,128)S(1)}, f32[8,1536]{1,0:T(8,128)S(1)}, u32[]{:S(2)}, u32[]{:S(2)}) collective-permute-start(f32[8,1536]{1,0:T(8,128)S(1)} %shard_map.94.refs_2_), channel_id=1, source_target_pairs={{0,3},{1,2},{2,1},{3,0},{4,7},{5,6},{6,5},{7,4},{8,11},{9,10},{10,... | collective-permute-start | bytes 147464 | tf_op jit(solution)/shard_map/ppermute | solution.py:589
  209.7 2.7 collective-permute-done.38.refs_4_
  212.4 3.5 %shard_map.95 = (bf16[720,512]{1,0:T(8,128)(2,1)S(1)}, bf16[720,512]{1,0:T(8,128)(2,1)S(1)}, bf16[720,1536]{1,0:T(8,128)(2,1)S(1)}, f32[1,768]{1,0:T(1,128)S(1)}) custom-call(s32[10]{0:T(128)S(1)} %stack.43.meta, f32[720,1536]{1,0:T(8,128)S(1)} %get-tuple-element.114.refs_0_, f32[8,1536]{1,0:T(8,128)S(1)} %get-tuple-element.115.mine_ref.refs_1_, ...), custom_call_target="tpu_custom_call" | custom-call | flops 2264924160 | bytes 10518528 | tf_op jit(solution)/shard_map/pallas_call | solution.py:446
  216.3 0.8 collective-permute-start.41
  217.1 6.9 %shard_map.96 = (bf16[720,512]{1,0:T(8,128)(2,1)}, bf16[720,512]{1,0:T(8,128)(2,1)}, bf16[720,512]{1,0:T(8,128)(2,1)}, f32[64,720]{1,0:T(8,128)S(1)}) custom-call(s32[10]{0:T(128)S(1)} %stack.43.meta, bf16[720,1536]{1,0:T(8,128)(2,1)S(1)} %get-tuple-element.119.refs_0_, bf16[192,768]{1,0:T(8,128)(2,1)S(1)} %get-tuple-element.112.refs_7_.refs_1_, ...), custom_call_target="tpu_custom_call" | custom-call | flops 3397386240 | bytes 13565952 | tf_op jit(solution)/shard_map/pallas_call | solution.py:446
  224.0 1.4 collective-permute-start.47
  225.5 11.6 %collective-permute-done.47 = f32[64,720]{1,0:T(8,128)S(1)} collective-permute-done((f32[64,720]{1,0:T(8,128)S(1)}, f32[64,720]{1,0:T(8,128)S(1)}, u32[]{:S(2)}, u32[]{:S(2)}) %collective-permute-start.47) | collective-permute-done | bytes 184352 | tf_op jit(solution)/shard_map/ppermute | solution.py:534
  237.6 5.2 %collective-permute-done.48 = f32[64,720]{1,0:T(8,128)S(1)} collective-permute-done((f32[64,720]{1,0:T(8,128)S(1)}, f32[64,720]{1,0:T(8,128)S(1)}, u32[]{:S(2)}, u32[]{:S(2)}) %collective-permute-start.48) | collective-permute-done | bytes 184352 | tf_op jit(solution)/shard_map/ppermute | solution.py:534
  242.9 4.9 %shard_map.97 = (f32[720,512]{1,0:T(8,128)S(1)}, f32[720,512]{1,0:T(8,128)S(1)}, f32[720,512]{1,0:T(8,128)S(1)}) custom-call(s32[10]{0:T(128)S(1)} %stack.43.meta, bf16[720,1536]{1,0:T(8,128)(2,1)S(1)} %get-tuple-element.119.refs_0_, bf16[1536,4096]{1,0:T(8,128)(2,1)S(1)} %get-tuple-element.116.refs_6_.refs_3_.refs_1_), custom_call_target="tpu_custom_call" | custom-call | flops 3397386240 | bytes 13565952 | tf_op jit(solution)/shard_map/pallas_call | solution.py:446
  247.9 2.9 shard_map.98
  251.3 1.3 collective-permute-start.45
  252.9 1.3 collective-permute-start.46
  254.9 0.9 maximum_select_fusion
  255.8 14.5 %collective-permute-done.42.a_ref = bf16[720,512]{1,0:T(8,128)(2,1)S(1)} collective-permute-done((bf16[720,512]{1,0:T(8,128)(2,1)}, bf16[720,512]{1,0:T(8,128)(2,1)S(1)}, u32[]{:S(2)}, u32[]{:S(2)}) %collective-permute-start.42) | collective-permute-done | bytes 737312 | tf_op jit(solution)/shard_map/ppermute | solution.py:538
  270.3 15.4 %collective-permute-done.43.c_ref = bf16[720,512]{1,0:T(8,128)(2,1)} collective-permute-done((bf16[720,512]{1,0:T(8,128)(2,1)}, bf16[720,512]{1,0:T(8,128)(2,1)}, u32[]{:S(2)}, u32[]{:S(2)}) %collective-permute-start.43) | collective-permute-done | bytes 737312 | tf_op jit(solution)/shard_map/ppermute | solution.py:538
  285.8 7.7 %shard_map.99 = f32[1440,512]{1,0:T(8,128)} custom-call(s32[10]{0:T(128)S(1)} %stack.43.meta, f32[720,512]{1,0:T(8,128)S(1)} %get-tuple-element.125.keep_ref, bf16[720,512]{1,0:T(8,128)(2,1)S(1)} %collective-permute-done.42.a_ref, bf16[720,512]{1,0:T(8,128)(2,1)} %collective-permute-done.43.c_ref, bf16[720,512]{1,0:T(8,128)(2,1)S(1)} %collective-permute-done.44.other_ref, ...), custom_call_target="tpu_custom_call" | custom-call | tf_op jit(solution)/shard_map/pallas_call | solution.py:496
  (71 shorter events, 7.0 us)
Async XLA Ops:
  3.0 59.3 %collective-permute-start.1 = (bf16[720,512]{1,0:T(8,128)(2,1)}, bf16[720,512]{1,0:T(8,128)(2,1)S(1)}, u32[]{:S(2)}, u32[]{:S(2)}) collective-permute-start(bf16[720,512]{1,0:T(8,128)(2,1)} %get-tuple-element.137), channel_id=1, source_target_pairs={{0,4},{4,0},{8,12},{12,8},{16,20},{20,16},{24,28},{28,24},{1,5},{5... | collective-permute-start | bytes 2211848 | tf_op jit(solution)/shard_map/ppermute | solution.py:534
  4.9 4.6 %copy-start = (bf16[1536,4096]{1,0:T(8,128)(2,1)S(1)}, bf16[1536,4096]{1,0:T(8,128)(2,1)}, u32[]{:S(2)}) copy-start(bf16[1536,4096]{1,0:T(8,128)(2,1)} %raw_ref.3) | copy-start | bytes 37748740
  9.5 4.6 %copy-start.1 = (bf16[1536,4096]{1,0:T(8,128)(2,1)S(1)}, bf16[1536,4096]{1,0:T(8,128)(2,1)}, u32[]{:S(2)}) copy-start(bf16[1536,4096]{1,0:T(8,128)(2,1)} %raw_ref.3) | copy-start | bytes 37748740
  14.1 51.1 %copy-start.2 = (f32[64,2048]{1,0:T(8,128)S(1)}, f32[64,2048]{1,0:T(8,128)}, u32[]{:S(2)}) copy-start(f32[64,2048]{1,0:T(8,128)} %refs_8_.3) | copy-start | bytes 1572868
  14.1 51.1 %copy-start.3 = (f32[2048]{0:T(1024)S(1)}, f32[2048]{0:T(1024)}, u32[]{:S(2)}) copy-start(f32[2048]{0:T(1024)} %param.10) | copy-start | bytes 24580
  17.2 3.2 %collective-permute-start.11 = (bf16[192,512]{1,0:T(8,128)(2,1)S(1)}, bf16[192,512]{1,0:T(8,128)(2,1)S(1)}, u32[]{:S(2)}, u32[]{:S(2)}) collective-permute-start(bf16[192,512]{1,0:T(8,128)(2,1)S(1)} %get-tuple-element.82), channel_id=1, source_target_pairs={{0,4},{4,0},{8,12},{12,8},{16,20},{20,16},{24,28},{28,24},{1,5},{5... | collective-permute-start | bytes 589832 | tf_op jit(solution)/shard_map/ppermute | solution.py:534
  17.4 8.6 %collective-permute-start.12 = (bf16[192,512]{1,0:T(8,128)(2,1)S(1)}, bf16[192,512]{1,0:T(8,128)(2,1)S(1)}, u32[]{:S(2)}, u32[]{:S(2)}) collective-permute-start(bf16[192,512]{1,0:T(8,128)(2,1)S(1)} %get-tuple-element.83), channel_id=1, source_target_pairs={{0,8},{4,12},{8,0},{12,4},{16,24},{20,28},{24,16},{28,20},{1,9},{5... | collective-permute-start | bytes 589832 | tf_op jit(solution)/shard_map/ppermute | solution.py:534
  20.3 16.3 %collective-permute-start = (bf16[192,640]{1,0:T(8,128)(2,1)S(1)}, bf16[192,640]{1,0:T(8,128)(2,1)S(1)}, u32[]{:S(2)}, u32[]{:S(2)}) collective-permute-start(bf16[192,640]{1,0:T(8,128)(2,1)S(1)} %get-tuple-element.71), channel_id=1, source_target_pairs={{0,4},{4,0},{8,12},{12,8},{16,20},{20,16},{24,28},{28,24},{1,5},{5... | collective-permute-start | bytes 737288 | tf_op jit(solution)/shard_map/ppermute | solution.py:534
  20.3 17.0 %collective-permute-start.2 = (bf16[192,640]{1,0:T(8,128)(2,1)S(1)}, bf16[192,640]{1,0:T(8,128)(2,1)S(1)}, u32[]{:S(2)}, u32[]{:S(2)}) collective-permute-start(bf16[192,640]{1,0:T(8,128)(2,1)S(1)} %get-tuple-element.73), channel_id=1, source_target_pairs={{0,8},{4,12},{8,0},{12,4},{16,24},{20,28},{24,16},{28,20},{1,9},{5... | collective-permute-start | bytes 737288 | tf_op jit(solution)/shard_map/ppermute | solution.py:534
  20.5 14.6 %collective-permute-start.13 = (bf16[192,512]{1,0:T(8,128)(2,1)S(1)}, bf16[192,512]{1,0:T(8,128)(2,1)S(1)}, u32[]{:S(2)}, u32[]{:S(2)}) collective-permute-start(bf16[192,512]{1,0:T(8,128)(2,1)S(1)} %get-tuple-element.84), channel_id=1, source_target_pairs={{0,12},{4,8},{8,4},{12,0},{16,28},{20,24},{24,20},{28,16},{1,13},{... | collective-permute-start | bytes 589832 | tf_op jit(solution)/shard_map/ppermute | solution.py:534
  26.0 14.0 %collective-permute-start.3 = (bf16[192,640]{1,0:T(8,128)(2,1)S(1)}, bf16[192,640]{1,0:T(8,128)(2,1)S(1)}, u32[]{:S(2)}, u32[]{:S(2)}) collective-permute-start(bf16[192,640]{1,0:T(8,128)(2,1)S(1)} %get-tuple-element.74), channel_id=1, source_target_pairs={{0,12},{4,8},{8,4},{12,0},{16,28},{20,24},{24,20},{28,16},{1,13},{... | collective-permute-start | bytes 737288 | tf_op jit(solution)/shard_map/ppermute | solution.py:534
  35.1 19.4 %collective-permute-start.4 = (bf16[192,640]{1,0:T(8,128)(2,1)S(1)}, bf16[192,640]{1,0:T(8,128)(2,1)S(1)}, u32[]{:S(2)}, u32[]{:S(2)}) collective-permute-start(bf16[192,640]{1,0:T(8,128)(2,1)S(1)} %get-tuple-element.75), channel_id=1, source_target_pairs={{0,16},{4,20},{8,24},{12,28},{16,0},{20,4},{24,8},{28,12},{1,17},{... | collective-permute-start | bytes 737288 | tf_op jit(solution)/shard_map/ppermute | solution.py:534
  36.6 22.9 %collective-permute-start.5 = (bf16[192,640]{1,0:T(8,128)(2,1)S(1)}, bf16[192,640]{1,0:T(8,128)(2,1)S(1)}, u32[]{:S(2)}, u32[]{:S(2)}) collective-permute-start(bf16[192,640]{1,0:T(8,128)(2,1)S(1)} %get-tuple-element.76), channel_id=1, source_target_pairs={{0,20},{4,16},{8,28},{12,24},{16,4},{20,0},{24,12},{28,8},{1,21},{... | collective-permute-start | bytes 737288 | tf_op jit(solution)/shard_map/ppermute | solution.py:534
  37.3 23.5 %collective-permute-start.6 = (bf16[192,640]{1,0:T(8,128)(2,1)S(1)}, bf16[192,640]{1,0:T(8,128)(2,1)S(1)}, u32[]{:S(2)}, u32[]{:S(2)}) collective-permute-start(bf16[192,640]{1,0:T(8,128)(2,1)S(1)} %get-tuple-element.77), channel_id=1, source_target_pairs={{0,24},{4,28},{8,16},{12,20},{16,8},{20,12},{24,0},{28,4},{1,25},{... | collective-permute-start | bytes 737288 | tf_op jit(solution)/shard_map/ppermute | solution.py:534
  40.0 23.7 %collective-permute-start.7 = (bf16[192,640]{1,0:T(8,128)(2,1)S(1)}, bf16[192,640]{1,0:T(8,128)(2,1)S(1)}, u32[]{:S(2)}, u32[]{:S(2)}) collective-permute-start(bf16[192,640]{1,0:T(8,128)(2,1)S(1)} %get-tuple-element.78), channel_id=1, source_target_pairs={{0,28},{4,24},{8,20},{12,16},{16,12},{20,8},{24,4},{28,0},{1,29},{... | collective-permute-start | bytes 737288 | tf_op jit(solution)/shard_map/ppermute | solution.py:534
  54.4 14.7 %collective-permute-start.14 = (bf16[192,512]{1,0:T(8,128)(2,1)S(1)}, bf16[192,512]{1,0:T(8,128)(2,1)S(1)}, u32[]{:S(2)}, u32[]{:S(2)}) collective-permute-start(bf16[192,512]{1,0:T(8,128)(2,1)S(1)} %get-tuple-element.85), channel_id=1, source_target_pairs={{0,16},{4,20},{8,24},{12,28},{16,0},{20,4},{24,8},{28,12},{1,17},{... | collective-permute-start | bytes 589832 | tf_op jit(solution)/shard_map/ppermute | solution.py:534
  59.5 16.9 %collective-permute-start.15 = (bf16[192,512]{1,0:T(8,128)(2,1)S(1)}, bf16[192,512]{1,0:T(8,128)(2,1)S(1)}, u32[]{:S(2)}, u32[]{:S(2)}) collective-permute-start(bf16[192,512]{1,0:T(8,128)(2,1)S(1)} %get-tuple-element.86), channel_id=1, source_target_pairs={{0,20},{4,16},{8,28},{12,24},{16,4},{20,0},{24,12},{28,8},{1,21},{... | collective-permute-start | bytes 589832 | tf_op jit(solution)/shard_map/ppermute | solution.py:534
  60.8 15.6 %collective-permute-start.16 = (bf16[192,512]{1,0:T(8,128)(2,1)S(1)}, bf16[192,512]{1,0:T(8,128)(2,1)S(1)}, u32[]{:S(2)}, u32[]{:S(2)}) collective-permute-start(bf16[192,512]{1,0:T(8,128)(2,1)S(1)} %get-tuple-element.87), channel_id=1, source_target_pairs={{0,24},{4,28},{8,16},{12,20},{16,8},{20,12},{24,0},{28,4},{1,25},{... | collective-permute-start | bytes 589832 | tf_op jit(solution)/shard_map/ppermute | solution.py:534
  62.3 14.1 %collective-permute-start.17 = (bf16[192,512]{1,0:T(8,128)(2,1)S(1)}, bf16[192,512]{1,0:T(8,128)(2,1)S(1)}, u32[]{:S(2)}, u32[]{:S(2)}) collective-permute-start(bf16[192,512]{1,0:T(8,128)(2,1)S(1)} %get-tuple-element.88), channel_id=1, source_target_pairs={{0,28},{4,24},{8,20},{12,16},{16,12},{20,8},{24,4},{28,0},{1,29},{... | collective-permute-start | bytes 589832 | tf_op jit(solution)/shard_map/ppermute | solution.py:534
  63.7 24.8 %collective-permute-start.19 = (bf16[720,512]{1,0:T(8,128)(2,1)S(1)}, bf16[720,512]{1,0:T(8,128)(2,1)S(1)}, u32[]{:S(2)}, u32[]{:S(2)}) collective-permute-start(bf16[720,512]{1,0:T(8,128)(2,1)S(1)} %get-tuple-element.91.refs_0_), channel_id=1, source_target_pairs={{0,8},{4,12},{8,0},{12,4},{16,24},{20,28},{24,16},{28,20},{1,9},{5... | collective-permute-start | bytes 2211848 | tf_op jit(solution)/shard_map/ppermute | solution.py:534
  78.5 36.1 %collective-permute-start.18 = (bf16[768,512]{1,0:T(8,128)(2,1)S(1)}, bf16[768,512]{1,0:T(8,128)(2,1)S(1)}, u32[]{:S(2)}, u32[]{:S(2)}) collective-permute-start(bf16[768,512]{1,0:T(8,128)(2,1)S(1)} %shard_map.88.refs_1_), channel_id=1, source_target_pairs={{0,1},{1,2},{2,3},{3,0},{4,5},{5,6},{6,7},{7,4},{8,9},{9,10},{10,1... | collective-permute-start | bytes 2359304 | tf_op jit(solution)/shard_map/ppermute | solution.py:541
  80.3 23.5 %collective-permute-start.20 = (bf16[720,512]{1,0:T(8,128)(2,1)S(1)}, bf16[720,512]{1,0:T(8,128)(2,1)S(1)}, u32[]{:S(2)}, u32[]{:S(2)}) collective-permute-start(bf16[720,512]{1,0:T(8,128)(2,1)S(1)} %collective-permute-done.1.refs_1_), channel_id=1, source_target_pairs={{0,8},{4,12},{8,0},{12,4},{16,24},{20,28},{24,16},{28,20},{1,9},{5... | collective-permute-start | bytes 2211848 | tf_op jit(solution)/shard_map/ppermute | solution.py:534
  81.0 22.8 %collective-permute-start.21 = (bf16[720,512]{1,0:T(8,128)(2,1)S(1)}, bf16[720,512]{1,0:T(8,128)(2,1)S(1)}, u32[]{:S(2)}, u32[]{:S(2)}) collective-permute-start(bf16[720,512]{1,0:T(8,128)(2,1)S(1)} %get-tuple-element.91.refs_0_), channel_id=1, source_target_pairs={{0,16},{4,20},{8,24},{12,28},{16,0},{20,4},{24,8},{28,12},{1,17},{... | collective-permute-start | bytes 2211848 | tf_op jit(solution)/shard_map/ppermute | solution.py:534
  82.6 32.0 %collective-permute-start.22 = (bf16[720,512]{1,0:T(8,128)(2,1)S(1)}, bf16[720,512]{1,0:T(8,128)(2,1)S(1)}, u32[]{:S(2)}, u32[]{:S(2)}) collective-permute-start(bf16[720,512]{1,0:T(8,128)(2,1)S(1)} %collective-permute-done.1.refs_1_), channel_id=1, source_target_pairs={{0,16},{4,20},{8,24},{12,28},{16,0},{20,4},{24,8},{28,12},{1,17},{... | collective-permute-start | bytes 2211848 | tf_op jit(solution)/shard_map/ppermute | solution.py:534
  88.6 30.5 %collective-permute-start.8 = (bf16[768,512]{1,0:T(8,128)(2,1)S(1)}, bf16[768,512]{1,0:T(8,128)(2,1)S(1)}, u32[]{:S(2)}, u32[]{:S(2)}) collective-permute-start(bf16[768,512]{1,0:T(8,128)(2,1)S(1)} %get-tuple-element.79.refs_0_), channel_id=1, source_target_pairs={{0,1},{1,2},{2,3},{3,0},{4,5},{5,6},{6,7},{7,4},{8,9},{9,10},{10,1... | collective-permute-start | bytes 2359304 | tf_op jit(solution)/shard_map/ppermute | solution.py:541
  114.6 16.8 %collective-permute-start.24 = (bf16[720,512]{1,0:T(8,128)(2,1)S(1)}, bf16[720,512]{1,0:T(8,128)(2,1)S(1)}, u32[]{:S(2)}, u32[]{:S(2)}) collective-permute-start(bf16[720,512]{1,0:T(8,128)(2,1)S(1)} %collective-permute-done.19.refs_2_), channel_id=1, source_target_pairs={{0,16},{4,20},{8,24},{12,28},{16,0},{20,4},{24,8},{28,12},{1,17},{... | collective-permute-start | bytes 2211848 | tf_op jit(solution)/shard_map/ppermute | solution.py:534
  115.7 16.6 %collective-permute-start.25 = (bf16[720,512]{1,0:T(8,128)(2,1)S(1)}, bf16[720,512]{1,0:T(8,128)(2,1)S(1)}, u32[]{:S(2)}, u32[]{:S(2)}) collective-permute-start(bf16[720,512]{1,0:T(8,128)(2,1)S(1)} %collective-permute-done.22.refs_5_), channel_id=1, source_target_pairs={{0,8},{4,12},{8,0},{12,4},{16,24},{20,28},{24,16},{28,20},{1,9},{5... | collective-permute-start | bytes 2211848 | tf_op jit(solution)/shard_map/ppermute | solution.py:534
  117.5 22.3 %collective-permute-start.23 = (bf16[768,512]{1,0:T(8,128)(2,1)S(1)}, bf16[768,512]{1,0:T(8,128)(2,1)S(1)}, u32[]{:S(2)}, u32[]{:S(2)}) collective-permute-start(bf16[768,512]{1,0:T(8,128)(2,1)S(1)} %collective-permute-done.18.refs_1_), channel_id=1, source_target_pairs={{0,1},{1,2},{2,3},{3,0},{4,5},{5,6},{6,7},{7,4},{8,9},{9,10},{10,1... | collective-permute-start | bytes 2359304 | tf_op jit(solution)/shard_map/ppermute | solution.py:541
  119.1 27.5 %collective-permute-start.32 = (bf16[768,512]{1,0:T(8,128)(2,1)S(1)}, bf16[768,512]{1,0:T(8,128)(2,1)S(1)}, u32[]{:S(2)}, u32[]{:S(2)}) collective-permute-start(bf16[768,512]{1,0:T(8,128)(2,1)S(1)} %shard_map.88.refs_1_), channel_id=1, source_target_pairs={{0,4},{4,0},{8,12},{12,8},{16,20},{20,16},{24,28},{28,24},{1,5},{5... | collective-permute-start | bytes 2359304 | tf_op jit(solution)/shard_map/ppermute | solution.py:534
  119.1 34.4 %collective-permute-start.9 = (bf16[768,512]{1,0:T(8,128)(2,1)S(1)}, bf16[768,512]{1,0:T(8,128)(2,1)S(1)}, u32[]{:S(2)}, u32[]{:S(2)}) collective-permute-start(bf16[768,512]{1,0:T(8,128)(2,1)S(1)} %collective-permute-done.8.refs_0_), channel_id=1, source_target_pairs={{0,1},{1,2},{2,3},{3,0},{4,5},{5,6},{6,7},{7,4},{8,9},{9,10},{10,1... | collective-permute-start | bytes 2359304 | tf_op jit(solution)/shard_map/ppermute | solution.py:541
  131.4 22.1 %collective-permute-start.31 = (bf16[768,512]{1,0:T(8,128)(2,1)S(1)}, bf16[768,512]{1,0:T(8,128)(2,1)S(1)}, u32[]{:S(2)}, u32[]{:S(2)}) collective-permute-start(bf16[768,512]{1,0:T(8,128)(2,1)S(1)} %get-tuple-element.79.refs_0_), channel_id=1, source_target_pairs={{0,4},{4,0},{8,12},{12,8},{16,20},{20,16},{24,28},{28,24},{1,5},{5... | collective-permute-start | bytes 2359304 | tf_op jit(solution)/shard_map/ppermute | solution.py:534
  132.3 21.2 %collective-permute-start.30 = (bf16[768,512]{1,0:T(8,128)(2,1)S(1)}, bf16[768,512]{1,0:T(8,128)(2,1)S(1)}, u32[]{:S(2)}, u32[]{:S(2)}) collective-permute-start(bf16[768,512]{1,0:T(8,128)(2,1)S(1)} %collective-permute-done.18.refs_1_), channel_id=1, source_target_pairs={{0,4},{4,0},{8,12},{12,8},{16,20},{20,16},{24,28},{28,24},{1,5},{5... | collective-permute-start | bytes 2359304 | tf_op jit(solution)/shard_map/ppermute | solution.py:534
  139.8 20.0 %collective-permute-start.29 = (bf16[768,512]{1,0:T(8,128)(2,1)S(1)}, bf16[768,512]{1,0:T(8,128)(2,1)S(1)}, u32[]{:S(2)}, u32[]{:S(2)}) collective-permute-start(bf16[768,512]{1,0:T(8,128)(2,1)S(1)} %collective-permute-done.8.refs_0_), channel_id=1, source_target_pairs={{0,4},{4,0},{8,12},{12,8},{16,20},{20,16},{24,28},{28,24},{1,5},{5... | collective-permute-start | bytes 2359304 | tf_op jit(solution)/shard_map/ppermute | solution.py:534
  146.6 18.5 %collective-permute-start.28 = (bf16[768,512]{1,0:T(8,128)(2,1)S(1)}, bf16[768,512]{1,0:T(8,128)(2,1)S(1)}, u32[]{:S(2)}, u32[]{:S(2)}) collective-permute-start(bf16[768,512]{1,0:T(8,128)(2,1)S(1)} %collective-permute-done.23.refs_1_), channel_id=1, source_target_pairs={{0,4},{4,0},{8,12},{12,8},{16,20},{20,16},{24,28},{28,24},{1,5},{5... | collective-permute-start | bytes 2359304 | tf_op jit(solution)/shard_map/ppermute | solution.py:534
  153.5 11.6 %collective-permute-start.27 = (bf16[768,512]{1,0:T(8,128)(2,1)S(1)}, bf16[768,512]{1,0:T(8,128)(2,1)S(1)}, u32[]{:S(2)}, u32[]{:S(2)}) collective-permute-start(bf16[768,512]{1,0:T(8,128)(2,1)S(1)} %collective-permute-done.9.refs_0_), channel_id=1, source_target_pairs={{0,4},{4,0},{8,12},{12,8},{16,20},{20,16},{24,28},{28,24},{1,5},{5... | collective-permute-start | bytes 2359304 | tf_op jit(solution)/shard_map/ppermute | solution.py:534
  153.5 22.1 %collective-permute-start.26 = (bf16[768,512]{1,0:T(8,128)(2,1)S(1)}, bf16[768,512]{1,0:T(8,128)(2,1)S(1)}, u32[]{:S(2)}, u32[]{:S(2)}) collective-permute-start(bf16[768,512]{1,0:T(8,128)(2,1)S(1)} %collective-permute-done.23.refs_1_), channel_id=1, source_target_pairs={{0,1},{1,2},{2,3},{3,0},{4,5},{5,6},{6,7},{7,4},{8,9},{9,10},{10,1... | collective-permute-start | bytes 2359304 | tf_op jit(solution)/shard_map/ppermute | solution.py:541
  153.5 38.6 %collective-permute-start.10 = (bf16[768,512]{1,0:T(8,128)(2,1)S(1)}, bf16[768,512]{1,0:T(8,128)(2,1)S(1)}, u32[]{:S(2)}, u32[]{:S(2)}) collective-permute-start(bf16[768,512]{1,0:T(8,128)(2,1)S(1)} %collective-permute-done.9.refs_0_), channel_id=1, source_target_pairs={{0,1},{1,2},{2,3},{3,0},{4,5},{5,6},{6,7},{7,4},{8,9},{9,10},{10,1... | collective-permute-start | bytes 2359304 | tf_op jit(solution)/shard_map/ppermute | solution.py:541
  192.1 3.8 %collective-permute-start.33 = (bf16[768,512]{1,0:T(8,128)(2,1)S(1)}, bf16[768,512]{1,0:T(8,128)(2,1)S(1)}, u32[]{:S(2)}, u32[]{:S(2)}) collective-permute-start(bf16[768,512]{1,0:T(8,128)(2,1)S(1)} %collective-permute-done.10.refs_0_), channel_id=1, source_target_pairs={{0,4},{4,0},{8,12},{12,8},{16,20},{20,16},{24,28},{28,24},{1,5},{5... | collective-permute-start | bytes 2359304 | tf_op jit(solution)/shard_map/ppermute | solution.py:534
  192.1 3.8 %collective-permute-start.34 = (bf16[768,512]{1,0:T(8,128)(2,1)S(1)}, bf16[768,512]{1,0:T(8,128)(2,1)S(1)}, u32[]{:S(2)}, u32[]{:S(2)}) collective-permute-start(bf16[768,512]{1,0:T(8,128)(2,1)S(1)} %collective-permute-done.26.refs_1_), channel_id=1, source_target_pairs={{0,4},{4,0},{8,12},{12,8},{16,20},{20,16},{24,28},{28,24},{1,5},{5... | collective-permute-start | bytes 2359304 | tf_op jit(solution)/shard_map/ppermute | solution.py:534
  192.6 3.3 %collective-permute-start.35 = (bf16[192,768]{1,0:T(8,128)(2,1)S(1)}, bf16[192,768]{1,0:T(8,128)(2,1)S(1)}, u32[]{:S(2)}, u32[]{:S(2)}) collective-permute-start(bf16[192,768]{1,0:T(8,128)(2,1)S(1)} %get-tuple-element.112.refs_7_.refs_1_), channel_id=1, source_target_pairs={{0,4},{4,0},{8,12},{12,8},{16,20},{20,16},{24,28},{28,24},{1,5},{5... | collective-permute-start | bytes 884744 | tf_op jit(solution)/shard_map/ppermute | solution.py:534
  203.1 1.3 collective-permute-start.36
  204.9 4.8 %collective-permute-start.37 = (f32[8,1536]{1,0:T(8,128)S(1)}, f32[8,1536]{1,0:T(8,128)S(1)}, u32[]{:S(2)}, u32[]{:S(2)}) collective-permute-start(f32[8,1536]{1,0:T(8,128)S(1)} %shard_map.94.refs_2_), channel_id=1, source_target_pairs={{0,1},{1,0},{2,3},{3,2},{4,5},{5,4},{6,7},{7,6},{8,9},{9,8},{10,11... | collective-permute-start | bytes 147464 | tf_op jit(solution)/shard_map/ppermute | solution.py:589
  205.0 7.4 %collective-permute-start.38 = (f32[8,1536]{1,0:T(8,128)S(1)}, f32[8,1536]{1,0:T(8,128)S(1)}, u32[]{:S(2)}, u32[]{:S(2)}) collective-permute-start(f32[8,1536]{1,0:T(8,128)S(1)} %shard_map.94.refs_2_), channel_id=1, source_target_pairs={{0,2},{1,3},{2,0},{3,1},{4,6},{5,7},{6,4},{7,5},{8,10},{9,11},{10,... | collective-permute-start | bytes 147464 | tf_op jit(solution)/shard_map/ppermute | solution.py:589
  205.1 7.3 %collective-permute-start.39 = (f32[8,1536]{1,0:T(8,128)S(1)}, f32[8,1536]{1,0:T(8,128)S(1)}, u32[]{:S(2)}, u32[]{:S(2)}) collective-permute-start(f32[8,1536]{1,0:T(8,128)S(1)} %shard_map.94.refs_2_), channel_id=1, source_target_pairs={{0,3},{1,2},{2,1},{3,0},{4,7},{5,6},{6,5},{7,4},{8,11},{9,10},{10,... | collective-permute-start | bytes 147464 | tf_op jit(solution)/shard_map/ppermute | solution.py:589
  216.0 31.9 %collective-permute-start.40 = (bf16[720,512]{1,0:T(8,128)(2,1)S(1)}, bf16[720,512]{1,0:T(8,128)(2,1)S(1)}, u32[]{:S(2)}, u32[]{:S(2)}) collective-permute-start(bf16[720,512]{1,0:T(8,128)(2,1)S(1)} %get-tuple-element.117), channel_id=1, source_target_pairs={{0,8},{4,12},{8,0},{12,4},{16,24},{20,28},{24,16},{28,20},{1,9},{5... | collective-permute-start | bytes 2211848 | tf_op jit(solution)/shard_map/ppermute | solution.py:534
  216.3 31.5 %collective-permute-start.41 = (bf16[720,512]{1,0:T(8,128)(2,1)S(1)}, bf16[720,512]{1,0:T(8,128)(2,1)S(1)}, u32[]{:S(2)}, u32[]{:S(2)}) collective-permute-start(bf16[720,512]{1,0:T(8,128)(2,1)S(1)} %get-tuple-element.118), channel_id=1, source_target_pairs={{0,16},{4,20},{8,24},{12,28},{16,0},{20,4},{24,8},{28,12},{1,17},{... | collective-permute-start | bytes 2211848 | tf_op jit(solution)/shard_map/ppermute | solution.py:534
  224.0 13.0 %collective-permute-start.47 = (f32[64,720]{1,0:T(8,128)S(1)}, f32[64,720]{1,0:T(8,128)S(1)}, u32[]{:S(2)}, u32[]{:S(2)}) collective-permute-start(f32[64,720]{1,0:T(8,128)S(1)} %get-tuple-element.135), channel_id=1, source_target_pairs={{0,8},{4,12},{8,0},{12,4},{16,24},{20,28},{24,16},{28,20},{1,9},{5... | collective-permute-start | bytes 552968 | tf_op jit(solution)/shard_map/ppermute | solution.py:534
  237.1 5.7 %collective-permute-start.48 = (f32[64,720]{1,0:T(8,128)S(1)}, f32[64,720]{1,0:T(8,128)S(1)}, u32[]{:S(2)}, u32[]{:S(2)}) collective-permute-start(f32[64,720]{1,0:T(8,128)S(1)} %add.40), channel_id=1, source_target_pairs={{0,16},{4,20},{8,24},{12,28},{16,0},{20,4},{24,8},{28,12},{1,17},{... | collective-permute-start | bytes 552968 | tf_op jit(solution)/shard_map/ppermute | solution.py:534
  237.6 18.2 %collective-permute-start.44 = (bf16[720,512]{1,0:T(8,128)(2,1)}, bf16[720,512]{1,0:T(8,128)(2,1)S(1)}, u32[]{:S(2)}, u32[]{:S(2)}) collective-permute-start(bf16[720,512]{1,0:T(8,128)(2,1)} %get-tuple-element.132), channel_id=1, source_target_pairs={{0,4},{4,0},{8,12},{12,8},{16,20},{20,16},{24,28},{28,24},{1,5},{5... | collective-permute-start | bytes 2211848 | tf_op jit(solution)/shard_map/ppermute | solution.py:534
  242.8 5.0 %copy-start.4 = (f32[64,720]{1,0:T(8,128)}, f32[64,720]{1,0:T(8,128)S(1)}, u32[]{:S(2)}) copy-start(f32[64,720]{1,0:T(8,128)S(1)} %add.41) | copy-start | bytes 552964
  242.8 10.1 %collective-permute-start.49 = (f32[64,720]{1,0:T(8,128)S(1)}, f32[64,720]{1,0:T(8,128)S(1)}, u32[]{:S(2)}, u32[]{:S(2)}) collective-permute-start(f32[64,720]{1,0:T(8,128)S(1)} %add.41), channel_id=1, source_target_pairs={{0,4},{4,0},{8,12},{12,8},{16,20},{20,16},{24,28},{28,24},{1,5},{5... | collective-permute-start | bytes 552968 | tf_op jit(solution)/shard_map/ppermute | solution.py:534
  247.8 7.0 %copy-start.5 = (f32[64,720]{1,0:T(8,128)S(1)}, f32[64,720]{1,0:T(8,128)}, u32[]{:S(2)}) copy-start(f32[64,720]{1,0:T(8,128)} %copy-done.4) | copy-start | bytes 552964
  250.8 19.6 %collective-permute-start.42 = (bf16[720,512]{1,0:T(8,128)(2,1)}, bf16[720,512]{1,0:T(8,128)(2,1)S(1)}, u32[]{:S(2)}, u32[]{:S(2)}) collective-permute-start(bf16[720,512]{1,0:T(8,128)(2,1)} %get-tuple-element.130), channel_id=1, source_target_pairs={{0,16},{4,12},{8,24},{12,4},{16,0},{20,28},{24,8},{28,20},{1,17},{... | collective-permute-start | bytes 2211848 | tf_op jit(solution)/shard_map/ppermute | solution.py:538
  251.3 19.1 %collective-permute-start.45 = (bf16[720,512]{1,0:T(8,128)(2,1)}, bf16[720,512]{1,0:T(8,128)(2,1)}, u32[]{:S(2)}, u32[]{:S(2)}) collective-permute-start(bf16[720,512]{1,0:T(8,128)(2,1)} %get-tuple-element.133), channel_id=1, source_target_pairs={{0,12},{4,16},{8,4},{12,24},{16,28},{20,0},{24,20},{28,8},{1,13},{... | collective-permute-start | bytes 2211848 | tf_op jit(solution)/shard_map/ppermute | solution.py:538
  252.6 33.2 %collective-permute-start.43 = (bf16[720,512]{1,0:T(8,128)(2,1)}, bf16[720,512]{1,0:T(8,128)(2,1)}, u32[]{:S(2)}, u32[]{:S(2)}) collective-permute-start(bf16[720,512]{1,0:T(8,128)(2,1)} %get-tuple-element.131), channel_id=1, source_target_pairs={{0,8},{4,20},{8,0},{12,28},{16,24},{20,4},{24,16},{28,12},{1,9},{5... | collective-permute-start | bytes 2211848 | tf_op jit(solution)/shard_map/ppermute | solution.py:538
  252.9 32.8 %collective-permute-start.46 = (bf16[720,512]{1,0:T(8,128)(2,1)}, bf16[720,512]{1,0:T(8,128)(2,1)}, u32[]{:S(2)}, u32[]{:S(2)}) collective-permute-start(bf16[720,512]{1,0:T(8,128)(2,1)} %get-tuple-element.134), channel_id=1, source_target_pairs={{0,20},{4,8},{8,28},{12,0},{16,4},{20,24},{24,12},{28,16},{1,21},{... | collective-permute-start | bytes 2211848 | tf_op jit(solution)/shard_map/ppermute | solution.py:538

commit v4 on v3

--- a/solution.py
+++ b/solution.py
@@ -39,7 +39,9 @@
         out_shape=out_shape,
         input_output_aliases=alias or {},
         compiler_params=pltpu.CompilerParams(vmem_limit_bytes=room * MIB),
-        cost_estimate=pl.CostEstimate(flops=flops, bytes_accessed=moved, transcendentals=0),
+        cost_estimate=pl.CostEstimate(
+            flops=flops // 16, bytes_accessed=moved // 16, transcendentals=0
+        ),
     )
 
 
@@ -79,7 +81,8 @@
 
 def pack_first_body(dom, shard_rows, cap, meta, dest_ref, bin_ref, raw_ref, *refs):
     outs, (place_ref, pick) = refs[:dom], refs[dom:]
-    dest = dest_ref[...]
+    dest = dest_ref[...].reshape(1, dest_ref.shape[0])
+    bins = bin_ref[...].reshape(1, dest_ref.shape[0])
     place, local = places_of(dest, shard_rows, cap, dom, meta[0])
     place_ref[...] = place
     one_hot_rows(pick, place)
@@ -87,7 +90,7 @@
     digits = jnp.where(
         which == 0,
         local >> 4,
-        jnp.where(which == 1, local & 15, jnp.where(which == 2, bin_ref[...], jnp.where(which == 3, 1, 0))),
+        jnp.where(which == 1, local & 15, jnp.where(which == 2, bins, jnp.where(which == 3, 1, 0))),
     )
     digits = jnp.where(dest >= 0, digits, 0).astype(F32).astype(BF16)
     codes = mm(pick[...], digits, NT).astype(BF16)
@@ -113,10 +116,15 @@
     return call(
         functools.partial(pack_first_body, dom, hold // 2, cap),
         (1,),
-        [row, row, pl.BlockSpec((hold, width), lambda j, m: (0, at(m)))],
+        [
+            pl.BlockSpec((hold,), lambda j, m: (0,)),
+            pl.BlockSpec((hold,), lambda j, m: (0,)),
+            pl.BlockSpec((hold, width), lambda j, m: (0, at(m))),
+        ],
         [pl.BlockSpec((cap, CODE + width), lambda j, m: (0, 0))] * dom + [row],
         [sds((cap, CODE + width), BF16)] * dom + [sds((1, hold), I32)],
         scratch=[pltpu.VMEM((slots, hold), BF16)],
+        room=54,
         flops=2 * slots * hold * width,
         moved=4 * hold * width,
     )(meta, dest, bins, raw_images)
@@ -136,6 +144,7 @@
         [pl.BlockSpec((cap, width), lambda j, m: (0, 0))] * dom,
         [sds((cap, width), BF16)] * dom,
         scratch=[pltpu.VMEM((slots, hold), BF16)],
+        room=54,
         flops=2 * slots * hold * width,
         moved=4 * hold * width,
     )(meta, place, raw_images)
@@ -285,8 +294,8 @@
     )(meta, *pieces, ctf, inv)
 
 
-def score_body(first, last, meta, *refs):
-    own, sib, panel_ref, refs = refs[:2], refs[2:4], refs[4], refs[5:]
+def score_body(parts, first, last, meta, *refs):
+    own, sib, panel_ref, refs = refs[:parts], refs[parts : 2 * parts], refs[2 * parts], refs[2 * parts + 1 :]
     if first:
         acc_out, full_ref = refs
     elif last:
@@ -321,31 +330,28 @@
         tile(sib, hot_sib if last else None)
 
 
-def score(meta, turn, turns, own, sib, panels, acc, full, hots=None, extra=None):
+def score(meta, at, own, sib, panels, acc=None, full=None, hots=None, extra=None):
     rows, part = own[0].shape
-    width = len(own) * part
+    parts = len(own)
+    width = parts * part
     tile = 256
     half = rows // tile
-    count = panels.shape[0]
-    first, last = turn == 0, turn == turns - 1
-
-    def share(m):
-        return lax.rem(m[1] + turns - turn, turns)
-
+    count, columns = panels.shape
+    first, last = acc is None, hots is not None
     front = pl.BlockSpec((tile, part), lambda j, m: (jnp.minimum(j, half - 1), 0))
     back = pl.BlockSpec((tile, part), lambda j, m: (jnp.maximum(j - half, 0), 0))
     acc_spec = pl.BlockSpec((count, tile), lambda j, m: (0, j))
-    full_spec = pl.BlockSpec((tile, width), lambda j, m: (j, share(m)))
-    in_specs = [front, front, back, back]
-    in_specs += [pl.BlockSpec((count, width), lambda j, m: (0, share(m)))]
+    full_spec = pl.BlockSpec((tile, width), lambda j, m: (j, at(m)))
+    in_specs = [front] * parts + [back] * parts
+    in_specs += [pl.BlockSpec((count, width), lambda j, m: (0, at(m)))]
     operands = [meta, *own, *sib, panels]
     alias = {}
     if not first:
         in_specs += [acc_spec, pl.BlockSpec(memory_space=pl.ANY)]
+        alias = {len(operands): 0, len(operands) + 1: 2 if last else 1}
         operands += [acc, full]
-        alias = {6: 0, 7: 2 if last else 1}
     out_specs = [acc_spec, full_spec]
-    full_shape = sds((2 * rows, width * turns), BF16)
+    full_shape = sds((2 * rows, columns), BF16)
     out_shape = [sds((count, 2 * rows), F32), full_shape]
     if last:
         depth = extra.shape[1]
@@ -358,12 +364,13 @@
         out_specs = [acc_spec, pl.BlockSpec((8, tile), lambda j, m: (0, j)), full_spec]
         out_shape = [out_shape[0], sds((8, 2 * rows), F32), full_shape]
     return call(
-        functools.partial(score_body, first, last),
+        functools.partial(score_body, parts, first, last),
         (2 * half,),
         in_specs,
         out_specs,
         out_shape,
         alias=alias,
+        room=16,
         flops=2 * count * 2 * rows * width,
         moved=8 * count * 2 * rows + 8 * rows * width,
     )(*operands)
@@ -382,7 +389,7 @@
 
 def merge(meta, mine, other):
     spec = pl.BlockSpec(mine.shape, lambda j, m: (0, 0))
-    return call(merge_body, (1,), [spec, spec], spec, sds(mine.shape, F32))(meta, mine, other)
+    return call(merge_body, (1,), [spec, spec], spec, sds(mine.shape, F32), room=4)(meta, mine, other)
 
 
 def class_body(kind, steps, meta, *refs):
@@ -449,6 +456,7 @@
         in_specs,
         out_specs,
         out_shape,
+        room=22 if kind == "first" else 18,
         flops=2 * count * rows * width * steps,
         moved=2 * rows * width * steps + 4 * count * (rows + width * steps),
     )(meta, *operands)
@@ -464,7 +472,7 @@
 def forward(meta, a_sum, b_sum, got_x, got_y):
     shape = a_sum.shape
     spec = pl.BlockSpec((shape[0] // 5, shape[1]), lambda j, m: (j, 0))
-    return call(forward_body, (5,), [spec] * 4, [spec] * 2, [sds(shape, BF16)] * 2)(
+    return call(forward_body, (5,), [spec] * 4, [spec] * 2, [sds(shape, BF16)] * 2, room=8)(
         meta, a_sum, b_sum, got_x, got_y
     )
 
@@ -484,7 +492,7 @@
 
 def finish(meta, keep, got_a, got_c, got_self, got_b, got_d):
     count, width = keep.shape
-    half = 5
+    half = 3
     tile = count // half
     front = pl.BlockSpec((tile, width), lambda j, m: (jnp.minimum(j, half - 1), 0))
     back = pl.BlockSpec((tile, width), lambda j, m: (jnp.maximum(j - half, 0), 0))
@@ -499,6 +507,7 @@
         [front] * 3 + [back] * 3,
         pl.BlockSpec((tile, width), place),
         sds((2 * count, width), F32),
+        room=12,
     )(meta, keep, got_a, got_c, got_self, got_b, got_d)
 
 
@@ -541,47 +550,51 @@
         return lax.ppermute(value, "rot", [(i, (i + 1) % turns) for i in range(turns)])
 
     width = columns // turns // 2
-    dest, bin_row = dest_row[None, :], defocus_bin[None, :]
     def exchange(blocks):
         got = [blocks[0]] + [None] * (dom - 1)
         for apart in (6, 7, 2, 4, 3, 5, 1):
             got[apart] = across(blocks[apart], apart)
         return got
 
-    *send_a, place = pack_first(meta, raw_images, dest, bin_row, dom, width, lambda m: 2 * m[1])
+    *send_a, place = pack_first(meta, raw_images, dest_row, defocus_bin, dom, width, lambda m: 2 * m[1])
     recv_a = exchange(send_a)
     send_b = pack_next(meta, raw_images, place, dom, width, lambda m: 2 * m[1] + 1)
-    recv_b = exchange(send_b)
+    together = lax.optimization_barrier
 
     count = panels.shape[0] // 2
     pieces = [None] * 8
+    place, panels = together((place, panels))
     pieces[0] = lax.dynamic_slice_in_dim(panels, core * count, count, 0)
     pieces[1] = across(lax.dynamic_slice_in_dim(panels, (1 - core) * count, count, 0), 1)
-    recv_a[1], *pieces[:2] = lax.optimization_barrier((recv_a[1], *pieces[:2]))
+
+    recv_a, send_b, pieces[:2] = together((recv_a, send_b, pieces[:2]))
+    share_a, hot, pick, wide = unpack_first(meta, recv_a, ctf_table, inv, lambda m: 2 * m[1])
+    share_a, send_b = together((share_a, send_b))
+    a1, recv_b = onward(share_a), exchange(send_b)
+    a1, recv_b, pieces[:2] = together((a1, recv_b, pieces[:2]))
     pieces[2], pieces[4] = across(pieces[0], 2), across(pieces[0], 4)
     pieces[3], pieces[5] = across(pieces[1], 2), across(pieces[1], 4)
-
-    share_a, hot, pick, wide = unpack_first(meta, recv_a, ctf_table, inv, lambda m: 2 * m[1])
     share_b = unpack_next(meta, pick, wide, recv_b, ctf_table, inv, lambda m: 2 * m[1] + 1)
     hots = (hot, across(hot, 1))
-    a1, b1 = onward(share_a), onward(share_b)
-    b1, *pieces[2:6] = lax.optimization_barrier((b1, *pieces[2:6]))
+    a2, b1 = onward(a1), onward(share_b)
+    a2, b1, pieces[2:6] = together((a2, b1, pieces[2:6]))
     pieces[6], pieces[7] = across(pieces[2], 4), across(pieces[5], 2)
-    a2, b2 = onward(a1), onward(b1)
+    a3, b2 = onward(a2), onward(b1)
     panel_full, extra = energy(meta, pieces, ctf_table, inv)
-    b2, panel_full, extra = lax.optimization_barrier((b2, panel_full, extra))
-    a3, b3 = onward(a2), onward(b2)
-
-    own = [(share_a, share_b), (a1, b1), (a2, b2), (a3, b3)]
+    a3, b2, panel_full, extra, hots = together((a3, b2, panel_full, extra, hots))
+    b3 = onward(b2)
+
+    def share(turn):
+        return lambda m: lax.rem(m[1] + turns - turn, turns)
+
     acc = full = None
-    for turn in range(turns - 1):
-        sib = [across(value, 1) for value in own[turn]]
-        acc, full = score(meta, turn, turns, own[turn], sib, panel_full, acc, full)
-    a3, b3, acc, full = lax.optimization_barrier((a3, b3, acc, full))
-    own[-1] = (a3, b3)
-    sib = [across(value, 1) for value in own[-1]]
+    for turn, own in enumerate([(share_a, share_b), (a1, b1), (a2, b2)]):
+        sib = [across(value, 1) for value in own]
+        acc, full = score(meta, share(turn), own, sib, panel_full, acc, full)
+    a3_sib, b3, acc = together((across(a3, 1), b3, acc))
+    sib = [a3_sib, across(b3, 1)]
     shifted, stat, full = score(
-        meta, turns - 1, turns, own[-1], sib, panel_full, acc, full, hots, extra
+        meta, share(turns - 1), [a3, b3], sib, panel_full, acc, full, hots, extra
     )
 
     pair = merge(meta, stat, across(stat, 1))
@@ -596,13 +609,15 @@
         meta, "mass", 4, 3, full, post=post, hots=hots, bins=bins
     )
     a_sum, b_sum, keep = class_part(meta, "rest", 7, 3, full, post=post)
+    got_self = across(give, 1)
     got_x, got_y, send_c, send_d, a_sum, b_sum, keep = lax.optimization_barrier(
         (got_x, got_y, send_c, send_d, a_sum, b_sum, keep)
     )
+    got_self, send_c, send_d = together((got_self, send_c, send_d))
     got_c, got_d = by_core(send_c, 2, 4), by_core(send_d, 5, 3)
     message_a, message_b = forward(meta, a_sum, b_sum, got_x, got_y)
+    mass, message_a = lax.optimization_barrier((mass, message_a))
     got_a, got_b = by_core(message_a, 4, 2), by_core(message_b, 3, 5)
-    got_self = across(give, 1)
     mass = mass + across(mass, 2)
     mass = mass + across(mass, 4)
     mass_other = across(mass, 1)

time: 294 us -> 257 us (0.87)
  waiting for transfers between devices: 167 us -> 134 us
  local copies, waits for them, and re-layouts: 8.41 us -> 1.65 us
    ppermute x4, waiting for transfers between devices: 30 us -> 0.01 us  [by_core(): return lax.ppermute(value, 'dom', pairs)]
    ppermute x6, waiting for transfers between devices: 35.4 us -> 22.4 us  [onward(): lax.ppermute(value, 'rot', [(i, (i + 1) % turns) for i in range(turns)])]
    ppermute x37, waiting for transfers between devices: 98.1 us -> 108 us  [across(): return lax.ppermute(value, 'dom', [(i, i ^ apart) for i in range(dom)])]
    unnamed x12, local copies, waits for them, and re-layouts: 4.62 us -> 0.94 us
  transfers between devices with their start and end apart: 50 -> 50, of which waited for: 22 -> 25; matrix products, arithmetic and copies ran while one was open for 1% -> 1% of each run, Pallas kernels for 17% -> 17%
where the time goes in v4:
time: 257 us
  waiting for transfers between devices  134 us (52%)
  Pallas kernels  72.6 us (28%)
  starting transfers between devices  46.5 us (18%)
    ppermute x37, waiting for transfers between devices, across(): return lax.ppermute(value, 'dom', [(i, i ^ apart) for i in range(dom)])  108 us
    ppermute x37, starting transfers between devices, across(): return lax.ppermute(value, 'dom', [(i, i ^ apart) for i in range(dom)])  32 us
    pallas_call x4, Pallas kernels, score(): call(functools.partial(score_body, parts, first, last), (2 * half,), in_s...  22.6 us
    ppermute x6, waiting for transfers between devices, onward(): lax.ppermute(value, 'rot', [(i, (i + 1) % turns) for i in range(turns)])  22.4 us
    pallas_call x3, Pallas kernels, class_part(): call(functools.partial(class_body, kind, steps), (steps,), in_specs, out_...  15.1 us
    pallas_call x1, Pallas kernels, pack_first(): call(functools.partial(pack_first_body, dom, hold // 2, cap), (1,), [pl.B...  7.15 us
    pallas_call x1, Pallas kernels, energy(): call(functools.partial(energy_body, bins, count), (count,), [pl.BlockSpec...  6.84 us
    ppermute x6, starting transfers between devices, onward(): lax.ppermute(value, 'rot', [(i, (i + 1) % turns) for i in range(turns)])  6.58 us
  transfers between devices with their start and end apart: 50, of which 25 were waited for; matrix products, arithmetic and copies ran while one was open for 1% of the time, Pallas kernels for 17%

profile of v4, /device:TPU:0, one launch (start us, length us, event | category | flops | bytes accessed | tf_op | source)
XLA Modules:
  0.0 257.0 jit_solution(17403542731088405230)
XLA Ops:
  0.7 0.6 stack.43.meta
  1.3 7.1 %shard_map.85 = (bf16[192,640]{1,0:T(8,128)(2,1)}, bf16[192,640]{1,0:T(8,128)(2,1)}, bf16[192,640]{1,0:T(8,128)(2,1)}, bf16[192,640]{1,0:T(8,128)(2,1)}, bf16[19...) custom-call(s32[10]{0:T(128)} %stack.43.meta, ...), custom_call_target="tpu_custom_call" | custom-call | flops 150994944 | bytes 196608 | tf_op jit(solution)/shard_map/pallas_call | solution.py:116
  9.1 2.9 %collective-permute-start.1 = (bf16[192,640]{1,0:T(8,128)(2,1)}, bf16[192,640]{1,0:T(8,128)(2,1)S(1)}, u32[]{:S(2)}, u32[]{:S(2)}) collective-permute-start(bf16[192,640]{1,0:T(8,128)(2,1)} %get-tuple-element.116), channel_id=1, source_target_pairs={{0,8},{4,12},{8,0},{12,4},{16,24},{20,28},{24,16},{28,20},{1,9},{5... | collective-permute-start | bytes 737288 | tf_op jit(solution)/shard_map/ppermute | solution.py:543
  12.1 1.5 collective-permute-start.3
  14.1 4.9 %collective-permute-done.1.refs_2_ = bf16[192,640]{1,0:T(8,128)(2,1)S(1)} collective-permute-done((bf16[192,640]{1,0:T(8,128)(2,1)}, bf16[192,640]{1,0:T(8,128)(2,1)S(1)}, u32[]{:S(2)}, u32[]{:S(2)}) %collective-permute-start.1) | collective-permute-done | bytes 245792 | tf_op jit(solution)/shard_map/ppermute | solution.py:543
  19.0 3.0 %collective-permute-start.5 = (bf16[192,640]{1,0:T(8,128)(2,1)}, bf16[192,640]{1,0:T(8,128)(2,1)S(1)}, u32[]{:S(2)}, u32[]{:S(2)}) collective-permute-start(bf16[192,640]{1,0:T(8,128)(2,1)} %get-tuple-element.120), channel_id=1, source_target_pairs={{0,24},{4,28},{8,16},{12,20},{16,8},{20,12},{24,0},{28,4},{1,25},{... | collective-permute-start | bytes 737288 | tf_op jit(solution)/shard_map/ppermute | solution.py:543
  22.0 1.9 collective-permute-done.2.refs_3_
  24.0 3.1 %collective-permute-start.6 = (bf16[192,640]{1,0:T(8,128)(2,1)}, bf16[192,640]{1,0:T(8,128)(2,1)S(1)}, u32[]{:S(2)}, u32[]{:S(2)}) collective-permute-start(bf16[192,640]{1,0:T(8,128)(2,1)} %get-tuple-element.121), channel_id=1, source_target_pairs={{0,28},{4,24},{8,20},{12,16},{16,12},{20,8},{24,4},{28,0},{1,29},{... | collective-permute-start | bytes 737288 | tf_op jit(solution)/shard_map/ppermute | solution.py:543
  27.1 5.5 %shard_map.86 = (bf16[192,512]{1,0:T(8,128)(2,1)}, bf16[192,512]{1,0:T(8,128)(2,1)}, bf16[192,512]{1,0:T(8,128)(2,1)}, bf16[192,512]{1,0:T(8,128)(2,1)}, bf16[19...) custom-call(s32[10]{0:T(128)} %stack.43.meta, ...), custom_call_target="tpu_custom_call" | custom-call | flops 150994944 | bytes 196608 | tf_op jit(solution)/shard_map/pallas_call | solution.py:137
  32.6 3.3 %collective-permute-done.4.refs_5_ = bf16[192,640]{1,0:T(8,128)(2,1)S(1)} collective-permute-done((bf16[192,640]{1,0:T(8,128)(2,1)}, bf16[192,640]{1,0:T(8,128)(2,1)S(1)}, u32[]{:S(2)}, u32[]{:S(2)}) %collective-permute-start.4) | collective-permute-done | bytes 245792 | tf_op jit(solution)/shard_map/ppermute | solution.py:543
  35.9 3.9 %shard_map.87 = (bf16[768,512]{1,0:T(8,128)(2,1)S(1)}, bf16[192,768]{1,0:T(8,128)(2,1)S(1)}, bf16[768,1536]{1,0:T(8,128)(2,1)S(1)}, bf16[768,192]{1,0:T(8,128)(2,1)S(1)}) custom-call(s32[10]{0:T(128)S(1)} %copy-done.3, bf16[192,640]{1,0:T(8,128)(2,1)S(1)} %copy-done.1, bf16[192,640]{1,0:T(8,128)(2,1)S(1)} %collective-permute-done.refs_1_, ...), custom_call_target="tpu_custom_call" | custom-call | flops 75497472 | bytes 122880 | tf_op jit(solution)/shard_map/pallas_call | solution.py:203
  39.8 2.0 collective-permute-start.8
  41.8 1.5 collective-permute-start.10
  43.4 1.5 collective-permute-start.12
  45.3 4.5 %collective-permute-done.10.refs_2_ = bf16[192,512]{1,0:T(8,128)(2,1)S(1)} collective-permute-done((bf16[192,512]{1,0:T(8,128)(2,1)}, bf16[192,512]{1,0:T(8,128)(2,1)S(1)}, u32[]{:S(2)}, u32[]{:S(2)}) %collective-permute-start.10) | collective-permute-done | bytes 196640 | tf_op jit(solution)/shard_map/ppermute | solution.py:543
  49.8 2.5 collective-permute-start.14
  52.3 0.9 collective-permute-done.11.refs_3_
  53.2 3.1 %collective-permute-start.15 = (bf16[192,512]{1,0:T(8,128)(2,1)}, bf16[192,512]{1,0:T(8,128)(2,1)S(1)}, u32[]{:S(2)}, u32[]{:S(2)}) collective-permute-start(bf16[192,512]{1,0:T(8,128)(2,1)} %get-tuple-element.157), channel_id=1, source_target_pairs={{0,28},{4,24},{8,20},{12,16},{16,12},{20,8},{24,4},{28,0},{1,29},{... | collective-permute-start | bytes 589832 | tf_op jit(solution)/shard_map/ppermute | solution.py:543
  56.3 7.1 %collective-permute-done.13.refs_5_ = bf16[192,512]{1,0:T(8,128)(2,1)S(1)} collective-permute-done((bf16[192,512]{1,0:T(8,128)(2,1)}, bf16[192,512]{1,0:T(8,128)(2,1)S(1)}, u32[]{:S(2)}, u32[]{:S(2)}) %collective-permute-start.13) | collective-permute-done | bytes 196640 | tf_op jit(solution)/shard_map/ppermute | solution.py:543
  63.4 1.9 collective-permute-start.18
  65.3 0.9 copy-done.2
  66.2 2.1 shard_map.88.refs_1_
  68.3 1.6 collective-permute-start.17
  70.0 1.6 collective-permute-start.16
  71.5 1.5 collective-permute-start.20
  73.2 9.5 %collective-permute-done.18.refs_2_ = bf16[720,512]{1,0:T(8,128)(2,1)S(1)} collective-permute-done((bf16[720,512]{1,0:T(8,128)(2,1)S(1)}, bf16[720,512]{1,0:T(8,128)(2,1)S(1)}, u32[]{:S(2)}, u32[]{:S(2)}) %collective-permute-start.18) | collective-permute-done | bytes 737312 | tf_op jit(solution)/shard_map/ppermute | solution.py:543
  82.8 1.5 collective-permute-start.21
  84.3 13.5 %collective-permute-done.19.refs_3_ = bf16[720,512]{1,0:T(8,128)(2,1)S(1)} collective-permute-done((bf16[720,512]{1,0:T(8,128)(2,1)S(1)}, bf16[720,512]{1,0:T(8,128)(2,1)S(1)}, u32[]{:S(2)}, u32[]{:S(2)}) %collective-permute-start.19) | collective-permute-done | bytes 737312 | tf_op jit(solution)/shard_map/ppermute | solution.py:543
  97.8 7.2 %collective-permute-done.21.refs_5_ = bf16[720,512]{1,0:T(8,128)(2,1)S(1)} collective-permute-done((bf16[720,512]{1,0:T(8,128)(2,1)S(1)}, bf16[720,512]{1,0:T(8,128)(2,1)S(1)}, u32[]{:S(2)}, u32[]{:S(2)}) %collective-permute-start.21) | collective-permute-done | bytes 737312 | tf_op jit(solution)/shard_map/ppermute | solution.py:543
  105.0 1.3 collective-permute-done.16.refs_0_
  106.3 1.5 collective-permute-start.24
  108.1 1.4 collective-permute-start.23
  109.8 13.8 %collective-permute-done.24.refs_6_ = bf16[720,512]{1,0:T(8,128)(2,1)S(1)} collective-permute-done((bf16[720,512]{1,0:T(8,128)(2,1)S(1)}, bf16[720,512]{1,0:T(8,128)(2,1)S(1)}, u32[]{:S(2)}, u32[]{:S(2)}) %collective-permute-start.24) | collective-permute-done | bytes 737312 | tf_op jit(solution)/shard_map/ppermute | solution.py:543
  123.7 1.2 collective-permute-done.25.refs_7_
  124.9 5.4 %collective-permute-done.22.refs_0_ = bf16[768,512]{1,0:T(8,128)(2,1)S(1)} collective-permute-done((bf16[768,512]{1,0:T(8,128)(2,1)S(1)}, bf16[768,512]{1,0:T(8,128)(2,1)S(1)}, u32[]{:S(2)}, u32[]{:S(2)}) %collective-permute-start.22) | collective-permute-done | bytes 786464 | tf_op jit(solution)/shard_map/ppermute | solution.py:550
  130.3 6.8 %shard_map.89 = (bf16[720,4096]{1,0:T(8,128)(2,1)S(1)}, bf16[720,192]{1,0:T(8,128)(2,1)S(1)}) custom-call(s32[10]{0:T(128)S(1)} %copy-done.3, bf16[720,512]{1,0:T(8,128)(2,1)S(1)} %get-tuple-element.171.refs_0_, bf16[720,512]{1,0:T(8,128)(2,1)S(1)} %collective-permute-done.7.refs_1_, bf16[720,512]{1,0:T(8,128)(2,1)S(1)} %collective-permute-done.18.refs_2_, ...), custom_call_target="tpu_custom_call" | custom-call | flops 283115520 | bytes 737280 | tf_op jit(solution)/shard_map/pallas_call | solution.py:278
  137.1 9.6 %collective-permute-done.23.refs_1_ = bf16[768,512]{1,0:T(8,128)(2,1)S(1)} collective-permute-done((bf16[768,512]{1,0:T(8,128)(2,1)S(1)}, bf16[768,512]{1,0:T(8,128)(2,1)S(1)}, u32[]{:S(2)}, u32[]{:S(2)}) %collective-permute-start.23) | collective-permute-done | bytes 786464 | tf_op jit(solution)/shard_map/ppermute | solution.py:550
  147.3 4.9 %shard_map.90 = (f32[720,1536]{1,0:T(8,128)S(1)}, bf16[1536,4096]{1,0:T(8,128)(2,1)S(1)}) custom-call(s32[10]{0:T(128)S(1)} %copy-done.3, bf16[768,512]{1,0:T(8,128)(2,1)S(1)} %get-tuple-element.149.refs_0_, bf16[768,512]{1,0:T(8,128)(2,1)S(1)} %shard_map.88.refs_1_, bf16[768,512]{1,0:T(8,128)(2,1)S(1)} %collective-permute-done.33.refs_2_, ...), custom_call_target="tpu_custom_call" | custom-call | flops 141557760 | bytes 946176 | tf_op jit(solution)/shard_map/pallas_call | solution.py:366
  152.3 5.3 %shard_map.91 = (f32[720,1536]{1,0:T(8,128)S(1)}, bf16[1536,4096]{1,0:T(8,128)(2,1)S(1)}) custom-call(s32[10]{0:T(128)S(1)} %copy-done.3, bf16[768,512]{1,0:T(8,128)(2,1)S(1)} %collective-permute-done.8.refs_0_, bf16[768,512]{1,0:T(8,128)(2,1)S(1)} %collective-permute-done.17.refs_1_, ...), custom_call_target="tpu_custom_call", output_to_operand_aliasing={{0}: (6, {}), {1}: (7, {})} | custom-call | flops 141557760 | bytes 946176 | tf_op jit(solution)/shard_map/pallas_call | solution.py:366
  157.6 5.3 %shard_map.92 = (f32[720,1536]{1,0:T(8,128)S(1)}, bf16[1536,4096]{1,0:T(8,128)(2,1)S(1)}) custom-call(s32[10]{0:T(128)S(1)} %copy-done.3, bf16[768,512]{1,0:T(8,128)(2,1)S(1)} %collective-permute-done.16.refs_0_, bf16[768,512]{1,0:T(8,128)(2,1)S(1)} %collective-permute-done.23.refs_1_, ...), custom_call_target="tpu_custom_call", output_to_operand_aliasing={{0}: (6, {}), {1}: (7, {})} | custom-call | flops 141557760 | bytes 946176 | tf_op jit(solution)/shard_map/pallas_call | solution.py:366
  162.9 6.1 %collective-permute-done.28.refs_1_ = bf16[768,512]{1,0:T(8,128)(2,1)S(1)} collective-permute-done((bf16[768,512]{1,0:T(8,128)(2,1)S(1)}, bf16[768,512]{1,0:T(8,128)(2,1)S(1)}, u32[]{:S(2)}, u32[]{:S(2)}) %collective-permute-start.28) | collective-permute-done | bytes 786464 | tf_op jit(solution)/shard_map/ppermute | solution.py:550
  169.0 2.3 collective-permute-done.35.refs_3_
  171.3 7.1 %shard_map.93 = (f32[720,1536]{1,0:T(8,128)S(1)}, f32[8,1536]{1,0:T(8,128)S(1)}, bf16[1536,4096]{1,0:T(8,128)(2,1)S(1)}) custom-call(s32[10]{0:T(128)S(1)} %copy-done.3, bf16[768,512]{1,0:T(8,128)(2,1)S(1)} %collective-permute-done.22.refs_0_, bf16[768,512]{1,0:T(8,128)(2,1)S(1)} %collective-permute-done.28.refs_1_, ...), custom_call_target="tpu_custom_call", output_to_operand_aliasing={{0}: (6, {}), {2}: (7, {})} | custom-call | flops 141557760 | bytes 946176 | tf_op jit(solution)/shard_map/pallas_call | solution.py:366
  178.6 1.1 collective-permute-done.36.other_ref
  179.7 0.6 shard_map.94.refs_2_
  180.5 4.3 %collective-permute-start.39 = (f32[8,1536]{1,0:T(8,128)S(1)}, f32[8,1536]{1,0:T(8,128)S(1)}, u32[]{:S(2)}, u32[]{:S(2)}) collective-permute-start(f32[8,1536]{1,0:T(8,128)S(1)} %shard_map.94.refs_2_), channel_id=1, source_target_pairs={{0,3},{1,2},{2,1},{3,0},{4,7},{5,6},{6,5},{7,4},{8,11},{9,10},{10,... | collective-permute-start | bytes 147464 | tf_op jit(solution)/shard_map/ppermute | solution.py:602
  185.1 2.7 %collective-permute-done.38.refs_4_ = f32[8,1536]{1,0:T(8,128)S(1)} collective-permute-done((f32[8,1536]{1,0:T(8,128)S(1)}, f32[8,1536]{1,0:T(8,128)S(1)}, u32[]{:S(2)}, u32[]{:S(2)}) %collective-permute-start.38) | collective-permute-done | bytes 49184 | tf_op jit(solution)/shard_map/ppermute | solution.py:602
  187.8 3.5 %shard_map.95 = (bf16[720,512]{1,0:T(8,128)(2,1)S(1)}, bf16[720,512]{1,0:T(8,128)(2,1)S(1)}, bf16[720,1536]{1,0:T(8,128)(2,1)S(1)}, f32[1,768]{1,0:T(1,128)S(1)}) custom-call(s32[10]{0:T(128)S(1)} %copy-done.3, f32[720,1536]{1,0:T(8,128)S(1)} %get-tuple-element.197.refs_0_, f32[8,1536]{1,0:T(8,128)S(1)} %get-tuple-element.198.mine_ref.refs_1_, ...), custom_call_target="tpu_custom_call" | custom-call | flops 141557760 | bytes 657408 | tf_op jit(solution)/shard_map/pallas_call | solution.py:453
  191.3 1.8 collective-permute-start.40
  193.7 6.7 %shard_map.96 = (bf16[720,512]{1,0:T(8,128)(2,1)}, bf16[720,512]{1,0:T(8,128)(2,1)}, bf16[720,512]{1,0:T(8,128)(2,1)S(1)}, f32[64,720]{1,0:T(8,128)S(1)}) custom-call(s32[10]{0:T(128)S(1)} %copy-done.3, bf16[720,1536]{1,0:T(8,128)(2,1)S(1)} %get-tuple-element.202.refs_0_, bf16[192,768]{1,0:T(8,128)(2,1)S(1)} %get-tuple-element.194.refs_7_.refs_1_, ...), custom_call_target="tpu_custom_call" | custom-call | flops 212336640 | bytes 847872 | tf_op jit(solution)/shard_map/pallas_call | solution.py:453
  200.3 4.9 %shard_map.97 = (f32[720,512]{1,0:T(8,128)S(1)}, f32[720,512]{1,0:T(8,128)S(1)}, f32[720,512]{1,0:T(8,128)S(1)}) custom-call(s32[10]{0:T(128)S(1)} %copy-done.3, bf16[720,1536]{1,0:T(8,128)(2,1)S(1)} %get-tuple-element.202.refs_0_, bf16[1536,4096]{1,0:T(8,128)(2,1)S(1)} %get-tuple-element.199.refs_6_.refs_3_.refs_1_), custom_call_target="tpu_custom_call" | custom-call | flops 212336640 | bytes 847872 | tf_op jit(solution)/shard_map/pallas_call | solution.py:453
  205.3 2.9 %collective-permute-done.40.down_ref = bf16[720,512]{1,0:T(8,128)(2,1)S(1)} collective-permute-done((bf16[720,512]{1,0:T(8,128)(2,1)S(1)}, bf16[720,512]{1,0:T(8,128)(2,1)S(1)}, u32[]{:S(2)}, u32[]{:S(2)}) %collective-permute-start.40) | collective-permute-done | bytes 737312 | tf_op jit(solution)/shard_map/ppermute | solution.py:543
  208.2 1.5 collective-permute-done.41.left_ref
  209.6 2.8 %shard_map.98 = (bf16[720,512]{1,0:T(8,128)(2,1)}, bf16[720,512]{1,0:T(8,128)(2,1)}) custom-call(s32[10]{0:T(128)S(1)} %copy-done.3, f32[720,512]{1,0:T(8,128)S(1)} %get-tuple-element.210.a_sum, f32[720,512]{1,0:T(8,128)S(1)} %get-tuple-element.211.b_sum, bf16[720,512]{1,0:T(8,128)(2,1)S(1)} %collective-permute-done.40.down_ref, ...), custom_call_target="tpu_custom_call" | custom-call | tf_op jit(solution)/shard_map/pallas_call | solution.py:475
  212.9 1.7 collective-permute-start.44
  214.5 0.5 collective-permute-start.42
  215.1 1.3 collective-permute-start.45
  216.3 2.2 collective-permute-done.47
  218.6 0.6 collective-permute-start.48
  219.2 29.4 %collective-permute-done.48 = f32[64,720]{1,0:T(8,128)S(1)} collective-permute-done((f32[64,720]{1,0:T(8,128)S(1)}, f32[64,720]{1,0:T(8,128)S(1)}, u32[]{:S(2)}, u32[]{:S(2)}) %collective-permute-start.48) | collective-permute-done | bytes 184352 | tf_op jit(solution)/shard_map/ppermute | solution.py:543
  248.7 0.6 reduce
  249.3 0.8 collective-permute-done.49
  250.1 0.9 maximum_select_fusion
  251.1 5.9 %shard_map.99 = f32[1440,512]{1,0:T(8,128)} custom-call(s32[10]{0:T(128)S(1)} %copy-done.3, f32[720,512]{1,0:T(8,128)S(1)} %get-tuple-element.208.keep_ref, bf16[720,512]{1,0:T(8,128)(2,1)} %collective-permute-done.42.a_ref, bf16[720,512]{1,0:T(8,128)(2,1)S(1)} %collective-permute-done.44.c_ref, bf16[720,512]{1,0:T(8,128)(2,1)S(1)} %collective-permute-done.43.other_ref, ...), custom_call_target="tpu_custom_call" | custom-call | tf_op jit(solution)/shard_map/pallas_call | solution.py:504
  (69 shorter events, 4.9 us)
Async XLA Ops:
  1.3 7.2 %copy-start.5 = (bf16[1440,512]{1,0:T(8,128)(2,1)S(1)}, bf16[1440,512]{1,0:T(8,128)(2,1)}, u32[]{:S(2)}) copy-start(bf16[1440,512]{1,0:T(8,128)(2,1)} %param.11) | copy-start | bytes 4423684
  8.5 27.3 %collective-permute-start.7 = (bf16[720,512]{1,0:T(8,128)(2,1)S(1)}, bf16[720,512]{1,0:T(8,128)(2,1)S(1)}, u32[]{:S(2)}, u32[]{:S(2)}) collective-permute-start(bf16[720,512]{1,0:T(8,128)(2,1)S(1)} %get-tuple-element.225), channel_id=1, source_target_pairs={{0,4},{4,0},{8,12},{12,8},{16,20},{20,16},{24,28},{28,24},{1,5},{5... | collective-permute-start | bytes 2211848 | tf_op jit(solution)/shard_map/ppermute | solution.py:543
  9.1 4.5 %collective-permute-start = (bf16[192,640]{1,0:T(8,128)(2,1)}, bf16[192,640]{1,0:T(8,128)(2,1)S(1)}, u32[]{:S(2)}, u32[]{:S(2)}) collective-permute-start(bf16[192,640]{1,0:T(8,128)(2,1)} %get-tuple-element.115), channel_id=1, source_target_pairs={{0,4},{4,0},{8,12},{12,8},{16,20},{20,16},{24,28},{28,24},{1,5},{5... | collective-permute-start | bytes 737288 | tf_op jit(solution)/shard_map/ppermute | solution.py:543
  9.1 9.9 %collective-permute-start.1 = (bf16[192,640]{1,0:T(8,128)(2,1)}, bf16[192,640]{1,0:T(8,128)(2,1)S(1)}, u32[]{:S(2)}, u32[]{:S(2)}) collective-permute-start(bf16[192,640]{1,0:T(8,128)(2,1)} %get-tuple-element.116), channel_id=1, source_target_pairs={{0,8},{4,12},{8,0},{12,4},{16,24},{20,28},{24,16},{28,20},{1,9},{5... | collective-permute-start | bytes 737288 | tf_op jit(solution)/shard_map/ppermute | solution.py:543
  12.1 11.9 %collective-permute-start.2 = (bf16[192,640]{1,0:T(8,128)(2,1)}, bf16[192,640]{1,0:T(8,128)(2,1)S(1)}, u32[]{:S(2)}, u32[]{:S(2)}) collective-permute-start(bf16[192,640]{1,0:T(8,128)(2,1)} %get-tuple-element.117), channel_id=1, source_target_pairs={{0,12},{4,8},{8,4},{12,0},{16,28},{20,24},{24,20},{28,16},{1,13},{... | collective-permute-start | bytes 737288 | tf_op jit(solution)/shard_map/ppermute | solution.py:543
  12.1 20.5 %collective-permute-start.3 = (bf16[192,640]{1,0:T(8,128)(2,1)}, bf16[192,640]{1,0:T(8,128)(2,1)S(1)}, u32[]{:S(2)}, u32[]{:S(2)}) collective-permute-start(bf16[192,640]{1,0:T(8,128)(2,1)} %get-tuple-element.118), channel_id=1, source_target_pairs={{0,16},{4,20},{8,24},{12,28},{16,0},{20,4},{24,8},{28,12},{1,17},{... | collective-permute-start | bytes 737288 | tf_op jit(solution)/shard_map/ppermute | solution.py:543
  13.6 22.3 %collective-permute-start.4 = (bf16[192,640]{1,0:T(8,128)(2,1)}, bf16[192,640]{1,0:T(8,128)(2,1)S(1)}, u32[]{:S(2)}, u32[]{:S(2)}) collective-permute-start(bf16[192,640]{1,0:T(8,128)(2,1)} %get-tuple-element.119), channel_id=1, source_target_pairs={{0,20},{4,16},{8,28},{12,24},{16,4},{20,0},{24,12},{28,8},{1,21},{... | collective-permute-start | bytes 737288 | tf_op jit(solution)/shard_map/ppermute | solution.py:543
  19.0 16.9 %collective-permute-start.5 = (bf16[192,640]{1,0:T(8,128)(2,1)}, bf16[192,640]{1,0:T(8,128)(2,1)S(1)}, u32[]{:S(2)}, u32[]{:S(2)}) collective-permute-start(bf16[192,640]{1,0:T(8,128)(2,1)} %get-tuple-element.120), channel_id=1, source_target_pairs={{0,24},{4,28},{8,16},{12,20},{16,8},{20,12},{24,0},{28,4},{1,25},{... | collective-permute-start | bytes 737288 | tf_op jit(solution)/shard_map/ppermute | solution.py:543
  24.0 11.9 %copy-start = (f32[64,2048]{1,0:T(8,128)S(1)}, f32[64,2048]{1,0:T(8,128)}, u32[]{:S(2)}) copy-start(f32[64,2048]{1,0:T(8,128)} %refs_8_.3) | copy-start | bytes 1572868
  24.0 11.9 %copy-start.1 = (bf16[192,640]{1,0:T(8,128)(2,1)S(1)}, bf16[192,640]{1,0:T(8,128)(2,1)}, u32[]{:S(2)}) copy-start(bf16[192,640]{1,0:T(8,128)(2,1)} %get-tuple-element.132.refs_0_) | copy-start | bytes 737284
  24.0 11.9 %copy-start.3 = (s32[10]{0:T(128)S(1)}, s32[10]{0:T(128)}, u32[]{:S(2)}) copy-start(s32[10]{0:T(128)} %stack.43.meta) | copy-start | bytes 124
  24.0 11.9 %copy-start.4 = (f32[2048]{0:T(1024)S(1)}, f32[2048]{0:T(1024)}, u32[]{:S(2)}) copy-start(f32[2048]{0:T(1024)} %param.10) | copy-start | bytes 24580
  24.0 11.9 %collective-permute-start.6 = (bf16[192,640]{1,0:T(8,128)(2,1)}, bf16[192,640]{1,0:T(8,128)(2,1)S(1)}, u32[]{:S(2)}, u32[]{:S(2)}) collective-permute-start(bf16[192,640]{1,0:T(8,128)(2,1)} %get-tuple-element.121), channel_id=1, source_target_pairs={{0,28},{4,24},{8,20},{12,16},{16,12},{20,8},{24,4},{28,0},{1,29},{... | collective-permute-start | bytes 737288 | tf_op jit(solution)/shard_map/ppermute | solution.py:543
  39.8 23.5 %collective-permute-start.8 = (bf16[768,512]{1,0:T(8,128)(2,1)S(1)}, bf16[768,512]{1,0:T(8,128)(2,1)S(1)}, u32[]{:S(2)}, u32[]{:S(2)}) collective-permute-start(bf16[768,512]{1,0:T(8,128)(2,1)S(1)} %get-tuple-element.149.refs_0_), channel_id=1, source_target_pairs={{0,1},{1,2},{2,3},{3,0},{4,5},{5,6},{6,7},{7,4},{8,9},{9,10},{10,1... | collective-permute-start | bytes 2359304 | tf_op jit(solution)/shard_map/ppermute | solution.py:550
  41.8 8.0 %collective-permute-start.10 = (bf16[192,512]{1,0:T(8,128)(2,1)}, bf16[192,512]{1,0:T(8,128)(2,1)S(1)}, u32[]{:S(2)}, u32[]{:S(2)}) collective-permute-start(bf16[192,512]{1,0:T(8,128)(2,1)} %get-tuple-element.152), channel_id=1, source_target_pairs={{0,8},{4,12},{8,0},{12,4},{16,24},{20,28},{24,16},{28,20},{1,9},{5... | collective-permute-start | bytes 589832 | tf_op jit(solution)/shard_map/ppermute | solution.py:543
  43.4 9.8 %collective-permute-start.11 = (bf16[192,512]{1,0:T(8,128)(2,1)}, bf16[192,512]{1,0:T(8,128)(2,1)S(1)}, u32[]{:S(2)}, u32[]{:S(2)}) collective-permute-start(bf16[192,512]{1,0:T(8,128)(2,1)} %get-tuple-element.153), channel_id=1, source_target_pairs={{0,12},{4,8},{8,4},{12,0},{16,28},{20,24},{24,20},{28,16},{1,13},{... | collective-permute-start | bytes 589832 | tf_op jit(solution)/shard_map/ppermute | solution.py:543
  43.4 12.9 %collective-permute-start.12 = (bf16[192,512]{1,0:T(8,128)(2,1)}, bf16[192,512]{1,0:T(8,128)(2,1)S(1)}, u32[]{:S(2)}, u32[]{:S(2)}) collective-permute-start(bf16[192,512]{1,0:T(8,128)(2,1)} %get-tuple-element.154), channel_id=1, source_target_pairs={{0,16},{4,20},{8,24},{12,28},{16,0},{20,4},{24,8},{28,12},{1,17},{... | collective-permute-start | bytes 589832 | tf_op jit(solution)/shard_map/ppermute | solution.py:543
  44.9 18.4 %collective-permute-start.13 = (bf16[192,512]{1,0:T(8,128)(2,1)}, bf16[192,512]{1,0:T(8,128)(2,1)S(1)}, u32[]{:S(2)}, u32[]{:S(2)}) collective-permute-start(bf16[192,512]{1,0:T(8,128)(2,1)} %get-tuple-element.155), channel_id=1, source_target_pairs={{0,20},{4,16},{8,28},{12,24},{16,4},{20,0},{24,12},{28,8},{1,21},{... | collective-permute-start | bytes 589832 | tf_op jit(solution)/shard_map/ppermute | solution.py:543
  49.8 13.5 %collective-permute-start.14 = (bf16[192,512]{1,0:T(8,128)(2,1)}, bf16[192,512]{1,0:T(8,128)(2,1)S(1)}, u32[]{:S(2)}, u32[]{:S(2)}) collective-permute-start(bf16[192,512]{1,0:T(8,128)(2,1)} %get-tuple-element.156), channel_id=1, source_target_pairs={{0,24},{4,28},{8,16},{12,20},{16,8},{20,12},{24,0},{28,4},{1,25},{... | collective-permute-start | bytes 589832 | tf_op jit(solution)/shard_map/ppermute | solution.py:543
  53.2 10.1 %collective-permute-start.15 = (bf16[192,512]{1,0:T(8,128)(2,1)}, bf16[192,512]{1,0:T(8,128)(2,1)S(1)}, u32[]{:S(2)}, u32[]{:S(2)}) collective-permute-start(bf16[192,512]{1,0:T(8,128)(2,1)} %get-tuple-element.157), channel_id=1, source_target_pairs={{0,28},{4,24},{8,20},{12,16},{16,12},{20,8},{24,4},{28,0},{1,29},{... | collective-permute-start | bytes 589832 | tf_op jit(solution)/shard_map/ppermute | solution.py:543
  56.3 7.1 %collective-permute-start.9 = (bf16[192,512]{1,0:T(8,128)(2,1)}, bf16[192,512]{1,0:T(8,128)(2,1)S(1)}, u32[]{:S(2)}, u32[]{:S(2)}) collective-permute-start(bf16[192,512]{1,0:T(8,128)(2,1)} %get-tuple-element.151), channel_id=1, source_target_pairs={{0,4},{4,0},{8,12},{12,8},{16,20},{20,16},{24,28},{28,24},{1,5},{5... | collective-permute-start | bytes 589832 | tf_op jit(solution)/shard_map/ppermute | solution.py:543
  63.4 19.4 %collective-permute-start.18 = (bf16[720,512]{1,0:T(8,128)(2,1)S(1)}, bf16[720,512]{1,0:T(8,128)(2,1)S(1)}, u32[]{:S(2)}, u32[]{:S(2)}) collective-permute-start(bf16[720,512]{1,0:T(8,128)(2,1)S(1)} %get-tuple-element.171.refs_0_), channel_id=1, source_target_pairs={{0,8},{4,12},{8,0},{12,4},{16,24},{20,28},{24,16},{28,20},{1,9},{5... | collective-permute-start | bytes 2211848 | tf_op jit(solution)/shard_map/ppermute | solution.py:543
  65.3 0.9 copy-start.2
  68.3 36.7 %collective-permute-start.17 = (bf16[768,512]{1,0:T(8,128)(2,1)S(1)}, bf16[768,512]{1,0:T(8,128)(2,1)S(1)}, u32[]{:S(2)}, u32[]{:S(2)}) collective-permute-start(bf16[768,512]{1,0:T(8,128)(2,1)S(1)} %shard_map.88.refs_1_), channel_id=1, source_target_pairs={{0,1},{1,2},{2,3},{3,0},{4,5},{5,6},{6,7},{7,4},{8,9},{9,10},{10,1... | collective-permute-start | bytes 2359304 | tf_op jit(solution)/shard_map/ppermute | solution.py:550
  70.0 36.4 %collective-permute-start.16 = (bf16[768,512]{1,0:T(8,128)(2,1)S(1)}, bf16[768,512]{1,0:T(8,128)(2,1)S(1)}, u32[]{:S(2)}, u32[]{:S(2)}) collective-permute-start(bf16[768,512]{1,0:T(8,128)(2,1)S(1)} %collective-permute-done.8.refs_0_), channel_id=1, source_target_pairs={{0,1},{1,2},{2,3},{3,0},{4,5},{5,6},{6,7},{7,4},{8,9},{9,10},{10,1... | collective-permute-start | bytes 2359304 | tf_op jit(solution)/shard_map/ppermute | solution.py:550
  71.5 26.3 %collective-permute-start.20 = (bf16[720,512]{1,0:T(8,128)(2,1)S(1)}, bf16[720,512]{1,0:T(8,128)(2,1)S(1)}, u32[]{:S(2)}, u32[]{:S(2)}) collective-permute-start(bf16[720,512]{1,0:T(8,128)(2,1)S(1)} %get-tuple-element.171.refs_0_), channel_id=1, source_target_pairs={{0,16},{4,20},{8,24},{12,28},{16,0},{20,4},{24,8},{28,12},{1,17},{... | collective-permute-start | bytes 2211848 | tf_op jit(solution)/shard_map/ppermute | solution.py:543
  73.1 24.8 %collective-permute-start.19 = (bf16[720,512]{1,0:T(8,128)(2,1)S(1)}, bf16[720,512]{1,0:T(8,128)(2,1)S(1)}, u32[]{:S(2)}, u32[]{:S(2)}) collective-permute-start(bf16[720,512]{1,0:T(8,128)(2,1)S(1)} %collective-permute-done.7.refs_1_), channel_id=1, source_target_pairs={{0,8},{4,12},{8,0},{12,4},{16,24},{20,28},{24,16},{28,20},{1,9},{5... | collective-permute-start | bytes 2211848 | tf_op jit(solution)/shard_map/ppermute | solution.py:543
  82.8 22.2 %collective-permute-start.21 = (bf16[720,512]{1,0:T(8,128)(2,1)S(1)}, bf16[720,512]{1,0:T(8,128)(2,1)S(1)}, u32[]{:S(2)}, u32[]{:S(2)}) collective-permute-start(bf16[720,512]{1,0:T(8,128)(2,1)S(1)} %collective-permute-done.7.refs_1_), channel_id=1, source_target_pairs={{0,16},{4,20},{8,24},{12,28},{16,0},{20,4},{24,8},{28,12},{1,17},{... | collective-permute-start | bytes 2211848 | tf_op jit(solution)/shard_map/ppermute | solution.py:543
  106.3 17.4 %collective-permute-start.24 = (bf16[720,512]{1,0:T(8,128)(2,1)S(1)}, bf16[720,512]{1,0:T(8,128)(2,1)S(1)}, u32[]{:S(2)}, u32[]{:S(2)}) collective-permute-start(bf16[720,512]{1,0:T(8,128)(2,1)S(1)} %collective-permute-done.18.refs_2_), channel_id=1, source_target_pairs={{0,16},{4,20},{8,24},{12,28},{16,0},{20,4},{24,8},{28,12},{1,17},{... | collective-permute-start | bytes 2211848 | tf_op jit(solution)/shard_map/ppermute | solution.py:543
  107.8 17.1 %collective-permute-start.25 = (bf16[720,512]{1,0:T(8,128)(2,1)S(1)}, bf16[720,512]{1,0:T(8,128)(2,1)S(1)}, u32[]{:S(2)}, u32[]{:S(2)}) collective-permute-start(bf16[720,512]{1,0:T(8,128)(2,1)S(1)} %collective-permute-done.21.refs_5_), channel_id=1, source_target_pairs={{0,8},{4,12},{8,0},{12,4},{16,24},{20,28},{24,16},{28,20},{1,9},{5... | collective-permute-start | bytes 2211848 | tf_op jit(solution)/shard_map/ppermute | solution.py:543
  108.1 1.6 collective-permute-start.26
  108.1 22.1 %collective-permute-start.22 = (bf16[768,512]{1,0:T(8,128)(2,1)S(1)}, bf16[768,512]{1,0:T(8,128)(2,1)S(1)}, u32[]{:S(2)}, u32[]{:S(2)}) collective-permute-start(bf16[768,512]{1,0:T(8,128)(2,1)S(1)} %collective-permute-done.16.refs_0_), channel_id=1, source_target_pairs={{0,1},{1,2},{2,3},{3,0},{4,5},{5,6},{6,7},{7,4},{8,9},{9,10},{10,1... | collective-permute-start | bytes 2359304 | tf_op jit(solution)/shard_map/ppermute | solution.py:550
  108.1 38.6 %collective-permute-start.23 = (bf16[768,512]{1,0:T(8,128)(2,1)S(1)}, bf16[768,512]{1,0:T(8,128)(2,1)S(1)}, u32[]{:S(2)}, u32[]{:S(2)}) collective-permute-start(bf16[768,512]{1,0:T(8,128)(2,1)S(1)} %collective-permute-done.17.refs_1_), channel_id=1, source_target_pairs={{0,1},{1,2},{2,3},{3,0},{4,5},{5,6},{6,7},{7,4},{8,9},{9,10},{10,1... | collective-permute-start | bytes 2359304 | tf_op jit(solution)/shard_map/ppermute | solution.py:550
  109.7 37.0 %collective-permute-start.33 = (bf16[768,512]{1,0:T(8,128)(2,1)S(1)}, bf16[768,512]{1,0:T(8,128)(2,1)S(1)}, u32[]{:S(2)}, u32[]{:S(2)}) collective-permute-start(bf16[768,512]{1,0:T(8,128)(2,1)S(1)} %get-tuple-element.149.refs_0_), channel_id=1, source_target_pairs={{0,4},{4,0},{8,12},{12,8},{16,20},{20,16},{24,28},{28,24},{1,5},{5... | collective-permute-start | bytes 2359304 | tf_op jit(solution)/shard_map/ppermute | solution.py:543
  123.7 23.6 %collective-permute-start.34 = (bf16[768,512]{1,0:T(8,128)(2,1)S(1)}, bf16[768,512]{1,0:T(8,128)(2,1)S(1)}, u32[]{:S(2)}, u32[]{:S(2)}) collective-permute-start(bf16[768,512]{1,0:T(8,128)(2,1)S(1)} %shard_map.88.refs_1_), channel_id=1, source_target_pairs={{0,4},{4,0},{8,12},{12,8},{16,20},{20,16},{24,28},{28,24},{1,5},{5... | collective-permute-start | bytes 2359304 | tf_op jit(solution)/shard_map/ppermute | solution.py:543
  124.9 22.4 %collective-permute-start.31 = (bf16[768,512]{1,0:T(8,128)(2,1)S(1)}, bf16[768,512]{1,0:T(8,128)(2,1)S(1)}, u32[]{:S(2)}, u32[]{:S(2)}) collective-permute-start(bf16[768,512]{1,0:T(8,128)(2,1)S(1)} %collective-permute-done.8.refs_0_), channel_id=1, source_target_pairs={{0,4},{4,0},{8,12},{12,8},{16,20},{20,16},{24,28},{28,24},{1,5},{5... | collective-permute-start | bytes 2359304 | tf_op jit(solution)/shard_map/ppermute | solution.py:543
  130.3 22.0 %collective-permute-start.32 = (bf16[768,512]{1,0:T(8,128)(2,1)S(1)}, bf16[768,512]{1,0:T(8,128)(2,1)S(1)}, u32[]{:S(2)}, u32[]{:S(2)}) collective-permute-start(bf16[768,512]{1,0:T(8,128)(2,1)S(1)} %collective-permute-done.17.refs_1_), channel_id=1, source_target_pairs={{0,4},{4,0},{8,12},{12,8},{16,20},{20,16},{24,28},{28,24},{1,5},{5... | collective-permute-start | bytes 2359304 | tf_op jit(solution)/shard_map/ppermute | solution.py:543
  146.7 10.8 %collective-permute-start.29 = (bf16[768,512]{1,0:T(8,128)(2,1)S(1)}, bf16[768,512]{1,0:T(8,128)(2,1)S(1)}, u32[]{:S(2)}, u32[]{:S(2)}) collective-permute-start(bf16[768,512]{1,0:T(8,128)(2,1)S(1)} %collective-permute-done.16.refs_0_), channel_id=1, source_target_pairs={{0,4},{4,0},{8,12},{12,8},{16,20},{20,16},{24,28},{28,24},{1,5},{5... | collective-permute-start | bytes 2359304 | tf_op jit(solution)/shard_map/ppermute | solution.py:543
  146.7 10.8 %collective-permute-start.30 = (bf16[768,512]{1,0:T(8,128)(2,1)S(1)}, bf16[768,512]{1,0:T(8,128)(2,1)S(1)}, u32[]{:S(2)}, u32[]{:S(2)}) collective-permute-start(bf16[768,512]{1,0:T(8,128)(2,1)S(1)} %collective-permute-done.23.refs_1_), channel_id=1, source_target_pairs={{0,4},{4,0},{8,12},{12,8},{16,20},{20,16},{24,28},{28,24},{1,5},{5... | collective-permute-start | bytes 2359304 | tf_op jit(solution)/shard_map/ppermute | solution.py:543
  147.3 15.6 %collective-permute-start.27 = (bf16[768,512]{1,0:T(8,128)(2,1)S(1)}, bf16[768,512]{1,0:T(8,128)(2,1)S(1)}, u32[]{:S(2)}, u32[]{:S(2)}) collective-permute-start(bf16[768,512]{1,0:T(8,128)(2,1)S(1)} %collective-permute-done.22.refs_0_), channel_id=1, source_target_pairs={{0,4},{4,0},{8,12},{12,8},{16,20},{20,16},{24,28},{28,24},{1,5},{5... | collective-permute-start | bytes 2359304 | tf_op jit(solution)/shard_map/ppermute | solution.py:543
  147.3 21.7 %collective-permute-start.28 = (bf16[768,512]{1,0:T(8,128)(2,1)S(1)}, bf16[768,512]{1,0:T(8,128)(2,1)S(1)}, u32[]{:S(2)}, u32[]{:S(2)}) collective-permute-start(bf16[768,512]{1,0:T(8,128)(2,1)S(1)} %collective-permute-done.23.refs_1_), channel_id=1, source_target_pairs={{0,1},{1,2},{2,3},{3,0},{4,5},{5,6},{6,7},{7,4},{8,9},{9,10},{10,1... | collective-permute-start | bytes 2359304 | tf_op jit(solution)/shard_map/ppermute | solution.py:550
  169.0 2.3 collective-permute-start.35
  178.4 1.3 collective-permute-start.36
  180.3 4.8 %collective-permute-start.37 = (f32[8,1536]{1,0:T(8,128)S(1)}, f32[8,1536]{1,0:T(8,128)S(1)}, u32[]{:S(2)}, u32[]{:S(2)}) collective-permute-start(f32[8,1536]{1,0:T(8,128)S(1)} %shard_map.94.refs_2_), channel_id=1, source_target_pairs={{0,1},{1,0},{2,3},{3,2},{4,5},{5,4},{6,7},{7,6},{8,9},{9,8},{10,11... | collective-permute-start | bytes 147464 | tf_op jit(solution)/shard_map/ppermute | solution.py:602
  180.4 7.4 %collective-permute-start.38 = (f32[8,1536]{1,0:T(8,128)S(1)}, f32[8,1536]{1,0:T(8,128)S(1)}, u32[]{:S(2)}, u32[]{:S(2)}) collective-permute-start(f32[8,1536]{1,0:T(8,128)S(1)} %shard_map.94.refs_2_), channel_id=1, source_target_pairs={{0,2},{1,3},{2,0},{3,1},{4,6},{5,7},{6,4},{7,5},{8,10},{9,11},{10,... | collective-permute-start | bytes 147464 | tf_op jit(solution)/shard_map/ppermute | solution.py:602
  180.5 7.3 %collective-permute-start.39 = (f32[8,1536]{1,0:T(8,128)S(1)}, f32[8,1536]{1,0:T(8,128)S(1)}, u32[]{:S(2)}, u32[]{:S(2)}) collective-permute-start(f32[8,1536]{1,0:T(8,128)S(1)} %shard_map.94.refs_2_), channel_id=1, source_target_pairs={{0,3},{1,2},{2,1},{3,0},{4,7},{5,6},{6,5},{7,4},{8,11},{9,10},{10,... | collective-permute-start | bytes 147464 | tf_op jit(solution)/shard_map/ppermute | solution.py:602
  191.3 16.8 %collective-permute-start.40 = (bf16[720,512]{1,0:T(8,128)(2,1)S(1)}, bf16[720,512]{1,0:T(8,128)(2,1)S(1)}, u32[]{:S(2)}, u32[]{:S(2)}) collective-permute-start(bf16[720,512]{1,0:T(8,128)(2,1)S(1)} %get-tuple-element.200), channel_id=1, source_target_pairs={{0,8},{4,12},{8,0},{12,4},{16,24},{20,28},{24,16},{28,20},{1,9},{5... | collective-permute-start | bytes 2211848 | tf_op jit(solution)/shard_map/ppermute | solution.py:543
  193.2 16.5 %collective-permute-start.41 = (bf16[720,512]{1,0:T(8,128)(2,1)S(1)}, bf16[720,512]{1,0:T(8,128)(2,1)S(1)}, u32[]{:S(2)}, u32[]{:S(2)}) collective-permute-start(bf16[720,512]{1,0:T(8,128)(2,1)S(1)} %get-tuple-element.201), channel_id=1, source_target_pairs={{0,16},{4,20},{8,24},{12,28},{16,0},{20,4},{24,8},{28,12},{1,17},{... | collective-permute-start | bytes 2211848 | tf_op jit(solution)/shard_map/ppermute | solution.py:543
  200.3 12.5 %collective-permute-start.43 = (bf16[720,512]{1,0:T(8,128)(2,1)S(1)}, bf16[720,512]{1,0:T(8,128)(2,1)S(1)}, u32[]{:S(2)}, u32[]{:S(2)}) collective-permute-start(bf16[720,512]{1,0:T(8,128)(2,1)S(1)} %get-tuple-element.216), channel_id=1, source_target_pairs={{0,4},{4,0},{8,12},{12,8},{16,20},{20,16},{24,28},{28,24},{1,5},{5... | collective-permute-start | bytes 2211848 | tf_op jit(solution)/shard_map/ppermute | solution.py:543
  212.5 6.0 %collective-permute-start.47 = (f32[64,720]{1,0:T(8,128)S(1)}, f32[64,720]{1,0:T(8,128)S(1)}, u32[]{:S(2)}, u32[]{:S(2)}) collective-permute-start(f32[64,720]{1,0:T(8,128)S(1)} %get-tuple-element.223), channel_id=1, source_target_pairs={{0,8},{4,12},{8,0},{12,4},{16,24},{20,28},{24,16},{28,20},{1,9},{5... | collective-permute-start | bytes 552968 | tf_op jit(solution)/shard_map/ppermute | solution.py:543
  212.9 38.2 %collective-permute-start.44 = (bf16[720,512]{1,0:T(8,128)(2,1)}, bf16[720,512]{1,0:T(8,128)(2,1)S(1)}, u32[]{:S(2)}, u32[]{:S(2)}) collective-permute-start(bf16[720,512]{1,0:T(8,128)(2,1)} %get-tuple-element.219), channel_id=1, source_target_pairs={{0,8},{4,20},{8,0},{12,28},{16,24},{20,4},{24,16},{28,12},{1,9},{5... | collective-permute-start | bytes 2211848 | tf_op jit(solution)/shard_map/ppermute | solution.py:547
  214.5 36.5 %collective-permute-start.46 = (bf16[720,512]{1,0:T(8,128)(2,1)}, bf16[720,512]{1,0:T(8,128)(2,1)}, u32[]{:S(2)}, u32[]{:S(2)}) collective-permute-start(bf16[720,512]{1,0:T(8,128)(2,1)} %get-tuple-element.222), channel_id=1, source_target_pairs={{0,20},{4,8},{8,28},{12,0},{16,4},{20,24},{24,12},{28,16},{1,21},{... | collective-permute-start | bytes 2211848 | tf_op jit(solution)/shard_map/ppermute | solution.py:547
  214.5 36.5 %collective-permute-start.42 = (bf16[720,512]{1,0:T(8,128)(2,1)}, bf16[720,512]{1,0:T(8,128)(2,1)}, u32[]{:S(2)}, u32[]{:S(2)}) collective-permute-start(bf16[720,512]{1,0:T(8,128)(2,1)} %get-tuple-element.215), channel_id=1, source_target_pairs={{0,16},{4,12},{8,24},{12,4},{16,0},{20,28},{24,8},{28,20},{1,17},{... | collective-permute-start | bytes 2211848 | tf_op jit(solution)/shard_map/ppermute | solution.py:547
  215.1 36.0 %collective-permute-start.45 = (bf16[720,512]{1,0:T(8,128)(2,1)}, bf16[720,512]{1,0:T(8,128)(2,1)}, u32[]{:S(2)}, u32[]{:S(2)}) collective-permute-start(bf16[720,512]{1,0:T(8,128)(2,1)} %get-tuple-element.221), channel_id=1, source_target_pairs={{0,12},{4,16},{8,4},{12,24},{16,28},{20,0},{24,20},{28,8},{1,13},{... | collective-permute-start | bytes 2211848 | tf_op jit(solution)/shard_map/ppermute | solution.py:547
  218.6 30.0 %collective-permute-start.48 = (f32[64,720]{1,0:T(8,128)S(1)}, f32[64,720]{1,0:T(8,128)S(1)}, u32[]{:S(2)}, u32[]{:S(2)}) collective-permute-start(f32[64,720]{1,0:T(8,128)S(1)} %add.40), channel_id=1, source_target_pairs={{0,16},{4,20},{8,24},{12,28},{16,0},{20,4},{24,8},{28,12},{1,17},{... | collective-permute-start | bytes 552968 | tf_op jit(solution)/shard_map/ppermute | solution.py:543
  248.6 1.5 collective-permute-start.49

commit v5 on v4

--- a/solution.py
+++ b/solution.py
@@ -394,8 +394,9 @@
 
 def class_body(kind, steps, meta, *refs):
     if kind == "first":
-        (shifted_ref, stat_ref), four, full_ref = refs[:2], refs[2:6], refs[6]
-        outs, (post_ref, log_ref) = refs[7 : 7 + steps], refs[7 + steps :]
+        (shifted_ref, stat_ref), four = refs[:2], refs[2:6]
+        hot_own, hot_sib, full_ref = refs[6:9]
+        outs, (post_ref, log_ref, mass_ref) = refs[9 : 9 + steps], refs[9 + steps :]
 
         @pl.when(pl.program_id(0) == 0)
         def _():
@@ -407,18 +408,10 @@
             factor = jnp.exp(stat_ref[0:1] - peak) / mass
             post_ref[...] = (shifted_ref[...] * factor).astype(BF16)
             log_ref[...] = (peak + jnp.log(mass))[:, : log_ref.shape[1]]
-
-    elif kind == "mass":
-        post_ref, hot_own, hot_sib, full_ref = refs[:4]
-        outs, mass_ref = refs[4 : 4 + steps], refs[4 + steps]
-        bins, _ = mass_ref.shape
-        rows = hot_own.shape[1]
-
-        @pl.when(pl.program_id(0) == 0)
-        def _():
-            mass_ref[...] = mm(hot_own[:bins, :], post_ref[:, :rows], NT) + mm(
-                hot_sib[:bins, :], post_ref[:, rows:], NT
-            )
+            bins, rows = mass_ref.shape[0], hot_own.shape[1]
+            weights = mm(hot_own[:bins, :], post_ref[:, :rows], NT)
+            weights = weights + mm(hot_sib[:bins, :], post_ref[:, rows:], NT)
+            mass_ref[...] = weights.astype(BF16)
 
     else:
         (post_ref, full_ref), outs = refs[:2], refs[2:]
@@ -438,15 +431,11 @@
     out_specs = [whole((count, width))] * steps
     out_shape = [sds((count, width), F32 if kind == "rest" else BF16)] * steps
     if kind == "first":
-        operands = [shifted, *stats, full]
-        in_specs = [whole(shifted.shape)] + [whole(stats[0].shape)] * 5 + [full_spec]
-        out_specs += [whole((count, rows)), whole((1, rows // 2))]
-        out_shape += [sds((count, rows), BF16), sds((1, rows // 2), F32)]
-    elif kind == "mass":
-        operands = [post, *hots, full]
-        in_specs = [whole(post.shape), whole(hots[0].shape), whole(hots[1].shape), full_spec]
-        out_specs += [whole((bins, count))]
-        out_shape += [sds((bins, count), F32)]
+        operands = [shifted, *stats, *hots, full]
+        in_specs = [whole(shifted.shape)] + [whole(stats[0].shape)] * 5
+        in_specs += [whole(hots[0].shape)] * 2 + [full_spec]
+        out_specs += [whole((count, rows)), whole((1, rows // 2)), whole((bins, count))]
+        out_shape += [sds((count, rows), BF16), sds((1, rows // 2), F32), sds((bins, count), BF16)]
     else:
         operands = [post, full]
         in_specs = [whole(post.shape), full_spec]
@@ -471,40 +460,43 @@
 
 def forward(meta, a_sum, b_sum, got_x, got_y):
     shape = a_sum.shape
-    spec = pl.BlockSpec((shape[0] // 5, shape[1]), lambda j, m: (j, 0))
-    return call(forward_body, (5,), [spec] * 4, [spec] * 2, [sds(shape, BF16)] * 2, room=8)(
+    spec = pl.BlockSpec(memory_space=pltpu.VMEM)
+    return call(forward_body, (1,), [spec] * 4, [spec] * 2, [sds(shape, BF16)] * 2, room=14)(
         meta, a_sum, b_sum, got_x, got_y
     )
 
 
-def finish_body(meta, keep_ref, a_ref, c_ref, other_ref, b_ref, d_ref, out_ref):
+def finish_body(tile, meta, keep_ref, a_ref, c_ref, other_ref, b_ref, d_ref, out_ref):
     half = pl.num_programs(0) // 2
-    wide = lambda ref: ref[...].astype(F32)
-
-    @pl.when(pl.program_id(0) < half)
+    step = pl.program_id(0)
+
+    def total(refs, at):
+        rows = pl.ds(pl.multiple_of(at * tile, tile), tile)
+        first, second, third = [ref[rows, :].astype(F32) for ref in refs]
+        out_ref[...] = first + second + third
+
+    @pl.when(step < half)
     def _():
-        out_ref[...] = keep_ref[...] + wide(c_ref) + wide(a_ref)
-
-    @pl.when(pl.program_id(0) >= half)
+        total((keep_ref, c_ref, a_ref), step)
+
+    @pl.when(step >= half)
     def _():
-        out_ref[...] = wide(other_ref) + wide(d_ref) + wide(b_ref)
+        total((other_ref, d_ref, b_ref), step - half)
 
 
 def finish(meta, keep, got_a, got_c, got_self, got_b, got_d):
     count, width = keep.shape
     half = 3
     tile = count // half
-    front = pl.BlockSpec((tile, width), lambda j, m: (jnp.minimum(j, half - 1), 0))
-    back = pl.BlockSpec((tile, width), lambda j, m: (jnp.maximum(j - half, 0), 0))
 
     def place(j, m):
         core = lax.rem(m[0], 2)
         return jnp.where(j < half, core * half + j, (1 - core) * half + j - half), 0
 
     return call(
-        finish_body,
+        functools.partial(finish_body, tile),
         (2 * half,),
-        [front] * 3 + [back] * 3,
+        [pl.BlockSpec(memory_space=pltpu.VMEM)] * 6,
         pl.BlockSpec((tile, width), place),
         sds((2 * count, width), F32),
         room=12,
@@ -571,17 +563,19 @@
     share_a, hot, pick, wide = unpack_first(meta, recv_a, ctf_table, inv, lambda m: 2 * m[1])
     share_a, send_b = together((share_a, send_b))
     a1, recv_b = onward(share_a), exchange(send_b)
-    a1, recv_b, pieces[:2] = together((a1, recv_b, pieces[:2]))
+    a2 = onward(a1)
+    recv_b, pieces[:2] = together((recv_b, pieces[:2]))
     pieces[2], pieces[4] = across(pieces[0], 2), across(pieces[0], 4)
     pieces[3], pieces[5] = across(pieces[1], 2), across(pieces[1], 4)
+    a2, recv_b = together((a2, recv_b))
     share_b = unpack_next(meta, pick, wide, recv_b, ctf_table, inv, lambda m: 2 * m[1] + 1)
     hots = (hot, across(hot, 1))
-    a2, b1 = onward(a1), onward(share_b)
-    a2, b1, pieces[2:6] = together((a2, b1, pieces[2:6]))
+    a3, b1 = onward(a2), onward(share_b)
+    a3, b1, pieces[2:6] = together((a3, b1, pieces[2:6]))
     pieces[6], pieces[7] = across(pieces[2], 4), across(pieces[5], 2)
-    a3, b2 = onward(a2), onward(b1)
+    b2 = onward(b1)
     panel_full, extra = energy(meta, pieces, ctf_table, inv)
-    a3, b2, panel_full, extra, hots = together((a3, b2, panel_full, extra, hots))
+    b2, panel_full, extra, hots = together((b2, panel_full, extra, hots))
     b3 = onward(b2)
 
     def share(turn):
@@ -601,25 +595,22 @@
     others = [
         lax.ppermute(pair, "rot", [(i, i ^ apart) for i in range(turns)]) for apart in (1, 2, 3)
     ]
-    to_x, to_y, post, log_evidence = class_part(
-        meta, "first", 2, 2, full, shifted=shifted, stats=[stat, pair, *others]
-    )
+    to_x, to_y, post, log_evidence, mass = class_part(
+        meta, "first", 2, 2, full, None, shifted, [stat, pair, *others], hots, bins
+    )
+    mass_x = across(mass, 2)
     got_x, got_y = across(to_x, 2), across(to_y, 4)
-    send_c, send_d, give, mass = class_part(
-        meta, "mass", 4, 3, full, post=post, hots=hots, bins=bins
-    )
-    a_sum, b_sum, keep = class_part(meta, "rest", 7, 3, full, post=post)
-    got_self = across(give, 1)
-    got_x, got_y, send_c, send_d, a_sum, b_sum, keep = lax.optimization_barrier(
-        (got_x, got_y, send_c, send_d, a_sum, b_sum, keep)
-    )
-    got_self, send_c, send_d = together((got_self, send_c, send_d))
+    send_c, send_d, give = class_part(meta, "next", 4, 3, full, post)
+    mass = mass.astype(F32) + mass_x.astype(F32)
+    mass = mass + across(mass, 4)
+    a_sum, b_sum, keep = class_part(meta, "rest", 7, 3, full, post)
+    got_x, got_y, send_c, send_d, a_sum, b_sum, keep, give, mass = together(
+        (got_x, got_y, send_c, send_d, a_sum, b_sum, keep, give, mass)
+    )
     got_c, got_d = by_core(send_c, 2, 4), by_core(send_d, 5, 3)
     message_a, message_b = forward(meta, a_sum, b_sum, got_x, got_y)
-    mass, message_a = lax.optimization_barrier((mass, message_a))
     got_a, got_b = by_core(message_a, 4, 2), by_core(message_b, 3, 5)
-    mass = mass + across(mass, 2)
-    mass = mass + across(mass, 4)
+    got_self = across(give, 1)
     mass_other = across(mass, 1)
     bin_weights = jnp.where(
         even,

time: 257 us -> 271 us (1.054)
  waiting for transfers between devices: 134 us -> 153 us
  starting transfers between devices: 46.5 us -> 42.9 us
    ppermute x4, waiting for transfers between devices: 0.01 us -> 29.7 us  [by_core(): return lax.ppermute(value, 'dom', pairs)]
    ppermute x37, waiting for transfers between devices: 108 us -> 87 us  [across(): return lax.ppermute(value, 'dom', [(i, i ^ apart) for i in range(dom)])]
    ppermute x6, waiting for transfers between devices: 22.4 us -> 33.1 us  [onward(): lax.ppermute(value, 'rot', [(i, (i + 1) % turns) for i in range(turns)])]
    ppermute x6, starting transfers between devices: 6.58 us -> 2.32 us  [onward(): lax.ppermute(value, 'rot', [(i, (i + 1) % turns) for i in range(turns)])]
  transfers between devices with their start and end apart: 50 -> 50, of which waited for: 25 -> 24; matrix products, arithmetic and copies ran while one was open for 1% -> 1% of each run, Pallas kernels for 17% -> 16%
where the time goes in v5:
time: 271 us
  waiting for transfers between devices  153 us (56%)
  Pallas kernels  70.9 us (26%)
  starting transfers between devices  42.9 us (16%)
    ppermute x37, waiting for transfers between devices, across(): return lax.ppermute(value, 'dom', [(i, i ^ apart) for i in range(dom)])  87 us
    ppermute x6, waiting for transfers between devices, onward(): lax.ppermute(value, 'rot', [(i, (i + 1) % turns) for i in range(turns)])  33.1 us
    ppermute x37, starting transfers between devices, across(): return lax.ppermute(value, 'dom', [(i, i ^ apart) for i in range(dom)])  32.4 us
    ppermute x4, waiting for transfers between devices, by_core(): return lax.ppermute(value, 'dom', pairs)  29.7 us
    pallas_call x4, Pallas kernels, score(): call(functools.partial(score_body, parts, first, last), (2 * half,), in_s...  22.6 us
    pallas_call x3, Pallas kernels, class_part(): call(functools.partial(class_body, kind, steps), (steps,), in_specs, out_...  15.4 us
    pallas_call x1, Pallas kernels, pack_first(): call(functools.partial(pack_first_body, dom, hold // 2, cap), (1,), [pl.B...  7.15 us
    pallas_call x1, Pallas kernels, energy(): call(functools.partial(energy_body, bins, count), (count,), [pl.BlockSpec...  6.82 us
  transfers between devices with their start and end apart: 50, of which 24 were waited for; matrix products, arithmetic and copies ran while one was open for 1% of the time, Pallas kernels for 16%

profile of v5, /device:TPU:0, one launch (start us, length us, event | category | flops | bytes accessed | tf_op | source)
XLA Modules:
  0.0 270.9 jit_solution(3308381631120934782)
XLA Ops:
  0.7 0.6 stack.43.meta
  1.3 7.1 %shard_map.85 = (bf16[192,640]{1,0:T(8,128)(2,1)}, bf16[192,640]{1,0:T(8,128)(2,1)}, bf16[192,640]{1,0:T(8,128)(2,1)}, bf16[192,640]{1,0:T(8,128)(2,1)}, bf16[19...) custom-call(s32[10]{0:T(128)} %stack.43.meta, ...), custom_call_target="tpu_custom_call" | custom-call | flops 150994944 | bytes 196608 | tf_op jit(solution)/shard_map/pallas_call | solution.py:116
  8.5 0.5 collective-permute-start.7
  9.1 2.9 %collective-permute-start.1 = (bf16[192,640]{1,0:T(8,128)(2,1)}, bf16[192,640]{1,0:T(8,128)(2,1)S(1)}, u32[]{:S(2)}, u32[]{:S(2)}) collective-permute-start(bf16[192,640]{1,0:T(8,128)(2,1)} %get-tuple-element.120), channel_id=1, source_target_pairs={{0,8},{4,12},{8,0},{12,4},{16,24},{20,28},{24,16},{28,20},{1,9},{5... | collective-permute-start | bytes 737288 | tf_op jit(solution)/shard_map/ppermute | solution.py:535
  12.1 1.5 collective-permute-start.3
  13.6 0.5 collective-permute-start.4
  14.1 4.9 %collective-permute-done.1.refs_2_ = bf16[192,640]{1,0:T(8,128)(2,1)S(1)} collective-permute-done((bf16[192,640]{1,0:T(8,128)(2,1)}, bf16[192,640]{1,0:T(8,128)(2,1)S(1)}, u32[]{:S(2)}, u32[]{:S(2)}) %collective-permute-start.1) | collective-permute-done | bytes 245792 | tf_op jit(solution)/shard_map/ppermute | solution.py:535
  19.0 3.0 %collective-permute-start.5 = (bf16[192,640]{1,0:T(8,128)(2,1)}, bf16[192,640]{1,0:T(8,128)(2,1)S(1)}, u32[]{:S(2)}, u32[]{:S(2)}) collective-permute-start(bf16[192,640]{1,0:T(8,128)(2,1)} %get-tuple-element.124), channel_id=1, source_target_pairs={{0,24},{4,28},{8,16},{12,20},{16,8},{20,12},{24,0},{28,4},{1,25},{... | collective-permute-start | bytes 737288 | tf_op jit(solution)/shard_map/ppermute | solution.py:535
  22.0 1.9 collective-permute-done.2.refs_3_
  24.0 3.1 %collective-permute-start.6 = (bf16[192,640]{1,0:T(8,128)(2,1)}, bf16[192,640]{1,0:T(8,128)(2,1)S(1)}, u32[]{:S(2)}, u32[]{:S(2)}) collective-permute-start(bf16[192,640]{1,0:T(8,128)(2,1)} %get-tuple-element.125), channel_id=1, source_target_pairs={{0,28},{4,24},{8,20},{12,16},{16,12},{20,8},{24,4},{28,0},{1,29},{... | collective-permute-start | bytes 737288 | tf_op jit(solution)/shard_map/ppermute | solution.py:535
  27.1 5.5 %shard_map.86 = (bf16[192,512]{1,0:T(8,128)(2,1)}, bf16[192,512]{1,0:T(8,128)(2,1)}, bf16[192,512]{1,0:T(8,128)(2,1)}, bf16[192,512]{1,0:T(8,128)(2,1)}, bf16[19...) custom-call(s32[10]{0:T(128)} %stack.43.meta, ...), custom_call_target="tpu_custom_call" | custom-call | flops 150994944 | bytes 196608 | tf_op jit(solution)/shard_map/pallas_call | solution.py:137
  32.6 3.3 %collective-permute-done.4.refs_5_ = bf16[192,640]{1,0:T(8,128)(2,1)S(1)} collective-permute-done((bf16[192,640]{1,0:T(8,128)(2,1)}, bf16[192,640]{1,0:T(8,128)(2,1)S(1)}, u32[]{:S(2)}, u32[]{:S(2)}) %collective-permute-start.4) | collective-permute-done | bytes 245792 | tf_op jit(solution)/shard_map/ppermute | solution.py:535
  35.9 3.9 %shard_map.87 = (bf16[768,512]{1,0:T(8,128)(2,1)S(1)}, bf16[192,768]{1,0:T(8,128)(2,1)S(1)}, bf16[768,1536]{1,0:T(8,128)(2,1)S(1)}, bf16[768,192]{1,0:T(8,128)(2,1)S(1)}) custom-call(s32[10]{0:T(128)S(1)} %copy-done.3, bf16[192,640]{1,0:T(8,128)(2,1)S(1)} %copy-done.1, bf16[192,640]{1,0:T(8,128)(2,1)S(1)} %collective-permute-done.refs_1_, ...), custom_call_target="tpu_custom_call" | custom-call | flops 75497472 | bytes 122880 | tf_op jit(solution)/shard_map/pallas_call | solution.py:203
  39.8 2.0 collective-permute-start.8
  41.8 1.5 collective-permute-start.11
  43.7 1.5 collective-permute-start.13
  45.3 4.4 %collective-permute-done.11.refs_2_ = bf16[192,512]{1,0:T(8,128)(2,1)S(1)} collective-permute-done((bf16[192,512]{1,0:T(8,128)(2,1)}, bf16[192,512]{1,0:T(8,128)(2,1)S(1)}, u32[]{:S(2)}, u32[]{:S(2)}) %collective-permute-start.11) | collective-permute-done | bytes 196640 | tf_op jit(solution)/shard_map/ppermute | solution.py:535
  49.7 2.5 collective-permute-start.15
  52.3 0.9 collective-permute-done.12.refs_3_
  53.2 3.0 %collective-permute-start.16 = (bf16[192,512]{1,0:T(8,128)(2,1)}, bf16[192,512]{1,0:T(8,128)(2,1)S(1)}, u32[]{:S(2)}, u32[]{:S(2)}) collective-permute-start(bf16[192,512]{1,0:T(8,128)(2,1)} %get-tuple-element.161), channel_id=1, source_target_pairs={{0,28},{4,24},{8,20},{12,16},{16,12},{20,8},{24,4},{28,0},{1,29},{... | collective-permute-start | bytes 589832 | tf_op jit(solution)/shard_map/ppermute | solution.py:535
  56.2 5.5 %collective-permute-done.8.refs_0_ = bf16[768,512]{1,0:T(8,128)(2,1)S(1)} collective-permute-done((bf16[768,512]{1,0:T(8,128)(2,1)S(1)}, bf16[768,512]{1,0:T(8,128)(2,1)S(1)}, u32[]{:S(2)}, u32[]{:S(2)}) %collective-permute-start.8) | collective-permute-done | bytes 786464 | tf_op jit(solution)/shard_map/ppermute | solution.py:542
  61.7 1.1 collective-permute-done.14.refs_5_
  62.8 1.6 collective-permute-start.19
  64.3 18.2 %collective-permute-done.9.refs_0_ = bf16[768,512]{1,0:T(8,128)(2,1)S(1)} collective-permute-done((bf16[768,512]{1,0:T(8,128)(2,1)S(1)}, bf16[768,512]{1,0:T(8,128)(2,1)S(1)}, u32[]{:S(2)}, u32[]{:S(2)}) %collective-permute-start.9) | collective-permute-done | bytes 786464 | tf_op jit(solution)/shard_map/ppermute | solution.py:542
  82.6 0.9 copy-done.2
  83.5 2.1 shard_map.88.refs_1_
  86.0 1.3 collective-permute-start.21
  87.3 1.5 collective-permute-start.20
  89.3 14.6 %collective-permute-done.20.refs_3_ = bf16[720,512]{1,0:T(8,128)(2,1)S(1)} collective-permute-done((bf16[720,512]{1,0:T(8,128)(2,1)S(1)}, bf16[720,512]{1,0:T(8,128)(2,1)S(1)}, u32[]{:S(2)}, u32[]{:S(2)}) %collective-permute-start.20) | collective-permute-done | bytes 737312 | tf_op jit(solution)/shard_map/ppermute | solution.py:535
  103.9 1.6 collective-permute-done.21.refs_4_
  105.5 13.5 %collective-permute-done.22.refs_5_ = bf16[720,512]{1,0:T(8,128)(2,1)S(1)} collective-permute-done((bf16[720,512]{1,0:T(8,128)(2,1)S(1)}, bf16[720,512]{1,0:T(8,128)(2,1)S(1)}, u32[]{:S(2)}, u32[]{:S(2)}) %collective-permute-start.22) | collective-permute-done | bytes 737312 | tf_op jit(solution)/shard_map/ppermute | solution.py:535
  119.0 3.6 %collective-permute-done.17.refs_0_ = bf16[768,512]{1,0:T(8,128)(2,1)S(1)} collective-permute-done((bf16[768,512]{1,0:T(8,128)(2,1)S(1)}, bf16[768,512]{1,0:T(8,128)(2,1)S(1)}, u32[]{:S(2)}, u32[]{:S(2)}) %collective-permute-start.17) | collective-permute-done | bytes 786464 | tf_op jit(solution)/shard_map/ppermute | solution.py:542
  122.5 1.0 collective-permute-start.25
  124.1 1.1 collective-permute-done.27.refs_8_.refs_7_
  125.3 13.5 %collective-permute-done.25.refs_6_ = bf16[720,512]{1,0:T(8,128)(2,1)S(1)} collective-permute-done((bf16[720,512]{1,0:T(8,128)(2,1)S(1)}, bf16[720,512]{1,0:T(8,128)(2,1)S(1)}, u32[]{:S(2)}, u32[]{:S(2)}) %collective-permute-start.25) | collective-permute-done | bytes 737312 | tf_op jit(solution)/shard_map/ppermute | solution.py:535
  138.7 0.6 collective-permute-start.26
  139.4 14.6 %collective-permute-done.26.refs_7_ = bf16[720,512]{1,0:T(8,128)(2,1)S(1)} collective-permute-done((bf16[720,512]{1,0:T(8,128)(2,1)S(1)}, bf16[720,512]{1,0:T(8,128)(2,1)S(1)}, u32[]{:S(2)}, u32[]{:S(2)}) %collective-permute-start.26) | collective-permute-done | bytes 737312 | tf_op jit(solution)/shard_map/ppermute | solution.py:535
  154.0 6.8 %shard_map.89 = (bf16[720,4096]{1,0:T(8,128)(2,1)S(1)}, bf16[720,192]{1,0:T(8,128)(2,1)S(1)}) custom-call(s32[10]{0:T(128)S(1)} %copy-done.3, bf16[720,512]{1,0:T(8,128)(2,1)S(1)} %get-tuple-element.183.refs_0_, bf16[720,512]{1,0:T(8,128)(2,1)S(1)} %collective-permute-done.7.refs_1_, bf16[720,512]{1,0:T(8,128)(2,1)S(1)} %collective-permute-done.19.refs_2_, ...), custom_call_target="tpu_custom_call" | custom-call | flops 283115520 | bytes 737280 | tf_op jit(solution)/shard_map/pallas_call | solution.py:278
  160.9 0.6 collective-permute-start.29
  162.0 4.9 %shard_map.90 = (f32[720,1536]{1,0:T(8,128)S(1)}, bf16[1536,4096]{1,0:T(8,128)(2,1)S(1)}) custom-call(s32[10]{0:T(128)S(1)} %copy-done.3, bf16[768,512]{1,0:T(8,128)(2,1)S(1)} %get-tuple-element.153.refs_0_, bf16[768,512]{1,0:T(8,128)(2,1)S(1)} %shard_map.88.refs_1_, bf16[768,512]{1,0:T(8,128)(2,1)S(1)} %collective-permute-done.33.refs_2_, ...), custom_call_target="tpu_custom_call" | custom-call | flops 141557760 | bytes 946176 | tf_op jit(solution)/shard_map/pallas_call | solution.py:366
  166.9 5.3 %shard_map.91 = (f32[720,1536]{1,0:T(8,128)S(1)}, bf16[1536,4096]{1,0:T(8,128)(2,1)S(1)}) custom-call(s32[10]{0:T(128)S(1)} %copy-done.3, bf16[768,512]{1,0:T(8,128)(2,1)S(1)} %collective-permute-done.8.refs_0_, bf16[768,512]{1,0:T(8,128)(2,1)S(1)} %collective-permute-done.18.refs_1_, ...), custom_call_target="tpu_custom_call", output_to_operand_aliasing={{0}: (6, {}), {1}: (7, {})} | custom-call | flops 141557760 | bytes 946176 | tf_op jit(solution)/shard_map/pallas_call | solution.py:366
  172.2 5.3 %shard_map.92 = (f32[720,1536]{1,0:T(8,128)S(1)}, bf16[1536,4096]{1,0:T(8,128)(2,1)S(1)}) custom-call(s32[10]{0:T(128)S(1)} %copy-done.3, bf16[768,512]{1,0:T(8,128)(2,1)S(1)} %collective-permute-done.9.refs_0_, bf16[768,512]{1,0:T(8,128)(2,1)S(1)} %collective-permute-done.24.refs_1_, ...), custom_call_target="tpu_custom_call", output_to_operand_aliasing={{0}: (6, {}), {1}: (7, {})} | custom-call | flops 141557760 | bytes 946176 | tf_op jit(solution)/shard_map/pallas_call | solution.py:366
  177.5 5.8 %collective-permute-done.28.refs_1_ = bf16[768,512]{1,0:T(8,128)(2,1)S(1)} collective-permute-done((bf16[768,512]{1,0:T(8,128)(2,1)S(1)}, bf16[768,512]{1,0:T(8,128)(2,1)S(1)}, u32[]{:S(2)}, u32[]{:S(2)}) %collective-permute-start.28) | collective-permute-done | bytes 786464 | tf_op jit(solution)/shard_map/ppermute | solution.py:542
  183.3 2.3 collective-permute-done.35.refs_3_
  185.6 7.1 %shard_map.93 = (f32[720,1536]{1,0:T(8,128)S(1)}, f32[8,1536]{1,0:T(8,128)S(1)}, bf16[1536,4096]{1,0:T(8,128)(2,1)S(1)}) custom-call(s32[10]{0:T(128)S(1)} %copy-done.3, bf16[768,512]{1,0:T(8,128)(2,1)S(1)} %collective-permute-done.17.refs_0_, bf16[768,512]{1,0:T(8,128)(2,1)S(1)} %collective-permute-done.28.refs_1_, ...), custom_call_target="tpu_custom_call", output_to_operand_aliasing={{0}: (6, {}), {2}: (7, {})} | custom-call | flops 141557760 | bytes 946176 | tf_op jit(solution)/shard_map/pallas_call | solution.py:366
  192.9 1.1 collective-permute-done.36.other_ref
  194.0 0.6 shard_map.94.refs_2_
  194.8 4.3 %collective-permute-start.39 = (f32[8,1536]{1,0:T(8,128)S(1)}, f32[8,1536]{1,0:T(8,128)S(1)}, u32[]{:S(2)}, u32[]{:S(2)}) collective-permute-start(f32[8,1536]{1,0:T(8,128)S(1)} %shard_map.94.refs_2_), channel_id=1, source_target_pairs={{0,3},{1,2},{2,1},{3,0},{4,7},{5,6},{6,5},{7,4},{8,11},{9,10},{10,... | collective-permute-start | bytes 147464 | tf_op jit(solution)/shard_map/ppermute | solution.py:596
  199.4 2.7 collective-permute-done.38.refs_4_
  202.1 4.2 %shard_map.95 = (bf16[720,512]{1,0:T(8,128)(2,1)S(1)}, bf16[720,512]{1,0:T(8,128)(2,1)S(1)}, bf16[720,1536]{1,0:T(8,128)(2,1)S(1)}, f32[1,768]{1,0:T(1,128)S(1)}, bf16[64,720]{1,0:T(8,128)(2,1)S(1)}) custom-call(s32[10]{0:T(128)S(1)} %copy-done.3, f32[720,1536]{1,0:T(8,128)S(1)} %get-tuple-element.208.refs_0_, ...), custom_call_target="tpu_custom_call" | custom-call | flops 141557760 | bytes 657408 | tf_op jit(solution)/shard_map/pallas_call | solution.py:442
  206.7 1.7 collective-permute-start.40
  208.9 3.3 %collective-permute-done.42 = bf16[64,720]{1,0:T(8,128)(2,1)S(1)} collective-permute-done((bf16[64,720]{1,0:T(8,128)(2,1)S(1)}, bf16[64,720]{1,0:T(8,128)(2,1)S(1)}, u32[]{:S(2)}, u32[]{:S(2)}) %collective-permute-start.42) | collective-permute-done | bytes 92192 | tf_op jit(solution)/shard_map/ppermute | solution.py:535
  212.2 0.5 collective-permute-start.43
  212.7 4.9 %shard_map.97 = (f32[720,512]{1,0:T(8,128)S(1)}, f32[720,512]{1,0:T(8,128)S(1)}, f32[720,512]{1,0:T(8,128)S(1)}) custom-call(s32[10]{0:T(128)S(1)} %copy-done.3, bf16[720,1536]{1,0:T(8,128)(2,1)S(1)} %get-tuple-element.213.refs_0_, bf16[1536,4096]{1,0:T(8,128)(2,1)S(1)} %get-tuple-element.210.refs_8_.refs_1_), custom_call_target="tpu_custom_call" | custom-call | flops 212336640 | bytes 847872 | tf_op jit(solution)/shard_map/pallas_call | solution.py:442
  217.6 6.3 %shard_map.96 = (bf16[720,512]{1,0:T(8,128)(2,1)}, bf16[720,512]{1,0:T(8,128)(2,1)}, bf16[720,512]{1,0:T(8,128)(2,1)}) custom-call(s32[10]{0:T(128)S(1)} %copy-done.3, bf16[720,1536]{1,0:T(8,128)(2,1)S(1)} %get-tuple-element.213.refs_0_, bf16[1536,4096]{1,0:T(8,128)(2,1)S(1)} %get-tuple-element.210.refs_8_.refs_1_), custom_call_target="tpu_custom_call" | custom-call | flops 212336640 | bytes 847872 | tf_op jit(solution)/shard_map/pallas_call | solution.py:442
  223.9 5.0 %collective-permute-done.43 = f32[64,720]{1,0:T(8,128)S(1)} collective-permute-done((f32[64,720]{1,0:T(8,128)S(1)}, f32[64,720]{1,0:T(8,128)S(1)}, u32[]{:S(2)}, u32[]{:S(2)}) %collective-permute-start.43) | collective-permute-done | bytes 184352 | tf_op jit(solution)/shard_map/ppermute | solution.py:535
  229.0 2.0 shard_map.98
  231.4 1.4 collective-permute-start.47
  233.3 1.5 collective-permute-start.48
  234.8 0.6 reduce
  235.4 0.9 maximum_select_fusion
  236.3 14.2 %collective-permute-done.44.a_ref = bf16[720,512]{1,0:T(8,128)(2,1)S(1)} collective-permute-done((bf16[720,512]{1,0:T(8,128)(2,1)}, bf16[720,512]{1,0:T(8,128)(2,1)S(1)}, u32[]{:S(2)}, u32[]{:S(2)}) %collective-permute-start.44) | collective-permute-done | bytes 737312 | tf_op jit(solution)/shard_map/ppermute | solution.py:539
  250.5 15.4 %collective-permute-done.45.c_ref = bf16[720,512]{1,0:T(8,128)(2,1)} collective-permute-done((bf16[720,512]{1,0:T(8,128)(2,1)}, bf16[720,512]{1,0:T(8,128)(2,1)}, u32[]{:S(2)}, u32[]{:S(2)}) %collective-permute-start.45) | collective-permute-done | bytes 737312 | tf_op jit(solution)/shard_map/ppermute | solution.py:539
  266.0 4.9 %shard_map.99 = f32[1440,512]{1,0:T(8,128)} custom-call(s32[10]{0:T(128)S(1)} %copy-done.3, f32[720,512]{1,0:T(8,128)S(1)} %get-tuple-element.221.keep_ref, bf16[720,512]{1,0:T(8,128)(2,1)S(1)} %collective-permute-done.44.a_ref, bf16[720,512]{1,0:T(8,128)(2,1)} %collective-permute-done.45.c_ref, bf16[720,512]{1,0:T(8,128)(2,1)} %collective-permute-done.46.other_ref, ...), custom_call_target="tpu_custom_call" | custom-call | tf_op jit(solution)/shard_map/pallas_call | solution.py:496
  (69 shorter events, 5.3 us)
Async XLA Ops:
  1.3 7.2 %copy-start.5 = (bf16[1440,512]{1,0:T(8,128)(2,1)S(1)}, bf16[1440,512]{1,0:T(8,128)(2,1)}, u32[]{:S(2)}) copy-start(bf16[1440,512]{1,0:T(8,128)(2,1)} %param.11) | copy-start | bytes 4423684
  8.5 27.3 %collective-permute-start.7 = (bf16[720,512]{1,0:T(8,128)(2,1)S(1)}, bf16[720,512]{1,0:T(8,128)(2,1)S(1)}, u32[]{:S(2)}, u32[]{:S(2)}) collective-permute-start(bf16[720,512]{1,0:T(8,128)(2,1)S(1)} %get-tuple-element.233), channel_id=1, source_target_pairs={{0,4},{4,0},{8,12},{12,8},{16,20},{20,16},{24,28},{28,24},{1,5},{5... | collective-permute-start | bytes 2211848 | tf_op jit(solution)/shard_map/ppermute | solution.py:535
  9.1 4.5 %collective-permute-start = (bf16[192,640]{1,0:T(8,128)(2,1)}, bf16[192,640]{1,0:T(8,128)(2,1)S(1)}, u32[]{:S(2)}, u32[]{:S(2)}) collective-permute-start(bf16[192,640]{1,0:T(8,128)(2,1)} %get-tuple-element.119), channel_id=1, source_target_pairs={{0,4},{4,0},{8,12},{12,8},{16,20},{20,16},{24,28},{28,24},{1,5},{5... | collective-permute-start | bytes 737288 | tf_op jit(solution)/shard_map/ppermute | solution.py:535
  9.1 9.9 %collective-permute-start.1 = (bf16[192,640]{1,0:T(8,128)(2,1)}, bf16[192,640]{1,0:T(8,128)(2,1)S(1)}, u32[]{:S(2)}, u32[]{:S(2)}) collective-permute-start(bf16[192,640]{1,0:T(8,128)(2,1)} %get-tuple-element.120), channel_id=1, source_target_pairs={{0,8},{4,12},{8,0},{12,4},{16,24},{20,28},{24,16},{28,20},{1,9},{5... | collective-permute-start | bytes 737288 | tf_op jit(solution)/shard_map/ppermute | solution.py:535
  12.1 11.9 %collective-permute-start.2 = (bf16[192,640]{1,0:T(8,128)(2,1)}, bf16[192,640]{1,0:T(8,128)(2,1)S(1)}, u32[]{:S(2)}, u32[]{:S(2)}) collective-permute-start(bf16[192,640]{1,0:T(8,128)(2,1)} %get-tuple-element.121), channel_id=1, source_target_pairs={{0,12},{4,8},{8,4},{12,0},{16,28},{20,24},{24,20},{28,16},{1,13},{... | collective-permute-start | bytes 737288 | tf_op jit(solution)/shard_map/ppermute | solution.py:535
  12.1 20.5 %collective-permute-start.3 = (bf16[192,640]{1,0:T(8,128)(2,1)}, bf16[192,640]{1,0:T(8,128)(2,1)S(1)}, u32[]{:S(2)}, u32[]{:S(2)}) collective-permute-start(bf16[192,640]{1,0:T(8,128)(2,1)} %get-tuple-element.122), channel_id=1, source_target_pairs={{0,16},{4,20},{8,24},{12,28},{16,0},{20,4},{24,8},{28,12},{1,17},{... | collective-permute-start | bytes 737288 | tf_op jit(solution)/shard_map/ppermute | solution.py:535
  13.6 22.3 %collective-permute-start.4 = (bf16[192,640]{1,0:T(8,128)(2,1)}, bf16[192,640]{1,0:T(8,128)(2,1)S(1)}, u32[]{:S(2)}, u32[]{:S(2)}) collective-permute-start(bf16[192,640]{1,0:T(8,128)(2,1)} %get-tuple-element.123), channel_id=1, source_target_pairs={{0,20},{4,16},{8,28},{12,24},{16,4},{20,0},{24,12},{28,8},{1,21},{... | collective-permute-start | bytes 737288 | tf_op jit(solution)/shard_map/ppermute | solution.py:535
  19.0 16.9 %collective-permute-start.5 = (bf16[192,640]{1,0:T(8,128)(2,1)}, bf16[192,640]{1,0:T(8,128)(2,1)S(1)}, u32[]{:S(2)}, u32[]{:S(2)}) collective-permute-start(bf16[192,640]{1,0:T(8,128)(2,1)} %get-tuple-element.124), channel_id=1, source_target_pairs={{0,24},{4,28},{8,16},{12,20},{16,8},{20,12},{24,0},{28,4},{1,25},{... | collective-permute-start | bytes 737288 | tf_op jit(solution)/shard_map/ppermute | solution.py:535
  24.0 11.9 %copy-start = (f32[64,2048]{1,0:T(8,128)S(1)}, f32[64,2048]{1,0:T(8,128)}, u32[]{:S(2)}) copy-start(f32[64,2048]{1,0:T(8,128)} %refs_8_.3) | copy-start | bytes 1572868
  24.0 11.9 %copy-start.1 = (bf16[192,640]{1,0:T(8,128)(2,1)S(1)}, bf16[192,640]{1,0:T(8,128)(2,1)}, u32[]{:S(2)}) copy-start(bf16[192,640]{1,0:T(8,128)(2,1)} %get-tuple-element.136.refs_0_) | copy-start | bytes 737284
  24.0 11.9 %copy-start.3 = (s32[10]{0:T(128)S(1)}, s32[10]{0:T(128)}, u32[]{:S(2)}) copy-start(s32[10]{0:T(128)} %stack.43.meta) | copy-start | bytes 124
  24.0 11.9 %copy-start.4 = (f32[2048]{0:T(1024)S(1)}, f32[2048]{0:T(1024)}, u32[]{:S(2)}) copy-start(f32[2048]{0:T(1024)} %param.10) | copy-start | bytes 24580
  24.0 11.9 %collective-permute-start.6 = (bf16[192,640]{1,0:T(8,128)(2,1)}, bf16[192,640]{1,0:T(8,128)(2,1)S(1)}, u32[]{:S(2)}, u32[]{:S(2)}) collective-permute-start(bf16[192,640]{1,0:T(8,128)(2,1)} %get-tuple-element.125), channel_id=1, source_target_pairs={{0,28},{4,24},{8,20},{12,16},{16,12},{20,8},{24,4},{28,0},{1,29},{... | collective-permute-start | bytes 737288 | tf_op jit(solution)/shard_map/ppermute | solution.py:535
  39.8 21.9 %collective-permute-start.8 = (bf16[768,512]{1,0:T(8,128)(2,1)S(1)}, bf16[768,512]{1,0:T(8,128)(2,1)S(1)}, u32[]{:S(2)}, u32[]{:S(2)}) collective-permute-start(bf16[768,512]{1,0:T(8,128)(2,1)S(1)} %get-tuple-element.153.refs_0_), channel_id=1, source_target_pairs={{0,1},{1,2},{2,3},{3,0},{4,5},{5,6},{6,7},{7,4},{8,9},{9,10},{10,1... | collective-permute-start | bytes 2359304 | tf_op jit(solution)/shard_map/ppermute | solution.py:542
  41.8 3.4 %collective-permute-start.10 = (bf16[192,512]{1,0:T(8,128)(2,1)}, bf16[192,512]{1,0:T(8,128)(2,1)S(1)}, u32[]{:S(2)}, u32[]{:S(2)}) collective-permute-start(bf16[192,512]{1,0:T(8,128)(2,1)} %get-tuple-element.155), channel_id=1, source_target_pairs={{0,4},{4,0},{8,12},{12,8},{16,20},{20,16},{24,28},{28,24},{1,5},{5... | collective-permute-start | bytes 589832 | tf_op jit(solution)/shard_map/ppermute | solution.py:535
  41.8 7.9 %collective-permute-start.11 = (bf16[192,512]{1,0:T(8,128)(2,1)}, bf16[192,512]{1,0:T(8,128)(2,1)S(1)}, u32[]{:S(2)}, u32[]{:S(2)}) collective-permute-start(bf16[192,512]{1,0:T(8,128)(2,1)} %get-tuple-element.156), channel_id=1, source_target_pairs={{0,8},{4,12},{8,0},{12,4},{16,24},{20,28},{24,16},{28,20},{1,9},{5... | collective-permute-start | bytes 589832 | tf_op jit(solution)/shard_map/ppermute | solution.py:535
  43.4 9.8 %collective-permute-start.12 = (bf16[192,512]{1,0:T(8,128)(2,1)}, bf16[192,512]{1,0:T(8,128)(2,1)S(1)}, u32[]{:S(2)}, u32[]{:S(2)}) collective-permute-start(bf16[192,512]{1,0:T(8,128)(2,1)} %get-tuple-element.157), channel_id=1, source_target_pairs={{0,12},{4,8},{8,4},{12,0},{16,28},{20,24},{24,20},{28,16},{1,13},{... | collective-permute-start | bytes 589832 | tf_op jit(solution)/shard_map/ppermute | solution.py:535
  43.7 18.0 %collective-permute-start.13 = (bf16[192,512]{1,0:T(8,128)(2,1)}, bf16[192,512]{1,0:T(8,128)(2,1)S(1)}, u32[]{:S(2)}, u32[]{:S(2)}) collective-permute-start(bf16[192,512]{1,0:T(8,128)(2,1)} %get-tuple-element.158), channel_id=1, source_target_pairs={{0,16},{4,20},{8,24},{12,28},{16,0},{20,4},{24,8},{28,12},{1,17},{... | collective-permute-start | bytes 589832 | tf_op jit(solution)/shard_map/ppermute | solution.py:535
  45.2 17.6 %collective-permute-start.14 = (bf16[192,512]{1,0:T(8,128)(2,1)}, bf16[192,512]{1,0:T(8,128)(2,1)S(1)}, u32[]{:S(2)}, u32[]{:S(2)}) collective-permute-start(bf16[192,512]{1,0:T(8,128)(2,1)} %get-tuple-element.159), channel_id=1, source_target_pairs={{0,20},{4,16},{8,28},{12,24},{16,4},{20,0},{24,12},{28,8},{1,21},{... | collective-permute-start | bytes 589832 | tf_op jit(solution)/shard_map/ppermute | solution.py:535
  49.7 13.0 %collective-permute-start.15 = (bf16[192,512]{1,0:T(8,128)(2,1)}, bf16[192,512]{1,0:T(8,128)(2,1)S(1)}, u32[]{:S(2)}, u32[]{:S(2)}) collective-permute-start(bf16[192,512]{1,0:T(8,128)(2,1)} %get-tuple-element.160), channel_id=1, source_target_pairs={{0,24},{4,28},{8,16},{12,20},{16,8},{20,12},{24,0},{28,4},{1,25},{... | collective-permute-start | bytes 589832 | tf_op jit(solution)/shard_map/ppermute | solution.py:535
  53.2 9.6 %collective-permute-start.16 = (bf16[192,512]{1,0:T(8,128)(2,1)}, bf16[192,512]{1,0:T(8,128)(2,1)S(1)}, u32[]{:S(2)}, u32[]{:S(2)}) collective-permute-start(bf16[192,512]{1,0:T(8,128)(2,1)} %get-tuple-element.161), channel_id=1, source_target_pairs={{0,28},{4,24},{8,20},{12,16},{16,12},{20,8},{24,4},{28,0},{1,29},{... | collective-permute-start | bytes 589832 | tf_op jit(solution)/shard_map/ppermute | solution.py:535
  61.7 20.9 %collective-permute-start.9 = (bf16[768,512]{1,0:T(8,128)(2,1)S(1)}, bf16[768,512]{1,0:T(8,128)(2,1)S(1)}, u32[]{:S(2)}, u32[]{:S(2)}) collective-permute-start(bf16[768,512]{1,0:T(8,128)(2,1)S(1)} %collective-permute-done.8.refs_0_), channel_id=1, source_target_pairs={{0,1},{1,2},{2,3},{3,0},{4,5},{5,6},{6,7},{7,4},{8,9},{9,10},{10,1... | collective-permute-start | bytes 2359304 | tf_op jit(solution)/shard_map/ppermute | solution.py:542
  62.8 26.0 %collective-permute-start.19 = (bf16[720,512]{1,0:T(8,128)(2,1)S(1)}, bf16[720,512]{1,0:T(8,128)(2,1)S(1)}, u32[]{:S(2)}, u32[]{:S(2)}) collective-permute-start(bf16[720,512]{1,0:T(8,128)(2,1)S(1)} %get-tuple-element.183.refs_0_), channel_id=1, source_target_pairs={{0,8},{4,12},{8,0},{12,4},{16,24},{20,28},{24,16},{28,20},{1,9},{5... | collective-permute-start | bytes 2211848 | tf_op jit(solution)/shard_map/ppermute | solution.py:535
  82.6 0.9 copy-start.2
  85.7 33.3 %collective-permute-start.18 = (bf16[768,512]{1,0:T(8,128)(2,1)S(1)}, bf16[768,512]{1,0:T(8,128)(2,1)S(1)}, u32[]{:S(2)}, u32[]{:S(2)}) collective-permute-start(bf16[768,512]{1,0:T(8,128)(2,1)S(1)} %shard_map.88.refs_1_), channel_id=1, source_target_pairs={{0,1},{1,2},{2,3},{3,0},{4,5},{5,6},{6,7},{7,4},{8,9},{9,10},{10,1... | collective-permute-start | bytes 2359304 | tf_op jit(solution)/shard_map/ppermute | solution.py:542
  85.7 36.8 %collective-permute-start.17 = (bf16[768,512]{1,0:T(8,128)(2,1)S(1)}, bf16[768,512]{1,0:T(8,128)(2,1)S(1)}, u32[]{:S(2)}, u32[]{:S(2)}) collective-permute-start(bf16[768,512]{1,0:T(8,128)(2,1)S(1)} %collective-permute-done.9.refs_0_), channel_id=1, source_target_pairs={{0,1},{1,2},{2,3},{3,0},{4,5},{5,6},{6,7},{7,4},{8,9},{9,10},{10,1... | collective-permute-start | bytes 2359304 | tf_op jit(solution)/shard_map/ppermute | solution.py:542
  86.0 19.5 %collective-permute-start.21 = (bf16[720,512]{1,0:T(8,128)(2,1)S(1)}, bf16[720,512]{1,0:T(8,128)(2,1)S(1)}, u32[]{:S(2)}, u32[]{:S(2)}) collective-permute-start(bf16[720,512]{1,0:T(8,128)(2,1)S(1)} %get-tuple-element.183.refs_0_), channel_id=1, source_target_pairs={{0,16},{4,20},{8,24},{12,28},{16,0},{20,4},{24,8},{28,12},{1,17},{... | collective-permute-start | bytes 2211848 | tf_op jit(solution)/shard_map/ppermute | solution.py:535
  87.3 16.6 %collective-permute-start.20 = (bf16[720,512]{1,0:T(8,128)(2,1)S(1)}, bf16[720,512]{1,0:T(8,128)(2,1)S(1)}, u32[]{:S(2)}, u32[]{:S(2)}) collective-permute-start(bf16[720,512]{1,0:T(8,128)(2,1)S(1)} %collective-permute-done.7.refs_1_), channel_id=1, source_target_pairs={{0,8},{4,12},{8,0},{12,4},{16,24},{20,28},{24,16},{28,20},{1,9},{5... | collective-permute-start | bytes 2211848 | tf_op jit(solution)/shard_map/ppermute | solution.py:535
  88.8 30.2 %collective-permute-start.22 = (bf16[720,512]{1,0:T(8,128)(2,1)S(1)}, bf16[720,512]{1,0:T(8,128)(2,1)S(1)}, u32[]{:S(2)}, u32[]{:S(2)}) collective-permute-start(bf16[720,512]{1,0:T(8,128)(2,1)S(1)} %collective-permute-done.7.refs_1_), channel_id=1, source_target_pairs={{0,16},{4,20},{8,24},{12,28},{16,0},{20,4},{24,8},{28,12},{1,17},{... | collective-permute-start | bytes 2211848 | tf_op jit(solution)/shard_map/ppermute | solution.py:535
  122.5 16.2 %collective-permute-start.25 = (bf16[720,512]{1,0:T(8,128)(2,1)S(1)}, bf16[720,512]{1,0:T(8,128)(2,1)S(1)}, u32[]{:S(2)}, u32[]{:S(2)}) collective-permute-start(bf16[720,512]{1,0:T(8,128)(2,1)S(1)} %collective-permute-done.19.refs_2_), channel_id=1, source_target_pairs={{0,16},{4,20},{8,24},{12,28},{16,0},{20,4},{24,8},{28,12},{1,17},{... | collective-permute-start | bytes 2211848 | tf_op jit(solution)/shard_map/ppermute | solution.py:535
  123.6 1.6 collective-permute-start.27
  123.6 37.3 %collective-permute-start.24 = (bf16[768,512]{1,0:T(8,128)(2,1)S(1)}, bf16[768,512]{1,0:T(8,128)(2,1)S(1)}, u32[]{:S(2)}, u32[]{:S(2)}) collective-permute-start(bf16[768,512]{1,0:T(8,128)(2,1)S(1)} %collective-permute-done.18.refs_1_), channel_id=1, source_target_pairs={{0,1},{1,2},{2,3},{3,0},{4,5},{5,6},{6,7},{7,4},{8,9},{9,10},{10,1... | collective-permute-start | bytes 2359304 | tf_op jit(solution)/shard_map/ppermute | solution.py:542
  123.6 37.9 %collective-permute-start.33 = (bf16[768,512]{1,0:T(8,128)(2,1)S(1)}, bf16[768,512]{1,0:T(8,128)(2,1)S(1)}, u32[]{:S(2)}, u32[]{:S(2)}) collective-permute-start(bf16[768,512]{1,0:T(8,128)(2,1)S(1)} %get-tuple-element.153.refs_0_), channel_id=1, source_target_pairs={{0,4},{4,0},{8,12},{12,8},{16,20},{20,16},{24,28},{28,24},{1,5},{5... | collective-permute-start | bytes 2359304 | tf_op jit(solution)/shard_map/ppermute | solution.py:535
  124.1 37.5 %collective-permute-start.31 = (bf16[768,512]{1,0:T(8,128)(2,1)S(1)}, bf16[768,512]{1,0:T(8,128)(2,1)S(1)}, u32[]{:S(2)}, u32[]{:S(2)}) collective-permute-start(bf16[768,512]{1,0:T(8,128)(2,1)S(1)} %collective-permute-done.8.refs_0_), channel_id=1, source_target_pairs={{0,4},{4,0},{8,12},{12,8},{16,20},{20,16},{24,28},{28,24},{1,5},{5... | collective-permute-start | bytes 2359304 | tf_op jit(solution)/shard_map/ppermute | solution.py:535
  125.1 36.8 %collective-permute-start.34 = (bf16[768,512]{1,0:T(8,128)(2,1)S(1)}, bf16[768,512]{1,0:T(8,128)(2,1)S(1)}, u32[]{:S(2)}, u32[]{:S(2)}) collective-permute-start(bf16[768,512]{1,0:T(8,128)(2,1)S(1)} %shard_map.88.refs_1_), channel_id=1, source_target_pairs={{0,4},{4,0},{8,12},{12,8},{16,20},{20,16},{24,28},{28,24},{1,5},{5... | collective-permute-start | bytes 2359304 | tf_op jit(solution)/shard_map/ppermute | solution.py:535
  138.7 15.3 %collective-permute-start.26 = (bf16[720,512]{1,0:T(8,128)(2,1)S(1)}, bf16[720,512]{1,0:T(8,128)(2,1)S(1)}, u32[]{:S(2)}, u32[]{:S(2)}) collective-permute-start(bf16[720,512]{1,0:T(8,128)(2,1)S(1)} %collective-permute-done.22.refs_5_), channel_id=1, source_target_pairs={{0,8},{4,12},{8,0},{12,4},{16,24},{20,28},{24,16},{28,20},{1,9},{5... | collective-permute-start | bytes 2211848 | tf_op jit(solution)/shard_map/ppermute | solution.py:535
  154.0 12.9 %collective-permute-start.32 = (bf16[768,512]{1,0:T(8,128)(2,1)S(1)}, bf16[768,512]{1,0:T(8,128)(2,1)S(1)}, u32[]{:S(2)}, u32[]{:S(2)}) collective-permute-start(bf16[768,512]{1,0:T(8,128)(2,1)S(1)} %collective-permute-done.18.refs_1_), channel_id=1, source_target_pairs={{0,4},{4,0},{8,12},{12,8},{16,20},{20,16},{24,28},{28,24},{1,5},{5... | collective-permute-start | bytes 2359304 | tf_op jit(solution)/shard_map/ppermute | solution.py:535
  160.9 11.3 %collective-permute-start.29 = (bf16[768,512]{1,0:T(8,128)(2,1)S(1)}, bf16[768,512]{1,0:T(8,128)(2,1)S(1)}, u32[]{:S(2)}, u32[]{:S(2)}) collective-permute-start(bf16[768,512]{1,0:T(8,128)(2,1)S(1)} %collective-permute-done.9.refs_0_), channel_id=1, source_target_pairs={{0,4},{4,0},{8,12},{12,8},{16,20},{20,16},{24,28},{28,24},{1,5},{5... | collective-permute-start | bytes 2359304 | tf_op jit(solution)/shard_map/ppermute | solution.py:535
  161.5 10.8 %collective-permute-start.30 = (bf16[768,512]{1,0:T(8,128)(2,1)S(1)}, bf16[768,512]{1,0:T(8,128)(2,1)S(1)}, u32[]{:S(2)}, u32[]{:S(2)}) collective-permute-start(bf16[768,512]{1,0:T(8,128)(2,1)S(1)} %collective-permute-done.24.refs_1_), channel_id=1, source_target_pairs={{0,4},{4,0},{8,12},{12,8},{16,20},{20,16},{24,28},{28,24},{1,5},{5... | collective-permute-start | bytes 2359304 | tf_op jit(solution)/shard_map/ppermute | solution.py:535
  161.6 16.0 %collective-permute-start.23 = (bf16[768,512]{1,0:T(8,128)(2,1)S(1)}, bf16[768,512]{1,0:T(8,128)(2,1)S(1)}, u32[]{:S(2)}, u32[]{:S(2)}) collective-permute-start(bf16[768,512]{1,0:T(8,128)(2,1)S(1)} %collective-permute-done.17.refs_0_), channel_id=1, source_target_pairs={{0,4},{4,0},{8,12},{12,8},{16,20},{20,16},{24,28},{28,24},{1,5},{5... | collective-permute-start | bytes 2359304 | tf_op jit(solution)/shard_map/ppermute | solution.py:535
  162.0 21.3 %collective-permute-start.28 = (bf16[768,512]{1,0:T(8,128)(2,1)S(1)}, bf16[768,512]{1,0:T(8,128)(2,1)S(1)}, u32[]{:S(2)}, u32[]{:S(2)}) collective-permute-start(bf16[768,512]{1,0:T(8,128)(2,1)S(1)} %collective-permute-done.24.refs_1_), channel_id=1, source_target_pairs={{0,1},{1,2},{2,3},{3,0},{4,5},{5,6},{6,7},{7,4},{8,9},{9,10},{10,1... | collective-permute-start | bytes 2359304 | tf_op jit(solution)/shard_map/ppermute | solution.py:542
  183.3 2.3 collective-permute-start.35
  192.7 1.3 collective-permute-start.36
  194.6 4.8 %collective-permute-start.37 = (f32[8,1536]{1,0:T(8,128)S(1)}, f32[8,1536]{1,0:T(8,128)S(1)}, u32[]{:S(2)}, u32[]{:S(2)}) collective-permute-start(f32[8,1536]{1,0:T(8,128)S(1)} %shard_map.94.refs_2_), channel_id=1, source_target_pairs={{0,1},{1,0},{2,3},{3,2},{4,5},{5,4},{6,7},{7,6},{8,9},{9,8},{10,11... | collective-permute-start | bytes 147464 | tf_op jit(solution)/shard_map/ppermute | solution.py:596
  194.7 7.4 %collective-permute-start.38 = (f32[8,1536]{1,0:T(8,128)S(1)}, f32[8,1536]{1,0:T(8,128)S(1)}, u32[]{:S(2)}, u32[]{:S(2)}) collective-permute-start(f32[8,1536]{1,0:T(8,128)S(1)} %shard_map.94.refs_2_), channel_id=1, source_target_pairs={{0,2},{1,3},{2,0},{3,1},{4,6},{5,7},{6,4},{7,5},{8,10},{9,11},{10,... | collective-permute-start | bytes 147464 | tf_op jit(solution)/shard_map/ppermute | solution.py:596
  194.8 7.3 %collective-permute-start.39 = (f32[8,1536]{1,0:T(8,128)S(1)}, f32[8,1536]{1,0:T(8,128)S(1)}, u32[]{:S(2)}, u32[]{:S(2)}) collective-permute-start(f32[8,1536]{1,0:T(8,128)S(1)} %shard_map.94.refs_2_), channel_id=1, source_target_pairs={{0,3},{1,2},{2,1},{3,0},{4,7},{5,6},{6,5},{7,4},{8,11},{9,10},{10,... | collective-permute-start | bytes 147464 | tf_op jit(solution)/shard_map/ppermute | solution.py:596
  206.3 5.8 %collective-permute-start.42 = (bf16[64,720]{1,0:T(8,128)(2,1)S(1)}, bf16[64,720]{1,0:T(8,128)(2,1)S(1)}, u32[]{:S(2)}, u32[]{:S(2)}) collective-permute-start(bf16[64,720]{1,0:T(8,128)(2,1)S(1)} %get-tuple-element.220), channel_id=1, source_target_pairs={{0,8},{4,12},{8,0},{12,4},{16,24},{20,28},{24,16},{28,20},{1,9},{5... | collective-permute-start | bytes 276488 | tf_op jit(solution)/shard_map/ppermute | solution.py:535
  206.7 22.2 %collective-permute-start.40 = (bf16[720,512]{1,0:T(8,128)(2,1)S(1)}, bf16[720,512]{1,0:T(8,128)(2,1)S(1)}, u32[]{:S(2)}, u32[]{:S(2)}) collective-permute-start(bf16[720,512]{1,0:T(8,128)(2,1)S(1)} %get-tuple-element.211), channel_id=1, source_target_pairs={{0,8},{4,12},{8,0},{12,4},{16,24},{20,28},{24,16},{28,20},{1,9},{5... | collective-permute-start | bytes 2211848 | tf_op jit(solution)/shard_map/ppermute | solution.py:535
  208.4 20.5 %collective-permute-start.41 = (bf16[720,512]{1,0:T(8,128)(2,1)S(1)}, bf16[720,512]{1,0:T(8,128)(2,1)S(1)}, u32[]{:S(2)}, u32[]{:S(2)}) collective-permute-start(bf16[720,512]{1,0:T(8,128)(2,1)S(1)} %get-tuple-element.212), channel_id=1, source_target_pairs={{0,16},{4,20},{8,24},{12,28},{16,0},{20,4},{24,8},{28,12},{1,17},{... | collective-permute-start | bytes 2211848 | tf_op jit(solution)/shard_map/ppermute | solution.py:535
  212.2 16.7 %collective-permute-start.43 = (f32[64,720]{1,0:T(8,128)S(1)}, f32[64,720]{1,0:T(8,128)S(1)}, u32[]{:S(2)}, u32[]{:S(2)}) collective-permute-start(f32[64,720]{1,0:T(8,128)S(1)} %convert_add_fusion), channel_id=1, source_target_pairs={{0,16},{4,20},{8,24},{12,28},{16,0},{20,4},{24,8},{28,12},{1,17},{... | collective-permute-start | bytes 552968 | tf_op jit(solution)/shard_map/ppermute | solution.py:535
  228.9 4.4 %collective-permute-start.49 = (f32[64,720]{1,0:T(8,128)S(1)}, f32[64,720]{1,0:T(8,128)S(1)}, u32[]{:S(2)}, u32[]{:S(2)}) collective-permute-start(f32[64,720]{1,0:T(8,128)S(1)} %fusion), channel_id=1, source_target_pairs={{0,4},{4,0},{8,12},{12,8},{16,20},{20,16},{24,28},{28,24},{1,5},{5... | collective-permute-start | bytes 552968 | tf_op jit(solution)/shard_map/ppermute | solution.py:535
  231.0 19.6 %collective-permute-start.44 = (bf16[720,512]{1,0:T(8,128)(2,1)}, bf16[720,512]{1,0:T(8,128)(2,1)S(1)}, u32[]{:S(2)}, u32[]{:S(2)}) collective-permute-start(bf16[720,512]{1,0:T(8,128)(2,1)} %get-tuple-element.226), channel_id=1, source_target_pairs={{0,16},{4,12},{8,24},{12,4},{16,0},{20,28},{24,8},{28,20},{1,17},{... | collective-permute-start | bytes 2211848 | tf_op jit(solution)/shard_map/ppermute | solution.py:539
  231.4 19.1 %collective-permute-start.47 = (bf16[720,512]{1,0:T(8,128)(2,1)}, bf16[720,512]{1,0:T(8,128)(2,1)S(1)}, u32[]{:S(2)}, u32[]{:S(2)}) collective-permute-start(bf16[720,512]{1,0:T(8,128)(2,1)} %get-tuple-element.229), channel_id=1, source_target_pairs={{0,12},{4,16},{8,4},{12,24},{16,28},{20,0},{24,20},{28,8},{1,13},{... | collective-permute-start | bytes 2211848 | tf_op jit(solution)/shard_map/ppermute | solution.py:539
  232.8 33.2 %collective-permute-start.45 = (bf16[720,512]{1,0:T(8,128)(2,1)}, bf16[720,512]{1,0:T(8,128)(2,1)}, u32[]{:S(2)}, u32[]{:S(2)}) collective-permute-start(bf16[720,512]{1,0:T(8,128)(2,1)} %get-tuple-element.227), channel_id=1, source_target_pairs={{0,8},{4,20},{8,0},{12,28},{16,24},{20,4},{24,16},{28,12},{1,9},{5... | collective-permute-start | bytes 2211848 | tf_op jit(solution)/shard_map/ppermute | solution.py:539
  233.2 32.8 %collective-permute-start.46 = (bf16[720,512]{1,0:T(8,128)(2,1)}, bf16[720,512]{1,0:T(8,128)(2,1)}, u32[]{:S(2)}, u32[]{:S(2)}) collective-permute-start(bf16[720,512]{1,0:T(8,128)(2,1)} %get-tuple-element.228), channel_id=1, source_target_pairs={{0,4},{4,0},{8,12},{12,8},{16,20},{20,16},{24,28},{28,24},{1,5},{5... | collective-permute-start | bytes 2211848 | tf_op jit(solution)/shard_map/ppermute | solution.py:535
  233.3 32.7 %collective-permute-start.48 = (bf16[720,512]{1,0:T(8,128)(2,1)}, bf16[720,512]{1,0:T(8,128)(2,1)}, u32[]{:S(2)}, u32[]{:S(2)}) collective-permute-start(bf16[720,512]{1,0:T(8,128)(2,1)} %get-tuple-element.230), channel_id=1, source_target_pairs={{0,20},{4,8},{8,28},{12,0},{16,4},{20,24},{24,12},{28,16},{1,21},{... | collective-permute-start | bytes 2211848 | tf_op jit(solution)/shard_map/ppermute | solution.py:539

commit v6 on v5

--- a/solution.py
+++ b/solution.py
@@ -10,7 +10,8 @@
 NN = (((1,), (0,)), ((), ()))
 NT = (((1,), (1,)), ((), ()))
 F32, BF16, I32 = jnp.float32, jnp.bfloat16, jnp.int32
-CODE = 128
+CODE = 16
+LANES = 128
 MIB = 1024 * 1024
 
 
@@ -79,8 +80,12 @@
     return jnp.concatenate(found, axis=1).astype(I32) - 1, local
 
 
-def pack_first_body(dom, shard_rows, cap, meta, dest_ref, bin_ref, raw_ref, *refs):
-    outs, (place_ref, pick) = refs[:dom], refs[dom:]
+def joined(refs):
+    return jnp.concatenate([ref[...] for ref in refs], axis=1)
+
+
+def pack_first_body(dom, shard_rows, cap, meta, dest_ref, bin_ref, *refs):
+    raw, outs, (place_ref, pick) = refs[: -dom - 2], refs[-dom - 2 : -2], refs[-2:]
     dest = dest_ref[...].reshape(1, dest_ref.shape[0])
     bins = bin_ref[...].reshape(1, dest_ref.shape[0])
     place, local = places_of(dest, shard_rows, cap, dom, meta[0])
@@ -93,84 +98,88 @@
         jnp.where(which == 1, local & 15, jnp.where(which == 2, bins, jnp.where(which == 3, 1, 0))),
     )
     digits = jnp.where(dest >= 0, digits, 0).astype(F32).astype(BF16)
-    codes = mm(pick[...], digits, NT).astype(BF16)
-    packed = mm(pick[...], raw_ref[...], NN).astype(BF16)
+    codes = mm(digits, pick[...], NT)
+    packed = mm(pick[...], joined(raw), NN).astype(BF16)
     for index, out_ref in enumerate(outs):
-        out_ref[:, :CODE] = codes[index * cap : (index + 1) * cap]
-        out_ref[:, CODE:] = packed[index * cap : (index + 1) * cap]
-
-
-def pack_next_body(cap, meta, place_ref, raw_ref, *refs):
-    outs, pick = refs[:-1], refs[-1]
+        block = slice(index * cap, (index + 1) * cap)
+        out_ref[:cap, :] = packed[block]
+        out_ref[cap:, :] = jnp.zeros((CODE, out_ref.shape[1]), BF16)
+        out_ref[cap:, :cap] = codes[:, block].astype(BF16)
+
+
+def pack_next_body(cap, dom, meta, place_ref, *refs):
+    raw, outs, pick = refs[: -dom - 1], refs[-dom - 1 : -1], refs[-1]
     one_hot_rows(pick, place_ref[...])
-    packed = mm(pick[...], raw_ref[...], NN).astype(BF16)
+    packed = mm(pick[...], joined(raw), NN).astype(BF16)
     for index, out_ref in enumerate(outs):
         out_ref[...] = packed[index * cap : (index + 1) * cap]
 
 
-def pack_first(meta, raw_images, dest, bins, dom, width, at):
+def raw_specs(hold, share, chunk):
+    first, width = chunk
+    at = lambda k: lambda j, m: (0, m[1] * (share // LANES) + first // LANES + k)
+    return [pl.BlockSpec((hold, LANES), at(k)) for k in range(width // LANES)]
+
+
+def pack_first(meta, raw_images, dest, bins, dom, share, chunk):
     hold, _ = raw_images.shape
+    width = chunk[1]
     cap = hold // dom
     slots = dom * cap
-    row = pl.BlockSpec((1, hold), lambda j, m: (0, 0))
+    specs = raw_specs(hold, share, chunk)
     return call(
         functools.partial(pack_first_body, dom, hold // 2, cap),
         (1,),
-        [
-            pl.BlockSpec((hold,), lambda j, m: (0,)),
-            pl.BlockSpec((hold,), lambda j, m: (0,)),
-            pl.BlockSpec((hold, width), lambda j, m: (0, at(m))),
-        ],
-        [pl.BlockSpec((cap, CODE + width), lambda j, m: (0, 0))] * dom + [row],
-        [sds((cap, CODE + width), BF16)] * dom + [sds((1, hold), I32)],
+        [pl.BlockSpec((hold,), lambda j, m: (0,))] * 2 + specs,
+        [pl.BlockSpec((cap + CODE, width), lambda j, m: (0, 0))] * dom
+        + [pl.BlockSpec((1, hold), lambda j, m: (0, 0))],
+        [sds((cap + CODE, width), BF16)] * dom + [sds((1, hold), I32)],
         scratch=[pltpu.VMEM((slots, hold), BF16)],
-        room=54,
+        room=51,
         flops=2 * slots * hold * width,
         moved=4 * hold * width,
-    )(meta, dest, bins, raw_images)
-
-
-def pack_next(meta, raw_images, place, dom, width, at):
+    )(meta, dest, bins, *[raw_images] * len(specs))
+
+
+def pack_next(meta, raw_images, place, dom, share, chunk):
     hold, _ = raw_images.shape
+    width = chunk[1]
     cap = hold // dom
     slots = dom * cap
+    specs = raw_specs(hold, share, chunk)
     return call(
-        functools.partial(pack_next_body, cap),
+        functools.partial(pack_next_body, cap, dom),
         (1,),
-        [
-            pl.BlockSpec((1, hold), lambda j, m: (0, 0)),
-            pl.BlockSpec((hold, width), lambda j, m: (0, at(m))),
-        ],
+        [pl.BlockSpec((1, hold), lambda j, m: (0, 0))] + specs,
         [pl.BlockSpec((cap, width), lambda j, m: (0, 0))] * dom,
         [sds((cap, width), BF16)] * dom,
         scratch=[pltpu.VMEM((slots, hold), BF16)],
-        room=54,
+        room=51,
         flops=2 * slots * hold * width,
         moved=4 * hold * width,
-    )(meta, place, raw_images)
-
-
-def weigh(pick, wide, recv, ctf_ref, inv_ref, out_ref):
-    table = jnp.concatenate(split3(ctf_ref[...] * inv_ref[...]), axis=0)
-    factor = mm(wide, table, NN)
-    out_ref[...] = (mm(pick, recv, NN) * factor).astype(BF16)
-
-
-def gather(pieces, whole):
-    rows = pieces[0].shape[0]
+    )(meta, place, *[raw_images] * len(specs))
+
+
+def weigh(first, share, pick, wide, recv, meta, ctf_ref, inv_ref, out_ref):
+    width = out_ref.shape[1]
+    start = lax.rem(meta[1] * share, ctf_ref.shape[1]) + first
+    columns = pl.ds(pl.multiple_of(start, LANES), width)
+    table = jnp.concatenate(split3(ctf_ref[:, columns] * inv_ref[:, columns]), axis=0)
+    out_ref[...] = (mm(pick, recv, NN) * mm(wide, table, NN)).astype(BF16)
+
+
+def gather(pieces, whole, rows):
     for index, piece in enumerate(pieces):
-        whole[index * rows : (index + 1) * rows, :] = piece[...]
-
-
-def unpack_first_body(dom, bins, meta, *refs):
-    recv_ref = refs[-1]
-    gather(refs[:dom], recv_ref)
+        whole[index * rows : (index + 1) * rows, :] = piece[:rows, :]
+
+
+def unpack_first_body(dom, bins, share, first, meta, *refs):
+    pieces, recv_ref = refs[:dom], refs[-1]
+    cap = pieces[0].shape[0] - CODE
+    gather(pieces, recv_ref, cap)
     ctf_ref, inv_ref, out_ref, hot_ref, pick, wide = refs[dom:-1]
     shard_rows = out_ref.shape[0]
-    chosen = jnp.where(
-        lax.broadcasted_iota(I32, (8, CODE), 0) == lax.broadcasted_iota(I32, (8, CODE), 1), 1.0, 0.0
-    ).astype(BF16)
-    got = mm(chosen, recv_ref[:, :CODE], NT)
+    got = jnp.concatenate([piece[cap:, :cap].astype(F32) for piece in pieces], axis=1)
     row = got[0:1] * 16.0 + got[1:2] + got[3:4] * 1024.0 - 1024.0
     one_hot_rows(pick, row.astype(I32))
     slot_bins = jnp.broadcast_to(got[2:3].astype(BF16), (8, got.shape[1]))
@@ -180,60 +189,48 @@
     wide[...] = jnp.where((lane & (bins - 1)) == down, 1.0, 0.0).astype(BF16)
     deep = lax.broadcasted_iota(I32, (3 * bins, shard_rows), 0)
     hot_ref[...] = jnp.where((deep & (bins - 1)) == across, 1.0, 0.0).astype(BF16)
-    weigh(pick[...], wide[...], recv_ref[:, CODE:], ctf_ref, inv_ref, out_ref)
-
-
-def unpack_next_body(dom, meta, *refs):
+    weigh(first, share, pick[...], wide[...], recv_ref[...], meta, ctf_ref, inv_ref, out_ref)
+
+
+def unpack_next_body(dom, share, first, meta, *refs):
     recv_ref = refs[-1]
-    gather(refs[:dom], recv_ref)
+    gather(refs[:dom], recv_ref, refs[0].shape[0])
     pick_ref, wide_ref, ctf_ref, inv_ref, out_ref = refs[dom:-1]
-    weigh(pick_ref[...], wide_ref[...], recv_ref[...], ctf_ref, inv_ref, out_ref)
-
-
-def unpack_first(meta, recv, ctf, inv, at):
-    cap, columns = recv[0].shape
+    weigh(first, share, pick_ref[...], wide_ref[...], recv_ref[...], meta, ctf_ref, inv_ref, out_ref)
+
+
+def unpack_first(meta, recv, ctf, inv, share, chunk):
+    first, width = chunk
     dom = len(recv)
-    slots = dom * cap
-    width = columns - CODE
+    slots = dom * (recv[0].shape[0] - CODE)
     rows = slots // 2
     bins, pix = ctf.shape
-    wrap = pix // width
     whole = lambda shape: pl.BlockSpec(shape, lambda j, m: (0, 0))
     shapes = [(rows, width), (3 * bins, rows), (rows, slots), (rows, 3 * bins)]
     return call(
-        functools.partial(unpack_first_body, dom, bins),
+        functools.partial(unpack_first_body, dom, bins, share, first),
+        (1,),
+        [whole(recv[0].shape)] * dom + [whole(ctf.shape), whole(inv.shape)],
+        [whole(s) for s in shapes],
+        [sds(s, BF16) for s in shapes],
+        scratch=[pltpu.VMEM((slots, width), BF16)],
+        room=28,
+        flops=2 * slots * rows * width,
+        moved=2 * slots * width,
+    )(meta, *recv, ctf, inv)
+
+
+def unpack_next(meta, pick, wide, recv, ctf, inv, share, chunk):
+    first, width = chunk
+    dom = len(recv)
+    slots = dom * recv[0].shape[0]
+    rows = slots // 2
+    whole = lambda shape: pl.BlockSpec(shape, lambda j, m: (0, 0))
+    return call(
+        functools.partial(unpack_next_body, dom, share, first),
         (1,),
         [whole(recv[0].shape)] * dom
-        + [
-            pl.BlockSpec((bins, width), lambda j, m: (0, lax.rem(at(m), wrap))),
-            pl.BlockSpec((1, width), lambda j, m: (0, lax.rem(at(m), wrap))),
-        ],
-        [whole(s) for s in shapes],
-        [sds(s, BF16) for s in shapes],
-        scratch=[pltpu.VMEM((slots, columns), BF16)],
-        flops=2 * slots * rows * width,
-        moved=2 * slots * columns,
-    )(meta, *recv, ctf, inv)
-
-
-def unpack_next(meta, pick, wide, recv, ctf, inv, at):
-    cap, width = recv[0].shape
-    dom = len(recv)
-    slots = dom * cap
-    rows = slots // 2
-    bins, pix = ctf.shape
-    wrap = pix // width
-    whole = lambda shape: pl.BlockSpec(shape, lambda j, m: (0, 0))
-    return call(
-        functools.partial(unpack_next_body, dom),
-        (1,),
-        [whole(recv[0].shape)] * dom
-        + [
-            whole(pick.shape),
-            whole(wide.shape),
-            pl.BlockSpec((bins, width), lambda j, m: (0, lax.rem(at(m), wrap))),
-            pl.BlockSpec((1, width), lambda j, m: (0, lax.rem(at(m), wrap))),
-        ],
+        + [whole(pick.shape), whole(wide.shape), whole(ctf.shape), whole(inv.shape)],
         whole((rows, width)),
         sds((rows, width), BF16),
         scratch=[pltpu.VMEM((slots, width), BF16)],
@@ -243,7 +240,12 @@
 
 
 def energy_body(bins, count, meta, *refs):
-    pieces, (ctf_ref, inv_ref, panel_ref, extra_ref, total) = refs[:count], refs[count:]
+    pieces, (ctf_ref, inv_ref, panel_ref, extra_ref, total) = refs[:-5], refs[-5:]
+    width = panel_ref.shape[1]
+    blocks = []
+    for piece in pieces:
+        for start in range(0, piece.shape[1], width):
+            blocks.append((piece, start))
     step = pl.program_id(0)
 
     @pl.when(step == 0)
@@ -252,11 +254,11 @@
 
     gain = ctf_ref[...] * ctf_ref[...] * inv_ref[...]
     gain3 = jnp.concatenate(split3(gain), axis=0)
-    for index, piece in enumerate(pieces):
+    for index, (piece, start) in enumerate(blocks):
 
         @pl.when(step == index)
         def _():
-            panel = piece[...]
+            panel = piece[:, start : start + width]
             panel_ref[...] = panel
             wide = panel.astype(F32)
             square = wide * wide
@@ -271,14 +273,14 @@
 
 
 def energy(meta, pieces, ctf, inv):
-    count = len(pieces)
-    rows, width = pieces[0].shape
+    rows, width = pieces[-1].shape
+    count = sum(piece.shape[1] for piece in pieces) // width
     bins, pix = ctf.shape
     wrap = pix // width
     return call(
         functools.partial(energy_body, bins, count),
         (count,),
-        [pl.BlockSpec((rows, width), lambda j, m: (0, 0))] * count
+        [pl.BlockSpec(piece.shape, lambda j, m: (0, 0)) for piece in pieces]
         + [
             pl.BlockSpec((bins, width), lambda j, m: (0, lax.rem(m[0] ^ j, wrap))),
             pl.BlockSpec((1, width), lambda j, m: (0, lax.rem(m[0] ^ j, wrap))),
@@ -294,20 +296,31 @@
     )(meta, *pieces, ctf, inv)
 
 
-def score_body(parts, first, last, meta, *refs):
-    own, sib, panel_ref, refs = refs[:parts], refs[parts : 2 * parts], refs[2 * parts], refs[2 * parts + 1 :]
+def score_body(parts, used, first, last, meta, *refs):
+    own, sib, panel_ref, refs = (
+        refs[:parts],
+        refs[parts : 2 * parts],
+        refs[2 * parts],
+        refs[2 * parts + 1 :],
+    )
     if first:
         acc_out, full_ref = refs
     elif last:
         acc_ref, _, hot_own, hot_sib, extra_ref, shifted_ref, stat_ref, full_ref = refs
+    elif used is None:
+        acc_ref, _, acc_out, full_ref = refs
     else:
-        acc_ref, _, acc_out, full_ref = refs
+        acc_ref, acc_out = refs
     half = pl.num_programs(0) // 2
 
     def tile(sources, hot):
         block = jnp.concatenate([source[...] for source in sources], axis=1)
-        full_ref[...] = block
-        total = mm(panel_ref[...], block, NT)
+        if used is None or last:
+            full_ref[...] = block
+        if last:
+            block = block[:, used[0] : used[0] + used[1]]
+        panel = panel_ref[...] if used is None else panel_ref[:, used[0] : used[0] + used[1]]
+        total = mm(panel, block, NT)
         if not first:
             total = acc_ref[...] + total
         if not last:
@@ -330,29 +343,32 @@
         tile(sib, hot_sib if last else None)
 
 
-def score(meta, at, own, sib, panels, acc=None, full=None, hots=None, extra=None):
-    rows, part = own[0].shape
+def score(meta, at, own, sib, panels, width, acc=None, full=None, hots=None, extra=None, used=None):
+    rows = own[0].shape[0]
     parts = len(own)
-    width = parts * part
     tile = 256
     half = rows // tile
     count, columns = panels.shape
     first, last = acc is None, hots is not None
-    front = pl.BlockSpec((tile, part), lambda j, m: (jnp.minimum(j, half - 1), 0))
-    back = pl.BlockSpec((tile, part), lambda j, m: (jnp.maximum(j - half, 0), 0))
+    store = used is None or last
+    fronts = [pl.BlockSpec((tile, v.shape[1]), lambda j, m: (jnp.minimum(j, half - 1), 0)) for v in own]
+    backs = [pl.BlockSpec((tile, v.shape[1]), lambda j, m: (jnp.maximum(j - half, 0), 0)) for v in own]
     acc_spec = pl.BlockSpec((count, tile), lambda j, m: (0, j))
     full_spec = pl.BlockSpec((tile, width), lambda j, m: (j, at(m)))
-    in_specs = [front] * parts + [back] * parts
-    in_specs += [pl.BlockSpec((count, width), lambda j, m: (0, at(m)))]
+    in_specs = fronts + backs + [pl.BlockSpec((count, width), lambda j, m: (0, at(m)))]
     operands = [meta, *own, *sib, panels]
     alias = {}
     if not first:
-        in_specs += [acc_spec, pl.BlockSpec(memory_space=pl.ANY)]
-        alias = {len(operands): 0, len(operands) + 1: 2 if last else 1}
-        operands += [acc, full]
-    out_specs = [acc_spec, full_spec]
+        in_specs += [acc_spec]
+        alias = {len(operands): 0}
+        operands += [acc]
+        if store:
+            in_specs += [pl.BlockSpec(memory_space=pl.ANY)]
+            alias[len(operands)] = 2 if last else 1
+            operands += [full]
     full_shape = sds((2 * rows, columns), BF16)
-    out_shape = [sds((count, 2 * rows), F32), full_shape]
+    acc_shape = sds((count, 2 * rows), F32)
+    out_specs, out_shape = [acc_spec, full_spec], [acc_shape, full_shape]
     if last:
         depth = extra.shape[1]
         in_specs += [
@@ -362,9 +378,11 @@
         ]
         operands += [*hots, extra]
         out_specs = [acc_spec, pl.BlockSpec((8, tile), lambda j, m: (0, j)), full_spec]
-        out_shape = [out_shape[0], sds((8, 2 * rows), F32), full_shape]
+        out_shape = [acc_shape, sds((8, 2 * rows), F32), full_shape]
+    elif not store:
+        out_specs, out_shape = acc_spec, acc_shape
     return call(
-        functools.partial(score_body, parts, first, last),
+        functools.partial(score_body, parts, used, first, last),
         (2 * half,),
         in_specs,
         out_specs,
@@ -376,10 +394,11 @@
     )(*operands)
 
 
-def merge_body(meta, mine_ref, other_ref, out_ref):
+def merge_body(turned, meta, mine_ref, other_ref, out_ref):
     rows = mine_ref.shape[1] // 2
     other = other_ref[...]
-    other = jnp.concatenate([other[:, rows:], other[:, :rows]], axis=1)
+    if turned:
+        other = jnp.concatenate([other[:, rows:], other[:, :rows]], axis=1)
     mine = mine_ref[...]
     peak = jnp.maximum(mine[0:1], other[0:1])
     mass = mine[1:2] * jnp.exp(mine[0:1] - peak) + other[1:2] * jnp.exp(other[0:1] - peak)
@@ -387,24 +406,19 @@
     out_ref[...] = jnp.where(which == 0, peak, mass)
 
 
-def merge(meta, mine, other):
+def merge(meta, mine, other, turned=False):
     spec = pl.BlockSpec(mine.shape, lambda j, m: (0, 0))
-    return call(merge_body, (1,), [spec, spec], spec, sds(mine.shape, F32), room=4)(meta, mine, other)
+    return call(functools.partial(merge_body, turned), (1,), [spec, spec], spec, sds(mine.shape, F32), room=4)(meta, mine, other)
 
 
 def class_body(kind, steps, meta, *refs):
     if kind == "first":
-        (shifted_ref, stat_ref), four = refs[:2], refs[2:6]
-        hot_own, hot_sib, full_ref = refs[6:9]
-        outs, (post_ref, log_ref, mass_ref) = refs[9 : 9 + steps], refs[9 + steps :]
+        shifted_ref, stat_ref, all_ref, hot_own, hot_sib, full_ref = refs[:6]
+        outs, (post_ref, log_ref, mass_ref) = refs[6 : 6 + steps], refs[6 + steps :]
 
         @pl.when(pl.program_id(0) == 0)
         def _():
-            stats = [ref[...] for ref in four]
-            peaks = [s[0:1] for s in stats]
-            peak = jnp.maximum(jnp.maximum(peaks[0], peaks[1]), jnp.maximum(peaks[2], peaks[3]))
-            parts = [s[1:2] * jnp.exp(p - peak) for s, p in zip(stats, peaks)]
-            mass = (parts[0] + parts[1]) + (parts[2] + parts[3])
+            peak, mass = all_ref[0:1], all_ref[1:2]
             factor = jnp.exp(stat_ref[0:1] - peak) / mass
             post_ref[...] = (shifted_ref[...] * factor).astype(BF16)
             log_ref[...] = (peak + jnp.log(mass))[:, : log_ref.shape[1]]
@@ -432,7 +446,7 @@
     out_shape = [sds((count, width), F32 if kind == "rest" else BF16)] * steps
     if kind == "first":
         operands = [shifted, *stats, *hots, full]
-        in_specs = [whole(shifted.shape)] + [whole(stats[0].shape)] * 5
+        in_specs = [whole(shifted.shape)] + [whole(stats[0].shape)] * 2
         in_specs += [whole(hots[0].shape)] * 2 + [full_spec]
         out_specs += [whole((count, rows)), whole((1, rows // 2)), whole((bins, count))]
         out_shape += [sds((count, rows), BF16), sds((1, rows // 2), F32), sds((bins, count), BF16)]
@@ -541,41 +555,42 @@
     def onward(value):
         return lax.ppermute(value, "rot", [(i, (i + 1) % turns) for i in range(turns)])
 
-    width = columns // turns // 2
+    width = columns // turns
+    cut = width * 5 // 8
+    chunk_a, chunk_b = (0, cut), (cut, width - cut)
+
     def exchange(blocks):
         got = [blocks[0]] + [None] * (dom - 1)
         for apart in (6, 7, 2, 4, 3, 5, 1):
             got[apart] = across(blocks[apart], apart)
         return got
 
-    *send_a, place = pack_first(meta, raw_images, dest_row, defocus_bin, dom, width, lambda m: 2 * m[1])
+    *send_a, place = pack_first(meta, raw_images, dest_row, defocus_bin, dom, width, chunk_a)
     recv_a = exchange(send_a)
-    send_b = pack_next(meta, raw_images, place, dom, width, lambda m: 2 * m[1] + 1)
+    send_b = pack_next(meta, raw_images, place, dom, width, chunk_b)
     together = lax.optimization_barrier
 
     count = panels.shape[0] // 2
-    pieces = [None] * 8
     place, panels = together((place, panels))
-    pieces[0] = lax.dynamic_slice_in_dim(panels, core * count, count, 0)
-    pieces[1] = across(lax.dynamic_slice_in_dim(panels, (1 - core) * count, count, 0), 1)
-
-    recv_a, send_b, pieces[:2] = together((recv_a, send_b, pieces[:2]))
-    share_a, hot, pick, wide = unpack_first(meta, recv_a, ctf_table, inv, lambda m: 2 * m[1])
+    mine = lax.dynamic_slice_in_dim(panels, core * count, count, 0)
+    other = across(lax.dynamic_slice_in_dim(panels, (1 - core) * count, count, 0), 1)
+    near = jnp.concatenate([mine, other], axis=1)
+
+    recv_a, send_b, near = together((recv_a, send_b, near))
+    share_a, hot, pick, wide = unpack_first(meta, recv_a, ctf_table, inv, width, chunk_a)
     share_a, send_b = together((share_a, send_b))
     a1, recv_b = onward(share_a), exchange(send_b)
-    a2 = onward(a1)
-    recv_b, pieces[:2] = together((recv_b, pieces[:2]))
-    pieces[2], pieces[4] = across(pieces[0], 2), across(pieces[0], 4)
-    pieces[3], pieces[5] = across(pieces[1], 2), across(pieces[1], 4)
-    a2, recv_b = together((a2, recv_b))
-    share_b = unpack_next(meta, pick, wide, recv_b, ctf_table, inv, lambda m: 2 * m[1] + 1)
+    a1, recv_b, near = together((a1, recv_b, near))
+    by_x, by_y = across(near, 2), across(near, 4)
+    share_b = unpack_next(meta, pick, wide, recv_b, ctf_table, inv, width, chunk_b)
     hots = (hot, across(hot, 1))
-    a3, b1 = onward(a2), onward(share_b)
-    a3, b1, pieces[2:6] = together((a3, b1, pieces[2:6]))
-    pieces[6], pieces[7] = across(pieces[2], 4), across(pieces[5], 2)
-    b2 = onward(b1)
-    panel_full, extra = energy(meta, pieces, ctf_table, inv)
-    b2, panel_full, extra, hots = together((b2, panel_full, extra, hots))
+    a2, b1 = onward(a1), onward(share_b)
+    a2, b1, by_x, by_y = together((a2, b1, by_x, by_y))
+    piece = near.shape[1] // 2
+    far_y, far_x = across(by_x[:, :piece], 4), across(by_y[:, piece:], 2)
+    a3, b2 = onward(a2), onward(b1)
+    panel_full, extra = energy(meta, [near, by_x, by_y, far_y, far_x], ctf_table, inv)
+    a3, b2, panel_full, extra, hots = together((a3, b2, panel_full, extra, hots))
     b3 = onward(b2)
 
     def share(turn):
@@ -584,19 +599,31 @@
     acc = full = None
     for turn, own in enumerate([(share_a, share_b), (a1, b1), (a2, b2)]):
         sib = [across(value, 1) for value in own]
-        acc, full = score(meta, share(turn), own, sib, panel_full, acc, full)
-    a3_sib, b3, acc = together((across(a3, 1), b3, acc))
-    sib = [a3_sib, across(b3, 1)]
+        acc, full = score(meta, share(turn), own, sib, panel_full, width, acc, full)
+    final = share(turns - 1)
+    a3_sib = across(a3, 1)
+    acc = score(meta, final, [a3], [a3_sib], panel_full, width, acc, used=chunk_a)
+    b3, acc = together((b3, acc))
     shifted, stat, full = score(
-        meta, share(turns - 1), [a3, b3], sib, panel_full, acc, full, hots, extra
-    )
-
-    pair = merge(meta, stat, across(stat, 1))
-    others = [
-        lax.ppermute(pair, "rot", [(i, i ^ apart) for i in range(turns)]) for apart in (1, 2, 3)
-    ]
+        meta,
+        final,
+        [a3, b3],
+        [a3_sib, across(b3, 1)],
+        panel_full,
+        width,
+        acc,
+        full,
+        hots,
+        extra,
+        chunk_b,
+    )
+
+    total = merge(meta, stat, across(stat, 1), turned=True)
+    for apart in (1, 2):
+        pairs = [(i, i ^ apart) for i in range(turns)]
+        total = merge(meta, total, lax.ppermute(total, "rot", pairs))
     to_x, to_y, post, log_evidence, mass = class_part(
-        meta, "first", 2, 2, full, None, shifted, [stat, pair, *others], hots, bins
+        meta, "first", 2, 2, full, None, shifted, [stat, total], hots, bins
     )
     mass_x = across(mass, 2)
     got_x, got_y = across(to_x, 2), across(to_y, 4)

time: 271 us -> 257 us (0.948)
  waiting for transfers between devices: 153 us -> 138 us
  starting transfers between devices: 42.9 us -> 36.6 us
  Pallas kernels: 70.9 us -> 75.7 us
    ppermute x37 -> x35, waiting for transfers between devices: 87 us -> 36.1 us  [across(): return lax.ppermute(value, 'dom', [(i, i ^ apart) for i in range(dom)])]
    ppermute x6, waiting for transfers between devices: 33.1 us -> 65.4 us  [onward(): lax.ppermute(value, 'rot', [(i, (i + 1) % turns) for i in range(turns)])]
    ppermute x37 -> x35, starting transfers between devices: 32.4 us -> 26.7 us  [across(): return lax.ppermute(value, 'dom', [(i, i ^ apart) for i in range(dom)])]
    pallas_call x8 -> x11, Pallas kernels: 34.7 us -> 39 us  [the longest x5 26.3 us: score(): call(functools.partial(score_body, parts, used, first, last), (2 * half,)...]
    ppermute x3 -> x2, waiting for transfers between devices: 3.03 us -> 6.71 us  [two_by_two(): total = merge(meta, total, lax.ppermute(total, 'rot', pairs))]
  transfers between devices with their start and end apart: 50 -> 47, of which waited for: 24 -> 18; matrix products, arithmetic and copies ran while one was open for 1% -> 1% of each run, Pallas kernels for 16% -> 18%
where the time goes in v6:
time: 257 us; the launch traced here: 256 us
  waiting for transfers between devices  138 us (54%)
  Pallas kernels  75.7 us (29%)
  starting transfers between devices  36.6 us (14%)
  local copies, waits for them, and re-layouts  3.06 us (1%)
    ppermute x6, waiting for transfers between devices, onward(): lax.ppermute(value, 'rot', [(i, (i + 1) % turns) for i in range(turns)])  65.4 us
    ppermute x35, waiting for transfers between devices, across(): return lax.ppermute(value, 'dom', [(i, i ^ apart) for i in range(dom)])  36.1 us
    ppermute x4, waiting for transfers between devices, by_core(): return lax.ppermute(value, 'dom', pairs)  29.9 us
    ppermute x35, starting transfers between devices, across(): return lax.ppermute(value, 'dom', [(i, i ^ apart) for i in range(dom)])  26.7 us
    pallas_call x5, Pallas kernels, score(): call(functools.partial(score_body, parts, used, first, last), (2 * half,)...  26.3 us
    pallas_call x3, Pallas kernels, class_part(): call(functools.partial(class_body, kind, steps), (steps,), in_specs, out_...  15.7 us
    pallas_call x1, Pallas kernels, pack_first(): call(functools.partial(pack_first_body, dom, hold // 2, cap), (1,), [pl.B...  7.28 us
    pallas_call x1, Pallas kernels, energy(): call(functools.partial(energy_body, bins, count), (count,), [pl.BlockSpec...  6.79 us
  transfers between devices with their start and end apart: 47, of which 18 were waited for; matrix products, arithmetic and copies ran while one was open for 1% of the time, Pallas kernels for 18%

profile of v6, /device:TPU:0, one launch (start us, length us, event | category | flops | bytes accessed | tf_op | source)
XLA Modules:
  0.0 256.3 jit_solution(3880596812006201214)
XLA Ops:
  0.8 0.7 copy-done.2
  1.5 0.7 copy-done.3
  2.2 7.3 %shard_map.85 = (bf16[208,640]{1,0:T(8,128)(2,1)S(1)}, bf16[208,640]{1,0:T(8,128)(2,1)S(1)}, bf16[208,640]{1,0:T(8,128)(2,1)S(1)}, bf16[208,640]{1,0:T(8,128)(2,...) custom-call(s32[10]{0:T(128)S(1)} %stack.43.meta, ...), custom_call_target="tpu_custom_call" | custom-call | flops 188743680 | bytes 245760 | tf_op jit(solution)/shard_map/pallas_call | solution.py:130
  9.5 1.4 constant_dynamic-slice_fusion.1
  10.9 0.5 collective-permute-start.7
  11.5 2.9 %collective-permute-start.1 = (bf16[208,640]{1,0:T(8,128)(2,1)S(1)}, bf16[208,640]{1,0:T(8,128)(2,1)S(1)}, u32[]{:S(2)}, u32[]{:S(2)}) collective-permute-start(bf16[208,640]{1,0:T(8,128)(2,1)S(1)} %get-tuple-element.108), channel_id=1, source_target_pairs={{0,8},{4,12},{8,0},{12,4},{16,24},{20,28},{24,16},{28,20},{1,9},{5... | collective-permute-start | bytes 798728 | tf_op jit(solution)/shard_map/ppermute | solution.py:549
  14.4 1.5 collective-permute-start.3
  16.3 5.3 %collective-permute-done.1.refs_2_ = bf16[208,640]{1,0:T(8,128)(2,1)S(1)} collective-permute-done((bf16[208,640]{1,0:T(8,128)(2,1)S(1)}, bf16[208,640]{1,0:T(8,128)(2,1)S(1)}, u32[]{:S(2)}, u32[]{:S(2)}) %collective-permute-start.1) | collective-permute-done | bytes 266272 | tf_op jit(solution)/shard_map/ppermute | solution.py:549
  21.6 3.0 %collective-permute-start.5 = (bf16[208,640]{1,0:T(8,128)(2,1)S(1)}, bf16[208,640]{1,0:T(8,128)(2,1)S(1)}, u32[]{:S(2)}, u32[]{:S(2)}) collective-permute-start(bf16[208,640]{1,0:T(8,128)(2,1)S(1)} %get-tuple-element.112), channel_id=1, source_target_pairs={{0,24},{4,28},{8,16},{12,20},{16,8},{20,12},{24,0},{28,4},{1,25},{... | collective-permute-start | bytes 798728 | tf_op jit(solution)/shard_map/ppermute | solution.py:549
  24.6 4.4 %shard_map.86 = (bf16[192,384]{1,0:T(8,128)(2,1)S(1)}, bf16[192,384]{1,0:T(8,128)(2,1)S(1)}, bf16[192,384]{1,0:T(8,128)(2,1)S(1)}, bf16[192,384]{1,0:T(8,128)(2,...) custom-call(s32[10]{0:T(128)S(1)} %stack.43.meta, ...), custom_call_target="tpu_custom_call" | custom-call | flops 113246208 | bytes 147456 | tf_op jit(solution)/shard_map/pallas_call | solution.py:150
  29.3 10.5 %collective-permute-done.4.refs_5_ = bf16[208,640]{1,0:T(8,128)(2,1)S(1)} collective-permute-done((bf16[208,640]{1,0:T(8,128)(2,1)S(1)}, bf16[208,640]{1,0:T(8,128)(2,1)S(1)}, u32[]{:S(2)}, u32[]{:S(2)}) %collective-permute-start.4) | collective-permute-done | bytes 266272 | tf_op jit(solution)/shard_map/ppermute | solution.py:549
  39.8 4.4 %shard_map.87 = (bf16[768,640]{1,0:T(8,128)(2,1)S(1)}, bf16[192,768]{1,0:T(8,128)(2,1)S(1)}, bf16[768,1536]{1,0:T(8,128)(2,1)S(1)}, bf16[768,192]{1,0:T(8,128)(2,1)S(1)}) custom-call(s32[10]{0:T(128)S(1)} %stack.43.meta, bf16[208,640]{1,0:T(8,128)(2,1)S(1)} %get-tuple-element.124.refs_0_, bf16[208,640]{1,0:T(8,128)(2,1)S(1)} %collective-permute-done.refs_1_, ...), custom_call_target="tpu_custom_call" | custom-call | flops 94371840 | bytes 122880 | tf_op jit(solution)/shard_map/pallas_call | solution.py:210
  44.2 2.2 collective-permute-start.8
  46.4 1.6 collective-permute-start.10
  47.9 1.5 collective-permute-start.12
  49.9 3.2 %collective-permute-done.10.refs_2_ = bf16[192,384]{1,0:T(8,128)(2,1)S(1)} collective-permute-done((bf16[192,384]{1,0:T(8,128)(2,1)S(1)}, bf16[192,384]{1,0:T(8,128)(2,1)S(1)}, u32[]{:S(2)}, u32[]{:S(2)}) %collective-permute-start.10) | collective-permute-done | bytes 147488 | tf_op jit(solution)/shard_map/ppermute | solution.py:549
  53.1 2.6 collective-permute-start.14
  55.6 2.9 %collective-permute-start.15 = (bf16[192,384]{1,0:T(8,128)(2,1)S(1)}, bf16[192,384]{1,0:T(8,128)(2,1)S(1)}, u32[]{:S(2)}, u32[]{:S(2)}) collective-permute-start(bf16[192,384]{1,0:T(8,128)(2,1)S(1)} %get-tuple-element.149), channel_id=1, source_target_pairs={{0,28},{4,24},{8,20},{12,16},{16,12},{20,8},{24,4},{28,0},{1,29},{... | collective-permute-start | bytes 442376 | tf_op jit(solution)/shard_map/ppermute | solution.py:549
  58.5 4.9 %collective-permute-done.13.refs_5_ = bf16[192,384]{1,0:T(8,128)(2,1)S(1)} collective-permute-done((bf16[192,384]{1,0:T(8,128)(2,1)S(1)}, bf16[192,384]{1,0:T(8,128)(2,1)S(1)}, u32[]{:S(2)}, u32[]{:S(2)}) %collective-permute-start.13) | collective-permute-done | bytes 147488 | tf_op jit(solution)/shard_map/ppermute | solution.py:549
  63.5 7.0 %collective-permute-done.8.refs_0_ = bf16[768,640]{1,0:T(8,128)(2,1)S(1)} collective-permute-done((bf16[768,640]{1,0:T(8,128)(2,1)S(1)}, bf16[768,640]{1,0:T(8,128)(2,1)S(1)}, u32[]{:S(2)}, u32[]{:S(2)}) %collective-permute-start.8) | collective-permute-done | bytes 983072 | tf_op jit(solution)/shard_map/ppermute | solution.py:556
  70.5 1.5 collective-permute-start.18
  72.0 1.5 collective-permute-start.19
  73.5 2.2 shard_map.88.refs_1_
  75.7 1.3 collective-permute-start.17
  77.1 33.3 %collective-permute-done.17.refs_1_ = bf16[768,384]{1,0:T(8,128)(2,1)S(1)} collective-permute-done((bf16[768,384]{1,0:T(8,128)(2,1)S(1)}, bf16[768,384]{1,0:T(8,128)(2,1)S(1)}, u32[]{:S(2)}, u32[]{:S(2)}) %collective-permute-start.17) | collective-permute-done | bytes 589856 | tf_op jit(solution)/shard_map/ppermute | solution.py:556
  110.6 0.6 collective-permute-start.22
  111.3 0.8 collective-permute-start.23
  112.1 0.7 collective-permute-done.24.refs_8_.refs_4_
  112.9 15.6 %collective-permute-done.21.refs_1_ = bf16[768,384]{1,0:T(8,128)(2,1)S(1)} collective-permute-done((bf16[768,384]{1,0:T(8,128)(2,1)S(1)}, bf16[768,384]{1,0:T(8,128)(2,1)S(1)}, u32[]{:S(2)}, u32[]{:S(2)}) %collective-permute-start.21) | collective-permute-done | bytes 589856 | tf_op jit(solution)/shard_map/ppermute | solution.py:556
  128.5 0.5 collective-permute-start.32
  129.1 1.2 collective-permute-done.23.refs_4_
  130.2 6.8 %shard_map.89 = (bf16[720,4096]{1,0:T(8,128)(2,1)S(1)}, bf16[720,192]{1,0:T(8,128)(2,1)S(1)}) custom-call(s32[10]{0:T(128)S(1)} %stack.43.meta, bf16[720,1024]{1,0:T(8,128)(2,1)S(1)} %pad_maximum_fusion.refs_0_, bf16[720,1024]{1,0:T(8,128)(2,1)S(1)} %collective-permute-done.18.refs_1_, bf16[720,1024]{1,0:T(8,128)(2,1)S(1)} %collective-permute-done.19.refs_2_, ...), custom_call_target="tpu_custom_call" | custom-call | flops 283115520 | bytes 737280 | tf_op jit(solution)/shard_map/pallas_call | solution.py:280
  137.0 9.4 %collective-permute-done.20.refs_0_ = bf16[768,640]{1,0:T(8,128)(2,1)S(1)} collective-permute-done((bf16[768,640]{1,0:T(8,128)(2,1)S(1)}, bf16[768,640]{1,0:T(8,128)(2,1)S(1)}, u32[]{:S(2)}, u32[]{:S(2)}) %collective-permute-start.20) | collective-permute-done | bytes 983072 | tf_op jit(solution)/shard_map/ppermute | solution.py:556
  146.5 0.5 collective-permute-start.30
  147.3 5.1 %shard_map.90 = (f32[720,1536]{1,0:T(8,128)S(1)}, bf16[1536,4096]{1,0:T(8,128)(2,1)S(1)}) custom-call(s32[10]{0:T(128)S(1)} %stack.43.meta, bf16[768,640]{1,0:T(8,128)(2,1)S(1)} %get-tuple-element.141.refs_0_, bf16[768,384]{1,0:T(8,128)(2,1)S(1)} %shard_map.88.refs_1_, bf16[768,640]{1,0:T(8,128)(2,1)S(1)} %collective-permute-done.31.refs_2_, ...), custom_call_target="tpu_custom_call" | custom-call | flops 141557760 | bytes 946176 | tf_op jit(solution)/shard_map/pallas_call | solution.py:384
  152.4 5.5 %shard_map.91 = (f32[720,1536]{1,0:T(8,128)S(1)}, bf16[1536,4096]{1,0:T(8,128)(2,1)S(1)}) custom-call(s32[10]{0:T(128)S(1)} %stack.43.meta, bf16[768,640]{1,0:T(8,128)(2,1)S(1)} %collective-permute-done.8.refs_0_, bf16[768,384]{1,0:T(8,128)(2,1)S(1)} %collective-permute-done.17.refs_1_, ...), custom_call_target="tpu_custom_call", output_to_operand_aliasing={{0}: (6, {}), {1}: (7, {})} | custom-call | flops 141557760 | bytes 946176 | tf_op jit(solution)/shard_map/pallas_call | solution.py:384
  157.9 5.4 %shard_map.92 = (f32[720,1536]{1,0:T(8,128)S(1)}, bf16[1536,4096]{1,0:T(8,128)(2,1)S(1)}) custom-call(s32[10]{0:T(128)S(1)} %stack.43.meta, bf16[768,640]{1,0:T(8,128)(2,1)S(1)} %collective-permute-done.16.refs_0_, bf16[768,384]{1,0:T(8,128)(2,1)S(1)} %collective-permute-done.21.refs_1_, ...), custom_call_target="tpu_custom_call", output_to_operand_aliasing={{0}: (6, {}), {1}: (7, {})} | custom-call | flops 141557760 | bytes 946176 | tf_op jit(solution)/shard_map/pallas_call | solution.py:384
  163.3 4.4 %shard_map.93.refs_5_ = f32[720,1536]{1,0:T(8,128)S(1)} custom-call(s32[10]{0:T(128)S(1)} %stack.43.meta, bf16[768,640]{1,0:T(8,128)(2,1)S(1)} %collective-permute-done.20.refs_0_, bf16[768,640]{1,0:T(8,128)(2,1)S(1)} %collective-permute-done.26.refs_1_.refs_2_, ...), custom_call_target="tpu_custom_call", output_to_operand_aliasing={{}: (4, {})} | custom-call | flops 141557760 | bytes 946176 | tf_op jit(solution)/shard_map/pallas_call | solution.py:384
  168.0 1.8 collective-permute-done.33.refs_3_
  169.8 5.9 %shard_map.94 = (f32[720,1536]{1,0:T(8,128)S(1)}, f32[8,1536]{1,0:T(8,128)S(1)}, bf16[1536,4096]{1,0:T(8,128)(2,1)S(1)}) custom-call(s32[10]{0:T(128)S(1)} %stack.43.meta, bf16[768,640]{1,0:T(8,128)(2,1)S(1)} %collective-permute-done.20.refs_0_, bf16[768,384]{1,0:T(8,128)(2,1)S(1)} %collective-permute-done.25.refs_1_, ...), custom_call_target="tpu_custom_call", output_to_operand_aliasing={{0}: (6, {}), {2}: (7, {})} | custom-call | flops 141557760 | bytes 946176 | tf_op jit(solution)/shard_map/pallas_call | solution.py:384
  176.0 1.0 collective-permute-done.34.other_ref
  177.1 0.6 shard_map.95.mine_ref
  177.7 4.1 %collective-permute-done.35.other_ref = f32[8,1536]{1,0:T(8,128)S(1)} collective-permute-done((f32[8,1536]{1,0:T(8,128)S(1)}, f32[8,1536]{1,0:T(8,128)S(1)}, u32[]{:S(2)}, u32[]{:S(2)}) %collective-permute-start.35) | collective-permute-done | bytes 49184 | tf_op jit(solution)/shard_map/ppermute | solution.py:624
  181.8 0.6 shard_map.96.mine_ref
  182.4 2.4 collective-permute-start.36
  184.8 2.6 %collective-permute-done.36.other_ref = f32[8,1536]{1,0:T(8,128)S(1)} collective-permute-done((f32[8,1536]{1,0:T(8,128)S(1)}, f32[8,1536]{1,0:T(8,128)S(1)}, u32[]{:S(2)}, u32[]{:S(2)}) %collective-permute-start.36) | collective-permute-done | bytes 49184 | tf_op jit(solution)/shard_map/ppermute | solution.py:624
  187.4 0.6 shard_map.97.refs_2_
  188.0 4.2 %shard_map.98 = (bf16[720,512]{1,0:T(8,128)(2,1)S(1)}, bf16[720,512]{1,0:T(8,128)(2,1)S(1)}, bf16[720,1536]{1,0:T(8,128)(2,1)S(1)}, f32[1,768]{1,0:T(1,128)S(1)}, bf16[64,720]{1,0:T(8,128)(2,1)S(1)}) custom-call(s32[10]{0:T(128)S(1)} %stack.43.meta, f32[720,1536]{1,0:T(8,128)S(1)} %get-tuple-element.184.refs_0_, ...), custom_call_target="tpu_custom_call" | custom-call | flops 141557760 | bytes 657408 | tf_op jit(solution)/shard_map/pallas_call | solution.py:456
  192.2 0.6 collective-permute-start.39
  192.8 1.5 collective-permute-start.37
  194.8 3.2 %collective-permute-done.39 = bf16[64,720]{1,0:T(8,128)(2,1)S(1)} collective-permute-done((bf16[64,720]{1,0:T(8,128)(2,1)S(1)}, bf16[64,720]{1,0:T(8,128)(2,1)S(1)}, u32[]{:S(2)}, u32[]{:S(2)}) %collective-permute-start.39) | collective-permute-done | bytes 92192 | tf_op jit(solution)/shard_map/ppermute | solution.py:549
  198.0 0.5 collective-permute-start.40
  198.6 4.9 %shard_map.100 = (f32[720,512]{1,0:T(8,128)S(1)}, f32[720,512]{1,0:T(8,128)S(1)}, f32[720,512]{1,0:T(8,128)S(1)}) custom-call(s32[10]{0:T(128)S(1)} %stack.43.meta, bf16[720,1536]{1,0:T(8,128)(2,1)S(1)} %get-tuple-element.189.refs_0_, bf16[1536,4096]{1,0:T(8,128)(2,1)S(1)} %get-tuple-element.186.refs_5_.refs_1_), custom_call_target="tpu_custom_call" | custom-call | flops 212336640 | bytes 847872 | tf_op jit(solution)/shard_map/pallas_call | solution.py:456
  203.5 6.5 %shard_map.99 = (bf16[720,512]{1,0:T(8,128)(2,1)}, bf16[720,512]{1,0:T(8,128)(2,1)}, bf16[720,512]{1,0:T(8,128)(2,1)}) custom-call(s32[10]{0:T(128)S(1)} %stack.43.meta, bf16[720,1536]{1,0:T(8,128)(2,1)S(1)} %get-tuple-element.189.refs_0_, bf16[1536,4096]{1,0:T(8,128)(2,1)S(1)} %get-tuple-element.186.refs_5_.refs_1_), custom_call_target="tpu_custom_call" | custom-call | flops 212336640 | bytes 847872 | tf_op jit(solution)/shard_map/pallas_call | solution.py:456
  210.0 4.2 %collective-permute-done.40 = f32[64,720]{1,0:T(8,128)S(1)} collective-permute-done((f32[64,720]{1,0:T(8,128)S(1)}, f32[64,720]{1,0:T(8,128)S(1)}, u32[]{:S(2)}, u32[]{:S(2)}) %collective-permute-start.40) | collective-permute-done | bytes 184352 | tf_op jit(solution)/shard_map/ppermute | solution.py:549
  214.4 2.0 shard_map.101
  216.8 1.4 collective-permute-start.44
  218.2 0.5 collective-permute-start.42
  218.7 1.1 collective-permute-start.45
  219.9 0.6 reduce
  220.5 0.9 maximum_select_fusion
  221.4 14.5 %collective-permute-done.41.a_ref = bf16[720,512]{1,0:T(8,128)(2,1)S(1)} collective-permute-done((bf16[720,512]{1,0:T(8,128)(2,1)}, bf16[720,512]{1,0:T(8,128)(2,1)S(1)}, u32[]{:S(2)}, u32[]{:S(2)}) %collective-permute-start.41) | collective-permute-done | bytes 737312 | tf_op jit(solution)/shard_map/ppermute | solution.py:553
  235.9 15.4 %collective-permute-done.42.c_ref = bf16[720,512]{1,0:T(8,128)(2,1)} collective-permute-done((bf16[720,512]{1,0:T(8,128)(2,1)}, bf16[720,512]{1,0:T(8,128)(2,1)}, u32[]{:S(2)}, u32[]{:S(2)}) %collective-permute-start.42) | collective-permute-done | bytes 737312 | tf_op jit(solution)/shard_map/ppermute | solution.py:553
  251.4 5.0 %shard_map.102 = f32[1440,512]{1,0:T(8,128)} custom-call(s32[10]{0:T(128)S(1)} %stack.43.meta, f32[720,512]{1,0:T(8,128)S(1)} %get-tuple-element.197.keep_ref, bf16[720,512]{1,0:T(8,128)(2,1)S(1)} %collective-permute-done.41.a_ref, bf16[720,512]{1,0:T(8,128)(2,1)} %collective-permute-done.42.c_ref, bf16[720,512]{1,0:T(8,128)(2,1)} %collective-permute-done.43.other_ref, ...), custom_call_target="tpu_custom_call" | custom-call | tf_op jit(solution)/shard_map/pallas_call | solution.py:510
  (65 shorter events, 3.6 us)
Async XLA Ops:
  0.8 0.7 copy-start.2
  1.5 0.7 copy-start.3
  10.9 13.7 %collective-permute-start.7 = (bf16[720,512]{1,0:T(8,128)(2,1)S(1)}, bf16[720,512]{1,0:T(8,128)(2,1)S(1)}, u32[]{:S(2)}, u32[]{:S(2)}) collective-permute-start(bf16[720,512]{1,0:T(8,128)(2,1)S(1)} %get-tuple-element.210), channel_id=1, source_target_pairs={{0,4},{4,0},{8,12},{12,8},{16,20},{20,16},{24,28},{28,24},{1,5},{5... | collective-permute-start | bytes 2211848 | tf_op jit(solution)/shard_map/ppermute | solution.py:549
  11.4 4.5 %collective-permute-start = (bf16[208,640]{1,0:T(8,128)(2,1)S(1)}, bf16[208,640]{1,0:T(8,128)(2,1)S(1)}, u32[]{:S(2)}, u32[]{:S(2)}) collective-permute-start(bf16[208,640]{1,0:T(8,128)(2,1)S(1)} %get-tuple-element.107), channel_id=1, source_target_pairs={{0,4},{4,0},{8,12},{12,8},{16,20},{20,16},{24,28},{28,24},{1,5},{5... | collective-permute-start | bytes 798728 | tf_op jit(solution)/shard_map/ppermute | solution.py:549
  11.5 10.1 %collective-permute-start.1 = (bf16[208,640]{1,0:T(8,128)(2,1)S(1)}, bf16[208,640]{1,0:T(8,128)(2,1)S(1)}, u32[]{:S(2)}, u32[]{:S(2)}) collective-permute-start(bf16[208,640]{1,0:T(8,128)(2,1)S(1)} %get-tuple-element.108), channel_id=1, source_target_pairs={{0,8},{4,12},{8,0},{12,4},{16,24},{20,28},{24,16},{28,20},{1,9},{5... | collective-permute-start | bytes 798728 | tf_op jit(solution)/shard_map/ppermute | solution.py:549
  14.4 14.8 %collective-permute-start.2 = (bf16[208,640]{1,0:T(8,128)(2,1)S(1)}, bf16[208,640]{1,0:T(8,128)(2,1)S(1)}, u32[]{:S(2)}, u32[]{:S(2)}) collective-permute-start(bf16[208,640]{1,0:T(8,128)(2,1)S(1)} %get-tuple-element.109), channel_id=1, source_target_pairs={{0,12},{4,8},{8,4},{12,0},{16,28},{20,24},{24,20},{28,16},{1,13},{... | collective-permute-start | bytes 798728 | tf_op jit(solution)/shard_map/ppermute | solution.py:549
  14.4 14.8 %collective-permute-start.3 = (bf16[208,640]{1,0:T(8,128)(2,1)S(1)}, bf16[208,640]{1,0:T(8,128)(2,1)S(1)}, u32[]{:S(2)}, u32[]{:S(2)}) collective-permute-start(bf16[208,640]{1,0:T(8,128)(2,1)S(1)} %get-tuple-element.110), channel_id=1, source_target_pairs={{0,16},{4,20},{8,24},{12,28},{16,0},{20,4},{24,8},{28,12},{1,17},{... | collective-permute-start | bytes 798728 | tf_op jit(solution)/shard_map/ppermute | solution.py:549
  15.9 23.8 %collective-permute-start.4 = (bf16[208,640]{1,0:T(8,128)(2,1)S(1)}, bf16[208,640]{1,0:T(8,128)(2,1)S(1)}, u32[]{:S(2)}, u32[]{:S(2)}) collective-permute-start(bf16[208,640]{1,0:T(8,128)(2,1)S(1)} %get-tuple-element.111), channel_id=1, source_target_pairs={{0,20},{4,16},{8,28},{12,24},{16,4},{20,0},{24,12},{28,8},{1,21},{... | collective-permute-start | bytes 798728 | tf_op jit(solution)/shard_map/ppermute | solution.py:549
  21.6 18.2 %collective-permute-start.5 = (bf16[208,640]{1,0:T(8,128)(2,1)S(1)}, bf16[208,640]{1,0:T(8,128)(2,1)S(1)}, u32[]{:S(2)}, u32[]{:S(2)}) collective-permute-start(bf16[208,640]{1,0:T(8,128)(2,1)S(1)} %get-tuple-element.112), channel_id=1, source_target_pairs={{0,24},{4,28},{8,16},{12,20},{16,8},{20,12},{24,0},{28,4},{1,25},{... | collective-permute-start | bytes 798728 | tf_op jit(solution)/shard_map/ppermute | solution.py:549
  24.6 15.2 %collective-permute-start.6 = (bf16[208,640]{1,0:T(8,128)(2,1)S(1)}, bf16[208,640]{1,0:T(8,128)(2,1)S(1)}, u32[]{:S(2)}, u32[]{:S(2)}) collective-permute-start(bf16[208,640]{1,0:T(8,128)(2,1)S(1)} %get-tuple-element.113), channel_id=1, source_target_pairs={{0,28},{4,24},{8,20},{12,16},{16,12},{20,8},{24,4},{28,0},{1,29},{... | collective-permute-start | bytes 798728 | tf_op jit(solution)/shard_map/ppermute | solution.py:549
  29.0 10.7 %copy-start = (f32[64,2048]{1,0:T(8,128)S(1)}, f32[64,2048]{1,0:T(8,128)}, u32[]{:S(2)}) copy-start(f32[64,2048]{1,0:T(8,128)} %refs_5_.1) | copy-start | bytes 1572868
  29.1 10.7 %copy-start.1 = (f32[2048]{0:T(1024)S(1)}, f32[2048]{0:T(1024)}, u32[]{:S(2)}) copy-start(f32[2048]{0:T(1024)} %param.10) | copy-start | bytes 24580
  44.2 26.3 %collective-permute-start.8 = (bf16[768,640]{1,0:T(8,128)(2,1)S(1)}, bf16[768,640]{1,0:T(8,128)(2,1)S(1)}, u32[]{:S(2)}, u32[]{:S(2)}) collective-permute-start(bf16[768,640]{1,0:T(8,128)(2,1)S(1)} %get-tuple-element.141.refs_0_), channel_id=1, source_target_pairs={{0,1},{1,2},{2,3},{3,0},{4,5},{5,6},{6,7},{7,4},{8,9},{9,10},{10,1... | collective-permute-start | bytes 2949128 | tf_op jit(solution)/shard_map/ppermute | solution.py:556
  46.4 6.7 %collective-permute-start.10 = (bf16[192,384]{1,0:T(8,128)(2,1)S(1)}, bf16[192,384]{1,0:T(8,128)(2,1)S(1)}, u32[]{:S(2)}, u32[]{:S(2)}) collective-permute-start(bf16[192,384]{1,0:T(8,128)(2,1)S(1)} %get-tuple-element.144), channel_id=1, source_target_pairs={{0,8},{4,12},{8,0},{12,4},{16,24},{20,28},{24,16},{28,20},{1,9},{5... | collective-permute-start | bytes 442376 | tf_op jit(solution)/shard_map/ppermute | solution.py:549
  47.9 7.7 %collective-permute-start.11 = (bf16[192,384]{1,0:T(8,128)(2,1)S(1)}, bf16[192,384]{1,0:T(8,128)(2,1)S(1)}, u32[]{:S(2)}, u32[]{:S(2)}) collective-permute-start(bf16[192,384]{1,0:T(8,128)(2,1)S(1)} %get-tuple-element.145), channel_id=1, source_target_pairs={{0,12},{4,8},{8,4},{12,0},{16,28},{20,24},{24,20},{28,16},{1,13},{... | collective-permute-start | bytes 442376 | tf_op jit(solution)/shard_map/ppermute | solution.py:549
  47.9 10.6 %collective-permute-start.12 = (bf16[192,384]{1,0:T(8,128)(2,1)S(1)}, bf16[192,384]{1,0:T(8,128)(2,1)S(1)}, u32[]{:S(2)}, u32[]{:S(2)}) collective-permute-start(bf16[192,384]{1,0:T(8,128)(2,1)S(1)} %get-tuple-element.146), channel_id=1, source_target_pairs={{0,16},{4,20},{8,24},{12,28},{16,0},{20,4},{24,8},{28,12},{1,17},{... | collective-permute-start | bytes 442376 | tf_op jit(solution)/shard_map/ppermute | solution.py:549
  49.5 14.0 %collective-permute-start.13 = (bf16[192,384]{1,0:T(8,128)(2,1)S(1)}, bf16[192,384]{1,0:T(8,128)(2,1)S(1)}, u32[]{:S(2)}, u32[]{:S(2)}) collective-permute-start(bf16[192,384]{1,0:T(8,128)(2,1)S(1)} %get-tuple-element.147), channel_id=1, source_target_pairs={{0,20},{4,16},{8,28},{12,24},{16,4},{20,0},{24,12},{28,8},{1,21},{... | collective-permute-start | bytes 442376 | tf_op jit(solution)/shard_map/ppermute | solution.py:549
  53.1 10.4 %collective-permute-start.14 = (bf16[192,384]{1,0:T(8,128)(2,1)S(1)}, bf16[192,384]{1,0:T(8,128)(2,1)S(1)}, u32[]{:S(2)}, u32[]{:S(2)}) collective-permute-start(bf16[192,384]{1,0:T(8,128)(2,1)S(1)} %get-tuple-element.148), channel_id=1, source_target_pairs={{0,24},{4,28},{8,16},{12,20},{16,8},{20,12},{24,0},{28,4},{1,25},{... | collective-permute-start | bytes 442376 | tf_op jit(solution)/shard_map/ppermute | solution.py:549
  55.6 7.8 %collective-permute-start.15 = (bf16[192,384]{1,0:T(8,128)(2,1)S(1)}, bf16[192,384]{1,0:T(8,128)(2,1)S(1)}, u32[]{:S(2)}, u32[]{:S(2)}) collective-permute-start(bf16[192,384]{1,0:T(8,128)(2,1)S(1)} %get-tuple-element.149), channel_id=1, source_target_pairs={{0,28},{4,24},{8,20},{12,16},{16,12},{20,8},{24,4},{28,0},{1,29},{... | collective-permute-start | bytes 442376 | tf_op jit(solution)/shard_map/ppermute | solution.py:549
  58.5 4.9 %collective-permute-start.9 = (bf16[192,384]{1,0:T(8,128)(2,1)S(1)}, bf16[192,384]{1,0:T(8,128)(2,1)S(1)}, u32[]{:S(2)}, u32[]{:S(2)}) collective-permute-start(bf16[192,384]{1,0:T(8,128)(2,1)S(1)} %get-tuple-element.143), channel_id=1, source_target_pairs={{0,4},{4,0},{8,12},{12,8},{16,20},{20,16},{24,28},{28,24},{1,5},{5... | collective-permute-start | bytes 442376 | tf_op jit(solution)/shard_map/ppermute | solution.py:549
  70.5 39.9 %collective-permute-start.18 = (bf16[720,1024]{1,0:T(8,128)(2,1)S(1)}, bf16[720,1024]{1,0:T(8,128)(2,1)S(1)}, u32[]{:S(2)}, u32[]{:S(2)}) collective-permute-start(bf16[720,1024]{1,0:T(8,128)(2,1)S(1)} %pad_maximum_fusion.refs_0_), channel_id=1, source_target_pairs={{0,8},{4,12},{8,0},{12,4},{16,24},{20,28},{24,16},{28,20},{1,9},{5... | collective-permute-start | bytes 4423688 | tf_op jit(solution)/shard_map/ppermute | solution.py:549
  72.0 38.4 %collective-permute-start.19 = (bf16[720,1024]{1,0:T(8,128)(2,1)S(1)}, bf16[720,1024]{1,0:T(8,128)(2,1)S(1)}, u32[]{:S(2)}, u32[]{:S(2)}) collective-permute-start(bf16[720,1024]{1,0:T(8,128)(2,1)S(1)} %pad_maximum_fusion.refs_0_), channel_id=1, source_target_pairs={{0,16},{4,20},{8,24},{12,28},{16,0},{20,4},{24,8},{28,12},{1,17},{... | collective-permute-start | bytes 4423688 | tf_op jit(solution)/shard_map/ppermute | solution.py:549
  73.5 36.9 %collective-permute-start.16 = (bf16[768,640]{1,0:T(8,128)(2,1)S(1)}, bf16[768,640]{1,0:T(8,128)(2,1)S(1)}, u32[]{:S(2)}, u32[]{:S(2)}) collective-permute-start(bf16[768,640]{1,0:T(8,128)(2,1)S(1)} %collective-permute-done.8.refs_0_), channel_id=1, source_target_pairs={{0,1},{1,2},{2,3},{3,0},{4,5},{5,6},{6,7},{7,4},{8,9},{9,10},{10,1... | collective-permute-start | bytes 2949128 | tf_op jit(solution)/shard_map/ppermute | solution.py:556
  75.7 34.7 %collective-permute-start.17 = (bf16[768,384]{1,0:T(8,128)(2,1)S(1)}, bf16[768,384]{1,0:T(8,128)(2,1)S(1)}, u32[]{:S(2)}, u32[]{:S(2)}) collective-permute-start(bf16[768,384]{1,0:T(8,128)(2,1)S(1)} %shard_map.88.refs_1_), channel_id=1, source_target_pairs={{0,1},{1,2},{2,3},{3,0},{4,5},{5,6},{6,7},{7,4},{8,9},{9,10},{10,1... | collective-permute-start | bytes 1769480 | tf_op jit(solution)/shard_map/ppermute | solution.py:556
  110.4 18.1 %collective-permute-start.21 = (bf16[768,384]{1,0:T(8,128)(2,1)S(1)}, bf16[768,384]{1,0:T(8,128)(2,1)S(1)}, u32[]{:S(2)}, u32[]{:S(2)}) collective-permute-start(bf16[768,384]{1,0:T(8,128)(2,1)S(1)} %collective-permute-done.17.refs_1_), channel_id=1, source_target_pairs={{0,1},{1,2},{2,3},{3,0},{4,5},{5,6},{6,7},{7,4},{8,9},{9,10},{10,1... | collective-permute-start | bytes 1769480 | tf_op jit(solution)/shard_map/ppermute | solution.py:556
  110.5 36.0 %collective-permute-start.20 = (bf16[768,640]{1,0:T(8,128)(2,1)S(1)}, bf16[768,640]{1,0:T(8,128)(2,1)S(1)}, u32[]{:S(2)}, u32[]{:S(2)}) collective-permute-start(bf16[768,640]{1,0:T(8,128)(2,1)S(1)} %collective-permute-done.16.refs_0_), channel_id=1, source_target_pairs={{0,1},{1,2},{2,3},{3,0},{4,5},{5,6},{6,7},{7,4},{8,9},{9,10},{10,1... | collective-permute-start | bytes 2949128 | tf_op jit(solution)/shard_map/ppermute | solution.py:556
  110.6 17.9 %collective-permute-start.22 = (bf16[720,512]{1,0:T(8,128)(2,1)S(1)}, bf16[720,512]{1,0:T(8,128)(2,1)S(1)}, u32[]{:S(2)}, u32[]{:S(2)}) collective-permute-start(bf16[720,512]{1,0:T(8,128)(2,1)S(1)} %slice.6), channel_id=1, source_target_pairs={{0,16},{4,20},{8,24},{12,28},{16,0},{20,4},{24,8},{28,12},{1,17},{... | collective-permute-start | bytes 2211848 | tf_op jit(solution)/shard_map/ppermute | solution.py:549
  111.2 1.6 collective-permute-start.24
  111.3 19.0 %collective-permute-start.23 = (bf16[720,512]{1,0:T(8,128)(2,1)S(1)}, bf16[720,512]{1,0:T(8,128)(2,1)S(1)}, u32[]{:S(2)}, u32[]{:S(2)}) collective-permute-start(bf16[720,512]{1,0:T(8,128)(2,1)S(1)} %slice.7), channel_id=1, source_target_pairs={{0,8},{4,12},{8,0},{12,4},{16,24},{20,28},{24,16},{28,20},{1,9},{5... | collective-permute-start | bytes 2211848 | tf_op jit(solution)/shard_map/ppermute | solution.py:549
  112.8 33.7 %collective-permute-start.31 = (bf16[768,640]{1,0:T(8,128)(2,1)S(1)}, bf16[768,640]{1,0:T(8,128)(2,1)S(1)}, u32[]{:S(2)}, u32[]{:S(2)}) collective-permute-start(bf16[768,640]{1,0:T(8,128)(2,1)S(1)} %get-tuple-element.141.refs_0_), channel_id=1, source_target_pairs={{0,4},{4,0},{8,12},{12,8},{16,20},{20,16},{24,28},{28,24},{1,5},{5... | collective-permute-start | bytes 2949128 | tf_op jit(solution)/shard_map/ppermute | solution.py:549
  128.5 18.5 %collective-permute-start.29 = (bf16[768,640]{1,0:T(8,128)(2,1)S(1)}, bf16[768,640]{1,0:T(8,128)(2,1)S(1)}, u32[]{:S(2)}, u32[]{:S(2)}) collective-permute-start(bf16[768,640]{1,0:T(8,128)(2,1)S(1)} %collective-permute-done.8.refs_0_), channel_id=1, source_target_pairs={{0,4},{4,0},{8,12},{12,8},{16,20},{20,16},{24,28},{28,24},{1,5},{5... | collective-permute-start | bytes 2949128 | tf_op jit(solution)/shard_map/ppermute | solution.py:549
  128.5 18.4 %collective-permute-start.32 = (bf16[768,384]{1,0:T(8,128)(2,1)S(1)}, bf16[768,384]{1,0:T(8,128)(2,1)S(1)}, u32[]{:S(2)}, u32[]{:S(2)}) collective-permute-start(bf16[768,384]{1,0:T(8,128)(2,1)S(1)} %shard_map.88.refs_1_), channel_id=1, source_target_pairs={{0,4},{4,0},{8,12},{12,8},{16,20},{20,16},{24,28},{28,24},{1,5},{5... | collective-permute-start | bytes 1769480 | tf_op jit(solution)/shard_map/ppermute | solution.py:549
  130.2 27.6 %collective-permute-start.27 = (bf16[768,640]{1,0:T(8,128)(2,1)S(1)}, bf16[768,640]{1,0:T(8,128)(2,1)S(1)}, u32[]{:S(2)}, u32[]{:S(2)}) collective-permute-start(bf16[768,640]{1,0:T(8,128)(2,1)S(1)} %collective-permute-done.16.refs_0_), channel_id=1, source_target_pairs={{0,4},{4,0},{8,12},{12,8},{16,20},{20,16},{24,28},{28,24},{1,5},{5... | collective-permute-start | bytes 2949128 | tf_op jit(solution)/shard_map/ppermute | solution.py:549
  146.4 16.9 %collective-permute-start.26 = (bf16[768,640]{1,0:T(8,128)(2,1)S(1)}, bf16[768,640]{1,0:T(8,128)(2,1)S(1)}, u32[]{:S(2)}, u32[]{:S(2)}) collective-permute-start(bf16[768,640]{1,0:T(8,128)(2,1)S(1)} %collective-permute-done.20.refs_0_), channel_id=1, source_target_pairs={{0,4},{4,0},{8,12},{12,8},{16,20},{20,16},{24,28},{28,24},{1,5},{5... | collective-permute-start | bytes 2949128 | tf_op jit(solution)/shard_map/ppermute | solution.py:549
  146.5 5.9 %collective-permute-start.30 = (bf16[768,384]{1,0:T(8,128)(2,1)S(1)}, bf16[768,384]{1,0:T(8,128)(2,1)S(1)}, u32[]{:S(2)}, u32[]{:S(2)}) collective-permute-start(bf16[768,384]{1,0:T(8,128)(2,1)S(1)} %collective-permute-done.17.refs_1_), channel_id=1, source_target_pairs={{0,4},{4,0},{8,12},{12,8},{16,20},{20,16},{24,28},{28,24},{1,5},{5... | collective-permute-start | bytes 1769480 | tf_op jit(solution)/shard_map/ppermute | solution.py:549
  147.0 10.9 %collective-permute-start.28 = (bf16[768,384]{1,0:T(8,128)(2,1)S(1)}, bf16[768,384]{1,0:T(8,128)(2,1)S(1)}, u32[]{:S(2)}, u32[]{:S(2)}) collective-permute-start(bf16[768,384]{1,0:T(8,128)(2,1)S(1)} %collective-permute-done.21.refs_1_), channel_id=1, source_target_pairs={{0,4},{4,0},{8,12},{12,8},{16,20},{20,16},{24,28},{28,24},{1,5},{5... | collective-permute-start | bytes 1769480 | tf_op jit(solution)/shard_map/ppermute | solution.py:549
  147.0 20.7 %collective-permute-start.25 = (bf16[768,384]{1,0:T(8,128)(2,1)S(1)}, bf16[768,384]{1,0:T(8,128)(2,1)S(1)}, u32[]{:S(2)}, u32[]{:S(2)}) collective-permute-start(bf16[768,384]{1,0:T(8,128)(2,1)S(1)} %collective-permute-done.21.refs_1_), channel_id=1, source_target_pairs={{0,1},{1,2},{2,3},{3,0},{4,5},{5,6},{6,7},{7,4},{8,9},{9,10},{10,1... | collective-permute-start | bytes 1769480 | tf_op jit(solution)/shard_map/ppermute | solution.py:556
  167.7 2.1 collective-permute-start.33
  175.8 1.3 collective-permute-start.34
  177.6 4.2 %collective-permute-start.35 = (f32[8,1536]{1,0:T(8,128)S(1)}, f32[8,1536]{1,0:T(8,128)S(1)}, u32[]{:S(2)}, u32[]{:S(2)}) collective-permute-start(f32[8,1536]{1,0:T(8,128)S(1)} %shard_map.95.mine_ref), channel_id=1, source_target_pairs={{0,1},{1,0},{2,3},{3,2},{4,5},{5,4},{6,7},{7,6},{8,9},{9,8},{10,11... | collective-permute-start | bytes 147464 | tf_op jit(solution)/shard_map/ppermute | solution.py:624
  182.4 5.1 %collective-permute-start.36 = (f32[8,1536]{1,0:T(8,128)S(1)}, f32[8,1536]{1,0:T(8,128)S(1)}, u32[]{:S(2)}, u32[]{:S(2)}) collective-permute-start(f32[8,1536]{1,0:T(8,128)S(1)} %shard_map.96.mine_ref), channel_id=1, source_target_pairs={{0,2},{1,3},{2,0},{3,1},{4,6},{5,7},{6,4},{7,5},{8,10},{9,11},{10,... | collective-permute-start | bytes 147464 | tf_op jit(solution)/shard_map/ppermute | solution.py:624
  192.2 5.8 %collective-permute-start.39 = (bf16[64,720]{1,0:T(8,128)(2,1)S(1)}, bf16[64,720]{1,0:T(8,128)(2,1)S(1)}, u32[]{:S(2)}, u32[]{:S(2)}) collective-permute-start(bf16[64,720]{1,0:T(8,128)(2,1)S(1)} %get-tuple-element.196), channel_id=1, source_target_pairs={{0,8},{4,12},{8,0},{12,4},{16,24},{20,28},{24,16},{28,20},{1,9},{5... | collective-permute-start | bytes 276488 | tf_op jit(solution)/shard_map/ppermute | solution.py:549
  192.8 21.5 %collective-permute-start.37 = (bf16[720,512]{1,0:T(8,128)(2,1)S(1)}, bf16[720,512]{1,0:T(8,128)(2,1)S(1)}, u32[]{:S(2)}, u32[]{:S(2)}) collective-permute-start(bf16[720,512]{1,0:T(8,128)(2,1)S(1)} %get-tuple-element.187), channel_id=1, source_target_pairs={{0,8},{4,12},{8,0},{12,4},{16,24},{20,28},{24,16},{28,20},{1,9},{5... | collective-permute-start | bytes 2211848 | tf_op jit(solution)/shard_map/ppermute | solution.py:549
  194.3 20.0 %collective-permute-start.38 = (bf16[720,512]{1,0:T(8,128)(2,1)S(1)}, bf16[720,512]{1,0:T(8,128)(2,1)S(1)}, u32[]{:S(2)}, u32[]{:S(2)}) collective-permute-start(bf16[720,512]{1,0:T(8,128)(2,1)S(1)} %get-tuple-element.188), channel_id=1, source_target_pairs={{0,16},{4,20},{8,24},{12,28},{16,0},{20,4},{24,8},{28,12},{1,17},{... | collective-permute-start | bytes 2211848 | tf_op jit(solution)/shard_map/ppermute | solution.py:549
  198.0 16.2 %collective-permute-start.40 = (f32[64,720]{1,0:T(8,128)S(1)}, f32[64,720]{1,0:T(8,128)S(1)}, u32[]{:S(2)}, u32[]{:S(2)}) collective-permute-start(f32[64,720]{1,0:T(8,128)S(1)} %convert_add_fusion), channel_id=1, source_target_pairs={{0,16},{4,20},{8,24},{12,28},{16,0},{20,4},{24,8},{28,12},{1,17},{... | collective-permute-start | bytes 552968 | tf_op jit(solution)/shard_map/ppermute | solution.py:549
  214.3 4.4 %collective-permute-start.46 = (f32[64,720]{1,0:T(8,128)S(1)}, f32[64,720]{1,0:T(8,128)S(1)}, u32[]{:S(2)}, u32[]{:S(2)}) collective-permute-start(f32[64,720]{1,0:T(8,128)S(1)} %fusion), channel_id=1, source_target_pairs={{0,4},{4,0},{8,12},{12,8},{16,20},{20,16},{24,28},{28,24},{1,5},{5... | collective-permute-start | bytes 552968 | tf_op jit(solution)/shard_map/ppermute | solution.py:549
  216.3 19.6 %collective-permute-start.41 = (bf16[720,512]{1,0:T(8,128)(2,1)}, bf16[720,512]{1,0:T(8,128)(2,1)S(1)}, u32[]{:S(2)}, u32[]{:S(2)}) collective-permute-start(bf16[720,512]{1,0:T(8,128)(2,1)} %get-tuple-element.202), channel_id=1, source_target_pairs={{0,16},{4,12},{8,24},{12,4},{16,0},{20,28},{24,8},{28,20},{1,17},{... | collective-permute-start | bytes 2211848 | tf_op jit(solution)/shard_map/ppermute | solution.py:553
  216.8 19.1 %collective-permute-start.44 = (bf16[720,512]{1,0:T(8,128)(2,1)}, bf16[720,512]{1,0:T(8,128)(2,1)S(1)}, u32[]{:S(2)}, u32[]{:S(2)}) collective-permute-start(bf16[720,512]{1,0:T(8,128)(2,1)} %get-tuple-element.205), channel_id=1, source_target_pairs={{0,12},{4,16},{8,4},{12,24},{16,28},{20,0},{24,20},{28,8},{1,13},{... | collective-permute-start | bytes 2211848 | tf_op jit(solution)/shard_map/ppermute | solution.py:553
  218.2 33.2 %collective-permute-start.42 = (bf16[720,512]{1,0:T(8,128)(2,1)}, bf16[720,512]{1,0:T(8,128)(2,1)}, u32[]{:S(2)}, u32[]{:S(2)}) collective-permute-start(bf16[720,512]{1,0:T(8,128)(2,1)} %get-tuple-element.203), channel_id=1, source_target_pairs={{0,8},{4,20},{8,0},{12,28},{16,24},{20,4},{24,16},{28,12},{1,9},{5... | collective-permute-start | bytes 2211848 | tf_op jit(solution)/shard_map/ppermute | solution.py:553
  218.7 32.6 %collective-permute-start.43 = (bf16[720,512]{1,0:T(8,128)(2,1)}, bf16[720,512]{1,0:T(8,128)(2,1)}, u32[]{:S(2)}, u32[]{:S(2)}) collective-permute-start(bf16[720,512]{1,0:T(8,128)(2,1)} %get-tuple-element.204), channel_id=1, source_target_pairs={{0,4},{4,0},{8,12},{12,8},{16,20},{20,16},{24,28},{28,24},{1,5},{5... | collective-permute-start | bytes 2211848 | tf_op jit(solution)/shard_map/ppermute | solution.py:549
  218.7 32.6 %collective-permute-start.45 = (bf16[720,512]{1,0:T(8,128)(2,1)}, bf16[720,512]{1,0:T(8,128)(2,1)}, u32[]{:S(2)}, u32[]{:S(2)}) collective-permute-start(bf16[720,512]{1,0:T(8,128)(2,1)} %get-tuple-element.206), channel_id=1, source_target_pairs={{0,20},{4,8},{8,28},{12,0},{16,4},{20,24},{24,12},{28,16},{1,21},{... | collective-permute-start | bytes 2211848 | tf_op jit(solution)/shard_map/ppermute | solution.py:553

commit v7 on v6

--- a/solution.py
+++ b/solution.py
@@ -394,11 +394,10 @@
     )(*operands)
 
 
-def merge_body(turned, meta, mine_ref, other_ref, out_ref):
+def merge_body(meta, mine_ref, other_ref, out_ref):
     rows = mine_ref.shape[1] // 2
     other = other_ref[...]
-    if turned:
-        other = jnp.concatenate([other[:, rows:], other[:, :rows]], axis=1)
+    other = jnp.concatenate([other[:, rows:], other[:, :rows]], axis=1)
     mine = mine_ref[...]
     peak = jnp.maximum(mine[0:1], other[0:1])
     mass = mine[1:2] * jnp.exp(mine[0:1] - peak) + other[1:2] * jnp.exp(other[0:1] - peak)
@@ -406,19 +405,34 @@
     out_ref[...] = jnp.where(which == 0, peak, mass)
 
 
-def merge(meta, mine, other, turned=False):
+def add_body(meta, mine_ref, other_ref, out_ref):
+    out_ref[...] = (mine_ref[...].astype(F32) + other_ref[...].astype(F32)).astype(BF16)
+
+
+def pairwise(body, meta, mine, other):
     spec = pl.BlockSpec(mine.shape, lambda j, m: (0, 0))
-    return call(functools.partial(merge_body, turned), (1,), [spec, spec], spec, sds(mine.shape, F32), room=4)(meta, mine, other)
+    return call(body, (1,), [spec, spec], spec, sds(mine.shape, mine.dtype), room=4)(
+        meta, mine, other
+    )
+
+
+merge = functools.partial(pairwise, merge_body)
+add_pair = functools.partial(pairwise, add_body)
 
 
 def class_body(kind, steps, meta, *refs):
     if kind == "first":
-        shifted_ref, stat_ref, all_ref, hot_own, hot_sib, full_ref = refs[:6]
-        outs, (post_ref, log_ref, mass_ref) = refs[6 : 6 + steps], refs[6 + steps :]
+        (shifted_ref, stat_ref), four = refs[:2], refs[2:6]
+        hot_own, hot_sib, full_ref = refs[6:9]
+        outs, (post_ref, log_ref, mass_ref) = refs[9 : 9 + steps], refs[9 + steps :]
 
         @pl.when(pl.program_id(0) == 0)
         def _():
-            peak, mass = all_ref[0:1], all_ref[1:2]
+            stats = [ref[...] for ref in four]
+            peaks = [s[0:1] for s in stats]
+            peak = jnp.maximum(jnp.maximum(peaks[0], peaks[1]), jnp.maximum(peaks[2], peaks[3]))
+            parts = [s[1:2] * jnp.exp(p - peak) for s, p in zip(stats, peaks)]
+            mass = (parts[0] + parts[1]) + (parts[2] + parts[3])
             factor = jnp.exp(stat_ref[0:1] - peak) / mass
             post_ref[...] = (shifted_ref[...] * factor).astype(BF16)
             log_ref[...] = (peak + jnp.log(mass))[:, : log_ref.shape[1]]
@@ -446,7 +460,7 @@
     out_shape = [sds((count, width), F32 if kind == "rest" else BF16)] * steps
     if kind == "first":
         operands = [shifted, *stats, *hots, full]
-        in_specs = [whole(shifted.shape)] + [whole(stats[0].shape)] * 2
+        in_specs = [whole(shifted.shape)] + [whole(stats[0].shape)] * 5
         in_specs += [whole(hots[0].shape)] * 2 + [full_spec]
         out_specs += [whole((count, rows)), whole((1, rows // 2)), whole((bins, count))]
         out_shape += [sds((count, rows), BF16), sds((1, rows // 2), F32), sds((bins, count), BF16)]
@@ -463,58 +477,6 @@
         flops=2 * count * rows * width * steps,
         moved=2 * rows * width * steps + 4 * count * (rows + width * steps),
     )(meta, *operands)
-
-
-def forward_body(meta, a_sum, b_sum, down_ref, left_ref, a_ref, b_ref):
-    even = meta[0] % 2 == 0
-    down, left = down_ref[...].astype(F32), left_ref[...].astype(F32)
-    a_ref[...] = (a_sum[...] + jnp.where(even, down, left)).astype(BF16)
-    b_ref[...] = (b_sum[...] + jnp.where(even, left, down)).astype(BF16)
-
-
-def forward(meta, a_sum, b_sum, got_x, got_y):
-    shape = a_sum.shape
-    spec = pl.BlockSpec(memory_space=pltpu.VMEM)
-    return call(forward_body, (1,), [spec] * 4, [spec] * 2, [sds(shape, BF16)] * 2, room=14)(
-        meta, a_sum, b_sum, got_x, got_y
-    )
-
-
-def finish_body(tile, meta, keep_ref, a_ref, c_ref, other_ref, b_ref, d_ref, out_ref):
-    half = pl.num_programs(0) // 2
-    step = pl.program_id(0)
-
-    def total(refs, at):
-        rows = pl.ds(pl.multiple_of(at * tile, tile), tile)
-        first, second, third = [ref[rows, :].astype(F32) for ref in refs]
-        out_ref[...] = first + second + third
-
-    @pl.when(step < half)
-    def _():
-        total((keep_ref, c_ref, a_ref), step)
-
-    @pl.when(step >= half)
-    def _():
-        total((other_ref, d_ref, b_ref), step - half)
-
-
-def finish(meta, keep, got_a, got_c, got_self, got_b, got_d):
-    count, width = keep.shape
-    half = 3
-    tile = count // half
-
-    def place(j, m):
-        core = lax.rem(m[0], 2)
-        return jnp.where(j < half, core * half + j, (1 - core) * half + j - half), 0
-
-    return call(
-        functools.partial(finish_body, tile),
-        (2 * half,),
-        [pl.BlockSpec(memory_space=pltpu.VMEM)] * 6,
-        pl.BlockSpec((tile, width), place),
-        sds((2 * count, width), F32),
-        room=12,
-    )(meta, keep, got_a, got_c, got_self, got_b, got_d)
 
 
 def two_by_two(raw_images, defocus_bin, dest_row, ctf_table, inv_noise, panels):
@@ -571,9 +533,8 @@
     together = lax.optimization_barrier
 
     count = panels.shape[0] // 2
-    place, panels = together((place, panels))
     mine = lax.dynamic_slice_in_dim(panels, core * count, count, 0)
-    other = across(lax.dynamic_slice_in_dim(panels, (1 - core) * count, count, 0), 1)
+    other = lax.dynamic_slice_in_dim(across(panels, 1), core * count, count, 0)
     near = jnp.concatenate([mine, other], axis=1)
 
     recv_a, send_b, near = together((recv_a, send_b, near))
@@ -583,23 +544,24 @@
     a1, recv_b, near = together((a1, recv_b, near))
     by_x, by_y = across(near, 2), across(near, 4)
     share_b = unpack_next(meta, pick, wide, recv_b, ctf_table, inv, width, chunk_b)
-    hots = (hot, across(hot, 1))
     a2, b1 = onward(a1), onward(share_b)
-    a2, b1, by_x, by_y = together((a2, b1, by_x, by_y))
+    sib0, sib1, hots = [across(share_a, 1), across(share_b, 1)], [across(a1, 1)], [hot, across(hot, 1)]
+    a2, b1, by_x, by_y, sib0, sib1, hots = together((a2, b1, by_x, by_y, sib0, sib1, hots))
+    sib1 = sib1 + [across(b1, 1)]
     piece = near.shape[1] // 2
     far_y, far_x = across(by_x[:, :piece], 4), across(by_y[:, piece:], 2)
     a3, b2 = onward(a2), onward(b1)
     panel_full, extra = energy(meta, [near, by_x, by_y, far_y, far_x], ctf_table, inv)
-    a3, b2, panel_full, extra, hots = together((a3, b2, panel_full, extra, hots))
-    b3 = onward(b2)
 
     def share(turn):
         return lambda m: lax.rem(m[1] + turns - turn, turns)
 
-    acc = full = None
-    for turn, own in enumerate([(share_a, share_b), (a1, b1), (a2, b2)]):
-        sib = [across(value, 1) for value in own]
-        acc, full = score(meta, share(turn), own, sib, panel_full, width, acc, full)
+    acc, full = score(meta, share(0), [share_a, share_b], sib0, panel_full, width)
+    acc, full = score(meta, share(1), [a1, b1], sib1, panel_full, width, acc, full)
+    a3, b2, acc, full = together((a3, b2, acc, full))
+    b3 = onward(b2)
+    sib2 = [across(a2, 1), across(b2, 1)]
+    acc, full = score(meta, share(2), [a2, b2], sib2, panel_full, width, acc, full)
     final = share(turns - 1)
     a3_sib = across(a3, 1)
     acc = score(meta, final, [a3], [a3_sib], panel_full, width, acc, used=chunk_a)
@@ -618,33 +580,43 @@
         chunk_b,
     )
 
-    total = merge(meta, stat, across(stat, 1), turned=True)
-    for apart in (1, 2):
-        pairs = [(i, i ^ apart) for i in range(turns)]
-        total = merge(meta, total, lax.ppermute(total, "rot", pairs))
+    pair = merge(meta, stat, across(stat, 1))
+    others = [
+        lax.ppermute(pair, "rot", [(i, i ^ apart) for i in range(turns)]) for apart in (1, 2, 3)
+    ]
     to_x, to_y, post, log_evidence, mass = class_part(
-        meta, "first", 2, 2, full, None, shifted, [stat, total], hots, bins
+        meta, "first", 2, 2, full, None, shifted, [stat, pair, *others], hots, bins
     )
     mass_x = across(mass, 2)
     got_x, got_y = across(to_x, 2), across(to_y, 4)
+    a_sum, b_sum, keep = class_part(meta, "rest", 7, 3, full, post)
+    mass_x, post, keep = together((mass_x, post, keep))
+    mass = add_pair(meta, mass, mass_x)
+    mass_y = across(mass, 4)
     send_c, send_d, give = class_part(meta, "next", 4, 3, full, post)
-    mass = mass.astype(F32) + mass_x.astype(F32)
-    mass = mass + across(mass, 4)
-    a_sum, b_sum, keep = class_part(meta, "rest", 7, 3, full, post)
-    got_x, got_y, send_c, send_d, a_sum, b_sum, keep, give, mass = together(
-        (got_x, got_y, send_c, send_d, a_sum, b_sum, keep, give, mass)
+    got_x, got_y, send_c, send_d, a_sum, b_sum, keep, give, mass, mass_y = together(
+        (got_x, got_y, send_c, send_d, a_sum, b_sum, keep, give, mass, mass_y)
     )
     got_c, got_d = by_core(send_c, 2, 4), by_core(send_d, 5, 3)
-    message_a, message_b = forward(meta, a_sum, b_sum, got_x, got_y)
+    down, left = got_x.astype(F32), got_y.astype(F32)
+    message_a = (a_sum + jnp.where(even, down, left)).astype(BF16)
+    message_b = (b_sum + jnp.where(even, left, down)).astype(BF16)
     got_a, got_b = by_core(message_a, 4, 2), by_core(message_b, 3, 5)
     got_self = across(give, 1)
+    mass = mass.astype(F32) + mass_y.astype(F32)
     mass_other = across(mass, 1)
     bin_weights = jnp.where(
         even,
         jnp.concatenate([mass, mass_other], axis=1),
         jnp.concatenate([mass_other, mass], axis=1),
     )
-    class_sums = finish(meta, keep, got_a, got_c, got_self, got_b, got_d).T
+    own_half = keep + got_c.astype(F32) + got_a.astype(F32)
+    other_half = got_self.astype(F32) + got_d.astype(F32) + got_b.astype(F32)
+    class_sums = jnp.where(
+        even,
+        jnp.concatenate([own_half, other_half], axis=0),
+        jnp.concatenate([other_half, own_half], axis=0),
+    ).T
     return class_sums, bin_weights, log_evidence.reshape(-1)
 
 

time: 257 us -> 254 us (0.988)
  Pallas kernels: 75.7 us -> 67.6 us
  other arithmetic: 1.77 us -> 8.86 us
    ppermute x35, waiting for transfers between devices: 36.1 us -> 63.6 us  [across(): return lax.ppermute(value, 'dom', [(i, i ^ apart) for i in range(dom)])]
    ppermute x6, waiting for transfers between devices: 65.4 us -> 46.5 us  [onward(): lax.ppermute(value, 'rot', [(i, (i + 1) % turns) for i in range(turns)])]
    pallas_call x5 -> x2, Pallas kernels: 8.63 us -> 1.14 us  [pairwise(): call(body, (1,), [spec, spec], spec, sds(mine.shape, mine.dtype), room=4)]
    ppermute x4, waiting for transfers between devices: 29.9 us -> 22.8 us  [by_core(): return lax.ppermute(value, 'dom', pairs)]
    ppermute x2 -> x3, waiting for transfers between devices: 6.71 us -> 3.03 us  [two_by_two(): lax.ppermute(pair, 'rot', [(i, i ^ apart) for i in range(turns)])]
    add x2 -> x3, other arithmetic: 0.06 us -> 3.48 us  [the longest x1 1.82 us: two_by_two(): other_half = got_self.astype(F32) + got_d.astype(F32) + got_b.astype(F32)]
    ppermute x35, starting transfers between devices: 26.7 us -> 24.1 us  [across(): return lax.ppermute(value, 'dom', [(i, i ^ apart) for i in range(dom)])]
  transfers between devices with their start and end apart: 47 -> 48, of which waited for: 18 -> 26; matrix products, arithmetic and copies ran while one was open for 1% -> 2% of each run, Pallas kernels for 18% -> 21%
where the time goes in v7:
time: 254 us; the launch traced here: 252 us
  waiting for transfers between devices  136 us (54%)
  Pallas kernels  67.6 us (27%)
  starting transfers between devices  36 us (14%)
  other arithmetic  8.86 us (3%)
  local copies, waits for them, and re-layouts  2.85 us (1%)
    ppermute x35, waiting for transfers between devices, across(): return lax.ppermute(value, 'dom', [(i, i ^ apart) for i in range(dom)])  63.6 us
    ppermute x6, waiting for transfers between devices, onward(): lax.ppermute(value, 'rot', [(i, (i + 1) % turns) for i in range(turns)])  46.5 us
    pallas_call x5, Pallas kernels, score(): call(functools.partial(score_body, parts, used, first, last), (2 * half,)...  26.4 us
    ppermute x35, starting transfers between devices, across(): return lax.ppermute(value, 'dom', [(i, i ^ apart) for i in range(dom)])  24.1 us
    ppermute x4, waiting for transfers between devices, by_core(): return lax.ppermute(value, 'dom', pairs)  22.8 us
    pallas_call x3, Pallas kernels, class_part(): call(functools.partial(class_body, kind, steps), (steps,), in_specs, out_...  14.9 us
    pallas_call x1, Pallas kernels, pack_first(): call(functools.partial(pack_first_body, dom, hold // 2, cap), (1,), [pl.B...  7.28 us
    pallas_call x1, Pallas kernels, energy(): call(functools.partial(energy_body, bins, count), (count,), [pl.BlockSpec...  6.86 us
  transfers between devices with their start and end apart: 48, of which 26 were waited for; matrix products, arithmetic and copies ran while one was open for 2% of the time, Pallas kernels for 21%

profile of v7, /device:TPU:0, one launch (start us, length us, event | category | flops | bytes accessed | tf_op | source)
XLA Modules:
  0.0 252.2 jit_solution(13306999679331294866)
XLA Ops:
  1.2 0.7 copy-done.2
  1.9 0.7 copy-done.3
  2.6 7.3 %shard_map.85 = (bf16[208,640]{1,0:T(8,128)(2,1)S(1)}, bf16[208,640]{1,0:T(8,128)(2,1)S(1)}, bf16[208,640]{1,0:T(8,128)(2,1)S(1)}, bf16[208,640]{1,0:T(8,128)(2,...) custom-call(s32[10]{0:T(128)S(1)} %stack.43.meta, ...), custom_call_target="tpu_custom_call" | custom-call | flops 188743680 | bytes 245760 | tf_op jit(solution)/shard_map/pallas_call | solution.py:130
  10.0 2.9 %collective-permute-start.1 = (bf16[208,640]{1,0:T(8,128)(2,1)S(1)}, bf16[208,640]{1,0:T(8,128)(2,1)S(1)}, u32[]{:S(2)}, u32[]{:S(2)}) collective-permute-start(bf16[208,640]{1,0:T(8,128)(2,1)S(1)} %get-tuple-element.112), channel_id=1, source_target_pairs={{0,8},{4,12},{8,0},{12,4},{16,24},{20,28},{24,16},{28,20},{1,9},{5... | collective-permute-start | bytes 798728 | tf_op jit(solution)/shard_map/ppermute | solution.py:511
  13.0 1.5 collective-permute-start.3
  14.5 4.4 %shard_map.86 = (bf16[192,384]{1,0:T(8,128)(2,1)S(1)}, bf16[192,384]{1,0:T(8,128)(2,1)S(1)}, bf16[192,384]{1,0:T(8,128)(2,1)S(1)}, bf16[192,384]{1,0:T(8,128)(2,...) custom-call(s32[10]{0:T(128)S(1)} %stack.43.meta, ...), custom_call_target="tpu_custom_call" | custom-call | flops 113246208 | bytes 147456 | tf_op jit(solution)/shard_map/pallas_call | solution.py:150
  19.3 0.8 collective-permute-done.1.refs_2_
  20.2 3.0 %collective-permute-start.5 = (bf16[208,640]{1,0:T(8,128)(2,1)S(1)}, bf16[208,640]{1,0:T(8,128)(2,1)S(1)}, u32[]{:S(2)}, u32[]{:S(2)}) collective-permute-start(bf16[208,640]{1,0:T(8,128)(2,1)S(1)} %get-tuple-element.116), channel_id=1, source_target_pairs={{0,24},{4,28},{8,16},{12,20},{16,8},{20,12},{24,0},{28,4},{1,25},{... | collective-permute-start | bytes 798728 | tf_op jit(solution)/shard_map/ppermute | solution.py:511
  23.2 1.2 constant_dynamic-slice_fusion
  24.6 0.9 collective-permute-done.2.refs_3_
  25.5 13.3 %collective-permute-done.4.refs_5_ = bf16[208,640]{1,0:T(8,128)(2,1)S(1)} collective-permute-done((bf16[208,640]{1,0:T(8,128)(2,1)S(1)}, bf16[208,640]{1,0:T(8,128)(2,1)S(1)}, u32[]{:S(2)}, u32[]{:S(2)}) %collective-permute-start.4) | collective-permute-done | bytes 266272 | tf_op jit(solution)/shard_map/ppermute | solution.py:511
  38.7 4.4 %shard_map.87 = (bf16[768,640]{1,0:T(8,128)(2,1)S(1)}, bf16[192,768]{1,0:T(8,128)(2,1)S(1)}, bf16[768,1536]{1,0:T(8,128)(2,1)S(1)}, bf16[768,192]{1,0:T(8,128)(2,1)S(1)}) custom-call(s32[10]{0:T(128)S(1)} %stack.43.meta, bf16[208,640]{1,0:T(8,128)(2,1)S(1)} %get-tuple-element.127.refs_0_, bf16[208,640]{1,0:T(8,128)(2,1)S(1)} %collective-permute-done.refs_1_, ...), custom_call_target="tpu_custom_call" | custom-call | flops 94371840 | bytes 122880 | tf_op jit(solution)/shard_map/pallas_call | solution.py:210
  43.1 1.8 collective-permute-start.8
  45.0 1.5 collective-permute-start.10
  46.8 1.5 collective-permute-start.12
  48.3 3.3 %collective-permute-done.10.refs_2_ = bf16[192,384]{1,0:T(8,128)(2,1)S(1)} collective-permute-done((bf16[192,384]{1,0:T(8,128)(2,1)S(1)}, bf16[192,384]{1,0:T(8,128)(2,1)S(1)}, u32[]{:S(2)}, u32[]{:S(2)}) %collective-permute-start.10) | collective-permute-done | bytes 147488 | tf_op jit(solution)/shard_map/ppermute | solution.py:511
  52.1 1.9 collective-permute-done.11.refs_3_
  54.0 2.5 collective-permute-start.14
  56.7 1.0 collective-permute-done.13.refs_5_
  57.9 3.6 %collective-permute-done.14.refs_6_ = bf16[192,384]{1,0:T(8,128)(2,1)S(1)} collective-permute-done((bf16[192,384]{1,0:T(8,128)(2,1)S(1)}, bf16[192,384]{1,0:T(8,128)(2,1)S(1)}, u32[]{:S(2)}, u32[]{:S(2)}) %collective-permute-start.14) | collective-permute-done | bytes 147488 | tf_op jit(solution)/shard_map/ppermute | solution.py:511
  61.5 2.4 collective-permute-done.15.refs_7_
  63.9 5.3 %collective-permute-done.8.refs_0_ = bf16[768,640]{1,0:T(8,128)(2,1)S(1)} collective-permute-done((bf16[768,640]{1,0:T(8,128)(2,1)S(1)}, bf16[768,640]{1,0:T(8,128)(2,1)S(1)}, u32[]{:S(2)}, u32[]{:S(2)}) %collective-permute-start.8) | collective-permute-done | bytes 983072 | tf_op jit(solution)/shard_map/ppermute | solution.py:518
  69.2 1.4 collective-permute-start.18
  70.6 1.5 collective-permute-start.19
  72.1 2.2 shard_map.88.refs_1_
  74.4 1.3 collective-permute-start.16
  75.6 16.6 %collective-permute-done.17.refs_1_ = bf16[768,384]{1,0:T(8,128)(2,1)S(1)} collective-permute-done((bf16[768,384]{1,0:T(8,128)(2,1)S(1)}, bf16[768,384]{1,0:T(8,128)(2,1)S(1)}, u32[]{:S(2)}, u32[]{:S(2)}) %collective-permute-start.17) | collective-permute-done | bytes 589856 | tf_op jit(solution)/shard_map/ppermute | solution.py:518
  92.3 2.0 collective-permute-done.21.refs_3_
  94.3 18.7 %collective-permute-done.16.refs_0_ = bf16[768,640]{1,0:T(8,128)(2,1)S(1)} collective-permute-done((bf16[768,640]{1,0:T(8,128)(2,1)S(1)}, bf16[768,640]{1,0:T(8,128)(2,1)S(1)}, u32[]{:S(2)}, u32[]{:S(2)}) %collective-permute-start.16) | collective-permute-done | bytes 983072 | tf_op jit(solution)/shard_map/ppermute | solution.py:518
  113.1 0.6 collective-permute-start.27
  113.8 0.7 collective-permute-start.28
  114.5 16.8 %collective-permute-done.27.refs_3_ = bf16[720,512]{1,0:T(8,128)(2,1)S(1)} collective-permute-done((bf16[720,512]{1,0:T(8,128)(2,1)S(1)}, bf16[720,512]{1,0:T(8,128)(2,1)S(1)}, u32[]{:S(2)}, u32[]{:S(2)}) %collective-permute-start.27) | collective-permute-done | bytes 737312 | tf_op jit(solution)/shard_map/ppermute | solution.py:511
  131.7 6.9 %shard_map.89 = (bf16[720,4096]{1,0:T(8,128)(2,1)S(1)}, bf16[720,192]{1,0:T(8,128)(2,1)S(1)}) custom-call(s32[10]{0:T(128)S(1)} %stack.43.meta, bf16[720,1024]{1,0:T(8,128)(2,1)S(1)} %pad_maximum_fusion.refs_0_, bf16[720,1024]{1,0:T(8,128)(2,1)S(1)} %collective-permute-done.18.refs_1_, bf16[720,1024]{1,0:T(8,128)(2,1)S(1)} %collective-permute-done.19.refs_2_, ...), custom_call_target="tpu_custom_call" | custom-call | flops 283115520 | bytes 737280 | tf_op jit(solution)/shard_map/pallas_call | solution.py:280
  138.6 5.1 %shard_map.90 = (f32[720,1536]{1,0:T(8,128)S(1)}, bf16[1536,4096]{1,0:T(8,128)(2,1)S(1)}) custom-call(s32[10]{0:T(128)S(1)} %stack.43.meta, bf16[768,640]{1,0:T(8,128)(2,1)S(1)} %get-tuple-element.144.refs_0_, bf16[768,384]{1,0:T(8,128)(2,1)S(1)} %shard_map.88.refs_1_, bf16[768,640]{1,0:T(8,128)(2,1)S(1)} %collective-permute-done.20.refs_2_, ...), custom_call_target="tpu_custom_call" | custom-call | flops 141557760 | bytes 946176 | tf_op jit(solution)/shard_map/pallas_call | solution.py:384
  143.7 5.5 %shard_map.91 = (f32[720,1536]{1,0:T(8,128)S(1)}, bf16[1536,4096]{1,0:T(8,128)(2,1)S(1)}) custom-call(s32[10]{0:T(128)S(1)} %stack.43.meta, bf16[768,640]{1,0:T(8,128)(2,1)S(1)} %collective-permute-done.8.refs_0_, bf16[768,384]{1,0:T(8,128)(2,1)S(1)} %collective-permute-done.17.refs_1_, ...), custom_call_target="tpu_custom_call", output_to_operand_aliasing={{0}: (6, {}), {1}: (7, {})} | custom-call | flops 141557760 | bytes 946176 | tf_op jit(solution)/shard_map/pallas_call | solution.py:384
  149.2 1.7 collective-permute-done.25.refs_1_
  151.4 2.9 %collective-permute-done.32.refs_3_ = bf16[768,384]{1,0:T(8,128)(2,1)S(1)} collective-permute-done((bf16[768,384]{1,0:T(8,128)(2,1)S(1)}, bf16[768,384]{1,0:T(8,128)(2,1)S(1)}, u32[]{:S(2)}, u32[]{:S(2)}) %collective-permute-start.32) | collective-permute-done | bytes 589856 | tf_op jit(solution)/shard_map/ppermute | solution.py:511
  154.3 5.5 %shard_map.92 = (f32[720,1536]{1,0:T(8,128)S(1)}, bf16[1536,4096]{1,0:T(8,128)(2,1)S(1)}) custom-call(s32[10]{0:T(128)S(1)} %stack.43.meta, bf16[768,640]{1,0:T(8,128)(2,1)S(1)} %collective-permute-done.16.refs_0_, bf16[768,384]{1,0:T(8,128)(2,1)S(1)} %collective-permute-done.25.refs_1_, ...), custom_call_target="tpu_custom_call", output_to_operand_aliasing={{0}: (6, {}), {1}: (7, {})} | custom-call | flops 141557760 | bytes 946176 | tf_op jit(solution)/shard_map/pallas_call | solution.py:384
  159.8 4.4 %shard_map.93.refs_5_ = f32[720,1536]{1,0:T(8,128)S(1)} custom-call(s32[10]{0:T(128)S(1)} %stack.43.meta, bf16[768,640]{1,0:T(8,128)(2,1)S(1)} %collective-permute-done.24.refs_0_, bf16[768,640]{1,0:T(8,128)(2,1)S(1)} %collective-permute-done.30.refs_1_.refs_2_, ...), custom_call_target="tpu_custom_call", output_to_operand_aliasing={{}: (4, {})} | custom-call | flops 141557760 | bytes 946176 | tf_op jit(solution)/shard_map/pallas_call | solution.py:384
  164.2 4.2 %collective-permute-done.29.refs_1_ = bf16[768,384]{1,0:T(8,128)(2,1)S(1)} collective-permute-done((bf16[768,384]{1,0:T(8,128)(2,1)S(1)}, bf16[768,384]{1,0:T(8,128)(2,1)S(1)}, u32[]{:S(2)}, u32[]{:S(2)}) %collective-permute-start.29) | collective-permute-done | bytes 589856 | tf_op jit(solution)/shard_map/ppermute | solution.py:518
  168.4 2.0 collective-permute-done.33.refs_3_
  170.4 5.9 %shard_map.94 = (f32[720,1536]{1,0:T(8,128)S(1)}, f32[8,1536]{1,0:T(8,128)S(1)}, bf16[1536,4096]{1,0:T(8,128)(2,1)S(1)}) custom-call(s32[10]{0:T(128)S(1)} %stack.43.meta, bf16[768,640]{1,0:T(8,128)(2,1)S(1)} %collective-permute-done.24.refs_0_, bf16[768,384]{1,0:T(8,128)(2,1)S(1)} %collective-permute-done.29.refs_1_, ...), custom_call_target="tpu_custom_call", output_to_operand_aliasing={{0}: (6, {}), {2}: (7, {})} | custom-call | flops 141557760 | bytes 946176 | tf_op jit(solution)/shard_map/pallas_call | solution.py:384
  176.6 1.1 collective-permute-done.34.other_ref
  178.3 0.8 collective-permute-start.36
  179.1 3.6 %collective-permute-start.37 = (f32[8,1536]{1,0:T(8,128)S(1)}, f32[8,1536]{1,0:T(8,128)S(1)}, u32[]{:S(2)}, u32[]{:S(2)}) collective-permute-start(f32[8,1536]{1,0:T(8,128)S(1)} %shard_map.95.refs_2_), channel_id=1, source_target_pairs={{0,3},{1,2},{2,1},{3,0},{4,7},{5,6},{6,5},{7,4},{8,11},{9,10},{10,... | collective-permute-start | bytes 147464 | tf_op jit(solution)/shard_map/ppermute | solution.py:585
  183.0 2.7 %collective-permute-done.36.refs_4_ = f32[8,1536]{1,0:T(8,128)S(1)} collective-permute-done((f32[8,1536]{1,0:T(8,128)S(1)}, f32[8,1536]{1,0:T(8,128)S(1)}, u32[]{:S(2)}, u32[]{:S(2)}) %collective-permute-start.36) | collective-permute-done | bytes 49184 | tf_op jit(solution)/shard_map/ppermute | solution.py:585
  185.7 4.2 %shard_map.96 = (bf16[720,512]{1,0:T(8,128)(2,1)S(1)}, bf16[720,512]{1,0:T(8,128)(2,1)S(1)}, bf16[720,1536]{1,0:T(8,128)(2,1)S(1)}, f32[1,768]{1,0:T(1,128)S(1)}, bf16[64,720]{1,0:T(8,128)(2,1)S(1)}) custom-call(s32[10]{0:T(128)S(1)} %stack.43.meta, f32[720,1536]{1,0:T(8,128)S(1)} %get-tuple-element.190.refs_0_, ...), custom_call_target="tpu_custom_call" | custom-call | flops 141557760 | bytes 657408 | tf_op jit(solution)/shard_map/pallas_call | solution.py:470
  190.5 0.8 collective-permute-start.39
  191.3 1.5 collective-permute-start.40
  192.8 4.9 %shard_map.97 = (f32[720,512]{1,0:T(8,128)S(1)}, f32[720,512]{1,0:T(8,128)S(1)}, f32[720,512]{1,0:T(8,128)S(1)}) custom-call(s32[10]{0:T(128)S(1)} %stack.43.meta, bf16[720,1536]{1,0:T(8,128)(2,1)S(1)} %get-tuple-element.198.refs_0_, bf16[1536,4096]{1,0:T(8,128)(2,1)S(1)} %get-tuple-element.192.refs_8_.refs_1_), custom_call_target="tpu_custom_call" | custom-call | flops 212336640 | bytes 847872 | tf_op jit(solution)/shard_map/pallas_call | solution.py:470
  197.7 11.2 %collective-permute-done.40.other_ref = bf16[64,720]{1,0:T(8,128)(2,1)S(1)} collective-permute-done((bf16[64,720]{1,0:T(8,128)(2,1)S(1)}, bf16[64,720]{1,0:T(8,128)(2,1)S(1)}, u32[]{:S(2)}, u32[]{:S(2)}) %collective-permute-start.40) | collective-permute-done | bytes 92192 | tf_op jit(solution)/shard_map/ppermute | solution.py:511
  209.5 1.1 collective-permute-start.41
  210.6 5.8 %shard_map.98 = (bf16[720,512]{1,0:T(8,128)(2,1)}, bf16[720,512]{1,0:T(8,128)(2,1)S(1)}, bf16[720,512]{1,0:T(8,128)(2,1)S(1)}) custom-call(s32[10]{0:T(128)S(1)} %stack.43.meta, bf16[720,1536]{1,0:T(8,128)(2,1)S(1)} %get-tuple-element.198.refs_0_, bf16[1536,4096]{1,0:T(8,128)(2,1)S(1)} %get-tuple-element.192.refs_8_.refs_1_), custom_call_target="tpu_custom_call" | custom-call | flops 212336640 | bytes 847872 | tf_op jit(solution)/shard_map/pallas_call | solution.py:470
  216.4 1.7 fusion.2
  218.1 1.0 collective-permute-start.43
  219.7 1.6 collective-permute-start.46
  221.3 1.1 collective-permute-start.45
  223.1 0.9 maximum_select_fusion.1
  224.0 13.8 %collective-permute-done.43 = bf16[720,512]{1,0:T(8,128)(2,1)} collective-permute-done((bf16[720,512]{1,0:T(8,128)(2,1)}, bf16[720,512]{1,0:T(8,128)(2,1)}, u32[]{:S(2)}, u32[]{:S(2)}) %collective-permute-start.43) | collective-permute-done | bytes 737312 | tf_op jit(solution)/shard_map/ppermute | solution.py:515
  237.8 1.0 collective-permute-done.42
  238.8 1.6 convert_add_fusion.1
  240.5 7.5 %collective-permute-done.46 = bf16[720,512]{1,0:T(8,128)(2,1)} collective-permute-done((bf16[720,512]{1,0:T(8,128)(2,1)}, bf16[720,512]{1,0:T(8,128)(2,1)}, u32[]{:S(2)}, u32[]{:S(2)}) %collective-permute-start.46) | collective-permute-done | bytes 737312 | tf_op jit(solution)/shard_map/ppermute | solution.py:515
  248.4 1.8 convert_add_fusion
  250.2 1.9 fusion
  (70 shorter events, 7.8 us)
Async XLA Ops:
  0.6 22.6 %collective-permute-start.7 = (bf16[1440,512]{1,0:T(8,128)(2,1)}, bf16[1440,512]{1,0:T(8,128)(2,1)}, u32[]{:S(2)}, u32[]{:S(2)}) collective-permute-start(bf16[1440,512]{1,0:T(8,128)(2,1)} %param.11), channel_id=1, source_target_pairs={{0,4},{4,0},{8,12},{12,8},{16,20},{20,16},{24,28},{28,24},{1,5},{5... | collective-permute-start | bytes 4423688 | tf_op jit(solution)/shard_map/ppermute | solution.py:511
  1.2 0.7 copy-start.2
  1.9 0.7 copy-start.3
  9.9 9.1 %collective-permute-start = (bf16[208,640]{1,0:T(8,128)(2,1)S(1)}, bf16[208,640]{1,0:T(8,128)(2,1)S(1)}, u32[]{:S(2)}, u32[]{:S(2)}) collective-permute-start(bf16[208,640]{1,0:T(8,128)(2,1)S(1)} %get-tuple-element.111), channel_id=1, source_target_pairs={{0,4},{4,0},{8,12},{12,8},{16,20},{20,16},{24,28},{28,24},{1,5},{5... | collective-permute-start | bytes 798728 | tf_op jit(solution)/shard_map/ppermute | solution.py:511
  10.0 10.1 %collective-permute-start.1 = (bf16[208,640]{1,0:T(8,128)(2,1)S(1)}, bf16[208,640]{1,0:T(8,128)(2,1)S(1)}, u32[]{:S(2)}, u32[]{:S(2)}) collective-permute-start(bf16[208,640]{1,0:T(8,128)(2,1)S(1)} %get-tuple-element.112), channel_id=1, source_target_pairs={{0,8},{4,12},{8,0},{12,4},{16,24},{20,28},{24,16},{28,20},{1,9},{5... | collective-permute-start | bytes 798728 | tf_op jit(solution)/shard_map/ppermute | solution.py:511
  13.0 12.5 %collective-permute-start.2 = (bf16[208,640]{1,0:T(8,128)(2,1)S(1)}, bf16[208,640]{1,0:T(8,128)(2,1)S(1)}, u32[]{:S(2)}, u32[]{:S(2)}) collective-permute-start(bf16[208,640]{1,0:T(8,128)(2,1)S(1)} %get-tuple-element.113), channel_id=1, source_target_pairs={{0,12},{4,8},{8,4},{12,0},{16,28},{20,24},{24,20},{28,16},{1,13},{... | collective-permute-start | bytes 798728 | tf_op jit(solution)/shard_map/ppermute | solution.py:511
  13.0 12.5 %collective-permute-start.3 = (bf16[208,640]{1,0:T(8,128)(2,1)S(1)}, bf16[208,640]{1,0:T(8,128)(2,1)S(1)}, u32[]{:S(2)}, u32[]{:S(2)}) collective-permute-start(bf16[208,640]{1,0:T(8,128)(2,1)S(1)} %get-tuple-element.114), channel_id=1, source_target_pairs={{0,16},{4,20},{8,24},{12,28},{16,0},{20,4},{24,8},{28,12},{1,17},{... | collective-permute-start | bytes 798728 | tf_op jit(solution)/shard_map/ppermute | solution.py:511
  14.5 4.4 %copy-start.4 = (bf16[1440,512]{1,0:T(8,128)(2,1)S(1)}, bf16[1440,512]{1,0:T(8,128)(2,1)}, u32[]{:S(2)}) copy-start(bf16[1440,512]{1,0:T(8,128)(2,1)} %param.11) | copy-start | bytes 4423684
  19.0 19.7 %collective-permute-start.4 = (bf16[208,640]{1,0:T(8,128)(2,1)S(1)}, bf16[208,640]{1,0:T(8,128)(2,1)S(1)}, u32[]{:S(2)}, u32[]{:S(2)}) collective-permute-start(bf16[208,640]{1,0:T(8,128)(2,1)S(1)} %get-tuple-element.115), channel_id=1, source_target_pairs={{0,20},{4,16},{8,28},{12,24},{16,4},{20,0},{24,12},{28,8},{1,21},{... | collective-permute-start | bytes 798728 | tf_op jit(solution)/shard_map/ppermute | solution.py:511
  20.2 18.6 %collective-permute-start.5 = (bf16[208,640]{1,0:T(8,128)(2,1)S(1)}, bf16[208,640]{1,0:T(8,128)(2,1)S(1)}, u32[]{:S(2)}, u32[]{:S(2)}) collective-permute-start(bf16[208,640]{1,0:T(8,128)(2,1)S(1)} %get-tuple-element.116), channel_id=1, source_target_pairs={{0,24},{4,28},{8,16},{12,20},{16,8},{20,12},{24,0},{28,4},{1,25},{... | collective-permute-start | bytes 798728 | tf_op jit(solution)/shard_map/ppermute | solution.py:511
  23.2 15.5 %collective-permute-start.6 = (bf16[208,640]{1,0:T(8,128)(2,1)S(1)}, bf16[208,640]{1,0:T(8,128)(2,1)S(1)}, u32[]{:S(2)}, u32[]{:S(2)}) collective-permute-start(bf16[208,640]{1,0:T(8,128)(2,1)S(1)} %get-tuple-element.117), channel_id=1, source_target_pairs={{0,28},{4,24},{8,20},{12,16},{16,12},{20,8},{24,4},{28,0},{1,29},{... | collective-permute-start | bytes 798728 | tf_op jit(solution)/shard_map/ppermute | solution.py:511
  24.4 14.4 %copy-start = (f32[64,2048]{1,0:T(8,128)S(1)}, f32[64,2048]{1,0:T(8,128)}, u32[]{:S(2)}) copy-start(f32[64,2048]{1,0:T(8,128)} %refs_5_.1) | copy-start | bytes 1572868
  24.4 14.4 %copy-start.1 = (f32[2048]{0:T(1024)S(1)}, f32[2048]{0:T(1024)}, u32[]{:S(2)}) copy-start(f32[2048]{0:T(1024)} %param.10) | copy-start | bytes 24580
  43.1 26.1 %collective-permute-start.8 = (bf16[768,640]{1,0:T(8,128)(2,1)S(1)}, bf16[768,640]{1,0:T(8,128)(2,1)S(1)}, u32[]{:S(2)}, u32[]{:S(2)}) collective-permute-start(bf16[768,640]{1,0:T(8,128)(2,1)S(1)} %get-tuple-element.144.refs_0_), channel_id=1, source_target_pairs={{0,1},{1,2},{2,3},{3,0},{4,5},{5,6},{6,7},{7,4},{8,9},{9,10},{10,1... | collective-permute-start | bytes 2949128 | tf_op jit(solution)/shard_map/ppermute | solution.py:518
  45.0 30.7 %collective-permute-start.20 = (bf16[768,640]{1,0:T(8,128)(2,1)S(1)}, bf16[768,640]{1,0:T(8,128)(2,1)S(1)}, u32[]{:S(2)}, u32[]{:S(2)}) collective-permute-start(bf16[768,640]{1,0:T(8,128)(2,1)S(1)} %get-tuple-element.144.refs_0_), channel_id=1, source_target_pairs={{0,4},{4,0},{8,12},{12,8},{16,20},{20,16},{24,28},{28,24},{1,5},{5... | collective-permute-start | bytes 2949128 | tf_op jit(solution)/shard_map/ppermute | solution.py:511
  45.0 6.6 %collective-permute-start.10 = (bf16[192,384]{1,0:T(8,128)(2,1)S(1)}, bf16[192,384]{1,0:T(8,128)(2,1)S(1)}, u32[]{:S(2)}, u32[]{:S(2)}) collective-permute-start(bf16[192,384]{1,0:T(8,128)(2,1)S(1)} %get-tuple-element.147), channel_id=1, source_target_pairs={{0,8},{4,12},{8,0},{12,4},{16,24},{20,28},{24,16},{28,20},{1,9},{5... | collective-permute-start | bytes 442376 | tf_op jit(solution)/shard_map/ppermute | solution.py:511
  46.4 7.6 %collective-permute-start.11 = (bf16[192,384]{1,0:T(8,128)(2,1)S(1)}, bf16[192,384]{1,0:T(8,128)(2,1)S(1)}, u32[]{:S(2)}, u32[]{:S(2)}) collective-permute-start(bf16[192,384]{1,0:T(8,128)(2,1)S(1)} %get-tuple-element.148), channel_id=1, source_target_pairs={{0,12},{4,8},{8,4},{12,0},{16,28},{20,24},{24,20},{28,16},{1,13},{... | collective-permute-start | bytes 442376 | tf_op jit(solution)/shard_map/ppermute | solution.py:511
  46.8 9.7 %collective-permute-start.12 = (bf16[192,384]{1,0:T(8,128)(2,1)S(1)}, bf16[192,384]{1,0:T(8,128)(2,1)S(1)}, u32[]{:S(2)}, u32[]{:S(2)}) collective-permute-start(bf16[192,384]{1,0:T(8,128)(2,1)S(1)} %get-tuple-element.149), channel_id=1, source_target_pairs={{0,16},{4,20},{8,24},{12,28},{16,0},{20,4},{24,8},{28,12},{1,17},{... | collective-permute-start | bytes 442376 | tf_op jit(solution)/shard_map/ppermute | solution.py:511
  51.6 6.1 %collective-permute-start.13 = (bf16[192,384]{1,0:T(8,128)(2,1)S(1)}, bf16[192,384]{1,0:T(8,128)(2,1)S(1)}, u32[]{:S(2)}, u32[]{:S(2)}) collective-permute-start(bf16[192,384]{1,0:T(8,128)(2,1)S(1)} %get-tuple-element.150), channel_id=1, source_target_pairs={{0,20},{4,16},{8,28},{12,24},{16,4},{20,0},{24,12},{28,8},{1,21},{... | collective-permute-start | bytes 442376 | tf_op jit(solution)/shard_map/ppermute | solution.py:511
  54.0 7.5 %collective-permute-start.14 = (bf16[192,384]{1,0:T(8,128)(2,1)S(1)}, bf16[192,384]{1,0:T(8,128)(2,1)S(1)}, u32[]{:S(2)}, u32[]{:S(2)}) collective-permute-start(bf16[192,384]{1,0:T(8,128)(2,1)S(1)} %get-tuple-element.151), channel_id=1, source_target_pairs={{0,24},{4,28},{8,16},{12,20},{16,8},{20,12},{24,0},{28,4},{1,25},{... | collective-permute-start | bytes 442376 | tf_op jit(solution)/shard_map/ppermute | solution.py:511
  56.5 7.4 %collective-permute-start.15 = (bf16[192,384]{1,0:T(8,128)(2,1)S(1)}, bf16[192,384]{1,0:T(8,128)(2,1)S(1)}, u32[]{:S(2)}, u32[]{:S(2)}) collective-permute-start(bf16[192,384]{1,0:T(8,128)(2,1)S(1)} %get-tuple-element.152), channel_id=1, source_target_pairs={{0,28},{4,24},{8,20},{12,16},{16,12},{20,8},{24,4},{28,0},{1,29},{... | collective-permute-start | bytes 442376 | tf_op jit(solution)/shard_map/ppermute | solution.py:511
  57.7 6.2 %collective-permute-start.9 = (bf16[192,384]{1,0:T(8,128)(2,1)S(1)}, bf16[192,384]{1,0:T(8,128)(2,1)S(1)}, u32[]{:S(2)}, u32[]{:S(2)}) collective-permute-start(bf16[192,384]{1,0:T(8,128)(2,1)S(1)} %get-tuple-element.146), channel_id=1, source_target_pairs={{0,4},{4,0},{8,12},{12,8},{16,20},{20,16},{24,28},{28,24},{1,5},{5... | collective-permute-start | bytes 442376 | tf_op jit(solution)/shard_map/ppermute | solution.py:511
  69.2 43.8 %collective-permute-start.18 = (bf16[720,1024]{1,0:T(8,128)(2,1)S(1)}, bf16[720,1024]{1,0:T(8,128)(2,1)S(1)}, u32[]{:S(2)}, u32[]{:S(2)}) collective-permute-start(bf16[720,1024]{1,0:T(8,128)(2,1)S(1)} %pad_maximum_fusion.refs_0_), channel_id=1, source_target_pairs={{0,8},{4,12},{8,0},{12,4},{16,24},{20,28},{24,16},{28,20},{1,9},{5... | collective-permute-start | bytes 4423688 | tf_op jit(solution)/shard_map/ppermute | solution.py:511
  70.6 42.4 %collective-permute-start.19 = (bf16[720,1024]{1,0:T(8,128)(2,1)S(1)}, bf16[720,1024]{1,0:T(8,128)(2,1)S(1)}, u32[]{:S(2)}, u32[]{:S(2)}) collective-permute-start(bf16[720,1024]{1,0:T(8,128)(2,1)S(1)} %pad_maximum_fusion.refs_0_), channel_id=1, source_target_pairs={{0,16},{4,20},{8,24},{12,28},{16,0},{20,4},{24,8},{28,12},{1,17},{... | collective-permute-start | bytes 4423688 | tf_op jit(solution)/shard_map/ppermute | solution.py:511
  72.1 2.3 collective-permute-start.23
  74.3 18.0 %collective-permute-start.17 = (bf16[768,384]{1,0:T(8,128)(2,1)S(1)}, bf16[768,384]{1,0:T(8,128)(2,1)S(1)}, u32[]{:S(2)}, u32[]{:S(2)}) collective-permute-start(bf16[768,384]{1,0:T(8,128)(2,1)S(1)} %shard_map.88.refs_1_), channel_id=1, source_target_pairs={{0,1},{1,2},{2,3},{3,0},{4,5},{5,6},{6,7},{7,4},{8,9},{9,10},{10,1... | collective-permute-start | bytes 1769480 | tf_op jit(solution)/shard_map/ppermute | solution.py:518
  74.4 38.6 %collective-permute-start.16 = (bf16[768,640]{1,0:T(8,128)(2,1)S(1)}, bf16[768,640]{1,0:T(8,128)(2,1)S(1)}, u32[]{:S(2)}, u32[]{:S(2)}) collective-permute-start(bf16[768,640]{1,0:T(8,128)(2,1)S(1)} %collective-permute-done.8.refs_0_), channel_id=1, source_target_pairs={{0,1},{1,2},{2,3},{3,0},{4,5},{5,6},{6,7},{7,4},{8,9},{9,10},{10,1... | collective-permute-start | bytes 2949128 | tf_op jit(solution)/shard_map/ppermute | solution.py:518
  75.6 37.3 %collective-permute-start.22 = (bf16[768,640]{1,0:T(8,128)(2,1)S(1)}, bf16[768,640]{1,0:T(8,128)(2,1)S(1)}, u32[]{:S(2)}, u32[]{:S(2)}) collective-permute-start(bf16[768,640]{1,0:T(8,128)(2,1)S(1)} %collective-permute-done.8.refs_0_), channel_id=1, source_target_pairs={{0,4},{4,0},{8,12},{12,8},{16,20},{20,16},{24,28},{28,24},{1,5},{5... | collective-permute-start | bytes 2949128 | tf_op jit(solution)/shard_map/ppermute | solution.py:511
  92.3 2.0 collective-permute-start.21
  113.0 37.9 %collective-permute-start.24 = (bf16[768,640]{1,0:T(8,128)(2,1)S(1)}, bf16[768,640]{1,0:T(8,128)(2,1)S(1)}, u32[]{:S(2)}, u32[]{:S(2)}) collective-permute-start(bf16[768,640]{1,0:T(8,128)(2,1)S(1)} %collective-permute-done.16.refs_0_), channel_id=1, source_target_pairs={{0,1},{1,2},{2,3},{3,0},{4,5},{5,6},{6,7},{7,4},{8,9},{9,10},{10,1... | collective-permute-start | bytes 2949128 | tf_op jit(solution)/shard_map/ppermute | solution.py:518
  113.1 18.2 %collective-permute-start.27 = (bf16[720,512]{1,0:T(8,128)(2,1)S(1)}, bf16[720,512]{1,0:T(8,128)(2,1)S(1)}, u32[]{:S(2)}, u32[]{:S(2)}) collective-permute-start(bf16[720,512]{1,0:T(8,128)(2,1)S(1)} %slice.6), channel_id=1, source_target_pairs={{0,16},{4,20},{8,24},{12,28},{16,0},{20,4},{24,8},{28,12},{1,17},{... | collective-permute-start | bytes 2211848 | tf_op jit(solution)/shard_map/ppermute | solution.py:511
  113.8 17.9 %collective-permute-start.28 = (bf16[720,512]{1,0:T(8,128)(2,1)S(1)}, bf16[720,512]{1,0:T(8,128)(2,1)S(1)}, u32[]{:S(2)}, u32[]{:S(2)}) collective-permute-start(bf16[720,512]{1,0:T(8,128)(2,1)S(1)} %slice.7), channel_id=1, source_target_pairs={{0,8},{4,12},{8,0},{12,4},{16,24},{20,28},{24,16},{28,20},{1,9},{5... | collective-permute-start | bytes 2211848 | tf_op jit(solution)/shard_map/ppermute | solution.py:511
  114.5 29.2 %collective-permute-start.26 = (bf16[768,384]{1,0:T(8,128)(2,1)S(1)}, bf16[768,384]{1,0:T(8,128)(2,1)S(1)}, u32[]{:S(2)}, u32[]{:S(2)}) collective-permute-start(bf16[768,384]{1,0:T(8,128)(2,1)S(1)} %collective-permute-done.17.refs_1_), channel_id=1, source_target_pairs={{0,4},{4,0},{8,12},{12,8},{16,20},{20,16},{24,28},{28,24},{1,5},{5... | collective-permute-start | bytes 1769480 | tf_op jit(solution)/shard_map/ppermute | solution.py:511
  114.5 36.4 %collective-permute-start.25 = (bf16[768,384]{1,0:T(8,128)(2,1)S(1)}, bf16[768,384]{1,0:T(8,128)(2,1)S(1)}, u32[]{:S(2)}, u32[]{:S(2)}) collective-permute-start(bf16[768,384]{1,0:T(8,128)(2,1)S(1)} %collective-permute-done.17.refs_1_), channel_id=1, source_target_pairs={{0,1},{1,2},{2,3},{3,0},{4,5},{5,6},{6,7},{7,4},{8,9},{9,10},{10,1... | collective-permute-start | bytes 1769480 | tf_op jit(solution)/shard_map/ppermute | solution.py:518
  131.3 20.1 %collective-permute-start.31 = (bf16[768,640]{1,0:T(8,128)(2,1)S(1)}, bf16[768,640]{1,0:T(8,128)(2,1)S(1)}, u32[]{:S(2)}, u32[]{:S(2)}) collective-permute-start(bf16[768,640]{1,0:T(8,128)(2,1)S(1)} %collective-permute-done.16.refs_0_), channel_id=1, source_target_pairs={{0,4},{4,0},{8,12},{12,8},{16,20},{20,16},{24,28},{28,24},{1,5},{5... | collective-permute-start | bytes 2949128 | tf_op jit(solution)/shard_map/ppermute | solution.py:511
  150.9 8.9 %collective-permute-start.30 = (bf16[768,640]{1,0:T(8,128)(2,1)S(1)}, bf16[768,640]{1,0:T(8,128)(2,1)S(1)}, u32[]{:S(2)}, u32[]{:S(2)}) collective-permute-start(bf16[768,640]{1,0:T(8,128)(2,1)S(1)} %collective-permute-done.24.refs_0_), channel_id=1, source_target_pairs={{0,4},{4,0},{8,12},{12,8},{16,20},{20,16},{24,28},{28,24},{1,5},{5... | collective-permute-start | bytes 2949128 | tf_op jit(solution)/shard_map/ppermute | solution.py:511
  150.9 3.4 %collective-permute-start.32 = (bf16[768,384]{1,0:T(8,128)(2,1)S(1)}, bf16[768,384]{1,0:T(8,128)(2,1)S(1)}, u32[]{:S(2)}, u32[]{:S(2)}) collective-permute-start(bf16[768,384]{1,0:T(8,128)(2,1)S(1)} %collective-permute-done.25.refs_1_), channel_id=1, source_target_pairs={{0,4},{4,0},{8,12},{12,8},{16,20},{20,16},{24,28},{28,24},{1,5},{5... | collective-permute-start | bytes 1769480 | tf_op jit(solution)/shard_map/ppermute | solution.py:511
  151.4 17.0 %collective-permute-start.29 = (bf16[768,384]{1,0:T(8,128)(2,1)S(1)}, bf16[768,384]{1,0:T(8,128)(2,1)S(1)}, u32[]{:S(2)}, u32[]{:S(2)}) collective-permute-start(bf16[768,384]{1,0:T(8,128)(2,1)S(1)} %collective-permute-done.25.refs_1_), channel_id=1, source_target_pairs={{0,1},{1,2},{2,3},{3,0},{4,5},{5,6},{6,7},{7,4},{8,9},{9,10},{10,1... | collective-permute-start | bytes 1769480 | tf_op jit(solution)/shard_map/ppermute | solution.py:518
  168.4 2.0 collective-permute-start.33
  176.4 1.3 collective-permute-start.34
  178.2 4.8 %collective-permute-start.35 = (f32[8,1536]{1,0:T(8,128)S(1)}, f32[8,1536]{1,0:T(8,128)S(1)}, u32[]{:S(2)}, u32[]{:S(2)}) collective-permute-start(f32[8,1536]{1,0:T(8,128)S(1)} %shard_map.95.refs_2_), channel_id=1, source_target_pairs={{0,1},{1,0},{2,3},{3,2},{4,5},{5,4},{6,7},{7,6},{8,9},{9,8},{10,11... | collective-permute-start | bytes 147464 | tf_op jit(solution)/shard_map/ppermute | solution.py:585
  178.3 7.4 %collective-permute-start.36 = (f32[8,1536]{1,0:T(8,128)S(1)}, f32[8,1536]{1,0:T(8,128)S(1)}, u32[]{:S(2)}, u32[]{:S(2)}) collective-permute-start(f32[8,1536]{1,0:T(8,128)S(1)} %shard_map.95.refs_2_), channel_id=1, source_target_pairs={{0,2},{1,3},{2,0},{3,1},{4,6},{5,7},{6,4},{7,5},{8,10},{9,11},{10,... | collective-permute-start | bytes 147464 | tf_op jit(solution)/shard_map/ppermute | solution.py:585
  179.1 6.6 %collective-permute-start.37 = (f32[8,1536]{1,0:T(8,128)S(1)}, f32[8,1536]{1,0:T(8,128)S(1)}, u32[]{:S(2)}, u32[]{:S(2)}) collective-permute-start(f32[8,1536]{1,0:T(8,128)S(1)} %shard_map.95.refs_2_), channel_id=1, source_target_pairs={{0,3},{1,2},{2,1},{3,0},{4,7},{5,6},{6,5},{7,4},{8,11},{9,10},{10,... | collective-permute-start | bytes 147464 | tf_op jit(solution)/shard_map/ppermute | solution.py:585
  190.0 26.4 %collective-permute-start.38 = (bf16[720,512]{1,0:T(8,128)(2,1)S(1)}, bf16[720,512]{1,0:T(8,128)(2,1)S(1)}, u32[]{:S(2)}, u32[]{:S(2)}) collective-permute-start(bf16[720,512]{1,0:T(8,128)(2,1)S(1)} %get-tuple-element.193), channel_id=1, source_target_pairs={{0,8},{4,12},{8,0},{12,4},{16,24},{20,28},{24,16},{28,20},{1,9},{5... | collective-permute-start | bytes 2211848 | tf_op jit(solution)/shard_map/ppermute | solution.py:511
  190.5 25.8 %collective-permute-start.39 = (bf16[720,512]{1,0:T(8,128)(2,1)S(1)}, bf16[720,512]{1,0:T(8,128)(2,1)S(1)}, u32[]{:S(2)}, u32[]{:S(2)}) collective-permute-start(bf16[720,512]{1,0:T(8,128)(2,1)S(1)} %get-tuple-element.194), channel_id=1, source_target_pairs={{0,16},{4,20},{8,24},{12,28},{16,0},{20,4},{24,8},{28,12},{1,17},{... | collective-permute-start | bytes 2211848 | tf_op jit(solution)/shard_map/ppermute | solution.py:511
  191.3 17.6 %collective-permute-start.40 = (bf16[64,720]{1,0:T(8,128)(2,1)S(1)}, bf16[64,720]{1,0:T(8,128)(2,1)S(1)}, u32[]{:S(2)}, u32[]{:S(2)}) collective-permute-start(bf16[64,720]{1,0:T(8,128)(2,1)S(1)} %get-tuple-element.195.mine_ref), channel_id=1, source_target_pairs={{0,8},{4,12},{8,0},{12,4},{16,24},{20,28},{24,16},{28,20},{1,9},{5... | collective-permute-start | bytes 276488 | tf_op jit(solution)/shard_map/ppermute | solution.py:511
  209.5 6.9 %collective-permute-start.41 = (bf16[64,720]{1,0:T(8,128)(2,1)S(1)}, bf16[64,720]{1,0:T(8,128)(2,1)S(1)}, u32[]{:S(2)}, u32[]{:S(2)}) collective-permute-start(bf16[64,720]{1,0:T(8,128)(2,1)S(1)} %shard_map.99), channel_id=1, source_target_pairs={{0,16},{4,20},{8,24},{12,28},{16,0},{20,4},{24,8},{28,12},{1,17},{... | collective-permute-start | bytes 276488 | tf_op jit(solution)/shard_map/ppermute | solution.py:511
  218.1 19.7 %collective-permute-start.43 = (bf16[720,512]{1,0:T(8,128)(2,1)}, bf16[720,512]{1,0:T(8,128)(2,1)}, u32[]{:S(2)}, u32[]{:S(2)}) collective-permute-start(bf16[720,512]{1,0:T(8,128)(2,1)} %get-tuple-element.217), channel_id=1, source_target_pairs={{0,16},{4,12},{8,24},{12,4},{16,0},{20,28},{24,8},{28,20},{1,17},{... | collective-permute-start | bytes 2211848 | tf_op jit(solution)/shard_map/ppermute | solution.py:515
  219.1 19.7 %collective-permute-start.42 = (bf16[720,512]{1,0:T(8,128)(2,1)}, bf16[720,512]{1,0:T(8,128)(2,1)}, u32[]{:S(2)}, u32[]{:S(2)}) collective-permute-start(bf16[720,512]{1,0:T(8,128)(2,1)} %get-tuple-element.207), channel_id=1, source_target_pairs={{0,8},{4,20},{8,0},{12,28},{16,24},{20,4},{24,16},{28,12},{1,9},{5... | collective-permute-start | bytes 2211848 | tf_op jit(solution)/shard_map/ppermute | solution.py:515
  219.6 1.7 collective-permute-start.47
  219.7 28.2 %collective-permute-start.46 = (bf16[720,512]{1,0:T(8,128)(2,1)}, bf16[720,512]{1,0:T(8,128)(2,1)}, u32[]{:S(2)}, u32[]{:S(2)}) collective-permute-start(bf16[720,512]{1,0:T(8,128)(2,1)} %get-tuple-element.218), channel_id=1, source_target_pairs={{0,12},{4,16},{8,4},{12,24},{16,28},{20,0},{24,20},{28,8},{1,13},{... | collective-permute-start | bytes 2211848 | tf_op jit(solution)/shard_map/ppermute | solution.py:515
  221.3 26.6 %collective-permute-start.44 = (bf16[720,512]{1,0:T(8,128)(2,1)S(1)}, bf16[720,512]{1,0:T(8,128)(2,1)}, u32[]{:S(2)}, u32[]{:S(2)}) collective-permute-start(bf16[720,512]{1,0:T(8,128)(2,1)S(1)} %get-tuple-element.211), channel_id=1, source_target_pairs={{0,4},{4,0},{8,12},{12,8},{16,20},{20,16},{24,28},{28,24},{1,5},{5... | collective-permute-start | bytes 2211848 | tf_op jit(solution)/shard_map/ppermute | solution.py:511
  221.3 27.1 %collective-permute-start.45 = (bf16[720,512]{1,0:T(8,128)(2,1)S(1)}, bf16[720,512]{1,0:T(8,128)(2,1)}, u32[]{:S(2)}, u32[]{:S(2)}) collective-permute-start(bf16[720,512]{1,0:T(8,128)(2,1)S(1)} %get-tuple-element.212), channel_id=1, source_target_pairs={{0,20},{4,8},{8,28},{12,0},{16,4},{20,24},{24,12},{28,16},{1,21},{... | collective-permute-start | bytes 2211848 | tf_op jit(solution)/shard_map/ppermute | solution.py:515

commit v8 on v7

--- a/solution.py
+++ b/solution.py
@@ -457,7 +457,9 @@
     whole = lambda shape: pl.BlockSpec(shape, lambda j, m: (0, 0))
     full_spec = pl.BlockSpec((rows, width), lambda j, m: (0, m[offset + j]))
     out_specs = [whole((count, width))] * steps
-    out_shape = [sds((count, width), F32 if kind == "rest" else BF16)] * steps
+    kept = steps // 2 if kind == "rest" else 0
+    types = [BF16] * (steps - kept) + [F32] * kept
+    out_shape = [sds((count, width), dtype) for dtype in types]
     if kind == "first":
         operands = [shifted, *stats, *hots, full]
         in_specs = [whole(shifted.shape)] + [whole(stats[0].shape)] * 5
@@ -473,7 +475,7 @@
         in_specs,
         out_specs,
         out_shape,
-        room=22 if kind == "first" else 18,
+        room=22 if kind == "first" else 28,
         flops=2 * count * rows * width * steps,
         moved=2 * rows * width * steps + 4 * count * (rows + width * steps),
     )(meta, *operands)
@@ -541,7 +543,7 @@
     share_a, hot, pick, wide = unpack_first(meta, recv_a, ctf_table, inv, width, chunk_a)
     share_a, send_b = together((share_a, send_b))
     a1, recv_b = onward(share_a), exchange(send_b)
-    a1, recv_b, near = together((a1, recv_b, near))
+    recv_b, near = together((recv_b, near))
     by_x, by_y = across(near, 2), across(near, 4)
     share_b = unpack_next(meta, pick, wide, recv_b, ctf_table, inv, width, chunk_b)
     a2, b1 = onward(a1), onward(share_b)
@@ -589,14 +591,11 @@
     )
     mass_x = across(mass, 2)
     got_x, got_y = across(to_x, 2), across(to_y, 4)
-    a_sum, b_sum, keep = class_part(meta, "rest", 7, 3, full, post)
-    mass_x, post, keep = together((mass_x, post, keep))
+    six = class_part(meta, "rest", 4, 6, full, post)
+    got_x, got_y, six, mass_x = together((got_x, got_y, six, mass_x))
+    send_c, send_d, give, a_sum, b_sum, keep = six
     mass = add_pair(meta, mass, mass_x)
     mass_y = across(mass, 4)
-    send_c, send_d, give = class_part(meta, "next", 4, 3, full, post)
-    got_x, got_y, send_c, send_d, a_sum, b_sum, keep, give, mass, mass_y = together(
-        (got_x, got_y, send_c, send_d, a_sum, b_sum, keep, give, mass, mass_y)
-    )
     got_c, got_d = by_core(send_c, 2, 4), by_core(send_d, 5, 3)
     down, left = got_x.astype(F32), got_y.astype(F32)
     message_a = (a_sum + jnp.where(even, down, left)).astype(BF16)

time: 254 us -> 247 us (0.972)
  waiting for transfers between devices: 136 us -> 126 us
  starting transfers between devices: 36 us -> 39.6 us
    ppermute x6, waiting for transfers between devices: 46.5 us -> 23.4 us  [onward(): lax.ppermute(value, 'rot', [(i, (i + 1) % turns) for i in range(turns)])]
    ppermute x35, waiting for transfers between devices: 63.6 us -> 74.9 us  [across(): return lax.ppermute(value, 'dom', [(i, i ^ apart) for i in range(dom)])]
    pallas_call x3 -> x2, Pallas kernels: 14.9 us -> 14.4 us  [class_part(): call(functools.partial(class_body, kind, steps), (steps,), in_specs, out_...]
  transfers between devices with their start and end apart: 48 -> 48, of which waited for: 26 -> 27; matrix products, arithmetic and copies ran while one was open for 2% -> 3% of each run, Pallas kernels for 21% -> 21%
where the time goes in v8:
time: 247 us; the launch traced here: 246 us
  waiting for transfers between devices  126 us (51%)
  Pallas kernels  67.9 us (27%)
  starting transfers between devices  39.6 us (16%)
  other arithmetic  8.83 us (4%)
  local copies, waits for them, and re-layouts  2.85 us (1%)
    ppermute x35, waiting for transfers between devices, across(): return lax.ppermute(value, 'dom', [(i, i ^ apart) for i in range(dom)])  74.9 us
    pallas_call x5, Pallas kernels, score(): call(functools.partial(score_body, parts, used, first, last), (2 * half,)...  27.3 us
    ppermute x35, starting transfers between devices, across(): return lax.ppermute(value, 'dom', [(i, i ^ apart) for i in range(dom)])  26.1 us
    ppermute x4, waiting for transfers between devices, by_core(): return lax.ppermute(value, 'dom', pairs)  23.5 us
    ppermute x6, waiting for transfers between devices, onward(): lax.ppermute(value, 'rot', [(i, (i + 1) % turns) for i in range(turns)])  23.4 us
    pallas_call x2, Pallas kernels, class_part(): call(functools.partial(class_body, kind, steps), (steps,), in_specs, out_...  14.4 us
    pallas_call x1, Pallas kernels, pack_first(): call(functools.partial(pack_first_body, dom, hold // 2, cap), (1,), [pl.B...  7.28 us
    pallas_call x1, Pallas kernels, energy(): call(functools.partial(energy_body, bins, count), (count,), [pl.BlockSpec...  6.84 us
  transfers between devices with their start and end apart: 48, of which 27 were waited for; matrix products, arithmetic and copies ran while one was open for 3% of the time, Pallas kernels for 21%

profile of v8, /device:TPU:0, one launch (start us, length us, event | category | flops | bytes accessed | tf_op | source)
XLA Modules:
  0.0 245.7 jit_solution(1165127184095117186)
XLA Ops:
  1.2 0.7 copy-done.2
  1.9 0.7 copy-done.3
  2.6 7.3 %shard_map.85 = (bf16[208,640]{1,0:T(8,128)(2,1)S(1)}, bf16[208,640]{1,0:T(8,128)(2,1)S(1)}, bf16[208,640]{1,0:T(8,128)(2,1)S(1)}, bf16[208,640]{1,0:T(8,128)(2,...) custom-call(s32[10]{0:T(128)S(1)} %stack.43.meta, ...), custom_call_target="tpu_custom_call" | custom-call | flops 188743680 | bytes 245760 | tf_op jit(solution)/shard_map/pallas_call | solution.py:130
  10.0 2.9 %collective-permute-start.1 = (bf16[208,640]{1,0:T(8,128)(2,1)S(1)}, bf16[208,640]{1,0:T(8,128)(2,1)S(1)}, u32[]{:S(2)}, u32[]{:S(2)}) collective-permute-start(bf16[208,640]{1,0:T(8,128)(2,1)S(1)} %get-tuple-element.107), channel_id=1, source_target_pairs={{0,8},{4,12},{8,0},{12,4},{16,24},{20,28},{24,16},{28,20},{1,9},{5... | collective-permute-start | bytes 798728 | tf_op jit(solution)/shard_map/ppermute | solution.py:513
  13.0 1.5 collective-permute-start.3
  14.5 4.4 %shard_map.86 = (bf16[192,384]{1,0:T(8,128)(2,1)S(1)}, bf16[192,384]{1,0:T(8,128)(2,1)S(1)}, bf16[192,384]{1,0:T(8,128)(2,1)S(1)}, bf16[192,384]{1,0:T(8,128)(2,...) custom-call(s32[10]{0:T(128)S(1)} %stack.43.meta, ...), custom_call_target="tpu_custom_call" | custom-call | flops 113246208 | bytes 147456 | tf_op jit(solution)/shard_map/pallas_call | solution.py:150
  19.3 0.8 collective-permute-done.1.refs_2_
  20.2 3.0 %collective-permute-start.5 = (bf16[208,640]{1,0:T(8,128)(2,1)S(1)}, bf16[208,640]{1,0:T(8,128)(2,1)S(1)}, u32[]{:S(2)}, u32[]{:S(2)}) collective-permute-start(bf16[208,640]{1,0:T(8,128)(2,1)S(1)} %get-tuple-element.111), channel_id=1, source_target_pairs={{0,24},{4,28},{8,16},{12,20},{16,8},{20,12},{24,0},{28,4},{1,25},{... | collective-permute-start | bytes 798728 | tf_op jit(solution)/shard_map/ppermute | solution.py:513
  23.2 1.2 constant_dynamic-slice_fusion
  24.6 0.9 collective-permute-done.2.refs_3_
  25.5 13.3 %collective-permute-done.4.refs_5_ = bf16[208,640]{1,0:T(8,128)(2,1)S(1)} collective-permute-done((bf16[208,640]{1,0:T(8,128)(2,1)S(1)}, bf16[208,640]{1,0:T(8,128)(2,1)S(1)}, u32[]{:S(2)}, u32[]{:S(2)}) %collective-permute-start.4) | collective-permute-done | bytes 266272 | tf_op jit(solution)/shard_map/ppermute | solution.py:513
  38.7 4.4 %shard_map.87 = (bf16[768,640]{1,0:T(8,128)(2,1)S(1)}, bf16[192,768]{1,0:T(8,128)(2,1)S(1)}, bf16[768,1536]{1,0:T(8,128)(2,1)S(1)}, bf16[768,192]{1,0:T(8,128)(2,1)S(1)}) custom-call(s32[10]{0:T(128)S(1)} %stack.43.meta, bf16[208,640]{1,0:T(8,128)(2,1)S(1)} %get-tuple-element.122.refs_0_, bf16[208,640]{1,0:T(8,128)(2,1)S(1)} %collective-permute-done.refs_1_, ...), custom_call_target="tpu_custom_call" | custom-call | flops 94371840 | bytes 122880 | tf_op jit(solution)/shard_map/pallas_call | solution.py:210
  43.1 1.8 collective-permute-start.8
  45.0 1.5 collective-permute-start.11
  46.8 1.5 collective-permute-start.13
  48.3 3.3 %collective-permute-done.11.refs_2_ = bf16[192,384]{1,0:T(8,128)(2,1)S(1)} collective-permute-done((bf16[192,384]{1,0:T(8,128)(2,1)S(1)}, bf16[192,384]{1,0:T(8,128)(2,1)S(1)}, u32[]{:S(2)}, u32[]{:S(2)}) %collective-permute-start.11) | collective-permute-done | bytes 147488 | tf_op jit(solution)/shard_map/ppermute | solution.py:513
  52.1 1.9 collective-permute-done.12.refs_3_
  54.0 2.5 %collective-permute-start.15 = (bf16[192,384]{1,0:T(8,128)(2,1)S(1)}, bf16[192,384]{1,0:T(8,128)(2,1)S(1)}, u32[]{:S(2)}, u32[]{:S(2)}) collective-permute-start(bf16[192,384]{1,0:T(8,128)(2,1)S(1)} %get-tuple-element.146), channel_id=1, source_target_pairs={{0,24},{4,28},{8,16},{12,20},{16,8},{20,12},{24,0},{28,4},{1,25},{... | collective-permute-start | bytes 442376 | tf_op jit(solution)/shard_map/ppermute | solution.py:513
  56.7 1.0 collective-permute-done.14.refs_5_
  57.7 3.8 %collective-permute-done.15.refs_6_ = bf16[192,384]{1,0:T(8,128)(2,1)S(1)} collective-permute-done((bf16[192,384]{1,0:T(8,128)(2,1)S(1)}, bf16[192,384]{1,0:T(8,128)(2,1)S(1)}, u32[]{:S(2)}, u32[]{:S(2)}) %collective-permute-start.15) | collective-permute-done | bytes 147488 | tf_op jit(solution)/shard_map/ppermute | solution.py:513
  61.5 2.4 collective-permute-done.16.refs_7_
  63.9 2.2 shard_map.88.refs_1_
  66.1 1.6 collective-permute-start.17
  67.8 1.4 collective-permute-start.18
  69.2 1.7 collective-permute-start.19
  70.8 12.9 %collective-permute-done.17.refs_1_ = bf16[768,384]{1,0:T(8,128)(2,1)S(1)} collective-permute-done((bf16[768,384]{1,0:T(8,128)(2,1)S(1)}, bf16[768,384]{1,0:T(8,128)(2,1)S(1)}, u32[]{:S(2)}, u32[]{:S(2)}) %collective-permute-start.17) | collective-permute-done | bytes 589856 | tf_op jit(solution)/shard_map/ppermute | solution.py:520
  84.2 2.0 collective-permute-done.20.refs_2_
  86.3 16.2 %collective-permute-done.18.refs_1_ = bf16[720,1024]{1,0:T(8,128)(2,1)S(1)} collective-permute-done((bf16[720,1024]{1,0:T(8,128)(2,1)S(1)}, bf16[720,1024]{1,0:T(8,128)(2,1)S(1)}, u32[]{:S(2)}, u32[]{:S(2)}) %collective-permute-start.18) | collective-permute-done | bytes 1474592 | tf_op jit(solution)/shard_map/ppermute | solution.py:513
  102.5 1.1 collective-permute-done.19.refs_2_
  103.6 6.1 %collective-permute-done.9.refs_0_ = bf16[768,640]{1,0:T(8,128)(2,1)S(1)} collective-permute-done((bf16[768,640]{1,0:T(8,128)(2,1)S(1)}, bf16[768,640]{1,0:T(8,128)(2,1)S(1)}, u32[]{:S(2)}, u32[]{:S(2)}) %collective-permute-start.9) | collective-permute-done | bytes 983072 | tf_op jit(solution)/shard_map/ppermute | solution.py:520
  109.8 1.6 collective-permute-start.27
  111.4 1.6 collective-permute-start.28
  113.1 14.4 %collective-permute-done.27.refs_3_ = bf16[720,512]{1,0:T(8,128)(2,1)S(1)} collective-permute-done((bf16[720,512]{1,0:T(8,128)(2,1)S(1)}, bf16[720,512]{1,0:T(8,128)(2,1)S(1)}, u32[]{:S(2)}, u32[]{:S(2)}) %collective-permute-start.27) | collective-permute-done | bytes 737312 | tf_op jit(solution)/shard_map/ppermute | solution.py:513
  127.5 1.4 collective-permute-done.28.refs_4_
  128.8 6.8 %shard_map.89 = (bf16[720,4096]{1,0:T(8,128)(2,1)S(1)}, bf16[720,192]{1,0:T(8,128)(2,1)S(1)}) custom-call(s32[10]{0:T(128)S(1)} %stack.43.meta, bf16[720,1024]{1,0:T(8,128)(2,1)S(1)} %pad_maximum_fusion.refs_0_, bf16[720,1024]{1,0:T(8,128)(2,1)S(1)} %collective-permute-done.18.refs_1_, bf16[720,1024]{1,0:T(8,128)(2,1)S(1)} %collective-permute-done.19.refs_2_, ...), custom_call_target="tpu_custom_call" | custom-call | flops 283115520 | bytes 737280 | tf_op jit(solution)/shard_map/pallas_call | solution.py:280
  135.7 5.1 %shard_map.90 = (f32[720,1536]{1,0:T(8,128)S(1)}, bf16[1536,4096]{1,0:T(8,128)(2,1)S(1)}) custom-call(s32[10]{0:T(128)S(1)} %stack.43.meta, bf16[768,640]{1,0:T(8,128)(2,1)S(1)} %get-tuple-element.139.refs_0_, bf16[768,384]{1,0:T(8,128)(2,1)S(1)} %shard_map.88.refs_1_, bf16[768,640]{1,0:T(8,128)(2,1)S(1)} %collective-permute-done.20.refs_2_, ...), custom_call_target="tpu_custom_call" | custom-call | flops 141557760 | bytes 946176 | tf_op jit(solution)/shard_map/pallas_call | solution.py:384
  140.8 6.3 %shard_map.91 = (f32[720,1536]{1,0:T(8,128)S(1)}, bf16[1536,4096]{1,0:T(8,128)(2,1)S(1)}) custom-call(s32[10]{0:T(128)S(1)} %stack.43.meta, bf16[768,640]{1,0:T(8,128)(2,1)S(1)} %collective-permute-done.8.refs_0_, bf16[768,384]{1,0:T(8,128)(2,1)S(1)} %collective-permute-done.17.refs_1_, ...), custom_call_target="tpu_custom_call", output_to_operand_aliasing={{0}: (6, {}), {1}: (7, {})} | custom-call | flops 141557760 | bytes 946176 | tf_op jit(solution)/shard_map/pallas_call | solution.py:384
  147.8 2.9 %collective-permute-done.32.refs_3_ = bf16[768,384]{1,0:T(8,128)(2,1)S(1)} collective-permute-done((bf16[768,384]{1,0:T(8,128)(2,1)S(1)}, bf16[768,384]{1,0:T(8,128)(2,1)S(1)}, u32[]{:S(2)}, u32[]{:S(2)}) %collective-permute-start.32) | collective-permute-done | bytes 589856 | tf_op jit(solution)/shard_map/ppermute | solution.py:513
  150.7 5.5 %shard_map.92 = (f32[720,1536]{1,0:T(8,128)S(1)}, bf16[1536,4096]{1,0:T(8,128)(2,1)S(1)}) custom-call(s32[10]{0:T(128)S(1)} %stack.43.meta, bf16[768,640]{1,0:T(8,128)(2,1)S(1)} %collective-permute-done.9.refs_0_, bf16[768,384]{1,0:T(8,128)(2,1)S(1)} %collective-permute-done.25.refs_1_, ...), custom_call_target="tpu_custom_call", output_to_operand_aliasing={{0}: (6, {}), {1}: (7, {})} | custom-call | flops 141557760 | bytes 946176 | tf_op jit(solution)/shard_map/pallas_call | solution.py:384
  156.1 4.4 %shard_map.93.refs_5_ = f32[720,1536]{1,0:T(8,128)S(1)} custom-call(s32[10]{0:T(128)S(1)} %stack.43.meta, bf16[768,640]{1,0:T(8,128)(2,1)S(1)} %collective-permute-done.24.refs_0_, bf16[768,640]{1,0:T(8,128)(2,1)S(1)} %collective-permute-done.30.refs_1_.refs_2_, ...), custom_call_target="tpu_custom_call", output_to_operand_aliasing={{}: (4, {})} | custom-call | flops 141557760 | bytes 946176 | tf_op jit(solution)/shard_map/pallas_call | solution.py:384
  160.5 4.3 %collective-permute-done.29.refs_1_ = bf16[768,384]{1,0:T(8,128)(2,1)S(1)} collective-permute-done((bf16[768,384]{1,0:T(8,128)(2,1)S(1)}, bf16[768,384]{1,0:T(8,128)(2,1)S(1)}, u32[]{:S(2)}, u32[]{:S(2)}) %collective-permute-start.29) | collective-permute-done | bytes 589856 | tf_op jit(solution)/shard_map/ppermute | solution.py:520
  164.9 2.0 collective-permute-done.33.refs_3_
  166.9 6.0 %shard_map.94 = (f32[720,1536]{1,0:T(8,128)S(1)}, f32[8,1536]{1,0:T(8,128)S(1)}, bf16[1536,4096]{1,0:T(8,128)(2,1)S(1)}) custom-call(s32[10]{0:T(128)S(1)} %stack.43.meta, bf16[768,640]{1,0:T(8,128)(2,1)S(1)} %collective-permute-done.24.refs_0_, bf16[768,384]{1,0:T(8,128)(2,1)S(1)} %collective-permute-done.29.refs_1_, ...), custom_call_target="tpu_custom_call", output_to_operand_aliasing={{0}: (6, {}), {2}: (7, {})} | custom-call | flops 141557760 | bytes 946176 | tf_op jit(solution)/shard_map/pallas_call | solution.py:384
  173.0 1.1 collective-permute-done.34.other_ref
  174.8 2.3 collective-permute-start.36
  177.1 2.1 collective-permute-start.37
  179.5 1.2 collective-permute-done.36.refs_4_
  180.7 2.3 collective-permute-done.37.refs_5_
  183.0 4.2 %shard_map.96 = (bf16[720,512]{1,0:T(8,128)(2,1)S(1)}, bf16[720,512]{1,0:T(8,128)(2,1)S(1)}, bf16[720,1536]{1,0:T(8,128)(2,1)S(1)}, f32[1,768]{1,0:T(1,128)S(1)}, bf16[64,720]{1,0:T(8,128)(2,1)S(1)}) custom-call(s32[10]{0:T(128)S(1)} %stack.43.meta, f32[720,1536]{1,0:T(8,128)S(1)} %get-tuple-element.184.refs_0_, ...), custom_call_target="tpu_custom_call" | custom-call | flops 141557760 | bytes 657408 | tf_op jit(solution)/shard_map/pallas_call | solution.py:472
  187.2 1.6 collective-permute-start.38
  190.0 10.2 %shard_map.97 = (bf16[720,512]{1,0:T(8,128)(2,1)}, bf16[720,512]{1,0:T(8,128)(2,1)S(1)}, bf16[720,512]{1,0:T(8,128)(2,1)S(1)}, f32[720,512]{1,0:T(8,128)S(1)}, f...) custom-call(s32[10]{0:T(128)S(1)} %stack.43.meta, bf16[720,1536]{1,0:T(8,128)(2,1)S(1)} %get-tuple-element.189.refs_0_, ...), custom_call_target="tpu_custom_call" | custom-call | flops 424673280 | bytes 1419264 | tf_op jit(solution)/shard_map/pallas_call | solution.py:472
  200.2 6.3 %collective-permute-done.40.other_ref = bf16[64,720]{1,0:T(8,128)(2,1)S(1)} collective-permute-done((bf16[64,720]{1,0:T(8,128)(2,1)S(1)}, bf16[64,720]{1,0:T(8,128)(2,1)S(1)}, u32[]{:S(2)}, u32[]{:S(2)}) %collective-permute-start.40) | collective-permute-done | bytes 92192 | tf_op jit(solution)/shard_map/ppermute | solution.py:513
  207.8 1.7 fusion.2
  209.4 1.4 collective-permute-start.42
  210.8 1.6 collective-permute-start.41
  212.7 1.9 collective-permute-start.45
  214.5 0.7 collective-permute-start.44
  215.9 0.9 maximum_select_fusion.1
  216.8 12.4 %collective-permute-done.42 = bf16[720,512]{1,0:T(8,128)(2,1)} collective-permute-done((bf16[720,512]{1,0:T(8,128)(2,1)}, bf16[720,512]{1,0:T(8,128)(2,1)}, u32[]{:S(2)}, u32[]{:S(2)}) %collective-permute-start.42) | collective-permute-done | bytes 737312 | tf_op jit(solution)/shard_map/ppermute | solution.py:517
  229.2 1.4 collective-permute-done.41
  230.6 1.6 convert_add_fusion.1
  232.2 9.7 %collective-permute-done.45 = bf16[720,512]{1,0:T(8,128)(2,1)} collective-permute-done((bf16[720,512]{1,0:T(8,128)(2,1)}, bf16[720,512]{1,0:T(8,128)(2,1)}, u32[]{:S(2)}, u32[]{:S(2)}) %collective-permute-start.45) | collective-permute-done | bytes 737312 | tf_op jit(solution)/shard_map/ppermute | solution.py:517
  241.9 1.8 convert_add_fusion
  243.8 1.9 fusion
  (69 shorter events, 8.1 us)
Async XLA Ops:
  0.6 22.6 %collective-permute-start.7 = (bf16[1440,512]{1,0:T(8,128)(2,1)}, bf16[1440,512]{1,0:T(8,128)(2,1)}, u32[]{:S(2)}, u32[]{:S(2)}) collective-permute-start(bf16[1440,512]{1,0:T(8,128)(2,1)} %param.11), channel_id=1, source_target_pairs={{0,4},{4,0},{8,12},{12,8},{16,20},{20,16},{24,28},{28,24},{1,5},{5... | collective-permute-start | bytes 4423688 | tf_op jit(solution)/shard_map/ppermute | solution.py:513
  1.2 0.7 copy-start.2
  1.9 0.7 copy-start.3
  9.9 9.1 %collective-permute-start = (bf16[208,640]{1,0:T(8,128)(2,1)S(1)}, bf16[208,640]{1,0:T(8,128)(2,1)S(1)}, u32[]{:S(2)}, u32[]{:S(2)}) collective-permute-start(bf16[208,640]{1,0:T(8,128)(2,1)S(1)} %get-tuple-element.106), channel_id=1, source_target_pairs={{0,4},{4,0},{8,12},{12,8},{16,20},{20,16},{24,28},{28,24},{1,5},{5... | collective-permute-start | bytes 798728 | tf_op jit(solution)/shard_map/ppermute | solution.py:513
  10.0 10.1 %collective-permute-start.1 = (bf16[208,640]{1,0:T(8,128)(2,1)S(1)}, bf16[208,640]{1,0:T(8,128)(2,1)S(1)}, u32[]{:S(2)}, u32[]{:S(2)}) collective-permute-start(bf16[208,640]{1,0:T(8,128)(2,1)S(1)} %get-tuple-element.107), channel_id=1, source_target_pairs={{0,8},{4,12},{8,0},{12,4},{16,24},{20,28},{24,16},{28,20},{1,9},{5... | collective-permute-start | bytes 798728 | tf_op jit(solution)/shard_map/ppermute | solution.py:513
  13.0 12.5 %collective-permute-start.2 = (bf16[208,640]{1,0:T(8,128)(2,1)S(1)}, bf16[208,640]{1,0:T(8,128)(2,1)S(1)}, u32[]{:S(2)}, u32[]{:S(2)}) collective-permute-start(bf16[208,640]{1,0:T(8,128)(2,1)S(1)} %get-tuple-element.108), channel_id=1, source_target_pairs={{0,12},{4,8},{8,4},{12,0},{16,28},{20,24},{24,20},{28,16},{1,13},{... | collective-permute-start | bytes 798728 | tf_op jit(solution)/shard_map/ppermute | solution.py:513
  13.0 12.5 %collective-permute-start.3 = (bf16[208,640]{1,0:T(8,128)(2,1)S(1)}, bf16[208,640]{1,0:T(8,128)(2,1)S(1)}, u32[]{:S(2)}, u32[]{:S(2)}) collective-permute-start(bf16[208,640]{1,0:T(8,128)(2,1)S(1)} %get-tuple-element.109), channel_id=1, source_target_pairs={{0,16},{4,20},{8,24},{12,28},{16,0},{20,4},{24,8},{28,12},{1,17},{... | collective-permute-start | bytes 798728 | tf_op jit(solution)/shard_map/ppermute | solution.py:513
  14.5 4.4 %copy-start.4 = (bf16[1440,512]{1,0:T(8,128)(2,1)S(1)}, bf16[1440,512]{1,0:T(8,128)(2,1)}, u32[]{:S(2)}) copy-start(bf16[1440,512]{1,0:T(8,128)(2,1)} %param.11) | copy-start | bytes 4423684
  19.0 19.7 %collective-permute-start.4 = (bf16[208,640]{1,0:T(8,128)(2,1)S(1)}, bf16[208,640]{1,0:T(8,128)(2,1)S(1)}, u32[]{:S(2)}, u32[]{:S(2)}) collective-permute-start(bf16[208,640]{1,0:T(8,128)(2,1)S(1)} %get-tuple-element.110), channel_id=1, source_target_pairs={{0,20},{4,16},{8,28},{12,24},{16,4},{20,0},{24,12},{28,8},{1,21},{... | collective-permute-start | bytes 798728 | tf_op jit(solution)/shard_map/ppermute | solution.py:513
  20.2 18.6 %collective-permute-start.5 = (bf16[208,640]{1,0:T(8,128)(2,1)S(1)}, bf16[208,640]{1,0:T(8,128)(2,1)S(1)}, u32[]{:S(2)}, u32[]{:S(2)}) collective-permute-start(bf16[208,640]{1,0:T(8,128)(2,1)S(1)} %get-tuple-element.111), channel_id=1, source_target_pairs={{0,24},{4,28},{8,16},{12,20},{16,8},{20,12},{24,0},{28,4},{1,25},{... | collective-permute-start | bytes 798728 | tf_op jit(solution)/shard_map/ppermute | solution.py:513
  23.2 15.5 %collective-permute-start.6 = (bf16[208,640]{1,0:T(8,128)(2,1)S(1)}, bf16[208,640]{1,0:T(8,128)(2,1)S(1)}, u32[]{:S(2)}, u32[]{:S(2)}) collective-permute-start(bf16[208,640]{1,0:T(8,128)(2,1)S(1)} %get-tuple-element.112), channel_id=1, source_target_pairs={{0,28},{4,24},{8,20},{12,16},{16,12},{20,8},{24,4},{28,0},{1,29},{... | collective-permute-start | bytes 798728 | tf_op jit(solution)/shard_map/ppermute | solution.py:513
  24.4 14.4 %copy-start = (f32[64,2048]{1,0:T(8,128)S(1)}, f32[64,2048]{1,0:T(8,128)}, u32[]{:S(2)}) copy-start(f32[64,2048]{1,0:T(8,128)} %refs_5_.1) | copy-start | bytes 1572868
  24.4 14.4 %copy-start.1 = (f32[2048]{0:T(1024)S(1)}, f32[2048]{0:T(1024)}, u32[]{:S(2)}) copy-start(f32[2048]{0:T(1024)} %param.10) | copy-start | bytes 24580
  43.1 40.6 %collective-permute-start.8 = (bf16[768,640]{1,0:T(8,128)(2,1)S(1)}, bf16[768,640]{1,0:T(8,128)(2,1)S(1)}, u32[]{:S(2)}, u32[]{:S(2)}) collective-permute-start(bf16[768,640]{1,0:T(8,128)(2,1)S(1)} %get-tuple-element.139.refs_0_), channel_id=1, source_target_pairs={{0,1},{1,2},{2,3},{3,0},{4,5},{5,6},{6,7},{7,4},{8,9},{9,10},{10,1... | collective-permute-start | bytes 2949128 | tf_op jit(solution)/shard_map/ppermute | solution.py:520
  45.0 3.4 %collective-permute-start.10 = (bf16[192,384]{1,0:T(8,128)(2,1)S(1)}, bf16[192,384]{1,0:T(8,128)(2,1)S(1)}, u32[]{:S(2)}, u32[]{:S(2)}) collective-permute-start(bf16[192,384]{1,0:T(8,128)(2,1)S(1)} %get-tuple-element.141), channel_id=1, source_target_pairs={{0,4},{4,0},{8,12},{12,8},{16,20},{20,16},{24,28},{28,24},{1,5},{5... | collective-permute-start | bytes 442376 | tf_op jit(solution)/shard_map/ppermute | solution.py:513
  45.0 6.6 %collective-permute-start.11 = (bf16[192,384]{1,0:T(8,128)(2,1)S(1)}, bf16[192,384]{1,0:T(8,128)(2,1)S(1)}, u32[]{:S(2)}, u32[]{:S(2)}) collective-permute-start(bf16[192,384]{1,0:T(8,128)(2,1)S(1)} %get-tuple-element.142), channel_id=1, source_target_pairs={{0,8},{4,12},{8,0},{12,4},{16,24},{20,28},{24,16},{28,20},{1,9},{5... | collective-permute-start | bytes 442376 | tf_op jit(solution)/shard_map/ppermute | solution.py:513
  46.4 7.6 %collective-permute-start.12 = (bf16[192,384]{1,0:T(8,128)(2,1)S(1)}, bf16[192,384]{1,0:T(8,128)(2,1)S(1)}, u32[]{:S(2)}, u32[]{:S(2)}) collective-permute-start(bf16[192,384]{1,0:T(8,128)(2,1)S(1)} %get-tuple-element.143), channel_id=1, source_target_pairs={{0,12},{4,8},{8,4},{12,0},{16,28},{20,24},{24,20},{28,16},{1,13},{... | collective-permute-start | bytes 442376 | tf_op jit(solution)/shard_map/ppermute | solution.py:513
  46.8 9.7 %collective-permute-start.13 = (bf16[192,384]{1,0:T(8,128)(2,1)S(1)}, bf16[192,384]{1,0:T(8,128)(2,1)S(1)}, u32[]{:S(2)}, u32[]{:S(2)}) collective-permute-start(bf16[192,384]{1,0:T(8,128)(2,1)S(1)} %get-tuple-element.144), channel_id=1, source_target_pairs={{0,16},{4,20},{8,24},{12,28},{16,0},{20,4},{24,8},{28,12},{1,17},{... | collective-permute-start | bytes 442376 | tf_op jit(solution)/shard_map/ppermute | solution.py:513
  48.3 20.8 %collective-permute-start.23 = (bf16[192,768]{1,0:T(8,128)(2,1)S(1)}, bf16[192,768]{1,0:T(8,128)(2,1)S(1)}, u32[]{:S(2)}, u32[]{:S(2)}) collective-permute-start(bf16[192,768]{1,0:T(8,128)(2,1)S(1)} %get-tuple-element.181.refs_7_.refs_6_), channel_id=1, source_target_pairs={{0,4},{4,0},{8,12},{12,8},{16,20},{20,16},{24,28},{28,24},{1,5},{5... | collective-permute-start | bytes 884744 | tf_op jit(solution)/shard_map/ppermute | solution.py:513
  51.6 6.1 %collective-permute-start.14 = (bf16[192,384]{1,0:T(8,128)(2,1)S(1)}, bf16[192,384]{1,0:T(8,128)(2,1)S(1)}, u32[]{:S(2)}, u32[]{:S(2)}) collective-permute-start(bf16[192,384]{1,0:T(8,128)(2,1)S(1)} %get-tuple-element.145), channel_id=1, source_target_pairs={{0,20},{4,16},{8,28},{12,24},{16,4},{20,0},{24,12},{28,8},{1,21},{... | collective-permute-start | bytes 442376 | tf_op jit(solution)/shard_map/ppermute | solution.py:513
  54.0 7.5 %collective-permute-start.15 = (bf16[192,384]{1,0:T(8,128)(2,1)S(1)}, bf16[192,384]{1,0:T(8,128)(2,1)S(1)}, u32[]{:S(2)}, u32[]{:S(2)}) collective-permute-start(bf16[192,384]{1,0:T(8,128)(2,1)S(1)} %get-tuple-element.146), channel_id=1, source_target_pairs={{0,24},{4,28},{8,16},{12,20},{16,8},{20,12},{24,0},{28,4},{1,25},{... | collective-permute-start | bytes 442376 | tf_op jit(solution)/shard_map/ppermute | solution.py:513
  56.5 7.4 %collective-permute-start.16 = (bf16[192,384]{1,0:T(8,128)(2,1)S(1)}, bf16[192,384]{1,0:T(8,128)(2,1)S(1)}, u32[]{:S(2)}, u32[]{:S(2)}) collective-permute-start(bf16[192,384]{1,0:T(8,128)(2,1)S(1)} %get-tuple-element.147), channel_id=1, source_target_pairs={{0,28},{4,24},{8,20},{12,16},{16,12},{20,8},{24,4},{28,0},{1,29},{... | collective-permute-start | bytes 442376 | tf_op jit(solution)/shard_map/ppermute | solution.py:513
  66.1 17.6 %collective-permute-start.17 = (bf16[768,384]{1,0:T(8,128)(2,1)S(1)}, bf16[768,384]{1,0:T(8,128)(2,1)S(1)}, u32[]{:S(2)}, u32[]{:S(2)}) collective-permute-start(bf16[768,384]{1,0:T(8,128)(2,1)S(1)} %shard_map.88.refs_1_), channel_id=1, source_target_pairs={{0,1},{1,2},{2,3},{3,0},{4,5},{5,6},{6,7},{7,4},{8,9},{9,10},{10,1... | collective-permute-start | bytes 1769480 | tf_op jit(solution)/shard_map/ppermute | solution.py:520
  67.7 16.5 %collective-permute-start.21 = (bf16[768,384]{1,0:T(8,128)(2,1)S(1)}, bf16[768,384]{1,0:T(8,128)(2,1)S(1)}, u32[]{:S(2)}, u32[]{:S(2)}) collective-permute-start(bf16[768,384]{1,0:T(8,128)(2,1)S(1)} %shard_map.88.refs_1_), channel_id=1, source_target_pairs={{0,4},{4,0},{8,12},{12,8},{16,20},{20,16},{24,28},{28,24},{1,5},{5... | collective-permute-start | bytes 1769480 | tf_op jit(solution)/shard_map/ppermute | solution.py:513
  67.8 34.7 %collective-permute-start.18 = (bf16[720,1024]{1,0:T(8,128)(2,1)S(1)}, bf16[720,1024]{1,0:T(8,128)(2,1)S(1)}, u32[]{:S(2)}, u32[]{:S(2)}) collective-permute-start(bf16[720,1024]{1,0:T(8,128)(2,1)S(1)} %pad_maximum_fusion.refs_0_), channel_id=1, source_target_pairs={{0,8},{4,12},{8,0},{12,4},{16,24},{20,28},{24,16},{28,20},{1,9},{5... | collective-permute-start | bytes 4423688 | tf_op jit(solution)/shard_map/ppermute | solution.py:513
  69.2 34.4 %collective-permute-start.19 = (bf16[720,1024]{1,0:T(8,128)(2,1)S(1)}, bf16[720,1024]{1,0:T(8,128)(2,1)S(1)}, u32[]{:S(2)}, u32[]{:S(2)}) collective-permute-start(bf16[720,1024]{1,0:T(8,128)(2,1)S(1)} %pad_maximum_fusion.refs_0_), channel_id=1, source_target_pairs={{0,16},{4,20},{8,24},{12,28},{16,0},{20,4},{24,8},{28,12},{1,17},{... | collective-permute-start | bytes 4423688 | tf_op jit(solution)/shard_map/ppermute | solution.py:513
  83.7 2.6 %collective-permute-start.20 = (bf16[768,640]{1,0:T(8,128)(2,1)S(1)}, bf16[768,640]{1,0:T(8,128)(2,1)S(1)}, u32[]{:S(2)}, u32[]{:S(2)}) collective-permute-start(bf16[768,640]{1,0:T(8,128)(2,1)S(1)} %get-tuple-element.139.refs_0_), channel_id=1, source_target_pairs={{0,4},{4,0},{8,12},{12,8},{16,20},{20,16},{24,28},{28,24},{1,5},{5... | collective-permute-start | bytes 2949128 | tf_op jit(solution)/shard_map/ppermute | solution.py:513
  83.7 19.9 %collective-permute-start.22 = (bf16[768,640]{1,0:T(8,128)(2,1)S(1)}, bf16[768,640]{1,0:T(8,128)(2,1)S(1)}, u32[]{:S(2)}, u32[]{:S(2)}) collective-permute-start(bf16[768,640]{1,0:T(8,128)(2,1)S(1)} %collective-permute-done.8.refs_0_), channel_id=1, source_target_pairs={{0,4},{4,0},{8,12},{12,8},{16,20},{20,16},{24,28},{28,24},{1,5},{5... | collective-permute-start | bytes 2949128 | tf_op jit(solution)/shard_map/ppermute | solution.py:513
  84.2 25.5 %collective-permute-start.9 = (bf16[768,640]{1,0:T(8,128)(2,1)S(1)}, bf16[768,640]{1,0:T(8,128)(2,1)S(1)}, u32[]{:S(2)}, u32[]{:S(2)}) collective-permute-start(bf16[768,640]{1,0:T(8,128)(2,1)S(1)} %collective-permute-done.8.refs_0_), channel_id=1, source_target_pairs={{0,1},{1,2},{2,3},{3,0},{4,5},{5,6},{6,7},{7,4},{8,9},{9,10},{10,1... | collective-permute-start | bytes 2949128 | tf_op jit(solution)/shard_map/ppermute | solution.py:520
  109.7 37.4 %collective-permute-start.24 = (bf16[768,640]{1,0:T(8,128)(2,1)S(1)}, bf16[768,640]{1,0:T(8,128)(2,1)S(1)}, u32[]{:S(2)}, u32[]{:S(2)}) collective-permute-start(bf16[768,640]{1,0:T(8,128)(2,1)S(1)} %collective-permute-done.9.refs_0_), channel_id=1, source_target_pairs={{0,1},{1,2},{2,3},{3,0},{4,5},{5,6},{6,7},{7,4},{8,9},{9,10},{10,1... | collective-permute-start | bytes 2949128 | tf_op jit(solution)/shard_map/ppermute | solution.py:520
  109.8 17.7 %collective-permute-start.27 = (bf16[720,512]{1,0:T(8,128)(2,1)S(1)}, bf16[720,512]{1,0:T(8,128)(2,1)S(1)}, u32[]{:S(2)}, u32[]{:S(2)}) collective-permute-start(bf16[720,512]{1,0:T(8,128)(2,1)S(1)} %slice.6), channel_id=1, source_target_pairs={{0,16},{4,20},{8,24},{12,28},{16,0},{20,4},{24,8},{28,12},{1,17},{... | collective-permute-start | bytes 2211848 | tf_op jit(solution)/shard_map/ppermute | solution.py:513
  111.4 17.4 %collective-permute-start.28 = (bf16[720,512]{1,0:T(8,128)(2,1)S(1)}, bf16[720,512]{1,0:T(8,128)(2,1)S(1)}, u32[]{:S(2)}, u32[]{:S(2)}) collective-permute-start(bf16[720,512]{1,0:T(8,128)(2,1)S(1)} %slice.7), channel_id=1, source_target_pairs={{0,8},{4,12},{8,0},{12,4},{16,24},{20,28},{24,16},{28,20},{1,9},{5... | collective-permute-start | bytes 2211848 | tf_op jit(solution)/shard_map/ppermute | solution.py:513
  113.1 27.7 %collective-permute-start.26 = (bf16[768,384]{1,0:T(8,128)(2,1)S(1)}, bf16[768,384]{1,0:T(8,128)(2,1)}, u32[]{:S(2)}, u32[]{:S(2)}) collective-permute-start(bf16[768,384]{1,0:T(8,128)(2,1)S(1)} %collective-permute-done.17.refs_1_), channel_id=1, source_target_pairs={{0,4},{4,0},{8,12},{12,8},{16,20},{20,16},{24,28},{28,24},{1,5},{5... | collective-permute-start | bytes 1769480 | tf_op jit(solution)/shard_map/ppermute | solution.py:513
  113.1 34.1 %collective-permute-start.25 = (bf16[768,384]{1,0:T(8,128)(2,1)S(1)}, bf16[768,384]{1,0:T(8,128)(2,1)S(1)}, u32[]{:S(2)}, u32[]{:S(2)}) collective-permute-start(bf16[768,384]{1,0:T(8,128)(2,1)S(1)} %collective-permute-done.17.refs_1_), channel_id=1, source_target_pairs={{0,1},{1,2},{2,3},{3,0},{4,5},{5,6},{6,7},{7,4},{8,9},{9,10},{10,1... | collective-permute-start | bytes 1769480 | tf_op jit(solution)/shard_map/ppermute | solution.py:520
  127.5 20.3 %collective-permute-start.31 = (bf16[768,640]{1,0:T(8,128)(2,1)S(1)}, bf16[768,640]{1,0:T(8,128)(2,1)S(1)}, u32[]{:S(2)}, u32[]{:S(2)}) collective-permute-start(bf16[768,640]{1,0:T(8,128)(2,1)S(1)} %collective-permute-done.9.refs_0_), channel_id=1, source_target_pairs={{0,4},{4,0},{8,12},{12,8},{16,20},{20,16},{24,28},{28,24},{1,5},{5... | collective-permute-start | bytes 2949128 | tf_op jit(solution)/shard_map/ppermute | solution.py:513
  147.2 8.9 %collective-permute-start.30 = (bf16[768,640]{1,0:T(8,128)(2,1)S(1)}, bf16[768,640]{1,0:T(8,128)(2,1)S(1)}, u32[]{:S(2)}, u32[]{:S(2)}) collective-permute-start(bf16[768,640]{1,0:T(8,128)(2,1)S(1)} %collective-permute-done.24.refs_0_), channel_id=1, source_target_pairs={{0,4},{4,0},{8,12},{12,8},{16,20},{20,16},{24,28},{28,24},{1,5},{5... | collective-permute-start | bytes 2949128 | tf_op jit(solution)/shard_map/ppermute | solution.py:513
  147.3 3.4 %collective-permute-start.32 = (bf16[768,384]{1,0:T(8,128)(2,1)S(1)}, bf16[768,384]{1,0:T(8,128)(2,1)S(1)}, u32[]{:S(2)}, u32[]{:S(2)}) collective-permute-start(bf16[768,384]{1,0:T(8,128)(2,1)S(1)} %collective-permute-done.25.refs_1_), channel_id=1, source_target_pairs={{0,4},{4,0},{8,12},{12,8},{16,20},{20,16},{24,28},{28,24},{1,5},{5... | collective-permute-start | bytes 1769480 | tf_op jit(solution)/shard_map/ppermute | solution.py:513
  147.8 17.1 %collective-permute-start.29 = (bf16[768,384]{1,0:T(8,128)(2,1)S(1)}, bf16[768,384]{1,0:T(8,128)(2,1)S(1)}, u32[]{:S(2)}, u32[]{:S(2)}) collective-permute-start(bf16[768,384]{1,0:T(8,128)(2,1)S(1)} %collective-permute-done.25.refs_1_), channel_id=1, source_target_pairs={{0,1},{1,2},{2,3},{3,0},{4,5},{5,6},{6,7},{7,4},{8,9},{9,10},{10,1... | collective-permute-start | bytes 1769480 | tf_op jit(solution)/shard_map/ppermute | solution.py:520
  164.9 2.0 collective-permute-start.33
  172.8 1.3 collective-permute-start.34
  174.7 4.8 %collective-permute-start.35 = (f32[8,1536]{1,0:T(8,128)S(1)}, f32[8,1536]{1,0:T(8,128)S(1)}, u32[]{:S(2)}, u32[]{:S(2)}) collective-permute-start(f32[8,1536]{1,0:T(8,128)S(1)} %shard_map.95.refs_2_), channel_id=1, source_target_pairs={{0,1},{1,0},{2,3},{3,2},{4,5},{5,4},{6,7},{7,6},{8,9},{9,8},{10,11... | collective-permute-start | bytes 147464 | tf_op jit(solution)/shard_map/ppermute | solution.py:587
  174.8 5.9 %collective-permute-start.36 = (f32[8,1536]{1,0:T(8,128)S(1)}, f32[8,1536]{1,0:T(8,128)S(1)}, u32[]{:S(2)}, u32[]{:S(2)}) collective-permute-start(f32[8,1536]{1,0:T(8,128)S(1)} %shard_map.95.refs_2_), channel_id=1, source_target_pairs={{0,2},{1,3},{2,0},{3,1},{4,6},{5,7},{6,4},{7,5},{8,10},{9,11},{10,... | collective-permute-start | bytes 147464 | tf_op jit(solution)/shard_map/ppermute | solution.py:587
  177.1 5.9 %collective-permute-start.37 = (f32[8,1536]{1,0:T(8,128)S(1)}, f32[8,1536]{1,0:T(8,128)S(1)}, u32[]{:S(2)}, u32[]{:S(2)}) collective-permute-start(f32[8,1536]{1,0:T(8,128)S(1)} %shard_map.95.refs_2_), channel_id=1, source_target_pairs={{0,3},{1,2},{2,1},{3,0},{4,7},{5,6},{6,5},{7,4},{8,11},{9,10},{10,... | collective-permute-start | bytes 147464 | tf_op jit(solution)/shard_map/ppermute | solution.py:587
  187.2 19.3 %collective-permute-start.38 = (bf16[720,512]{1,0:T(8,128)(2,1)S(1)}, bf16[720,512]{1,0:T(8,128)(2,1)S(1)}, u32[]{:S(2)}, u32[]{:S(2)}) collective-permute-start(bf16[720,512]{1,0:T(8,128)(2,1)S(1)} %get-tuple-element.187), channel_id=1, source_target_pairs={{0,8},{4,12},{8,0},{12,4},{16,24},{20,28},{24,16},{28,20},{1,9},{5... | collective-permute-start | bytes 2211848 | tf_op jit(solution)/shard_map/ppermute | solution.py:513
  188.8 17.6 %collective-permute-start.39 = (bf16[720,512]{1,0:T(8,128)(2,1)S(1)}, bf16[720,512]{1,0:T(8,128)(2,1)S(1)}, u32[]{:S(2)}, u32[]{:S(2)}) collective-permute-start(bf16[720,512]{1,0:T(8,128)(2,1)S(1)} %get-tuple-element.188), channel_id=1, source_target_pairs={{0,16},{4,20},{8,24},{12,28},{16,0},{20,4},{24,8},{28,12},{1,17},{... | collective-permute-start | bytes 2211848 | tf_op jit(solution)/shard_map/ppermute | solution.py:513
  189.5 17.0 %collective-permute-start.40 = (bf16[64,720]{1,0:T(8,128)(2,1)S(1)}, bf16[64,720]{1,0:T(8,128)(2,1)S(1)}, u32[]{:S(2)}, u32[]{:S(2)}) collective-permute-start(bf16[64,720]{1,0:T(8,128)(2,1)S(1)} %get-tuple-element.196.mine_ref), channel_id=1, source_target_pairs={{0,8},{4,12},{8,0},{12,4},{16,24},{20,28},{24,16},{28,20},{1,9},{5... | collective-permute-start | bytes 276488 | tf_op jit(solution)/shard_map/ppermute | solution.py:513
  207.1 5.5 %collective-permute-start.46 = (bf16[64,720]{1,0:T(8,128)(2,1)S(1)}, bf16[64,720]{1,0:T(8,128)(2,1)S(1)}, u32[]{:S(2)}, u32[]{:S(2)}) collective-permute-start(bf16[64,720]{1,0:T(8,128)(2,1)S(1)} %shard_map.98), channel_id=1, source_target_pairs={{0,16},{4,20},{8,24},{12,28},{16,0},{20,4},{24,8},{28,12},{1,17},{... | collective-permute-start | bytes 276488 | tf_op jit(solution)/shard_map/ppermute | solution.py:513
  209.4 19.7 %collective-permute-start.42 = (bf16[720,512]{1,0:T(8,128)(2,1)}, bf16[720,512]{1,0:T(8,128)(2,1)}, u32[]{:S(2)}, u32[]{:S(2)}) collective-permute-start(bf16[720,512]{1,0:T(8,128)(2,1)} %get-tuple-element.207), channel_id=1, source_target_pairs={{0,16},{4,12},{8,24},{12,4},{16,0},{20,28},{24,8},{28,20},{1,17},{... | collective-permute-start | bytes 2211848 | tf_op jit(solution)/shard_map/ppermute | solution.py:517
  210.8 19.7 %collective-permute-start.41 = (bf16[720,512]{1,0:T(8,128)(2,1)}, bf16[720,512]{1,0:T(8,128)(2,1)}, u32[]{:S(2)}, u32[]{:S(2)}) collective-permute-start(bf16[720,512]{1,0:T(8,128)(2,1)} %get-tuple-element.198), channel_id=1, source_target_pairs={{0,8},{4,20},{8,0},{12,28},{16,24},{20,4},{24,16},{28,12},{1,9},{5... | collective-permute-start | bytes 2211848 | tf_op jit(solution)/shard_map/ppermute | solution.py:517
  212.6 2.0 collective-permute-start.47
  212.7 29.3 %collective-permute-start.45 = (bf16[720,512]{1,0:T(8,128)(2,1)}, bf16[720,512]{1,0:T(8,128)(2,1)}, u32[]{:S(2)}, u32[]{:S(2)}) collective-permute-start(bf16[720,512]{1,0:T(8,128)(2,1)} %get-tuple-element.208), channel_id=1, source_target_pairs={{0,12},{4,16},{8,4},{12,24},{16,28},{20,0},{24,20},{28,8},{1,13},{... | collective-permute-start | bytes 2211848 | tf_op jit(solution)/shard_map/ppermute | solution.py:517
  214.5 27.4 %collective-permute-start.43 = (bf16[720,512]{1,0:T(8,128)(2,1)S(1)}, bf16[720,512]{1,0:T(8,128)(2,1)}, u32[]{:S(2)}, u32[]{:S(2)}) collective-permute-start(bf16[720,512]{1,0:T(8,128)(2,1)S(1)} %get-tuple-element.202), channel_id=1, source_target_pairs={{0,4},{4,0},{8,12},{12,8},{16,20},{20,16},{24,28},{28,24},{1,5},{5... | collective-permute-start | bytes 2211848 | tf_op jit(solution)/shard_map/ppermute | solution.py:513
  214.5 27.4 %collective-permute-start.44 = (bf16[720,512]{1,0:T(8,128)(2,1)S(1)}, bf16[720,512]{1,0:T(8,128)(2,1)}, u32[]{:S(2)}, u32[]{:S(2)}) collective-permute-start(bf16[720,512]{1,0:T(8,128)(2,1)S(1)} %get-tuple-element.203), channel_id=1, source_target_pairs={{0,20},{4,8},{8,28},{12,0},{16,4},{20,24},{24,12},{28,16},{1,21},{... | collective-permute-start | bytes 2211848 | tf_op jit(solution)/shard_map/ppermute | solution.py:517

commit v9 on v8

--- a/solution.py
+++ b/solution.py
@@ -52,10 +52,12 @@
 
 def one_hot_rows(out_ref, wanted):
     rows, width = out_ref.shape
+    short = wanted.astype(jnp.int16)
+    one, zero = jnp.ones((), BF16), jnp.zeros((), BF16)
     step = 256 if rows % 256 == 0 else rows
     for start in range(0, rows, step):
-        index = lax.broadcasted_iota(I32, (step, width), 0) + start
-        out_ref[start : start + step, :] = jnp.where(index == wanted, 1.0, 0.0).astype(BF16)
+        index = lax.broadcasted_iota(jnp.int16, (step, width), 0) + jnp.int16(start)
+        out_ref[start : start + step, :] = jnp.where(index == short, one, zero)
 
 
 def places_of(dest, shard_rows, cap, dom, device):
@@ -84,10 +86,10 @@
     return jnp.concatenate([ref[...] for ref in refs], axis=1)
 
 
-def pack_first_body(dom, shard_rows, cap, meta, dest_ref, bin_ref, *refs):
+def pack_first_body(dom, shard_rows, cap, bins, meta, slot_ref, *refs):
     raw, outs, (place_ref, pick) = refs[: -dom - 2], refs[-dom - 2 : -2], refs[-2:]
-    dest = dest_ref[...].reshape(1, dest_ref.shape[0])
-    bins = bin_ref[...].reshape(1, dest_ref.shape[0])
+    slot = slot_ref[...].reshape(1, slot_ref.shape[0])
+    dest, slot_bin = slot >> (bins.bit_length() - 1), slot & (bins - 1)
     place, local = places_of(dest, shard_rows, cap, dom, meta[0])
     place_ref[...] = place
     one_hot_rows(pick, place)
@@ -95,7 +97,7 @@
     digits = jnp.where(
         which == 0,
         local >> 4,
-        jnp.where(which == 1, local & 15, jnp.where(which == 2, bins, jnp.where(which == 3, 1, 0))),
+        jnp.where(which == 1, local & 15, jnp.where(which == 2, slot_bin, jnp.where(which == 3, 1, 0))),
     )
     digits = jnp.where(dest >= 0, digits, 0).astype(F32).astype(BF16)
     codes = mm(digits, pick[...], NT)
@@ -121,16 +123,16 @@
     return [pl.BlockSpec((hold, LANES), at(k)) for k in range(width // LANES)]
 
 
-def pack_first(meta, raw_images, dest, bins, dom, share, chunk):
+def pack_first(meta, raw_images, slot, bins, dom, share, chunk):
     hold, _ = raw_images.shape
     width = chunk[1]
     cap = hold // dom
     slots = dom * cap
     specs = raw_specs(hold, share, chunk)
     return call(
-        functools.partial(pack_first_body, dom, hold // 2, cap),
+        functools.partial(pack_first_body, dom, hold // 2, cap, bins),
         (1,),
-        [pl.BlockSpec((hold,), lambda j, m: (0,))] * 2 + specs,
+        [pl.BlockSpec((hold,), lambda j, m: (0,))] + specs,
         [pl.BlockSpec((cap + CODE, width), lambda j, m: (0, 0))] * dom
         + [pl.BlockSpec((1, hold), lambda j, m: (0, 0))],
         [sds((cap + CODE, width), BF16)] * dom + [sds((1, hold), I32)],
@@ -138,7 +140,7 @@
         room=51,
         flops=2 * slots * hold * width,
         moved=4 * hold * width,
-    )(meta, dest, bins, *[raw_images] * len(specs))
+    )(meta, slot, *[raw_images] * len(specs))
 
 
 def pack_next(meta, raw_images, place, dom, share, chunk):
@@ -481,6 +483,25 @@
     )(meta, *operands)
 
 
+def own_half_body(tile, meta, keep_ref, c_ref, a_ref, out_ref):
+    rows = pl.ds(pl.multiple_of(pl.program_id(0) * tile, tile), tile)
+    out_ref[...] = keep_ref[rows, :] + c_ref[rows, :].astype(F32) + a_ref[rows, :].astype(F32)
+
+
+def own_half(meta, keep, got_c, got_a):
+    count, width = keep.shape
+    parts = 3
+    tile = count // parts
+    return call(
+        functools.partial(own_half_body, tile),
+        (parts,),
+        [pl.BlockSpec(memory_space=pltpu.VMEM)] * 3,
+        pl.BlockSpec((tile, width), lambda j, m: (lax.rem(m[0], 2) * parts + j, 0)),
+        sds((2 * count, width), F32),
+        room=8,
+    )(meta, keep, got_c, got_a)
+
+
 def two_by_two(raw_images, defocus_bin, dest_row, ctf_table, inv_noise, panels):
     dom, turns = lax.axis_size("dom"), lax.axis_size("rot")
     device, plane = lax.axis_index("dom"), lax.axis_index("rot")
@@ -524,19 +545,19 @@
     chunk_a, chunk_b = (0, cut), (cut, width - cut)
 
     def exchange(blocks):
-        got = [blocks[0]] + [None] * (dom - 1)
-        for apart in (6, 7, 2, 4, 3, 5, 1):
-            got[apart] = across(blocks[apart], apart)
-        return got
-
-    *send_a, place = pack_first(meta, raw_images, dest_row, defocus_bin, dom, width, chunk_a)
+        far_first = [across(blocks[apart], apart) for apart in (6, 7, 4, 2, 5, 3, 1)]
+        return far_first + [blocks[0]]
+
+    slot = jnp.where(dest_row >= 0, dest_row * bins + defocus_bin, -1)
+    *send_a, place = pack_first(meta, raw_images, slot, bins, dom, width, chunk_a)
     recv_a = exchange(send_a)
+    swapped, place = lax.optimization_barrier((across(panels, 1), place))
     send_b = pack_next(meta, raw_images, place, dom, width, chunk_b)
     together = lax.optimization_barrier
 
     count = panels.shape[0] // 2
     mine = lax.dynamic_slice_in_dim(panels, core * count, count, 0)
-    other = lax.dynamic_slice_in_dim(across(panels, 1), core * count, count, 0)
+    other = lax.dynamic_slice_in_dim(swapped, core * count, count, 0)
     near = jnp.concatenate([mine, other], axis=1)
 
     recv_a, send_b, near = together((recv_a, send_b, near))
@@ -609,13 +630,9 @@
         jnp.concatenate([mass, mass_other], axis=1),
         jnp.concatenate([mass_other, mass], axis=1),
     )
-    own_half = keep + got_c.astype(F32) + got_a.astype(F32)
+    sums = own_half(meta, keep, got_c, got_a)
     other_half = got_self.astype(F32) + got_d.astype(F32) + got_b.astype(F32)
-    class_sums = jnp.where(
-        even,
-        jnp.concatenate([own_half, other_half], axis=0),
-        jnp.concatenate([other_half, own_half], axis=0),
-    ).T
+    class_sums = lax.dynamic_update_slice_in_dim(sums, other_half, (1 - core) * count, 0).T
     return class_sums, bin_weights, log_evidence.reshape(-1)
 
 

time: 247 us -> 250 us (1.012)
  waiting for transfers between devices: 126 us -> 129 us
  Pallas kernels: 67.9 us -> 70.5 us
    ppermute x4, waiting for transfers between devices: 23.5 us -> 27.9 us  [by_core(): return lax.ppermute(value, 'dom', pairs)]
    ppermute x35, starting transfers between devices: 26.1 us -> 29.7 us  [across(): return lax.ppermute(value, 'dom', [(i, i ^ apart) for i in range(dom)])]
    add x2 -> x0, other arithmetic: 3.45 us -> none  [the longest x1 1.83 us: two_by_two(): other_half = got_self.astype(F32) + got_d.astype(F32) + got_b.astype(F32)]
    ppermute x4, starting transfers between devices: 5.55 us -> 2.19 us  [by_core(): return lax.ppermute(value, 'dom', pairs)]
    dynamic_update_slice x0 -> x1, other arithmetic: none -> 2.94 us  [two_by_two(): lax.dynamic_update_slice_in_dim(sums, other_half, (1 - core) * count, 0)]
    pallas_call x1 -> x2, Pallas kernels: 7.28 us -> 9.53 us  [the longest x1 7.28 us: pack_first(): call(functools.partial(pack_first_body, dom, hold // 2, cap, bins), (1,),...]
  transfers between devices with their start and end apart: 48 -> 48, of which waited for: 27 -> 28; matrix products, arithmetic and copies ran while one was open for 3% -> 3% of each run, Pallas kernels for 21% -> 22%
where the time goes in v9:
time: 250 us
  waiting for transfers between devices  129 us (52%)
  Pallas kernels  70.5 us (28%)
  starting transfers between devices  40 us (16%)
  other arithmetic  7.15 us (3%)
  local copies, waits for them, and re-layouts  2.55 us (1%)
    ppermute x35, waiting for transfers between devices, across(): return lax.ppermute(value, 'dom', [(i, i ^ apart) for i in range(dom)])  73.9 us
    ppermute x35, starting transfers between devices, across(): return lax.ppermute(value, 'dom', [(i, i ^ apart) for i in range(dom)])  29.7 us
    ppermute x4, waiting for transfers between devices, by_core(): return lax.ppermute(value, 'dom', pairs)  27.9 us
    pallas_call x5, Pallas kernels, score(): call(functools.partial(score_body, parts, used, first, last), (2 * half,)...  27.2 us
    ppermute x6, waiting for transfers between devices, onward(): lax.ppermute(value, 'rot', [(i, (i + 1) % turns) for i in range(turns)])  23 us
    pallas_call x2, Pallas kernels, class_part(): call(functools.partial(class_body, kind, steps), (steps,), in_specs, out_...  15 us
    pallas_call x1, Pallas kernels, pack_first(): call(functools.partial(pack_first_body, dom, hold // 2, cap, bins), (1,),...  7.28 us
    pallas_call x1, Pallas kernels, energy(): call(functools.partial(energy_body, bins, count), (count,), [pl.BlockSpec...  6.78 us
  transfers between devices with their start and end apart: 48, of which 28 were waited for; matrix products, arithmetic and copies ran while one was open for 3% of the time, Pallas kernels for 22%

profile of v9, /device:TPU:0, one launch (start us, length us, event | category | flops | bytes accessed | tf_op | source)
XLA Modules:
  0.0 249.7 jit_solution(4250345420437730648)
XLA Ops:
  1.2 0.7 add_select_fusion.slot_ref
  2.0 7.3 %shard_map.85 = (bf16[208,640]{1,0:T(8,128)(2,1)S(1)}, bf16[208,640]{1,0:T(8,128)(2,1)S(1)}, bf16[208,640]{1,0:T(8,128)(2,1)S(1)}, bf16[208,640]{1,0:T(8,128)(2,...) custom-call(s32[10]{0:T(128)S(1)} %stack.43.meta, ...), custom_call_target="tpu_custom_call" | custom-call | flops 188743680 | bytes 245760 | tf_op jit(solution)/shard_map/pallas_call | solution.py:132
  9.2 3.6 %collective-permute-start = (bf16[208,640]{1,0:T(8,128)(2,1)S(1)}, bf16[208,640]{1,0:T(8,128)(2,1)S(1)}, u32[]{:S(2)}, u32[]{:S(2)}) collective-permute-start(bf16[208,640]{1,0:T(8,128)(2,1)S(1)} %get-tuple-element.107), channel_id=1, source_target_pairs={{0,24},{4,28},{8,16},{12,20},{16,8},{20,12},{24,0},{28,4},{1,25},{... | collective-permute-start | bytes 798728 | tf_op jit(solution)/shard_map/ppermute | solution.py:534
  12.9 1.6 collective-permute-start.2
  14.6 1.5 collective-permute-start.3
  16.1 1.2 constant_dynamic-slice_fusion.1
  17.3 4.4 %shard_map.86 = (bf16[192,384]{1,0:T(8,128)(2,1)S(1)}, bf16[192,384]{1,0:T(8,128)(2,1)S(1)}, bf16[192,384]{1,0:T(8,128)(2,1)S(1)}, bf16[192,384]{1,0:T(8,128)(2,...) custom-call(s32[10]{0:T(128)S(1)} %stack.43.meta, ...), custom_call_target="tpu_custom_call" | custom-call | flops 113246208 | bytes 147456 | tf_op jit(solution)/shard_map/pallas_call | solution.py:152
  22.4 2.9 %collective-permute-done.1.refs_1_ = bf16[208,640]{1,0:T(8,128)(2,1)S(1)} collective-permute-done((bf16[208,640]{1,0:T(8,128)(2,1)S(1)}, bf16[208,640]{1,0:T(8,128)(2,1)S(1)}, u32[]{:S(2)}, u32[]{:S(2)}) %collective-permute-start.1) | collective-permute-done | bytes 266272 | tf_op jit(solution)/shard_map/ppermute | solution.py:534
  25.6 1.2 constant_dynamic-slice_fusion
  27.0 4.3 %collective-permute-done.2.refs_2_ = bf16[208,640]{1,0:T(8,128)(2,1)S(1)} collective-permute-done((bf16[208,640]{1,0:T(8,128)(2,1)S(1)}, bf16[208,640]{1,0:T(8,128)(2,1)S(1)}, u32[]{:S(2)}, u32[]{:S(2)}) %collective-permute-start.2) | collective-permute-done | bytes 266272 | tf_op jit(solution)/shard_map/ppermute | solution.py:534
  32.0 4.9 %collective-permute-done.4.refs_4_ = bf16[208,640]{1,0:T(8,128)(2,1)S(1)} collective-permute-done((bf16[208,640]{1,0:T(8,128)(2,1)S(1)}, bf16[208,640]{1,0:T(8,128)(2,1)S(1)}, u32[]{:S(2)}, u32[]{:S(2)}) %collective-permute-start.4) | collective-permute-done | bytes 266272 | tf_op jit(solution)/shard_map/ppermute | solution.py:534
  36.9 4.2 %shard_map.87 = (bf16[768,640]{1,0:T(8,128)(2,1)S(1)}, bf16[192,768]{1,0:T(8,128)(2,1)S(1)}, bf16[768,1536]{1,0:T(8,128)(2,1)S(1)}, bf16[768,192]{1,0:T(8,128)(2,1)S(1)}) custom-call(s32[10]{0:T(128)S(1)} %stack.43.meta, bf16[208,640]{1,0:T(8,128)(2,1)S(1)} %collective-permute-done.refs_0_, bf16[208,640]{1,0:T(8,128)(2,1)S(1)} %collective-permute-done.1.refs_1_, ...), custom_call_target="tpu_custom_call" | custom-call | flops 94371840 | bytes 122880 | tf_op jit(solution)/shard_map/pallas_call | solution.py:212
  41.1 1.8 collective-permute-start.8
  42.9 2.4 collective-permute-start.10
  45.4 1.2 collective-permute-start.12
  46.5 1.5 collective-permute-start.13
  48.0 1.6 collective-permute-done.10.refs_0_
  49.7 3.2 %collective-permute-done.11.refs_1_ = bf16[192,384]{1,0:T(8,128)(2,1)S(1)} collective-permute-done((bf16[192,384]{1,0:T(8,128)(2,1)S(1)}, bf16[192,384]{1,0:T(8,128)(2,1)S(1)}, u32[]{:S(2)}, u32[]{:S(2)}) %collective-permute-start.11) | collective-permute-done | bytes 147488 | tf_op jit(solution)/shard_map/ppermute | solution.py:534
  52.8 2.2 collective-permute-start.14
  55.0 0.7 collective-permute-done.12.refs_2_
  55.7 1.2 collective-permute-start.15
  57.4 1.8 collective-permute-done.14.refs_4_
  59.2 2.5 collective-permute-done.15.refs_5_
  61.6 2.2 shard_map.88.refs_1_
  63.8 1.8 collective-permute-start.17
  65.7 1.5 collective-permute-start.18
  67.3 1.5 collective-permute-start.19
  68.8 12.7 %collective-permute-done.17.refs_1_ = bf16[768,384]{1,0:T(8,128)(2,1)S(1)} collective-permute-done((bf16[768,384]{1,0:T(8,128)(2,1)S(1)}, bf16[768,384]{1,0:T(8,128)(2,1)S(1)}, u32[]{:S(2)}, u32[]{:S(2)}) %collective-permute-start.17) | collective-permute-done | bytes 589856 | tf_op jit(solution)/shard_map/ppermute | solution.py:541
  82.0 2.0 collective-permute-done.20.refs_2_
  84.0 16.3 %collective-permute-done.18.refs_1_ = bf16[720,1024]{1,0:T(8,128)(2,1)S(1)} collective-permute-done((bf16[720,1024]{1,0:T(8,128)(2,1)S(1)}, bf16[720,1024]{1,0:T(8,128)(2,1)S(1)}, u32[]{:S(2)}, u32[]{:S(2)}) %collective-permute-start.18) | collective-permute-done | bytes 1474592 | tf_op jit(solution)/shard_map/ppermute | solution.py:534
  100.4 1.1 collective-permute-done.19.refs_2_
  101.5 6.0 %collective-permute-done.9.refs_0_ = bf16[768,640]{1,0:T(8,128)(2,1)S(1)} collective-permute-done((bf16[768,640]{1,0:T(8,128)(2,1)S(1)}, bf16[768,640]{1,0:T(8,128)(2,1)S(1)}, u32[]{:S(2)}, u32[]{:S(2)}) %collective-permute-start.9) | collective-permute-done | bytes 983072 | tf_op jit(solution)/shard_map/ppermute | solution.py:541
  107.6 1.6 collective-permute-start.27
  109.2 1.6 collective-permute-start.28
  110.8 14.4 %collective-permute-done.27.refs_3_ = bf16[720,512]{1,0:T(8,128)(2,1)S(1)} collective-permute-done((bf16[720,512]{1,0:T(8,128)(2,1)S(1)}, bf16[720,512]{1,0:T(8,128)(2,1)S(1)}, u32[]{:S(2)}, u32[]{:S(2)}) %collective-permute-start.27) | collective-permute-done | bytes 737312 | tf_op jit(solution)/shard_map/ppermute | solution.py:534
  125.3 1.4 collective-permute-done.28.refs_4_
  126.6 6.8 %shard_map.89 = (bf16[720,4096]{1,0:T(8,128)(2,1)S(1)}, bf16[720,192]{1,0:T(8,128)(2,1)S(1)}) custom-call(s32[10]{0:T(128)S(1)} %stack.43.meta, bf16[720,1024]{1,0:T(8,128)(2,1)S(1)} %pad_maximum_fusion.refs_0_, bf16[720,1024]{1,0:T(8,128)(2,1)S(1)} %collective-permute-done.18.refs_1_, bf16[720,1024]{1,0:T(8,128)(2,1)S(1)} %collective-permute-done.19.refs_2_, ...), custom_call_target="tpu_custom_call" | custom-call | flops 283115520 | bytes 737280 | tf_op jit(solution)/shard_map/pallas_call | solution.py:282
  133.4 5.1 %shard_map.90 = (f32[720,1536]{1,0:T(8,128)S(1)}, bf16[1536,4096]{1,0:T(8,128)(2,1)S(1)}) custom-call(s32[10]{0:T(128)S(1)} %stack.43.meta, bf16[768,640]{1,0:T(8,128)(2,1)S(1)} %get-tuple-element.143.refs_0_, bf16[768,384]{1,0:T(8,128)(2,1)S(1)} %shard_map.88.refs_1_, bf16[768,640]{1,0:T(8,128)(2,1)S(1)} %collective-permute-done.20.refs_2_, ...), custom_call_target="tpu_custom_call" | custom-call | flops 141557760 | bytes 946176 | tf_op jit(solution)/shard_map/pallas_call | solution.py:386
  138.6 6.3 %shard_map.91 = (f32[720,1536]{1,0:T(8,128)S(1)}, bf16[1536,4096]{1,0:T(8,128)(2,1)S(1)}) custom-call(s32[10]{0:T(128)S(1)} %stack.43.meta, bf16[768,640]{1,0:T(8,128)(2,1)S(1)} %collective-permute-done.8.refs_0_, bf16[768,384]{1,0:T(8,128)(2,1)S(1)} %collective-permute-done.17.refs_1_, ...), custom_call_target="tpu_custom_call", output_to_operand_aliasing={{0}: (6, {}), {1}: (7, {})} | custom-call | flops 141557760 | bytes 946176 | tf_op jit(solution)/shard_map/pallas_call | solution.py:386
  145.5 2.9 %collective-permute-done.32.refs_3_ = bf16[768,384]{1,0:T(8,128)(2,1)S(1)} collective-permute-done((bf16[768,384]{1,0:T(8,128)(2,1)S(1)}, bf16[768,384]{1,0:T(8,128)(2,1)S(1)}, u32[]{:S(2)}, u32[]{:S(2)}) %collective-permute-start.32) | collective-permute-done | bytes 589856 | tf_op jit(solution)/shard_map/ppermute | solution.py:534
  148.4 5.4 %shard_map.92 = (f32[720,1536]{1,0:T(8,128)S(1)}, bf16[1536,4096]{1,0:T(8,128)(2,1)S(1)}) custom-call(s32[10]{0:T(128)S(1)} %stack.43.meta, bf16[768,640]{1,0:T(8,128)(2,1)S(1)} %collective-permute-done.9.refs_0_, bf16[768,384]{1,0:T(8,128)(2,1)S(1)} %collective-permute-done.25.refs_1_, ...), custom_call_target="tpu_custom_call", output_to_operand_aliasing={{0}: (6, {}), {1}: (7, {})} | custom-call | flops 141557760 | bytes 946176 | tf_op jit(solution)/shard_map/pallas_call | solution.py:386
  153.9 4.4 %shard_map.93.refs_5_ = f32[720,1536]{1,0:T(8,128)S(1)} custom-call(s32[10]{0:T(128)S(1)} %stack.43.meta, bf16[768,640]{1,0:T(8,128)(2,1)S(1)} %collective-permute-done.24.refs_0_, bf16[768,640]{1,0:T(8,128)(2,1)S(1)} %collective-permute-done.30.refs_1_.refs_2_, ...), custom_call_target="tpu_custom_call", output_to_operand_aliasing={{}: (4, {})} | custom-call | flops 141557760 | bytes 946176 | tf_op jit(solution)/shard_map/pallas_call | solution.py:386
  158.3 4.4 %collective-permute-done.29.refs_1_ = bf16[768,384]{1,0:T(8,128)(2,1)S(1)} collective-permute-done((bf16[768,384]{1,0:T(8,128)(2,1)S(1)}, bf16[768,384]{1,0:T(8,128)(2,1)S(1)}, u32[]{:S(2)}, u32[]{:S(2)}) %collective-permute-start.29) | collective-permute-done | bytes 589856 | tf_op jit(solution)/shard_map/ppermute | solution.py:541
  162.6 2.0 collective-permute-done.33.refs_3_
  164.6 5.9 %shard_map.94 = (f32[720,1536]{1,0:T(8,128)S(1)}, f32[8,1536]{1,0:T(8,128)S(1)}, bf16[1536,4096]{1,0:T(8,128)(2,1)S(1)}) custom-call(s32[10]{0:T(128)S(1)} %stack.43.meta, bf16[768,640]{1,0:T(8,128)(2,1)S(1)} %collective-permute-done.24.refs_0_, bf16[768,384]{1,0:T(8,128)(2,1)S(1)} %collective-permute-done.29.refs_1_, ...), custom_call_target="tpu_custom_call", output_to_operand_aliasing={{0}: (6, {}), {2}: (7, {})} | custom-call | flops 141557760 | bytes 946176 | tf_op jit(solution)/shard_map/pallas_call | solution.py:386
  170.8 1.1 collective-permute-done.34.other_ref
  172.5 2.3 collective-permute-start.36
  174.8 2.1 collective-permute-start.37
  177.2 1.2 collective-permute-done.36.refs_4_
  178.4 2.3 collective-permute-done.37.refs_5_
  180.7 4.2 %shard_map.96 = (bf16[720,512]{1,0:T(8,128)(2,1)S(1)}, bf16[720,512]{1,0:T(8,128)(2,1)S(1)}, bf16[720,1536]{1,0:T(8,128)(2,1)S(1)}, f32[1,768]{1,0:T(1,128)S(1)}, bf16[64,720]{1,0:T(8,128)(2,1)S(1)}) custom-call(s32[10]{0:T(128)S(1)} %stack.43.meta, f32[720,1536]{1,0:T(8,128)S(1)} %get-tuple-element.188.refs_0_, ...), custom_call_target="tpu_custom_call" | custom-call | flops 141557760 | bytes 657408 | tf_op jit(solution)/shard_map/pallas_call | solution.py:474
  184.9 1.6 collective-permute-start.38
  187.7 10.7 %shard_map.97 = (bf16[720,512]{1,0:T(8,128)(2,1)}, bf16[720,512]{1,0:T(8,128)(2,1)}, bf16[720,512]{1,0:T(8,128)(2,1)}, f32[720,512]{1,0:T(8,128)S(1)}, f32[720,512]{1,0:T(8,128)S(1)}, /*index=5*/f32[720,512]{1,0:T(8,128)S(1)}) custom-call(s32[10]{0:T(128)S(1)} %stack.43.meta, bf16[720,1536]{1,0:T(8,128)(2,1)S(1)} %get-tuple-element.193.refs_0_, ...), custom_call_target="tpu_custom_call" | custom-call | flops 424673280 | bytes 1419264 | tf_op jit(solution)/shard_map/pallas_call | solution.py:474
  198.4 5.8 %collective-permute-done.40.other_ref = bf16[64,720]{1,0:T(8,128)(2,1)S(1)} collective-permute-done((bf16[64,720]{1,0:T(8,128)(2,1)S(1)}, bf16[64,720]{1,0:T(8,128)(2,1)S(1)}, u32[]{:S(2)}, u32[]{:S(2)}) %collective-permute-start.40) | collective-permute-done | bytes 92192 | tf_op jit(solution)/shard_map/ppermute | solution.py:534
  205.4 4.1 %collective-permute-done.46 = bf16[64,720]{1,0:T(8,128)(2,1)S(1)} collective-permute-done((bf16[64,720]{1,0:T(8,128)(2,1)S(1)}, bf16[64,720]{1,0:T(8,128)(2,1)S(1)}, u32[]{:S(2)}, u32[]{:S(2)}) %collective-permute-start.46) | collective-permute-done | bytes 92192 | tf_op jit(solution)/shard_map/ppermute | solution.py:534
  209.6 1.7 fusion.3
  211.8 1.5 collective-permute-start.41
  213.4 1.6 collective-permute-start.43
  215.7 0.9 maximum_select_fusion
  216.6 13.6 %collective-permute-done.42.a_ref = bf16[720,512]{1,0:T(8,128)(2,1)S(1)} collective-permute-done((bf16[720,512]{1,0:T(8,128)(2,1)}, bf16[720,512]{1,0:T(8,128)(2,1)S(1)}, u32[]{:S(2)}, u32[]{:S(2)}) %collective-permute-start.42) | collective-permute-done | bytes 737312 | tf_op jit(solution)/shard_map/ppermute | solution.py:538
  230.2 1.2 collective-permute-done.41.c_ref
  231.4 2.3 shard_map.98
  233.7 13.1 %collective-permute-done.45 = bf16[720,512]{1,0:T(8,128)(2,1)} collective-permute-done((bf16[720,512]{1,0:T(8,128)(2,1)}, bf16[720,512]{1,0:T(8,128)(2,1)}, u32[]{:S(2)}, u32[]{:S(2)}) %collective-permute-start.45) | collective-permute-done | bytes 737312 | tf_op jit(solution)/shard_map/ppermute | solution.py:538
  246.8 2.9 %add_dynamic-update-slice_fusion = f32[1440,512]{1,0:T(8,128)} fusion(f32[1440,512]{1,0:T(8,128)} %shard_map.98, s32[]{:T(128)S(6)} %select_n.65, bf16[720,512]{1,0:T(8,128)(2,1)} %collective-permute-done.45, bf16[720,512]{1,0:T(8,128)(2,1)} %collective-permute-done.44, bf16[720,512]{1,0:T(8,128)(2,1)} %collective-permute-done.43), kind=kLoop, calls=%fused_computation.7 | loop fusion | flops 1843200 | bytes 3686404 | tf_op jit(solution)/shard_map/dynamic_update_slice | solution.py:635
  (63 shorter events, 9.2 us)
Async XLA Ops:
  0.6 16.6 %collective-permute-start.7 = (bf16[1440,512]{1,0:T(8,128)(2,1)}, bf16[1440,512]{1,0:T(8,128)(2,1)}, u32[]{:S(2)}, u32[]{:S(2)}) collective-permute-start(bf16[1440,512]{1,0:T(8,128)(2,1)} %param.11), channel_id=1, source_target_pairs={{0,4},{4,0},{8,12},{12,8},{16,20},{20,16},{24,28},{28,24},{1,5},{5... | collective-permute-start | bytes 4423688 | tf_op jit(solution)/shard_map/ppermute | solution.py:534
  9.2 12.5 %collective-permute-start = (bf16[208,640]{1,0:T(8,128)(2,1)S(1)}, bf16[208,640]{1,0:T(8,128)(2,1)S(1)}, u32[]{:S(2)}, u32[]{:S(2)}) collective-permute-start(bf16[208,640]{1,0:T(8,128)(2,1)S(1)} %get-tuple-element.107), channel_id=1, source_target_pairs={{0,24},{4,28},{8,16},{12,20},{16,8},{20,12},{24,0},{28,4},{1,25},{... | collective-permute-start | bytes 798728 | tf_op jit(solution)/shard_map/ppermute | solution.py:534
  12.8 12.6 %collective-permute-start.1 = (bf16[208,640]{1,0:T(8,128)(2,1)S(1)}, bf16[208,640]{1,0:T(8,128)(2,1)S(1)}, u32[]{:S(2)}, u32[]{:S(2)}) collective-permute-start(bf16[208,640]{1,0:T(8,128)(2,1)S(1)} %get-tuple-element.108), channel_id=1, source_target_pairs={{0,28},{4,24},{8,20},{12,16},{16,12},{20,8},{24,4},{28,0},{1,29},{... | collective-permute-start | bytes 798728 | tf_op jit(solution)/shard_map/ppermute | solution.py:534
  12.9 18.4 %collective-permute-start.2 = (bf16[208,640]{1,0:T(8,128)(2,1)S(1)}, bf16[208,640]{1,0:T(8,128)(2,1)S(1)}, u32[]{:S(2)}, u32[]{:S(2)}) collective-permute-start(bf16[208,640]{1,0:T(8,128)(2,1)S(1)} %get-tuple-element.109), channel_id=1, source_target_pairs={{0,16},{4,20},{8,24},{12,28},{16,0},{20,4},{24,8},{28,12},{1,17},{... | collective-permute-start | bytes 798728 | tf_op jit(solution)/shard_map/ppermute | solution.py:534
  14.6 17.4 %collective-permute-start.3 = (bf16[208,640]{1,0:T(8,128)(2,1)S(1)}, bf16[208,640]{1,0:T(8,128)(2,1)S(1)}, u32[]{:S(2)}, u32[]{:S(2)}) collective-permute-start(bf16[208,640]{1,0:T(8,128)(2,1)S(1)} %get-tuple-element.110), channel_id=1, source_target_pairs={{0,8},{4,12},{8,0},{12,4},{16,24},{20,28},{24,16},{28,20},{1,9},{5... | collective-permute-start | bytes 798728 | tf_op jit(solution)/shard_map/ppermute | solution.py:534
  17.2 19.6 %collective-permute-start.4 = (bf16[208,640]{1,0:T(8,128)(2,1)S(1)}, bf16[208,640]{1,0:T(8,128)(2,1)S(1)}, u32[]{:S(2)}, u32[]{:S(2)}) collective-permute-start(bf16[208,640]{1,0:T(8,128)(2,1)S(1)} %get-tuple-element.111), channel_id=1, source_target_pairs={{0,20},{4,16},{8,28},{12,24},{16,4},{20,0},{24,12},{28,8},{1,21},{... | collective-permute-start | bytes 798728 | tf_op jit(solution)/shard_map/ppermute | solution.py:534
  21.8 15.1 %collective-permute-start.5 = (bf16[208,640]{1,0:T(8,128)(2,1)S(1)}, bf16[208,640]{1,0:T(8,128)(2,1)S(1)}, u32[]{:S(2)}, u32[]{:S(2)}) collective-permute-start(bf16[208,640]{1,0:T(8,128)(2,1)S(1)} %get-tuple-element.112), channel_id=1, source_target_pairs={{0,12},{4,8},{8,4},{12,0},{16,28},{20,24},{24,20},{28,16},{1,13},{... | collective-permute-start | bytes 798728 | tf_op jit(solution)/shard_map/ppermute | solution.py:534
  25.4 11.5 %collective-permute-start.6 = (bf16[208,640]{1,0:T(8,128)(2,1)S(1)}, bf16[208,640]{1,0:T(8,128)(2,1)S(1)}, u32[]{:S(2)}, u32[]{:S(2)}) collective-permute-start(bf16[208,640]{1,0:T(8,128)(2,1)S(1)} %get-tuple-element.113), channel_id=1, source_target_pairs={{0,4},{4,0},{8,12},{12,8},{16,20},{20,16},{24,28},{28,24},{1,5},{5... | collective-permute-start | bytes 798728 | tf_op jit(solution)/shard_map/ppermute | solution.py:534
  26.8 10.1 %copy-start = (f32[64,2048]{1,0:T(8,128)S(1)}, f32[64,2048]{1,0:T(8,128)}, u32[]{:S(2)}) copy-start(f32[64,2048]{1,0:T(8,128)} %refs_5_.1) | copy-start | bytes 1572868
  26.8 10.1 %copy-start.1 = (f32[2048]{0:T(1024)S(1)}, f32[2048]{0:T(1024)}, u32[]{:S(2)}) copy-start(f32[2048]{0:T(1024)} %param.10) | copy-start | bytes 24580
  41.1 40.4 %collective-permute-start.8 = (bf16[768,640]{1,0:T(8,128)(2,1)S(1)}, bf16[768,640]{1,0:T(8,128)(2,1)S(1)}, u32[]{:S(2)}, u32[]{:S(2)}) collective-permute-start(bf16[768,640]{1,0:T(8,128)(2,1)S(1)} %get-tuple-element.143.refs_0_), channel_id=1, source_target_pairs={{0,1},{1,2},{2,3},{3,0},{4,5},{5,6},{6,7},{7,4},{8,9},{9,10},{10,1... | collective-permute-start | bytes 2949128 | tf_op jit(solution)/shard_map/ppermute | solution.py:541
  42.9 6.7 %collective-permute-start.10 = (bf16[192,384]{1,0:T(8,128)(2,1)S(1)}, bf16[192,384]{1,0:T(8,128)(2,1)S(1)}, u32[]{:S(2)}, u32[]{:S(2)}) collective-permute-start(bf16[192,384]{1,0:T(8,128)(2,1)S(1)} %get-tuple-element.144), channel_id=1, source_target_pairs={{0,24},{4,28},{8,16},{12,20},{16,8},{20,12},{24,0},{28,4},{1,25},{... | collective-permute-start | bytes 442376 | tf_op jit(solution)/shard_map/ppermute | solution.py:534
  45.4 7.5 %collective-permute-start.11 = (bf16[192,384]{1,0:T(8,128)(2,1)S(1)}, bf16[192,384]{1,0:T(8,128)(2,1)S(1)}, u32[]{:S(2)}, u32[]{:S(2)}) collective-permute-start(bf16[192,384]{1,0:T(8,128)(2,1)S(1)} %get-tuple-element.145), channel_id=1, source_target_pairs={{0,28},{4,24},{8,20},{12,16},{16,12},{20,8},{24,4},{28,0},{1,29},{... | collective-permute-start | bytes 442376 | tf_op jit(solution)/shard_map/ppermute | solution.py:534
  45.4 10.4 %collective-permute-start.12 = (bf16[192,384]{1,0:T(8,128)(2,1)S(1)}, bf16[192,384]{1,0:T(8,128)(2,1)S(1)}, u32[]{:S(2)}, u32[]{:S(2)}) collective-permute-start(bf16[192,384]{1,0:T(8,128)(2,1)S(1)} %get-tuple-element.146), channel_id=1, source_target_pairs={{0,16},{4,20},{8,24},{12,28},{16,0},{20,4},{24,8},{28,12},{1,17},{... | collective-permute-start | bytes 442376 | tf_op jit(solution)/shard_map/ppermute | solution.py:534
  46.5 10.4 %collective-permute-start.13 = (bf16[192,384]{1,0:T(8,128)(2,1)S(1)}, bf16[192,384]{1,0:T(8,128)(2,1)S(1)}, u32[]{:S(2)}, u32[]{:S(2)}) collective-permute-start(bf16[192,384]{1,0:T(8,128)(2,1)S(1)} %get-tuple-element.147), channel_id=1, source_target_pairs={{0,8},{4,12},{8,0},{12,4},{16,24},{20,28},{24,16},{28,20},{1,9},{5... | collective-permute-start | bytes 442376 | tf_op jit(solution)/shard_map/ppermute | solution.py:534
  49.7 17.6 %collective-permute-start.23 = (bf16[192,768]{1,0:T(8,128)(2,1)S(1)}, bf16[192,768]{1,0:T(8,128)(2,1)S(1)}, u32[]{:S(2)}, u32[]{:S(2)}) collective-permute-start(bf16[192,768]{1,0:T(8,128)(2,1)S(1)} %get-tuple-element.185.refs_7_.refs_6_), channel_id=1, source_target_pairs={{0,4},{4,0},{8,12},{12,8},{16,20},{20,16},{24,28},{28,24},{1,5},{5... | collective-permute-start | bytes 884744 | tf_op jit(solution)/shard_map/ppermute | solution.py:534
  52.8 6.3 %collective-permute-start.14 = (bf16[192,384]{1,0:T(8,128)(2,1)S(1)}, bf16[192,384]{1,0:T(8,128)(2,1)S(1)}, u32[]{:S(2)}, u32[]{:S(2)}) collective-permute-start(bf16[192,384]{1,0:T(8,128)(2,1)S(1)} %get-tuple-element.148), channel_id=1, source_target_pairs={{0,20},{4,16},{8,28},{12,24},{16,4},{20,0},{24,12},{28,8},{1,21},{... | collective-permute-start | bytes 442376 | tf_op jit(solution)/shard_map/ppermute | solution.py:534
  55.7 5.9 %collective-permute-start.15 = (bf16[192,384]{1,0:T(8,128)(2,1)S(1)}, bf16[192,384]{1,0:T(8,128)(2,1)S(1)}, u32[]{:S(2)}, u32[]{:S(2)}) collective-permute-start(bf16[192,384]{1,0:T(8,128)(2,1)S(1)} %get-tuple-element.149), channel_id=1, source_target_pairs={{0,12},{4,8},{8,4},{12,0},{16,28},{20,24},{24,20},{28,16},{1,13},{... | collective-permute-start | bytes 442376 | tf_op jit(solution)/shard_map/ppermute | solution.py:534
  57.0 4.7 %collective-permute-start.16 = (bf16[192,384]{1,0:T(8,128)(2,1)S(1)}, bf16[192,384]{1,0:T(8,128)(2,1)S(1)}, u32[]{:S(2)}, u32[]{:S(2)}) collective-permute-start(bf16[192,384]{1,0:T(8,128)(2,1)S(1)} %get-tuple-element.150), channel_id=1, source_target_pairs={{0,4},{4,0},{8,12},{12,8},{16,20},{20,16},{24,28},{28,24},{1,5},{5... | collective-permute-start | bytes 442376 | tf_op jit(solution)/shard_map/ppermute | solution.py:534
  63.8 17.6 %collective-permute-start.17 = (bf16[768,384]{1,0:T(8,128)(2,1)S(1)}, bf16[768,384]{1,0:T(8,128)(2,1)S(1)}, u32[]{:S(2)}, u32[]{:S(2)}) collective-permute-start(bf16[768,384]{1,0:T(8,128)(2,1)S(1)} %shard_map.88.refs_1_), channel_id=1, source_target_pairs={{0,1},{1,2},{2,3},{3,0},{4,5},{5,6},{6,7},{7,4},{8,9},{9,10},{10,1... | collective-permute-start | bytes 1769480 | tf_op jit(solution)/shard_map/ppermute | solution.py:541
  65.7 16.3 %collective-permute-start.21 = (bf16[768,384]{1,0:T(8,128)(2,1)S(1)}, bf16[768,384]{1,0:T(8,128)(2,1)S(1)}, u32[]{:S(2)}, u32[]{:S(2)}) collective-permute-start(bf16[768,384]{1,0:T(8,128)(2,1)S(1)} %shard_map.88.refs_1_), channel_id=1, source_target_pairs={{0,4},{4,0},{8,12},{12,8},{16,20},{20,16},{24,28},{28,24},{1,5},{5... | collective-permute-start | bytes 1769480 | tf_op jit(solution)/shard_map/ppermute | solution.py:534
  65.7 34.6 %collective-permute-start.18 = (bf16[720,1024]{1,0:T(8,128)(2,1)S(1)}, bf16[720,1024]{1,0:T(8,128)(2,1)S(1)}, u32[]{:S(2)}, u32[]{:S(2)}) collective-permute-start(bf16[720,1024]{1,0:T(8,128)(2,1)S(1)} %pad_maximum_fusion.refs_0_), channel_id=1, source_target_pairs={{0,8},{4,12},{8,0},{12,4},{16,24},{20,28},{24,16},{28,20},{1,9},{5... | collective-permute-start | bytes 4423688 | tf_op jit(solution)/shard_map/ppermute | solution.py:534
  67.3 34.3 %collective-permute-start.19 = (bf16[720,1024]{1,0:T(8,128)(2,1)S(1)}, bf16[720,1024]{1,0:T(8,128)(2,1)S(1)}, u32[]{:S(2)}, u32[]{:S(2)}) collective-permute-start(bf16[720,1024]{1,0:T(8,128)(2,1)S(1)} %pad_maximum_fusion.refs_0_), channel_id=1, source_target_pairs={{0,16},{4,20},{8,24},{12,28},{16,0},{20,4},{24,8},{28,12},{1,17},{... | collective-permute-start | bytes 4423688 | tf_op jit(solution)/shard_map/ppermute | solution.py:534
  81.5 2.6 %collective-permute-start.20 = (bf16[768,640]{1,0:T(8,128)(2,1)S(1)}, bf16[768,640]{1,0:T(8,128)(2,1)S(1)}, u32[]{:S(2)}, u32[]{:S(2)}) collective-permute-start(bf16[768,640]{1,0:T(8,128)(2,1)S(1)} %get-tuple-element.143.refs_0_), channel_id=1, source_target_pairs={{0,4},{4,0},{8,12},{12,8},{16,20},{20,16},{24,28},{28,24},{1,5},{5... | collective-permute-start | bytes 2949128 | tf_op jit(solution)/shard_map/ppermute | solution.py:534
  81.5 20.0 %collective-permute-start.22 = (bf16[768,640]{1,0:T(8,128)(2,1)S(1)}, bf16[768,640]{1,0:T(8,128)(2,1)S(1)}, u32[]{:S(2)}, u32[]{:S(2)}) collective-permute-start(bf16[768,640]{1,0:T(8,128)(2,1)S(1)} %collective-permute-done.8.refs_0_), channel_id=1, source_target_pairs={{0,4},{4,0},{8,12},{12,8},{16,20},{20,16},{24,28},{28,24},{1,5},{5... | collective-permute-start | bytes 2949128 | tf_op jit(solution)/shard_map/ppermute | solution.py:534
  82.0 25.5 %collective-permute-start.9 = (bf16[768,640]{1,0:T(8,128)(2,1)S(1)}, bf16[768,640]{1,0:T(8,128)(2,1)S(1)}, u32[]{:S(2)}, u32[]{:S(2)}) collective-permute-start(bf16[768,640]{1,0:T(8,128)(2,1)S(1)} %collective-permute-done.8.refs_0_), channel_id=1, source_target_pairs={{0,1},{1,2},{2,3},{3,0},{4,5},{5,6},{6,7},{7,4},{8,9},{9,10},{10,1... | collective-permute-start | bytes 2949128 | tf_op jit(solution)/shard_map/ppermute | solution.py:541
  107.5 37.4 %collective-permute-start.24 = (bf16[768,640]{1,0:T(8,128)(2,1)S(1)}, bf16[768,640]{1,0:T(8,128)(2,1)S(1)}, u32[]{:S(2)}, u32[]{:S(2)}) collective-permute-start(bf16[768,640]{1,0:T(8,128)(2,1)S(1)} %collective-permute-done.9.refs_0_), channel_id=1, source_target_pairs={{0,1},{1,2},{2,3},{3,0},{4,5},{5,6},{6,7},{7,4},{8,9},{9,10},{10,1... | collective-permute-start | bytes 2949128 | tf_op jit(solution)/shard_map/ppermute | solution.py:541
  107.6 17.7 %collective-permute-start.27 = (bf16[720,512]{1,0:T(8,128)(2,1)S(1)}, bf16[720,512]{1,0:T(8,128)(2,1)S(1)}, u32[]{:S(2)}, u32[]{:S(2)}) collective-permute-start(bf16[720,512]{1,0:T(8,128)(2,1)S(1)} %slice.6), channel_id=1, source_target_pairs={{0,16},{4,20},{8,24},{12,28},{16,0},{20,4},{24,8},{28,12},{1,17},{... | collective-permute-start | bytes 2211848 | tf_op jit(solution)/shard_map/ppermute | solution.py:534
  109.2 17.4 %collective-permute-start.28 = (bf16[720,512]{1,0:T(8,128)(2,1)S(1)}, bf16[720,512]{1,0:T(8,128)(2,1)S(1)}, u32[]{:S(2)}, u32[]{:S(2)}) collective-permute-start(bf16[720,512]{1,0:T(8,128)(2,1)S(1)} %slice.7), channel_id=1, source_target_pairs={{0,8},{4,12},{8,0},{12,4},{16,24},{20,28},{24,16},{28,20},{1,9},{5... | collective-permute-start | bytes 2211848 | tf_op jit(solution)/shard_map/ppermute | solution.py:534
  110.8 27.7 %collective-permute-start.26 = (bf16[768,384]{1,0:T(8,128)(2,1)S(1)}, bf16[768,384]{1,0:T(8,128)(2,1)}, u32[]{:S(2)}, u32[]{:S(2)}) collective-permute-start(bf16[768,384]{1,0:T(8,128)(2,1)S(1)} %collective-permute-done.17.refs_1_), channel_id=1, source_target_pairs={{0,4},{4,0},{8,12},{12,8},{16,20},{20,16},{24,28},{28,24},{1,5},{5... | collective-permute-start | bytes 1769480 | tf_op jit(solution)/shard_map/ppermute | solution.py:534
  110.8 34.1 %collective-permute-start.25 = (bf16[768,384]{1,0:T(8,128)(2,1)S(1)}, bf16[768,384]{1,0:T(8,128)(2,1)S(1)}, u32[]{:S(2)}, u32[]{:S(2)}) collective-permute-start(bf16[768,384]{1,0:T(8,128)(2,1)S(1)} %collective-permute-done.17.refs_1_), channel_id=1, source_target_pairs={{0,1},{1,2},{2,3},{3,0},{4,5},{5,6},{6,7},{7,4},{8,9},{9,10},{10,1... | collective-permute-start | bytes 1769480 | tf_op jit(solution)/shard_map/ppermute | solution.py:541
  125.3 20.3 %collective-permute-start.31 = (bf16[768,640]{1,0:T(8,128)(2,1)S(1)}, bf16[768,640]{1,0:T(8,128)(2,1)S(1)}, u32[]{:S(2)}, u32[]{:S(2)}) collective-permute-start(bf16[768,640]{1,0:T(8,128)(2,1)S(1)} %collective-permute-done.9.refs_0_), channel_id=1, source_target_pairs={{0,4},{4,0},{8,12},{12,8},{16,20},{20,16},{24,28},{28,24},{1,5},{5... | collective-permute-start | bytes 2949128 | tf_op jit(solution)/shard_map/ppermute | solution.py:534
  144.9 8.9 %collective-permute-start.30 = (bf16[768,640]{1,0:T(8,128)(2,1)S(1)}, bf16[768,640]{1,0:T(8,128)(2,1)S(1)}, u32[]{:S(2)}, u32[]{:S(2)}) collective-permute-start(bf16[768,640]{1,0:T(8,128)(2,1)S(1)} %collective-permute-done.24.refs_0_), channel_id=1, source_target_pairs={{0,4},{4,0},{8,12},{12,8},{16,20},{20,16},{24,28},{28,24},{1,5},{5... | collective-permute-start | bytes 2949128 | tf_op jit(solution)/shard_map/ppermute | solution.py:534
  145.0 3.4 %collective-permute-start.32 = (bf16[768,384]{1,0:T(8,128)(2,1)S(1)}, bf16[768,384]{1,0:T(8,128)(2,1)S(1)}, u32[]{:S(2)}, u32[]{:S(2)}) collective-permute-start(bf16[768,384]{1,0:T(8,128)(2,1)S(1)} %collective-permute-done.25.refs_1_), channel_id=1, source_target_pairs={{0,4},{4,0},{8,12},{12,8},{16,20},{20,16},{24,28},{28,24},{1,5},{5... | collective-permute-start | bytes 1769480 | tf_op jit(solution)/shard_map/ppermute | solution.py:534
  145.5 17.1 %collective-permute-start.29 = (bf16[768,384]{1,0:T(8,128)(2,1)S(1)}, bf16[768,384]{1,0:T(8,128)(2,1)S(1)}, u32[]{:S(2)}, u32[]{:S(2)}) collective-permute-start(bf16[768,384]{1,0:T(8,128)(2,1)S(1)} %collective-permute-done.25.refs_1_), channel_id=1, source_target_pairs={{0,1},{1,2},{2,3},{3,0},{4,5},{5,6},{6,7},{7,4},{8,9},{9,10},{10,1... | collective-permute-start | bytes 1769480 | tf_op jit(solution)/shard_map/ppermute | solution.py:541
  162.6 2.0 collective-permute-start.33
  170.6 1.3 collective-permute-start.34
  172.4 4.8 %collective-permute-start.35 = (f32[8,1536]{1,0:T(8,128)S(1)}, f32[8,1536]{1,0:T(8,128)S(1)}, u32[]{:S(2)}, u32[]{:S(2)}) collective-permute-start(f32[8,1536]{1,0:T(8,128)S(1)} %shard_map.95.refs_2_), channel_id=1, source_target_pairs={{0,1},{1,0},{2,3},{3,2},{4,5},{5,4},{6,7},{7,6},{8,9},{9,8},{10,11... | collective-permute-start | bytes 147464 | tf_op jit(solution)/shard_map/ppermute | solution.py:608
  172.5 5.9 %collective-permute-start.36 = (f32[8,1536]{1,0:T(8,128)S(1)}, f32[8,1536]{1,0:T(8,128)S(1)}, u32[]{:S(2)}, u32[]{:S(2)}) collective-permute-start(f32[8,1536]{1,0:T(8,128)S(1)} %shard_map.95.refs_2_), channel_id=1, source_target_pairs={{0,2},{1,3},{2,0},{3,1},{4,6},{5,7},{6,4},{7,5},{8,10},{9,11},{10,... | collective-permute-start | bytes 147464 | tf_op jit(solution)/shard_map/ppermute | solution.py:608
  174.8 5.9 %collective-permute-start.37 = (f32[8,1536]{1,0:T(8,128)S(1)}, f32[8,1536]{1,0:T(8,128)S(1)}, u32[]{:S(2)}, u32[]{:S(2)}) collective-permute-start(f32[8,1536]{1,0:T(8,128)S(1)} %shard_map.95.refs_2_), channel_id=1, source_target_pairs={{0,3},{1,2},{2,1},{3,0},{4,7},{5,6},{6,5},{7,4},{8,11},{9,10},{10,... | collective-permute-start | bytes 147464 | tf_op jit(solution)/shard_map/ppermute | solution.py:608
  184.9 19.3 %collective-permute-start.38 = (bf16[720,512]{1,0:T(8,128)(2,1)S(1)}, bf16[720,512]{1,0:T(8,128)(2,1)S(1)}, u32[]{:S(2)}, u32[]{:S(2)}) collective-permute-start(bf16[720,512]{1,0:T(8,128)(2,1)S(1)} %get-tuple-element.191), channel_id=1, source_target_pairs={{0,8},{4,12},{8,0},{12,4},{16,24},{20,28},{24,16},{28,20},{1,9},{5... | collective-permute-start | bytes 2211848 | tf_op jit(solution)/shard_map/ppermute | solution.py:534
  186.5 17.7 %collective-permute-start.39 = (bf16[720,512]{1,0:T(8,128)(2,1)S(1)}, bf16[720,512]{1,0:T(8,128)(2,1)S(1)}, u32[]{:S(2)}, u32[]{:S(2)}) collective-permute-start(bf16[720,512]{1,0:T(8,128)(2,1)S(1)} %get-tuple-element.192), channel_id=1, source_target_pairs={{0,16},{4,20},{8,24},{12,28},{16,0},{20,4},{24,8},{28,12},{1,17},{... | collective-permute-start | bytes 2211848 | tf_op jit(solution)/shard_map/ppermute | solution.py:534
  187.1 17.1 %collective-permute-start.40 = (bf16[64,720]{1,0:T(8,128)(2,1)S(1)}, bf16[64,720]{1,0:T(8,128)(2,1)S(1)}, u32[]{:S(2)}, u32[]{:S(2)}) collective-permute-start(bf16[64,720]{1,0:T(8,128)(2,1)S(1)} %get-tuple-element.200.mine_ref), channel_id=1, source_target_pairs={{0,8},{4,12},{8,0},{12,4},{16,24},{20,28},{24,16},{28,20},{1,9},{5... | collective-permute-start | bytes 276488 | tf_op jit(solution)/shard_map/ppermute | solution.py:534
  204.8 4.7 %collective-permute-start.46 = (bf16[64,720]{1,0:T(8,128)(2,1)S(1)}, bf16[64,720]{1,0:T(8,128)(2,1)S(1)}, u32[]{:S(2)}, u32[]{:S(2)}) collective-permute-start(bf16[64,720]{1,0:T(8,128)(2,1)S(1)} %shard_map.99), channel_id=1, source_target_pairs={{0,16},{4,20},{8,24},{12,28},{16,0},{20,4},{24,8},{28,12},{1,17},{... | collective-permute-start | bytes 276488 | tf_op jit(solution)/shard_map/ppermute | solution.py:534
  209.5 5.4 %collective-permute-start.47 = (f32[64,720]{1,0:T(8,128)S(1)}, f32[64,720]{1,0:T(8,128)S(1)}, u32[]{:S(2)}, u32[]{:S(2)}) collective-permute-start(f32[64,720]{1,0:T(8,128)S(1)} %convert_add_fusion), channel_id=1, source_target_pairs={{0,4},{4,0},{8,12},{12,8},{16,20},{20,16},{24,28},{28,24},{1,5},{5... | collective-permute-start | bytes 552968 | tf_op jit(solution)/shard_map/ppermute | solution.py:534
  211.3 18.9 %collective-permute-start.42 = (bf16[720,512]{1,0:T(8,128)(2,1)}, bf16[720,512]{1,0:T(8,128)(2,1)S(1)}, u32[]{:S(2)}, u32[]{:S(2)}) collective-permute-start(bf16[720,512]{1,0:T(8,128)(2,1)} %get-tuple-element.212), channel_id=1, source_target_pairs={{0,16},{4,12},{8,24},{12,4},{16,0},{20,28},{24,8},{28,20},{1,17},{... | collective-permute-start | bytes 2211848 | tf_op jit(solution)/shard_map/ppermute | solution.py:538
  211.8 19.6 %collective-permute-start.41 = (bf16[720,512]{1,0:T(8,128)(2,1)}, bf16[720,512]{1,0:T(8,128)(2,1)S(1)}, u32[]{:S(2)}, u32[]{:S(2)}) collective-permute-start(bf16[720,512]{1,0:T(8,128)(2,1)} %get-tuple-element.202), channel_id=1, source_target_pairs={{0,8},{4,20},{8,0},{12,28},{16,24},{20,4},{24,16},{28,12},{1,9},{5... | collective-permute-start | bytes 2211848 | tf_op jit(solution)/shard_map/ppermute | solution.py:538
  213.3 33.5 %collective-permute-start.45 = (bf16[720,512]{1,0:T(8,128)(2,1)}, bf16[720,512]{1,0:T(8,128)(2,1)}, u32[]{:S(2)}, u32[]{:S(2)}) collective-permute-start(bf16[720,512]{1,0:T(8,128)(2,1)} %get-tuple-element.211), channel_id=1, source_target_pairs={{0,12},{4,16},{8,4},{12,24},{16,28},{20,0},{24,20},{28,8},{1,13},{... | collective-permute-start | bytes 2211848 | tf_op jit(solution)/shard_map/ppermute | solution.py:538
  213.4 33.4 %collective-permute-start.43 = (bf16[720,512]{1,0:T(8,128)(2,1)}, bf16[720,512]{1,0:T(8,128)(2,1)}, u32[]{:S(2)}, u32[]{:S(2)}) collective-permute-start(bf16[720,512]{1,0:T(8,128)(2,1)} %get-tuple-element.206), channel_id=1, source_target_pairs={{0,4},{4,0},{8,12},{12,8},{16,20},{20,16},{24,28},{28,24},{1,5},{5... | collective-permute-start | bytes 2211848 | tf_op jit(solution)/shard_map/ppermute | solution.py:534
  215.0 31.9 %collective-permute-start.44 = (bf16[720,512]{1,0:T(8,128)(2,1)}, bf16[720,512]{1,0:T(8,128)(2,1)}, u32[]{:S(2)}, u32[]{:S(2)}) collective-permute-start(bf16[720,512]{1,0:T(8,128)(2,1)} %get-tuple-element.207), channel_id=1, source_target_pairs={{0,20},{4,8},{8,28},{12,0},{16,4},{20,24},{24,12},{28,16},{1,21},{... | collective-permute-start | bytes 2211848 | tf_op jit(solution)/shard_map/ppermute | solution.py:538

commit v10 on v9

--- a/solution.py
+++ b/solution.py
@@ -236,6 +236,7 @@
         whole((rows, width)),
         sds((rows, width), BF16),
         scratch=[pltpu.VMEM((slots, width), BF16)],
+        room=28,
         flops=2 * slots * rows * width,
         moved=2 * slots * width,
     )(meta, *recv, pick, wide, ctf, inv)
@@ -541,7 +542,7 @@
         return lax.ppermute(value, "rot", [(i, (i + 1) % turns) for i in range(turns)])
 
     width = columns // turns
-    cut = width * 5 // 8
+    cut = width * 3 // 8
     chunk_a, chunk_b = (0, cut), (cut, width - cut)
 
     def exchange(blocks):
@@ -564,26 +565,28 @@
     share_a, hot, pick, wide = unpack_first(meta, recv_a, ctf_table, inv, width, chunk_a)
     share_a, send_b = together((share_a, send_b))
     a1, recv_b = onward(share_a), exchange(send_b)
-    recv_b, near = together((recv_b, near))
+    a1, recv_b[:2] = together((a1, recv_b[:2]))
+    a2 = onward(a1)
+    share_b = unpack_next(meta, pick, wide, recv_b, ctf_table, inv, width, chunk_b)
+    a2, share_b, near = together((a2, share_b, near))
     by_x, by_y = across(near, 2), across(near, 4)
-    share_b = unpack_next(meta, pick, wide, recv_b, ctf_table, inv, width, chunk_b)
-    a2, b1 = onward(a1), onward(share_b)
+    a3, b1 = onward(a2), onward(share_b)
     sib0, sib1, hots = [across(share_a, 1), across(share_b, 1)], [across(a1, 1)], [hot, across(hot, 1)]
-    a2, b1, by_x, by_y, sib0, sib1, hots = together((a2, b1, by_x, by_y, sib0, sib1, hots))
-    sib1 = sib1 + [across(b1, 1)]
+    a3, b1, by_x, by_y, sib0, sib1, hots = together((a3, b1, by_x, by_y, sib0, sib1, hots))
+    sib1, sib2 = sib1 + [across(b1, 1)], [across(a2, 1)]
     piece = near.shape[1] // 2
     far_y, far_x = across(by_x[:, :piece], 4), across(by_y[:, piece:], 2)
-    a3, b2 = onward(a2), onward(b1)
+    b2 = onward(b1)
     panel_full, extra = energy(meta, [near, by_x, by_y, far_y, far_x], ctf_table, inv)
+    b2, panel_full, extra, sib1, sib2 = together((b2, panel_full, extra, sib1, sib2))
+    b3 = onward(b2)
+    sib2 = sib2 + [across(b2, 1)]
 
     def share(turn):
         return lambda m: lax.rem(m[1] + turns - turn, turns)
 
     acc, full = score(meta, share(0), [share_a, share_b], sib0, panel_full, width)
     acc, full = score(meta, share(1), [a1, b1], sib1, panel_full, width, acc, full)
-    a3, b2, acc, full = together((a3, b2, acc, full))
-    b3 = onward(b2)
-    sib2 = [across(a2, 1), across(b2, 1)]
     acc, full = score(meta, share(2), [a2, b2], sib2, panel_full, width, acc, full)
     final = share(turns - 1)
     a3_sib = across(a3, 1)
@@ -623,6 +626,7 @@
     message_b = (b_sum + jnp.where(even, left, down)).astype(BF16)
     got_a, got_b = by_core(message_a, 4, 2), by_core(message_b, 3, 5)
     got_self = across(give, 1)
+    mass_y, got_a, got_c = together((mass_y, got_a, got_c))
     mass = mass.astype(F32) + mass_y.astype(F32)
     mass_other = across(mass, 1)
     bin_weights = jnp.where(
@@ -631,6 +635,7 @@
         jnp.concatenate([mass_other, mass], axis=1),
     )
     sums = own_half(meta, keep, got_c, got_a)
+    bin_weights, got_b = together((bin_weights, got_b))
     other_half = got_self.astype(F32) + got_d.astype(F32) + got_b.astype(F32)
     class_sums = lax.dynamic_update_slice_in_dim(sums, other_half, (1 - core) * count, 0).T
     return class_sums, bin_weights, log_evidence.reshape(-1)

time: 250 us -> 241 us (0.964)
  waiting for transfers between devices: 129 us -> 124 us
  starting transfers between devices: 40 us -> 36.7 us
    ppermute x4, waiting for transfers between devices: 27.9 us -> 6.75 us  [by_core(): return lax.ppermute(value, 'dom', pairs)]
    ppermute x6, waiting for transfers between devices: 23 us -> 43.4 us  [onward(): lax.ppermute(value, 'rot', [(i, (i + 1) % turns) for i in range(turns)])]
    ppermute x35, waiting for transfers between devices: 73.9 us -> 70.3 us  [across(): return lax.ppermute(value, 'dom', [(i, i ^ apart) for i in range(dom)])]
    ppermute x35, starting transfers between devices: 29.7 us -> 26.1 us  [across(): return lax.ppermute(value, 'dom', [(i, i ^ apart) for i in range(dom)])]
  transfers between devices with their start and end apart: 48 -> 48, of which waited for: 28 -> 25; matrix products, arithmetic and copies ran while one was open for 3% -> 2% of each run, Pallas kernels for 22% -> 23%
where the time goes in v10:
time: 241 us; the launch traced here: 240 us
  waiting for transfers between devices  124 us (51%)
  Pallas kernels  69.7 us (29%)
  starting transfers between devices  36.7 us (15%)
  other arithmetic  6.82 us (3%)
    ppermute x35, waiting for transfers between devices, across(): return lax.ppermute(value, 'dom', [(i, i ^ apart) for i in range(dom)])  70.3 us
    ppermute x6, waiting for transfers between devices, onward(): lax.ppermute(value, 'rot', [(i, (i + 1) % turns) for i in range(turns)])  43.4 us
    pallas_call x5, Pallas kernels, score(): call(functools.partial(score_body, parts, used, first, last), (2 * half,)...  26.3 us
    ppermute x35, starting transfers between devices, across(): return lax.ppermute(value, 'dom', [(i, i ^ apart) for i in range(dom)])  26.1 us
    pallas_call x2, Pallas kernels, class_part(): call(functools.partial(class_body, kind, steps), (steps,), in_specs, out_...  15 us
    pallas_call x1, Pallas kernels, energy(): call(functools.partial(energy_body, bins, count), (count,), [pl.BlockSpec...  6.8 us
    ppermute x4, waiting for transfers between devices, by_core(): return lax.ppermute(value, 'dom', pairs)  6.75 us
    pallas_call x1, Pallas kernels, pack_next(): call(functools.partial(pack_next_body, cap, dom), (1,), [pl.BlockSpec((1,...  5.9 us
  transfers between devices with their start and end apart: 48, of which 25 were waited for; matrix products, arithmetic and copies ran while one was open for 2% of the time, Pallas kernels for 23%

profile of v10, /device:TPU:0, one launch (start us, length us, event | category | flops | bytes accessed | tf_op | source)
XLA Modules:
  0.0 240.0 jit_solution(53917814861148904)
XLA Ops:
  1.2 0.7 add_select_fusion.slot_ref
  2.0 5.8 %shard_map.85 = (bf16[208,384]{1,0:T(8,128)(2,1)S(1)}, bf16[208,384]{1,0:T(8,128)(2,1)S(1)}, bf16[208,384]{1,0:T(8,128)(2,1)S(1)}, bf16[208,384]{1,0:T(8,128)(2,...) custom-call(s32[10]{0:T(128)S(1)} %stack.43.meta, ...), custom_call_target="tpu_custom_call" | custom-call | flops 113246208 | bytes 147456 | tf_op jit(solution)/shard_map/pallas_call | solution.py:132
  7.7 3.6 %collective-permute-start = (bf16[208,384]{1,0:T(8,128)(2,1)S(1)}, bf16[208,384]{1,0:T(8,128)(2,1)S(1)}, u32[]{:S(2)}, u32[]{:S(2)}) collective-permute-start(bf16[208,384]{1,0:T(8,128)(2,1)S(1)} %get-tuple-element.111), channel_id=1, source_target_pairs={{0,24},{4,28},{8,16},{12,20},{16,8},{20,12},{24,0},{28,4},{1,25},{... | collective-permute-start | bytes 479240 | tf_op jit(solution)/shard_map/ppermute | solution.py:535
  11.4 1.6 collective-permute-start.2
  13.1 1.5 collective-permute-start.3
  14.7 1.2 constant_dynamic-slice_fusion
  16.4 0.6 collective-permute-start.5
  17.0 2.3 collective-permute-done.1.refs_1_
  19.6 5.9 %shard_map.86 = (bf16[192,640]{1,0:T(8,128)(2,1)S(1)}, bf16[192,640]{1,0:T(8,128)(2,1)S(1)}, bf16[192,640]{1,0:T(8,128)(2,1)S(1)}, bf16[192,640]{1,0:T(8,128)(2,...) custom-call(s32[10]{0:T(128)S(1)} %stack.43.meta, ...), custom_call_target="tpu_custom_call" | custom-call | flops 188743680 | bytes 245760 | tf_op jit(solution)/shard_map/pallas_call | solution.py:152
  26.5 3.5 %shard_map.87 = (bf16[768,384]{1,0:T(8,128)(2,1)S(1)}, bf16[192,768]{1,0:T(8,128)(2,1)S(1)}, bf16[768,1536]{1,0:T(8,128)(2,1)S(1)}, bf16[768,192]{1,0:T(8,128)(2,1)S(1)}) custom-call(s32[10]{0:T(128)S(1)} %stack.43.meta, bf16[208,384]{1,0:T(8,128)(2,1)S(1)} %collective-permute-done.refs_0_, bf16[208,384]{1,0:T(8,128)(2,1)S(1)} %collective-permute-done.1.refs_1_, ...), custom_call_target="tpu_custom_call" | custom-call | flops 56623104 | bytes 73728 | tf_op jit(solution)/shard_map/pallas_call | solution.py:212
  30.0 2.0 collective-permute-start.8
  32.1 1.8 collective-permute-start.10
  33.8 0.7 collective-permute-start.9
  34.5 6.6 %collective-permute-done.10.refs_1_ = bf16[192,640]{1,0:T(8,128)(2,1)S(1)} collective-permute-done((bf16[192,640]{1,0:T(8,128)(2,1)S(1)}, bf16[192,640]{1,0:T(8,128)(2,1)S(1)}, u32[]{:S(2)}, u32[]{:S(2)}) %collective-permute-start.10) | collective-permute-done | bytes 245792 | tf_op jit(solution)/shard_map/ppermute | solution.py:535
  41.1 5.4 %collective-permute-done.9.refs_0_ = bf16[192,640]{1,0:T(8,128)(2,1)S(1)} collective-permute-done((bf16[192,640]{1,0:T(8,128)(2,1)S(1)}, bf16[192,640]{1,0:T(8,128)(2,1)S(1)}, u32[]{:S(2)}, u32[]{:S(2)}) %collective-permute-start.9) | collective-permute-done | bytes 245792 | tf_op jit(solution)/shard_map/ppermute | solution.py:535
  46.5 1.1 collective-permute-done.8.refs_0_
  48.1 1.3 collective-permute-start.12
  49.4 1.5 collective-permute-start.13
  50.9 1.0 collective-permute-start.15
  51.8 5.1 %collective-permute-done.12.refs_2_ = bf16[192,640]{1,0:T(8,128)(2,1)S(1)} collective-permute-done((bf16[192,640]{1,0:T(8,128)(2,1)S(1)}, bf16[192,640]{1,0:T(8,128)(2,1)S(1)}, u32[]{:S(2)}, u32[]{:S(2)}) %collective-permute-start.12) | collective-permute-done | bytes 245792 | tf_op jit(solution)/shard_map/ppermute | solution.py:535
  56.9 1.3 collective-permute-done.13.refs_3_
  58.3 1.6 collective-permute-done.14.refs_4_
  59.9 1.2 collective-permute-done.15.refs_5_
  61.1 2.9 %shard_map.88.refs_1_ = bf16[768,640]{1,0:T(8,128)(2,1)S(1)} custom-call(s32[10]{0:T(128)S(1)} %stack.43.meta, bf16[192,640]{1,0:T(8,128)(2,1)S(1)} %collective-permute-done.9.refs_0_, bf16[192,640]{1,0:T(8,128)(2,1)S(1)} %collective-permute-done.10.refs_1_, bf16[192,640]{1,0:T(8,128)(2,1)S(1)} %collective-permute-done.12.refs_2_, ...), custom_call_target="tpu_custom_call" | custom-call | flops 94371840 | bytes 122880 | tf_op jit(solution)/shard_map/pallas_call | solution.py:231
  64.1 1.3 collective-permute-start.19
  65.3 1.5 collective-permute-start.20
  67.4 1.1 collective-permute-done.24.refs_8_.refs_7_
  68.4 1.0 collective-permute-start.18
  69.5 0.8 collective-permute-start.17
  70.3 36.4 %collective-permute-done.17.refs_0_ = bf16[768,384]{1,0:T(8,128)(2,1)S(1)} collective-permute-done((bf16[768,384]{1,0:T(8,128)(2,1)S(1)}, bf16[768,384]{1,0:T(8,128)(2,1)S(1)}, u32[]{:S(2)}, u32[]{:S(2)}) %collective-permute-start.17) | collective-permute-done | bytes 589856 | tf_op jit(solution)/shard_map/ppermute | solution.py:542
  106.9 1.2 collective-permute-start.26
  108.8 17.0 %collective-permute-done.26.refs_3_ = bf16[720,512]{1,0:T(8,128)(2,1)S(1)} collective-permute-done((bf16[720,512]{1,0:T(8,128)(2,1)S(1)}, bf16[720,512]{1,0:T(8,128)(2,1)S(1)}, u32[]{:S(2)}, u32[]{:S(2)}) %collective-permute-start.26) | collective-permute-done | bytes 737312 | tf_op jit(solution)/shard_map/ppermute | solution.py:535
  125.9 1.0 collective-permute-done.27.refs_4_
  126.9 6.8 %shard_map.89 = (bf16[720,4096]{1,0:T(8,128)(2,1)S(1)}, bf16[720,192]{1,0:T(8,128)(2,1)S(1)}) custom-call(s32[10]{0:T(128)S(1)} %stack.43.meta, bf16[720,1024]{1,0:T(8,128)(2,1)S(1)} %pad_maximum_fusion.refs_0_, bf16[720,1024]{1,0:T(8,128)(2,1)S(1)} %collective-permute-done.19.refs_1_, bf16[720,1024]{1,0:T(8,128)(2,1)S(1)} %collective-permute-done.20.refs_2_, ...), custom_call_target="tpu_custom_call" | custom-call | flops 283115520 | bytes 737280 | tf_op jit(solution)/shard_map/pallas_call | solution.py:283
  134.3 5.1 %shard_map.90 = (f32[720,1536]{1,0:T(8,128)S(1)}, bf16[1536,4096]{1,0:T(8,128)(2,1)S(1)}) custom-call(s32[10]{0:T(128)S(1)} %stack.43.meta, bf16[768,384]{1,0:T(8,128)(2,1)S(1)} %get-tuple-element.147.refs_0_, bf16[768,640]{1,0:T(8,128)(2,1)S(1)} %shard_map.88.refs_1_, bf16[768,384]{1,0:T(8,128)(2,1)S(1)} %collective-permute-done.21.refs_2_, ...), custom_call_target="tpu_custom_call" | custom-call | flops 141557760 | bytes 946176 | tf_op jit(solution)/shard_map/pallas_call | solution.py:387
  139.4 5.5 %shard_map.91 = (f32[720,1536]{1,0:T(8,128)S(1)}, bf16[1536,4096]{1,0:T(8,128)(2,1)S(1)}) custom-call(s32[10]{0:T(128)S(1)} %stack.43.meta, bf16[768,384]{1,0:T(8,128)(2,1)S(1)} %collective-permute-done.8.refs_0_, bf16[768,640]{1,0:T(8,128)(2,1)S(1)} %collective-permute-done.18.refs_1_, ...), custom_call_target="tpu_custom_call", output_to_operand_aliasing={{0}: (6, {}), {1}: (7, {})} | custom-call | flops 141557760 | bytes 946176 | tf_op jit(solution)/shard_map/pallas_call | solution.py:387
  144.9 5.5 %shard_map.92 = (f32[720,1536]{1,0:T(8,128)S(1)}, bf16[1536,4096]{1,0:T(8,128)(2,1)S(1)}) custom-call(s32[10]{0:T(128)S(1)} %stack.43.meta, bf16[768,384]{1,0:T(8,128)(2,1)S(1)} %collective-permute-done.11.refs_0_, bf16[768,640]{1,0:T(8,128)(2,1)S(1)} %collective-permute-done.25.refs_1_, ...), custom_call_target="tpu_custom_call", output_to_operand_aliasing={{0}: (6, {}), {1}: (7, {})} | custom-call | flops 141557760 | bytes 946176 | tf_op jit(solution)/shard_map/pallas_call | solution.py:387
  150.4 3.7 %shard_map.93.refs_5_ = f32[720,1536]{1,0:T(8,128)S(1)} custom-call(s32[10]{0:T(128)S(1)} %stack.43.meta, bf16[768,384]{1,0:T(8,128)(2,1)S(1)} %collective-permute-done.17.refs_0_, bf16[768,384]{1,0:T(8,128)(2,1)S(1)} %collective-permute-done.31.refs_1_.refs_2_, ...), custom_call_target="tpu_custom_call", output_to_operand_aliasing={{}: (4, {})} | custom-call | flops 141557760 | bytes 946176 | tf_op jit(solution)/shard_map/pallas_call | solution.py:387
  154.1 5.9 %collective-permute-done.30.refs_1_ = bf16[768,640]{1,0:T(8,128)(2,1)S(1)} collective-permute-done((bf16[768,640]{1,0:T(8,128)(2,1)S(1)}, bf16[768,640]{1,0:T(8,128)(2,1)S(1)}, u32[]{:S(2)}, u32[]{:S(2)}) %collective-permute-start.30) | collective-permute-done | bytes 983072 | tf_op jit(solution)/shard_map/ppermute | solution.py:542
  159.9 2.6 %collective-permute-done.33.refs_3_ = bf16[768,640]{1,0:T(8,128)(2,1)S(1)} collective-permute-done((bf16[768,640]{1,0:T(8,128)(2,1)S(1)}, bf16[768,640]{1,0:T(8,128)(2,1)S(1)}, u32[]{:S(2)}, u32[]{:S(2)}) %collective-permute-start.33) | collective-permute-done | bytes 983072 | tf_op jit(solution)/shard_map/ppermute | solution.py:535
  162.5 6.6 %shard_map.94 = (f32[720,1536]{1,0:T(8,128)S(1)}, f32[8,1536]{1,0:T(8,128)S(1)}, bf16[1536,4096]{1,0:T(8,128)(2,1)S(1)}) custom-call(s32[10]{0:T(128)S(1)} %stack.43.meta, bf16[768,384]{1,0:T(8,128)(2,1)S(1)} %collective-permute-done.17.refs_0_, bf16[768,640]{1,0:T(8,128)(2,1)S(1)} %collective-permute-done.30.refs_1_, ...), custom_call_target="tpu_custom_call", output_to_operand_aliasing={{0}: (6, {}), {2}: (7, {})} | custom-call | flops 141557760 | bytes 946176 | tf_op jit(solution)/shard_map/pallas_call | solution.py:387
  169.3 1.1 collective-permute-done.34.other_ref
  171.1 2.3 collective-permute-start.36
  173.4 2.1 collective-permute-start.37
  175.8 1.2 collective-permute-done.36.refs_4_
  177.0 2.3 collective-permute-done.37.refs_5_
  179.3 4.2 %shard_map.96 = (bf16[720,512]{1,0:T(8,128)(2,1)S(1)}, bf16[720,512]{1,0:T(8,128)(2,1)S(1)}, bf16[720,1536]{1,0:T(8,128)(2,1)S(1)}, f32[1,768]{1,0:T(1,128)S(1)}, bf16[64,720]{1,0:T(8,128)(2,1)S(1)}) custom-call(s32[10]{0:T(128)S(1)} %stack.43.meta, f32[720,1536]{1,0:T(8,128)S(1)} %get-tuple-element.191.refs_0_, ...), custom_call_target="tpu_custom_call" | custom-call | flops 141557760 | bytes 657408 | tf_op jit(solution)/shard_map/pallas_call | solution.py:475
  183.5 0.6 collective-permute-start.38
  184.1 0.9 collective-permute-start.39
  185.0 1.5 collective-permute-start.40
  186.5 10.8 %shard_map.97 = (bf16[720,512]{1,0:T(8,128)(2,1)S(1)}, bf16[720,512]{1,0:T(8,128)(2,1)}, bf16[720,512]{1,0:T(8,128)(2,1)}, f32[720,512]{1,0:T(8,128)S(1)}, f32[7...) custom-call(s32[10]{0:T(128)S(1)} %stack.43.meta, bf16[720,1536]{1,0:T(8,128)(2,1)S(1)} %get-tuple-element.196.refs_0_, ...), custom_call_target="tpu_custom_call" | custom-call | flops 424673280 | bytes 1419264 | tf_op jit(solution)/shard_map/pallas_call | solution.py:475
  197.3 5.5 %collective-permute-done.40.other_ref = bf16[64,720]{1,0:T(8,128)(2,1)S(1)} collective-permute-done((bf16[64,720]{1,0:T(8,128)(2,1)S(1)}, bf16[64,720]{1,0:T(8,128)(2,1)S(1)}, u32[]{:S(2)}, u32[]{:S(2)}) %collective-permute-start.40) | collective-permute-done | bytes 92192 | tf_op jit(solution)/shard_map/ppermute | solution.py:535
  202.8 1.4 fusion.3
  204.2 0.9 collective-permute-start.42
  206.2 1.2 collective-permute-start.41
  207.4 1.0 collective-permute-start.44
  208.4 17.3 %collective-permute-done.41 = bf16[64,720]{1,0:T(8,128)(2,1)S(1)} collective-permute-done((bf16[64,720]{1,0:T(8,128)(2,1)S(1)}, bf16[64,720]{1,0:T(8,128)(2,1)S(1)}, u32[]{:S(2)}, u32[]{:S(2)}) %collective-permute-start.41) | collective-permute-done | bytes 92192 | tf_op jit(solution)/shard_map/ppermute | solution.py:535
  225.8 0.7 collective-permute-start.46
  226.5 0.6 reduce
  227.1 2.3 shard_map.99
  229.4 0.9 maximum_select_fusion
  230.3 2.7 %collective-permute-done.47 = bf16[720,512]{1,0:T(8,128)(2,1)} collective-permute-done((bf16[720,512]{1,0:T(8,128)(2,1)}, bf16[720,512]{1,0:T(8,128)(2,1)}, u32[]{:S(2)}, u32[]{:S(2)}) %collective-permute-start.47) | collective-permute-done | bytes 737312 | tf_op jit(solution)/shard_map/ppermute | solution.py:539
  233.0 4.1 %collective-permute-done.45 = bf16[720,512]{1,0:T(8,128)(2,1)} collective-permute-done((bf16[720,512]{1,0:T(8,128)(2,1)}, bf16[720,512]{1,0:T(8,128)(2,1)}, u32[]{:S(2)}, u32[]{:S(2)}) %collective-permute-start.45) | collective-permute-done | bytes 737312 | tf_op jit(solution)/shard_map/ppermute | solution.py:539
  237.1 2.9 %add_dynamic-update-slice_fusion = f32[1440,512]{1,0:T(8,128)} fusion(f32[1440,512]{1,0:T(8,128)} %shard_map.99, s32[]{:T(128)S(6)} %select_n.67, bf16[720,512]{1,0:T(8,128)(2,1)} %collective-permute-done.47, bf16[720,512]{1,0:T(8,128)(2,1)} %collective-permute-done.45, bf16[720,512]{1,0:T(8,128)(2,1)} %collective-permute-done.44), kind=kLoop, calls=%fused_computation.7 | loop fusion | flops 1843200 | bytes 3686404 | tf_op jit(solution)/shard_map/dynamic_update_slice | solution.py:640
  (65 shorter events, 7.5 us)
Async XLA Ops:
  0.6 14.0 %collective-permute-start.7 = (bf16[1440,512]{1,0:T(8,128)(2,1)}, bf16[1440,512]{1,0:T(8,128)(2,1)}, u32[]{:S(2)}, u32[]{:S(2)}) collective-permute-start(bf16[1440,512]{1,0:T(8,128)(2,1)} %param.11), channel_id=1, source_target_pairs={{0,4},{4,0},{8,12},{12,8},{16,20},{20,16},{24,28},{28,24},{1,5},{5... | collective-permute-start | bytes 4423688 | tf_op jit(solution)/shard_map/ppermute | solution.py:535
  2.0 12.6 %copy-start.2 = (bf16[1440,512]{1,0:T(8,128)(2,1)S(1)}, bf16[1440,512]{1,0:T(8,128)(2,1)}, u32[]{:S(2)}) copy-start(bf16[1440,512]{1,0:T(8,128)(2,1)} %param.11) | copy-start | bytes 4423684
  7.7 8.6 %collective-permute-start = (bf16[208,384]{1,0:T(8,128)(2,1)S(1)}, bf16[208,384]{1,0:T(8,128)(2,1)S(1)}, u32[]{:S(2)}, u32[]{:S(2)}) collective-permute-start(bf16[208,384]{1,0:T(8,128)(2,1)S(1)} %get-tuple-element.111), channel_id=1, source_target_pairs={{0,24},{4,28},{8,16},{12,20},{16,8},{20,12},{24,0},{28,4},{1,25},{... | collective-permute-start | bytes 479240 | tf_op jit(solution)/shard_map/ppermute | solution.py:535
  11.3 8.0 %collective-permute-start.1 = (bf16[208,384]{1,0:T(8,128)(2,1)S(1)}, bf16[208,384]{1,0:T(8,128)(2,1)S(1)}, u32[]{:S(2)}, u32[]{:S(2)}) collective-permute-start(bf16[208,384]{1,0:T(8,128)(2,1)S(1)} %get-tuple-element.112), channel_id=1, source_target_pairs={{0,28},{4,24},{8,20},{12,16},{16,12},{20,8},{24,4},{28,0},{1,29},{... | collective-permute-start | bytes 479240 | tf_op jit(solution)/shard_map/ppermute | solution.py:535
  11.4 14.2 %collective-permute-start.2 = (bf16[208,384]{1,0:T(8,128)(2,1)S(1)}, bf16[208,384]{1,0:T(8,128)(2,1)S(1)}, u32[]{:S(2)}, u32[]{:S(2)}) collective-permute-start(bf16[208,384]{1,0:T(8,128)(2,1)S(1)} %get-tuple-element.113), channel_id=1, source_target_pairs={{0,16},{4,20},{8,24},{12,28},{16,0},{20,4},{24,8},{28,12},{1,17},{... | collective-permute-start | bytes 479240 | tf_op jit(solution)/shard_map/ppermute | solution.py:535
  13.1 12.6 %collective-permute-start.3 = (bf16[208,384]{1,0:T(8,128)(2,1)S(1)}, bf16[208,384]{1,0:T(8,128)(2,1)S(1)}, u32[]{:S(2)}, u32[]{:S(2)}) collective-permute-start(bf16[208,384]{1,0:T(8,128)(2,1)S(1)} %get-tuple-element.114), channel_id=1, source_target_pairs={{0,8},{4,12},{8,0},{12,4},{16,24},{20,28},{24,16},{28,20},{1,9},{5... | collective-permute-start | bytes 479240 | tf_op jit(solution)/shard_map/ppermute | solution.py:535
  14.6 11.6 %collective-permute-start.4 = (bf16[208,384]{1,0:T(8,128)(2,1)S(1)}, bf16[208,384]{1,0:T(8,128)(2,1)S(1)}, u32[]{:S(2)}, u32[]{:S(2)}) collective-permute-start(bf16[208,384]{1,0:T(8,128)(2,1)S(1)} %get-tuple-element.115), channel_id=1, source_target_pairs={{0,20},{4,16},{8,28},{12,24},{16,4},{20,0},{24,12},{28,8},{1,21},{... | collective-permute-start | bytes 479240 | tf_op jit(solution)/shard_map/ppermute | solution.py:535
  16.4 9.9 %collective-permute-start.5 = (bf16[208,384]{1,0:T(8,128)(2,1)S(1)}, bf16[208,384]{1,0:T(8,128)(2,1)S(1)}, u32[]{:S(2)}, u32[]{:S(2)}) collective-permute-start(bf16[208,384]{1,0:T(8,128)(2,1)S(1)} %get-tuple-element.116), channel_id=1, source_target_pairs={{0,12},{4,8},{8,4},{12,0},{16,28},{20,24},{24,20},{28,16},{1,13},{... | collective-permute-start | bytes 479240 | tf_op jit(solution)/shard_map/ppermute | solution.py:535
  19.3 6.9 %collective-permute-start.6 = (bf16[208,384]{1,0:T(8,128)(2,1)S(1)}, bf16[208,384]{1,0:T(8,128)(2,1)S(1)}, u32[]{:S(2)}, u32[]{:S(2)}) collective-permute-start(bf16[208,384]{1,0:T(8,128)(2,1)S(1)} %get-tuple-element.117), channel_id=1, source_target_pairs={{0,4},{4,0},{8,12},{12,8},{16,20},{20,16},{24,28},{28,24},{1,5},{5... | collective-permute-start | bytes 479240 | tf_op jit(solution)/shard_map/ppermute | solution.py:535
  25.5 1.0 copy-start
  25.5 1.0 copy-start.1
  30.0 17.6 %collective-permute-start.8 = (bf16[768,384]{1,0:T(8,128)(2,1)S(1)}, bf16[768,384]{1,0:T(8,128)(2,1)S(1)}, u32[]{:S(2)}, u32[]{:S(2)}) collective-permute-start(bf16[768,384]{1,0:T(8,128)(2,1)S(1)} %get-tuple-element.147.refs_0_), channel_id=1, source_target_pairs={{0,1},{1,2},{2,3},{3,0},{4,5},{5,6},{6,7},{7,4},{8,9},{9,10},{10,1... | collective-permute-start | bytes 1769480 | tf_op jit(solution)/shard_map/ppermute | solution.py:542
  32.1 9.1 %collective-permute-start.10 = (bf16[192,640]{1,0:T(8,128)(2,1)S(1)}, bf16[192,640]{1,0:T(8,128)(2,1)S(1)}, u32[]{:S(2)}, u32[]{:S(2)}) collective-permute-start(bf16[192,640]{1,0:T(8,128)(2,1)S(1)} %get-tuple-element.149), channel_id=1, source_target_pairs={{0,28},{4,24},{8,20},{12,16},{16,12},{20,8},{24,4},{28,0},{1,29},{... | collective-permute-start | bytes 737288 | tf_op jit(solution)/shard_map/ppermute | solution.py:535
  33.8 12.6 %collective-permute-start.9 = (bf16[192,640]{1,0:T(8,128)(2,1)S(1)}, bf16[192,640]{1,0:T(8,128)(2,1)S(1)}, u32[]{:S(2)}, u32[]{:S(2)}) collective-permute-start(bf16[192,640]{1,0:T(8,128)(2,1)S(1)} %get-tuple-element.148), channel_id=1, source_target_pairs={{0,24},{4,28},{8,16},{12,20},{16,8},{20,12},{24,0},{28,4},{1,25},{... | collective-permute-start | bytes 737288 | tf_op jit(solution)/shard_map/ppermute | solution.py:535
  47.6 16.5 %collective-permute-start.11 = (bf16[768,384]{1,0:T(8,128)(2,1)S(1)}, bf16[768,384]{1,0:T(8,128)(2,1)S(1)}, u32[]{:S(2)}, u32[]{:S(2)}) collective-permute-start(bf16[768,384]{1,0:T(8,128)(2,1)S(1)} %collective-permute-done.8.refs_0_), channel_id=1, source_target_pairs={{0,1},{1,2},{2,3},{3,0},{4,5},{5,6},{6,7},{7,4},{8,9},{9,10},{10,1... | collective-permute-start | bytes 1769480 | tf_op jit(solution)/shard_map/ppermute | solution.py:542
  48.1 8.9 %collective-permute-start.12 = (bf16[192,640]{1,0:T(8,128)(2,1)S(1)}, bf16[192,640]{1,0:T(8,128)(2,1)S(1)}, u32[]{:S(2)}, u32[]{:S(2)}) collective-permute-start(bf16[192,640]{1,0:T(8,128)(2,1)S(1)} %get-tuple-element.153), channel_id=1, source_target_pairs={{0,16},{4,20},{8,24},{12,28},{16,0},{20,4},{24,8},{28,12},{1,17},{... | collective-permute-start | bytes 737288 | tf_op jit(solution)/shard_map/ppermute | solution.py:535
  49.4 8.9 %collective-permute-start.13 = (bf16[192,640]{1,0:T(8,128)(2,1)S(1)}, bf16[192,640]{1,0:T(8,128)(2,1)S(1)}, u32[]{:S(2)}, u32[]{:S(2)}) collective-permute-start(bf16[192,640]{1,0:T(8,128)(2,1)S(1)} %get-tuple-element.154), channel_id=1, source_target_pairs={{0,8},{4,12},{8,0},{12,4},{16,24},{20,28},{24,16},{28,20},{1,9},{5... | collective-permute-start | bytes 737288 | tf_op jit(solution)/shard_map/ppermute | solution.py:535
  50.9 9.0 %collective-permute-start.14 = (bf16[192,640]{1,0:T(8,128)(2,1)S(1)}, bf16[192,640]{1,0:T(8,128)(2,1)S(1)}, u32[]{:S(2)}, u32[]{:S(2)}) collective-permute-start(bf16[192,640]{1,0:T(8,128)(2,1)S(1)} %get-tuple-element.155), channel_id=1, source_target_pairs={{0,20},{4,16},{8,28},{12,24},{16,4},{20,0},{24,12},{28,8},{1,21},{... | collective-permute-start | bytes 737288 | tf_op jit(solution)/shard_map/ppermute | solution.py:535
  50.9 10.2 %collective-permute-start.15 = (bf16[192,640]{1,0:T(8,128)(2,1)S(1)}, bf16[192,640]{1,0:T(8,128)(2,1)S(1)}, u32[]{:S(2)}, u32[]{:S(2)}) collective-permute-start(bf16[192,640]{1,0:T(8,128)(2,1)S(1)} %get-tuple-element.156), channel_id=1, source_target_pairs={{0,12},{4,8},{8,4},{12,0},{16,28},{20,24},{24,20},{28,16},{1,13},{... | collective-permute-start | bytes 737288 | tf_op jit(solution)/shard_map/ppermute | solution.py:535
  56.9 4.2 %collective-permute-start.16 = (bf16[192,640]{1,0:T(8,128)(2,1)S(1)}, bf16[192,640]{1,0:T(8,128)(2,1)S(1)}, u32[]{:S(2)}, u32[]{:S(2)}) collective-permute-start(bf16[192,640]{1,0:T(8,128)(2,1)S(1)} %get-tuple-element.157), channel_id=1, source_target_pairs={{0,4},{4,0},{8,12},{12,8},{16,20},{20,16},{24,28},{28,24},{1,5},{5... | collective-permute-start | bytes 737288 | tf_op jit(solution)/shard_map/ppermute | solution.py:535
  58.3 11.2 %collective-permute-start.21 = (bf16[768,384]{1,0:T(8,128)(2,1)S(1)}, bf16[768,384]{1,0:T(8,128)(2,1)S(1)}, u32[]{:S(2)}, u32[]{:S(2)}) collective-permute-start(bf16[768,384]{1,0:T(8,128)(2,1)S(1)} %get-tuple-element.147.refs_0_), channel_id=1, source_target_pairs={{0,4},{4,0},{8,12},{12,8},{16,20},{20,16},{24,28},{28,24},{1,5},{5... | collective-permute-start | bytes 1769480 | tf_op jit(solution)/shard_map/ppermute | solution.py:535
  64.1 42.6 %collective-permute-start.19 = (bf16[720,1024]{1,0:T(8,128)(2,1)S(1)}, bf16[720,1024]{1,0:T(8,128)(2,1)S(1)}, u32[]{:S(2)}, u32[]{:S(2)}) collective-permute-start(bf16[720,1024]{1,0:T(8,128)(2,1)S(1)} %pad_maximum_fusion.refs_0_), channel_id=1, source_target_pairs={{0,8},{4,12},{8,0},{12,4},{16,24},{20,28},{24,16},{28,20},{1,9},{5... | collective-permute-start | bytes 4423688 | tf_op jit(solution)/shard_map/ppermute | solution.py:535
  65.3 41.4 %collective-permute-start.20 = (bf16[720,1024]{1,0:T(8,128)(2,1)S(1)}, bf16[720,1024]{1,0:T(8,128)(2,1)S(1)}, u32[]{:S(2)}, u32[]{:S(2)}) collective-permute-start(bf16[720,1024]{1,0:T(8,128)(2,1)S(1)} %pad_maximum_fusion.refs_0_), channel_id=1, source_target_pairs={{0,16},{4,20},{8,24},{12,28},{16,0},{20,4},{24,8},{28,12},{1,17},{... | collective-permute-start | bytes 4423688 | tf_op jit(solution)/shard_map/ppermute | solution.py:535
  66.9 1.6 collective-permute-start.24
  66.9 2.7 %collective-permute-start.23 = (bf16[768,384]{1,0:T(8,128)(2,1)S(1)}, bf16[768,384]{1,0:T(8,128)(2,1)S(1)}, u32[]{:S(2)}, u32[]{:S(2)}) collective-permute-start(bf16[768,384]{1,0:T(8,128)(2,1)S(1)} %collective-permute-done.8.refs_0_), channel_id=1, source_target_pairs={{0,4},{4,0},{8,12},{12,8},{16,20},{20,16},{24,28},{28,24},{1,5},{5... | collective-permute-start | bytes 1769480 | tf_op jit(solution)/shard_map/ppermute | solution.py:535
  68.4 38.2 %collective-permute-start.18 = (bf16[768,640]{1,0:T(8,128)(2,1)S(1)}, bf16[768,640]{1,0:T(8,128)(2,1)S(1)}, u32[]{:S(2)}, u32[]{:S(2)}) collective-permute-start(bf16[768,640]{1,0:T(8,128)(2,1)S(1)} %shard_map.88.refs_1_), channel_id=1, source_target_pairs={{0,1},{1,2},{2,3},{3,0},{4,5},{5,6},{6,7},{7,4},{8,9},{9,10},{10,1... | collective-permute-start | bytes 2949128 | tf_op jit(solution)/shard_map/ppermute | solution.py:542
  69.4 37.2 %collective-permute-start.22 = (bf16[768,640]{1,0:T(8,128)(2,1)S(1)}, bf16[768,640]{1,0:T(8,128)(2,1)S(1)}, u32[]{:S(2)}, u32[]{:S(2)}) collective-permute-start(bf16[768,640]{1,0:T(8,128)(2,1)S(1)} %shard_map.88.refs_1_), channel_id=1, source_target_pairs={{0,4},{4,0},{8,12},{12,8},{16,20},{20,16},{24,28},{28,24},{1,5},{5... | collective-permute-start | bytes 2949128 | tf_op jit(solution)/shard_map/ppermute | solution.py:535
  69.5 37.1 %collective-permute-start.17 = (bf16[768,384]{1,0:T(8,128)(2,1)S(1)}, bf16[768,384]{1,0:T(8,128)(2,1)S(1)}, u32[]{:S(2)}, u32[]{:S(2)}) collective-permute-start(bf16[768,384]{1,0:T(8,128)(2,1)S(1)} %collective-permute-done.11.refs_0_), channel_id=1, source_target_pairs={{0,1},{1,2},{2,3},{3,0},{4,5},{5,6},{6,7},{7,4},{8,9},{9,10},{10,1... | collective-permute-start | bytes 1769480 | tf_op jit(solution)/shard_map/ppermute | solution.py:542
  106.7 27.0 %collective-permute-start.25 = (bf16[768,640]{1,0:T(8,128)(2,1)S(1)}, bf16[768,640]{1,0:T(8,128)(2,1)S(1)}, u32[]{:S(2)}, u32[]{:S(2)}) collective-permute-start(bf16[768,640]{1,0:T(8,128)(2,1)S(1)} %collective-permute-done.18.refs_1_), channel_id=1, source_target_pairs={{0,1},{1,2},{2,3},{3,0},{4,5},{5,6},{6,7},{7,4},{8,9},{9,10},{10,1... | collective-permute-start | bytes 2949128 | tf_op jit(solution)/shard_map/ppermute | solution.py:542
  106.8 27.0 %collective-permute-start.28 = (bf16[768,640]{1,0:T(8,128)(2,1)S(1)}, bf16[768,640]{1,0:T(8,128)(2,1)S(1)}, u32[]{:S(2)}, u32[]{:S(2)}) collective-permute-start(bf16[768,640]{1,0:T(8,128)(2,1)S(1)} %collective-permute-done.18.refs_1_), channel_id=1, source_target_pairs={{0,4},{4,0},{8,12},{12,8},{16,20},{20,16},{24,28},{28,24},{1,5},{5... | collective-permute-start | bytes 2949128 | tf_op jit(solution)/shard_map/ppermute | solution.py:535
  106.9 19.0 %collective-permute-start.26 = (bf16[720,512]{1,0:T(8,128)(2,1)S(1)}, bf16[720,512]{1,0:T(8,128)(2,1)S(1)}, u32[]{:S(2)}, u32[]{:S(2)}) collective-permute-start(bf16[720,512]{1,0:T(8,128)(2,1)S(1)} %slice.6), channel_id=1, source_target_pairs={{0,16},{4,20},{8,24},{12,28},{16,0},{20,4},{24,8},{28,12},{1,17},{... | collective-permute-start | bytes 2211848 | tf_op jit(solution)/shard_map/ppermute | solution.py:535
  108.2 18.7 %collective-permute-start.27 = (bf16[720,512]{1,0:T(8,128)(2,1)S(1)}, bf16[720,512]{1,0:T(8,128)(2,1)S(1)}, u32[]{:S(2)}, u32[]{:S(2)}) collective-permute-start(bf16[720,512]{1,0:T(8,128)(2,1)S(1)} %slice.7), channel_id=1, source_target_pairs={{0,8},{4,12},{8,0},{12,4},{16,24},{20,28},{24,16},{28,20},{1,9},{5... | collective-permute-start | bytes 2211848 | tf_op jit(solution)/shard_map/ppermute | solution.py:535
  108.8 24.9 %collective-permute-start.29 = (bf16[768,384]{1,0:T(8,128)(2,1)S(1)}, bf16[768,384]{1,0:T(8,128)(2,1)S(1)}, u32[]{:S(2)}, u32[]{:S(2)}) collective-permute-start(bf16[768,384]{1,0:T(8,128)(2,1)S(1)} %collective-permute-done.11.refs_0_), channel_id=1, source_target_pairs={{0,4},{4,0},{8,12},{12,8},{16,20},{20,16},{24,28},{28,24},{1,5},{5... | collective-permute-start | bytes 1769480 | tf_op jit(solution)/shard_map/ppermute | solution.py:535
  133.7 11.1 %collective-permute-start.32 = (bf16[768,640]{1,0:T(8,128)(2,1)S(1)}, bf16[768,640]{1,0:T(8,128)(2,1)S(1)}, u32[]{:S(2)}, u32[]{:S(2)}) collective-permute-start(bf16[768,640]{1,0:T(8,128)(2,1)S(1)} %collective-permute-done.25.refs_1_), channel_id=1, source_target_pairs={{0,4},{4,0},{8,12},{12,8},{16,20},{20,16},{24,28},{28,24},{1,5},{5... | collective-permute-start | bytes 2949128 | tf_op jit(solution)/shard_map/ppermute | solution.py:535
  133.8 26.1 %collective-permute-start.30 = (bf16[768,640]{1,0:T(8,128)(2,1)S(1)}, bf16[768,640]{1,0:T(8,128)(2,1)S(1)}, u32[]{:S(2)}, u32[]{:S(2)}) collective-permute-start(bf16[768,640]{1,0:T(8,128)(2,1)S(1)} %collective-permute-done.25.refs_1_), channel_id=1, source_target_pairs={{0,1},{1,2},{2,3},{3,0},{4,5},{5,6},{6,7},{7,4},{8,9},{9,10},{10,1... | collective-permute-start | bytes 2949128 | tf_op jit(solution)/shard_map/ppermute | solution.py:542
  134.1 16.2 %collective-permute-start.31 = (bf16[768,384]{1,0:T(8,128)(2,1)S(1)}, bf16[768,384]{1,0:T(8,128)(2,1)S(1)}, u32[]{:S(2)}, u32[]{:S(2)}) collective-permute-start(bf16[768,384]{1,0:T(8,128)(2,1)S(1)} %collective-permute-done.17.refs_0_), channel_id=1, source_target_pairs={{0,4},{4,0},{8,12},{12,8},{16,20},{20,16},{24,28},{28,24},{1,5},{5... | collective-permute-start | bytes 1769480 | tf_op jit(solution)/shard_map/ppermute | solution.py:535
  159.9 2.6 %collective-permute-start.33 = (bf16[768,640]{1,0:T(8,128)(2,1)S(1)}, bf16[768,640]{1,0:T(8,128)(2,1)S(1)}, u32[]{:S(2)}, u32[]{:S(2)}) collective-permute-start(bf16[768,640]{1,0:T(8,128)(2,1)S(1)} %collective-permute-done.30.refs_1_), channel_id=1, source_target_pairs={{0,4},{4,0},{8,12},{12,8},{16,20},{20,16},{24,28},{28,24},{1,5},{5... | collective-permute-start | bytes 2949128 | tf_op jit(solution)/shard_map/ppermute | solution.py:535
  169.1 1.3 collective-permute-start.34
  171.0 4.8 %collective-permute-start.35 = (f32[8,1536]{1,0:T(8,128)S(1)}, f32[8,1536]{1,0:T(8,128)S(1)}, u32[]{:S(2)}, u32[]{:S(2)}) collective-permute-start(f32[8,1536]{1,0:T(8,128)S(1)} %shard_map.95.refs_2_), channel_id=1, source_target_pairs={{0,1},{1,0},{2,3},{3,2},{4,5},{5,4},{6,7},{7,6},{8,9},{9,8},{10,11... | collective-permute-start | bytes 147464 | tf_op jit(solution)/shard_map/ppermute | solution.py:611
  171.1 5.9 %collective-permute-start.36 = (f32[8,1536]{1,0:T(8,128)S(1)}, f32[8,1536]{1,0:T(8,128)S(1)}, u32[]{:S(2)}, u32[]{:S(2)}) collective-permute-start(f32[8,1536]{1,0:T(8,128)S(1)} %shard_map.95.refs_2_), channel_id=1, source_target_pairs={{0,2},{1,3},{2,0},{3,1},{4,6},{5,7},{6,4},{7,5},{8,10},{9,11},{10,... | collective-permute-start | bytes 147464 | tf_op jit(solution)/shard_map/ppermute | solution.py:611
  173.4 5.9 %collective-permute-start.37 = (f32[8,1536]{1,0:T(8,128)S(1)}, f32[8,1536]{1,0:T(8,128)S(1)}, u32[]{:S(2)}, u32[]{:S(2)}) collective-permute-start(f32[8,1536]{1,0:T(8,128)S(1)} %shard_map.95.refs_2_), channel_id=1, source_target_pairs={{0,3},{1,2},{2,1},{3,0},{4,7},{5,6},{6,5},{7,4},{8,11},{9,10},{10,... | collective-permute-start | bytes 147464 | tf_op jit(solution)/shard_map/ppermute | solution.py:611
  183.5 19.3 %collective-permute-start.38 = (bf16[720,512]{1,0:T(8,128)(2,1)S(1)}, bf16[720,512]{1,0:T(8,128)(2,1)S(1)}, u32[]{:S(2)}, u32[]{:S(2)}) collective-permute-start(bf16[720,512]{1,0:T(8,128)(2,1)S(1)} %get-tuple-element.194), channel_id=1, source_target_pairs={{0,8},{4,12},{8,0},{12,4},{16,24},{20,28},{24,16},{28,20},{1,9},{5... | collective-permute-start | bytes 2211848 | tf_op jit(solution)/shard_map/ppermute | solution.py:535
  184.1 18.7 %collective-permute-start.39 = (bf16[720,512]{1,0:T(8,128)(2,1)S(1)}, bf16[720,512]{1,0:T(8,128)(2,1)S(1)}, u32[]{:S(2)}, u32[]{:S(2)}) collective-permute-start(bf16[720,512]{1,0:T(8,128)(2,1)S(1)} %get-tuple-element.195), channel_id=1, source_target_pairs={{0,16},{4,20},{8,24},{12,28},{16,0},{20,4},{24,8},{28,12},{1,17},{... | collective-permute-start | bytes 2211848 | tf_op jit(solution)/shard_map/ppermute | solution.py:535
  185.0 17.8 %collective-permute-start.40 = (bf16[64,720]{1,0:T(8,128)(2,1)S(1)}, bf16[64,720]{1,0:T(8,128)(2,1)S(1)}, u32[]{:S(2)}, u32[]{:S(2)}) collective-permute-start(bf16[64,720]{1,0:T(8,128)(2,1)S(1)} %get-tuple-element.203.mine_ref), channel_id=1, source_target_pairs={{0,8},{4,12},{8,0},{12,4},{16,24},{20,28},{24,16},{28,20},{1,9},{5... | collective-permute-start | bytes 276488 | tf_op jit(solution)/shard_map/ppermute | solution.py:535
  204.2 21.5 %collective-permute-start.42 = (bf16[720,512]{1,0:T(8,128)(2,1)S(1)}, bf16[720,512]{1,0:T(8,128)(2,1)S(1)}, u32[]{:S(2)}, u32[]{:S(2)}) collective-permute-start(bf16[720,512]{1,0:T(8,128)(2,1)S(1)} %get-tuple-element.220), channel_id=1, source_target_pairs={{0,16},{4,12},{8,24},{12,4},{16,0},{20,28},{24,8},{28,20},{1,17},{... | collective-permute-start | bytes 2211848 | tf_op jit(solution)/shard_map/ppermute | solution.py:539
  205.1 20.7 %collective-permute-start.43 = (bf16[720,512]{1,0:T(8,128)(2,1)S(1)}, bf16[720,512]{1,0:T(8,128)(2,1)S(1)}, u32[]{:S(2)}, u32[]{:S(2)}) collective-permute-start(bf16[720,512]{1,0:T(8,128)(2,1)S(1)} %get-tuple-element.209), channel_id=1, source_target_pairs={{0,8},{4,20},{8,0},{12,28},{16,24},{20,4},{24,16},{28,12},{1,9},{5... | collective-permute-start | bytes 2211848 | tf_op jit(solution)/shard_map/ppermute | solution.py:539
  206.2 19.6 %collective-permute-start.41 = (bf16[64,720]{1,0:T(8,128)(2,1)S(1)}, bf16[64,720]{1,0:T(8,128)(2,1)S(1)}, u32[]{:S(2)}, u32[]{:S(2)}) collective-permute-start(bf16[64,720]{1,0:T(8,128)(2,1)S(1)} %shard_map.98), channel_id=1, source_target_pairs={{0,16},{4,20},{8,24},{12,28},{16,0},{20,4},{24,8},{28,12},{1,17},{... | collective-permute-start | bytes 276488 | tf_op jit(solution)/shard_map/ppermute | solution.py:535
  207.4 25.6 %collective-permute-start.47 = (bf16[720,512]{1,0:T(8,128)(2,1)}, bf16[720,512]{1,0:T(8,128)(2,1)}, u32[]{:S(2)}, u32[]{:S(2)}) collective-permute-start(bf16[720,512]{1,0:T(8,128)(2,1)} %get-tuple-element.219), channel_id=1, source_target_pairs={{0,12},{4,16},{8,4},{12,24},{16,28},{20,0},{24,20},{28,8},{1,13},{... | collective-permute-start | bytes 2211848 | tf_op jit(solution)/shard_map/ppermute | solution.py:539
  207.4 25.6 %collective-permute-start.44 = (bf16[720,512]{1,0:T(8,128)(2,1)}, bf16[720,512]{1,0:T(8,128)(2,1)}, u32[]{:S(2)}, u32[]{:S(2)}) collective-permute-start(bf16[720,512]{1,0:T(8,128)(2,1)} %get-tuple-element.212), channel_id=1, source_target_pairs={{0,4},{4,0},{8,12},{12,8},{16,20},{20,16},{24,28},{28,24},{1,5},{5... | collective-permute-start | bytes 2211848 | tf_op jit(solution)/shard_map/ppermute | solution.py:535
  225.8 11.3 %collective-permute-start.45 = (bf16[720,512]{1,0:T(8,128)(2,1)}, bf16[720,512]{1,0:T(8,128)(2,1)}, u32[]{:S(2)}, u32[]{:S(2)}) collective-permute-start(bf16[720,512]{1,0:T(8,128)(2,1)} %get-tuple-element.213), channel_id=1, source_target_pairs={{0,20},{4,8},{8,28},{12,0},{16,4},{20,24},{24,12},{28,16},{1,21},{... | collective-permute-start | bytes 2211848 | tf_op jit(solution)/shard_map/ppermute | solution.py:539
  225.8 3.6 %collective-permute-start.46 = (f32[64,720]{1,0:T(8,128)S(1)}, f32[64,720]{1,0:T(8,128)S(1)}, u32[]{:S(2)}, u32[]{:S(2)}) collective-permute-start(f32[64,720]{1,0:T(8,128)S(1)} %convert_add_fusion), channel_id=1, source_target_pairs={{0,4},{4,0},{8,12},{12,8},{16,20},{20,16},{24,28},{28,24},{1,5},{5... | collective-permute-start | bytes 552968 | tf_op jit(solution)/shard_map/ppermute | solution.py:535

commit v11 on v10

--- a/solution.py
+++ b/solution.py
@@ -571,14 +571,13 @@
     a2, share_b, near = together((a2, share_b, near))
     by_x, by_y = across(near, 2), across(near, 4)
     a3, b1 = onward(a2), onward(share_b)
-    sib0, sib1, hots = [across(share_a, 1), across(share_b, 1)], [across(a1, 1)], [hot, across(hot, 1)]
-    a3, b1, by_x, by_y, sib0, sib1, hots = together((a3, b1, by_x, by_y, sib0, sib1, hots))
-    sib1, sib2 = sib1 + [across(b1, 1)], [across(a2, 1)]
+    sib0, hots = [across(share_a, 1), across(share_b, 1)], [hot, across(hot, 1)]
+    sib1, sib2 = [across(a1, 1), across(b1, 1)], [across(a2, 1)]
     piece = near.shape[1] // 2
     far_y, far_x = across(by_x[:, :piece], 4), across(by_y[:, piece:], 2)
     b2 = onward(b1)
     panel_full, extra = energy(meta, [near, by_x, by_y, far_y, far_x], ctf_table, inv)
-    b2, panel_full, extra, sib1, sib2 = together((b2, panel_full, extra, sib1, sib2))
+    a3, b2, panel_full, hots = together((a3, b2, panel_full, hots))
     b3 = onward(b2)
     sib2 = sib2 + [across(b2, 1)]
 

time: 241 us -> 233 us (0.967)
  waiting for transfers between devices: 124 us -> 113 us
  starting transfers between devices: 36.7 us -> 39.4 us
    ppermute x6, waiting for transfers between devices: 43.4 us -> 34.6 us  [onward(): lax.ppermute(value, 'rot', [(i, (i + 1) % turns) for i in range(turns)])]
  transfers between devices with their start and end apart: 48 -> 48, of which waited for: 25 -> 26; matrix products, arithmetic and copies ran while one was open for 2% -> 2% of each run, Pallas kernels for 23% -> 24%
where the time goes in v11:
time: 233 us; the launch traced here: 232 us
  waiting for transfers between devices  113 us (48%)
  Pallas kernels  69.6 us (30%)
  starting transfers between devices  39.4 us (17%)
  other arithmetic  6.82 us (3%)
    ppermute x35, waiting for transfers between devices, across(): return lax.ppermute(value, 'dom', [(i, i ^ apart) for i in range(dom)])  69.1 us
    ppermute x6, waiting for transfers between devices, onward(): lax.ppermute(value, 'rot', [(i, (i + 1) % turns) for i in range(turns)])  34.6 us
    ppermute x35, starting transfers between devices, across(): return lax.ppermute(value, 'dom', [(i, i ^ apart) for i in range(dom)])  27.9 us
    pallas_call x5, Pallas kernels, score(): call(functools.partial(score_body, parts, used, first, last), (2 * half,)...  26.3 us
    pallas_call x2, Pallas kernels, class_part(): call(functools.partial(class_body, kind, steps), (steps,), in_specs, out_...  15 us
    pallas_call x1, Pallas kernels, energy(): call(functools.partial(energy_body, bins, count), (count,), [pl.BlockSpec...  6.8 us
    ppermute x4, waiting for transfers between devices, by_core(): return lax.ppermute(value, 'dom', pairs)  6.4 us
    pallas_call x1, Pallas kernels, pack_next(): call(functools.partial(pack_next_body, cap, dom), (1,), [pl.BlockSpec((1,...  5.9 us
  transfers between devices with their start and end apart: 48, of which 26 were waited for; matrix products, arithmetic and copies ran while one was open for 2% of the time, Pallas kernels for 24%

profile of v11, /device:TPU:0, one launch (start us, length us, event | category | flops | bytes accessed | tf_op | source)
XLA Modules:
  0.0 231.5 jit_solution(12356326141492437124)
XLA Ops:
  1.2 0.7 add_select_fusion.slot_ref
  2.0 5.8 %shard_map.85 = (bf16[208,384]{1,0:T(8,128)(2,1)S(1)}, bf16[208,384]{1,0:T(8,128)(2,1)S(1)}, bf16[208,384]{1,0:T(8,128)(2,1)S(1)}, bf16[208,384]{1,0:T(8,128)(2,...) custom-call(s32[10]{0:T(128)S(1)} %stack.43.meta, ...), custom_call_target="tpu_custom_call" | custom-call | flops 113246208 | bytes 147456 | tf_op jit(solution)/shard_map/pallas_call | solution.py:132
  7.7 3.6 %collective-permute-start = (bf16[208,384]{1,0:T(8,128)(2,1)S(1)}, bf16[208,384]{1,0:T(8,128)(2,1)S(1)}, u32[]{:S(2)}, u32[]{:S(2)}) collective-permute-start(bf16[208,384]{1,0:T(8,128)(2,1)S(1)} %get-tuple-element.101), channel_id=1, source_target_pairs={{0,24},{4,28},{8,16},{12,20},{16,8},{20,12},{24,0},{28,4},{1,25},{... | collective-permute-start | bytes 479240 | tf_op jit(solution)/shard_map/ppermute | solution.py:535
  11.4 1.6 collective-permute-start.2
  13.1 1.5 collective-permute-start.3
  14.7 1.2 constant_dynamic-slice_fusion
  16.4 0.6 collective-permute-start.5
  17.0 2.3 %collective-permute-done.1.refs_1_ = bf16[208,384]{1,0:T(8,128)(2,1)S(1)} collective-permute-done((bf16[208,384]{1,0:T(8,128)(2,1)S(1)}, bf16[208,384]{1,0:T(8,128)(2,1)S(1)}, u32[]{:S(2)}, u32[]{:S(2)}) %collective-permute-start.1) | collective-permute-done | bytes 159776 | tf_op jit(solution)/shard_map/ppermute | solution.py:535
  19.6 5.9 %shard_map.86 = (bf16[192,640]{1,0:T(8,128)(2,1)S(1)}, bf16[192,640]{1,0:T(8,128)(2,1)S(1)}, bf16[192,640]{1,0:T(8,128)(2,1)S(1)}, bf16[192,640]{1,0:T(8,128)(2,...) custom-call(s32[10]{0:T(128)S(1)} %stack.43.meta, ...), custom_call_target="tpu_custom_call" | custom-call | flops 188743680 | bytes 245760 | tf_op jit(solution)/shard_map/pallas_call | solution.py:152
  26.5 3.5 %shard_map.87 = (bf16[768,384]{1,0:T(8,128)(2,1)S(1)}, bf16[192,768]{1,0:T(8,128)(2,1)S(1)}, bf16[768,1536]{1,0:T(8,128)(2,1)S(1)}, bf16[768,192]{1,0:T(8,128)(2,1)S(1)}) custom-call(s32[10]{0:T(128)S(1)} %stack.43.meta, bf16[208,384]{1,0:T(8,128)(2,1)S(1)} %collective-permute-done.refs_0_, bf16[208,384]{1,0:T(8,128)(2,1)S(1)} %collective-permute-done.1.refs_1_, ...), custom_call_target="tpu_custom_call" | custom-call | flops 56623104 | bytes 73728 | tf_op jit(solution)/shard_map/pallas_call | solution.py:212
  30.0 2.0 collective-permute-start.8
  32.1 1.8 collective-permute-start.10
  33.8 0.7 collective-permute-start.9
  34.5 6.6 %collective-permute-done.10.refs_1_ = bf16[192,640]{1,0:T(8,128)(2,1)S(1)} collective-permute-done((bf16[192,640]{1,0:T(8,128)(2,1)S(1)}, bf16[192,640]{1,0:T(8,128)(2,1)S(1)}, u32[]{:S(2)}, u32[]{:S(2)}) %collective-permute-start.10) | collective-permute-done | bytes 245792 | tf_op jit(solution)/shard_map/ppermute | solution.py:535
  41.1 5.4 %collective-permute-done.9.refs_0_ = bf16[192,640]{1,0:T(8,128)(2,1)S(1)} collective-permute-done((bf16[192,640]{1,0:T(8,128)(2,1)S(1)}, bf16[192,640]{1,0:T(8,128)(2,1)S(1)}, u32[]{:S(2)}, u32[]{:S(2)}) %collective-permute-start.9) | collective-permute-done | bytes 245792 | tf_op jit(solution)/shard_map/ppermute | solution.py:535
  46.5 1.1 collective-permute-done.8.refs_0_
  48.1 1.3 collective-permute-start.12
  49.4 1.5 collective-permute-start.13
  50.9 1.0 collective-permute-start.15
  51.8 5.1 %collective-permute-done.12.refs_2_ = bf16[192,640]{1,0:T(8,128)(2,1)S(1)} collective-permute-done((bf16[192,640]{1,0:T(8,128)(2,1)S(1)}, bf16[192,640]{1,0:T(8,128)(2,1)S(1)}, u32[]{:S(2)}, u32[]{:S(2)}) %collective-permute-start.12) | collective-permute-done | bytes 245792 | tf_op jit(solution)/shard_map/ppermute | solution.py:535
  56.9 1.3 collective-permute-done.13.refs_3_
  58.3 1.6 collective-permute-done.14.refs_4_
  59.9 1.2 collective-permute-done.15.refs_5_
  61.1 2.9 %shard_map.88.refs_1_ = bf16[768,640]{1,0:T(8,128)(2,1)S(1)} custom-call(s32[10]{0:T(128)S(1)} %stack.43.meta, bf16[192,640]{1,0:T(8,128)(2,1)S(1)} %collective-permute-done.9.refs_0_, bf16[192,640]{1,0:T(8,128)(2,1)S(1)} %collective-permute-done.10.refs_1_, bf16[192,640]{1,0:T(8,128)(2,1)S(1)} %collective-permute-done.12.refs_2_, ...), custom_call_target="tpu_custom_call" | custom-call | flops 94371840 | bytes 122880 | tf_op jit(solution)/shard_map/pallas_call | solution.py:231
  64.1 1.3 collective-permute-start.20
  65.3 1.5 collective-permute-start.21
  67.8 25.5 %collective-permute-done.18.refs_1_ = bf16[768,640]{1,0:T(8,128)(2,1)S(1)} collective-permute-done((bf16[768,640]{1,0:T(8,128)(2,1)S(1)}, bf16[768,640]{1,0:T(8,128)(2,1)S(1)}, u32[]{:S(2)}, u32[]{:S(2)}) %collective-permute-start.18) | collective-permute-done | bytes 983072 | tf_op jit(solution)/shard_map/ppermute | solution.py:542
  93.3 5.8 %collective-permute-done.20.refs_1_ = bf16[720,1024]{1,0:T(8,128)(2,1)S(1)} collective-permute-done((bf16[720,1024]{1,0:T(8,128)(2,1)S(1)}, bf16[720,1024]{1,0:T(8,128)(2,1)S(1)}, u32[]{:S(2)}, u32[]{:S(2)}) %collective-permute-start.20) | collective-permute-done | bytes 1474592 | tf_op jit(solution)/shard_map/ppermute | solution.py:535
  99.2 0.9 collective-permute-start.22
  100.5 1.2 collective-permute-start.23
  101.9 4.0 %collective-permute-done.17.refs_0_ = bf16[768,384]{1,0:T(8,128)(2,1)S(1)} collective-permute-done((bf16[768,384]{1,0:T(8,128)(2,1)S(1)}, bf16[768,384]{1,0:T(8,128)(2,1)S(1)}, u32[]{:S(2)}, u32[]{:S(2)}) %collective-permute-start.17) | collective-permute-done | bytes 589856 | tf_op jit(solution)/shard_map/ppermute | solution.py:542
  105.9 12.0 %collective-permute-done.22.refs_3_ = bf16[720,512]{1,0:T(8,128)(2,1)S(1)} collective-permute-done((bf16[720,512]{1,0:T(8,128)(2,1)S(1)}, bf16[720,512]{1,0:T(8,128)(2,1)S(1)}, u32[]{:S(2)}, u32[]{:S(2)}) %collective-permute-start.22) | collective-permute-done | bytes 737312 | tf_op jit(solution)/shard_map/ppermute | solution.py:535
  117.9 1.3 collective-permute-done.23.refs_4_
  119.2 6.8 %shard_map.89 = (bf16[720,4096]{1,0:T(8,128)(2,1)S(1)}, bf16[720,192]{1,0:T(8,128)(2,1)S(1)}) custom-call(s32[10]{0:T(128)S(1)} %stack.43.meta, bf16[720,1024]{1,0:T(8,128)(2,1)S(1)} %pad_maximum_fusion.refs_0_, bf16[720,1024]{1,0:T(8,128)(2,1)S(1)} %collective-permute-done.20.refs_1_, bf16[720,1024]{1,0:T(8,128)(2,1)S(1)} %collective-permute-done.21.refs_2_, ...), custom_call_target="tpu_custom_call" | custom-call | flops 283115520 | bytes 737280 | tf_op jit(solution)/shard_map/pallas_call | solution.py:283
  126.6 1.3 collective-permute-start.25
  128.4 5.1 %shard_map.90 = (f32[720,1536]{1,0:T(8,128)S(1)}, bf16[1536,4096]{1,0:T(8,128)(2,1)S(1)}) custom-call(s32[10]{0:T(128)S(1)} %stack.43.meta, bf16[768,384]{1,0:T(8,128)(2,1)S(1)} %get-tuple-element.137.refs_0_, bf16[768,640]{1,0:T(8,128)(2,1)S(1)} %shard_map.88.refs_1_, bf16[768,384]{1,0:T(8,128)(2,1)S(1)} %collective-permute-done.31.refs_2_, ...), custom_call_target="tpu_custom_call" | custom-call | flops 141557760 | bytes 946176 | tf_op jit(solution)/shard_map/pallas_call | solution.py:387
  133.5 5.5 %shard_map.91 = (f32[720,1536]{1,0:T(8,128)S(1)}, bf16[1536,4096]{1,0:T(8,128)(2,1)S(1)}) custom-call(s32[10]{0:T(128)S(1)} %stack.43.meta, bf16[768,384]{1,0:T(8,128)(2,1)S(1)} %collective-permute-done.8.refs_0_, bf16[768,640]{1,0:T(8,128)(2,1)S(1)} %collective-permute-done.18.refs_1_, ...), custom_call_target="tpu_custom_call", output_to_operand_aliasing={{0}: (6, {}), {1}: (7, {})} | custom-call | flops 141557760 | bytes 946176 | tf_op jit(solution)/shard_map/pallas_call | solution.py:387
  139.0 5.4 %shard_map.92 = (f32[720,1536]{1,0:T(8,128)S(1)}, bf16[1536,4096]{1,0:T(8,128)(2,1)S(1)}) custom-call(s32[10]{0:T(128)S(1)} %stack.43.meta, bf16[768,384]{1,0:T(8,128)(2,1)S(1)} %collective-permute-done.11.refs_0_, bf16[768,640]{1,0:T(8,128)(2,1)S(1)} %collective-permute-done.19.refs_1_, ...), custom_call_target="tpu_custom_call", output_to_operand_aliasing={{0}: (6, {}), {1}: (7, {})} | custom-call | flops 141557760 | bytes 946176 | tf_op jit(solution)/shard_map/pallas_call | solution.py:387
  144.5 3.7 %shard_map.93.refs_5_ = f32[720,1536]{1,0:T(8,128)S(1)} custom-call(s32[10]{0:T(128)S(1)} %stack.43.meta, bf16[768,384]{1,0:T(8,128)(2,1)S(1)} %collective-permute-done.17.refs_0_, bf16[768,384]{1,0:T(8,128)(2,1)S(1)} %collective-permute-done.26.refs_1_.refs_2_, ...), custom_call_target="tpu_custom_call", output_to_operand_aliasing={{}: (4, {})} | custom-call | flops 141557760 | bytes 946176 | tf_op jit(solution)/shard_map/pallas_call | solution.py:387
  148.2 3.9 %collective-permute-done.25.refs_1_ = bf16[768,640]{1,0:T(8,128)(2,1)S(1)} collective-permute-done((bf16[768,640]{1,0:T(8,128)(2,1)S(1)}, bf16[768,640]{1,0:T(8,128)(2,1)S(1)}, u32[]{:S(2)}, u32[]{:S(2)}) %collective-permute-start.25) | collective-permute-done | bytes 983072 | tf_op jit(solution)/shard_map/ppermute | solution.py:542
  152.1 2.6 %collective-permute-done.33.refs_3_ = bf16[768,640]{1,0:T(8,128)(2,1)S(1)} collective-permute-done((bf16[768,640]{1,0:T(8,128)(2,1)S(1)}, bf16[768,640]{1,0:T(8,128)(2,1)S(1)}, u32[]{:S(2)}, u32[]{:S(2)}) %collective-permute-start.33) | collective-permute-done | bytes 983072 | tf_op jit(solution)/shard_map/ppermute | solution.py:535
  154.7 6.6 %shard_map.94 = (f32[720,1536]{1,0:T(8,128)S(1)}, f32[8,1536]{1,0:T(8,128)S(1)}, bf16[1536,4096]{1,0:T(8,128)(2,1)S(1)}) custom-call(s32[10]{0:T(128)S(1)} %stack.43.meta, bf16[768,384]{1,0:T(8,128)(2,1)S(1)} %collective-permute-done.17.refs_0_, bf16[768,640]{1,0:T(8,128)(2,1)S(1)} %collective-permute-done.25.refs_1_, ...), custom_call_target="tpu_custom_call", output_to_operand_aliasing={{0}: (6, {}), {2}: (7, {})} | custom-call | flops 141557760 | bytes 946176 | tf_op jit(solution)/shard_map/pallas_call | solution.py:387
  161.5 1.1 collective-permute-done.34.other_ref
  163.2 0.9 collective-permute-start.36
  164.1 3.5 %collective-permute-start.37 = (f32[8,1536]{1,0:T(8,128)S(1)}, f32[8,1536]{1,0:T(8,128)S(1)}, u32[]{:S(2)}, u32[]{:S(2)}) collective-permute-start(f32[8,1536]{1,0:T(8,128)S(1)} %shard_map.95.refs_2_), channel_id=1, source_target_pairs={{0,3},{1,2},{2,1},{3,0},{4,7},{5,6},{6,5},{7,4},{8,11},{9,10},{10,... | collective-permute-start | bytes 147464 | tf_op jit(solution)/shard_map/ppermute | solution.py:610
  167.9 2.7 %collective-permute-done.36.refs_4_ = f32[8,1536]{1,0:T(8,128)S(1)} collective-permute-done((f32[8,1536]{1,0:T(8,128)S(1)}, f32[8,1536]{1,0:T(8,128)S(1)}, u32[]{:S(2)}, u32[]{:S(2)}) %collective-permute-start.36) | collective-permute-done | bytes 49184 | tf_op jit(solution)/shard_map/ppermute | solution.py:610
  170.7 4.2 %shard_map.96 = (bf16[720,512]{1,0:T(8,128)(2,1)S(1)}, bf16[720,512]{1,0:T(8,128)(2,1)S(1)}, bf16[720,1536]{1,0:T(8,128)(2,1)S(1)}, f32[1,768]{1,0:T(1,128)S(1)}, bf16[64,720]{1,0:T(8,128)(2,1)S(1)}) custom-call(s32[10]{0:T(128)S(1)} %stack.43.meta, f32[720,1536]{1,0:T(8,128)S(1)} %get-tuple-element.171.refs_0_, ...), custom_call_target="tpu_custom_call" | custom-call | flops 141557760 | bytes 657408 | tf_op jit(solution)/shard_map/pallas_call | solution.py:475
  174.9 1.4 collective-permute-start.38
  176.3 0.8 collective-permute-start.39
  177.2 1.0 collective-permute-start.40
  178.2 10.7 %shard_map.97 = (bf16[720,512]{1,0:T(8,128)(2,1)S(1)}, bf16[720,512]{1,0:T(8,128)(2,1)}, bf16[720,512]{1,0:T(8,128)(2,1)}, f32[720,512]{1,0:T(8,128)S(1)}, f32[7...) custom-call(s32[10]{0:T(128)S(1)} %stack.43.meta, bf16[720,1536]{1,0:T(8,128)(2,1)S(1)} %get-tuple-element.176.refs_0_, ...), custom_call_target="tpu_custom_call" | custom-call | flops 424673280 | bytes 1419264 | tf_op jit(solution)/shard_map/pallas_call | solution.py:475
  188.9 5.0 %collective-permute-done.40.other_ref = bf16[64,720]{1,0:T(8,128)(2,1)S(1)} collective-permute-done((bf16[64,720]{1,0:T(8,128)(2,1)S(1)}, bf16[64,720]{1,0:T(8,128)(2,1)S(1)}, u32[]{:S(2)}, u32[]{:S(2)}) %collective-permute-start.40) | collective-permute-done | bytes 92192 | tf_op jit(solution)/shard_map/ppermute | solution.py:535
  193.9 1.4 fusion.3
  195.3 1.2 collective-permute-start.42
  196.5 1.0 collective-permute-start.43
  198.1 1.3 collective-permute-start.41
  199.3 0.9 collective-permute-start.44
  200.3 16.6 %collective-permute-done.41 = bf16[64,720]{1,0:T(8,128)(2,1)S(1)} collective-permute-done((bf16[64,720]{1,0:T(8,128)(2,1)S(1)}, bf16[64,720]{1,0:T(8,128)(2,1)S(1)}, u32[]{:S(2)}, u32[]{:S(2)}) %collective-permute-start.41) | collective-permute-done | bytes 92192 | tf_op jit(solution)/shard_map/ppermute | solution.py:535
  216.9 1.5 collective-permute-start.46
  219.0 2.3 shard_map.99
  221.3 0.9 maximum_select_fusion
  222.2 2.6 %collective-permute-done.47 = bf16[720,512]{1,0:T(8,128)(2,1)} collective-permute-done((bf16[720,512]{1,0:T(8,128)(2,1)}, bf16[720,512]{1,0:T(8,128)(2,1)}, u32[]{:S(2)}, u32[]{:S(2)}) %collective-permute-start.47) | collective-permute-done | bytes 737312 | tf_op jit(solution)/shard_map/ppermute | solution.py:539
  224.8 3.8 %collective-permute-done.45 = bf16[720,512]{1,0:T(8,128)(2,1)} collective-permute-done((bf16[720,512]{1,0:T(8,128)(2,1)}, bf16[720,512]{1,0:T(8,128)(2,1)}, u32[]{:S(2)}, u32[]{:S(2)}) %collective-permute-start.45) | collective-permute-done | bytes 737312 | tf_op jit(solution)/shard_map/ppermute | solution.py:539
  228.6 2.9 %add_dynamic-update-slice_fusion = f32[1440,512]{1,0:T(8,128)} fusion(f32[1440,512]{1,0:T(8,128)} %shard_map.99, s32[]{:T(128)S(6)} %select_n.67, bf16[720,512]{1,0:T(8,128)(2,1)} %collective-permute-done.47, bf16[720,512]{1,0:T(8,128)(2,1)} %collective-permute-done.45, bf16[720,512]{1,0:T(8,128)(2,1)} %collective-permute-done.44), kind=kLoop, calls=%fused_computation.7 | loop fusion | flops 1843200 | bytes 3686404 | tf_op jit(solution)/shard_map/dynamic_update_slice | solution.py:639
  (65 shorter events, 8.2 us)
Async XLA Ops:
  0.6 14.0 %collective-permute-start.7 = (bf16[1440,512]{1,0:T(8,128)(2,1)}, bf16[1440,512]{1,0:T(8,128)(2,1)}, u32[]{:S(2)}, u32[]{:S(2)}) collective-permute-start(bf16[1440,512]{1,0:T(8,128)(2,1)} %param.11), channel_id=1, source_target_pairs={{0,4},{4,0},{8,12},{12,8},{16,20},{20,16},{24,28},{28,24},{1,5},{5... | collective-permute-start | bytes 4423688 | tf_op jit(solution)/shard_map/ppermute | solution.py:535
  2.0 12.6 %copy-start.2 = (bf16[1440,512]{1,0:T(8,128)(2,1)S(1)}, bf16[1440,512]{1,0:T(8,128)(2,1)}, u32[]{:S(2)}) copy-start(bf16[1440,512]{1,0:T(8,128)(2,1)} %param.11) | copy-start | bytes 4423684
  7.7 8.6 %collective-permute-start = (bf16[208,384]{1,0:T(8,128)(2,1)S(1)}, bf16[208,384]{1,0:T(8,128)(2,1)S(1)}, u32[]{:S(2)}, u32[]{:S(2)}) collective-permute-start(bf16[208,384]{1,0:T(8,128)(2,1)S(1)} %get-tuple-element.101), channel_id=1, source_target_pairs={{0,24},{4,28},{8,16},{12,20},{16,8},{20,12},{24,0},{28,4},{1,25},{... | collective-permute-start | bytes 479240 | tf_op jit(solution)/shard_map/ppermute | solution.py:535
  11.3 8.0 %collective-permute-start.1 = (bf16[208,384]{1,0:T(8,128)(2,1)S(1)}, bf16[208,384]{1,0:T(8,128)(2,1)S(1)}, u32[]{:S(2)}, u32[]{:S(2)}) collective-permute-start(bf16[208,384]{1,0:T(8,128)(2,1)S(1)} %get-tuple-element.102), channel_id=1, source_target_pairs={{0,28},{4,24},{8,20},{12,16},{16,12},{20,8},{24,4},{28,0},{1,29},{... | collective-permute-start | bytes 479240 | tf_op jit(solution)/shard_map/ppermute | solution.py:535
  11.4 14.2 %collective-permute-start.2 = (bf16[208,384]{1,0:T(8,128)(2,1)S(1)}, bf16[208,384]{1,0:T(8,128)(2,1)S(1)}, u32[]{:S(2)}, u32[]{:S(2)}) collective-permute-start(bf16[208,384]{1,0:T(8,128)(2,1)S(1)} %get-tuple-element.103), channel_id=1, source_target_pairs={{0,16},{4,20},{8,24},{12,28},{16,0},{20,4},{24,8},{28,12},{1,17},{... | collective-permute-start | bytes 479240 | tf_op jit(solution)/shard_map/ppermute | solution.py:535
  13.1 12.6 %collective-permute-start.3 = (bf16[208,384]{1,0:T(8,128)(2,1)S(1)}, bf16[208,384]{1,0:T(8,128)(2,1)S(1)}, u32[]{:S(2)}, u32[]{:S(2)}) collective-permute-start(bf16[208,384]{1,0:T(8,128)(2,1)S(1)} %get-tuple-element.104), channel_id=1, source_target_pairs={{0,8},{4,12},{8,0},{12,4},{16,24},{20,28},{24,16},{28,20},{1,9},{5... | collective-permute-start | bytes 479240 | tf_op jit(solution)/shard_map/ppermute | solution.py:535
  14.6 11.6 %collective-permute-start.4 = (bf16[208,384]{1,0:T(8,128)(2,1)S(1)}, bf16[208,384]{1,0:T(8,128)(2,1)S(1)}, u32[]{:S(2)}, u32[]{:S(2)}) collective-permute-start(bf16[208,384]{1,0:T(8,128)(2,1)S(1)} %get-tuple-element.105), channel_id=1, source_target_pairs={{0,20},{4,16},{8,28},{12,24},{16,4},{20,0},{24,12},{28,8},{1,21},{... | collective-permute-start | bytes 479240 | tf_op jit(solution)/shard_map/ppermute | solution.py:535
  16.4 9.9 %collective-permute-start.5 = (bf16[208,384]{1,0:T(8,128)(2,1)S(1)}, bf16[208,384]{1,0:T(8,128)(2,1)S(1)}, u32[]{:S(2)}, u32[]{:S(2)}) collective-permute-start(bf16[208,384]{1,0:T(8,128)(2,1)S(1)} %get-tuple-element.106), channel_id=1, source_target_pairs={{0,12},{4,8},{8,4},{12,0},{16,28},{20,24},{24,20},{28,16},{1,13},{... | collective-permute-start | bytes 479240 | tf_op jit(solution)/shard_map/ppermute | solution.py:535
  19.3 6.9 %collective-permute-start.6 = (bf16[208,384]{1,0:T(8,128)(2,1)S(1)}, bf16[208,384]{1,0:T(8,128)(2,1)S(1)}, u32[]{:S(2)}, u32[]{:S(2)}) collective-permute-start(bf16[208,384]{1,0:T(8,128)(2,1)S(1)} %get-tuple-element.107), channel_id=1, source_target_pairs={{0,4},{4,0},{8,12},{12,8},{16,20},{20,16},{24,28},{28,24},{1,5},{5... | collective-permute-start | bytes 479240 | tf_op jit(solution)/shard_map/ppermute | solution.py:535
  25.5 1.0 copy-start
  25.5 1.0 copy-start.1
  30.0 17.6 %collective-permute-start.8 = (bf16[768,384]{1,0:T(8,128)(2,1)S(1)}, bf16[768,384]{1,0:T(8,128)(2,1)S(1)}, u32[]{:S(2)}, u32[]{:S(2)}) collective-permute-start(bf16[768,384]{1,0:T(8,128)(2,1)S(1)} %get-tuple-element.137.refs_0_), channel_id=1, source_target_pairs={{0,1},{1,2},{2,3},{3,0},{4,5},{5,6},{6,7},{7,4},{8,9},{9,10},{10,1... | collective-permute-start | bytes 1769480 | tf_op jit(solution)/shard_map/ppermute | solution.py:542
  32.1 9.1 %collective-permute-start.10 = (bf16[192,640]{1,0:T(8,128)(2,1)S(1)}, bf16[192,640]{1,0:T(8,128)(2,1)S(1)}, u32[]{:S(2)}, u32[]{:S(2)}) collective-permute-start(bf16[192,640]{1,0:T(8,128)(2,1)S(1)} %get-tuple-element.139), channel_id=1, source_target_pairs={{0,28},{4,24},{8,20},{12,16},{16,12},{20,8},{24,4},{28,0},{1,29},{... | collective-permute-start | bytes 737288 | tf_op jit(solution)/shard_map/ppermute | solution.py:535
  33.8 12.6 %collective-permute-start.9 = (bf16[192,640]{1,0:T(8,128)(2,1)S(1)}, bf16[192,640]{1,0:T(8,128)(2,1)S(1)}, u32[]{:S(2)}, u32[]{:S(2)}) collective-permute-start(bf16[192,640]{1,0:T(8,128)(2,1)S(1)} %get-tuple-element.138), channel_id=1, source_target_pairs={{0,24},{4,28},{8,16},{12,20},{16,8},{20,12},{24,0},{28,4},{1,25},{... | collective-permute-start | bytes 737288 | tf_op jit(solution)/shard_map/ppermute | solution.py:535
  47.6 16.5 %collective-permute-start.11 = (bf16[768,384]{1,0:T(8,128)(2,1)S(1)}, bf16[768,384]{1,0:T(8,128)(2,1)S(1)}, u32[]{:S(2)}, u32[]{:S(2)}) collective-permute-start(bf16[768,384]{1,0:T(8,128)(2,1)S(1)} %collective-permute-done.8.refs_0_), channel_id=1, source_target_pairs={{0,1},{1,2},{2,3},{3,0},{4,5},{5,6},{6,7},{7,4},{8,9},{9,10},{10,1... | collective-permute-start | bytes 1769480 | tf_op jit(solution)/shard_map/ppermute | solution.py:542
  48.1 8.9 %collective-permute-start.12 = (bf16[192,640]{1,0:T(8,128)(2,1)S(1)}, bf16[192,640]{1,0:T(8,128)(2,1)S(1)}, u32[]{:S(2)}, u32[]{:S(2)}) collective-permute-start(bf16[192,640]{1,0:T(8,128)(2,1)S(1)} %get-tuple-element.143), channel_id=1, source_target_pairs={{0,16},{4,20},{8,24},{12,28},{16,0},{20,4},{24,8},{28,12},{1,17},{... | collective-permute-start | bytes 737288 | tf_op jit(solution)/shard_map/ppermute | solution.py:535
  49.4 8.9 %collective-permute-start.13 = (bf16[192,640]{1,0:T(8,128)(2,1)S(1)}, bf16[192,640]{1,0:T(8,128)(2,1)S(1)}, u32[]{:S(2)}, u32[]{:S(2)}) collective-permute-start(bf16[192,640]{1,0:T(8,128)(2,1)S(1)} %get-tuple-element.144), channel_id=1, source_target_pairs={{0,8},{4,12},{8,0},{12,4},{16,24},{20,28},{24,16},{28,20},{1,9},{5... | collective-permute-start | bytes 737288 | tf_op jit(solution)/shard_map/ppermute | solution.py:535
  50.9 9.0 %collective-permute-start.14 = (bf16[192,640]{1,0:T(8,128)(2,1)S(1)}, bf16[192,640]{1,0:T(8,128)(2,1)S(1)}, u32[]{:S(2)}, u32[]{:S(2)}) collective-permute-start(bf16[192,640]{1,0:T(8,128)(2,1)S(1)} %get-tuple-element.145), channel_id=1, source_target_pairs={{0,20},{4,16},{8,28},{12,24},{16,4},{20,0},{24,12},{28,8},{1,21},{... | collective-permute-start | bytes 737288 | tf_op jit(solution)/shard_map/ppermute | solution.py:535
  50.9 10.2 %collective-permute-start.15 = (bf16[192,640]{1,0:T(8,128)(2,1)S(1)}, bf16[192,640]{1,0:T(8,128)(2,1)S(1)}, u32[]{:S(2)}, u32[]{:S(2)}) collective-permute-start(bf16[192,640]{1,0:T(8,128)(2,1)S(1)} %get-tuple-element.146), channel_id=1, source_target_pairs={{0,12},{4,8},{8,4},{12,0},{16,28},{20,24},{24,20},{28,16},{1,13},{... | collective-permute-start | bytes 737288 | tf_op jit(solution)/shard_map/ppermute | solution.py:535
  56.9 4.2 %collective-permute-start.16 = (bf16[192,640]{1,0:T(8,128)(2,1)S(1)}, bf16[192,640]{1,0:T(8,128)(2,1)S(1)}, u32[]{:S(2)}, u32[]{:S(2)}) collective-permute-start(bf16[192,640]{1,0:T(8,128)(2,1)S(1)} %get-tuple-element.147), channel_id=1, source_target_pairs={{0,4},{4,0},{8,12},{12,8},{16,20},{20,16},{24,28},{28,24},{1,5},{5... | collective-permute-start | bytes 737288 | tf_op jit(solution)/shard_map/ppermute | solution.py:535
  64.1 35.0 %collective-permute-start.20 = (bf16[720,1024]{1,0:T(8,128)(2,1)S(1)}, bf16[720,1024]{1,0:T(8,128)(2,1)S(1)}, u32[]{:S(2)}, u32[]{:S(2)}) collective-permute-start(bf16[720,1024]{1,0:T(8,128)(2,1)S(1)} %pad_maximum_fusion.refs_0_), channel_id=1, source_target_pairs={{0,8},{4,12},{8,0},{12,4},{16,24},{20,28},{24,16},{28,20},{1,9},{5... | collective-permute-start | bytes 4423688 | tf_op jit(solution)/shard_map/ppermute | solution.py:535
  65.3 35.1 %collective-permute-start.21 = (bf16[720,1024]{1,0:T(8,128)(2,1)S(1)}, bf16[720,1024]{1,0:T(8,128)(2,1)S(1)}, u32[]{:S(2)}, u32[]{:S(2)}) collective-permute-start(bf16[720,1024]{1,0:T(8,128)(2,1)S(1)} %pad_maximum_fusion.refs_0_), channel_id=1, source_target_pairs={{0,16},{4,20},{8,24},{12,28},{16,0},{20,4},{24,8},{28,12},{1,17},{... | collective-permute-start | bytes 4423688 | tf_op jit(solution)/shard_map/ppermute | solution.py:535
  66.9 26.4 %collective-permute-start.18 = (bf16[768,640]{1,0:T(8,128)(2,1)S(1)}, bf16[768,640]{1,0:T(8,128)(2,1)S(1)}, u32[]{:S(2)}, u32[]{:S(2)}) collective-permute-start(bf16[768,640]{1,0:T(8,128)(2,1)S(1)} %shard_map.88.refs_1_), channel_id=1, source_target_pairs={{0,1},{1,2},{2,3},{3,0},{4,5},{5,6},{6,7},{7,4},{8,9},{9,10},{10,1... | collective-permute-start | bytes 2949128 | tf_op jit(solution)/shard_map/ppermute | solution.py:542
  67.3 38.7 %collective-permute-start.17 = (bf16[768,384]{1,0:T(8,128)(2,1)S(1)}, bf16[768,384]{1,0:T(8,128)(2,1)S(1)}, u32[]{:S(2)}, u32[]{:S(2)}) collective-permute-start(bf16[768,384]{1,0:T(8,128)(2,1)S(1)} %collective-permute-done.11.refs_0_), channel_id=1, source_target_pairs={{0,1},{1,2},{2,3},{3,0},{4,5},{5,6},{6,7},{7,4},{8,9},{9,10},{10,1... | collective-permute-start | bytes 1769480 | tf_op jit(solution)/shard_map/ppermute | solution.py:542
  93.3 32.7 %collective-permute-start.19 = (bf16[768,640]{1,0:T(8,128)(2,1)S(1)}, bf16[768,640]{1,0:T(8,128)(2,1)S(1)}, u32[]{:S(2)}, u32[]{:S(2)}) collective-permute-start(bf16[768,640]{1,0:T(8,128)(2,1)S(1)} %collective-permute-done.18.refs_1_), channel_id=1, source_target_pairs={{0,1},{1,2},{2,3},{3,0},{4,5},{5,6},{6,7},{7,4},{8,9},{9,10},{10,1... | collective-permute-start | bytes 2949128 | tf_op jit(solution)/shard_map/ppermute | solution.py:542
  99.2 18.7 %collective-permute-start.22 = (bf16[720,512]{1,0:T(8,128)(2,1)S(1)}, bf16[720,512]{1,0:T(8,128)(2,1)S(1)}, u32[]{:S(2)}, u32[]{:S(2)}) collective-permute-start(bf16[720,512]{1,0:T(8,128)(2,1)S(1)} %slice.8), channel_id=1, source_target_pairs={{0,16},{4,20},{8,24},{12,28},{16,0},{20,4},{24,8},{28,12},{1,17},{... | collective-permute-start | bytes 2211848 | tf_op jit(solution)/shard_map/ppermute | solution.py:535
  100.1 1.6 collective-permute-start.24
  100.5 18.7 %collective-permute-start.23 = (bf16[720,512]{1,0:T(8,128)(2,1)S(1)}, bf16[720,512]{1,0:T(8,128)(2,1)S(1)}, u32[]{:S(2)}, u32[]{:S(2)}) collective-permute-start(bf16[720,512]{1,0:T(8,128)(2,1)S(1)} %slice.9), channel_id=1, source_target_pairs={{0,8},{4,12},{8,0},{12,4},{16,24},{20,28},{24,16},{28,20},{1,9},{5... | collective-permute-start | bytes 2211848 | tf_op jit(solution)/shard_map/ppermute | solution.py:535
  101.7 26.2 %collective-permute-start.32 = (bf16[768,640]{1,0:T(8,128)(2,1)S(1)}, bf16[768,640]{1,0:T(8,128)(2,1)S(1)}, u32[]{:S(2)}, u32[]{:S(2)}) collective-permute-start(bf16[768,640]{1,0:T(8,128)(2,1)S(1)} %shard_map.88.refs_1_), channel_id=1, source_target_pairs={{0,4},{4,0},{8,12},{12,8},{16,20},{20,16},{24,28},{28,24},{1,5},{5... | collective-permute-start | bytes 2949128 | tf_op jit(solution)/shard_map/ppermute | solution.py:535
  105.9 20.6 %collective-permute-start.31 = (bf16[768,384]{1,0:T(8,128)(2,1)S(1)}, bf16[768,384]{1,0:T(8,128)(2,1)S(1)}, u32[]{:S(2)}, u32[]{:S(2)}) collective-permute-start(bf16[768,384]{1,0:T(8,128)(2,1)S(1)} %get-tuple-element.137.refs_0_), channel_id=1, source_target_pairs={{0,4},{4,0},{8,12},{12,8},{16,20},{20,16},{24,28},{28,24},{1,5},{5... | collective-permute-start | bytes 1769480 | tf_op jit(solution)/shard_map/ppermute | solution.py:535
  117.9 10.0 %collective-permute-start.29 = (bf16[768,384]{1,0:T(8,128)(2,1)S(1)}, bf16[768,384]{1,0:T(8,128)(2,1)S(1)}, u32[]{:S(2)}, u32[]{:S(2)}) collective-permute-start(bf16[768,384]{1,0:T(8,128)(2,1)S(1)} %collective-permute-done.8.refs_0_), channel_id=1, source_target_pairs={{0,4},{4,0},{8,12},{12,8},{16,20},{20,16},{24,28},{28,24},{1,5},{5... | collective-permute-start | bytes 1769480 | tf_op jit(solution)/shard_map/ppermute | solution.py:535
  119.2 14.3 %collective-permute-start.30 = (bf16[768,640]{1,0:T(8,128)(2,1)S(1)}, bf16[768,640]{1,0:T(8,128)(2,1)S(1)}, u32[]{:S(2)}, u32[]{:S(2)}) collective-permute-start(bf16[768,640]{1,0:T(8,128)(2,1)S(1)} %collective-permute-done.18.refs_1_), channel_id=1, source_target_pairs={{0,4},{4,0},{8,12},{12,8},{16,20},{20,16},{24,28},{28,24},{1,5},{5... | collective-permute-start | bytes 2949128 | tf_op jit(solution)/shard_map/ppermute | solution.py:535
  126.0 13.0 %collective-permute-start.28 = (bf16[768,640]{1,0:T(8,128)(2,1)S(1)}, bf16[768,640]{1,0:T(8,128)(2,1)S(1)}, u32[]{:S(2)}, u32[]{:S(2)}) collective-permute-start(bf16[768,640]{1,0:T(8,128)(2,1)S(1)} %collective-permute-done.19.refs_1_), channel_id=1, source_target_pairs={{0,4},{4,0},{8,12},{12,8},{16,20},{20,16},{24,28},{28,24},{1,5},{5... | collective-permute-start | bytes 2949128 | tf_op jit(solution)/shard_map/ppermute | solution.py:535
  126.6 25.5 %collective-permute-start.25 = (bf16[768,640]{1,0:T(8,128)(2,1)S(1)}, bf16[768,640]{1,0:T(8,128)(2,1)S(1)}, u32[]{:S(2)}, u32[]{:S(2)}) collective-permute-start(bf16[768,640]{1,0:T(8,128)(2,1)S(1)} %collective-permute-done.19.refs_1_), channel_id=1, source_target_pairs={{0,1},{1,2},{2,3},{3,0},{4,5},{5,6},{6,7},{7,4},{8,9},{9,10},{10,1... | collective-permute-start | bytes 2949128 | tf_op jit(solution)/shard_map/ppermute | solution.py:542
  127.9 11.1 %collective-permute-start.27 = (bf16[768,384]{1,0:T(8,128)(2,1)S(1)}, bf16[768,384]{1,0:T(8,128)(2,1)S(1)}, u32[]{:S(2)}, u32[]{:S(2)}) collective-permute-start(bf16[768,384]{1,0:T(8,128)(2,1)S(1)} %collective-permute-done.11.refs_0_), channel_id=1, source_target_pairs={{0,4},{4,0},{8,12},{12,8},{16,20},{20,16},{24,28},{28,24},{1,5},{5... | collective-permute-start | bytes 1769480 | tf_op jit(solution)/shard_map/ppermute | solution.py:535
  127.9 16.5 %collective-permute-start.26 = (bf16[768,384]{1,0:T(8,128)(2,1)S(1)}, bf16[768,384]{1,0:T(8,128)(2,1)S(1)}, u32[]{:S(2)}, u32[]{:S(2)}) collective-permute-start(bf16[768,384]{1,0:T(8,128)(2,1)S(1)} %collective-permute-done.17.refs_0_), channel_id=1, source_target_pairs={{0,4},{4,0},{8,12},{12,8},{16,20},{20,16},{24,28},{28,24},{1,5},{5... | collective-permute-start | bytes 1769480 | tf_op jit(solution)/shard_map/ppermute | solution.py:535
  152.1 2.6 %collective-permute-start.33 = (bf16[768,640]{1,0:T(8,128)(2,1)S(1)}, bf16[768,640]{1,0:T(8,128)(2,1)S(1)}, u32[]{:S(2)}, u32[]{:S(2)}) collective-permute-start(bf16[768,640]{1,0:T(8,128)(2,1)S(1)} %collective-permute-done.25.refs_1_), channel_id=1, source_target_pairs={{0,4},{4,0},{8,12},{12,8},{16,20},{20,16},{24,28},{28,24},{1,5},{5... | collective-permute-start | bytes 2949128 | tf_op jit(solution)/shard_map/ppermute | solution.py:535
  161.3 1.3 collective-permute-start.34
  163.2 4.8 %collective-permute-start.35 = (f32[8,1536]{1,0:T(8,128)S(1)}, f32[8,1536]{1,0:T(8,128)S(1)}, u32[]{:S(2)}, u32[]{:S(2)}) collective-permute-start(f32[8,1536]{1,0:T(8,128)S(1)} %shard_map.95.refs_2_), channel_id=1, source_target_pairs={{0,1},{1,0},{2,3},{3,2},{4,5},{5,4},{6,7},{7,6},{8,9},{9,8},{10,11... | collective-permute-start | bytes 147464 | tf_op jit(solution)/shard_map/ppermute | solution.py:610
  163.2 7.4 %collective-permute-start.36 = (f32[8,1536]{1,0:T(8,128)S(1)}, f32[8,1536]{1,0:T(8,128)S(1)}, u32[]{:S(2)}, u32[]{:S(2)}) collective-permute-start(f32[8,1536]{1,0:T(8,128)S(1)} %shard_map.95.refs_2_), channel_id=1, source_target_pairs={{0,2},{1,3},{2,0},{3,1},{4,6},{5,7},{6,4},{7,5},{8,10},{9,11},{10,... | collective-permute-start | bytes 147464 | tf_op jit(solution)/shard_map/ppermute | solution.py:610
  164.1 6.5 %collective-permute-start.37 = (f32[8,1536]{1,0:T(8,128)S(1)}, f32[8,1536]{1,0:T(8,128)S(1)}, u32[]{:S(2)}, u32[]{:S(2)}) collective-permute-start(f32[8,1536]{1,0:T(8,128)S(1)} %shard_map.95.refs_2_), channel_id=1, source_target_pairs={{0,3},{1,2},{2,1},{3,0},{4,7},{5,6},{6,5},{7,4},{8,11},{9,10},{10,... | collective-permute-start | bytes 147464 | tf_op jit(solution)/shard_map/ppermute | solution.py:610
  174.9 19.0 %collective-permute-start.38 = (bf16[720,512]{1,0:T(8,128)(2,1)S(1)}, bf16[720,512]{1,0:T(8,128)(2,1)S(1)}, u32[]{:S(2)}, u32[]{:S(2)}) collective-permute-start(bf16[720,512]{1,0:T(8,128)(2,1)S(1)} %get-tuple-element.174), channel_id=1, source_target_pairs={{0,8},{4,12},{8,0},{12,4},{16,24},{20,28},{24,16},{28,20},{1,9},{5... | collective-permute-start | bytes 2211848 | tf_op jit(solution)/shard_map/ppermute | solution.py:535
  176.3 17.5 %collective-permute-start.39 = (bf16[720,512]{1,0:T(8,128)(2,1)S(1)}, bf16[720,512]{1,0:T(8,128)(2,1)S(1)}, u32[]{:S(2)}, u32[]{:S(2)}) collective-permute-start(bf16[720,512]{1,0:T(8,128)(2,1)S(1)} %get-tuple-element.175), channel_id=1, source_target_pairs={{0,16},{4,20},{8,24},{12,28},{16,0},{20,4},{24,8},{28,12},{1,17},{... | collective-permute-start | bytes 2211848 | tf_op jit(solution)/shard_map/ppermute | solution.py:535
  177.2 16.7 %collective-permute-start.40 = (bf16[64,720]{1,0:T(8,128)(2,1)S(1)}, bf16[64,720]{1,0:T(8,128)(2,1)S(1)}, u32[]{:S(2)}, u32[]{:S(2)}) collective-permute-start(bf16[64,720]{1,0:T(8,128)(2,1)S(1)} %get-tuple-element.183.mine_ref), channel_id=1, source_target_pairs={{0,8},{4,12},{8,0},{12,4},{16,24},{20,28},{24,16},{28,20},{1,9},{5... | collective-permute-start | bytes 276488 | tf_op jit(solution)/shard_map/ppermute | solution.py:535
  195.3 21.5 %collective-permute-start.42 = (bf16[720,512]{1,0:T(8,128)(2,1)S(1)}, bf16[720,512]{1,0:T(8,128)(2,1)S(1)}, u32[]{:S(2)}, u32[]{:S(2)}) collective-permute-start(bf16[720,512]{1,0:T(8,128)(2,1)S(1)} %get-tuple-element.200), channel_id=1, source_target_pairs={{0,16},{4,12},{8,24},{12,4},{16,0},{20,28},{24,8},{28,20},{1,17},{... | collective-permute-start | bytes 2211848 | tf_op jit(solution)/shard_map/ppermute | solution.py:539
  196.5 20.4 %collective-permute-start.43 = (bf16[720,512]{1,0:T(8,128)(2,1)S(1)}, bf16[720,512]{1,0:T(8,128)(2,1)S(1)}, u32[]{:S(2)}, u32[]{:S(2)}) collective-permute-start(bf16[720,512]{1,0:T(8,128)(2,1)S(1)} %get-tuple-element.189), channel_id=1, source_target_pairs={{0,8},{4,20},{8,0},{12,28},{16,24},{20,4},{24,16},{28,12},{1,9},{5... | collective-permute-start | bytes 2211848 | tf_op jit(solution)/shard_map/ppermute | solution.py:539
  198.1 18.8 %collective-permute-start.41 = (bf16[64,720]{1,0:T(8,128)(2,1)S(1)}, bf16[64,720]{1,0:T(8,128)(2,1)S(1)}, u32[]{:S(2)}, u32[]{:S(2)}) collective-permute-start(bf16[64,720]{1,0:T(8,128)(2,1)S(1)} %shard_map.98), channel_id=1, source_target_pairs={{0,16},{4,20},{8,24},{12,28},{16,0},{20,4},{24,8},{28,12},{1,17},{... | collective-permute-start | bytes 276488 | tf_op jit(solution)/shard_map/ppermute | solution.py:535
  199.3 25.4 %collective-permute-start.47 = (bf16[720,512]{1,0:T(8,128)(2,1)}, bf16[720,512]{1,0:T(8,128)(2,1)}, u32[]{:S(2)}, u32[]{:S(2)}) collective-permute-start(bf16[720,512]{1,0:T(8,128)(2,1)} %get-tuple-element.199), channel_id=1, source_target_pairs={{0,12},{4,16},{8,4},{12,24},{16,28},{20,0},{24,20},{28,8},{1,13},{... | collective-permute-start | bytes 2211848 | tf_op jit(solution)/shard_map/ppermute | solution.py:539
  199.3 25.4 %collective-permute-start.44 = (bf16[720,512]{1,0:T(8,128)(2,1)}, bf16[720,512]{1,0:T(8,128)(2,1)}, u32[]{:S(2)}, u32[]{:S(2)}) collective-permute-start(bf16[720,512]{1,0:T(8,128)(2,1)} %get-tuple-element.192), channel_id=1, source_target_pairs={{0,4},{4,0},{8,12},{12,8},{16,20},{20,16},{24,28},{28,24},{1,5},{5... | collective-permute-start | bytes 2211848 | tf_op jit(solution)/shard_map/ppermute | solution.py:535
  216.8 11.8 %collective-permute-start.45 = (bf16[720,512]{1,0:T(8,128)(2,1)}, bf16[720,512]{1,0:T(8,128)(2,1)}, u32[]{:S(2)}, u32[]{:S(2)}) collective-permute-start(bf16[720,512]{1,0:T(8,128)(2,1)} %get-tuple-element.193), channel_id=1, source_target_pairs={{0,20},{4,8},{8,28},{12,0},{16,4},{20,24},{24,12},{28,16},{1,21},{... | collective-permute-start | bytes 2211848 | tf_op jit(solution)/shard_map/ppermute | solution.py:539
  216.9 4.4 %collective-permute-start.46 = (f32[64,720]{1,0:T(8,128)S(1)}, f32[64,720]{1,0:T(8,128)S(1)}, u32[]{:S(2)}, u32[]{:S(2)}) collective-permute-start(f32[64,720]{1,0:T(8,128)S(1)} %convert_add_fusion), channel_id=1, source_target_pairs={{0,4},{4,0},{8,12},{12,8},{16,20},{20,16},{24,28},{28,24},{1,5},{5... | collective-permute-start | bytes 552968 | tf_op jit(solution)/shard_map/ppermute | solution.py:535

commit v12 on v11

--- a/solution.py
+++ b/solution.py
@@ -484,23 +484,32 @@
     )(meta, *operands)
 
 
-def own_half_body(tile, meta, keep_ref, c_ref, a_ref, out_ref):
+def half_body(tile, meta, *refs):
     rows = pl.ds(pl.multiple_of(pl.program_id(0) * tile, tile), tile)
-    out_ref[...] = keep_ref[rows, :] + c_ref[rows, :].astype(F32) + a_ref[rows, :].astype(F32)
-
-
-def own_half(meta, keep, got_c, got_a):
-    count, width = keep.shape
+    first, second, third = [ref[rows, :].astype(F32) for ref in refs[:3]]
+    refs[-1][...] = first + second + third
+
+
+def half_sums(meta, terms, sums=None):
+    count, width = terms[0].shape
     parts = 3
     tile = count // parts
+    own = sums is None
+
+    def place(j, m):
+        core = lax.rem(m[0], 2)
+        return (core if own else 1 - core) * parts + j, 0
+
     return call(
-        functools.partial(own_half_body, tile),
+        functools.partial(half_body, tile),
         (parts,),
-        [pl.BlockSpec(memory_space=pltpu.VMEM)] * 3,
-        pl.BlockSpec((tile, width), lambda j, m: (lax.rem(m[0], 2) * parts + j, 0)),
+        [pl.BlockSpec(memory_space=pltpu.VMEM)] * 3
+        + ([] if own else [pl.BlockSpec(memory_space=pl.ANY)]),
+        pl.BlockSpec((tile, width), place),
         sds((2 * count, width), F32),
+        alias=None if own else {4: 0},
         room=8,
-    )(meta, keep, got_c, got_a)
+    )(meta, *terms, *([] if own else [sums]))
 
 
 def two_by_two(raw_images, defocus_bin, dest_row, ctf_table, inv_noise, panels):
@@ -567,8 +576,8 @@
     a1, recv_b = onward(share_a), exchange(send_b)
     a1, recv_b[:2] = together((a1, recv_b[:2]))
     a2 = onward(a1)
+    a2, recv_b, near = together((a2, recv_b, near))
     share_b = unpack_next(meta, pick, wide, recv_b, ctf_table, inv, width, chunk_b)
-    a2, share_b, near = together((a2, share_b, near))
     by_x, by_y = across(near, 2), across(near, 4)
     a3, b1 = onward(a2), onward(share_b)
     sib0, hots = [across(share_a, 1), across(share_b, 1)], [hot, across(hot, 1)]
@@ -633,10 +642,9 @@
         jnp.concatenate([mass, mass_other], axis=1),
         jnp.concatenate([mass_other, mass], axis=1),
     )
-    sums = own_half(meta, keep, got_c, got_a)
+    sums = half_sums(meta, [keep, got_c, got_a])
     bin_weights, got_b = together((bin_weights, got_b))
-    other_half = got_self.astype(F32) + got_d.astype(F32) + got_b.astype(F32)
-    class_sums = lax.dynamic_update_slice_in_dim(sums, other_half, (1 - core) * count, 0).T
+    class_sums = half_sums(meta, [got_self, got_d, got_b], sums).T
     return class_sums, bin_weights, log_evidence.reshape(-1)
 
 

time: 233 us -> 234 us (level)
  waiting for transfers between devices: 113 us -> 117 us
  Pallas kernels: 69.6 us -> 73.4 us
  starting transfers between devices: 39.4 us -> 36.1 us
  other arithmetic: 6.82 us -> 3.88 us
    ppermute x6, waiting for transfers between devices: 34.6 us -> 47.2 us  [onward(): lax.ppermute(value, 'rot', [(i, (i + 1) % turns) for i in range(turns)])]
    ppermute x35, waiting for transfers between devices: 69.1 us -> 59.6 us  [across(): return lax.ppermute(value, 'dom', [(i, i ^ apart) for i in range(dom)])]
    pallas_call x1 -> x2, Pallas kernels: 2.25 us -> 6.1 us  [half_sums(): call(functools.partial(half_body, tile), (parts,), [pl.BlockSpec(memory_s...]
    dynamic_update_slice x1 -> x0, other arithmetic: 2.93 us -> none  [two_by_two(): lax.dynamic_update_slice_in_dim(sums, other_half, (1 - core) * count, 0)]
  transfers between devices with their start and end apart: 48 -> 48, of which waited for: 26 -> 26; matrix products, arithmetic and copies ran while one was open for 2% -> 2% of each run, Pallas kernels for 24% -> 23%
where the time goes in v12:
time: 234 us; the launch traced here: 232 us
  waiting for transfers between devices  117 us (50%)
  Pallas kernels  73.4 us (31%)
  starting transfers between devices  36.1 us (15%)
  other arithmetic  3.88 us (2%)
    ppermute x35, waiting for transfers between devices, across(): return lax.ppermute(value, 'dom', [(i, i ^ apart) for i in range(dom)])  59.6 us
    ppermute x6, waiting for transfers between devices, onward(): lax.ppermute(value, 'rot', [(i, (i + 1) % turns) for i in range(turns)])  47.2 us
    ppermute x35, starting transfers between devices, across(): return lax.ppermute(value, 'dom', [(i, i ^ apart) for i in range(dom)])  26.6 us
    pallas_call x5, Pallas kernels, score(): call(functools.partial(score_body, parts, used, first, last), (2 * half,)...  26.3 us
    pallas_call x2, Pallas kernels, class_part(): call(functools.partial(class_body, kind, steps), (steps,), in_specs, out_...  15 us
    pallas_call x1, Pallas kernels, energy(): call(functools.partial(energy_body, bins, count), (count,), [pl.BlockSpec...  6.78 us
    ppermute x4, waiting for transfers between devices, by_core(): return lax.ppermute(value, 'dom', pairs)  6.69 us
    pallas_call x2, Pallas kernels, half_sums(): call(functools.partial(half_body, tile), (parts,), [pl.BlockSpec(memory_s...  6.1 us
  transfers between devices with their start and end apart: 48, of which 26 were waited for; matrix products, arithmetic and copies ran while one was open for 2% of the time, Pallas kernels for 23%

profile of v12, /device:TPU:0, one launch (start us, length us, event | category | flops | bytes accessed | tf_op | source)
XLA Modules:
  0.0 232.5 jit_solution(7864155150943733240)
XLA Ops:
  1.2 0.7 add_select_fusion.slot_ref
  2.0 5.8 %shard_map.85 = (bf16[208,384]{1,0:T(8,128)(2,1)S(1)}, bf16[208,384]{1,0:T(8,128)(2,1)S(1)}, bf16[208,384]{1,0:T(8,128)(2,1)S(1)}, bf16[208,384]{1,0:T(8,128)(2,...) custom-call(s32[10]{0:T(128)S(1)} %stack.43.meta, ...), custom_call_target="tpu_custom_call" | custom-call | flops 113246208 | bytes 147456 | tf_op jit(solution)/shard_map/pallas_call | solution.py:132
  7.7 3.6 %collective-permute-start = (bf16[208,384]{1,0:T(8,128)(2,1)S(1)}, bf16[208,384]{1,0:T(8,128)(2,1)S(1)}, u32[]{:S(2)}, u32[]{:S(2)}) collective-permute-start(bf16[208,384]{1,0:T(8,128)(2,1)S(1)} %get-tuple-element.108), channel_id=1, source_target_pairs={{0,24},{4,28},{8,16},{12,20},{16,8},{20,12},{24,0},{28,4},{1,25},{... | collective-permute-start | bytes 479240 | tf_op jit(solution)/shard_map/ppermute | solution.py:544
  11.4 1.6 collective-permute-start.2
  13.1 1.5 collective-permute-start.3
  14.7 1.2 constant_dynamic-slice_fusion
  16.4 0.6 collective-permute-start.5
  17.0 2.3 %collective-permute-done.1.refs_1_ = bf16[208,384]{1,0:T(8,128)(2,1)S(1)} collective-permute-done((bf16[208,384]{1,0:T(8,128)(2,1)S(1)}, bf16[208,384]{1,0:T(8,128)(2,1)S(1)}, u32[]{:S(2)}, u32[]{:S(2)}) %collective-permute-start.1) | collective-permute-done | bytes 159776 | tf_op jit(solution)/shard_map/ppermute | solution.py:544
  19.6 5.9 %shard_map.86 = (bf16[192,640]{1,0:T(8,128)(2,1)S(1)}, bf16[192,640]{1,0:T(8,128)(2,1)S(1)}, bf16[192,640]{1,0:T(8,128)(2,1)S(1)}, bf16[192,640]{1,0:T(8,128)(2,...) custom-call(s32[10]{0:T(128)S(1)} %stack.43.meta, ...), custom_call_target="tpu_custom_call" | custom-call | flops 188743680 | bytes 245760 | tf_op jit(solution)/shard_map/pallas_call | solution.py:152
  26.5 3.5 %shard_map.87 = (bf16[768,384]{1,0:T(8,128)(2,1)S(1)}, bf16[192,768]{1,0:T(8,128)(2,1)S(1)}, bf16[768,1536]{1,0:T(8,128)(2,1)S(1)}, bf16[768,192]{1,0:T(8,128)(2,1)S(1)}) custom-call(s32[10]{0:T(128)S(1)} %stack.43.meta, bf16[208,384]{1,0:T(8,128)(2,1)S(1)} %collective-permute-done.refs_0_, bf16[208,384]{1,0:T(8,128)(2,1)S(1)} %collective-permute-done.1.refs_1_, ...), custom_call_target="tpu_custom_call" | custom-call | flops 56623104 | bytes 73728 | tf_op jit(solution)/shard_map/pallas_call | solution.py:212
  30.0 2.0 collective-permute-start.8
  32.0 1.8 collective-permute-start.10
  33.8 0.7 collective-permute-start.9
  34.5 6.6 %collective-permute-done.10.refs_1_ = bf16[192,640]{1,0:T(8,128)(2,1)S(1)} collective-permute-done((bf16[192,640]{1,0:T(8,128)(2,1)S(1)}, bf16[192,640]{1,0:T(8,128)(2,1)S(1)}, u32[]{:S(2)}, u32[]{:S(2)}) %collective-permute-start.10) | collective-permute-done | bytes 245792 | tf_op jit(solution)/shard_map/ppermute | solution.py:544
  41.1 5.4 %collective-permute-done.9.refs_0_ = bf16[192,640]{1,0:T(8,128)(2,1)S(1)} collective-permute-done((bf16[192,640]{1,0:T(8,128)(2,1)S(1)}, bf16[192,640]{1,0:T(8,128)(2,1)S(1)}, u32[]{:S(2)}, u32[]{:S(2)}) %collective-permute-start.9) | collective-permute-done | bytes 245792 | tf_op jit(solution)/shard_map/ppermute | solution.py:544
  46.5 1.1 collective-permute-done.8.refs_0_
  48.0 1.3 collective-permute-start.12
  49.4 1.5 collective-permute-start.13
  50.9 0.9 collective-permute-start.15
  51.8 5.1 %collective-permute-done.12.refs_2_ = bf16[192,640]{1,0:T(8,128)(2,1)S(1)} collective-permute-done((bf16[192,640]{1,0:T(8,128)(2,1)S(1)}, bf16[192,640]{1,0:T(8,128)(2,1)S(1)}, u32[]{:S(2)}, u32[]{:S(2)}) %collective-permute-start.12) | collective-permute-done | bytes 245792 | tf_op jit(solution)/shard_map/ppermute | solution.py:544
  56.9 1.3 collective-permute-done.13.refs_3_
  58.3 1.6 collective-permute-done.14.refs_4_
  59.9 1.2 collective-permute-done.15.refs_5_
  61.1 3.0 %collective-permute-done.11.refs_0_ = bf16[768,384]{1,0:T(8,128)(2,1)S(1)} collective-permute-done((bf16[768,384]{1,0:T(8,128)(2,1)S(1)}, bf16[768,384]{1,0:T(8,128)(2,1)S(1)}, u32[]{:S(2)}, u32[]{:S(2)}) %collective-permute-start.11) | collective-permute-done | bytes 589856 | tf_op jit(solution)/shard_map/ppermute | solution.py:551
  64.1 1.3 collective-permute-start.20
  65.3 1.5 collective-permute-start.21
  66.8 2.9 %shard_map.88.refs_1_ = bf16[768,640]{1,0:T(8,128)(2,1)S(1)} custom-call(s32[10]{0:T(128)S(1)} %stack.43.meta, bf16[192,640]{1,0:T(8,128)(2,1)S(1)} %collective-permute-done.9.refs_0_, bf16[192,640]{1,0:T(8,128)(2,1)S(1)} %collective-permute-done.10.refs_1_, bf16[192,640]{1,0:T(8,128)(2,1)S(1)} %collective-permute-done.12.refs_2_, ...), custom_call_target="tpu_custom_call" | custom-call | flops 94371840 | bytes 122880 | tf_op jit(solution)/shard_map/pallas_call | solution.py:231
  69.8 0.9 collective-permute-start.17
  70.8 25.5 %collective-permute-done.18.refs_1_ = bf16[768,640]{1,0:T(8,128)(2,1)S(1)} collective-permute-done((bf16[768,640]{1,0:T(8,128)(2,1)S(1)}, bf16[768,640]{1,0:T(8,128)(2,1)S(1)}, u32[]{:S(2)}, u32[]{:S(2)}) %collective-permute-start.18) | collective-permute-done | bytes 983072 | tf_op jit(solution)/shard_map/ppermute | solution.py:551
  96.9 1.1 collective-permute-start.22
  98.0 1.6 collective-permute-start.23
  99.9 9.1 %collective-permute-done.17.refs_0_ = bf16[768,384]{1,0:T(8,128)(2,1)S(1)} collective-permute-done((bf16[768,384]{1,0:T(8,128)(2,1)S(1)}, bf16[768,384]{1,0:T(8,128)(2,1)S(1)}, u32[]{:S(2)}, u32[]{:S(2)}) %collective-permute-start.17) | collective-permute-done | bytes 589856 | tf_op jit(solution)/shard_map/ppermute | solution.py:551
  109.0 4.4 %collective-permute-done.22.refs_3_ = bf16[720,512]{1,0:T(8,128)(2,1)S(1)} collective-permute-done((bf16[720,512]{1,0:T(8,128)(2,1)S(1)}, bf16[720,512]{1,0:T(8,128)(2,1)S(1)}, u32[]{:S(2)}, u32[]{:S(2)}) %collective-permute-start.22) | collective-permute-done | bytes 737312 | tf_op jit(solution)/shard_map/ppermute | solution.py:544
  113.4 3.6 %collective-permute-done.23.refs_4_ = bf16[720,512]{1,0:T(8,128)(2,1)S(1)} collective-permute-done((bf16[720,512]{1,0:T(8,128)(2,1)S(1)}, bf16[720,512]{1,0:T(8,128)(2,1)S(1)}, u32[]{:S(2)}, u32[]{:S(2)}) %collective-permute-start.23) | collective-permute-done | bytes 737312 | tf_op jit(solution)/shard_map/ppermute | solution.py:544
  117.0 6.8 %shard_map.89 = (bf16[720,4096]{1,0:T(8,128)(2,1)S(1)}, bf16[720,192]{1,0:T(8,128)(2,1)S(1)}) custom-call(s32[10]{0:T(128)S(1)} %stack.43.meta, bf16[720,1024]{1,0:T(8,128)(2,1)S(1)} %pad_maximum_fusion.refs_0_, bf16[720,1024]{1,0:T(8,128)(2,1)S(1)} %collective-permute-done.20.refs_1_, bf16[720,1024]{1,0:T(8,128)(2,1)S(1)} %collective-permute-done.21.refs_2_, ...), custom_call_target="tpu_custom_call" | custom-call | flops 283115520 | bytes 737280 | tf_op jit(solution)/shard_map/pallas_call | solution.py:283
  123.8 3.0 %collective-permute-done.19.refs_1_ = bf16[768,640]{1,0:T(8,128)(2,1)S(1)} collective-permute-done((bf16[768,640]{1,0:T(8,128)(2,1)S(1)}, bf16[768,640]{1,0:T(8,128)(2,1)S(1)}, u32[]{:S(2)}, u32[]{:S(2)}) %collective-permute-start.19) | collective-permute-done | bytes 983072 | tf_op jit(solution)/shard_map/ppermute | solution.py:551
  127.4 5.1 %shard_map.90 = (f32[720,1536]{1,0:T(8,128)S(1)}, bf16[1536,4096]{1,0:T(8,128)(2,1)S(1)}) custom-call(s32[10]{0:T(128)S(1)} %stack.43.meta, bf16[768,384]{1,0:T(8,128)(2,1)S(1)} %get-tuple-element.144.refs_0_, bf16[768,640]{1,0:T(8,128)(2,1)S(1)} %shard_map.88.refs_1_, bf16[768,384]{1,0:T(8,128)(2,1)S(1)} %collective-permute-done.31.refs_2_, ...), custom_call_target="tpu_custom_call" | custom-call | flops 141557760 | bytes 946176 | tf_op jit(solution)/shard_map/pallas_call | solution.py:387
  132.5 5.4 %shard_map.91 = (f32[720,1536]{1,0:T(8,128)S(1)}, bf16[1536,4096]{1,0:T(8,128)(2,1)S(1)}) custom-call(s32[10]{0:T(128)S(1)} %stack.43.meta, bf16[768,384]{1,0:T(8,128)(2,1)S(1)} %collective-permute-done.8.refs_0_, bf16[768,640]{1,0:T(8,128)(2,1)S(1)} %collective-permute-done.18.refs_1_, ...), custom_call_target="tpu_custom_call", output_to_operand_aliasing={{0}: (6, {}), {1}: (7, {})} | custom-call | flops 141557760 | bytes 946176 | tf_op jit(solution)/shard_map/pallas_call | solution.py:387
  138.0 5.4 %shard_map.92 = (f32[720,1536]{1,0:T(8,128)S(1)}, bf16[1536,4096]{1,0:T(8,128)(2,1)S(1)}) custom-call(s32[10]{0:T(128)S(1)} %stack.43.meta, bf16[768,384]{1,0:T(8,128)(2,1)S(1)} %collective-permute-done.11.refs_0_, bf16[768,640]{1,0:T(8,128)(2,1)S(1)} %collective-permute-done.19.refs_1_, ...), custom_call_target="tpu_custom_call", output_to_operand_aliasing={{0}: (6, {}), {1}: (7, {})} | custom-call | flops 141557760 | bytes 946176 | tf_op jit(solution)/shard_map/pallas_call | solution.py:387
  143.5 3.7 %shard_map.93.refs_5_ = f32[720,1536]{1,0:T(8,128)S(1)} custom-call(s32[10]{0:T(128)S(1)} %stack.43.meta, bf16[768,384]{1,0:T(8,128)(2,1)S(1)} %collective-permute-done.17.refs_0_, bf16[768,384]{1,0:T(8,128)(2,1)S(1)} %collective-permute-done.26.refs_1_.refs_2_, ...), custom_call_target="tpu_custom_call", output_to_operand_aliasing={{}: (4, {})} | custom-call | flops 141557760 | bytes 946176 | tf_op jit(solution)/shard_map/pallas_call | solution.py:387
  147.2 5.5 %collective-permute-done.25.refs_1_ = bf16[768,640]{1,0:T(8,128)(2,1)S(1)} collective-permute-done((bf16[768,640]{1,0:T(8,128)(2,1)S(1)}, bf16[768,640]{1,0:T(8,128)(2,1)S(1)}, u32[]{:S(2)}, u32[]{:S(2)}) %collective-permute-start.25) | collective-permute-done | bytes 983072 | tf_op jit(solution)/shard_map/ppermute | solution.py:551
  152.7 2.6 %collective-permute-done.33.refs_3_ = bf16[768,640]{1,0:T(8,128)(2,1)S(1)} collective-permute-done((bf16[768,640]{1,0:T(8,128)(2,1)S(1)}, bf16[768,640]{1,0:T(8,128)(2,1)S(1)}, u32[]{:S(2)}, u32[]{:S(2)}) %collective-permute-start.33) | collective-permute-done | bytes 983072 | tf_op jit(solution)/shard_map/ppermute | solution.py:544
  155.3 6.6 %shard_map.94 = (f32[720,1536]{1,0:T(8,128)S(1)}, f32[8,1536]{1,0:T(8,128)S(1)}, bf16[1536,4096]{1,0:T(8,128)(2,1)S(1)}) custom-call(s32[10]{0:T(128)S(1)} %stack.43.meta, bf16[768,384]{1,0:T(8,128)(2,1)S(1)} %collective-permute-done.17.refs_0_, bf16[768,640]{1,0:T(8,128)(2,1)S(1)} %collective-permute-done.25.refs_1_, ...), custom_call_target="tpu_custom_call", output_to_operand_aliasing={{0}: (6, {}), {2}: (7, {})} | custom-call | flops 141557760 | bytes 946176 | tf_op jit(solution)/shard_map/pallas_call | solution.py:387
  162.1 1.1 collective-permute-done.34.other_ref
  163.2 0.6 shard_map.95.refs_2_
  164.0 4.3 %collective-permute-start.37 = (f32[8,1536]{1,0:T(8,128)S(1)}, f32[8,1536]{1,0:T(8,128)S(1)}, u32[]{:S(2)}, u32[]{:S(2)}) collective-permute-start(f32[8,1536]{1,0:T(8,128)S(1)} %shard_map.95.refs_2_), channel_id=1, source_target_pairs={{0,3},{1,2},{2,1},{3,0},{4,7},{5,6},{6,5},{7,4},{8,11},{9,10},{10,... | collective-permute-start | bytes 147464 | tf_op jit(solution)/shard_map/ppermute | solution.py:619
  168.6 2.7 %collective-permute-done.36.refs_4_ = f32[8,1536]{1,0:T(8,128)S(1)} collective-permute-done((f32[8,1536]{1,0:T(8,128)S(1)}, f32[8,1536]{1,0:T(8,128)S(1)}, u32[]{:S(2)}, u32[]{:S(2)}) %collective-permute-start.36) | collective-permute-done | bytes 49184 | tf_op jit(solution)/shard_map/ppermute | solution.py:619
  171.3 4.2 %shard_map.96 = (bf16[720,512]{1,0:T(8,128)(2,1)S(1)}, bf16[720,512]{1,0:T(8,128)(2,1)S(1)}, bf16[720,1536]{1,0:T(8,128)(2,1)S(1)}, f32[1,768]{1,0:T(1,128)S(1)}, bf16[64,720]{1,0:T(8,128)(2,1)S(1)}) custom-call(s32[10]{0:T(128)S(1)} %stack.43.meta, f32[720,1536]{1,0:T(8,128)S(1)} %get-tuple-element.185.refs_0_, ...), custom_call_target="tpu_custom_call" | custom-call | flops 141557760 | bytes 657408 | tf_op jit(solution)/shard_map/pallas_call | solution.py:475
  176.1 1.0 collective-permute-start.39
  177.1 1.0 collective-permute-start.40
  178.1 10.7 %shard_map.97 = (bf16[720,512]{1,0:T(8,128)(2,1)S(1)}, bf16[720,512]{1,0:T(8,128)(2,1)}, bf16[720,512]{1,0:T(8,128)(2,1)}, f32[720,512]{1,0:T(8,128)S(1)}, f32[7...) custom-call(s32[10]{0:T(128)S(1)} %stack.43.meta, bf16[720,1536]{1,0:T(8,128)(2,1)S(1)} %get-tuple-element.190.refs_0_, ...), custom_call_target="tpu_custom_call" | custom-call | flops 424673280 | bytes 1419264 | tf_op jit(solution)/shard_map/pallas_call | solution.py:475
  188.9 5.6 %collective-permute-done.40.other_ref = bf16[64,720]{1,0:T(8,128)(2,1)S(1)} collective-permute-done((bf16[64,720]{1,0:T(8,128)(2,1)S(1)}, bf16[64,720]{1,0:T(8,128)(2,1)S(1)}, u32[]{:S(2)}, u32[]{:S(2)}) %collective-permute-start.40) | collective-permute-done | bytes 92192 | tf_op jit(solution)/shard_map/ppermute | solution.py:544
  194.5 1.4 fusion.3
  196.4 1.0 collective-permute-start.45
  198.0 1.1 collective-permute-start.43
  199.1 1.1 collective-permute-start.41
  200.2 17.2 %collective-permute-done.43 = bf16[64,720]{1,0:T(8,128)(2,1)S(1)} collective-permute-done((bf16[64,720]{1,0:T(8,128)(2,1)S(1)}, bf16[64,720]{1,0:T(8,128)(2,1)S(1)}, u32[]{:S(2)}, u32[]{:S(2)}) %collective-permute-start.43) | collective-permute-done | bytes 92192 | tf_op jit(solution)/shard_map/ppermute | solution.py:544
  217.5 0.7 collective-permute-start.46
  218.1 0.6 reduce
  218.8 2.3 shard_map.99.refs_3_
  221.0 0.9 maximum_select_fusion
  221.9 2.3 %collective-permute-done.47.refs_2_ = bf16[720,512]{1,0:T(8,128)(2,1)} collective-permute-done((bf16[720,512]{1,0:T(8,128)(2,1)}, bf16[720,512]{1,0:T(8,128)(2,1)}, u32[]{:S(2)}, u32[]{:S(2)}) %collective-permute-start.47) | collective-permute-done | bytes 737312 | tf_op jit(solution)/shard_map/ppermute | solution.py:548
  224.3 4.3 %collective-permute-done.42.refs_1_ = bf16[720,512]{1,0:T(8,128)(2,1)} collective-permute-done((bf16[720,512]{1,0:T(8,128)(2,1)}, bf16[720,512]{1,0:T(8,128)(2,1)}, u32[]{:S(2)}, u32[]{:S(2)}) %collective-permute-start.42) | collective-permute-done | bytes 737312 | tf_op jit(solution)/shard_map/ppermute | solution.py:548
  228.6 3.9 %shard_map.100 = f32[1440,512]{1,0:T(8,128)} custom-call(s32[10]{0:T(128)S(1)} %stack.43.meta, bf16[720,512]{1,0:T(8,128)(2,1)} %collective-permute-done.41.refs_0_, bf16[720,512]{1,0:T(8,128)(2,1)} %collective-permute-done.42.refs_1_, bf16[720,512]{1,0:T(8,128)(2,1)} %collective-permute-done.47.refs_2_, ...), custom_call_target="tpu_custom_call", output_to_operand_aliasing={{}: (4, {})} | custom-call | tf_op jit(solution)/shard_map/pallas_call | solution.py:503
  (65 shorter events, 7.1 us)
Async XLA Ops:
  0.6 14.0 %collective-permute-start.7 = (bf16[1440,512]{1,0:T(8,128)(2,1)}, bf16[1440,512]{1,0:T(8,128)(2,1)}, u32[]{:S(2)}, u32[]{:S(2)}) collective-permute-start(bf16[1440,512]{1,0:T(8,128)(2,1)} %param.11), channel_id=1, source_target_pairs={{0,4},{4,0},{8,12},{12,8},{16,20},{20,16},{24,28},{28,24},{1,5},{5... | collective-permute-start | bytes 4423688 | tf_op jit(solution)/shard_map/ppermute | solution.py:544
  2.0 12.6 %copy-start.2 = (bf16[1440,512]{1,0:T(8,128)(2,1)S(1)}, bf16[1440,512]{1,0:T(8,128)(2,1)}, u32[]{:S(2)}) copy-start(bf16[1440,512]{1,0:T(8,128)(2,1)} %param.11) | copy-start | bytes 4423684
  7.7 8.6 %collective-permute-start = (bf16[208,384]{1,0:T(8,128)(2,1)S(1)}, bf16[208,384]{1,0:T(8,128)(2,1)S(1)}, u32[]{:S(2)}, u32[]{:S(2)}) collective-permute-start(bf16[208,384]{1,0:T(8,128)(2,1)S(1)} %get-tuple-element.108), channel_id=1, source_target_pairs={{0,24},{4,28},{8,16},{12,20},{16,8},{20,12},{24,0},{28,4},{1,25},{... | collective-permute-start | bytes 479240 | tf_op jit(solution)/shard_map/ppermute | solution.py:544
  11.3 8.0 %collective-permute-start.1 = (bf16[208,384]{1,0:T(8,128)(2,1)S(1)}, bf16[208,384]{1,0:T(8,128)(2,1)S(1)}, u32[]{:S(2)}, u32[]{:S(2)}) collective-permute-start(bf16[208,384]{1,0:T(8,128)(2,1)S(1)} %get-tuple-element.109), channel_id=1, source_target_pairs={{0,28},{4,24},{8,20},{12,16},{16,12},{20,8},{24,4},{28,0},{1,29},{... | collective-permute-start | bytes 479240 | tf_op jit(solution)/shard_map/ppermute | solution.py:544
  11.4 14.2 %collective-permute-start.2 = (bf16[208,384]{1,0:T(8,128)(2,1)S(1)}, bf16[208,384]{1,0:T(8,128)(2,1)S(1)}, u32[]{:S(2)}, u32[]{:S(2)}) collective-permute-start(bf16[208,384]{1,0:T(8,128)(2,1)S(1)} %get-tuple-element.110), channel_id=1, source_target_pairs={{0,16},{4,20},{8,24},{12,28},{16,0},{20,4},{24,8},{28,12},{1,17},{... | collective-permute-start | bytes 479240 | tf_op jit(solution)/shard_map/ppermute | solution.py:544
  13.1 12.6 %collective-permute-start.3 = (bf16[208,384]{1,0:T(8,128)(2,1)S(1)}, bf16[208,384]{1,0:T(8,128)(2,1)S(1)}, u32[]{:S(2)}, u32[]{:S(2)}) collective-permute-start(bf16[208,384]{1,0:T(8,128)(2,1)S(1)} %get-tuple-element.111), channel_id=1, source_target_pairs={{0,8},{4,12},{8,0},{12,4},{16,24},{20,28},{24,16},{28,20},{1,9},{5... | collective-permute-start | bytes 479240 | tf_op jit(solution)/shard_map/ppermute | solution.py:544
  14.6 11.6 %collective-permute-start.4 = (bf16[208,384]{1,0:T(8,128)(2,1)S(1)}, bf16[208,384]{1,0:T(8,128)(2,1)S(1)}, u32[]{:S(2)}, u32[]{:S(2)}) collective-permute-start(bf16[208,384]{1,0:T(8,128)(2,1)S(1)} %get-tuple-element.112), channel_id=1, source_target_pairs={{0,20},{4,16},{8,28},{12,24},{16,4},{20,0},{24,12},{28,8},{1,21},{... | collective-permute-start | bytes 479240 | tf_op jit(solution)/shard_map/ppermute | solution.py:544
  16.4 9.9 %collective-permute-start.5 = (bf16[208,384]{1,0:T(8,128)(2,1)S(1)}, bf16[208,384]{1,0:T(8,128)(2,1)S(1)}, u32[]{:S(2)}, u32[]{:S(2)}) collective-permute-start(bf16[208,384]{1,0:T(8,128)(2,1)S(1)} %get-tuple-element.113), channel_id=1, source_target_pairs={{0,12},{4,8},{8,4},{12,0},{16,28},{20,24},{24,20},{28,16},{1,13},{... | collective-permute-start | bytes 479240 | tf_op jit(solution)/shard_map/ppermute | solution.py:544
  19.3 6.9 %collective-permute-start.6 = (bf16[208,384]{1,0:T(8,128)(2,1)S(1)}, bf16[208,384]{1,0:T(8,128)(2,1)S(1)}, u32[]{:S(2)}, u32[]{:S(2)}) collective-permute-start(bf16[208,384]{1,0:T(8,128)(2,1)S(1)} %get-tuple-element.114), channel_id=1, source_target_pairs={{0,4},{4,0},{8,12},{12,8},{16,20},{20,16},{24,28},{28,24},{1,5},{5... | collective-permute-start | bytes 479240 | tf_op jit(solution)/shard_map/ppermute | solution.py:544
  25.5 1.0 copy-start
  25.5 1.0 copy-start.1
  30.0 17.6 %collective-permute-start.8 = (bf16[768,384]{1,0:T(8,128)(2,1)S(1)}, bf16[768,384]{1,0:T(8,128)(2,1)S(1)}, u32[]{:S(2)}, u32[]{:S(2)}) collective-permute-start(bf16[768,384]{1,0:T(8,128)(2,1)S(1)} %get-tuple-element.144.refs_0_), channel_id=1, source_target_pairs={{0,1},{1,2},{2,3},{3,0},{4,5},{5,6},{6,7},{7,4},{8,9},{9,10},{10,1... | collective-permute-start | bytes 1769480 | tf_op jit(solution)/shard_map/ppermute | solution.py:551
  32.0 9.1 %collective-permute-start.10 = (bf16[192,640]{1,0:T(8,128)(2,1)S(1)}, bf16[192,640]{1,0:T(8,128)(2,1)S(1)}, u32[]{:S(2)}, u32[]{:S(2)}) collective-permute-start(bf16[192,640]{1,0:T(8,128)(2,1)S(1)} %get-tuple-element.146), channel_id=1, source_target_pairs={{0,28},{4,24},{8,20},{12,16},{16,12},{20,8},{24,4},{28,0},{1,29},{... | collective-permute-start | bytes 737288 | tf_op jit(solution)/shard_map/ppermute | solution.py:544
  33.8 12.6 %collective-permute-start.9 = (bf16[192,640]{1,0:T(8,128)(2,1)S(1)}, bf16[192,640]{1,0:T(8,128)(2,1)S(1)}, u32[]{:S(2)}, u32[]{:S(2)}) collective-permute-start(bf16[192,640]{1,0:T(8,128)(2,1)S(1)} %get-tuple-element.145), channel_id=1, source_target_pairs={{0,24},{4,28},{8,16},{12,20},{16,8},{20,12},{24,0},{28,4},{1,25},{... | collective-permute-start | bytes 737288 | tf_op jit(solution)/shard_map/ppermute | solution.py:544
  47.6 16.5 %collective-permute-start.11 = (bf16[768,384]{1,0:T(8,128)(2,1)S(1)}, bf16[768,384]{1,0:T(8,128)(2,1)S(1)}, u32[]{:S(2)}, u32[]{:S(2)}) collective-permute-start(bf16[768,384]{1,0:T(8,128)(2,1)S(1)} %collective-permute-done.8.refs_0_), channel_id=1, source_target_pairs={{0,1},{1,2},{2,3},{3,0},{4,5},{5,6},{6,7},{7,4},{8,9},{9,10},{10,1... | collective-permute-start | bytes 1769480 | tf_op jit(solution)/shard_map/ppermute | solution.py:551
  48.0 8.9 %collective-permute-start.12 = (bf16[192,640]{1,0:T(8,128)(2,1)S(1)}, bf16[192,640]{1,0:T(8,128)(2,1)S(1)}, u32[]{:S(2)}, u32[]{:S(2)}) collective-permute-start(bf16[192,640]{1,0:T(8,128)(2,1)S(1)} %get-tuple-element.150), channel_id=1, source_target_pairs={{0,16},{4,20},{8,24},{12,28},{16,0},{20,4},{24,8},{28,12},{1,17},{... | collective-permute-start | bytes 737288 | tf_op jit(solution)/shard_map/ppermute | solution.py:544
  49.4 8.9 %collective-permute-start.13 = (bf16[192,640]{1,0:T(8,128)(2,1)S(1)}, bf16[192,640]{1,0:T(8,128)(2,1)S(1)}, u32[]{:S(2)}, u32[]{:S(2)}) collective-permute-start(bf16[192,640]{1,0:T(8,128)(2,1)S(1)} %get-tuple-element.151), channel_id=1, source_target_pairs={{0,8},{4,12},{8,0},{12,4},{16,24},{20,28},{24,16},{28,20},{1,9},{5... | collective-permute-start | bytes 737288 | tf_op jit(solution)/shard_map/ppermute | solution.py:544
  50.9 9.0 %collective-permute-start.14 = (bf16[192,640]{1,0:T(8,128)(2,1)S(1)}, bf16[192,640]{1,0:T(8,128)(2,1)S(1)}, u32[]{:S(2)}, u32[]{:S(2)}) collective-permute-start(bf16[192,640]{1,0:T(8,128)(2,1)S(1)} %get-tuple-element.152), channel_id=1, source_target_pairs={{0,20},{4,16},{8,28},{12,24},{16,4},{20,0},{24,12},{28,8},{1,21},{... | collective-permute-start | bytes 737288 | tf_op jit(solution)/shard_map/ppermute | solution.py:544
  50.9 10.2 %collective-permute-start.15 = (bf16[192,640]{1,0:T(8,128)(2,1)S(1)}, bf16[192,640]{1,0:T(8,128)(2,1)S(1)}, u32[]{:S(2)}, u32[]{:S(2)}) collective-permute-start(bf16[192,640]{1,0:T(8,128)(2,1)S(1)} %get-tuple-element.153), channel_id=1, source_target_pairs={{0,12},{4,8},{8,4},{12,0},{16,28},{20,24},{24,20},{28,16},{1,13},{... | collective-permute-start | bytes 737288 | tf_op jit(solution)/shard_map/ppermute | solution.py:544
  56.9 4.2 %collective-permute-start.16 = (bf16[192,640]{1,0:T(8,128)(2,1)S(1)}, bf16[192,640]{1,0:T(8,128)(2,1)S(1)}, u32[]{:S(2)}, u32[]{:S(2)}) collective-permute-start(bf16[192,640]{1,0:T(8,128)(2,1)S(1)} %get-tuple-element.154), channel_id=1, source_target_pairs={{0,4},{4,0},{8,12},{12,8},{16,20},{20,16},{24,28},{28,24},{1,5},{5... | collective-permute-start | bytes 737288 | tf_op jit(solution)/shard_map/ppermute | solution.py:544
  64.1 32.7 %collective-permute-start.20 = (bf16[720,1024]{1,0:T(8,128)(2,1)S(1)}, bf16[720,1024]{1,0:T(8,128)(2,1)S(1)}, u32[]{:S(2)}, u32[]{:S(2)}) collective-permute-start(bf16[720,1024]{1,0:T(8,128)(2,1)S(1)} %pad_maximum_fusion.refs_0_), channel_id=1, source_target_pairs={{0,8},{4,12},{8,0},{12,4},{16,24},{20,28},{24,16},{28,20},{1,9},{5... | collective-permute-start | bytes 4423688 | tf_op jit(solution)/shard_map/ppermute | solution.py:544
  65.3 32.6 %collective-permute-start.21 = (bf16[720,1024]{1,0:T(8,128)(2,1)S(1)}, bf16[720,1024]{1,0:T(8,128)(2,1)S(1)}, u32[]{:S(2)}, u32[]{:S(2)}) collective-permute-start(bf16[720,1024]{1,0:T(8,128)(2,1)S(1)} %pad_maximum_fusion.refs_0_), channel_id=1, source_target_pairs={{0,16},{4,20},{8,24},{12,28},{16,0},{20,4},{24,8},{28,12},{1,17},{... | collective-permute-start | bytes 4423688 | tf_op jit(solution)/shard_map/ppermute | solution.py:544
  69.8 26.5 %collective-permute-start.18 = (bf16[768,640]{1,0:T(8,128)(2,1)S(1)}, bf16[768,640]{1,0:T(8,128)(2,1)S(1)}, u32[]{:S(2)}, u32[]{:S(2)}) collective-permute-start(bf16[768,640]{1,0:T(8,128)(2,1)S(1)} %shard_map.88.refs_1_), channel_id=1, source_target_pairs={{0,1},{1,2},{2,3},{3,0},{4,5},{5,6},{6,7},{7,4},{8,9},{9,10},{10,1... | collective-permute-start | bytes 2949128 | tf_op jit(solution)/shard_map/ppermute | solution.py:551
  69.8 39.1 %collective-permute-start.17 = (bf16[768,384]{1,0:T(8,128)(2,1)S(1)}, bf16[768,384]{1,0:T(8,128)(2,1)S(1)}, u32[]{:S(2)}, u32[]{:S(2)}) collective-permute-start(bf16[768,384]{1,0:T(8,128)(2,1)S(1)} %collective-permute-done.11.refs_0_), channel_id=1, source_target_pairs={{0,1},{1,2},{2,3},{3,0},{4,5},{5,6},{6,7},{7,4},{8,9},{9,10},{10,1... | collective-permute-start | bytes 1769480 | tf_op jit(solution)/shard_map/ppermute | solution.py:551
  96.3 30.4 %collective-permute-start.19 = (bf16[768,640]{1,0:T(8,128)(2,1)S(1)}, bf16[768,640]{1,0:T(8,128)(2,1)S(1)}, u32[]{:S(2)}, u32[]{:S(2)}) collective-permute-start(bf16[768,640]{1,0:T(8,128)(2,1)S(1)} %collective-permute-done.18.refs_1_), channel_id=1, source_target_pairs={{0,1},{1,2},{2,3},{3,0},{4,5},{5,6},{6,7},{7,4},{8,9},{9,10},{10,1... | collective-permute-start | bytes 2949128 | tf_op jit(solution)/shard_map/ppermute | solution.py:551
  96.9 16.5 %collective-permute-start.22 = (bf16[720,512]{1,0:T(8,128)(2,1)S(1)}, bf16[720,512]{1,0:T(8,128)(2,1)S(1)}, u32[]{:S(2)}, u32[]{:S(2)}) collective-permute-start(bf16[720,512]{1,0:T(8,128)(2,1)S(1)} %slice.8), channel_id=1, source_target_pairs={{0,16},{4,20},{8,24},{12,28},{16,0},{20,4},{24,8},{28,12},{1,17},{... | collective-permute-start | bytes 2211848 | tf_op jit(solution)/shard_map/ppermute | solution.py:544
  98.0 1.7 collective-permute-start.24
  98.0 19.0 %collective-permute-start.23 = (bf16[720,512]{1,0:T(8,128)(2,1)S(1)}, bf16[720,512]{1,0:T(8,128)(2,1)S(1)}, u32[]{:S(2)}, u32[]{:S(2)}) collective-permute-start(bf16[720,512]{1,0:T(8,128)(2,1)S(1)} %slice.9), channel_id=1, source_target_pairs={{0,8},{4,12},{8,0},{12,4},{16,24},{20,28},{24,16},{28,20},{1,9},{5... | collective-permute-start | bytes 2211848 | tf_op jit(solution)/shard_map/ppermute | solution.py:544
  99.6 27.7 %collective-permute-start.32 = (bf16[768,640]{1,0:T(8,128)(2,1)S(1)}, bf16[768,640]{1,0:T(8,128)(2,1)S(1)}, u32[]{:S(2)}, u32[]{:S(2)}) collective-permute-start(bf16[768,640]{1,0:T(8,128)(2,1)S(1)} %shard_map.88.refs_1_), channel_id=1, source_target_pairs={{0,4},{4,0},{8,12},{12,8},{16,20},{20,16},{24,28},{28,24},{1,5},{5... | collective-permute-start | bytes 2949128 | tf_op jit(solution)/shard_map/ppermute | solution.py:544
  109.0 17.8 %collective-permute-start.31 = (bf16[768,384]{1,0:T(8,128)(2,1)S(1)}, bf16[768,384]{1,0:T(8,128)(2,1)S(1)}, u32[]{:S(2)}, u32[]{:S(2)}) collective-permute-start(bf16[768,384]{1,0:T(8,128)(2,1)S(1)} %get-tuple-element.144.refs_0_), channel_id=1, source_target_pairs={{0,4},{4,0},{8,12},{12,8},{16,20},{20,16},{24,28},{28,24},{1,5},{5... | collective-permute-start | bytes 1769480 | tf_op jit(solution)/shard_map/ppermute | solution.py:544
  113.4 13.4 %collective-permute-start.29 = (bf16[768,384]{1,0:T(8,128)(2,1)S(1)}, bf16[768,384]{1,0:T(8,128)(2,1)S(1)}, u32[]{:S(2)}, u32[]{:S(2)}) collective-permute-start(bf16[768,384]{1,0:T(8,128)(2,1)S(1)} %collective-permute-done.8.refs_0_), channel_id=1, source_target_pairs={{0,4},{4,0},{8,12},{12,8},{16,20},{20,16},{24,28},{28,24},{1,5},{5... | collective-permute-start | bytes 1769480 | tf_op jit(solution)/shard_map/ppermute | solution.py:544
  117.0 15.5 %collective-permute-start.30 = (bf16[768,640]{1,0:T(8,128)(2,1)S(1)}, bf16[768,640]{1,0:T(8,128)(2,1)S(1)}, u32[]{:S(2)}, u32[]{:S(2)}) collective-permute-start(bf16[768,640]{1,0:T(8,128)(2,1)S(1)} %collective-permute-done.18.refs_1_), channel_id=1, source_target_pairs={{0,4},{4,0},{8,12},{12,8},{16,20},{20,16},{24,28},{28,24},{1,5},{5... | collective-permute-start | bytes 2949128 | tf_op jit(solution)/shard_map/ppermute | solution.py:544
  126.7 11.2 %collective-permute-start.28 = (bf16[768,640]{1,0:T(8,128)(2,1)S(1)}, bf16[768,640]{1,0:T(8,128)(2,1)S(1)}, u32[]{:S(2)}, u32[]{:S(2)}) collective-permute-start(bf16[768,640]{1,0:T(8,128)(2,1)S(1)} %collective-permute-done.19.refs_1_), channel_id=1, source_target_pairs={{0,4},{4,0},{8,12},{12,8},{16,20},{20,16},{24,28},{28,24},{1,5},{5... | collective-permute-start | bytes 2949128 | tf_op jit(solution)/shard_map/ppermute | solution.py:544
  126.8 26.0 %collective-permute-start.25 = (bf16[768,640]{1,0:T(8,128)(2,1)S(1)}, bf16[768,640]{1,0:T(8,128)(2,1)S(1)}, u32[]{:S(2)}, u32[]{:S(2)}) collective-permute-start(bf16[768,640]{1,0:T(8,128)(2,1)S(1)} %collective-permute-done.19.refs_1_), channel_id=1, source_target_pairs={{0,1},{1,2},{2,3},{3,0},{4,5},{5,6},{6,7},{7,4},{8,9},{9,10},{10,1... | collective-permute-start | bytes 2949128 | tf_op jit(solution)/shard_map/ppermute | solution.py:551
  126.8 11.2 %collective-permute-start.27 = (bf16[768,384]{1,0:T(8,128)(2,1)S(1)}, bf16[768,384]{1,0:T(8,128)(2,1)S(1)}, u32[]{:S(2)}, u32[]{:S(2)}) collective-permute-start(bf16[768,384]{1,0:T(8,128)(2,1)S(1)} %collective-permute-done.11.refs_0_), channel_id=1, source_target_pairs={{0,4},{4,0},{8,12},{12,8},{16,20},{20,16},{24,28},{28,24},{1,5},{5... | collective-permute-start | bytes 1769480 | tf_op jit(solution)/shard_map/ppermute | solution.py:544
  127.3 16.1 %collective-permute-start.26 = (bf16[768,384]{1,0:T(8,128)(2,1)S(1)}, bf16[768,384]{1,0:T(8,128)(2,1)S(1)}, u32[]{:S(2)}, u32[]{:S(2)}) collective-permute-start(bf16[768,384]{1,0:T(8,128)(2,1)S(1)} %collective-permute-done.17.refs_0_), channel_id=1, source_target_pairs={{0,4},{4,0},{8,12},{12,8},{16,20},{20,16},{24,28},{28,24},{1,5},{5... | collective-permute-start | bytes 1769480 | tf_op jit(solution)/shard_map/ppermute | solution.py:544
  152.7 2.6 %collective-permute-start.33 = (bf16[768,640]{1,0:T(8,128)(2,1)S(1)}, bf16[768,640]{1,0:T(8,128)(2,1)S(1)}, u32[]{:S(2)}, u32[]{:S(2)}) collective-permute-start(bf16[768,640]{1,0:T(8,128)(2,1)S(1)} %collective-permute-done.25.refs_1_), channel_id=1, source_target_pairs={{0,4},{4,0},{8,12},{12,8},{16,20},{20,16},{24,28},{28,24},{1,5},{5... | collective-permute-start | bytes 2949128 | tf_op jit(solution)/shard_map/ppermute | solution.py:544
  161.9 1.3 collective-permute-start.34
  163.8 4.8 %collective-permute-start.35 = (f32[8,1536]{1,0:T(8,128)S(1)}, f32[8,1536]{1,0:T(8,128)S(1)}, u32[]{:S(2)}, u32[]{:S(2)}) collective-permute-start(f32[8,1536]{1,0:T(8,128)S(1)} %shard_map.95.refs_2_), channel_id=1, source_target_pairs={{0,1},{1,0},{2,3},{3,2},{4,5},{5,4},{6,7},{7,6},{8,9},{9,8},{10,11... | collective-permute-start | bytes 147464 | tf_op jit(solution)/shard_map/ppermute | solution.py:619
  163.9 7.4 %collective-permute-start.36 = (f32[8,1536]{1,0:T(8,128)S(1)}, f32[8,1536]{1,0:T(8,128)S(1)}, u32[]{:S(2)}, u32[]{:S(2)}) collective-permute-start(f32[8,1536]{1,0:T(8,128)S(1)} %shard_map.95.refs_2_), channel_id=1, source_target_pairs={{0,2},{1,3},{2,0},{3,1},{4,6},{5,7},{6,4},{7,5},{8,10},{9,11},{10,... | collective-permute-start | bytes 147464 | tf_op jit(solution)/shard_map/ppermute | solution.py:619
  164.0 7.3 %collective-permute-start.37 = (f32[8,1536]{1,0:T(8,128)S(1)}, f32[8,1536]{1,0:T(8,128)S(1)}, u32[]{:S(2)}, u32[]{:S(2)}) collective-permute-start(f32[8,1536]{1,0:T(8,128)S(1)} %shard_map.95.refs_2_), channel_id=1, source_target_pairs={{0,3},{1,2},{2,1},{3,0},{4,7},{5,6},{6,5},{7,4},{8,11},{9,10},{10,... | collective-permute-start | bytes 147464 | tf_op jit(solution)/shard_map/ppermute | solution.py:619
  175.5 19.0 %collective-permute-start.38 = (bf16[720,512]{1,0:T(8,128)(2,1)S(1)}, bf16[720,512]{1,0:T(8,128)(2,1)S(1)}, u32[]{:S(2)}, u32[]{:S(2)}) collective-permute-start(bf16[720,512]{1,0:T(8,128)(2,1)S(1)} %get-tuple-element.188), channel_id=1, source_target_pairs={{0,8},{4,12},{8,0},{12,4},{16,24},{20,28},{24,16},{28,20},{1,9},{5... | collective-permute-start | bytes 2211848 | tf_op jit(solution)/shard_map/ppermute | solution.py:544
  176.1 18.4 %collective-permute-start.39 = (bf16[720,512]{1,0:T(8,128)(2,1)S(1)}, bf16[720,512]{1,0:T(8,128)(2,1)S(1)}, u32[]{:S(2)}, u32[]{:S(2)}) collective-permute-start(bf16[720,512]{1,0:T(8,128)(2,1)S(1)} %get-tuple-element.189), channel_id=1, source_target_pairs={{0,16},{4,20},{8,24},{12,28},{16,0},{20,4},{24,8},{28,12},{1,17},{... | collective-permute-start | bytes 2211848 | tf_op jit(solution)/shard_map/ppermute | solution.py:544
  177.1 17.4 %collective-permute-start.40 = (bf16[64,720]{1,0:T(8,128)(2,1)S(1)}, bf16[64,720]{1,0:T(8,128)(2,1)S(1)}, u32[]{:S(2)}, u32[]{:S(2)}) collective-permute-start(bf16[64,720]{1,0:T(8,128)(2,1)S(1)} %get-tuple-element.197.mine_ref), channel_id=1, source_target_pairs={{0,8},{4,12},{8,0},{12,4},{16,24},{20,28},{24,16},{28,20},{1,9},{5... | collective-permute-start | bytes 276488 | tf_op jit(solution)/shard_map/ppermute | solution.py:544
  195.9 21.5 %collective-permute-start.44 = (bf16[720,512]{1,0:T(8,128)(2,1)S(1)}, bf16[720,512]{1,0:T(8,128)(2,1)S(1)}, u32[]{:S(2)}, u32[]{:S(2)}) collective-permute-start(bf16[720,512]{1,0:T(8,128)(2,1)S(1)} %get-tuple-element.214), channel_id=1, source_target_pairs={{0,16},{4,12},{8,24},{12,4},{16,0},{20,28},{24,8},{28,20},{1,17},{... | collective-permute-start | bytes 2211848 | tf_op jit(solution)/shard_map/ppermute | solution.py:548
  196.4 21.0 %collective-permute-start.45 = (bf16[720,512]{1,0:T(8,128)(2,1)S(1)}, bf16[720,512]{1,0:T(8,128)(2,1)S(1)}, u32[]{:S(2)}, u32[]{:S(2)}) collective-permute-start(bf16[720,512]{1,0:T(8,128)(2,1)S(1)} %get-tuple-element.204), channel_id=1, source_target_pairs={{0,8},{4,20},{8,0},{12,28},{16,24},{20,4},{24,16},{28,12},{1,9},{5... | collective-permute-start | bytes 2211848 | tf_op jit(solution)/shard_map/ppermute | solution.py:548
  198.0 19.4 %collective-permute-start.43 = (bf16[64,720]{1,0:T(8,128)(2,1)S(1)}, bf16[64,720]{1,0:T(8,128)(2,1)S(1)}, u32[]{:S(2)}, u32[]{:S(2)}) collective-permute-start(bf16[64,720]{1,0:T(8,128)(2,1)S(1)} %shard_map.98), channel_id=1, source_target_pairs={{0,16},{4,20},{8,24},{12,28},{16,0},{20,4},{24,8},{28,12},{1,17},{... | collective-permute-start | bytes 276488 | tf_op jit(solution)/shard_map/ppermute | solution.py:544
  199.1 25.2 %collective-permute-start.47 = (bf16[720,512]{1,0:T(8,128)(2,1)}, bf16[720,512]{1,0:T(8,128)(2,1)}, u32[]{:S(2)}, u32[]{:S(2)}) collective-permute-start(bf16[720,512]{1,0:T(8,128)(2,1)} %get-tuple-element.213), channel_id=1, source_target_pairs={{0,12},{4,16},{8,4},{12,24},{16,28},{20,0},{24,20},{28,8},{1,13},{... | collective-permute-start | bytes 2211848 | tf_op jit(solution)/shard_map/ppermute | solution.py:548
  199.1 25.2 %collective-permute-start.41 = (bf16[720,512]{1,0:T(8,128)(2,1)}, bf16[720,512]{1,0:T(8,128)(2,1)}, u32[]{:S(2)}, u32[]{:S(2)}) collective-permute-start(bf16[720,512]{1,0:T(8,128)(2,1)} %get-tuple-element.198), channel_id=1, source_target_pairs={{0,4},{4,0},{8,12},{12,8},{16,20},{20,16},{24,28},{28,24},{1,5},{5... | collective-permute-start | bytes 2211848 | tf_op jit(solution)/shard_map/ppermute | solution.py:544
  217.4 11.2 %collective-permute-start.42 = (bf16[720,512]{1,0:T(8,128)(2,1)}, bf16[720,512]{1,0:T(8,128)(2,1)}, u32[]{:S(2)}, u32[]{:S(2)}) collective-permute-start(bf16[720,512]{1,0:T(8,128)(2,1)} %get-tuple-element.199), channel_id=1, source_target_pairs={{0,20},{4,8},{8,28},{12,0},{16,4},{20,24},{24,12},{28,16},{1,21},{... | collective-permute-start | bytes 2211848 | tf_op jit(solution)/shard_map/ppermute | solution.py:548
  217.5 3.5 %collective-permute-start.46 = (f32[64,720]{1,0:T(8,128)S(1)}, f32[64,720]{1,0:T(8,128)S(1)}, u32[]{:S(2)}, u32[]{:S(2)}) collective-permute-start(f32[64,720]{1,0:T(8,128)S(1)} %convert_add_fusion), channel_id=1, source_target_pairs={{0,4},{4,0},{8,12},{12,8},{16,20},{20,16},{24,28},{28,24},{1,5},{5... | collective-permute-start | bytes 552968 | tf_op jit(solution)/shard_map/ppermute | solution.py:544

commit v13 on v11

--- a/solution.py
+++ b/solution.py
@@ -306,14 +306,15 @@
         refs[2 * parts],
         refs[2 * parts + 1 :],
     )
+    hot_own = hot_sib = None
     if first:
         acc_out, full_ref = refs
     elif last:
-        acc_ref, _, hot_own, hot_sib, extra_ref, shifted_ref, stat_ref, full_ref = refs
+        acc_ref, _, shifted_ref, stat_ref, full_ref = refs
     elif used is None:
         acc_ref, _, acc_out, full_ref = refs
     else:
-        acc_ref, acc_out = refs
+        acc_ref, hot_own, hot_sib, extra_ref, acc_out = refs
     half = pl.num_programs(0) // 2
 
     def tile(sources, hot):
@@ -326,10 +327,11 @@
         total = mm(panel, block, NT)
         if not first:
             total = acc_ref[...] + total
+        if hot is not None:
+            total = total + mm(extra_ref[...], hot[...], NN)
         if not last:
             acc_out[...] = total
             return
-        total = total + mm(extra_ref[...], hot[...], NN)
         peak = jnp.max(total, axis=0, keepdims=True)
         shifted = jnp.exp(total - peak)
         shifted_ref[...] = shifted
@@ -339,20 +341,20 @@
 
     @pl.when(pl.program_id(0) < half)
     def _():
-        tile(own, hot_own if last else None)
+        tile(own, hot_own)
 
     @pl.when(pl.program_id(0) >= half)
     def _():
-        tile(sib, hot_sib if last else None)
-
-
-def score(meta, at, own, sib, panels, width, acc=None, full=None, hots=None, extra=None, used=None):
+        tile(sib, hot_sib)
+
+
+def score(meta, at, own, sib, panels, width, acc=None, full=None, used=None, hots=None, extra=None):
     rows = own[0].shape[0]
     parts = len(own)
     tile = 256
     half = rows // tile
     count, columns = panels.shape
-    first, last = acc is None, hots is not None
+    first, last = acc is None, used is not None and hots is None
     store = used is None or last
     fronts = [pl.BlockSpec((tile, v.shape[1]), lambda j, m: (jnp.minimum(j, half - 1), 0)) for v in own]
     backs = [pl.BlockSpec((tile, v.shape[1]), lambda j, m: (jnp.maximum(j - half, 0), 0)) for v in own]
@@ -373,6 +375,9 @@
     acc_shape = sds((count, 2 * rows), F32)
     out_specs, out_shape = [acc_spec, full_spec], [acc_shape, full_shape]
     if last:
+        out_specs = [acc_spec, pl.BlockSpec((8, tile), lambda j, m: (0, j)), full_spec]
+        out_shape = [acc_shape, sds((8, 2 * rows), F32), full_shape]
+    elif not store:
         depth = extra.shape[1]
         in_specs += [
             pl.BlockSpec((depth, tile), lambda j, m: (0, jnp.minimum(j, half - 1))),
@@ -380,9 +385,6 @@
             pl.BlockSpec((count, depth), lambda j, m: (0, 0)),
         ]
         operands += [*hots, extra]
-        out_specs = [acc_spec, pl.BlockSpec((8, tile), lambda j, m: (0, j)), full_spec]
-        out_shape = [acc_shape, sds((8, 2 * rows), F32), full_shape]
-    elif not store:
         out_specs, out_shape = acc_spec, acc_shape
     return call(
         functools.partial(score_body, parts, used, first, last),
@@ -589,7 +591,9 @@
     acc, full = score(meta, share(2), [a2, b2], sib2, panel_full, width, acc, full)
     final = share(turns - 1)
     a3_sib = across(a3, 1)
-    acc = score(meta, final, [a3], [a3_sib], panel_full, width, acc, used=chunk_a)
+    acc = score(
+        meta, final, [a3], [a3_sib], panel_full, width, acc, None, chunk_a, hots, extra
+    )
     b3, acc = together((b3, acc))
     shifted, stat, full = score(
         meta,
@@ -600,8 +604,6 @@
         width,
         acc,
         full,
-        hots,
-        extra,
         chunk_b,
     )
 

time: 233 us -> 232 us (level)
  no operation moved by 1% of the time
where the time goes in v13:
time: 232 us; the launch traced here: 231 us
  waiting for transfers between devices  112 us (48%)
  Pallas kernels  69.7 us (30%)
  starting transfers between devices  39.4 us (17%)
  other arithmetic  6.82 us (3%)
    ppermute x35, waiting for transfers between devices, across(): return lax.ppermute(value, 'dom', [(i, i ^ apart) for i in range(dom)])  69.1 us
    ppermute x6, waiting for transfers between devices, onward(): lax.ppermute(value, 'rot', [(i, (i + 1) % turns) for i in range(turns)])  33.9 us
    ppermute x35, starting transfers between devices, across(): return lax.ppermute(value, 'dom', [(i, i ^ apart) for i in range(dom)])  28 us
    pallas_call x5, Pallas kernels, score(): call(functools.partial(score_body, parts, used, first, last), (2 * half,)...  26.4 us
    pallas_call x2, Pallas kernels, class_part(): call(functools.partial(class_body, kind, steps), (steps,), in_specs, out_...  15 us
    pallas_call x1, Pallas kernels, energy(): call(functools.partial(energy_body, bins, count), (count,), [pl.BlockSpec...  6.79 us
    ppermute x4, waiting for transfers between devices, by_core(): return lax.ppermute(value, 'dom', pairs)  6.39 us
    pallas_call x1, Pallas kernels, pack_next(): call(functools.partial(pack_next_body, cap, dom), (1,), [pl.BlockSpec((1,...  5.9 us
  transfers between devices with their start and end apart: 48, of which 26 were waited for; matrix products, arithmetic and copies ran while one was open for 2% of the time, Pallas kernels for 24%

profile of v13, /device:TPU:0, one launch (start us, length us, event | category | flops | bytes accessed | tf_op | source)
XLA Modules:
  0.0 231.0 jit_solution(9320563856772652971)
XLA Ops:
  1.2 0.7 add_select_fusion.slot_ref
  2.0 5.8 %shard_map.85 = (bf16[208,384]{1,0:T(8,128)(2,1)S(1)}, bf16[208,384]{1,0:T(8,128)(2,1)S(1)}, bf16[208,384]{1,0:T(8,128)(2,1)S(1)}, bf16[208,384]{1,0:T(8,128)(2,...) custom-call(s32[10]{0:T(128)S(1)} %stack.43.meta, ...), custom_call_target="tpu_custom_call" | custom-call | flops 113246208 | bytes 147456 | tf_op jit(solution)/shard_map/pallas_call | solution.py:132
  7.7 3.6 %collective-permute-start = (bf16[208,384]{1,0:T(8,128)(2,1)S(1)}, bf16[208,384]{1,0:T(8,128)(2,1)S(1)}, u32[]{:S(2)}, u32[]{:S(2)}) collective-permute-start(bf16[208,384]{1,0:T(8,128)(2,1)S(1)} %get-tuple-element.101), channel_id=1, source_target_pairs={{0,24},{4,28},{8,16},{12,20},{16,8},{20,12},{24,0},{28,4},{1,25},{... | collective-permute-start | bytes 479240 | tf_op jit(solution)/shard_map/ppermute | solution.py:537
  11.4 1.6 collective-permute-start.2
  13.1 1.5 collective-permute-start.3
  14.7 1.2 constant_dynamic-slice_fusion
  16.4 0.6 collective-permute-start.5
  17.0 2.3 %collective-permute-done.1.refs_1_ = bf16[208,384]{1,0:T(8,128)(2,1)S(1)} collective-permute-done((bf16[208,384]{1,0:T(8,128)(2,1)S(1)}, bf16[208,384]{1,0:T(8,128)(2,1)S(1)}, u32[]{:S(2)}, u32[]{:S(2)}) %collective-permute-start.1) | collective-permute-done | bytes 159776 | tf_op jit(solution)/shard_map/ppermute | solution.py:537
  19.6 5.9 %shard_map.86 = (bf16[192,640]{1,0:T(8,128)(2,1)S(1)}, bf16[192,640]{1,0:T(8,128)(2,1)S(1)}, bf16[192,640]{1,0:T(8,128)(2,1)S(1)}, bf16[192,640]{1,0:T(8,128)(2,...) custom-call(s32[10]{0:T(128)S(1)} %stack.43.meta, ...), custom_call_target="tpu_custom_call" | custom-call | flops 188743680 | bytes 245760 | tf_op jit(solution)/shard_map/pallas_call | solution.py:152
  26.5 3.5 %shard_map.87 = (bf16[768,384]{1,0:T(8,128)(2,1)S(1)}, bf16[192,768]{1,0:T(8,128)(2,1)S(1)}, bf16[768,1536]{1,0:T(8,128)(2,1)S(1)}, bf16[768,192]{1,0:T(8,128)(2,1)S(1)}) custom-call(s32[10]{0:T(128)S(1)} %stack.43.meta, bf16[208,384]{1,0:T(8,128)(2,1)S(1)} %collective-permute-done.refs_0_, bf16[208,384]{1,0:T(8,128)(2,1)S(1)} %collective-permute-done.1.refs_1_, ...), custom_call_target="tpu_custom_call" | custom-call | flops 56623104 | bytes 73728 | tf_op jit(solution)/shard_map/pallas_call | solution.py:212
  30.0 2.0 collective-permute-start.8
  32.1 1.8 collective-permute-start.10
  33.8 0.7 collective-permute-start.9
  34.5 6.6 %collective-permute-done.10.refs_1_ = bf16[192,640]{1,0:T(8,128)(2,1)S(1)} collective-permute-done((bf16[192,640]{1,0:T(8,128)(2,1)S(1)}, bf16[192,640]{1,0:T(8,128)(2,1)S(1)}, u32[]{:S(2)}, u32[]{:S(2)}) %collective-permute-start.10) | collective-permute-done | bytes 245792 | tf_op jit(solution)/shard_map/ppermute | solution.py:537
  41.1 5.4 %collective-permute-done.9.refs_0_ = bf16[192,640]{1,0:T(8,128)(2,1)S(1)} collective-permute-done((bf16[192,640]{1,0:T(8,128)(2,1)S(1)}, bf16[192,640]{1,0:T(8,128)(2,1)S(1)}, u32[]{:S(2)}, u32[]{:S(2)}) %collective-permute-start.9) | collective-permute-done | bytes 245792 | tf_op jit(solution)/shard_map/ppermute | solution.py:537
  46.5 1.1 collective-permute-done.8.refs_0_
  48.1 1.3 collective-permute-start.12
  49.4 1.5 collective-permute-start.13
  50.9 1.0 collective-permute-start.15
  51.8 5.1 %collective-permute-done.12.refs_2_ = bf16[192,640]{1,0:T(8,128)(2,1)S(1)} collective-permute-done((bf16[192,640]{1,0:T(8,128)(2,1)S(1)}, bf16[192,640]{1,0:T(8,128)(2,1)S(1)}, u32[]{:S(2)}, u32[]{:S(2)}) %collective-permute-start.12) | collective-permute-done | bytes 245792 | tf_op jit(solution)/shard_map/ppermute | solution.py:537
  56.9 1.3 collective-permute-done.13.refs_3_
  58.3 1.6 collective-permute-done.14.refs_4_
  59.9 1.2 collective-permute-done.15.refs_5_
  61.1 2.9 %shard_map.88.refs_1_ = bf16[768,640]{1,0:T(8,128)(2,1)S(1)} custom-call(s32[10]{0:T(128)S(1)} %stack.43.meta, bf16[192,640]{1,0:T(8,128)(2,1)S(1)} %collective-permute-done.9.refs_0_, bf16[192,640]{1,0:T(8,128)(2,1)S(1)} %collective-permute-done.10.refs_1_, bf16[192,640]{1,0:T(8,128)(2,1)S(1)} %collective-permute-done.12.refs_2_, ...), custom_call_target="tpu_custom_call" | custom-call | flops 94371840 | bytes 122880 | tf_op jit(solution)/shard_map/pallas_call | solution.py:231
  64.1 1.3 collective-permute-start.20
  65.3 1.5 collective-permute-start.21
  67.8 25.5 %collective-permute-done.18.refs_1_ = bf16[768,640]{1,0:T(8,128)(2,1)S(1)} collective-permute-done((bf16[768,640]{1,0:T(8,128)(2,1)S(1)}, bf16[768,640]{1,0:T(8,128)(2,1)S(1)}, u32[]{:S(2)}, u32[]{:S(2)}) %collective-permute-start.18) | collective-permute-done | bytes 983072 | tf_op jit(solution)/shard_map/ppermute | solution.py:544
  93.3 5.8 %collective-permute-done.20.refs_1_ = bf16[720,1024]{1,0:T(8,128)(2,1)S(1)} collective-permute-done((bf16[720,1024]{1,0:T(8,128)(2,1)S(1)}, bf16[720,1024]{1,0:T(8,128)(2,1)S(1)}, u32[]{:S(2)}, u32[]{:S(2)}) %collective-permute-start.20) | collective-permute-done | bytes 1474592 | tf_op jit(solution)/shard_map/ppermute | solution.py:537
  99.2 0.9 collective-permute-start.22
  100.5 1.2 collective-permute-start.23
  101.9 4.0 %collective-permute-done.17.refs_0_ = bf16[768,384]{1,0:T(8,128)(2,1)S(1)} collective-permute-done((bf16[768,384]{1,0:T(8,128)(2,1)S(1)}, bf16[768,384]{1,0:T(8,128)(2,1)S(1)}, u32[]{:S(2)}, u32[]{:S(2)}) %collective-permute-start.17) | collective-permute-done | bytes 589856 | tf_op jit(solution)/shard_map/ppermute | solution.py:544
  105.9 12.0 %collective-permute-done.22.refs_3_ = bf16[720,512]{1,0:T(8,128)(2,1)S(1)} collective-permute-done((bf16[720,512]{1,0:T(8,128)(2,1)S(1)}, bf16[720,512]{1,0:T(8,128)(2,1)S(1)}, u32[]{:S(2)}, u32[]{:S(2)}) %collective-permute-start.22) | collective-permute-done | bytes 737312 | tf_op jit(solution)/shard_map/ppermute | solution.py:537
  117.9 1.3 collective-permute-done.23.refs_4_
  119.2 6.8 %shard_map.89 = (bf16[720,4096]{1,0:T(8,128)(2,1)S(1)}, bf16[720,192]{1,0:T(8,128)(2,1)S(1)}) custom-call(s32[10]{0:T(128)S(1)} %stack.43.meta, bf16[720,1024]{1,0:T(8,128)(2,1)S(1)} %pad_maximum_fusion.refs_0_, bf16[720,1024]{1,0:T(8,128)(2,1)S(1)} %collective-permute-done.20.refs_1_, bf16[720,1024]{1,0:T(8,128)(2,1)S(1)} %collective-permute-done.21.refs_2_, ...), custom_call_target="tpu_custom_call" | custom-call | flops 283115520 | bytes 737280 | tf_op jit(solution)/shard_map/pallas_call | solution.py:283
  126.6 1.3 collective-permute-start.25
  128.4 5.1 %shard_map.90 = (f32[720,1536]{1,0:T(8,128)S(1)}, bf16[1536,4096]{1,0:T(8,128)(2,1)S(1)}) custom-call(s32[10]{0:T(128)S(1)} %stack.43.meta, bf16[768,384]{1,0:T(8,128)(2,1)S(1)} %get-tuple-element.137.refs_0_, bf16[768,640]{1,0:T(8,128)(2,1)S(1)} %shard_map.88.refs_1_, bf16[768,384]{1,0:T(8,128)(2,1)S(1)} %collective-permute-done.31.refs_2_, ...), custom_call_target="tpu_custom_call" | custom-call | flops 141557760 | bytes 946176 | tf_op jit(solution)/shard_map/pallas_call | solution.py:389
  133.5 5.4 %shard_map.91 = (f32[720,1536]{1,0:T(8,128)S(1)}, bf16[1536,4096]{1,0:T(8,128)(2,1)S(1)}) custom-call(s32[10]{0:T(128)S(1)} %stack.43.meta, bf16[768,384]{1,0:T(8,128)(2,1)S(1)} %collective-permute-done.8.refs_0_, bf16[768,640]{1,0:T(8,128)(2,1)S(1)} %collective-permute-done.18.refs_1_, ...), custom_call_target="tpu_custom_call", output_to_operand_aliasing={{0}: (6, {}), {1}: (7, {})} | custom-call | flops 141557760 | bytes 946176 | tf_op jit(solution)/shard_map/pallas_call | solution.py:389
  139.0 5.4 %shard_map.92 = (f32[720,1536]{1,0:T(8,128)S(1)}, bf16[1536,4096]{1,0:T(8,128)(2,1)S(1)}) custom-call(s32[10]{0:T(128)S(1)} %stack.43.meta, bf16[768,384]{1,0:T(8,128)(2,1)S(1)} %collective-permute-done.11.refs_0_, bf16[768,640]{1,0:T(8,128)(2,1)S(1)} %collective-permute-done.19.refs_1_, ...), custom_call_target="tpu_custom_call", output_to_operand_aliasing={{0}: (6, {}), {1}: (7, {})} | custom-call | flops 141557760 | bytes 946176 | tf_op jit(solution)/shard_map/pallas_call | solution.py:389
  144.4 4.4 %shard_map.93.refs_5_ = f32[720,1536]{1,0:T(8,128)S(1)} custom-call(s32[10]{0:T(128)S(1)} %stack.43.meta, bf16[768,384]{1,0:T(8,128)(2,1)S(1)} %collective-permute-done.17.refs_0_, bf16[768,384]{1,0:T(8,128)(2,1)S(1)} %collective-permute-done.26.refs_1_.refs_2_, ...), custom_call_target="tpu_custom_call", output_to_operand_aliasing={{}: (4, {})} | custom-call | flops 141557760 | bytes 946176 | tf_op jit(solution)/shard_map/pallas_call | solution.py:389
  148.8 3.3 %collective-permute-done.25.refs_1_ = bf16[768,640]{1,0:T(8,128)(2,1)S(1)} collective-permute-done((bf16[768,640]{1,0:T(8,128)(2,1)S(1)}, bf16[768,640]{1,0:T(8,128)(2,1)S(1)}, u32[]{:S(2)}, u32[]{:S(2)}) %collective-permute-start.25) | collective-permute-done | bytes 983072 | tf_op jit(solution)/shard_map/ppermute | solution.py:544
  152.1 2.6 %collective-permute-done.33.refs_3_ = bf16[768,640]{1,0:T(8,128)(2,1)S(1)} collective-permute-done((bf16[768,640]{1,0:T(8,128)(2,1)S(1)}, bf16[768,640]{1,0:T(8,128)(2,1)S(1)}, u32[]{:S(2)}, u32[]{:S(2)}) %collective-permute-start.33) | collective-permute-done | bytes 983072 | tf_op jit(solution)/shard_map/ppermute | solution.py:537
  154.7 6.1 %shard_map.94 = (f32[720,1536]{1,0:T(8,128)S(1)}, f32[8,1536]{1,0:T(8,128)S(1)}, bf16[1536,4096]{1,0:T(8,128)(2,1)S(1)}) custom-call(s32[10]{0:T(128)S(1)} %stack.43.meta, bf16[768,384]{1,0:T(8,128)(2,1)S(1)} %collective-permute-done.17.refs_0_, bf16[768,640]{1,0:T(8,128)(2,1)S(1)} %collective-permute-done.25.refs_1_, ...), custom_call_target="tpu_custom_call", output_to_operand_aliasing={{0}: (6, {}), {2}: (7, {})} | custom-call | flops 141557760 | bytes 946176 | tf_op jit(solution)/shard_map/pallas_call | solution.py:389
  160.9 1.1 collective-permute-done.34.other_ref
  162.7 0.9 collective-permute-start.36
  163.6 3.5 %collective-permute-start.37 = (f32[8,1536]{1,0:T(8,128)S(1)}, f32[8,1536]{1,0:T(8,128)S(1)}, u32[]{:S(2)}, u32[]{:S(2)}) collective-permute-start(f32[8,1536]{1,0:T(8,128)S(1)} %shard_map.95.refs_2_), channel_id=1, source_target_pairs={{0,3},{1,2},{2,1},{3,0},{4,7},{5,6},{6,5},{7,4},{8,11},{9,10},{10,... | collective-permute-start | bytes 147464 | tf_op jit(solution)/shard_map/ppermute | solution.py:612
  167.4 2.7 %collective-permute-done.36.refs_4_ = f32[8,1536]{1,0:T(8,128)S(1)} collective-permute-done((f32[8,1536]{1,0:T(8,128)S(1)}, f32[8,1536]{1,0:T(8,128)S(1)}, u32[]{:S(2)}, u32[]{:S(2)}) %collective-permute-start.36) | collective-permute-done | bytes 49184 | tf_op jit(solution)/shard_map/ppermute | solution.py:612
  170.1 4.2 %shard_map.96 = (bf16[720,512]{1,0:T(8,128)(2,1)S(1)}, bf16[720,512]{1,0:T(8,128)(2,1)S(1)}, bf16[720,1536]{1,0:T(8,128)(2,1)S(1)}, f32[1,768]{1,0:T(1,128)S(1)}, bf16[64,720]{1,0:T(8,128)(2,1)S(1)}) custom-call(s32[10]{0:T(128)S(1)} %stack.43.meta, f32[720,1536]{1,0:T(8,128)S(1)} %get-tuple-element.171.refs_0_, ...), custom_call_target="tpu_custom_call" | custom-call | flops 141557760 | bytes 657408 | tf_op jit(solution)/shard_map/pallas_call | solution.py:477
  174.3 1.4 collective-permute-start.38
  175.8 0.8 collective-permute-start.39
  176.6 1.0 collective-permute-start.40
  177.6 10.7 %shard_map.97 = (bf16[720,512]{1,0:T(8,128)(2,1)S(1)}, bf16[720,512]{1,0:T(8,128)(2,1)}, bf16[720,512]{1,0:T(8,128)(2,1)}, f32[720,512]{1,0:T(8,128)S(1)}, f32[7...) custom-call(s32[10]{0:T(128)S(1)} %stack.43.meta, bf16[720,1536]{1,0:T(8,128)(2,1)S(1)} %get-tuple-element.176.refs_0_, ...), custom_call_target="tpu_custom_call" | custom-call | flops 424673280 | bytes 1419264 | tf_op jit(solution)/shard_map/pallas_call | solution.py:477
  188.4 4.9 %collective-permute-done.40.other_ref = bf16[64,720]{1,0:T(8,128)(2,1)S(1)} collective-permute-done((bf16[64,720]{1,0:T(8,128)(2,1)S(1)}, bf16[64,720]{1,0:T(8,128)(2,1)S(1)}, u32[]{:S(2)}, u32[]{:S(2)}) %collective-permute-start.40) | collective-permute-done | bytes 92192 | tf_op jit(solution)/shard_map/ppermute | solution.py:537
  193.3 1.4 fusion.3
  194.7 1.2 collective-permute-start.42
  195.9 1.0 collective-permute-start.43
  197.5 1.3 collective-permute-start.41
  198.8 0.9 collective-permute-start.44
  199.7 16.6 %collective-permute-done.41 = bf16[64,720]{1,0:T(8,128)(2,1)S(1)} collective-permute-done((bf16[64,720]{1,0:T(8,128)(2,1)S(1)}, bf16[64,720]{1,0:T(8,128)(2,1)S(1)}, u32[]{:S(2)}, u32[]{:S(2)}) %collective-permute-start.41) | collective-permute-done | bytes 92192 | tf_op jit(solution)/shard_map/ppermute | solution.py:537
  216.3 1.5 collective-permute-start.46
  218.5 2.3 shard_map.99
  220.7 0.9 maximum_select_fusion
  221.6 2.5 %collective-permute-done.47 = bf16[720,512]{1,0:T(8,128)(2,1)} collective-permute-done((bf16[720,512]{1,0:T(8,128)(2,1)}, bf16[720,512]{1,0:T(8,128)(2,1)}, u32[]{:S(2)}, u32[]{:S(2)}) %collective-permute-start.47) | collective-permute-done | bytes 737312 | tf_op jit(solution)/shard_map/ppermute | solution.py:541
  224.2 3.9 %collective-permute-done.45 = bf16[720,512]{1,0:T(8,128)(2,1)} collective-permute-done((bf16[720,512]{1,0:T(8,128)(2,1)}, bf16[720,512]{1,0:T(8,128)(2,1)}, u32[]{:S(2)}, u32[]{:S(2)}) %collective-permute-start.45) | collective-permute-done | bytes 737312 | tf_op jit(solution)/shard_map/ppermute | solution.py:541
  228.0 2.9 %add_dynamic-update-slice_fusion = f32[1440,512]{1,0:T(8,128)} fusion(f32[1440,512]{1,0:T(8,128)} %shard_map.99, s32[]{:T(128)S(6)} %select_n.67, bf16[720,512]{1,0:T(8,128)(2,1)} %collective-permute-done.47, bf16[720,512]{1,0:T(8,128)(2,1)} %collective-permute-done.45, bf16[720,512]{1,0:T(8,128)(2,1)} %collective-permute-done.44), kind=kLoop, calls=%fused_computation.7 | loop fusion | flops 1843200 | bytes 3686404 | tf_op jit(solution)/shard_map/dynamic_update_slice | solution.py:641
  (65 shorter events, 8.2 us)
Async XLA Ops:
  0.6 14.0 %collective-permute-start.7 = (bf16[1440,512]{1,0:T(8,128)(2,1)}, bf16[1440,512]{1,0:T(8,128)(2,1)}, u32[]{:S(2)}, u32[]{:S(2)}) collective-permute-start(bf16[1440,512]{1,0:T(8,128)(2,1)} %param.11), channel_id=1, source_target_pairs={{0,4},{4,0},{8,12},{12,8},{16,20},{20,16},{24,28},{28,24},{1,5},{5... | collective-permute-start | bytes 4423688 | tf_op jit(solution)/shard_map/ppermute | solution.py:537
  2.0 12.6 %copy-start.2 = (bf16[1440,512]{1,0:T(8,128)(2,1)S(1)}, bf16[1440,512]{1,0:T(8,128)(2,1)}, u32[]{:S(2)}) copy-start(bf16[1440,512]{1,0:T(8,128)(2,1)} %param.11) | copy-start | bytes 4423684
  7.7 8.6 %collective-permute-start = (bf16[208,384]{1,0:T(8,128)(2,1)S(1)}, bf16[208,384]{1,0:T(8,128)(2,1)S(1)}, u32[]{:S(2)}, u32[]{:S(2)}) collective-permute-start(bf16[208,384]{1,0:T(8,128)(2,1)S(1)} %get-tuple-element.101), channel_id=1, source_target_pairs={{0,24},{4,28},{8,16},{12,20},{16,8},{20,12},{24,0},{28,4},{1,25},{... | collective-permute-start | bytes 479240 | tf_op jit(solution)/shard_map/ppermute | solution.py:537
  11.3 8.0 %collective-permute-start.1 = (bf16[208,384]{1,0:T(8,128)(2,1)S(1)}, bf16[208,384]{1,0:T(8,128)(2,1)S(1)}, u32[]{:S(2)}, u32[]{:S(2)}) collective-permute-start(bf16[208,384]{1,0:T(8,128)(2,1)S(1)} %get-tuple-element.102), channel_id=1, source_target_pairs={{0,28},{4,24},{8,20},{12,16},{16,12},{20,8},{24,4},{28,0},{1,29},{... | collective-permute-start | bytes 479240 | tf_op jit(solution)/shard_map/ppermute | solution.py:537
  11.4 14.2 %collective-permute-start.2 = (bf16[208,384]{1,0:T(8,128)(2,1)S(1)}, bf16[208,384]{1,0:T(8,128)(2,1)S(1)}, u32[]{:S(2)}, u32[]{:S(2)}) collective-permute-start(bf16[208,384]{1,0:T(8,128)(2,1)S(1)} %get-tuple-element.103), channel_id=1, source_target_pairs={{0,16},{4,20},{8,24},{12,28},{16,0},{20,4},{24,8},{28,12},{1,17},{... | collective-permute-start | bytes 479240 | tf_op jit(solution)/shard_map/ppermute | solution.py:537
  13.1 12.6 %collective-permute-start.3 = (bf16[208,384]{1,0:T(8,128)(2,1)S(1)}, bf16[208,384]{1,0:T(8,128)(2,1)S(1)}, u32[]{:S(2)}, u32[]{:S(2)}) collective-permute-start(bf16[208,384]{1,0:T(8,128)(2,1)S(1)} %get-tuple-element.104), channel_id=1, source_target_pairs={{0,8},{4,12},{8,0},{12,4},{16,24},{20,28},{24,16},{28,20},{1,9},{5... | collective-permute-start | bytes 479240 | tf_op jit(solution)/shard_map/ppermute | solution.py:537
  14.6 11.6 %collective-permute-start.4 = (bf16[208,384]{1,0:T(8,128)(2,1)S(1)}, bf16[208,384]{1,0:T(8,128)(2,1)S(1)}, u32[]{:S(2)}, u32[]{:S(2)}) collective-permute-start(bf16[208,384]{1,0:T(8,128)(2,1)S(1)} %get-tuple-element.105), channel_id=1, source_target_pairs={{0,20},{4,16},{8,28},{12,24},{16,4},{20,0},{24,12},{28,8},{1,21},{... | collective-permute-start | bytes 479240 | tf_op jit(solution)/shard_map/ppermute | solution.py:537
  16.4 9.9 %collective-permute-start.5 = (bf16[208,384]{1,0:T(8,128)(2,1)S(1)}, bf16[208,384]{1,0:T(8,128)(2,1)S(1)}, u32[]{:S(2)}, u32[]{:S(2)}) collective-permute-start(bf16[208,384]{1,0:T(8,128)(2,1)S(1)} %get-tuple-element.106), channel_id=1, source_target_pairs={{0,12},{4,8},{8,4},{12,0},{16,28},{20,24},{24,20},{28,16},{1,13},{... | collective-permute-start | bytes 479240 | tf_op jit(solution)/shard_map/ppermute | solution.py:537
  19.3 6.9 %collective-permute-start.6 = (bf16[208,384]{1,0:T(8,128)(2,1)S(1)}, bf16[208,384]{1,0:T(8,128)(2,1)S(1)}, u32[]{:S(2)}, u32[]{:S(2)}) collective-permute-start(bf16[208,384]{1,0:T(8,128)(2,1)S(1)} %get-tuple-element.107), channel_id=1, source_target_pairs={{0,4},{4,0},{8,12},{12,8},{16,20},{20,16},{24,28},{28,24},{1,5},{5... | collective-permute-start | bytes 479240 | tf_op jit(solution)/shard_map/ppermute | solution.py:537
  25.5 1.0 copy-start
  25.5 1.0 copy-start.1
  30.0 17.6 %collective-permute-start.8 = (bf16[768,384]{1,0:T(8,128)(2,1)S(1)}, bf16[768,384]{1,0:T(8,128)(2,1)S(1)}, u32[]{:S(2)}, u32[]{:S(2)}) collective-permute-start(bf16[768,384]{1,0:T(8,128)(2,1)S(1)} %get-tuple-element.137.refs_0_), channel_id=1, source_target_pairs={{0,1},{1,2},{2,3},{3,0},{4,5},{5,6},{6,7},{7,4},{8,9},{9,10},{10,1... | collective-permute-start | bytes 1769480 | tf_op jit(solution)/shard_map/ppermute | solution.py:544
  32.1 9.1 %collective-permute-start.10 = (bf16[192,640]{1,0:T(8,128)(2,1)S(1)}, bf16[192,640]{1,0:T(8,128)(2,1)S(1)}, u32[]{:S(2)}, u32[]{:S(2)}) collective-permute-start(bf16[192,640]{1,0:T(8,128)(2,1)S(1)} %get-tuple-element.139), channel_id=1, source_target_pairs={{0,28},{4,24},{8,20},{12,16},{16,12},{20,8},{24,4},{28,0},{1,29},{... | collective-permute-start | bytes 737288 | tf_op jit(solution)/shard_map/ppermute | solution.py:537
  33.8 12.6 %collective-permute-start.9 = (bf16[192,640]{1,0:T(8,128)(2,1)S(1)}, bf16[192,640]{1,0:T(8,128)(2,1)S(1)}, u32[]{:S(2)}, u32[]{:S(2)}) collective-permute-start(bf16[192,640]{1,0:T(8,128)(2,1)S(1)} %get-tuple-element.138), channel_id=1, source_target_pairs={{0,24},{4,28},{8,16},{12,20},{16,8},{20,12},{24,0},{28,4},{1,25},{... | collective-permute-start | bytes 737288 | tf_op jit(solution)/shard_map/ppermute | solution.py:537
  47.6 16.5 %collective-permute-start.11 = (bf16[768,384]{1,0:T(8,128)(2,1)S(1)}, bf16[768,384]{1,0:T(8,128)(2,1)S(1)}, u32[]{:S(2)}, u32[]{:S(2)}) collective-permute-start(bf16[768,384]{1,0:T(8,128)(2,1)S(1)} %collective-permute-done.8.refs_0_), channel_id=1, source_target_pairs={{0,1},{1,2},{2,3},{3,0},{4,5},{5,6},{6,7},{7,4},{8,9},{9,10},{10,1... | collective-permute-start | bytes 1769480 | tf_op jit(solution)/shard_map/ppermute | solution.py:544
  48.1 8.9 %collective-permute-start.12 = (bf16[192,640]{1,0:T(8,128)(2,1)S(1)}, bf16[192,640]{1,0:T(8,128)(2,1)S(1)}, u32[]{:S(2)}, u32[]{:S(2)}) collective-permute-start(bf16[192,640]{1,0:T(8,128)(2,1)S(1)} %get-tuple-element.143), channel_id=1, source_target_pairs={{0,16},{4,20},{8,24},{12,28},{16,0},{20,4},{24,8},{28,12},{1,17},{... | collective-permute-start | bytes 737288 | tf_op jit(solution)/shard_map/ppermute | solution.py:537
  49.4 8.9 %collective-permute-start.13 = (bf16[192,640]{1,0:T(8,128)(2,1)S(1)}, bf16[192,640]{1,0:T(8,128)(2,1)S(1)}, u32[]{:S(2)}, u32[]{:S(2)}) collective-permute-start(bf16[192,640]{1,0:T(8,128)(2,1)S(1)} %get-tuple-element.144), channel_id=1, source_target_pairs={{0,8},{4,12},{8,0},{12,4},{16,24},{20,28},{24,16},{28,20},{1,9},{5... | collective-permute-start | bytes 737288 | tf_op jit(solution)/shard_map/ppermute | solution.py:537
  50.9 9.0 %collective-permute-start.14 = (bf16[192,640]{1,0:T(8,128)(2,1)S(1)}, bf16[192,640]{1,0:T(8,128)(2,1)S(1)}, u32[]{:S(2)}, u32[]{:S(2)}) collective-permute-start(bf16[192,640]{1,0:T(8,128)(2,1)S(1)} %get-tuple-element.145), channel_id=1, source_target_pairs={{0,20},{4,16},{8,28},{12,24},{16,4},{20,0},{24,12},{28,8},{1,21},{... | collective-permute-start | bytes 737288 | tf_op jit(solution)/shard_map/ppermute | solution.py:537
  50.9 10.2 %collective-permute-start.15 = (bf16[192,640]{1,0:T(8,128)(2,1)S(1)}, bf16[192,640]{1,0:T(8,128)(2,1)S(1)}, u32[]{:S(2)}, u32[]{:S(2)}) collective-permute-start(bf16[192,640]{1,0:T(8,128)(2,1)S(1)} %get-tuple-element.146), channel_id=1, source_target_pairs={{0,12},{4,8},{8,4},{12,0},{16,28},{20,24},{24,20},{28,16},{1,13},{... | collective-permute-start | bytes 737288 | tf_op jit(solution)/shard_map/ppermute | solution.py:537
  56.9 4.2 %collective-permute-start.16 = (bf16[192,640]{1,0:T(8,128)(2,1)S(1)}, bf16[192,640]{1,0:T(8,128)(2,1)S(1)}, u32[]{:S(2)}, u32[]{:S(2)}) collective-permute-start(bf16[192,640]{1,0:T(8,128)(2,1)S(1)} %get-tuple-element.147), channel_id=1, source_target_pairs={{0,4},{4,0},{8,12},{12,8},{16,20},{20,16},{24,28},{28,24},{1,5},{5... | collective-permute-start | bytes 737288 | tf_op jit(solution)/shard_map/ppermute | solution.py:537
  64.1 35.0 %collective-permute-start.20 = (bf16[720,1024]{1,0:T(8,128)(2,1)S(1)}, bf16[720,1024]{1,0:T(8,128)(2,1)S(1)}, u32[]{:S(2)}, u32[]{:S(2)}) collective-permute-start(bf16[720,1024]{1,0:T(8,128)(2,1)S(1)} %pad_maximum_fusion.refs_0_), channel_id=1, source_target_pairs={{0,8},{4,12},{8,0},{12,4},{16,24},{20,28},{24,16},{28,20},{1,9},{5... | collective-permute-start | bytes 4423688 | tf_op jit(solution)/shard_map/ppermute | solution.py:537
  65.3 35.1 %collective-permute-start.21 = (bf16[720,1024]{1,0:T(8,128)(2,1)S(1)}, bf16[720,1024]{1,0:T(8,128)(2,1)S(1)}, u32[]{:S(2)}, u32[]{:S(2)}) collective-permute-start(bf16[720,1024]{1,0:T(8,128)(2,1)S(1)} %pad_maximum_fusion.refs_0_), channel_id=1, source_target_pairs={{0,16},{4,20},{8,24},{12,28},{16,0},{20,4},{24,8},{28,12},{1,17},{... | collective-permute-start | bytes 4423688 | tf_op jit(solution)/shard_map/ppermute | solution.py:537
  66.9 26.4 %collective-permute-start.18 = (bf16[768,640]{1,0:T(8,128)(2,1)S(1)}, bf16[768,640]{1,0:T(8,128)(2,1)S(1)}, u32[]{:S(2)}, u32[]{:S(2)}) collective-permute-start(bf16[768,640]{1,0:T(8,128)(2,1)S(1)} %shard_map.88.refs_1_), channel_id=1, source_target_pairs={{0,1},{1,2},{2,3},{3,0},{4,5},{5,6},{6,7},{7,4},{8,9},{9,10},{10,1... | collective-permute-start | bytes 2949128 | tf_op jit(solution)/shard_map/ppermute | solution.py:544
  67.3 38.7 %collective-permute-start.17 = (bf16[768,384]{1,0:T(8,128)(2,1)S(1)}, bf16[768,384]{1,0:T(8,128)(2,1)S(1)}, u32[]{:S(2)}, u32[]{:S(2)}) collective-permute-start(bf16[768,384]{1,0:T(8,128)(2,1)S(1)} %collective-permute-done.11.refs_0_), channel_id=1, source_target_pairs={{0,1},{1,2},{2,3},{3,0},{4,5},{5,6},{6,7},{7,4},{8,9},{9,10},{10,1... | collective-permute-start | bytes 1769480 | tf_op jit(solution)/shard_map/ppermute | solution.py:544
  93.3 32.7 %collective-permute-start.19 = (bf16[768,640]{1,0:T(8,128)(2,1)S(1)}, bf16[768,640]{1,0:T(8,128)(2,1)S(1)}, u32[]{:S(2)}, u32[]{:S(2)}) collective-permute-start(bf16[768,640]{1,0:T(8,128)(2,1)S(1)} %collective-permute-done.18.refs_1_), channel_id=1, source_target_pairs={{0,1},{1,2},{2,3},{3,0},{4,5},{5,6},{6,7},{7,4},{8,9},{9,10},{10,1... | collective-permute-start | bytes 2949128 | tf_op jit(solution)/shard_map/ppermute | solution.py:544
  99.2 18.7 %collective-permute-start.22 = (bf16[720,512]{1,0:T(8,128)(2,1)S(1)}, bf16[720,512]{1,0:T(8,128)(2,1)S(1)}, u32[]{:S(2)}, u32[]{:S(2)}) collective-permute-start(bf16[720,512]{1,0:T(8,128)(2,1)S(1)} %slice.8), channel_id=1, source_target_pairs={{0,16},{4,20},{8,24},{12,28},{16,0},{20,4},{24,8},{28,12},{1,17},{... | collective-permute-start | bytes 2211848 | tf_op jit(solution)/shard_map/ppermute | solution.py:537
  100.1 1.6 collective-permute-start.24
  100.5 18.7 %collective-permute-start.23 = (bf16[720,512]{1,0:T(8,128)(2,1)S(1)}, bf16[720,512]{1,0:T(8,128)(2,1)S(1)}, u32[]{:S(2)}, u32[]{:S(2)}) collective-permute-start(bf16[720,512]{1,0:T(8,128)(2,1)S(1)} %slice.9), channel_id=1, source_target_pairs={{0,8},{4,12},{8,0},{12,4},{16,24},{20,28},{24,16},{28,20},{1,9},{5... | collective-permute-start | bytes 2211848 | tf_op jit(solution)/shard_map/ppermute | solution.py:537
  101.7 26.2 %collective-permute-start.32 = (bf16[768,640]{1,0:T(8,128)(2,1)S(1)}, bf16[768,640]{1,0:T(8,128)(2,1)S(1)}, u32[]{:S(2)}, u32[]{:S(2)}) collective-permute-start(bf16[768,640]{1,0:T(8,128)(2,1)S(1)} %shard_map.88.refs_1_), channel_id=1, source_target_pairs={{0,4},{4,0},{8,12},{12,8},{16,20},{20,16},{24,28},{28,24},{1,5},{5... | collective-permute-start | bytes 2949128 | tf_op jit(solution)/shard_map/ppermute | solution.py:537
  105.9 20.6 %collective-permute-start.31 = (bf16[768,384]{1,0:T(8,128)(2,1)S(1)}, bf16[768,384]{1,0:T(8,128)(2,1)S(1)}, u32[]{:S(2)}, u32[]{:S(2)}) collective-permute-start(bf16[768,384]{1,0:T(8,128)(2,1)S(1)} %get-tuple-element.137.refs_0_), channel_id=1, source_target_pairs={{0,4},{4,0},{8,12},{12,8},{16,20},{20,16},{24,28},{28,24},{1,5},{5... | collective-permute-start | bytes 1769480 | tf_op jit(solution)/shard_map/ppermute | solution.py:537
  117.9 10.0 %collective-permute-start.29 = (bf16[768,384]{1,0:T(8,128)(2,1)S(1)}, bf16[768,384]{1,0:T(8,128)(2,1)S(1)}, u32[]{:S(2)}, u32[]{:S(2)}) collective-permute-start(bf16[768,384]{1,0:T(8,128)(2,1)S(1)} %collective-permute-done.8.refs_0_), channel_id=1, source_target_pairs={{0,4},{4,0},{8,12},{12,8},{16,20},{20,16},{24,28},{28,24},{1,5},{5... | collective-permute-start | bytes 1769480 | tf_op jit(solution)/shard_map/ppermute | solution.py:537
  119.2 14.3 %collective-permute-start.30 = (bf16[768,640]{1,0:T(8,128)(2,1)S(1)}, bf16[768,640]{1,0:T(8,128)(2,1)S(1)}, u32[]{:S(2)}, u32[]{:S(2)}) collective-permute-start(bf16[768,640]{1,0:T(8,128)(2,1)S(1)} %collective-permute-done.18.refs_1_), channel_id=1, source_target_pairs={{0,4},{4,0},{8,12},{12,8},{16,20},{20,16},{24,28},{28,24},{1,5},{5... | collective-permute-start | bytes 2949128 | tf_op jit(solution)/shard_map/ppermute | solution.py:537
  126.0 13.0 %collective-permute-start.28 = (bf16[768,640]{1,0:T(8,128)(2,1)S(1)}, bf16[768,640]{1,0:T(8,128)(2,1)S(1)}, u32[]{:S(2)}, u32[]{:S(2)}) collective-permute-start(bf16[768,640]{1,0:T(8,128)(2,1)S(1)} %collective-permute-done.19.refs_1_), channel_id=1, source_target_pairs={{0,4},{4,0},{8,12},{12,8},{16,20},{20,16},{24,28},{28,24},{1,5},{5... | collective-permute-start | bytes 2949128 | tf_op jit(solution)/shard_map/ppermute | solution.py:537
  126.6 25.5 %collective-permute-start.25 = (bf16[768,640]{1,0:T(8,128)(2,1)S(1)}, bf16[768,640]{1,0:T(8,128)(2,1)S(1)}, u32[]{:S(2)}, u32[]{:S(2)}) collective-permute-start(bf16[768,640]{1,0:T(8,128)(2,1)S(1)} %collective-permute-done.19.refs_1_), channel_id=1, source_target_pairs={{0,1},{1,2},{2,3},{3,0},{4,5},{5,6},{6,7},{7,4},{8,9},{9,10},{10,1... | collective-permute-start | bytes 2949128 | tf_op jit(solution)/shard_map/ppermute | solution.py:544
  127.9 11.1 %collective-permute-start.27 = (bf16[768,384]{1,0:T(8,128)(2,1)S(1)}, bf16[768,384]{1,0:T(8,128)(2,1)S(1)}, u32[]{:S(2)}, u32[]{:S(2)}) collective-permute-start(bf16[768,384]{1,0:T(8,128)(2,1)S(1)} %collective-permute-done.11.refs_0_), channel_id=1, source_target_pairs={{0,4},{4,0},{8,12},{12,8},{16,20},{20,16},{24,28},{28,24},{1,5},{5... | collective-permute-start | bytes 1769480 | tf_op jit(solution)/shard_map/ppermute | solution.py:537
  127.9 16.5 %collective-permute-start.26 = (bf16[768,384]{1,0:T(8,128)(2,1)S(1)}, bf16[768,384]{1,0:T(8,128)(2,1)S(1)}, u32[]{:S(2)}, u32[]{:S(2)}) collective-permute-start(bf16[768,384]{1,0:T(8,128)(2,1)S(1)} %collective-permute-done.17.refs_0_), channel_id=1, source_target_pairs={{0,4},{4,0},{8,12},{12,8},{16,20},{20,16},{24,28},{28,24},{1,5},{5... | collective-permute-start | bytes 1769480 | tf_op jit(solution)/shard_map/ppermute | solution.py:537
  152.1 2.6 %collective-permute-start.33 = (bf16[768,640]{1,0:T(8,128)(2,1)S(1)}, bf16[768,640]{1,0:T(8,128)(2,1)S(1)}, u32[]{:S(2)}, u32[]{:S(2)}) collective-permute-start(bf16[768,640]{1,0:T(8,128)(2,1)S(1)} %collective-permute-done.25.refs_1_), channel_id=1, source_target_pairs={{0,4},{4,0},{8,12},{12,8},{16,20},{20,16},{24,28},{28,24},{1,5},{5... | collective-permute-start | bytes 2949128 | tf_op jit(solution)/shard_map/ppermute | solution.py:537
  160.7 1.3 collective-permute-start.34
  162.6 4.8 %collective-permute-start.35 = (f32[8,1536]{1,0:T(8,128)S(1)}, f32[8,1536]{1,0:T(8,128)S(1)}, u32[]{:S(2)}, u32[]{:S(2)}) collective-permute-start(f32[8,1536]{1,0:T(8,128)S(1)} %shard_map.95.refs_2_), channel_id=1, source_target_pairs={{0,1},{1,0},{2,3},{3,2},{4,5},{5,4},{6,7},{7,6},{8,9},{9,8},{10,11... | collective-permute-start | bytes 147464 | tf_op jit(solution)/shard_map/ppermute | solution.py:612
  162.7 7.4 %collective-permute-start.36 = (f32[8,1536]{1,0:T(8,128)S(1)}, f32[8,1536]{1,0:T(8,128)S(1)}, u32[]{:S(2)}, u32[]{:S(2)}) collective-permute-start(f32[8,1536]{1,0:T(8,128)S(1)} %shard_map.95.refs_2_), channel_id=1, source_target_pairs={{0,2},{1,3},{2,0},{3,1},{4,6},{5,7},{6,4},{7,5},{8,10},{9,11},{10,... | collective-permute-start | bytes 147464 | tf_op jit(solution)/shard_map/ppermute | solution.py:612
  163.6 6.5 %collective-permute-start.37 = (f32[8,1536]{1,0:T(8,128)S(1)}, f32[8,1536]{1,0:T(8,128)S(1)}, u32[]{:S(2)}, u32[]{:S(2)}) collective-permute-start(f32[8,1536]{1,0:T(8,128)S(1)} %shard_map.95.refs_2_), channel_id=1, source_target_pairs={{0,3},{1,2},{2,1},{3,0},{4,7},{5,6},{6,5},{7,4},{8,11},{9,10},{10,... | collective-permute-start | bytes 147464 | tf_op jit(solution)/shard_map/ppermute | solution.py:612
  174.3 19.0 %collective-permute-start.38 = (bf16[720,512]{1,0:T(8,128)(2,1)S(1)}, bf16[720,512]{1,0:T(8,128)(2,1)S(1)}, u32[]{:S(2)}, u32[]{:S(2)}) collective-permute-start(bf16[720,512]{1,0:T(8,128)(2,1)S(1)} %get-tuple-element.174), channel_id=1, source_target_pairs={{0,8},{4,12},{8,0},{12,4},{16,24},{20,28},{24,16},{28,20},{1,9},{5... | collective-permute-start | bytes 2211848 | tf_op jit(solution)/shard_map/ppermute | solution.py:537
  175.8 17.5 %collective-permute-start.39 = (bf16[720,512]{1,0:T(8,128)(2,1)S(1)}, bf16[720,512]{1,0:T(8,128)(2,1)S(1)}, u32[]{:S(2)}, u32[]{:S(2)}) collective-permute-start(bf16[720,512]{1,0:T(8,128)(2,1)S(1)} %get-tuple-element.175), channel_id=1, source_target_pairs={{0,16},{4,20},{8,24},{12,28},{16,0},{20,4},{24,8},{28,12},{1,17},{... | collective-permute-start | bytes 2211848 | tf_op jit(solution)/shard_map/ppermute | solution.py:537
  176.6 16.7 %collective-permute-start.40 = (bf16[64,720]{1,0:T(8,128)(2,1)S(1)}, bf16[64,720]{1,0:T(8,128)(2,1)S(1)}, u32[]{:S(2)}, u32[]{:S(2)}) collective-permute-start(bf16[64,720]{1,0:T(8,128)(2,1)S(1)} %get-tuple-element.183.mine_ref), channel_id=1, source_target_pairs={{0,8},{4,12},{8,0},{12,4},{16,24},{20,28},{24,16},{28,20},{1,9},{5... | collective-permute-start | bytes 276488 | tf_op jit(solution)/shard_map/ppermute | solution.py:537
  194.7 21.5 %collective-permute-start.42 = (bf16[720,512]{1,0:T(8,128)(2,1)S(1)}, bf16[720,512]{1,0:T(8,128)(2,1)S(1)}, u32[]{:S(2)}, u32[]{:S(2)}) collective-permute-start(bf16[720,512]{1,0:T(8,128)(2,1)S(1)} %get-tuple-element.200), channel_id=1, source_target_pairs={{0,16},{4,12},{8,24},{12,4},{16,0},{20,28},{24,8},{28,20},{1,17},{... | collective-permute-start | bytes 2211848 | tf_op jit(solution)/shard_map/ppermute | solution.py:541
  195.9 20.3 %collective-permute-start.43 = (bf16[720,512]{1,0:T(8,128)(2,1)S(1)}, bf16[720,512]{1,0:T(8,128)(2,1)S(1)}, u32[]{:S(2)}, u32[]{:S(2)}) collective-permute-start(bf16[720,512]{1,0:T(8,128)(2,1)S(1)} %get-tuple-element.189), channel_id=1, source_target_pairs={{0,8},{4,20},{8,0},{12,28},{16,24},{20,4},{24,16},{28,12},{1,9},{5... | collective-permute-start | bytes 2211848 | tf_op jit(solution)/shard_map/ppermute | solution.py:541
  197.5 18.8 %collective-permute-start.41 = (bf16[64,720]{1,0:T(8,128)(2,1)S(1)}, bf16[64,720]{1,0:T(8,128)(2,1)S(1)}, u32[]{:S(2)}, u32[]{:S(2)}) collective-permute-start(bf16[64,720]{1,0:T(8,128)(2,1)S(1)} %shard_map.98), channel_id=1, source_target_pairs={{0,16},{4,20},{8,24},{12,28},{16,0},{20,4},{24,8},{28,12},{1,17},{... | collective-permute-start | bytes 276488 | tf_op jit(solution)/shard_map/ppermute | solution.py:537
  198.8 25.4 %collective-permute-start.47 = (bf16[720,512]{1,0:T(8,128)(2,1)}, bf16[720,512]{1,0:T(8,128)(2,1)}, u32[]{:S(2)}, u32[]{:S(2)}) collective-permute-start(bf16[720,512]{1,0:T(8,128)(2,1)} %get-tuple-element.199), channel_id=1, source_target_pairs={{0,12},{4,16},{8,4},{12,24},{16,28},{20,0},{24,20},{28,8},{1,13},{... | collective-permute-start | bytes 2211848 | tf_op jit(solution)/shard_map/ppermute | solution.py:541
  198.8 25.4 %collective-permute-start.44 = (bf16[720,512]{1,0:T(8,128)(2,1)}, bf16[720,512]{1,0:T(8,128)(2,1)}, u32[]{:S(2)}, u32[]{:S(2)}) collective-permute-start(bf16[720,512]{1,0:T(8,128)(2,1)} %get-tuple-element.192), channel_id=1, source_target_pairs={{0,4},{4,0},{8,12},{12,8},{16,20},{20,16},{24,28},{28,24},{1,5},{5... | collective-permute-start | bytes 2211848 | tf_op jit(solution)/shard_map/ppermute | solution.py:537
  216.3 11.8 %collective-permute-start.45 = (bf16[720,512]{1,0:T(8,128)(2,1)}, bf16[720,512]{1,0:T(8,128)(2,1)}, u32[]{:S(2)}, u32[]{:S(2)}) collective-permute-start(bf16[720,512]{1,0:T(8,128)(2,1)} %get-tuple-element.193), channel_id=1, source_target_pairs={{0,20},{4,8},{8,28},{12,0},{16,4},{20,24},{24,12},{28,16},{1,21},{... | collective-permute-start | bytes 2211848 | tf_op jit(solution)/shard_map/ppermute | solution.py:541
  216.3 4.4 %collective-permute-start.46 = (f32[64,720]{1,0:T(8,128)S(1)}, f32[64,720]{1,0:T(8,128)S(1)}, u32[]{:S(2)}, u32[]{:S(2)}) collective-permute-start(f32[64,720]{1,0:T(8,128)S(1)} %convert_add_fusion), channel_id=1, source_target_pairs={{0,4},{4,0},{8,12},{12,8},{16,20},{20,16},{24,28},{28,24},{1,5},{5... | collective-permute-start | bytes 552968 | tf_op jit(solution)/shard_map/ppermute | solution.py:537

commit v14 on v13

--- a/solution.py
+++ b/solution.py
@@ -242,32 +242,64 @@
     )(meta, *recv, pick, wide, ctf, inv)
 
 
-def energy_body(bins, count, meta, *refs):
-    pieces, (ctf_ref, inv_ref, panel_ref, extra_ref, total) = refs[:-5], refs[-5:]
+def energy_body(bins, count, last, meta, *refs):
+    if last:
+        pieces, refs = refs[:-6], refs[-6:]
+        ctf_ref, inv_ref, _, _, panel_ref, _ = refs
+    else:
+        pieces, (ctf_ref, inv_ref, panel_ref, _) = refs[:-4], refs[-4:]
     width = panel_ref.shape[1]
     blocks = []
     for piece in pieces:
         for start in range(0, piece.shape[1], width):
             blocks.append((piece, start))
     step = pl.program_id(0)
+    gain = ctf_ref[...] * ctf_ref[...] * inv_ref[...]
+    gain3 = jnp.concatenate(split3(gain), axis=0)
+    return step, blocks, gain3, width
+
+
+def add_energy(panel, gain3):
+    wide = panel.astype(F32)
+    square = wide * wide
+    high = square.astype(BF16)
+    low = (square - high.astype(F32)).astype(BF16)
+    return mm(high, gain3, NT) + mm(low, gain3, NT)
+
+
+def near_energy_body(bins, count, meta, *refs):
+    step, blocks, gain3, width = energy_body(bins, count, False, meta, *refs)
+    panel_ref, total = refs[-2:]
 
     @pl.when(step == 0)
     def _():
         total[...] = jnp.zeros_like(total)
 
-    gain = ctf_ref[...] * ctf_ref[...] * inv_ref[...]
-    gain3 = jnp.concatenate(split3(gain), axis=0)
     for index, (piece, start) in enumerate(blocks):
 
         @pl.when(step == index)
         def _():
             panel = piece[:, start : start + width]
             panel_ref[...] = panel
-            wide = panel.astype(F32)
-            square = wide * wide
-            high = square.astype(BF16)
-            low = (square - high.astype(F32)).astype(BF16)
-            total[...] += mm(high, gain3, NT) + mm(low, gain3, NT)
+            total[...] += add_energy(panel, gain3)
+
+
+def far_energy_body(bins, count, meta, *refs):
+    refs, total = refs[:-1], refs[-1]
+    step, blocks, gain3, width = energy_body(bins, count, True, meta, *refs)
+    before_ref, _, panel_ref, extra_ref = refs[-4:]
+
+    @pl.when(step == 0)
+    def _():
+        total[...] = before_ref[...]
+
+    for index, (piece, start) in enumerate(blocks):
+
+        @pl.when(step == index)
+        def _():
+            panel = piece[:, start : start + width]
+            panel_ref[...] = panel
+            total[...] += add_energy(panel, gain3)
 
     @pl.when(step == count - 1)
     def _():
@@ -275,28 +307,35 @@
         extra_ref[...] = jnp.concatenate(split3(-0.5 * whole), axis=1)
 
 
-def energy(meta, pieces, ctf, inv):
-    rows, width = pieces[-1].shape
+def energy(meta, pieces, ctf, inv, width, first, before=None, panels=None):
+    rows = pieces[0].shape[0]
     count = sum(piece.shape[1] for piece in pieces) // width
     bins, pix = ctf.shape
     wrap = pix // width
+    last = before is not None
+    whole = lambda shape: pl.BlockSpec(shape, lambda j, m: (0, 0))
+    table = lambda height: pl.BlockSpec(
+        (height, width), lambda j, m: (0, lax.rem(m[0] ^ (first + j), wrap))
+    )
+    in_specs = [whole(piece.shape) for piece in pieces] + [table(bins), table(1)]
+    operands = [meta, *pieces, ctf, inv]
+    alias = None
+    if last:
+        in_specs += [whole(before.shape), pl.BlockSpec(memory_space=pl.ANY)]
+        alias = {len(operands) + 1: 0}
+        operands += [before, panels]
+    sums = sds((rows, 3 * bins), BF16 if last else F32)
     return call(
-        functools.partial(energy_body, bins, count),
+        functools.partial(far_energy_body if last else near_energy_body, bins, count),
         (count,),
-        [pl.BlockSpec(piece.shape, lambda j, m: (0, 0)) for piece in pieces]
-        + [
-            pl.BlockSpec((bins, width), lambda j, m: (0, lax.rem(m[0] ^ j, wrap))),
-            pl.BlockSpec((1, width), lambda j, m: (0, lax.rem(m[0] ^ j, wrap))),
-        ],
-        [
-            pl.BlockSpec((rows, width), lambda j, m: (0, m[0] ^ j)),
-            pl.BlockSpec((rows, 3 * bins), lambda j, m: (0, 0)),
-        ],
-        [sds((rows, count * width), BF16), sds((rows, 3 * bins), BF16)],
-        scratch=[pltpu.VMEM((rows, 3 * bins), F32)],
+        in_specs,
+        [pl.BlockSpec((rows, width), lambda j, m: (0, m[0] ^ (first + j))), whole(sums.shape)],
+        [sds((rows, 2 * pix), BF16), sums],
+        scratch=[pltpu.VMEM((rows, 3 * bins), F32)] if last else [],
+        alias=alias,
         flops=2 * 4 * rows * bins * count * width * 3,
         moved=4 * rows * count * width,
-    )(meta, *pieces, ctf, inv)
+    )(*operands)
 
 
 def score_body(parts, used, first, last, meta, *refs):
@@ -567,7 +606,9 @@
     share_a, hot, pick, wide = unpack_first(meta, recv_a, ctf_table, inv, width, chunk_a)
     share_a, send_b = together((share_a, send_b))
     a1, recv_b = onward(share_a), exchange(send_b)
-    a1, recv_b[:2] = together((a1, recv_b[:2]))
+    piece = near.shape[1] // 2
+    panel_full, energies = energy(meta, [near], ctf_table, inv, piece, 0)
+    a1, recv_b[:2], panel_full, energies = together((a1, recv_b[:2], panel_full, energies))
     a2 = onward(a1)
     share_b = unpack_next(meta, pick, wide, recv_b, ctf_table, inv, width, chunk_b)
     a2, share_b, near = together((a2, share_b, near))
@@ -578,7 +619,9 @@
     piece = near.shape[1] // 2
     far_y, far_x = across(by_x[:, :piece], 4), across(by_y[:, piece:], 2)
     b2 = onward(b1)
-    panel_full, extra = energy(meta, [near, by_x, by_y, far_y, far_x], ctf_table, inv)
+    panel_full, extra = energy(
+        meta, [by_x, by_y, far_y, far_x], ctf_table, inv, piece, 2, energies, panel_full
+    )
     a3, b2, panel_full, hots = together((a3, b2, panel_full, hots))
     b3 = onward(b2)
     sib2 = sib2 + [across(b2, 1)]

time: 232 us -> 231 us (level)
    ppermute x6, waiting for transfers between devices: 33.9 us -> 36.7 us  [onward(): lax.ppermute(value, 'rot', [(i, (i + 1) % turns) for i in range(turns)])]
    pallas_call x1 -> x2, Pallas kernels: 6.79 us -> 7.22 us  [energy(): call(functools.partial(far_energy_body if last else near_energy_body, bin...]
  transfers between devices with their start and end apart: 48 -> 48, of which waited for: 26 -> 27; matrix products, arithmetic and copies ran while one was open for 2% -> 2% of each run, Pallas kernels for 24% -> 24%
where the time goes in v14:
time: 231 us; the launch traced here: 230 us
  waiting for transfers between devices  114 us (49%)
  Pallas kernels  70.1 us (30%)
  starting transfers between devices  37.4 us (16%)
  other arithmetic  6.8 us (3%)
    ppermute x35, waiting for transfers between devices, across(): return lax.ppermute(value, 'dom', [(i, i ^ apart) for i in range(dom)])  66.8 us
    ppermute x6, waiting for transfers between devices, onward(): lax.ppermute(value, 'rot', [(i, (i + 1) % turns) for i in range(turns)])  36.7 us
    ppermute x35, starting transfers between devices, across(): return lax.ppermute(value, 'dom', [(i, i ^ apart) for i in range(dom)])  27 us
    pallas_call x5, Pallas kernels, score(): call(functools.partial(score_body, parts, used, first, last), (2 * half,)...  26.4 us
    pallas_call x2, Pallas kernels, class_part(): call(functools.partial(class_body, kind, steps), (steps,), in_specs, out_...  15 us
    pallas_call x2, Pallas kernels, energy(): call(functools.partial(far_energy_body if last else near_energy_body, bin...  7.22 us
    ppermute x4, waiting for transfers between devices, by_core(): return lax.ppermute(value, 'dom', pairs)  6.99 us
    pallas_call x1, Pallas kernels, pack_next(): call(functools.partial(pack_next_body, cap, dom), (1,), [pl.BlockSpec((1,...  5.9 us
  transfers between devices with their start and end apart: 48, of which 27 were waited for; matrix products, arithmetic and copies ran while one was open for 2% of the time, Pallas kernels for 24%

profile of v14, /device:TPU:0, one launch (start us, length us, event | category | flops | bytes accessed | tf_op | source)
XLA Modules:
  0.0 230.5 jit_solution(9323947347225080045)
XLA Ops:
  1.2 0.7 add_select_fusion.slot_ref
  2.0 5.8 %shard_map.85 = (bf16[208,384]{1,0:T(8,128)(2,1)S(1)}, bf16[208,384]{1,0:T(8,128)(2,1)S(1)}, bf16[208,384]{1,0:T(8,128)(2,1)S(1)}, bf16[208,384]{1,0:T(8,128)(2,...) custom-call(s32[10]{0:T(128)S(1)} %stack.43.meta, ...), custom_call_target="tpu_custom_call" | custom-call | flops 113246208 | bytes 147456 | tf_op jit(solution)/shard_map/pallas_call | solution.py:132
  7.7 3.6 %collective-permute-start = (bf16[208,384]{1,0:T(8,128)(2,1)S(1)}, bf16[208,384]{1,0:T(8,128)(2,1)S(1)}, u32[]{:S(2)}, u32[]{:S(2)}) collective-permute-start(bf16[208,384]{1,0:T(8,128)(2,1)S(1)} %get-tuple-element.105), channel_id=1, source_target_pairs={{0,24},{4,28},{8,16},{12,20},{16,8},{20,12},{24,0},{28,4},{1,25},{... | collective-permute-start | bytes 479240 | tf_op jit(solution)/shard_map/ppermute | solution.py:576
  11.4 1.6 collective-permute-start.2
  13.1 1.5 collective-permute-start.3
  14.7 1.2 constant_dynamic-slice_fusion
  16.4 0.6 collective-permute-start.5
  17.0 2.3 %collective-permute-done.1.refs_1_ = bf16[208,384]{1,0:T(8,128)(2,1)S(1)} collective-permute-done((bf16[208,384]{1,0:T(8,128)(2,1)S(1)}, bf16[208,384]{1,0:T(8,128)(2,1)S(1)}, u32[]{:S(2)}, u32[]{:S(2)}) %collective-permute-start.1) | collective-permute-done | bytes 159776 | tf_op jit(solution)/shard_map/ppermute | solution.py:576
  19.6 5.9 %shard_map.86 = (bf16[192,640]{1,0:T(8,128)(2,1)S(1)}, bf16[192,640]{1,0:T(8,128)(2,1)S(1)}, bf16[192,640]{1,0:T(8,128)(2,1)S(1)}, bf16[192,640]{1,0:T(8,128)(2,...) custom-call(s32[10]{0:T(128)S(1)} %stack.43.meta, ...), custom_call_target="tpu_custom_call" | custom-call | flops 188743680 | bytes 245760 | tf_op jit(solution)/shard_map/pallas_call | solution.py:152
  26.5 3.5 %shard_map.87 = (bf16[768,384]{1,0:T(8,128)(2,1)S(1)}, bf16[192,768]{1,0:T(8,128)(2,1)S(1)}, bf16[768,1536]{1,0:T(8,128)(2,1)S(1)}, bf16[768,192]{1,0:T(8,128)(2,1)S(1)}) custom-call(s32[10]{0:T(128)S(1)} %stack.43.meta, bf16[208,384]{1,0:T(8,128)(2,1)S(1)} %collective-permute-done.refs_0_, bf16[208,384]{1,0:T(8,128)(2,1)S(1)} %collective-permute-done.1.refs_1_, ...), custom_call_target="tpu_custom_call" | custom-call | flops 56623104 | bytes 73728 | tf_op jit(solution)/shard_map/pallas_call | solution.py:212
  30.0 2.0 collective-permute-start.8
  32.0 1.8 collective-permute-start.10
  33.8 0.7 collective-permute-start.9
  34.5 2.1 shard_map.88
  36.6 4.5 %collective-permute-done.10.refs_1_ = bf16[192,640]{1,0:T(8,128)(2,1)S(1)} collective-permute-done((bf16[192,640]{1,0:T(8,128)(2,1)S(1)}, bf16[192,640]{1,0:T(8,128)(2,1)S(1)}, u32[]{:S(2)}, u32[]{:S(2)}) %collective-permute-start.10) | collective-permute-done | bytes 245792 | tf_op jit(solution)/shard_map/ppermute | solution.py:576
  41.1 5.4 %collective-permute-done.9.refs_0_ = bf16[192,640]{1,0:T(8,128)(2,1)S(1)} collective-permute-done((bf16[192,640]{1,0:T(8,128)(2,1)S(1)}, bf16[192,640]{1,0:T(8,128)(2,1)S(1)}, u32[]{:S(2)}, u32[]{:S(2)}) %collective-permute-start.9) | collective-permute-done | bytes 245792 | tf_op jit(solution)/shard_map/ppermute | solution.py:576
  46.5 1.1 collective-permute-done.8.refs_0_
  48.1 1.3 collective-permute-start.12
  49.4 1.5 collective-permute-start.13
  50.9 1.0 collective-permute-start.15
  51.8 5.1 %collective-permute-done.12.refs_2_ = bf16[192,640]{1,0:T(8,128)(2,1)S(1)} collective-permute-done((bf16[192,640]{1,0:T(8,128)(2,1)S(1)}, bf16[192,640]{1,0:T(8,128)(2,1)S(1)}, u32[]{:S(2)}, u32[]{:S(2)}) %collective-permute-start.12) | collective-permute-done | bytes 245792 | tf_op jit(solution)/shard_map/ppermute | solution.py:576
  56.9 1.3 collective-permute-done.13.refs_3_
  58.3 1.6 collective-permute-done.14.refs_4_
  59.9 1.2 collective-permute-done.15.refs_5_
  61.1 2.9 %shard_map.89.refs_1_ = bf16[768,640]{1,0:T(8,128)(2,1)S(1)} custom-call(s32[10]{0:T(128)S(1)} %stack.43.meta, bf16[192,640]{1,0:T(8,128)(2,1)S(1)} %collective-permute-done.9.refs_0_, bf16[192,640]{1,0:T(8,128)(2,1)S(1)} %collective-permute-done.10.refs_1_, bf16[192,640]{1,0:T(8,128)(2,1)S(1)} %collective-permute-done.12.refs_2_, ...), custom_call_target="tpu_custom_call" | custom-call | flops 94371840 | bytes 122880 | tf_op jit(solution)/shard_map/pallas_call | solution.py:231
  64.1 1.3 collective-permute-start.20
  65.3 1.5 collective-permute-start.21
  67.8 25.5 %collective-permute-done.18.refs_1_ = bf16[768,640]{1,0:T(8,128)(2,1)S(1)} collective-permute-done((bf16[768,640]{1,0:T(8,128)(2,1)S(1)}, bf16[768,640]{1,0:T(8,128)(2,1)S(1)}, u32[]{:S(2)}, u32[]{:S(2)}) %collective-permute-start.18) | collective-permute-done | bytes 983072 | tf_op jit(solution)/shard_map/ppermute | solution.py:583
  93.3 5.8 %collective-permute-done.20.refs_0_ = bf16[720,1024]{1,0:T(8,128)(2,1)S(1)} collective-permute-done((bf16[720,1024]{1,0:T(8,128)(2,1)S(1)}, bf16[720,1024]{1,0:T(8,128)(2,1)S(1)}, u32[]{:S(2)}, u32[]{:S(2)}) %collective-permute-start.20) | collective-permute-done | bytes 1474592 | tf_op jit(solution)/shard_map/ppermute | solution.py:576
  99.2 0.9 collective-permute-start.22
  100.5 1.2 collective-permute-start.23
  101.9 4.0 %collective-permute-done.17.refs_0_ = bf16[768,384]{1,0:T(8,128)(2,1)S(1)} collective-permute-done((bf16[768,384]{1,0:T(8,128)(2,1)S(1)}, bf16[768,384]{1,0:T(8,128)(2,1)S(1)}, u32[]{:S(2)}, u32[]{:S(2)}) %collective-permute-start.17) | collective-permute-done | bytes 589856 | tf_op jit(solution)/shard_map/ppermute | solution.py:583
  105.9 11.9 %collective-permute-done.22.refs_2_ = bf16[720,512]{1,0:T(8,128)(2,1)S(1)} collective-permute-done((bf16[720,512]{1,0:T(8,128)(2,1)S(1)}, bf16[720,512]{1,0:T(8,128)(2,1)S(1)}, u32[]{:S(2)}, u32[]{:S(2)}) %collective-permute-start.22) | collective-permute-done | bytes 737312 | tf_op jit(solution)/shard_map/ppermute | solution.py:576
  117.9 1.3 collective-permute-done.23.refs_3_
  119.2 5.2 %shard_map.90 = (bf16[720,4096]{1,0:T(8,128)(2,1)S(1)}, bf16[720,192]{1,0:T(8,128)(2,1)S(1)}) custom-call(s32[10]{0:T(128)S(1)} %stack.43.meta, bf16[720,1024]{1,0:T(8,128)(2,1)S(1)} %collective-permute-done.20.refs_0_, bf16[720,1024]{1,0:T(8,128)(2,1)S(1)} %collective-permute-done.21.refs_1_, ...), custom_call_target="tpu_custom_call", output_to_operand_aliasing={{0}: (8, {})} | custom-call | flops 212336640 | bytes 552960 | tf_op jit(solution)/shard_map/pallas_call | solution.py:328
  124.3 1.5 collective-permute-done.19.refs_1_
  126.8 5.1 %shard_map.91 = (f32[720,1536]{1,0:T(8,128)S(1)}, bf16[1536,4096]{1,0:T(8,128)(2,1)S(1)}) custom-call(s32[10]{0:T(128)S(1)} %stack.43.meta, bf16[768,384]{1,0:T(8,128)(2,1)S(1)} %get-tuple-element.141.refs_0_, bf16[768,640]{1,0:T(8,128)(2,1)S(1)} %shard_map.89.refs_1_, bf16[768,384]{1,0:T(8,128)(2,1)S(1)} %collective-permute-done.31.refs_2_, ...), custom_call_target="tpu_custom_call" | custom-call | flops 141557760 | bytes 946176 | tf_op jit(solution)/shard_map/pallas_call | solution.py:428
  131.8 5.4 %shard_map.92 = (f32[720,1536]{1,0:T(8,128)S(1)}, bf16[1536,4096]{1,0:T(8,128)(2,1)S(1)}) custom-call(s32[10]{0:T(128)S(1)} %stack.43.meta, bf16[768,384]{1,0:T(8,128)(2,1)S(1)} %collective-permute-done.8.refs_0_, bf16[768,640]{1,0:T(8,128)(2,1)S(1)} %collective-permute-done.18.refs_1_, ...), custom_call_target="tpu_custom_call", output_to_operand_aliasing={{0}: (6, {}), {1}: (7, {})} | custom-call | flops 141557760 | bytes 946176 | tf_op jit(solution)/shard_map/pallas_call | solution.py:428
  137.3 5.4 %shard_map.93 = (f32[720,1536]{1,0:T(8,128)S(1)}, bf16[1536,4096]{1,0:T(8,128)(2,1)S(1)}) custom-call(s32[10]{0:T(128)S(1)} %stack.43.meta, bf16[768,384]{1,0:T(8,128)(2,1)S(1)} %collective-permute-done.11.refs_0_, bf16[768,640]{1,0:T(8,128)(2,1)S(1)} %collective-permute-done.19.refs_1_, ...), custom_call_target="tpu_custom_call", output_to_operand_aliasing={{0}: (6, {}), {1}: (7, {})} | custom-call | flops 141557760 | bytes 946176 | tf_op jit(solution)/shard_map/pallas_call | solution.py:428
  142.8 4.4 %shard_map.94.refs_5_ = f32[720,1536]{1,0:T(8,128)S(1)} custom-call(s32[10]{0:T(128)S(1)} %stack.43.meta, bf16[768,384]{1,0:T(8,128)(2,1)S(1)} %collective-permute-done.17.refs_0_, bf16[768,384]{1,0:T(8,128)(2,1)S(1)} %collective-permute-done.26.refs_1_.refs_2_, ...), custom_call_target="tpu_custom_call", output_to_operand_aliasing={{}: (4, {})} | custom-call | flops 141557760 | bytes 946176 | tf_op jit(solution)/shard_map/pallas_call | solution.py:428
  147.2 4.6 %collective-permute-done.25.refs_1_ = bf16[768,640]{1,0:T(8,128)(2,1)S(1)} collective-permute-done((bf16[768,640]{1,0:T(8,128)(2,1)S(1)}, bf16[768,640]{1,0:T(8,128)(2,1)S(1)}, u32[]{:S(2)}, u32[]{:S(2)}) %collective-permute-start.25) | collective-permute-done | bytes 983072 | tf_op jit(solution)/shard_map/ppermute | solution.py:583
  151.8 2.6 %collective-permute-done.33.refs_3_ = bf16[768,640]{1,0:T(8,128)(2,1)S(1)} collective-permute-done((bf16[768,640]{1,0:T(8,128)(2,1)S(1)}, bf16[768,640]{1,0:T(8,128)(2,1)S(1)}, u32[]{:S(2)}, u32[]{:S(2)}) %collective-permute-start.33) | collective-permute-done | bytes 983072 | tf_op jit(solution)/shard_map/ppermute | solution.py:576
  154.3 6.0 %shard_map.95 = (f32[720,1536]{1,0:T(8,128)S(1)}, f32[8,1536]{1,0:T(8,128)S(1)}, bf16[1536,4096]{1,0:T(8,128)(2,1)S(1)}) custom-call(s32[10]{0:T(128)S(1)} %stack.43.meta, bf16[768,384]{1,0:T(8,128)(2,1)S(1)} %collective-permute-done.17.refs_0_, bf16[768,640]{1,0:T(8,128)(2,1)S(1)} %collective-permute-done.25.refs_1_, ...), custom_call_target="tpu_custom_call", output_to_operand_aliasing={{0}: (6, {}), {2}: (7, {})} | custom-call | flops 141557760 | bytes 946176 | tf_op jit(solution)/shard_map/pallas_call | solution.py:428
  160.6 1.1 collective-permute-done.34.other_ref
  162.4 4.3 %collective-permute-start.37 = (f32[8,1536]{1,0:T(8,128)S(1)}, f32[8,1536]{1,0:T(8,128)S(1)}, u32[]{:S(2)}, u32[]{:S(2)}) collective-permute-start(f32[8,1536]{1,0:T(8,128)S(1)} %shard_map.96.refs_2_), channel_id=1, source_target_pairs={{0,3},{1,2},{2,1},{3,0},{4,7},{5,6},{6,5},{7,4},{8,11},{9,10},{10,... | collective-permute-start | bytes 147464 | tf_op jit(solution)/shard_map/ppermute | solution.py:655
  167.0 2.7 %collective-permute-done.36.refs_4_ = f32[8,1536]{1,0:T(8,128)S(1)} collective-permute-done((f32[8,1536]{1,0:T(8,128)S(1)}, f32[8,1536]{1,0:T(8,128)S(1)}, u32[]{:S(2)}, u32[]{:S(2)}) %collective-permute-start.36) | collective-permute-done | bytes 49184 | tf_op jit(solution)/shard_map/ppermute | solution.py:655
  169.8 4.2 %shard_map.97 = (bf16[720,512]{1,0:T(8,128)(2,1)S(1)}, bf16[720,512]{1,0:T(8,128)(2,1)S(1)}, bf16[720,1536]{1,0:T(8,128)(2,1)S(1)}, f32[1,768]{1,0:T(1,128)S(1)}, bf16[64,720]{1,0:T(8,128)(2,1)S(1)}) custom-call(s32[10]{0:T(128)S(1)} %stack.43.meta, f32[720,1536]{1,0:T(8,128)S(1)} %get-tuple-element.179.refs_0_, ...), custom_call_target="tpu_custom_call" | custom-call | flops 141557760 | bytes 657408 | tf_op jit(solution)/shard_map/pallas_call | solution.py:516
  174.0 0.7 collective-permute-start.38
  174.7 1.4 collective-permute-start.39
  176.1 1.5 collective-permute-start.40
  177.6 10.7 %shard_map.98 = (bf16[720,512]{1,0:T(8,128)(2,1)S(1)}, bf16[720,512]{1,0:T(8,128)(2,1)}, bf16[720,512]{1,0:T(8,128)(2,1)}, f32[720,512]{1,0:T(8,128)S(1)}, f32[7...) custom-call(s32[10]{0:T(128)S(1)} %stack.43.meta, bf16[720,1536]{1,0:T(8,128)(2,1)S(1)} %get-tuple-element.184.refs_0_, ...), custom_call_target="tpu_custom_call" | custom-call | flops 424673280 | bytes 1419264 | tf_op jit(solution)/shard_map/pallas_call | solution.py:516
  188.4 4.6 %collective-permute-done.40.other_ref = bf16[64,720]{1,0:T(8,128)(2,1)S(1)} collective-permute-done((bf16[64,720]{1,0:T(8,128)(2,1)S(1)}, bf16[64,720]{1,0:T(8,128)(2,1)S(1)}, u32[]{:S(2)}, u32[]{:S(2)}) %collective-permute-start.40) | collective-permute-done | bytes 92192 | tf_op jit(solution)/shard_map/ppermute | solution.py:576
  193.0 1.4 fusion.3
  194.4 1.5 collective-permute-start.42
  197.0 0.7 collective-permute-start.41
  197.7 1.5 collective-permute-start.44
  199.2 16.7 %collective-permute-done.41 = bf16[64,720]{1,0:T(8,128)(2,1)S(1)} collective-permute-done((bf16[64,720]{1,0:T(8,128)(2,1)S(1)}, bf16[64,720]{1,0:T(8,128)(2,1)S(1)}, u32[]{:S(2)}, u32[]{:S(2)}) %collective-permute-start.41) | collective-permute-done | bytes 92192 | tf_op jit(solution)/shard_map/ppermute | solution.py:576
  215.9 0.8 collective-permute-start.46
  216.8 0.6 reduce
  217.4 2.3 shard_map.100
  219.6 0.9 maximum_select_fusion
  220.6 1.5 collective-permute-done.47
  222.0 5.5 %collective-permute-done.45 = bf16[720,512]{1,0:T(8,128)(2,1)} collective-permute-done((bf16[720,512]{1,0:T(8,128)(2,1)}, bf16[720,512]{1,0:T(8,128)(2,1)}, u32[]{:S(2)}, u32[]{:S(2)}) %collective-permute-start.45) | collective-permute-done | bytes 737312 | tf_op jit(solution)/shard_map/ppermute | solution.py:580
  227.5 2.9 %add_dynamic-update-slice_fusion = f32[1440,512]{1,0:T(8,128)} fusion(f32[1440,512]{1,0:T(8,128)} %shard_map.100, s32[]{:T(128)S(6)} %select_n.67, bf16[720,512]{1,0:T(8,128)(2,1)} %collective-permute-done.47, bf16[720,512]{1,0:T(8,128)(2,1)} %collective-permute-done.45, bf16[720,512]{1,0:T(8,128)(2,1)} %collective-permute-done.44), kind=kLoop, calls=%fused_computation.7 | loop fusion | flops 1843200 | bytes 3686404 | tf_op jit(solution)/shard_map/dynamic_update_slice | solution.py:684
  (66 shorter events, 8.1 us)
Async XLA Ops:
  0.6 14.0 %collective-permute-start.7 = (bf16[1440,512]{1,0:T(8,128)(2,1)}, bf16[1440,512]{1,0:T(8,128)(2,1)}, u32[]{:S(2)}, u32[]{:S(2)}) collective-permute-start(bf16[1440,512]{1,0:T(8,128)(2,1)} %param.11), channel_id=1, source_target_pairs={{0,4},{4,0},{8,12},{12,8},{16,20},{20,16},{24,28},{28,24},{1,5},{5... | collective-permute-start | bytes 4423688 | tf_op jit(solution)/shard_map/ppermute | solution.py:576
  2.0 12.6 %copy-start.2 = (bf16[1440,512]{1,0:T(8,128)(2,1)S(1)}, bf16[1440,512]{1,0:T(8,128)(2,1)}, u32[]{:S(2)}) copy-start(bf16[1440,512]{1,0:T(8,128)(2,1)} %param.11) | copy-start | bytes 4423684
  7.7 8.6 %collective-permute-start = (bf16[208,384]{1,0:T(8,128)(2,1)S(1)}, bf16[208,384]{1,0:T(8,128)(2,1)S(1)}, u32[]{:S(2)}, u32[]{:S(2)}) collective-permute-start(bf16[208,384]{1,0:T(8,128)(2,1)S(1)} %get-tuple-element.105), channel_id=1, source_target_pairs={{0,24},{4,28},{8,16},{12,20},{16,8},{20,12},{24,0},{28,4},{1,25},{... | collective-permute-start | bytes 479240 | tf_op jit(solution)/shard_map/ppermute | solution.py:576
  11.3 8.0 %collective-permute-start.1 = (bf16[208,384]{1,0:T(8,128)(2,1)S(1)}, bf16[208,384]{1,0:T(8,128)(2,1)S(1)}, u32[]{:S(2)}, u32[]{:S(2)}) collective-permute-start(bf16[208,384]{1,0:T(8,128)(2,1)S(1)} %get-tuple-element.106), channel_id=1, source_target_pairs={{0,28},{4,24},{8,20},{12,16},{16,12},{20,8},{24,4},{28,0},{1,29},{... | collective-permute-start | bytes 479240 | tf_op jit(solution)/shard_map/ppermute | solution.py:576
  11.4 14.2 %collective-permute-start.2 = (bf16[208,384]{1,0:T(8,128)(2,1)S(1)}, bf16[208,384]{1,0:T(8,128)(2,1)S(1)}, u32[]{:S(2)}, u32[]{:S(2)}) collective-permute-start(bf16[208,384]{1,0:T(8,128)(2,1)S(1)} %get-tuple-element.107), channel_id=1, source_target_pairs={{0,16},{4,20},{8,24},{12,28},{16,0},{20,4},{24,8},{28,12},{1,17},{... | collective-permute-start | bytes 479240 | tf_op jit(solution)/shard_map/ppermute | solution.py:576
  13.1 12.6 %collective-permute-start.3 = (bf16[208,384]{1,0:T(8,128)(2,1)S(1)}, bf16[208,384]{1,0:T(8,128)(2,1)S(1)}, u32[]{:S(2)}, u32[]{:S(2)}) collective-permute-start(bf16[208,384]{1,0:T(8,128)(2,1)S(1)} %get-tuple-element.108), channel_id=1, source_target_pairs={{0,8},{4,12},{8,0},{12,4},{16,24},{20,28},{24,16},{28,20},{1,9},{5... | collective-permute-start | bytes 479240 | tf_op jit(solution)/shard_map/ppermute | solution.py:576
  14.6 11.6 %collective-permute-start.4 = (bf16[208,384]{1,0:T(8,128)(2,1)S(1)}, bf16[208,384]{1,0:T(8,128)(2,1)S(1)}, u32[]{:S(2)}, u32[]{:S(2)}) collective-permute-start(bf16[208,384]{1,0:T(8,128)(2,1)S(1)} %get-tuple-element.109), channel_id=1, source_target_pairs={{0,20},{4,16},{8,28},{12,24},{16,4},{20,0},{24,12},{28,8},{1,21},{... | collective-permute-start | bytes 479240 | tf_op jit(solution)/shard_map/ppermute | solution.py:576
  16.4 9.9 %collective-permute-start.5 = (bf16[208,384]{1,0:T(8,128)(2,1)S(1)}, bf16[208,384]{1,0:T(8,128)(2,1)S(1)}, u32[]{:S(2)}, u32[]{:S(2)}) collective-permute-start(bf16[208,384]{1,0:T(8,128)(2,1)S(1)} %get-tuple-element.110), channel_id=1, source_target_pairs={{0,12},{4,8},{8,4},{12,0},{16,28},{20,24},{24,20},{28,16},{1,13},{... | collective-permute-start | bytes 479240 | tf_op jit(solution)/shard_map/ppermute | solution.py:576
  19.3 6.9 %collective-permute-start.6 = (bf16[208,384]{1,0:T(8,128)(2,1)S(1)}, bf16[208,384]{1,0:T(8,128)(2,1)S(1)}, u32[]{:S(2)}, u32[]{:S(2)}) collective-permute-start(bf16[208,384]{1,0:T(8,128)(2,1)S(1)} %get-tuple-element.111), channel_id=1, source_target_pairs={{0,4},{4,0},{8,12},{12,8},{16,20},{20,16},{24,28},{28,24},{1,5},{5... | collective-permute-start | bytes 479240 | tf_op jit(solution)/shard_map/ppermute | solution.py:576
  25.5 1.0 copy-start
  25.5 1.0 copy-start.1
  30.0 17.6 %collective-permute-start.8 = (bf16[768,384]{1,0:T(8,128)(2,1)S(1)}, bf16[768,384]{1,0:T(8,128)(2,1)S(1)}, u32[]{:S(2)}, u32[]{:S(2)}) collective-permute-start(bf16[768,384]{1,0:T(8,128)(2,1)S(1)} %get-tuple-element.141.refs_0_), channel_id=1, source_target_pairs={{0,1},{1,2},{2,3},{3,0},{4,5},{5,6},{6,7},{7,4},{8,9},{9,10},{10,1... | collective-permute-start | bytes 1769480 | tf_op jit(solution)/shard_map/ppermute | solution.py:583
  32.0 9.1 %collective-permute-start.10 = (bf16[192,640]{1,0:T(8,128)(2,1)S(1)}, bf16[192,640]{1,0:T(8,128)(2,1)S(1)}, u32[]{:S(2)}, u32[]{:S(2)}) collective-permute-start(bf16[192,640]{1,0:T(8,128)(2,1)S(1)} %get-tuple-element.143), channel_id=1, source_target_pairs={{0,28},{4,24},{8,20},{12,16},{16,12},{20,8},{24,4},{28,0},{1,29},{... | collective-permute-start | bytes 737288 | tf_op jit(solution)/shard_map/ppermute | solution.py:576
  33.8 12.6 %collective-permute-start.9 = (bf16[192,640]{1,0:T(8,128)(2,1)S(1)}, bf16[192,640]{1,0:T(8,128)(2,1)S(1)}, u32[]{:S(2)}, u32[]{:S(2)}) collective-permute-start(bf16[192,640]{1,0:T(8,128)(2,1)S(1)} %get-tuple-element.142), channel_id=1, source_target_pairs={{0,24},{4,28},{8,16},{12,20},{16,8},{20,12},{24,0},{28,4},{1,25},{... | collective-permute-start | bytes 737288 | tf_op jit(solution)/shard_map/ppermute | solution.py:576
  47.6 16.5 %collective-permute-start.11 = (bf16[768,384]{1,0:T(8,128)(2,1)S(1)}, bf16[768,384]{1,0:T(8,128)(2,1)S(1)}, u32[]{:S(2)}, u32[]{:S(2)}) collective-permute-start(bf16[768,384]{1,0:T(8,128)(2,1)S(1)} %collective-permute-done.8.refs_0_), channel_id=1, source_target_pairs={{0,1},{1,2},{2,3},{3,0},{4,5},{5,6},{6,7},{7,4},{8,9},{9,10},{10,1... | collective-permute-start | bytes 1769480 | tf_op jit(solution)/shard_map/ppermute | solution.py:583
  48.1 8.9 %collective-permute-start.12 = (bf16[192,640]{1,0:T(8,128)(2,1)S(1)}, bf16[192,640]{1,0:T(8,128)(2,1)S(1)}, u32[]{:S(2)}, u32[]{:S(2)}) collective-permute-start(bf16[192,640]{1,0:T(8,128)(2,1)S(1)} %get-tuple-element.150), channel_id=1, source_target_pairs={{0,16},{4,20},{8,24},{12,28},{16,0},{20,4},{24,8},{28,12},{1,17},{... | collective-permute-start | bytes 737288 | tf_op jit(solution)/shard_map/ppermute | solution.py:576
  49.4 8.9 %collective-permute-start.13 = (bf16[192,640]{1,0:T(8,128)(2,1)S(1)}, bf16[192,640]{1,0:T(8,128)(2,1)S(1)}, u32[]{:S(2)}, u32[]{:S(2)}) collective-permute-start(bf16[192,640]{1,0:T(8,128)(2,1)S(1)} %get-tuple-element.151), channel_id=1, source_target_pairs={{0,8},{4,12},{8,0},{12,4},{16,24},{20,28},{24,16},{28,20},{1,9},{5... | collective-permute-start | bytes 737288 | tf_op jit(solution)/shard_map/ppermute | solution.py:576
  50.9 9.0 %collective-permute-start.14 = (bf16[192,640]{1,0:T(8,128)(2,1)S(1)}, bf16[192,640]{1,0:T(8,128)(2,1)S(1)}, u32[]{:S(2)}, u32[]{:S(2)}) collective-permute-start(bf16[192,640]{1,0:T(8,128)(2,1)S(1)} %get-tuple-element.152), channel_id=1, source_target_pairs={{0,20},{4,16},{8,28},{12,24},{16,4},{20,0},{24,12},{28,8},{1,21},{... | collective-permute-start | bytes 737288 | tf_op jit(solution)/shard_map/ppermute | solution.py:576
  50.9 10.2 %collective-permute-start.15 = (bf16[192,640]{1,0:T(8,128)(2,1)S(1)}, bf16[192,640]{1,0:T(8,128)(2,1)S(1)}, u32[]{:S(2)}, u32[]{:S(2)}) collective-permute-start(bf16[192,640]{1,0:T(8,128)(2,1)S(1)} %get-tuple-element.153), channel_id=1, source_target_pairs={{0,12},{4,8},{8,4},{12,0},{16,28},{20,24},{24,20},{28,16},{1,13},{... | collective-permute-start | bytes 737288 | tf_op jit(solution)/shard_map/ppermute | solution.py:576
  56.9 4.2 %collective-permute-start.16 = (bf16[192,640]{1,0:T(8,128)(2,1)S(1)}, bf16[192,640]{1,0:T(8,128)(2,1)S(1)}, u32[]{:S(2)}, u32[]{:S(2)}) collective-permute-start(bf16[192,640]{1,0:T(8,128)(2,1)S(1)} %get-tuple-element.154), channel_id=1, source_target_pairs={{0,4},{4,0},{8,12},{12,8},{16,20},{20,16},{24,28},{28,24},{1,5},{5... | collective-permute-start | bytes 737288 | tf_op jit(solution)/shard_map/ppermute | solution.py:576
  64.1 35.0 %collective-permute-start.20 = (bf16[720,1024]{1,0:T(8,128)(2,1)S(1)}, bf16[720,1024]{1,0:T(8,128)(2,1)S(1)}, u32[]{:S(2)}, u32[]{:S(2)}) collective-permute-start(bf16[720,1024]{1,0:T(8,128)(2,1)S(1)} %pad_maximum_fusion.refs_0_), channel_id=1, source_target_pairs={{0,8},{4,12},{8,0},{12,4},{16,24},{20,28},{24,16},{28,20},{1,9},{5... | collective-permute-start | bytes 4423688 | tf_op jit(solution)/shard_map/ppermute | solution.py:576
  65.3 35.1 %collective-permute-start.21 = (bf16[720,1024]{1,0:T(8,128)(2,1)S(1)}, bf16[720,1024]{1,0:T(8,128)(2,1)S(1)}, u32[]{:S(2)}, u32[]{:S(2)}) collective-permute-start(bf16[720,1024]{1,0:T(8,128)(2,1)S(1)} %pad_maximum_fusion.refs_0_), channel_id=1, source_target_pairs={{0,16},{4,20},{8,24},{12,28},{16,0},{20,4},{24,8},{28,12},{1,17},{... | collective-permute-start | bytes 4423688 | tf_op jit(solution)/shard_map/ppermute | solution.py:576
  66.8 26.4 %collective-permute-start.18 = (bf16[768,640]{1,0:T(8,128)(2,1)S(1)}, bf16[768,640]{1,0:T(8,128)(2,1)S(1)}, u32[]{:S(2)}, u32[]{:S(2)}) collective-permute-start(bf16[768,640]{1,0:T(8,128)(2,1)S(1)} %shard_map.89.refs_1_), channel_id=1, source_target_pairs={{0,1},{1,2},{2,3},{3,0},{4,5},{5,6},{6,7},{7,4},{8,9},{9,10},{10,1... | collective-permute-start | bytes 2949128 | tf_op jit(solution)/shard_map/ppermute | solution.py:583
  67.3 38.7 %collective-permute-start.17 = (bf16[768,384]{1,0:T(8,128)(2,1)S(1)}, bf16[768,384]{1,0:T(8,128)(2,1)S(1)}, u32[]{:S(2)}, u32[]{:S(2)}) collective-permute-start(bf16[768,384]{1,0:T(8,128)(2,1)S(1)} %collective-permute-done.11.refs_0_), channel_id=1, source_target_pairs={{0,1},{1,2},{2,3},{3,0},{4,5},{5,6},{6,7},{7,4},{8,9},{9,10},{10,1... | collective-permute-start | bytes 1769480 | tf_op jit(solution)/shard_map/ppermute | solution.py:583
  93.3 32.5 %collective-permute-start.19 = (bf16[768,640]{1,0:T(8,128)(2,1)S(1)}, bf16[768,640]{1,0:T(8,128)(2,1)S(1)}, u32[]{:S(2)}, u32[]{:S(2)}) collective-permute-start(bf16[768,640]{1,0:T(8,128)(2,1)S(1)} %collective-permute-done.18.refs_1_), channel_id=1, source_target_pairs={{0,1},{1,2},{2,3},{3,0},{4,5},{5,6},{6,7},{7,4},{8,9},{9,10},{10,1... | collective-permute-start | bytes 2949128 | tf_op jit(solution)/shard_map/ppermute | solution.py:583
  99.2 18.7 %collective-permute-start.22 = (bf16[720,512]{1,0:T(8,128)(2,1)S(1)}, bf16[720,512]{1,0:T(8,128)(2,1)S(1)}, u32[]{:S(2)}, u32[]{:S(2)}) collective-permute-start(bf16[720,512]{1,0:T(8,128)(2,1)S(1)} %slice.8), channel_id=1, source_target_pairs={{0,16},{4,20},{8,24},{12,28},{16,0},{20,4},{24,8},{28,12},{1,17},{... | collective-permute-start | bytes 2211848 | tf_op jit(solution)/shard_map/ppermute | solution.py:576
  100.1 1.6 collective-permute-start.24
  100.5 18.7 %collective-permute-start.23 = (bf16[720,512]{1,0:T(8,128)(2,1)S(1)}, bf16[720,512]{1,0:T(8,128)(2,1)S(1)}, u32[]{:S(2)}, u32[]{:S(2)}) collective-permute-start(bf16[720,512]{1,0:T(8,128)(2,1)S(1)} %slice.9), channel_id=1, source_target_pairs={{0,8},{4,12},{8,0},{12,4},{16,24},{20,28},{24,16},{28,20},{1,9},{5... | collective-permute-start | bytes 2211848 | tf_op jit(solution)/shard_map/ppermute | solution.py:576
  101.7 24.7 %collective-permute-start.32 = (bf16[768,640]{1,0:T(8,128)(2,1)S(1)}, bf16[768,640]{1,0:T(8,128)(2,1)S(1)}, u32[]{:S(2)}, u32[]{:S(2)}) collective-permute-start(bf16[768,640]{1,0:T(8,128)(2,1)S(1)} %shard_map.89.refs_1_), channel_id=1, source_target_pairs={{0,4},{4,0},{8,12},{12,8},{16,20},{20,16},{24,28},{28,24},{1,5},{5... | collective-permute-start | bytes 2949128 | tf_op jit(solution)/shard_map/ppermute | solution.py:576
  105.9 19.9 %collective-permute-start.31 = (bf16[768,384]{1,0:T(8,128)(2,1)S(1)}, bf16[768,384]{1,0:T(8,128)(2,1)S(1)}, u32[]{:S(2)}, u32[]{:S(2)}) collective-permute-start(bf16[768,384]{1,0:T(8,128)(2,1)S(1)} %get-tuple-element.141.refs_0_), channel_id=1, source_target_pairs={{0,4},{4,0},{8,12},{12,8},{16,20},{20,16},{24,28},{28,24},{1,5},{5... | collective-permute-start | bytes 1769480 | tf_op jit(solution)/shard_map/ppermute | solution.py:576
  117.9 8.3 %collective-permute-start.29 = (bf16[768,384]{1,0:T(8,128)(2,1)S(1)}, bf16[768,384]{1,0:T(8,128)(2,1)S(1)}, u32[]{:S(2)}, u32[]{:S(2)}) collective-permute-start(bf16[768,384]{1,0:T(8,128)(2,1)S(1)} %collective-permute-done.8.refs_0_), channel_id=1, source_target_pairs={{0,4},{4,0},{8,12},{12,8},{16,20},{20,16},{24,28},{28,24},{1,5},{5... | collective-permute-start | bytes 1769480 | tf_op jit(solution)/shard_map/ppermute | solution.py:576
  119.2 12.7 %collective-permute-start.30 = (bf16[768,640]{1,0:T(8,128)(2,1)S(1)}, bf16[768,640]{1,0:T(8,128)(2,1)S(1)}, u32[]{:S(2)}, u32[]{:S(2)}) collective-permute-start(bf16[768,640]{1,0:T(8,128)(2,1)S(1)} %collective-permute-done.18.refs_1_), channel_id=1, source_target_pairs={{0,4},{4,0},{8,12},{12,8},{16,20},{20,16},{24,28},{28,24},{1,5},{5... | collective-permute-start | bytes 2949128 | tf_op jit(solution)/shard_map/ppermute | solution.py:576
  125.8 11.5 %collective-permute-start.28 = (bf16[768,640]{1,0:T(8,128)(2,1)S(1)}, bf16[768,640]{1,0:T(8,128)(2,1)S(1)}, u32[]{:S(2)}, u32[]{:S(2)}) collective-permute-start(bf16[768,640]{1,0:T(8,128)(2,1)S(1)} %collective-permute-done.19.refs_1_), channel_id=1, source_target_pairs={{0,4},{4,0},{8,12},{12,8},{16,20},{20,16},{24,28},{28,24},{1,5},{5... | collective-permute-start | bytes 2949128 | tf_op jit(solution)/shard_map/ppermute | solution.py:576
  125.8 26.0 %collective-permute-start.25 = (bf16[768,640]{1,0:T(8,128)(2,1)S(1)}, bf16[768,640]{1,0:T(8,128)(2,1)S(1)}, u32[]{:S(2)}, u32[]{:S(2)}) collective-permute-start(bf16[768,640]{1,0:T(8,128)(2,1)S(1)} %collective-permute-done.19.refs_1_), channel_id=1, source_target_pairs={{0,1},{1,2},{2,3},{3,0},{4,5},{5,6},{6,7},{7,4},{8,9},{9,10},{10,1... | collective-permute-start | bytes 2949128 | tf_op jit(solution)/shard_map/ppermute | solution.py:583
  126.2 11.1 %collective-permute-start.27 = (bf16[768,384]{1,0:T(8,128)(2,1)S(1)}, bf16[768,384]{1,0:T(8,128)(2,1)S(1)}, u32[]{:S(2)}, u32[]{:S(2)}) collective-permute-start(bf16[768,384]{1,0:T(8,128)(2,1)S(1)} %collective-permute-done.11.refs_0_), channel_id=1, source_target_pairs={{0,4},{4,0},{8,12},{12,8},{16,20},{20,16},{24,28},{28,24},{1,5},{5... | collective-permute-start | bytes 1769480 | tf_op jit(solution)/shard_map/ppermute | solution.py:576
  126.4 16.4 %collective-permute-start.26 = (bf16[768,384]{1,0:T(8,128)(2,1)S(1)}, bf16[768,384]{1,0:T(8,128)(2,1)S(1)}, u32[]{:S(2)}, u32[]{:S(2)}) collective-permute-start(bf16[768,384]{1,0:T(8,128)(2,1)S(1)} %collective-permute-done.17.refs_0_), channel_id=1, source_target_pairs={{0,4},{4,0},{8,12},{12,8},{16,20},{20,16},{24,28},{28,24},{1,5},{5... | collective-permute-start | bytes 1769480 | tf_op jit(solution)/shard_map/ppermute | solution.py:576
  151.8 2.6 %collective-permute-start.33 = (bf16[768,640]{1,0:T(8,128)(2,1)S(1)}, bf16[768,640]{1,0:T(8,128)(2,1)S(1)}, u32[]{:S(2)}, u32[]{:S(2)}) collective-permute-start(bf16[768,640]{1,0:T(8,128)(2,1)S(1)} %collective-permute-done.25.refs_1_), channel_id=1, source_target_pairs={{0,4},{4,0},{8,12},{12,8},{16,20},{20,16},{24,28},{28,24},{1,5},{5... | collective-permute-start | bytes 2949128 | tf_op jit(solution)/shard_map/ppermute | solution.py:576
  160.4 1.3 collective-permute-start.34
  162.3 4.8 %collective-permute-start.35 = (f32[8,1536]{1,0:T(8,128)S(1)}, f32[8,1536]{1,0:T(8,128)S(1)}, u32[]{:S(2)}, u32[]{:S(2)}) collective-permute-start(f32[8,1536]{1,0:T(8,128)S(1)} %shard_map.96.refs_2_), channel_id=1, source_target_pairs={{0,1},{1,0},{2,3},{3,2},{4,5},{5,4},{6,7},{7,6},{8,9},{9,8},{10,11... | collective-permute-start | bytes 147464 | tf_op jit(solution)/shard_map/ppermute | solution.py:655
  162.3 7.4 %collective-permute-start.36 = (f32[8,1536]{1,0:T(8,128)S(1)}, f32[8,1536]{1,0:T(8,128)S(1)}, u32[]{:S(2)}, u32[]{:S(2)}) collective-permute-start(f32[8,1536]{1,0:T(8,128)S(1)} %shard_map.96.refs_2_), channel_id=1, source_target_pairs={{0,2},{1,3},{2,0},{3,1},{4,6},{5,7},{6,4},{7,5},{8,10},{9,11},{10,... | collective-permute-start | bytes 147464 | tf_op jit(solution)/shard_map/ppermute | solution.py:655
  162.4 7.3 %collective-permute-start.37 = (f32[8,1536]{1,0:T(8,128)S(1)}, f32[8,1536]{1,0:T(8,128)S(1)}, u32[]{:S(2)}, u32[]{:S(2)}) collective-permute-start(f32[8,1536]{1,0:T(8,128)S(1)} %shard_map.96.refs_2_), channel_id=1, source_target_pairs={{0,3},{1,2},{2,1},{3,0},{4,7},{5,6},{6,5},{7,4},{8,11},{9,10},{10,... | collective-permute-start | bytes 147464 | tf_op jit(solution)/shard_map/ppermute | solution.py:655
  174.0 19.0 %collective-permute-start.38 = (bf16[720,512]{1,0:T(8,128)(2,1)S(1)}, bf16[720,512]{1,0:T(8,128)(2,1)S(1)}, u32[]{:S(2)}, u32[]{:S(2)}) collective-permute-start(bf16[720,512]{1,0:T(8,128)(2,1)S(1)} %get-tuple-element.182), channel_id=1, source_target_pairs={{0,8},{4,12},{8,0},{12,4},{16,24},{20,28},{24,16},{28,20},{1,9},{5... | collective-permute-start | bytes 2211848 | tf_op jit(solution)/shard_map/ppermute | solution.py:576
  174.7 18.3 %collective-permute-start.39 = (bf16[720,512]{1,0:T(8,128)(2,1)S(1)}, bf16[720,512]{1,0:T(8,128)(2,1)S(1)}, u32[]{:S(2)}, u32[]{:S(2)}) collective-permute-start(bf16[720,512]{1,0:T(8,128)(2,1)S(1)} %get-tuple-element.183), channel_id=1, source_target_pairs={{0,16},{4,20},{8,24},{12,28},{16,0},{20,4},{24,8},{28,12},{1,17},{... | collective-permute-start | bytes 2211848 | tf_op jit(solution)/shard_map/ppermute | solution.py:576
  176.1 16.8 %collective-permute-start.40 = (bf16[64,720]{1,0:T(8,128)(2,1)S(1)}, bf16[64,720]{1,0:T(8,128)(2,1)S(1)}, u32[]{:S(2)}, u32[]{:S(2)}) collective-permute-start(bf16[64,720]{1,0:T(8,128)(2,1)S(1)} %get-tuple-element.191.mine_ref), channel_id=1, source_target_pairs={{0,8},{4,12},{8,0},{12,4},{16,24},{20,28},{24,16},{28,20},{1,9},{5... | collective-permute-start | bytes 276488 | tf_op jit(solution)/shard_map/ppermute | solution.py:576
  194.4 21.5 %collective-permute-start.42 = (bf16[720,512]{1,0:T(8,128)(2,1)S(1)}, bf16[720,512]{1,0:T(8,128)(2,1)S(1)}, u32[]{:S(2)}, u32[]{:S(2)}) collective-permute-start(bf16[720,512]{1,0:T(8,128)(2,1)S(1)} %get-tuple-element.208), channel_id=1, source_target_pairs={{0,16},{4,12},{8,24},{12,4},{16,0},{20,28},{24,8},{28,20},{1,17},{... | collective-permute-start | bytes 2211848 | tf_op jit(solution)/shard_map/ppermute | solution.py:580
  195.9 20.0 %collective-permute-start.43 = (bf16[720,512]{1,0:T(8,128)(2,1)S(1)}, bf16[720,512]{1,0:T(8,128)(2,1)S(1)}, u32[]{:S(2)}, u32[]{:S(2)}) collective-permute-start(bf16[720,512]{1,0:T(8,128)(2,1)S(1)} %get-tuple-element.197), channel_id=1, source_target_pairs={{0,8},{4,20},{8,0},{12,28},{16,24},{20,4},{24,16},{28,12},{1,9},{5... | collective-permute-start | bytes 2211848 | tf_op jit(solution)/shard_map/ppermute | solution.py:580
  197.0 18.9 %collective-permute-start.41 = (bf16[64,720]{1,0:T(8,128)(2,1)S(1)}, bf16[64,720]{1,0:T(8,128)(2,1)S(1)}, u32[]{:S(2)}, u32[]{:S(2)}) collective-permute-start(bf16[64,720]{1,0:T(8,128)(2,1)S(1)} %shard_map.99), channel_id=1, source_target_pairs={{0,16},{4,20},{8,24},{12,28},{16,0},{20,4},{24,8},{28,12},{1,17},{... | collective-permute-start | bytes 276488 | tf_op jit(solution)/shard_map/ppermute | solution.py:576
  197.7 24.4 %collective-permute-start.47 = (bf16[720,512]{1,0:T(8,128)(2,1)}, bf16[720,512]{1,0:T(8,128)(2,1)}, u32[]{:S(2)}, u32[]{:S(2)}) collective-permute-start(bf16[720,512]{1,0:T(8,128)(2,1)} %get-tuple-element.207), channel_id=1, source_target_pairs={{0,12},{4,16},{8,4},{12,24},{16,28},{20,0},{24,20},{28,8},{1,13},{... | collective-permute-start | bytes 2211848 | tf_op jit(solution)/shard_map/ppermute | solution.py:580
  197.7 24.4 %collective-permute-start.44 = (bf16[720,512]{1,0:T(8,128)(2,1)}, bf16[720,512]{1,0:T(8,128)(2,1)}, u32[]{:S(2)}, u32[]{:S(2)}) collective-permute-start(bf16[720,512]{1,0:T(8,128)(2,1)} %get-tuple-element.200), channel_id=1, source_target_pairs={{0,4},{4,0},{8,12},{12,8},{16,20},{20,16},{24,28},{28,24},{1,5},{5... | collective-permute-start | bytes 2211848 | tf_op jit(solution)/shard_map/ppermute | solution.py:576
  215.9 11.6 %collective-permute-start.45 = (bf16[720,512]{1,0:T(8,128)(2,1)}, bf16[720,512]{1,0:T(8,128)(2,1)}, u32[]{:S(2)}, u32[]{:S(2)}) collective-permute-start(bf16[720,512]{1,0:T(8,128)(2,1)} %get-tuple-element.201), channel_id=1, source_target_pairs={{0,20},{4,8},{8,28},{12,0},{16,4},{20,24},{24,12},{28,16},{1,21},{... | collective-permute-start | bytes 2211848 | tf_op jit(solution)/shard_map/ppermute | solution.py:580
  215.9 3.7 %collective-permute-start.46 = (f32[64,720]{1,0:T(8,128)S(1)}, f32[64,720]{1,0:T(8,128)S(1)}, u32[]{:S(2)}, u32[]{:S(2)}) collective-permute-start(f32[64,720]{1,0:T(8,128)S(1)} %convert_add_fusion), channel_id=1, source_target_pairs={{0,4},{4,0},{8,12},{12,8},{16,20},{20,16},{24,28},{28,24},{1,5},{5... | collective-permute-start | bytes 552968 | tf_op jit(solution)/shard_map/ppermute | solution.py:576

commit v15 on v14

--- a/solution.py
+++ b/solution.py
@@ -610,8 +610,9 @@
     panel_full, energies = energy(meta, [near], ctf_table, inv, piece, 0)
     a1, recv_b[:2], panel_full, energies = together((a1, recv_b[:2], panel_full, energies))
     a2 = onward(a1)
+    recv_b, near = together((recv_b, near))
     share_b = unpack_next(meta, pick, wide, recv_b, ctf_table, inv, width, chunk_b)
-    a2, share_b, near = together((a2, share_b, near))
+    a2, share_b = together((a2, share_b))
     by_x, by_y = across(near, 2), across(near, 4)
     a3, b1 = onward(a2), onward(share_b)
     sib0, hots = [across(share_a, 1), across(share_b, 1)], [hot, across(hot, 1)]

time: 231 us -> 233 us (level)
  starting transfers between devices: 37.4 us -> 42.8 us
  waiting for transfers between devices: 114 us -> 110 us
    ppermute x35, waiting for transfers between devices: 66.8 us -> 49 us  [across(): return lax.ppermute(value, 'dom', [(i, i ^ apart) for i in range(dom)])]
    ppermute x6, waiting for transfers between devices: 36.7 us -> 51.2 us  [onward(): lax.ppermute(value, 'rot', [(i, (i + 1) % turns) for i in range(turns)])]
    ppermute x35, starting transfers between devices: 27 us -> 30.4 us  [across(): return lax.ppermute(value, 'dom', [(i, i ^ apart) for i in range(dom)])]
  transfers between devices with their start and end apart: 48 -> 48, of which waited for: 27 -> 23; matrix products, arithmetic and copies ran while one was open for 2% -> 2% of each run, Pallas kernels for 24% -> 24%
where the time goes in v15:
time: 233 us
  waiting for transfers between devices  110 us (47%)
  Pallas kernels  70.1 us (30%)
  starting transfers between devices  42.8 us (18%)
  other arithmetic  6.84 us (3%)
    ppermute x6, waiting for transfers between devices, onward(): lax.ppermute(value, 'rot', [(i, (i + 1) % turns) for i in range(turns)])  51.2 us
    ppermute x35, waiting for transfers between devices, across(): return lax.ppermute(value, 'dom', [(i, i ^ apart) for i in range(dom)])  49 us
    ppermute x35, starting transfers between devices, across(): return lax.ppermute(value, 'dom', [(i, i ^ apart) for i in range(dom)])  30.4 us
    pallas_call x5, Pallas kernels, score(): call(functools.partial(score_body, parts, used, first, last), (2 * half,)...  26.4 us
    pallas_call x2, Pallas kernels, class_part(): call(functools.partial(class_body, kind, steps), (steps,), in_specs, out_...  15 us
    pallas_call x2, Pallas kernels, energy(): call(functools.partial(far_energy_body if last else near_energy_body, bin...  7.21 us
    ppermute x4, waiting for transfers between devices, by_core(): return lax.ppermute(value, 'dom', pairs)  7.08 us
    pallas_call x1, Pallas kernels, pack_next(): call(functools.partial(pack_next_body, cap, dom), (1,), [pl.BlockSpec((1,...  5.9 us
  transfers between devices with their start and end apart: 48, of which 23 were waited for; matrix products, arithmetic and copies ran while one was open for 2% of the time, Pallas kernels for 24%

profile of v15, /device:TPU:0, one launch (start us, length us, event | category | flops | bytes accessed | tf_op | source)
XLA Modules:
  0.0 232.7 jit_solution(3030461974601548032)
XLA Ops:
  1.2 0.7 add_select_fusion.slot_ref
  2.0 5.8 %shard_map.85 = (bf16[208,384]{1,0:T(8,128)(2,1)S(1)}, bf16[208,384]{1,0:T(8,128)(2,1)S(1)}, bf16[208,384]{1,0:T(8,128)(2,1)S(1)}, bf16[208,384]{1,0:T(8,128)(2,...) custom-call(s32[10]{0:T(128)S(1)} %stack.43.meta, ...), custom_call_target="tpu_custom_call" | custom-call | flops 113246208 | bytes 147456 | tf_op jit(solution)/shard_map/pallas_call | solution.py:132
  7.7 3.6 %collective-permute-start = (bf16[208,384]{1,0:T(8,128)(2,1)S(1)}, bf16[208,384]{1,0:T(8,128)(2,1)S(1)}, u32[]{:S(2)}, u32[]{:S(2)}) collective-permute-start(bf16[208,384]{1,0:T(8,128)(2,1)S(1)} %get-tuple-element.113), channel_id=1, source_target_pairs={{0,24},{4,28},{8,16},{12,20},{16,8},{20,12},{24,0},{28,4},{1,25},{... | collective-permute-start | bytes 479240 | tf_op jit(solution)/shard_map/ppermute | solution.py:576
  11.4 1.6 collective-permute-start.2
  13.1 1.5 collective-permute-start.3
  14.7 1.2 constant_dynamic-slice_fusion
  16.4 0.6 collective-permute-start.5
  17.0 2.3 collective-permute-done.1.refs_1_
  19.6 5.9 %shard_map.86 = (bf16[192,640]{1,0:T(8,128)(2,1)S(1)}, bf16[192,640]{1,0:T(8,128)(2,1)S(1)}, bf16[192,640]{1,0:T(8,128)(2,1)S(1)}, bf16[192,640]{1,0:T(8,128)(2,...) custom-call(s32[10]{0:T(128)S(1)} %stack.43.meta, ...), custom_call_target="tpu_custom_call" | custom-call | flops 188743680 | bytes 245760 | tf_op jit(solution)/shard_map/pallas_call | solution.py:152
  26.5 3.5 %shard_map.87 = (bf16[768,384]{1,0:T(8,128)(2,1)S(1)}, bf16[192,768]{1,0:T(8,128)(2,1)S(1)}, bf16[768,1536]{1,0:T(8,128)(2,1)S(1)}, bf16[768,192]{1,0:T(8,128)(2,1)S(1)}) custom-call(s32[10]{0:T(128)S(1)} %stack.43.meta, bf16[208,384]{1,0:T(8,128)(2,1)S(1)} %collective-permute-done.refs_0_, bf16[208,384]{1,0:T(8,128)(2,1)S(1)} %collective-permute-done.1.refs_1_, ...), custom_call_target="tpu_custom_call" | custom-call | flops 56623104 | bytes 73728 | tf_op jit(solution)/shard_map/pallas_call | solution.py:212
  30.0 2.0 collective-permute-start.8
  32.1 1.8 collective-permute-start.10
  33.8 0.7 collective-permute-start.9
  34.5 1.3 collective-permute-start.12
  35.8 1.5 collective-permute-start.13
  37.3 3.9 %collective-permute-done.10.refs_1_ = bf16[192,640]{1,0:T(8,128)(2,1)S(1)} collective-permute-done((bf16[192,640]{1,0:T(8,128)(2,1)S(1)}, bf16[192,640]{1,0:T(8,128)(2,1)S(1)}, u32[]{:S(2)}, u32[]{:S(2)}) %collective-permute-start.10) | collective-permute-done | bytes 245792 | tf_op jit(solution)/shard_map/ppermute | solution.py:576
  41.2 1.1 collective-permute-start.14
  42.3 4.3 %collective-permute-done.9.refs_0_ = bf16[192,640]{1,0:T(8,128)(2,1)S(1)} collective-permute-done((bf16[192,640]{1,0:T(8,128)(2,1)S(1)}, bf16[192,640]{1,0:T(8,128)(2,1)S(1)}, u32[]{:S(2)}, u32[]{:S(2)}) %collective-permute-start.9) | collective-permute-done | bytes 245792 | tf_op jit(solution)/shard_map/ppermute | solution.py:576
  46.6 1.1 collective-permute-start.15
  48.0 2.1 shard_map.88
  50.1 1.7 collective-permute-done.12.refs_2_
  51.8 1.6 collective-permute-start.11
  53.4 3.6 %collective-permute-done.14.refs_4_ = bf16[192,640]{1,0:T(8,128)(2,1)S(1)} collective-permute-done((bf16[192,640]{1,0:T(8,128)(2,1)S(1)}, bf16[192,640]{1,0:T(8,128)(2,1)S(1)}, u32[]{:S(2)}, u32[]{:S(2)}) %collective-permute-start.14) | collective-permute-done | bytes 245792 | tf_op jit(solution)/shard_map/ppermute | solution.py:576
  57.0 1.5 collective-permute-start.20
  58.5 1.4 collective-permute-start.21
  59.9 2.9 %shard_map.89.refs_1_ = bf16[768,640]{1,0:T(8,128)(2,1)S(1)} custom-call(s32[10]{0:T(128)S(1)} %stack.43.meta, bf16[192,640]{1,0:T(8,128)(2,1)S(1)} %collective-permute-done.9.refs_0_, bf16[192,640]{1,0:T(8,128)(2,1)S(1)} %collective-permute-done.10.refs_1_, bf16[192,640]{1,0:T(8,128)(2,1)S(1)} %collective-permute-done.12.refs_2_, ...), custom_call_target="tpu_custom_call" | custom-call | flops 94371840 | bytes 122880 | tf_op jit(solution)/shard_map/pallas_call | solution.py:231
  62.8 6.0 %collective-permute-done.11.refs_0_ = bf16[768,384]{1,0:T(8,128)(2,1)S(1)} collective-permute-done((bf16[768,384]{1,0:T(8,128)(2,1)S(1)}, bf16[768,384]{1,0:T(8,128)(2,1)S(1)}, u32[]{:S(2)}, u32[]{:S(2)}) %collective-permute-start.11) | collective-permute-done | bytes 589856 | tf_op jit(solution)/shard_map/ppermute | solution.py:583
  68.8 1.3 collective-permute-start.17
  70.2 25.1 %collective-permute-done.18.refs_1_ = bf16[768,640]{1,0:T(8,128)(2,1)S(1)} collective-permute-done((bf16[768,640]{1,0:T(8,128)(2,1)S(1)}, bf16[768,640]{1,0:T(8,128)(2,1)S(1)}, u32[]{:S(2)}, u32[]{:S(2)}) %collective-permute-start.18) | collective-permute-done | bytes 983072 | tf_op jit(solution)/shard_map/ppermute | solution.py:583
  95.4 1.5 collective-permute-start.22
  97.0 1.6 collective-permute-start.23
  98.8 9.2 %collective-permute-done.17.refs_0_ = bf16[768,384]{1,0:T(8,128)(2,1)S(1)} collective-permute-done((bf16[768,384]{1,0:T(8,128)(2,1)S(1)}, bf16[768,384]{1,0:T(8,128)(2,1)S(1)}, u32[]{:S(2)}, u32[]{:S(2)}) %collective-permute-start.17) | collective-permute-done | bytes 589856 | tf_op jit(solution)/shard_map/ppermute | solution.py:583
  108.0 2.2 collective-permute-done.22.refs_2_
  110.2 5.8 %collective-permute-done.23.refs_3_ = bf16[720,512]{1,0:T(8,128)(2,1)S(1)} collective-permute-done((bf16[720,512]{1,0:T(8,128)(2,1)S(1)}, bf16[720,512]{1,0:T(8,128)(2,1)S(1)}, u32[]{:S(2)}, u32[]{:S(2)}) %collective-permute-start.23) | collective-permute-done | bytes 737312 | tf_op jit(solution)/shard_map/ppermute | solution.py:576
  115.9 5.2 %shard_map.90 = (bf16[720,4096]{1,0:T(8,128)(2,1)S(1)}, bf16[720,192]{1,0:T(8,128)(2,1)S(1)}) custom-call(s32[10]{0:T(128)S(1)} %stack.43.meta, bf16[720,1024]{1,0:T(8,128)(2,1)S(1)} %collective-permute-done.20.refs_0_, bf16[720,1024]{1,0:T(8,128)(2,1)S(1)} %collective-permute-done.21.refs_1_, ...), custom_call_target="tpu_custom_call", output_to_operand_aliasing={{0}: (8, {})} | custom-call | flops 212336640 | bytes 552960 | tf_op jit(solution)/shard_map/pallas_call | solution.py:328
  121.1 6.0 %collective-permute-done.19.refs_1_ = bf16[768,640]{1,0:T(8,128)(2,1)S(1)} collective-permute-done((bf16[768,640]{1,0:T(8,128)(2,1)S(1)}, bf16[768,640]{1,0:T(8,128)(2,1)S(1)}, u32[]{:S(2)}, u32[]{:S(2)}) %collective-permute-start.19) | collective-permute-done | bytes 983072 | tf_op jit(solution)/shard_map/ppermute | solution.py:583
  127.8 5.1 %shard_map.91 = (f32[720,1536]{1,0:T(8,128)S(1)}, bf16[1536,4096]{1,0:T(8,128)(2,1)S(1)}) custom-call(s32[10]{0:T(128)S(1)} %stack.43.meta, bf16[768,384]{1,0:T(8,128)(2,1)S(1)} %get-tuple-element.149.refs_0_, bf16[768,640]{1,0:T(8,128)(2,1)S(1)} %shard_map.89.refs_1_, bf16[768,384]{1,0:T(8,128)(2,1)S(1)} %collective-permute-done.31.refs_2_, ...), custom_call_target="tpu_custom_call" | custom-call | flops 141557760 | bytes 946176 | tf_op jit(solution)/shard_map/pallas_call | solution.py:428
  132.9 5.4 %shard_map.92 = (f32[720,1536]{1,0:T(8,128)S(1)}, bf16[1536,4096]{1,0:T(8,128)(2,1)S(1)}) custom-call(s32[10]{0:T(128)S(1)} %stack.43.meta, bf16[768,384]{1,0:T(8,128)(2,1)S(1)} %collective-permute-done.8.refs_0_, bf16[768,640]{1,0:T(8,128)(2,1)S(1)} %collective-permute-done.18.refs_1_, ...), custom_call_target="tpu_custom_call", output_to_operand_aliasing={{0}: (6, {}), {1}: (7, {})} | custom-call | flops 141557760 | bytes 946176 | tf_op jit(solution)/shard_map/pallas_call | solution.py:428
  138.4 5.4 %shard_map.93 = (f32[720,1536]{1,0:T(8,128)S(1)}, bf16[1536,4096]{1,0:T(8,128)(2,1)S(1)}) custom-call(s32[10]{0:T(128)S(1)} %stack.43.meta, bf16[768,384]{1,0:T(8,128)(2,1)S(1)} %collective-permute-done.11.refs_0_, bf16[768,640]{1,0:T(8,128)(2,1)S(1)} %collective-permute-done.19.refs_1_, ...), custom_call_target="tpu_custom_call", output_to_operand_aliasing={{0}: (6, {}), {1}: (7, {})} | custom-call | flops 141557760 | bytes 946176 | tf_op jit(solution)/shard_map/pallas_call | solution.py:428
  143.8 4.4 %shard_map.94.refs_5_ = f32[720,1536]{1,0:T(8,128)S(1)} custom-call(s32[10]{0:T(128)S(1)} %stack.43.meta, bf16[768,384]{1,0:T(8,128)(2,1)S(1)} %collective-permute-done.17.refs_0_, bf16[768,384]{1,0:T(8,128)(2,1)S(1)} %collective-permute-done.26.refs_1_.refs_2_, ...), custom_call_target="tpu_custom_call", output_to_operand_aliasing={{}: (4, {})} | custom-call | flops 141557760 | bytes 946176 | tf_op jit(solution)/shard_map/pallas_call | solution.py:428
  148.2 4.9 %collective-permute-done.25.refs_1_ = bf16[768,640]{1,0:T(8,128)(2,1)S(1)} collective-permute-done((bf16[768,640]{1,0:T(8,128)(2,1)S(1)}, bf16[768,640]{1,0:T(8,128)(2,1)S(1)}, u32[]{:S(2)}, u32[]{:S(2)}) %collective-permute-start.25) | collective-permute-done | bytes 983072 | tf_op jit(solution)/shard_map/ppermute | solution.py:583
  153.1 2.6 %collective-permute-done.33.refs_3_ = bf16[768,640]{1,0:T(8,128)(2,1)S(1)} collective-permute-done((bf16[768,640]{1,0:T(8,128)(2,1)S(1)}, bf16[768,640]{1,0:T(8,128)(2,1)S(1)}, u32[]{:S(2)}, u32[]{:S(2)}) %collective-permute-start.33) | collective-permute-done | bytes 983072 | tf_op jit(solution)/shard_map/ppermute | solution.py:576
  155.7 6.0 %shard_map.95 = (f32[720,1536]{1,0:T(8,128)S(1)}, f32[8,1536]{1,0:T(8,128)S(1)}, bf16[1536,4096]{1,0:T(8,128)(2,1)S(1)}) custom-call(s32[10]{0:T(128)S(1)} %stack.43.meta, bf16[768,384]{1,0:T(8,128)(2,1)S(1)} %collective-permute-done.17.refs_0_, bf16[768,640]{1,0:T(8,128)(2,1)S(1)} %collective-permute-done.25.refs_1_, ...), custom_call_target="tpu_custom_call", output_to_operand_aliasing={{0}: (6, {}), {2}: (7, {})} | custom-call | flops 141557760 | bytes 946176 | tf_op jit(solution)/shard_map/pallas_call | solution.py:428
  161.9 1.1 collective-permute-done.34.other_ref
  163.0 0.6 shard_map.96.refs_2_
  163.8 4.3 %collective-permute-start.37 = (f32[8,1536]{1,0:T(8,128)S(1)}, f32[8,1536]{1,0:T(8,128)S(1)}, u32[]{:S(2)}, u32[]{:S(2)}) collective-permute-start(f32[8,1536]{1,0:T(8,128)S(1)} %shard_map.96.refs_2_), channel_id=1, source_target_pairs={{0,3},{1,2},{2,1},{3,0},{4,7},{5,6},{6,5},{7,4},{8,11},{9,10},{10,... | collective-permute-start | bytes 147464 | tf_op jit(solution)/shard_map/ppermute | solution.py:656
  168.4 2.7 %collective-permute-done.36.refs_4_ = f32[8,1536]{1,0:T(8,128)S(1)} collective-permute-done((f32[8,1536]{1,0:T(8,128)S(1)}, f32[8,1536]{1,0:T(8,128)S(1)}, u32[]{:S(2)}, u32[]{:S(2)}) %collective-permute-start.36) | collective-permute-done | bytes 49184 | tf_op jit(solution)/shard_map/ppermute | solution.py:656
  171.1 4.2 %shard_map.97 = (bf16[720,512]{1,0:T(8,128)(2,1)S(1)}, bf16[720,512]{1,0:T(8,128)(2,1)S(1)}, bf16[720,1536]{1,0:T(8,128)(2,1)S(1)}, f32[1,768]{1,0:T(1,128)S(1)}, bf16[64,720]{1,0:T(8,128)(2,1)S(1)}) custom-call(s32[10]{0:T(128)S(1)} %stack.43.meta, f32[720,1536]{1,0:T(8,128)S(1)} %get-tuple-element.195.refs_0_, ...), custom_call_target="tpu_custom_call" | custom-call | flops 141557760 | bytes 657408 | tf_op jit(solution)/shard_map/pallas_call | solution.py:516
  175.3 1.5 collective-permute-start.38
  176.9 1.5 collective-permute-start.39
  178.9 10.7 %shard_map.98 = (bf16[720,512]{1,0:T(8,128)(2,1)S(1)}, bf16[720,512]{1,0:T(8,128)(2,1)}, bf16[720,512]{1,0:T(8,128)(2,1)}, f32[720,512]{1,0:T(8,128)S(1)}, f32[7...) custom-call(s32[10]{0:T(128)S(1)} %stack.43.meta, bf16[720,1536]{1,0:T(8,128)(2,1)S(1)} %get-tuple-element.200.refs_0_, ...), custom_call_target="tpu_custom_call" | custom-call | flops 424673280 | bytes 1419264 | tf_op jit(solution)/shard_map/pallas_call | solution.py:516
  189.7 4.6 %collective-permute-done.40.other_ref = bf16[64,720]{1,0:T(8,128)(2,1)S(1)} collective-permute-done((bf16[64,720]{1,0:T(8,128)(2,1)S(1)}, bf16[64,720]{1,0:T(8,128)(2,1)S(1)}, u32[]{:S(2)}, u32[]{:S(2)}) %collective-permute-start.40) | collective-permute-done | bytes 92192 | tf_op jit(solution)/shard_map/ppermute | solution.py:576
  194.3 1.4 fusion.3
  195.7 1.5 collective-permute-start.42
  197.2 1.5 collective-permute-start.43
  199.8 1.6 collective-permute-start.44
  201.5 15.8 %collective-permute-done.41 = bf16[64,720]{1,0:T(8,128)(2,1)S(1)} collective-permute-done((bf16[64,720]{1,0:T(8,128)(2,1)S(1)}, bf16[64,720]{1,0:T(8,128)(2,1)S(1)}, u32[]{:S(2)}, u32[]{:S(2)}) %collective-permute-start.41) | collective-permute-done | bytes 92192 | tf_op jit(solution)/shard_map/ppermute | solution.py:576
  217.3 1.6 collective-permute-start.46
  218.9 0.6 reduce
  219.5 2.3 shard_map.100
  221.8 0.9 maximum_select_fusion
  222.7 2.3 %collective-permute-done.47 = bf16[720,512]{1,0:T(8,128)(2,1)} collective-permute-done((bf16[720,512]{1,0:T(8,128)(2,1)}, bf16[720,512]{1,0:T(8,128)(2,1)}, u32[]{:S(2)}, u32[]{:S(2)}) %collective-permute-start.47) | collective-permute-done | bytes 737312 | tf_op jit(solution)/shard_map/ppermute | solution.py:580
  225.1 4.7 %collective-permute-done.45 = bf16[720,512]{1,0:T(8,128)(2,1)} collective-permute-done((bf16[720,512]{1,0:T(8,128)(2,1)}, bf16[720,512]{1,0:T(8,128)(2,1)}, u32[]{:S(2)}, u32[]{:S(2)}) %collective-permute-start.45) | collective-permute-done | bytes 737312 | tf_op jit(solution)/shard_map/ppermute | solution.py:580
  229.8 2.9 %add_dynamic-update-slice_fusion = f32[1440,512]{1,0:T(8,128)} fusion(f32[1440,512]{1,0:T(8,128)} %shard_map.100, s32[]{:T(128)S(6)} %select_n.67, bf16[720,512]{1,0:T(8,128)(2,1)} %collective-permute-done.47, bf16[720,512]{1,0:T(8,128)(2,1)} %collective-permute-done.45, bf16[720,512]{1,0:T(8,128)(2,1)} %collective-permute-done.44), kind=kLoop, calls=%fused_computation.7 | loop fusion | flops 1843200 | bytes 3686404 | tf_op jit(solution)/shard_map/dynamic_update_slice | solution.py:685
  (66 shorter events, 6.4 us)
Async XLA Ops:
  0.6 14.0 %collective-permute-start.7 = (bf16[1440,512]{1,0:T(8,128)(2,1)}, bf16[1440,512]{1,0:T(8,128)(2,1)}, u32[]{:S(2)}, u32[]{:S(2)}) collective-permute-start(bf16[1440,512]{1,0:T(8,128)(2,1)} %param.11), channel_id=1, source_target_pairs={{0,4},{4,0},{8,12},{12,8},{16,20},{20,16},{24,28},{28,24},{1,5},{5... | collective-permute-start | bytes 4423688 | tf_op jit(solution)/shard_map/ppermute | solution.py:576
  2.0 12.6 %copy-start.2 = (bf16[1440,512]{1,0:T(8,128)(2,1)S(1)}, bf16[1440,512]{1,0:T(8,128)(2,1)}, u32[]{:S(2)}) copy-start(bf16[1440,512]{1,0:T(8,128)(2,1)} %param.11) | copy-start | bytes 4423684
  7.7 8.6 %collective-permute-start = (bf16[208,384]{1,0:T(8,128)(2,1)S(1)}, bf16[208,384]{1,0:T(8,128)(2,1)S(1)}, u32[]{:S(2)}, u32[]{:S(2)}) collective-permute-start(bf16[208,384]{1,0:T(8,128)(2,1)S(1)} %get-tuple-element.113), channel_id=1, source_target_pairs={{0,24},{4,28},{8,16},{12,20},{16,8},{20,12},{24,0},{28,4},{1,25},{... | collective-permute-start | bytes 479240 | tf_op jit(solution)/shard_map/ppermute | solution.py:576
  11.3 8.0 %collective-permute-start.1 = (bf16[208,384]{1,0:T(8,128)(2,1)S(1)}, bf16[208,384]{1,0:T(8,128)(2,1)S(1)}, u32[]{:S(2)}, u32[]{:S(2)}) collective-permute-start(bf16[208,384]{1,0:T(8,128)(2,1)S(1)} %get-tuple-element.114), channel_id=1, source_target_pairs={{0,28},{4,24},{8,20},{12,16},{16,12},{20,8},{24,4},{28,0},{1,29},{... | collective-permute-start | bytes 479240 | tf_op jit(solution)/shard_map/ppermute | solution.py:576
  11.4 14.3 %collective-permute-start.2 = (bf16[208,384]{1,0:T(8,128)(2,1)S(1)}, bf16[208,384]{1,0:T(8,128)(2,1)S(1)}, u32[]{:S(2)}, u32[]{:S(2)}) collective-permute-start(bf16[208,384]{1,0:T(8,128)(2,1)S(1)} %get-tuple-element.115), channel_id=1, source_target_pairs={{0,16},{4,20},{8,24},{12,28},{16,0},{20,4},{24,8},{28,12},{1,17},{... | collective-permute-start | bytes 479240 | tf_op jit(solution)/shard_map/ppermute | solution.py:576
  13.1 12.6 %collective-permute-start.3 = (bf16[208,384]{1,0:T(8,128)(2,1)S(1)}, bf16[208,384]{1,0:T(8,128)(2,1)S(1)}, u32[]{:S(2)}, u32[]{:S(2)}) collective-permute-start(bf16[208,384]{1,0:T(8,128)(2,1)S(1)} %get-tuple-element.116), channel_id=1, source_target_pairs={{0,8},{4,12},{8,0},{12,4},{16,24},{20,28},{24,16},{28,20},{1,9},{5... | collective-permute-start | bytes 479240 | tf_op jit(solution)/shard_map/ppermute | solution.py:576
  14.6 11.6 %collective-permute-start.4 = (bf16[208,384]{1,0:T(8,128)(2,1)S(1)}, bf16[208,384]{1,0:T(8,128)(2,1)S(1)}, u32[]{:S(2)}, u32[]{:S(2)}) collective-permute-start(bf16[208,384]{1,0:T(8,128)(2,1)S(1)} %get-tuple-element.117), channel_id=1, source_target_pairs={{0,20},{4,16},{8,28},{12,24},{16,4},{20,0},{24,12},{28,8},{1,21},{... | collective-permute-start | bytes 479240 | tf_op jit(solution)/shard_map/ppermute | solution.py:576
  16.4 9.9 %collective-permute-start.5 = (bf16[208,384]{1,0:T(8,128)(2,1)S(1)}, bf16[208,384]{1,0:T(8,128)(2,1)S(1)}, u32[]{:S(2)}, u32[]{:S(2)}) collective-permute-start(bf16[208,384]{1,0:T(8,128)(2,1)S(1)} %get-tuple-element.118), channel_id=1, source_target_pairs={{0,12},{4,8},{8,4},{12,0},{16,28},{20,24},{24,20},{28,16},{1,13},{... | collective-permute-start | bytes 479240 | tf_op jit(solution)/shard_map/ppermute | solution.py:576
  19.3 6.9 %collective-permute-start.6 = (bf16[208,384]{1,0:T(8,128)(2,1)S(1)}, bf16[208,384]{1,0:T(8,128)(2,1)S(1)}, u32[]{:S(2)}, u32[]{:S(2)}) collective-permute-start(bf16[208,384]{1,0:T(8,128)(2,1)S(1)} %get-tuple-element.119), channel_id=1, source_target_pairs={{0,4},{4,0},{8,12},{12,8},{16,20},{20,16},{24,28},{28,24},{1,5},{5... | collective-permute-start | bytes 479240 | tf_op jit(solution)/shard_map/ppermute | solution.py:576
  25.5 1.0 copy-start
  25.5 1.0 copy-start.1
  30.0 17.7 %collective-permute-start.8 = (bf16[768,384]{1,0:T(8,128)(2,1)S(1)}, bf16[768,384]{1,0:T(8,128)(2,1)S(1)}, u32[]{:S(2)}, u32[]{:S(2)}) collective-permute-start(bf16[768,384]{1,0:T(8,128)(2,1)S(1)} %get-tuple-element.149.refs_0_), channel_id=1, source_target_pairs={{0,1},{1,2},{2,3},{3,0},{4,5},{5,6},{6,7},{7,4},{8,9},{9,10},{10,1... | collective-permute-start | bytes 1769480 | tf_op jit(solution)/shard_map/ppermute | solution.py:583
  32.1 9.2 %collective-permute-start.10 = (bf16[192,640]{1,0:T(8,128)(2,1)S(1)}, bf16[192,640]{1,0:T(8,128)(2,1)S(1)}, u32[]{:S(2)}, u32[]{:S(2)}) collective-permute-start(bf16[192,640]{1,0:T(8,128)(2,1)S(1)} %get-tuple-element.151), channel_id=1, source_target_pairs={{0,28},{4,24},{8,20},{12,16},{16,12},{20,8},{24,4},{28,0},{1,29},{... | collective-permute-start | bytes 737288 | tf_op jit(solution)/shard_map/ppermute | solution.py:576
  33.8 12.8 %collective-permute-start.9 = (bf16[192,640]{1,0:T(8,128)(2,1)S(1)}, bf16[192,640]{1,0:T(8,128)(2,1)S(1)}, u32[]{:S(2)}, u32[]{:S(2)}) collective-permute-start(bf16[192,640]{1,0:T(8,128)(2,1)S(1)} %get-tuple-element.150), channel_id=1, source_target_pairs={{0,24},{4,28},{8,16},{12,20},{16,8},{20,12},{24,0},{28,4},{1,25},{... | collective-permute-start | bytes 737288 | tf_op jit(solution)/shard_map/ppermute | solution.py:576
  34.5 17.3 %collective-permute-start.12 = (bf16[192,640]{1,0:T(8,128)(2,1)S(1)}, bf16[192,640]{1,0:T(8,128)(2,1)S(1)}, u32[]{:S(2)}, u32[]{:S(2)}) collective-permute-start(bf16[192,640]{1,0:T(8,128)(2,1)S(1)} %get-tuple-element.158), channel_id=1, source_target_pairs={{0,16},{4,20},{8,24},{12,28},{16,0},{20,4},{24,8},{28,12},{1,17},{... | collective-permute-start | bytes 737288 | tf_op jit(solution)/shard_map/ppermute | solution.py:576
  35.8 17.6 %collective-permute-start.13 = (bf16[192,640]{1,0:T(8,128)(2,1)S(1)}, bf16[192,640]{1,0:T(8,128)(2,1)S(1)}, u32[]{:S(2)}, u32[]{:S(2)}) collective-permute-start(bf16[192,640]{1,0:T(8,128)(2,1)S(1)} %get-tuple-element.159), channel_id=1, source_target_pairs={{0,8},{4,12},{8,0},{12,4},{16,24},{20,28},{24,16},{28,20},{1,9},{5... | collective-permute-start | bytes 737288 | tf_op jit(solution)/shard_map/ppermute | solution.py:576
  41.2 15.7 %collective-permute-start.14 = (bf16[192,640]{1,0:T(8,128)(2,1)S(1)}, bf16[192,640]{1,0:T(8,128)(2,1)S(1)}, u32[]{:S(2)}, u32[]{:S(2)}) collective-permute-start(bf16[192,640]{1,0:T(8,128)(2,1)S(1)} %get-tuple-element.160), channel_id=1, source_target_pairs={{0,20},{4,16},{8,28},{12,24},{16,4},{20,0},{24,12},{28,8},{1,21},{... | collective-permute-start | bytes 737288 | tf_op jit(solution)/shard_map/ppermute | solution.py:576
  46.6 10.4 %collective-permute-start.15 = (bf16[192,640]{1,0:T(8,128)(2,1)S(1)}, bf16[192,640]{1,0:T(8,128)(2,1)S(1)}, u32[]{:S(2)}, u32[]{:S(2)}) collective-permute-start(bf16[192,640]{1,0:T(8,128)(2,1)S(1)} %get-tuple-element.161), channel_id=1, source_target_pairs={{0,12},{4,8},{8,4},{12,0},{16,28},{20,24},{24,20},{28,16},{1,13},{... | collective-permute-start | bytes 737288 | tf_op jit(solution)/shard_map/ppermute | solution.py:576
  47.7 9.3 %collective-permute-start.16 = (bf16[192,640]{1,0:T(8,128)(2,1)S(1)}, bf16[192,640]{1,0:T(8,128)(2,1)S(1)}, u32[]{:S(2)}, u32[]{:S(2)}) collective-permute-start(bf16[192,640]{1,0:T(8,128)(2,1)S(1)} %get-tuple-element.162), channel_id=1, source_target_pairs={{0,4},{4,0},{8,12},{12,8},{16,20},{20,16},{24,28},{28,24},{1,5},{5... | collective-permute-start | bytes 737288 | tf_op jit(solution)/shard_map/ppermute | solution.py:576
  51.8 17.0 %collective-permute-start.11 = (bf16[768,384]{1,0:T(8,128)(2,1)S(1)}, bf16[768,384]{1,0:T(8,128)(2,1)S(1)}, u32[]{:S(2)}, u32[]{:S(2)}) collective-permute-start(bf16[768,384]{1,0:T(8,128)(2,1)S(1)} %collective-permute-done.8.refs_0_), channel_id=1, source_target_pairs={{0,1},{1,2},{2,3},{3,0},{4,5},{5,6},{6,7},{7,4},{8,9},{9,10},{10,1... | collective-permute-start | bytes 1769480 | tf_op jit(solution)/shard_map/ppermute | solution.py:583
  57.0 38.3 %collective-permute-start.20 = (bf16[720,1024]{1,0:T(8,128)(2,1)S(1)}, bf16[720,1024]{1,0:T(8,128)(2,1)S(1)}, u32[]{:S(2)}, u32[]{:S(2)}) collective-permute-start(bf16[720,1024]{1,0:T(8,128)(2,1)S(1)} %pad_maximum_fusion.refs_0_), channel_id=1, source_target_pairs={{0,8},{4,12},{8,0},{12,4},{16,24},{20,28},{24,16},{28,20},{1,9},{5... | collective-permute-start | bytes 4423688 | tf_op jit(solution)/shard_map/ppermute | solution.py:576
  58.5 38.4 %collective-permute-start.21 = (bf16[720,1024]{1,0:T(8,128)(2,1)S(1)}, bf16[720,1024]{1,0:T(8,128)(2,1)S(1)}, u32[]{:S(2)}, u32[]{:S(2)}) collective-permute-start(bf16[720,1024]{1,0:T(8,128)(2,1)S(1)} %pad_maximum_fusion.refs_0_), channel_id=1, source_target_pairs={{0,16},{4,20},{8,24},{12,28},{16,0},{20,4},{24,8},{28,12},{1,17},{... | collective-permute-start | bytes 4423688 | tf_op jit(solution)/shard_map/ppermute | solution.py:576
  68.8 26.5 %collective-permute-start.18 = (bf16[768,640]{1,0:T(8,128)(2,1)S(1)}, bf16[768,640]{1,0:T(8,128)(2,1)S(1)}, u32[]{:S(2)}, u32[]{:S(2)}) collective-permute-start(bf16[768,640]{1,0:T(8,128)(2,1)S(1)} %shard_map.89.refs_1_), channel_id=1, source_target_pairs={{0,1},{1,2},{2,3},{3,0},{4,5},{5,6},{6,7},{7,4},{8,9},{9,10},{10,1... | collective-permute-start | bytes 2949128 | tf_op jit(solution)/shard_map/ppermute | solution.py:583
  68.8 39.1 %collective-permute-start.17 = (bf16[768,384]{1,0:T(8,128)(2,1)S(1)}, bf16[768,384]{1,0:T(8,128)(2,1)S(1)}, u32[]{:S(2)}, u32[]{:S(2)}) collective-permute-start(bf16[768,384]{1,0:T(8,128)(2,1)S(1)} %collective-permute-done.11.refs_0_), channel_id=1, source_target_pairs={{0,1},{1,2},{2,3},{3,0},{4,5},{5,6},{6,7},{7,4},{8,9},{9,10},{10,1... | collective-permute-start | bytes 1769480 | tf_op jit(solution)/shard_map/ppermute | solution.py:583
  95.3 31.8 %collective-permute-start.19 = (bf16[768,640]{1,0:T(8,128)(2,1)S(1)}, bf16[768,640]{1,0:T(8,128)(2,1)S(1)}, u32[]{:S(2)}, u32[]{:S(2)}) collective-permute-start(bf16[768,640]{1,0:T(8,128)(2,1)S(1)} %collective-permute-done.18.refs_1_), channel_id=1, source_target_pairs={{0,1},{1,2},{2,3},{3,0},{4,5},{5,6},{6,7},{7,4},{8,9},{9,10},{10,1... | collective-permute-start | bytes 2949128 | tf_op jit(solution)/shard_map/ppermute | solution.py:583
  95.4 14.8 %collective-permute-start.22 = (bf16[720,512]{1,0:T(8,128)(2,1)S(1)}, bf16[720,512]{1,0:T(8,128)(2,1)S(1)}, u32[]{:S(2)}, u32[]{:S(2)}) collective-permute-start(bf16[720,512]{1,0:T(8,128)(2,1)S(1)} %slice.8), channel_id=1, source_target_pairs={{0,16},{4,20},{8,24},{12,28},{16,0},{20,4},{24,8},{28,12},{1,17},{... | collective-permute-start | bytes 2211848 | tf_op jit(solution)/shard_map/ppermute | solution.py:576
  96.9 1.6 collective-permute-start.24
  97.0 19.0 %collective-permute-start.23 = (bf16[720,512]{1,0:T(8,128)(2,1)S(1)}, bf16[720,512]{1,0:T(8,128)(2,1)S(1)}, u32[]{:S(2)}, u32[]{:S(2)}) collective-permute-start(bf16[720,512]{1,0:T(8,128)(2,1)S(1)} %slice.9), channel_id=1, source_target_pairs={{0,8},{4,12},{8,0},{12,4},{16,24},{20,28},{24,16},{28,20},{1,9},{5... | collective-permute-start | bytes 2211848 | tf_op jit(solution)/shard_map/ppermute | solution.py:576
  98.5 29.2 %collective-permute-start.32 = (bf16[768,640]{1,0:T(8,128)(2,1)S(1)}, bf16[768,640]{1,0:T(8,128)(2,1)S(1)}, u32[]{:S(2)}, u32[]{:S(2)}) collective-permute-start(bf16[768,640]{1,0:T(8,128)(2,1)S(1)} %shard_map.89.refs_1_), channel_id=1, source_target_pairs={{0,4},{4,0},{8,12},{12,8},{16,20},{20,16},{24,28},{28,24},{1,5},{5... | collective-permute-start | bytes 2949128 | tf_op jit(solution)/shard_map/ppermute | solution.py:576
  108.0 19.2 %collective-permute-start.31 = (bf16[768,384]{1,0:T(8,128)(2,1)S(1)}, bf16[768,384]{1,0:T(8,128)(2,1)S(1)}, u32[]{:S(2)}, u32[]{:S(2)}) collective-permute-start(bf16[768,384]{1,0:T(8,128)(2,1)S(1)} %get-tuple-element.149.refs_0_), channel_id=1, source_target_pairs={{0,4},{4,0},{8,12},{12,8},{16,20},{20,16},{24,28},{28,24},{1,5},{5... | collective-permute-start | bytes 1769480 | tf_op jit(solution)/shard_map/ppermute | solution.py:576
  110.2 17.0 %collective-permute-start.29 = (bf16[768,384]{1,0:T(8,128)(2,1)S(1)}, bf16[768,384]{1,0:T(8,128)(2,1)S(1)}, u32[]{:S(2)}, u32[]{:S(2)}) collective-permute-start(bf16[768,384]{1,0:T(8,128)(2,1)S(1)} %collective-permute-done.8.refs_0_), channel_id=1, source_target_pairs={{0,4},{4,0},{8,12},{12,8},{16,20},{20,16},{24,28},{28,24},{1,5},{5... | collective-permute-start | bytes 1769480 | tf_op jit(solution)/shard_map/ppermute | solution.py:576
  115.9 17.0 %collective-permute-start.30 = (bf16[768,640]{1,0:T(8,128)(2,1)S(1)}, bf16[768,640]{1,0:T(8,128)(2,1)S(1)}, u32[]{:S(2)}, u32[]{:S(2)}) collective-permute-start(bf16[768,640]{1,0:T(8,128)(2,1)S(1)} %collective-permute-done.18.refs_1_), channel_id=1, source_target_pairs={{0,4},{4,0},{8,12},{12,8},{16,20},{20,16},{24,28},{28,24},{1,5},{5... | collective-permute-start | bytes 2949128 | tf_op jit(solution)/shard_map/ppermute | solution.py:576
  127.1 11.2 %collective-permute-start.28 = (bf16[768,640]{1,0:T(8,128)(2,1)S(1)}, bf16[768,640]{1,0:T(8,128)(2,1)S(1)}, u32[]{:S(2)}, u32[]{:S(2)}) collective-permute-start(bf16[768,640]{1,0:T(8,128)(2,1)S(1)} %collective-permute-done.19.refs_1_), channel_id=1, source_target_pairs={{0,4},{4,0},{8,12},{12,8},{16,20},{20,16},{24,28},{28,24},{1,5},{5... | collective-permute-start | bytes 2949128 | tf_op jit(solution)/shard_map/ppermute | solution.py:576
  127.1 26.0 %collective-permute-start.25 = (bf16[768,640]{1,0:T(8,128)(2,1)S(1)}, bf16[768,640]{1,0:T(8,128)(2,1)S(1)}, u32[]{:S(2)}, u32[]{:S(2)}) collective-permute-start(bf16[768,640]{1,0:T(8,128)(2,1)S(1)} %collective-permute-done.19.refs_1_), channel_id=1, source_target_pairs={{0,1},{1,2},{2,3},{3,0},{4,5},{5,6},{6,7},{7,4},{8,9},{9,10},{10,1... | collective-permute-start | bytes 2949128 | tf_op jit(solution)/shard_map/ppermute | solution.py:583
  127.2 11.2 %collective-permute-start.27 = (bf16[768,384]{1,0:T(8,128)(2,1)S(1)}, bf16[768,384]{1,0:T(8,128)(2,1)S(1)}, u32[]{:S(2)}, u32[]{:S(2)}) collective-permute-start(bf16[768,384]{1,0:T(8,128)(2,1)S(1)} %collective-permute-done.11.refs_0_), channel_id=1, source_target_pairs={{0,4},{4,0},{8,12},{12,8},{16,20},{20,16},{24,28},{28,24},{1,5},{5... | collective-permute-start | bytes 1769480 | tf_op jit(solution)/shard_map/ppermute | solution.py:576
  127.7 16.1 %collective-permute-start.26 = (bf16[768,384]{1,0:T(8,128)(2,1)S(1)}, bf16[768,384]{1,0:T(8,128)(2,1)S(1)}, u32[]{:S(2)}, u32[]{:S(2)}) collective-permute-start(bf16[768,384]{1,0:T(8,128)(2,1)S(1)} %collective-permute-done.17.refs_0_), channel_id=1, source_target_pairs={{0,4},{4,0},{8,12},{12,8},{16,20},{20,16},{24,28},{28,24},{1,5},{5... | collective-permute-start | bytes 1769480 | tf_op jit(solution)/shard_map/ppermute | solution.py:576
  153.1 2.6 %collective-permute-start.33 = (bf16[768,640]{1,0:T(8,128)(2,1)S(1)}, bf16[768,640]{1,0:T(8,128)(2,1)S(1)}, u32[]{:S(2)}, u32[]{:S(2)}) collective-permute-start(bf16[768,640]{1,0:T(8,128)(2,1)S(1)} %collective-permute-done.25.refs_1_), channel_id=1, source_target_pairs={{0,4},{4,0},{8,12},{12,8},{16,20},{20,16},{24,28},{28,24},{1,5},{5... | collective-permute-start | bytes 2949128 | tf_op jit(solution)/shard_map/ppermute | solution.py:576
  161.7 1.3 collective-permute-start.34
  163.6 4.8 %collective-permute-start.35 = (f32[8,1536]{1,0:T(8,128)S(1)}, f32[8,1536]{1,0:T(8,128)S(1)}, u32[]{:S(2)}, u32[]{:S(2)}) collective-permute-start(f32[8,1536]{1,0:T(8,128)S(1)} %shard_map.96.refs_2_), channel_id=1, source_target_pairs={{0,1},{1,0},{2,3},{3,2},{4,5},{5,4},{6,7},{7,6},{8,9},{9,8},{10,11... | collective-permute-start | bytes 147464 | tf_op jit(solution)/shard_map/ppermute | solution.py:656
  163.7 7.4 %collective-permute-start.36 = (f32[8,1536]{1,0:T(8,128)S(1)}, f32[8,1536]{1,0:T(8,128)S(1)}, u32[]{:S(2)}, u32[]{:S(2)}) collective-permute-start(f32[8,1536]{1,0:T(8,128)S(1)} %shard_map.96.refs_2_), channel_id=1, source_target_pairs={{0,2},{1,3},{2,0},{3,1},{4,6},{5,7},{6,4},{7,5},{8,10},{9,11},{10,... | collective-permute-start | bytes 147464 | tf_op jit(solution)/shard_map/ppermute | solution.py:656
  163.8 7.3 %collective-permute-start.37 = (f32[8,1536]{1,0:T(8,128)S(1)}, f32[8,1536]{1,0:T(8,128)S(1)}, u32[]{:S(2)}, u32[]{:S(2)}) collective-permute-start(f32[8,1536]{1,0:T(8,128)S(1)} %shard_map.96.refs_2_), channel_id=1, source_target_pairs={{0,3},{1,2},{2,1},{3,0},{4,7},{5,6},{6,5},{7,4},{8,11},{9,10},{10,... | collective-permute-start | bytes 147464 | tf_op jit(solution)/shard_map/ppermute | solution.py:656
  175.3 19.0 %collective-permute-start.38 = (bf16[720,512]{1,0:T(8,128)(2,1)S(1)}, bf16[720,512]{1,0:T(8,128)(2,1)S(1)}, u32[]{:S(2)}, u32[]{:S(2)}) collective-permute-start(bf16[720,512]{1,0:T(8,128)(2,1)S(1)} %get-tuple-element.198), channel_id=1, source_target_pairs={{0,8},{4,12},{8,0},{12,4},{16,24},{20,28},{24,16},{28,20},{1,9},{5... | collective-permute-start | bytes 2211848 | tf_op jit(solution)/shard_map/ppermute | solution.py:576
  176.9 17.4 %collective-permute-start.39 = (bf16[720,512]{1,0:T(8,128)(2,1)S(1)}, bf16[720,512]{1,0:T(8,128)(2,1)S(1)}, u32[]{:S(2)}, u32[]{:S(2)}) collective-permute-start(bf16[720,512]{1,0:T(8,128)(2,1)S(1)} %get-tuple-element.199), channel_id=1, source_target_pairs={{0,16},{4,20},{8,24},{12,28},{16,0},{20,4},{24,8},{28,12},{1,17},{... | collective-permute-start | bytes 2211848 | tf_op jit(solution)/shard_map/ppermute | solution.py:576
  178.4 15.9 %collective-permute-start.40 = (bf16[64,720]{1,0:T(8,128)(2,1)S(1)}, bf16[64,720]{1,0:T(8,128)(2,1)S(1)}, u32[]{:S(2)}, u32[]{:S(2)}) collective-permute-start(bf16[64,720]{1,0:T(8,128)(2,1)S(1)} %get-tuple-element.207.mine_ref), channel_id=1, source_target_pairs={{0,8},{4,12},{8,0},{12,4},{16,24},{20,28},{24,16},{28,20},{1,9},{5... | collective-permute-start | bytes 276488 | tf_op jit(solution)/shard_map/ppermute | solution.py:576
  195.7 21.5 %collective-permute-start.42 = (bf16[720,512]{1,0:T(8,128)(2,1)S(1)}, bf16[720,512]{1,0:T(8,128)(2,1)S(1)}, u32[]{:S(2)}, u32[]{:S(2)}) collective-permute-start(bf16[720,512]{1,0:T(8,128)(2,1)S(1)} %get-tuple-element.224), channel_id=1, source_target_pairs={{0,16},{4,12},{8,24},{12,4},{16,0},{20,28},{24,8},{28,20},{1,17},{... | collective-permute-start | bytes 2211848 | tf_op jit(solution)/shard_map/ppermute | solution.py:580
  197.2 20.1 %collective-permute-start.43 = (bf16[720,512]{1,0:T(8,128)(2,1)S(1)}, bf16[720,512]{1,0:T(8,128)(2,1)S(1)}, u32[]{:S(2)}, u32[]{:S(2)}) collective-permute-start(bf16[720,512]{1,0:T(8,128)(2,1)S(1)} %get-tuple-element.213), channel_id=1, source_target_pairs={{0,8},{4,20},{8,0},{12,28},{16,24},{20,4},{24,16},{28,12},{1,9},{5... | collective-permute-start | bytes 2211848 | tf_op jit(solution)/shard_map/ppermute | solution.py:580
  199.3 18.0 %collective-permute-start.41 = (bf16[64,720]{1,0:T(8,128)(2,1)S(1)}, bf16[64,720]{1,0:T(8,128)(2,1)S(1)}, u32[]{:S(2)}, u32[]{:S(2)}) collective-permute-start(bf16[64,720]{1,0:T(8,128)(2,1)S(1)} %shard_map.99), channel_id=1, source_target_pairs={{0,16},{4,20},{8,24},{12,28},{16,0},{20,4},{24,8},{28,12},{1,17},{... | collective-permute-start | bytes 276488 | tf_op jit(solution)/shard_map/ppermute | solution.py:576
  199.8 25.2 %collective-permute-start.47 = (bf16[720,512]{1,0:T(8,128)(2,1)}, bf16[720,512]{1,0:T(8,128)(2,1)}, u32[]{:S(2)}, u32[]{:S(2)}) collective-permute-start(bf16[720,512]{1,0:T(8,128)(2,1)} %get-tuple-element.223), channel_id=1, source_target_pairs={{0,12},{4,16},{8,4},{12,24},{16,28},{20,0},{24,20},{28,8},{1,13},{... | collective-permute-start | bytes 2211848 | tf_op jit(solution)/shard_map/ppermute | solution.py:580
  199.8 25.2 %collective-permute-start.44 = (bf16[720,512]{1,0:T(8,128)(2,1)}, bf16[720,512]{1,0:T(8,128)(2,1)}, u32[]{:S(2)}, u32[]{:S(2)}) collective-permute-start(bf16[720,512]{1,0:T(8,128)(2,1)} %get-tuple-element.216), channel_id=1, source_target_pairs={{0,4},{4,0},{8,12},{12,8},{16,20},{20,16},{24,28},{28,24},{1,5},{5... | collective-permute-start | bytes 2211848 | tf_op jit(solution)/shard_map/ppermute | solution.py:576
  217.2 12.6 %collective-permute-start.45 = (bf16[720,512]{1,0:T(8,128)(2,1)}, bf16[720,512]{1,0:T(8,128)(2,1)}, u32[]{:S(2)}, u32[]{:S(2)}) collective-permute-start(bf16[720,512]{1,0:T(8,128)(2,1)} %get-tuple-element.217), channel_id=1, source_target_pairs={{0,20},{4,8},{8,28},{12,0},{16,4},{20,24},{24,12},{28,16},{1,21},{... | collective-permute-start | bytes 2211848 | tf_op jit(solution)/shard_map/ppermute | solution.py:580
  217.3 4.5 %collective-permute-start.46 = (f32[64,720]{1,0:T(8,128)S(1)}, f32[64,720]{1,0:T(8,128)S(1)}, u32[]{:S(2)}, u32[]{:S(2)}) collective-permute-start(f32[64,720]{1,0:T(8,128)S(1)} %convert_add_fusion), channel_id=1, source_target_pairs={{0,4},{4,0},{8,12},{12,8},{16,20},{20,16},{24,28},{28,24},{1,5},{5... | collective-permute-start | bytes 552968 | tf_op jit(solution)/shard_map/ppermute | solution.py:576

commit v16 on v14

--- a/solution.py
+++ b/solution.py
@@ -390,7 +390,7 @@
 def score(meta, at, own, sib, panels, width, acc=None, full=None, used=None, hots=None, extra=None):
     rows = own[0].shape[0]
     parts = len(own)
-    tile = 256
+    tile = 384
     half = rows // tile
     count, columns = panels.shape
     first, last = acc is None, used is not None and hots is None
@@ -432,7 +432,7 @@
         out_specs,
         out_shape,
         alias=alias,
-        room=16,
+        room=24,
         flops=2 * count * 2 * rows * width,
         moved=8 * count * 2 * rows + 8 * rows * width,
     )(*operands)

time: 231 us -> 234 us (1.013)
  local copies, waits for them, and re-layouts: 1.72 us -> 6.02 us
    ppermute x6, waiting for transfers between devices: 36.7 us -> 32.2 us  [onward(): lax.ppermute(value, 'rot', [(i, (i + 1) % turns) for i in range(turns)])]
    unnamed x6 -> x10, local copies, waits for them, and re-layouts: 0.29 us -> 4.59 us
    ppermute x3, waiting for transfers between devices: 3.03 us -> 5.47 us  [two_by_two(): lax.ppermute(pair, 'rot', [(i, i ^ apart) for i in range(turns)])]
  transfers between devices with their start and end apart: 48 -> 48, of which waited for: 27 -> 26; matrix products, arithmetic and copies ran while one was open for 2% -> 2% of each run, Pallas kernels for 24% -> 24%
where the time goes in v16:
time: 234 us
  waiting for transfers between devices  112 us (48%)
  Pallas kernels  70.6 us (30%)
  starting transfers between devices  37.6 us (16%)
  other arithmetic  6.8 us (3%)
  local copies, waits for them, and re-layouts  6.02 us (3%)
    ppermute x35, waiting for transfers between devices, across(): return lax.ppermute(value, 'dom', [(i, i ^ apart) for i in range(dom)])  67 us
    ppermute x6, waiting for transfers between devices, onward(): lax.ppermute(value, 'rot', [(i, (i + 1) % turns) for i in range(turns)])  32.2 us
    ppermute x35, starting transfers between devices, across(): return lax.ppermute(value, 'dom', [(i, i ^ apart) for i in range(dom)])  27.2 us
    pallas_call x5, Pallas kernels, score(): call(functools.partial(score_body, parts, used, first, last), (2 * half,)...  26.9 us
    pallas_call x2, Pallas kernels, class_part(): call(functools.partial(class_body, kind, steps), (steps,), in_specs, out_...  15 us
    pallas_call x2, Pallas kernels, energy(): call(functools.partial(far_energy_body if last else near_energy_body, bin...  7.21 us
    ppermute x4, waiting for transfers between devices, by_core(): return lax.ppermute(value, 'dom', pairs)  7.12 us
    pallas_call x1, Pallas kernels, pack_next(): call(functools.partial(pack_next_body, cap, dom), (1,), [pl.BlockSpec((1,...  5.9 us
  transfers between devices with their start and end apart: 48, of which 26 were waited for; matrix products, arithmetic and copies ran while one was open for 2% of the time, Pallas kernels for 24%

profile of v16, /device:TPU:0, one launch (start us, length us, event | category | flops | bytes accessed | tf_op | source)
XLA Modules:
  0.0 233.7 jit_solution(9873025535482324209)
XLA Ops:
  1.2 0.7 add_select_fusion.slot_ref
  2.0 5.8 %shard_map.85 = (bf16[208,384]{1,0:T(8,128)(2,1)S(1)}, bf16[208,384]{1,0:T(8,128)(2,1)S(1)}, bf16[208,384]{1,0:T(8,128)(2,1)S(1)}, bf16[208,384]{1,0:T(8,128)(2,...) custom-call(s32[10]{0:T(128)S(1)} %stack.43.meta, ...), custom_call_target="tpu_custom_call" | custom-call | flops 113246208 | bytes 147456 | tf_op jit(solution)/shard_map/pallas_call | solution.py:132
  7.7 3.6 %collective-permute-start = (bf16[208,384]{1,0:T(8,128)(2,1)S(1)}, bf16[208,384]{1,0:T(8,128)(2,1)S(1)}, u32[]{:S(2)}, u32[]{:S(2)}) collective-permute-start(bf16[208,384]{1,0:T(8,128)(2,1)S(1)} %get-tuple-element.105), channel_id=1, source_target_pairs={{0,24},{4,28},{8,16},{12,20},{16,8},{20,12},{24,0},{28,4},{1,25},{... | collective-permute-start | bytes 479240 | tf_op jit(solution)/shard_map/ppermute | solution.py:576
  11.4 1.6 collective-permute-start.2
  13.1 1.5 collective-permute-start.3
  14.7 1.2 constant_dynamic-slice_fusion
  17.0 2.3 collective-permute-done.1.refs_1_
  19.6 5.9 %shard_map.86 = (bf16[192,640]{1,0:T(8,128)(2,1)S(1)}, bf16[192,640]{1,0:T(8,128)(2,1)S(1)}, bf16[192,640]{1,0:T(8,128)(2,1)S(1)}, bf16[192,640]{1,0:T(8,128)(2,...) custom-call(s32[10]{0:T(128)S(1)} %stack.43.meta, ...), custom_call_target="tpu_custom_call" | custom-call | flops 188743680 | bytes 245760 | tf_op jit(solution)/shard_map/pallas_call | solution.py:152
  26.5 3.5 %shard_map.87 = (bf16[768,384]{1,0:T(8,128)(2,1)S(1)}, bf16[192,768]{1,0:T(8,128)(2,1)S(1)}, bf16[768,1536]{1,0:T(8,128)(2,1)S(1)}, bf16[768,192]{1,0:T(8,128)(2,1)S(1)}) custom-call(s32[10]{0:T(128)S(1)} %stack.43.meta, bf16[208,384]{1,0:T(8,128)(2,1)S(1)} %collective-permute-done.refs_0_, bf16[208,384]{1,0:T(8,128)(2,1)S(1)} %collective-permute-done.1.refs_1_, ...), custom_call_target="tpu_custom_call" | custom-call | flops 56623104 | bytes 73728 | tf_op jit(solution)/shard_map/pallas_call | solution.py:212
  30.0 2.0 collective-permute-start.8
  32.0 1.8 collective-permute-start.10
  33.8 0.7 collective-permute-start.9
  34.5 2.1 shard_map.88
  36.6 4.5 %collective-permute-done.10.refs_1_ = bf16[192,640]{1,0:T(8,128)(2,1)S(1)} collective-permute-done((bf16[192,640]{1,0:T(8,128)(2,1)S(1)}, bf16[192,640]{1,0:T(8,128)(2,1)S(1)}, u32[]{:S(2)}, u32[]{:S(2)}) %collective-permute-start.10) | collective-permute-done | bytes 245792 | tf_op jit(solution)/shard_map/ppermute | solution.py:576
  41.1 5.4 %collective-permute-done.9.refs_0_ = bf16[192,640]{1,0:T(8,128)(2,1)S(1)} collective-permute-done((bf16[192,640]{1,0:T(8,128)(2,1)S(1)}, bf16[192,640]{1,0:T(8,128)(2,1)S(1)}, u32[]{:S(2)}, u32[]{:S(2)}) %collective-permute-start.9) | collective-permute-done | bytes 245792 | tf_op jit(solution)/shard_map/ppermute | solution.py:576
  46.5 1.1 collective-permute-done.8.refs_0_
  48.1 1.3 collective-permute-start.12
  49.4 1.5 collective-permute-start.13
  50.9 1.0 collective-permute-start.15
  51.8 5.1 %collective-permute-done.12.refs_2_ = bf16[192,640]{1,0:T(8,128)(2,1)S(1)} collective-permute-done((bf16[192,640]{1,0:T(8,128)(2,1)S(1)}, bf16[192,640]{1,0:T(8,128)(2,1)S(1)}, u32[]{:S(2)}, u32[]{:S(2)}) %collective-permute-start.12) | collective-permute-done | bytes 245792 | tf_op jit(solution)/shard_map/ppermute | solution.py:576
  56.9 1.3 collective-permute-done.13.refs_3_
  58.3 1.6 collective-permute-done.14.refs_4_
  59.9 1.2 collective-permute-done.15.refs_5_
  61.1 2.9 %shard_map.89.refs_1_ = bf16[768,640]{1,0:T(8,128)(2,1)S(1)} custom-call(s32[10]{0:T(128)S(1)} %stack.43.meta, bf16[192,640]{1,0:T(8,128)(2,1)S(1)} %collective-permute-done.9.refs_0_, bf16[192,640]{1,0:T(8,128)(2,1)S(1)} %collective-permute-done.10.refs_1_, bf16[192,640]{1,0:T(8,128)(2,1)S(1)} %collective-permute-done.12.refs_2_, ...), custom_call_target="tpu_custom_call" | custom-call | flops 94371840 | bytes 122880 | tf_op jit(solution)/shard_map/pallas_call | solution.py:231
  64.1 1.3 collective-permute-start.20
  65.3 1.5 collective-permute-start.21
  67.8 25.5 %collective-permute-done.18.refs_1_ = bf16[768,640]{1,0:T(8,128)(2,1)S(1)} collective-permute-done((bf16[768,640]{1,0:T(8,128)(2,1)S(1)}, bf16[768,640]{1,0:T(8,128)(2,1)S(1)}, u32[]{:S(2)}, u32[]{:S(2)}) %collective-permute-start.18) | collective-permute-done | bytes 983072 | tf_op jit(solution)/shard_map/ppermute | solution.py:583
  93.3 5.8 %collective-permute-done.20.refs_0_ = bf16[720,1024]{1,0:T(8,128)(2,1)S(1)} collective-permute-done((bf16[720,1024]{1,0:T(8,128)(2,1)S(1)}, bf16[720,1024]{1,0:T(8,128)(2,1)S(1)}, u32[]{:S(2)}, u32[]{:S(2)}) %collective-permute-start.20) | collective-permute-done | bytes 1474592 | tf_op jit(solution)/shard_map/ppermute | solution.py:576
  99.2 0.9 collective-permute-start.22
  100.5 1.2 collective-permute-start.23
  101.9 4.0 %collective-permute-done.17.refs_0_ = bf16[768,384]{1,0:T(8,128)(2,1)S(1)} collective-permute-done((bf16[768,384]{1,0:T(8,128)(2,1)S(1)}, bf16[768,384]{1,0:T(8,128)(2,1)S(1)}, u32[]{:S(2)}, u32[]{:S(2)}) %collective-permute-start.17) | collective-permute-done | bytes 589856 | tf_op jit(solution)/shard_map/ppermute | solution.py:583
  105.9 11.9 %collective-permute-done.22.refs_2_ = bf16[720,512]{1,0:T(8,128)(2,1)S(1)} collective-permute-done((bf16[720,512]{1,0:T(8,128)(2,1)S(1)}, bf16[720,512]{1,0:T(8,128)(2,1)S(1)}, u32[]{:S(2)}, u32[]{:S(2)}) %collective-permute-start.22) | collective-permute-done | bytes 737312 | tf_op jit(solution)/shard_map/ppermute | solution.py:576
  117.9 1.3 collective-permute-done.23.refs_3_
  119.2 5.2 %shard_map.90 = (bf16[720,4096]{1,0:T(8,128)(2,1)S(1)}, bf16[720,192]{1,0:T(8,128)(2,1)S(1)}) custom-call(s32[10]{0:T(128)S(1)} %stack.43.meta, bf16[720,1024]{1,0:T(8,128)(2,1)S(1)} %collective-permute-done.20.refs_0_, bf16[720,1024]{1,0:T(8,128)(2,1)S(1)} %collective-permute-done.21.refs_1_, ...), custom_call_target="tpu_custom_call", output_to_operand_aliasing={{0}: (8, {})} | custom-call | flops 212336640 | bytes 552960 | tf_op jit(solution)/shard_map/pallas_call | solution.py:328
  124.3 1.5 collective-permute-done.19.refs_1_
  126.7 5.3 %shard_map.91 = (f32[720,1536]{1,0:T(8,128)S(1)}, bf16[1536,4096]{1,0:T(8,128)(2,1)S(1)}) custom-call(s32[10]{0:T(128)S(1)} %stack.43.meta, bf16[768,384]{1,0:T(8,128)(2,1)S(1)} %get-tuple-element.141.refs_0_, bf16[768,640]{1,0:T(8,128)(2,1)S(1)} %shard_map.89.refs_1_, bf16[768,384]{1,0:T(8,128)(2,1)S(1)} %collective-permute-done.31.refs_2_, ...), custom_call_target="tpu_custom_call" | custom-call | flops 141557760 | bytes 946176 | tf_op jit(solution)/shard_map/pallas_call | solution.py:428
  132.0 5.6 %shard_map.92 = (f32[720,1536]{1,0:T(8,128)S(1)}, bf16[1536,4096]{1,0:T(8,128)(2,1)S(1)}) custom-call(s32[10]{0:T(128)S(1)} %stack.43.meta, bf16[768,384]{1,0:T(8,128)(2,1)S(1)} %collective-permute-done.8.refs_0_, bf16[768,640]{1,0:T(8,128)(2,1)S(1)} %collective-permute-done.18.refs_1_, ...), custom_call_target="tpu_custom_call", output_to_operand_aliasing={{0}: (6, {}), {1}: (7, {})} | custom-call | flops 141557760 | bytes 946176 | tf_op jit(solution)/shard_map/pallas_call | solution.py:428
  137.7 5.6 %shard_map.93 = (f32[720,1536]{1,0:T(8,128)S(1)}, bf16[1536,4096]{1,0:T(8,128)(2,1)S(1)}) custom-call(s32[10]{0:T(128)S(1)} %stack.43.meta, bf16[768,384]{1,0:T(8,128)(2,1)S(1)} %collective-permute-done.11.refs_0_, bf16[768,640]{1,0:T(8,128)(2,1)S(1)} %collective-permute-done.19.refs_1_, ...), custom_call_target="tpu_custom_call", output_to_operand_aliasing={{0}: (6, {}), {1}: (7, {})} | custom-call | flops 141557760 | bytes 946176 | tf_op jit(solution)/shard_map/pallas_call | solution.py:428
  143.4 2.0 copy-done
  145.4 2.3 copy-done.1
  147.7 4.5 %shard_map.94.refs_5_ = f32[720,1536]{1,0:T(8,128)S(1)} custom-call(s32[10]{0:T(128)S(1)} %stack.43.meta, bf16[768,384]{1,0:T(8,128)(2,1)S(1)} %collective-permute-done.17.refs_0_, bf16[768,384]{1,0:T(8,128)(2,1)S(1)} %collective-permute-done.26.refs_1_.refs_2_, ...), custom_call_target="tpu_custom_call", output_to_operand_aliasing={{}: (4, {})} | custom-call | flops 141557760 | bytes 946176 | tf_op jit(solution)/shard_map/pallas_call | solution.py:428
  152.5 2.4 %collective-permute-done.33.refs_3_ = bf16[768,640]{1,0:T(8,128)(2,1)S(1)} collective-permute-done((bf16[768,640]{1,0:T(8,128)(2,1)S(1)}, bf16[768,640]{1,0:T(8,128)(2,1)S(1)}, u32[]{:S(2)}, u32[]{:S(2)}) %collective-permute-start.33) | collective-permute-done | bytes 983072 | tf_op jit(solution)/shard_map/ppermute | solution.py:576
  154.9 5.8 %shard_map.95 = (f32[720,1536]{1,0:T(8,128)S(1)}, f32[8,1536]{1,0:T(8,128)S(1)}, bf16[1536,4096]{1,0:T(8,128)(2,1)S(1)}) custom-call(s32[10]{0:T(128)S(1)} %stack.43.meta, bf16[768,384]{1,0:T(8,128)(2,1)S(1)} %collective-permute-done.17.refs_0_, bf16[768,640]{1,0:T(8,128)(2,1)S(1)} %collective-permute-done.25.refs_1_, ...), custom_call_target="tpu_custom_call", output_to_operand_aliasing={{0}: (6, {}), {2}: (7, {})} | custom-call | flops 141557760 | bytes 946176 | tf_op jit(solution)/shard_map/pallas_call | solution.py:428
  160.9 1.1 collective-permute-done.34.other_ref
  162.8 3.7 %collective-permute-start.36 = (f32[8,1536]{1,0:T(8,128)S(1)}, f32[8,1536]{1,0:T(8,128)S(1)}, u32[]{:S(2)}, u32[]{:S(2)}) collective-permute-start(f32[8,1536]{1,0:T(8,128)S(1)} %shard_map.96.refs_2_), channel_id=1, source_target_pairs={{0,2},{1,3},{2,0},{3,1},{4,6},{5,7},{6,4},{7,5},{8,10},{9,11},{10,... | collective-permute-start | bytes 147464 | tf_op jit(solution)/shard_map/ppermute | solution.py:655
  167.0 2.7 %collective-permute-done.36.refs_4_ = f32[8,1536]{1,0:T(8,128)S(1)} collective-permute-done((f32[8,1536]{1,0:T(8,128)S(1)}, f32[8,1536]{1,0:T(8,128)S(1)}, u32[]{:S(2)}, u32[]{:S(2)}) %collective-permute-start.36) | collective-permute-done | bytes 49184 | tf_op jit(solution)/shard_map/ppermute | solution.py:655
  169.7 2.7 %collective-permute-done.37.refs_5_ = f32[8,1536]{1,0:T(8,128)S(1)} collective-permute-done((f32[8,1536]{1,0:T(8,128)S(1)}, f32[8,1536]{1,0:T(8,128)S(1)}, u32[]{:S(2)}, u32[]{:S(2)}) %collective-permute-start.37) | collective-permute-done | bytes 49184 | tf_op jit(solution)/shard_map/ppermute | solution.py:655
  172.4 4.5 %shard_map.97 = (bf16[720,512]{1,0:T(8,128)(2,1)S(1)}, bf16[720,512]{1,0:T(8,128)(2,1)S(1)}, bf16[720,1536]{1,0:T(8,128)(2,1)S(1)}, f32[1,768]{1,0:T(1,128)S(1)}, bf16[64,720]{1,0:T(8,128)(2,1)S(1)}) custom-call(s32[10]{0:T(128)S(1)} %stack.43.meta, f32[720,1536]{1,0:T(8,128)S(1)} %get-tuple-element.179.refs_0_, ...), custom_call_target="tpu_custom_call" | custom-call | flops 141557760 | bytes 657408 | tf_op jit(solution)/shard_map/pallas_call | solution.py:516
  176.9 0.7 collective-permute-start.38
  177.6 1.4 collective-permute-start.39
  179.1 1.5 collective-permute-start.40
  180.5 10.5 %shard_map.98 = (bf16[720,512]{1,0:T(8,128)(2,1)S(1)}, bf16[720,512]{1,0:T(8,128)(2,1)}, bf16[720,512]{1,0:T(8,128)(2,1)}, f32[720,512]{1,0:T(8,128)S(1)}, f32[7...) custom-call(s32[10]{0:T(128)S(1)} %stack.43.meta, bf16[720,1536]{1,0:T(8,128)(2,1)S(1)} %get-tuple-element.184.refs_0_, ...), custom_call_target="tpu_custom_call" | custom-call | flops 424673280 | bytes 1419264 | tf_op jit(solution)/shard_map/pallas_call | solution.py:516
  191.1 5.0 %collective-permute-done.40.other_ref = bf16[64,720]{1,0:T(8,128)(2,1)S(1)} collective-permute-done((bf16[64,720]{1,0:T(8,128)(2,1)S(1)}, bf16[64,720]{1,0:T(8,128)(2,1)S(1)}, u32[]{:S(2)}, u32[]{:S(2)}) %collective-permute-start.40) | collective-permute-done | bytes 92192 | tf_op jit(solution)/shard_map/ppermute | solution.py:576
  196.0 1.4 fusion.3
  197.4 1.5 collective-permute-start.42
  200.1 0.7 collective-permute-start.41
  200.7 1.5 collective-permute-start.44
  202.3 16.7 %collective-permute-done.41 = bf16[64,720]{1,0:T(8,128)(2,1)S(1)} collective-permute-done((bf16[64,720]{1,0:T(8,128)(2,1)S(1)}, bf16[64,720]{1,0:T(8,128)(2,1)S(1)}, u32[]{:S(2)}, u32[]{:S(2)}) %collective-permute-start.41) | collective-permute-done | bytes 92192 | tf_op jit(solution)/shard_map/ppermute | solution.py:576
  219.0 0.8 collective-permute-start.46
  220.4 2.3 shard_map.100
  222.7 0.9 maximum_select_fusion
  223.6 1.7 collective-permute-done.47
  225.3 5.4 %collective-permute-done.45 = bf16[720,512]{1,0:T(8,128)(2,1)} collective-permute-done((bf16[720,512]{1,0:T(8,128)(2,1)}, bf16[720,512]{1,0:T(8,128)(2,1)}, u32[]{:S(2)}, u32[]{:S(2)}) %collective-permute-start.45) | collective-permute-done | bytes 737312 | tf_op jit(solution)/shard_map/ppermute | solution.py:580
  230.7 2.9 %add_dynamic-update-slice_fusion = f32[1440,512]{1,0:T(8,128)} fusion(f32[1440,512]{1,0:T(8,128)} %shard_map.100, s32[]{:T(128)S(6)} %select_n.67, bf16[720,512]{1,0:T(8,128)(2,1)} %collective-permute-done.47, bf16[720,512]{1,0:T(8,128)(2,1)} %collective-permute-done.45, bf16[720,512]{1,0:T(8,128)(2,1)} %collective-permute-done.44), kind=kLoop, calls=%fused_computation.7 | loop fusion | flops 1843200 | bytes 3686404 | tf_op jit(solution)/shard_map/dynamic_update_slice | solution.py:684
  (70 shorter events, 9.8 us)
Async XLA Ops:
  0.6 14.0 %collective-permute-start.7 = (bf16[1440,512]{1,0:T(8,128)(2,1)}, bf16[1440,512]{1,0:T(8,128)(2,1)}, u32[]{:S(2)}, u32[]{:S(2)}) collective-permute-start(bf16[1440,512]{1,0:T(8,128)(2,1)} %param.11), channel_id=1, source_target_pairs={{0,4},{4,0},{8,12},{12,8},{16,20},{20,16},{24,28},{28,24},{1,5},{5... | collective-permute-start | bytes 4423688 | tf_op jit(solution)/shard_map/ppermute | solution.py:576
  2.0 12.6 %copy-start.4 = (bf16[1440,512]{1,0:T(8,128)(2,1)S(1)}, bf16[1440,512]{1,0:T(8,128)(2,1)}, u32[]{:S(2)}) copy-start(bf16[1440,512]{1,0:T(8,128)(2,1)} %param.11) | copy-start | bytes 4423684
  7.7 8.6 %collective-permute-start = (bf16[208,384]{1,0:T(8,128)(2,1)S(1)}, bf16[208,384]{1,0:T(8,128)(2,1)S(1)}, u32[]{:S(2)}, u32[]{:S(2)}) collective-permute-start(bf16[208,384]{1,0:T(8,128)(2,1)S(1)} %get-tuple-element.105), channel_id=1, source_target_pairs={{0,24},{4,28},{8,16},{12,20},{16,8},{20,12},{24,0},{28,4},{1,25},{... | collective-permute-start | bytes 479240 | tf_op jit(solution)/shard_map/ppermute | solution.py:576
  11.3 8.0 %collective-permute-start.1 = (bf16[208,384]{1,0:T(8,128)(2,1)S(1)}, bf16[208,384]{1,0:T(8,128)(2,1)S(1)}, u32[]{:S(2)}, u32[]{:S(2)}) collective-permute-start(bf16[208,384]{1,0:T(8,128)(2,1)S(1)} %get-tuple-element.106), channel_id=1, source_target_pairs={{0,28},{4,24},{8,20},{12,16},{16,12},{20,8},{24,4},{28,0},{1,29},{... | collective-permute-start | bytes 479240 | tf_op jit(solution)/shard_map/ppermute | solution.py:576
  11.4 14.2 %collective-permute-start.2 = (bf16[208,384]{1,0:T(8,128)(2,1)S(1)}, bf16[208,384]{1,0:T(8,128)(2,1)S(1)}, u32[]{:S(2)}, u32[]{:S(2)}) collective-permute-start(bf16[208,384]{1,0:T(8,128)(2,1)S(1)} %get-tuple-element.107), channel_id=1, source_target_pairs={{0,16},{4,20},{8,24},{12,28},{16,0},{20,4},{24,8},{28,12},{1,17},{... | collective-permute-start | bytes 479240 | tf_op jit(solution)/shard_map/ppermute | solution.py:576
  13.1 12.6 %collective-permute-start.3 = (bf16[208,384]{1,0:T(8,128)(2,1)S(1)}, bf16[208,384]{1,0:T(8,128)(2,1)S(1)}, u32[]{:S(2)}, u32[]{:S(2)}) collective-permute-start(bf16[208,384]{1,0:T(8,128)(2,1)S(1)} %get-tuple-element.108), channel_id=1, source_target_pairs={{0,8},{4,12},{8,0},{12,4},{16,24},{20,28},{24,16},{28,20},{1,9},{5... | collective-permute-start | bytes 479240 | tf_op jit(solution)/shard_map/ppermute | solution.py:576
  14.6 11.6 %collective-permute-start.4 = (bf16[208,384]{1,0:T(8,128)(2,1)S(1)}, bf16[208,384]{1,0:T(8,128)(2,1)S(1)}, u32[]{:S(2)}, u32[]{:S(2)}) collective-permute-start(bf16[208,384]{1,0:T(8,128)(2,1)S(1)} %get-tuple-element.109), channel_id=1, source_target_pairs={{0,20},{4,16},{8,28},{12,24},{16,4},{20,0},{24,12},{28,8},{1,21},{... | collective-permute-start | bytes 479240 | tf_op jit(solution)/shard_map/ppermute | solution.py:576
  16.4 9.9 %collective-permute-start.5 = (bf16[208,384]{1,0:T(8,128)(2,1)S(1)}, bf16[208,384]{1,0:T(8,128)(2,1)S(1)}, u32[]{:S(2)}, u32[]{:S(2)}) collective-permute-start(bf16[208,384]{1,0:T(8,128)(2,1)S(1)} %get-tuple-element.110), channel_id=1, source_target_pairs={{0,12},{4,8},{8,4},{12,0},{16,28},{20,24},{24,20},{28,16},{1,13},{... | collective-permute-start | bytes 479240 | tf_op jit(solution)/shard_map/ppermute | solution.py:576
  19.3 6.9 %collective-permute-start.6 = (bf16[208,384]{1,0:T(8,128)(2,1)S(1)}, bf16[208,384]{1,0:T(8,128)(2,1)S(1)}, u32[]{:S(2)}, u32[]{:S(2)}) collective-permute-start(bf16[208,384]{1,0:T(8,128)(2,1)S(1)} %get-tuple-element.111), channel_id=1, source_target_pairs={{0,4},{4,0},{8,12},{12,8},{16,20},{20,16},{24,28},{28,24},{1,5},{5... | collective-permute-start | bytes 479240 | tf_op jit(solution)/shard_map/ppermute | solution.py:576
  25.5 1.0 copy-start.2
  25.5 1.0 copy-start.3
  30.0 17.6 %collective-permute-start.8 = (bf16[768,384]{1,0:T(8,128)(2,1)S(1)}, bf16[768,384]{1,0:T(8,128)(2,1)S(1)}, u32[]{:S(2)}, u32[]{:S(2)}) collective-permute-start(bf16[768,384]{1,0:T(8,128)(2,1)S(1)} %get-tuple-element.141.refs_0_), channel_id=1, source_target_pairs={{0,1},{1,2},{2,3},{3,0},{4,5},{5,6},{6,7},{7,4},{8,9},{9,10},{10,1... | collective-permute-start | bytes 1769480 | tf_op jit(solution)/shard_map/ppermute | solution.py:583
  32.0 9.1 %collective-permute-start.10 = (bf16[192,640]{1,0:T(8,128)(2,1)S(1)}, bf16[192,640]{1,0:T(8,128)(2,1)S(1)}, u32[]{:S(2)}, u32[]{:S(2)}) collective-permute-start(bf16[192,640]{1,0:T(8,128)(2,1)S(1)} %get-tuple-element.143), channel_id=1, source_target_pairs={{0,28},{4,24},{8,20},{12,16},{16,12},{20,8},{24,4},{28,0},{1,29},{... | collective-permute-start | bytes 737288 | tf_op jit(solution)/shard_map/ppermute | solution.py:576
  33.8 12.6 %collective-permute-start.9 = (bf16[192,640]{1,0:T(8,128)(2,1)S(1)}, bf16[192,640]{1,0:T(8,128)(2,1)S(1)}, u32[]{:S(2)}, u32[]{:S(2)}) collective-permute-start(bf16[192,640]{1,0:T(8,128)(2,1)S(1)} %get-tuple-element.142), channel_id=1, source_target_pairs={{0,24},{4,28},{8,16},{12,20},{16,8},{20,12},{24,0},{28,4},{1,25},{... | collective-permute-start | bytes 737288 | tf_op jit(solution)/shard_map/ppermute | solution.py:576
  47.6 16.5 %collective-permute-start.11 = (bf16[768,384]{1,0:T(8,128)(2,1)S(1)}, bf16[768,384]{1,0:T(8,128)(2,1)S(1)}, u32[]{:S(2)}, u32[]{:S(2)}) collective-permute-start(bf16[768,384]{1,0:T(8,128)(2,1)S(1)} %collective-permute-done.8.refs_0_), channel_id=1, source_target_pairs={{0,1},{1,2},{2,3},{3,0},{4,5},{5,6},{6,7},{7,4},{8,9},{9,10},{10,1... | collective-permute-start | bytes 1769480 | tf_op jit(solution)/shard_map/ppermute | solution.py:583
  48.1 8.9 %collective-permute-start.12 = (bf16[192,640]{1,0:T(8,128)(2,1)S(1)}, bf16[192,640]{1,0:T(8,128)(2,1)S(1)}, u32[]{:S(2)}, u32[]{:S(2)}) collective-permute-start(bf16[192,640]{1,0:T(8,128)(2,1)S(1)} %get-tuple-element.150), channel_id=1, source_target_pairs={{0,16},{4,20},{8,24},{12,28},{16,0},{20,4},{24,8},{28,12},{1,17},{... | collective-permute-start | bytes 737288 | tf_op jit(solution)/shard_map/ppermute | solution.py:576
  49.4 8.9 %collective-permute-start.13 = (bf16[192,640]{1,0:T(8,128)(2,1)S(1)}, bf16[192,640]{1,0:T(8,128)(2,1)S(1)}, u32[]{:S(2)}, u32[]{:S(2)}) collective-permute-start(bf16[192,640]{1,0:T(8,128)(2,1)S(1)} %get-tuple-element.151), channel_id=1, source_target_pairs={{0,8},{4,12},{8,0},{12,4},{16,24},{20,28},{24,16},{28,20},{1,9},{5... | collective-permute-start | bytes 737288 | tf_op jit(solution)/shard_map/ppermute | solution.py:576
  50.9 9.0 %collective-permute-start.14 = (bf16[192,640]{1,0:T(8,128)(2,1)S(1)}, bf16[192,640]{1,0:T(8,128)(2,1)S(1)}, u32[]{:S(2)}, u32[]{:S(2)}) collective-permute-start(bf16[192,640]{1,0:T(8,128)(2,1)S(1)} %get-tuple-element.152), channel_id=1, source_target_pairs={{0,20},{4,16},{8,28},{12,24},{16,4},{20,0},{24,12},{28,8},{1,21},{... | collective-permute-start | bytes 737288 | tf_op jit(solution)/shard_map/ppermute | solution.py:576
  50.9 10.2 %collective-permute-start.15 = (bf16[192,640]{1,0:T(8,128)(2,1)S(1)}, bf16[192,640]{1,0:T(8,128)(2,1)S(1)}, u32[]{:S(2)}, u32[]{:S(2)}) collective-permute-start(bf16[192,640]{1,0:T(8,128)(2,1)S(1)} %get-tuple-element.153), channel_id=1, source_target_pairs={{0,12},{4,8},{8,4},{12,0},{16,28},{20,24},{24,20},{28,16},{1,13},{... | collective-permute-start | bytes 737288 | tf_op jit(solution)/shard_map/ppermute | solution.py:576
  56.9 4.2 %collective-permute-start.16 = (bf16[192,640]{1,0:T(8,128)(2,1)S(1)}, bf16[192,640]{1,0:T(8,128)(2,1)S(1)}, u32[]{:S(2)}, u32[]{:S(2)}) collective-permute-start(bf16[192,640]{1,0:T(8,128)(2,1)S(1)} %get-tuple-element.154), channel_id=1, source_target_pairs={{0,4},{4,0},{8,12},{12,8},{16,20},{20,16},{24,28},{28,24},{1,5},{5... | collective-permute-start | bytes 737288 | tf_op jit(solution)/shard_map/ppermute | solution.py:576
  64.1 35.0 %collective-permute-start.20 = (bf16[720,1024]{1,0:T(8,128)(2,1)S(1)}, bf16[720,1024]{1,0:T(8,128)(2,1)S(1)}, u32[]{:S(2)}, u32[]{:S(2)}) collective-permute-start(bf16[720,1024]{1,0:T(8,128)(2,1)S(1)} %pad_maximum_fusion.refs_0_), channel_id=1, source_target_pairs={{0,8},{4,12},{8,0},{12,4},{16,24},{20,28},{24,16},{28,20},{1,9},{5... | collective-permute-start | bytes 4423688 | tf_op jit(solution)/shard_map/ppermute | solution.py:576
  65.3 35.1 %collective-permute-start.21 = (bf16[720,1024]{1,0:T(8,128)(2,1)S(1)}, bf16[720,1024]{1,0:T(8,128)(2,1)S(1)}, u32[]{:S(2)}, u32[]{:S(2)}) collective-permute-start(bf16[720,1024]{1,0:T(8,128)(2,1)S(1)} %pad_maximum_fusion.refs_0_), channel_id=1, source_target_pairs={{0,16},{4,20},{8,24},{12,28},{16,0},{20,4},{24,8},{28,12},{1,17},{... | collective-permute-start | bytes 4423688 | tf_op jit(solution)/shard_map/ppermute | solution.py:576
  66.8 26.4 %collective-permute-start.18 = (bf16[768,640]{1,0:T(8,128)(2,1)S(1)}, bf16[768,640]{1,0:T(8,128)(2,1)S(1)}, u32[]{:S(2)}, u32[]{:S(2)}) collective-permute-start(bf16[768,640]{1,0:T(8,128)(2,1)S(1)} %shard_map.89.refs_1_), channel_id=1, source_target_pairs={{0,1},{1,2},{2,3},{3,0},{4,5},{5,6},{6,7},{7,4},{8,9},{9,10},{10,1... | collective-permute-start | bytes 2949128 | tf_op jit(solution)/shard_map/ppermute | solution.py:583
  67.3 38.7 %collective-permute-start.17 = (bf16[768,384]{1,0:T(8,128)(2,1)S(1)}, bf16[768,384]{1,0:T(8,128)(2,1)S(1)}, u32[]{:S(2)}, u32[]{:S(2)}) collective-permute-start(bf16[768,384]{1,0:T(8,128)(2,1)S(1)} %collective-permute-done.11.refs_0_), channel_id=1, source_target_pairs={{0,1},{1,2},{2,3},{3,0},{4,5},{5,6},{6,7},{7,4},{8,9},{9,10},{10,1... | collective-permute-start | bytes 1769480 | tf_op jit(solution)/shard_map/ppermute | solution.py:583
  93.3 32.5 %collective-permute-start.19 = (bf16[768,640]{1,0:T(8,128)(2,1)S(1)}, bf16[768,640]{1,0:T(8,128)(2,1)S(1)}, u32[]{:S(2)}, u32[]{:S(2)}) collective-permute-start(bf16[768,640]{1,0:T(8,128)(2,1)S(1)} %collective-permute-done.18.refs_1_), channel_id=1, source_target_pairs={{0,1},{1,2},{2,3},{3,0},{4,5},{5,6},{6,7},{7,4},{8,9},{9,10},{10,1... | collective-permute-start | bytes 2949128 | tf_op jit(solution)/shard_map/ppermute | solution.py:583
  99.2 18.7 %collective-permute-start.22 = (bf16[720,512]{1,0:T(8,128)(2,1)S(1)}, bf16[720,512]{1,0:T(8,128)(2,1)S(1)}, u32[]{:S(2)}, u32[]{:S(2)}) collective-permute-start(bf16[720,512]{1,0:T(8,128)(2,1)S(1)} %slice.8), channel_id=1, source_target_pairs={{0,16},{4,20},{8,24},{12,28},{16,0},{20,4},{24,8},{28,12},{1,17},{... | collective-permute-start | bytes 2211848 | tf_op jit(solution)/shard_map/ppermute | solution.py:576
  100.1 1.6 collective-permute-start.24
  100.5 18.7 %collective-permute-start.23 = (bf16[720,512]{1,0:T(8,128)(2,1)S(1)}, bf16[720,512]{1,0:T(8,128)(2,1)S(1)}, u32[]{:S(2)}, u32[]{:S(2)}) collective-permute-start(bf16[720,512]{1,0:T(8,128)(2,1)S(1)} %slice.9), channel_id=1, source_target_pairs={{0,8},{4,12},{8,0},{12,4},{16,24},{20,28},{24,16},{28,20},{1,9},{5... | collective-permute-start | bytes 2211848 | tf_op jit(solution)/shard_map/ppermute | solution.py:576
  101.7 24.7 %collective-permute-start.32 = (bf16[768,640]{1,0:T(8,128)(2,1)S(1)}, bf16[768,640]{1,0:T(8,128)(2,1)S(1)}, u32[]{:S(2)}, u32[]{:S(2)}) collective-permute-start(bf16[768,640]{1,0:T(8,128)(2,1)S(1)} %shard_map.89.refs_1_), channel_id=1, source_target_pairs={{0,4},{4,0},{8,12},{12,8},{16,20},{20,16},{24,28},{28,24},{1,5},{5... | collective-permute-start | bytes 2949128 | tf_op jit(solution)/shard_map/ppermute | solution.py:576
  105.9 19.9 %collective-permute-start.31 = (bf16[768,384]{1,0:T(8,128)(2,1)S(1)}, bf16[768,384]{1,0:T(8,128)(2,1)S(1)}, u32[]{:S(2)}, u32[]{:S(2)}) collective-permute-start(bf16[768,384]{1,0:T(8,128)(2,1)S(1)} %get-tuple-element.141.refs_0_), channel_id=1, source_target_pairs={{0,4},{4,0},{8,12},{12,8},{16,20},{20,16},{24,28},{28,24},{1,5},{5... | collective-permute-start | bytes 1769480 | tf_op jit(solution)/shard_map/ppermute | solution.py:576
  117.9 8.3 %collective-permute-start.29 = (bf16[768,384]{1,0:T(8,128)(2,1)S(1)}, bf16[768,384]{1,0:T(8,128)(2,1)S(1)}, u32[]{:S(2)}, u32[]{:S(2)}) collective-permute-start(bf16[768,384]{1,0:T(8,128)(2,1)S(1)} %collective-permute-done.8.refs_0_), channel_id=1, source_target_pairs={{0,4},{4,0},{8,12},{12,8},{16,20},{20,16},{24,28},{28,24},{1,5},{5... | collective-permute-start | bytes 1769480 | tf_op jit(solution)/shard_map/ppermute | solution.py:576
  119.2 12.9 %collective-permute-start.30 = (bf16[768,640]{1,0:T(8,128)(2,1)S(1)}, bf16[768,640]{1,0:T(8,128)(2,1)S(1)}, u32[]{:S(2)}, u32[]{:S(2)}) collective-permute-start(bf16[768,640]{1,0:T(8,128)(2,1)S(1)} %collective-permute-done.18.refs_1_), channel_id=1, source_target_pairs={{0,4},{4,0},{8,12},{12,8},{16,20},{20,16},{24,28},{28,24},{1,5},{5... | collective-permute-start | bytes 2949128 | tf_op jit(solution)/shard_map/ppermute | solution.py:576
  125.8 11.9 %collective-permute-start.28 = (bf16[768,640]{1,0:T(8,128)(2,1)S(1)}, bf16[768,640]{1,0:T(8,128)(2,1)S(1)}, u32[]{:S(2)}, u32[]{:S(2)}) collective-permute-start(bf16[768,640]{1,0:T(8,128)(2,1)S(1)} %collective-permute-done.19.refs_1_), channel_id=1, source_target_pairs={{0,4},{4,0},{8,12},{12,8},{16,20},{20,16},{24,28},{28,24},{1,5},{5... | collective-permute-start | bytes 2949128 | tf_op jit(solution)/shard_map/ppermute | solution.py:576
  125.8 26.4 %collective-permute-start.25 = (bf16[768,640]{1,0:T(8,128)(2,1)S(1)}, bf16[768,640]{1,0:T(8,128)(2,1)S(1)}, u32[]{:S(2)}, u32[]{:S(2)}) collective-permute-start(bf16[768,640]{1,0:T(8,128)(2,1)S(1)} %collective-permute-done.19.refs_1_), channel_id=1, source_target_pairs={{0,1},{1,2},{2,3},{3,0},{4,5},{5,6},{6,7},{7,4},{8,9},{9,10},{10,1... | collective-permute-start | bytes 2949128 | tf_op jit(solution)/shard_map/ppermute | solution.py:583
  126.2 11.5 %collective-permute-start.27 = (bf16[768,384]{1,0:T(8,128)(2,1)S(1)}, bf16[768,384]{1,0:T(8,128)(2,1)S(1)}, u32[]{:S(2)}, u32[]{:S(2)}) collective-permute-start(bf16[768,384]{1,0:T(8,128)(2,1)S(1)} %collective-permute-done.11.refs_0_), channel_id=1, source_target_pairs={{0,4},{4,0},{8,12},{12,8},{16,20},{20,16},{24,28},{28,24},{1,5},{5... | collective-permute-start | bytes 1769480 | tf_op jit(solution)/shard_map/ppermute | solution.py:576
  126.4 19.0 %collective-permute-start.26 = (bf16[768,384]{1,0:T(8,128)(2,1)S(1)}, bf16[768,384]{1,0:T(8,128)(2,1)S(1)}, u32[]{:S(2)}, u32[]{:S(2)}) collective-permute-start(bf16[768,384]{1,0:T(8,128)(2,1)S(1)} %collective-permute-done.17.refs_0_), channel_id=1, source_target_pairs={{0,4},{4,0},{8,12},{12,8},{16,20},{20,16},{24,28},{28,24},{1,5},{5... | collective-permute-start | bytes 1769480 | tf_op jit(solution)/shard_map/ppermute | solution.py:576
  143.4 2.1 copy-start
  145.4 2.3 copy-start.1
  152.2 2.6 %collective-permute-start.33 = (bf16[768,640]{1,0:T(8,128)(2,1)S(1)}, bf16[768,640]{1,0:T(8,128)(2,1)S(1)}, u32[]{:S(2)}, u32[]{:S(2)}) collective-permute-start(bf16[768,640]{1,0:T(8,128)(2,1)S(1)} %collective-permute-done.25.refs_1_), channel_id=1, source_target_pairs={{0,4},{4,0},{8,12},{12,8},{16,20},{20,16},{24,28},{28,24},{1,5},{5... | collective-permute-start | bytes 2949128 | tf_op jit(solution)/shard_map/ppermute | solution.py:576
  160.6 1.3 collective-permute-start.34
  162.5 4.5 %collective-permute-start.35 = (f32[8,1536]{1,0:T(8,128)S(1)}, f32[8,1536]{1,0:T(8,128)S(1)}, u32[]{:S(2)}, u32[]{:S(2)}) collective-permute-start(f32[8,1536]{1,0:T(8,128)S(1)} %shard_map.96.refs_2_), channel_id=1, source_target_pairs={{0,1},{1,0},{2,3},{3,2},{4,5},{5,4},{6,7},{7,6},{8,9},{9,8},{10,11... | collective-permute-start | bytes 147464 | tf_op jit(solution)/shard_map/ppermute | solution.py:655
  162.8 6.9 %collective-permute-start.36 = (f32[8,1536]{1,0:T(8,128)S(1)}, f32[8,1536]{1,0:T(8,128)S(1)}, u32[]{:S(2)}, u32[]{:S(2)}) collective-permute-start(f32[8,1536]{1,0:T(8,128)S(1)} %shard_map.96.refs_2_), channel_id=1, source_target_pairs={{0,2},{1,3},{2,0},{3,1},{4,6},{5,7},{6,4},{7,5},{8,10},{9,11},{10,... | collective-permute-start | bytes 147464 | tf_op jit(solution)/shard_map/ppermute | solution.py:655
  166.6 5.9 %collective-permute-start.37 = (f32[8,1536]{1,0:T(8,128)S(1)}, f32[8,1536]{1,0:T(8,128)S(1)}, u32[]{:S(2)}, u32[]{:S(2)}) collective-permute-start(f32[8,1536]{1,0:T(8,128)S(1)} %shard_map.96.refs_2_), channel_id=1, source_target_pairs={{0,3},{1,2},{2,1},{3,0},{4,7},{5,6},{6,5},{7,4},{8,11},{9,10},{10,... | collective-permute-start | bytes 147464 | tf_op jit(solution)/shard_map/ppermute | solution.py:655
  176.9 19.1 %collective-permute-start.38 = (bf16[720,512]{1,0:T(8,128)(2,1)S(1)}, bf16[720,512]{1,0:T(8,128)(2,1)S(1)}, u32[]{:S(2)}, u32[]{:S(2)}) collective-permute-start(bf16[720,512]{1,0:T(8,128)(2,1)S(1)} %get-tuple-element.182), channel_id=1, source_target_pairs={{0,8},{4,12},{8,0},{12,4},{16,24},{20,28},{24,16},{28,20},{1,9},{5... | collective-permute-start | bytes 2211848 | tf_op jit(solution)/shard_map/ppermute | solution.py:576
  177.6 18.4 %collective-permute-start.39 = (bf16[720,512]{1,0:T(8,128)(2,1)S(1)}, bf16[720,512]{1,0:T(8,128)(2,1)S(1)}, u32[]{:S(2)}, u32[]{:S(2)}) collective-permute-start(bf16[720,512]{1,0:T(8,128)(2,1)S(1)} %get-tuple-element.183), channel_id=1, source_target_pairs={{0,16},{4,20},{8,24},{12,28},{16,0},{20,4},{24,8},{28,12},{1,17},{... | collective-permute-start | bytes 2211848 | tf_op jit(solution)/shard_map/ppermute | solution.py:576
  179.1 17.0 %collective-permute-start.40 = (bf16[64,720]{1,0:T(8,128)(2,1)S(1)}, bf16[64,720]{1,0:T(8,128)(2,1)S(1)}, u32[]{:S(2)}, u32[]{:S(2)}) collective-permute-start(bf16[64,720]{1,0:T(8,128)(2,1)S(1)} %get-tuple-element.191.mine_ref), channel_id=1, source_target_pairs={{0,8},{4,12},{8,0},{12,4},{16,24},{20,28},{24,16},{28,20},{1,9},{5... | collective-permute-start | bytes 276488 | tf_op jit(solution)/shard_map/ppermute | solution.py:576
  197.4 21.5 %collective-permute-start.42 = (bf16[720,512]{1,0:T(8,128)(2,1)S(1)}, bf16[720,512]{1,0:T(8,128)(2,1)S(1)}, u32[]{:S(2)}, u32[]{:S(2)}) collective-permute-start(bf16[720,512]{1,0:T(8,128)(2,1)S(1)} %get-tuple-element.208), channel_id=1, source_target_pairs={{0,16},{4,12},{8,24},{12,4},{16,0},{20,28},{24,8},{28,20},{1,17},{... | collective-permute-start | bytes 2211848 | tf_op jit(solution)/shard_map/ppermute | solution.py:580
  199.0 20.0 %collective-permute-start.43 = (bf16[720,512]{1,0:T(8,128)(2,1)S(1)}, bf16[720,512]{1,0:T(8,128)(2,1)S(1)}, u32[]{:S(2)}, u32[]{:S(2)}) collective-permute-start(bf16[720,512]{1,0:T(8,128)(2,1)S(1)} %get-tuple-element.197), channel_id=1, source_target_pairs={{0,8},{4,20},{8,0},{12,28},{16,24},{20,4},{24,16},{28,12},{1,9},{5... | collective-permute-start | bytes 2211848 | tf_op jit(solution)/shard_map/ppermute | solution.py:580
  200.1 18.9 %collective-permute-start.41 = (bf16[64,720]{1,0:T(8,128)(2,1)S(1)}, bf16[64,720]{1,0:T(8,128)(2,1)S(1)}, u32[]{:S(2)}, u32[]{:S(2)}) collective-permute-start(bf16[64,720]{1,0:T(8,128)(2,1)S(1)} %shard_map.99), channel_id=1, source_target_pairs={{0,16},{4,20},{8,24},{12,28},{16,0},{20,4},{24,8},{28,12},{1,17},{... | collective-permute-start | bytes 276488 | tf_op jit(solution)/shard_map/ppermute | solution.py:576
  200.7 24.6 %collective-permute-start.47 = (bf16[720,512]{1,0:T(8,128)(2,1)}, bf16[720,512]{1,0:T(8,128)(2,1)}, u32[]{:S(2)}, u32[]{:S(2)}) collective-permute-start(bf16[720,512]{1,0:T(8,128)(2,1)} %get-tuple-element.207), channel_id=1, source_target_pairs={{0,12},{4,16},{8,4},{12,24},{16,28},{20,0},{24,20},{28,8},{1,13},{... | collective-permute-start | bytes 2211848 | tf_op jit(solution)/shard_map/ppermute | solution.py:580
  200.7 24.6 %collective-permute-start.44 = (bf16[720,512]{1,0:T(8,128)(2,1)}, bf16[720,512]{1,0:T(8,128)(2,1)}, u32[]{:S(2)}, u32[]{:S(2)}) collective-permute-start(bf16[720,512]{1,0:T(8,128)(2,1)} %get-tuple-element.200), channel_id=1, source_target_pairs={{0,4},{4,0},{8,12},{12,8},{16,20},{20,16},{24,28},{28,24},{1,5},{5... | collective-permute-start | bytes 2211848 | tf_op jit(solution)/shard_map/ppermute | solution.py:576
  219.0 11.8 %collective-permute-start.45 = (bf16[720,512]{1,0:T(8,128)(2,1)}, bf16[720,512]{1,0:T(8,128)(2,1)}, u32[]{:S(2)}, u32[]{:S(2)}) collective-permute-start(bf16[720,512]{1,0:T(8,128)(2,1)} %get-tuple-element.201), channel_id=1, source_target_pairs={{0,20},{4,8},{8,28},{12,0},{16,4},{20,24},{24,12},{28,16},{1,21},{... | collective-permute-start | bytes 2211848 | tf_op jit(solution)/shard_map/ppermute | solution.py:580
  219.0 3.7 %collective-permute-start.46 = (f32[64,720]{1,0:T(8,128)S(1)}, f32[64,720]{1,0:T(8,128)S(1)}, u32[]{:S(2)}, u32[]{:S(2)}) collective-permute-start(f32[64,720]{1,0:T(8,128)S(1)} %convert_add_fusion), channel_id=1, source_target_pairs={{0,4},{4,0},{8,12},{12,8},{16,20},{20,16},{24,28},{28,24},{1,5},{5... | collective-permute-start | bytes 552968 | tf_op jit(solution)/shard_map/ppermute | solution.py:576
